TPU v7x, 32 devices: a whole 2x2x4 slice. The times are simulated.
32 devices in a mesh: sp: 8 (over z, x), bd: 4 (over y, core).
Axes of the slice: x: 2, y: 2, z: 4, core: 2. Of those that a mesh axis runs over, the one named last changes fastest.
Arguments:
- cube: float32 [4, 768, 32, 256], P('bd', 'sp'), may hold values from 0.02 to 25
- taps_x: float32 [4, 768, 25], P('bd', 'sp'), may hold values from 0.1 to 1
- taps_y: float32 [4, 768, 25], P('bd', 'sp'), may hold values from 0.1 to 1
- factor_w: float32 [4, 768, 48], P('bd'), may hold values from 0.1 to 1
- factor_h: float32 [48, 32, 256], P(None, None, 'sp'), may hold values from 0.1 to 1
Outputs:
- w_next: float32 [4, 768, 48], P('bd')
- h_next: float32 [48, 32, 256], P(None, None, 'sp')
All inputs are finite; a program needn't handle non-finite values.
Results may differ from a plain program's by a relative error of at most 0.000071.
Values sent between devices are 32-bit elements; how exact they have to be, the bound alone decides.
No kernel may reach another device: no remote copies, remote signals or barrier semaphores. Data moves between devices by JAX's collectives and lax.ppermute only.
A program may use at most 128 MiB of HBM per device.

v0:
```python
import jax
import jax.numpy as jnp
from jax import lax
from jax.sharding import PartitionSpec as P


def normalized(kernel):
    return kernel / jnp.sum(kernel, axis=-1, keepdims=True)


def band_weights(kernel, size_in, size_out, offset):
    tap_count = kernel.shape[-1]
    in_index = lax.broadcasted_iota(jnp.int32, (size_in, size_out, tap_count), 0)
    out_index = lax.broadcasted_iota(jnp.int32, (size_in, size_out, tap_count), 1)
    tap_index = lax.broadcasted_iota(jnp.int32, (size_in, size_out, tap_count), 2)
    select = (tap_index == in_index - out_index + offset).astype(jnp.float32)
    return jnp.einsum("pk,iok->pio", kernel, select, precision=lax.Precision.HIGHEST)


def blur_rows(planes, kernel_y):
    margin = (kernel_y.shape[-1] - 1) // 2
    height = planes.shape[1]
    band_table = band_weights(kernel_y, height, height, margin)
    return jnp.einsum("piz,pio->poz", planes, band_table, precision=lax.Precision.HIGHEST)


def blur_columns(planes, kernel_x):
    margin = (kernel_x.shape[-1] - 1) // 2
    count, height, length = planes.shape
    blocks = planes.reshape(count, height, length // 128, 128)
    empty = jnp.zeros((count, height, 1, 128), jnp.float32)
    left_block = jnp.concatenate([empty, blocks[:, :, :-1]], axis=2)
    right_block = jnp.concatenate([blocks[:, :, 1:], empty], axis=2)
    window = jnp.concatenate([left_block, blocks, right_block], axis=3)
    band_table = band_weights(kernel_x, 384, 128, margin - 128)
    result = jnp.einsum("pybi,pio->pybo", window, band_table, precision=lax.Precision.HIGHEST)
    return result.reshape(count, height, length)


def local(cube, taps_x, taps_y, factor_w, factor_h):
    highest = lax.Precision.HIGHEST
    kernel_x = normalized(taps_x[0])
    kernel_y = normalized(taps_y[0])
    rows_done = blur_rows(cube[0], kernel_y)
    w_band = factor_w[0]
    blurred = blur_columns(rows_done, kernel_x)[None]
    moved = lax.all_to_all(blurred, "sp", split_axis=3, concat_axis=1, tiled=True)
    numer_part = jnp.einsum("lr,plyx->pryx", w_band, moved, precision=highest)
    gram_part = jnp.dot(w_band.T, w_band, precision=highest)
    numer_h, gram_w = lax.psum((numer_part[0], gram_part), "bd")
    h_next = factor_h * numer_h / jnp.einsum("rq,qyx->ryx", gram_w, factor_h, precision=highest)
    x_band = moved[0]
    gram_h_part = jnp.einsum("ryx,qyx->rq", h_next, h_next, precision=highest)
    numer_w_part = jnp.einsum("lyx,ryx->lr", x_band, h_next, precision=highest)
    numer_w, gram_h = lax.psum((numer_w_part, gram_h_part), "sp")
    w_next = w_band * numer_w / jnp.dot(w_band, gram_h, precision=highest)
    return (w_next[None], h_next)


def solution(mesh):
    in_specs = (
        P("bd", "sp", None, None),
        P("bd", "sp", None),
        P("bd", "sp", None),
        P("bd", None, None),
        P(None, None, "sp"),
    )
    out_specs = (P("bd", None, None), P(None, None, "sp"))
    return jax.shard_map(local, mesh=mesh, in_specs=in_specs, out_specs=out_specs, check_vma=False)
```

profile of v0, /device:TPU:0, one launch (start us, length us, event | category | flops | bytes accessed | tf_op | source)
XLA Modules:
  0.0 317.6 jit_solution(7674492828194875349)
XLA Ops:
  7.2 0.0 copy-start
  7.2 0.9 reduce_sum.18
  8.1 1.9 fusion.16
  10.0 3.3 %copy.29 = f32[96,32,32]{1,2,0:T(8,128)} copy(f32[96,32,32]{0,2,1:T(8,128)} %fusion.16) | data formatting | bytes 786432 | tf_op jit(solution)/shard_map/pk,iok->pio/dot_general | solution.py:17
  13.4 0.0 copy-done
  13.4 4.5 %fusion.11 = f32[96,4,2,8,128]{4,3,2,1,0:T(8,128)S(1)} fusion(f32[96,32,32]{1,2,0:T(8,128)} %copy.29, f32[1,96,32,256]{3,2,1,0:T(8,128)S(1)} %copy-done), kind=kOutput, calls=%fused_computation.18 | convolution fusion | flops 301989888 | bytes 6684672 | tf_op jit(solution)/shard_map/piz,pio->poz/dot_general | solution.py:24
  17.8 0.4 copy.57
  18.2 0.0 copy-start.1
  18.2 1.7 copy-done.1
  19.9 0.0 copy-start.7
  19.9 2.0 fusion.36
  21.9 0.0 copy-done.7
  22.0 0.0 copy-start.2
  22.0 0.0 copy-start.4
  22.0 0.0 copy-start.5
  22.0 7.8 %convolution_bitcast_fusion = f32[96,384,128,1]{2,0,1,3:T(8,128)S(1)} fusion(f32[1,96,25]{1,0,2:T(1,128)S(1)} %copy-done.7, f32[96]{0:T(128)S(1)} %reduce_sum.19), kind=kOutput, calls=%fused_computation.9 | convolution fusion | flops 1419266432 | bytes 18884352 | tf_op jit(solution)/shard_map/pk,iok->pio/dot_general | solution.py:17
  29.8 0.0 copy-done.2
  29.8 0.0 copy-done.4
  29.8 0.0 copy-done.5
  29.9 42.0 %fusion = f32[96,32,2,128]{3,1,2,0:T(8,128)} fusion(f32[96,384,128,1]{2,0,1,3:T(8,128)S(1)} %convolution_bitcast_fusion, f32[96,32,1,128]{3,1,2,0:T(8,128)S(1)} %copy-done.5, f32[96,32,1,128]{3,1,2,0:T(8,128)S(1)} %copy-done.4, f32[96,32,2,128]{3,1,2,0:T(8,128)S(1)} %bitcast.79), kind=kOutput, calls=%fused_computation | convolution fusion | flops 3638034432 | bytes 28311552 | tf_op jit(solution)/shard_map/pybi,pio->pybo/dot_general | solution.py:36
  71.9 5.5 %copy.41 = f32[96,32,2,128]{0,1,3,2:T(8,128)} copy(f32[96,32,2,128]{3,1,2,0:T(8,128)} %fusion) | data formatting | bytes 6291456 | tf_op jit(solution)/shard_map/broadcast_in_dim;reshape | solution.py:46
  77.4 0.0 copy-start.6
  77.4 7.4 %all-to-all-start = ((f32[1,96,32,256]{1,2,0,3:T(8,128)}), f32[1,96,32,256]{1,2,0,3:T(8,128)}, u32[]{:S(2)}, u32[]{:S(2)}) async-start(f32[1,96,32,256]{1,2,0,3:T(8,128)} %bitcast.76), calls=%async_computation | async-start | bytes 8388608 | tf_op jit(solution)/shard_map/all_to_all | solution.py:47
  84.8 0.0 all-reduce.5.cloned.1.call-start
  84.8 0.0 copy-done.6
  84.8 0.3 fusion.19
  85.1 11.6 %psum.29 = f32[48,48]{1,0:T(8,128)S(1)} all-reduce(f32[48,48]{1,0:T(8,128)S(1)} %fusion.19), channel_id=1, replica_groups=mesh['sp'=8,'bd'=4] {'bd'}, use_global_device_ids=true, to_apply=%region_3.0 | all-reduce | flops 2304 | bytes 18432 | tf_op jit(solution)/shard_map/psum | solution.py:50
  96.7 81.4 %all-to-all-done = f32[1,96,32,256]{1,2,0,3:T(8,128)} async-done(((f32[1,96,32,256]{1,2,0,3:T(8,128)}), f32[1,96,32,256]{1,2,0,3:T(8,128)}, u32[]{:S(2)}, u32[]{:S(2)}) %all-to-all-start) | async-done | bytes 3145760 | tf_op jit(solution)/shard_map/all_to_all | solution.py:47
  178.1 4.6 %copy.36 = f32[1,96,32,256]{1,3,2,0:T(8,128)S(1)} copy(f32[1,96,32,256]{1,2,0,3:T(8,128)} %all-to-all-done) | data formatting | bytes 6291456 | tf_op jit(solution)/shard_map/all_to_all | solution.py:47
  182.7 5.7 %copy.37 = f32[1,8,96,32,32]{2,1,4,3,0:T(8,128)} copy(f32[1,8,96,32,32]{2,4,1,3,0:T(8,128)S(1)} %bitcast.77) | data formatting | bytes 6291456 | tf_op jit(solution)/shard_map/all_to_all | solution.py:47
  188.4 5.2 %squeeze.22 = f32[768,32,32]{0,2,1:T(8,128)} reshape(f32[1,8,96,32,32]{2,1,4,3,0:T(8,128)} %copy.37) | data formatting | bytes 6291456 | tf_op jit(solution)/shard_map/squeeze | solution.py:52
  193.6 5.3 %convolution_bitcast_fusion.1 = f32[48,32,32]{0,2,1:T(8,128)} fusion(f32[768,32,32]{0,2,1:T(8,128)} %squeeze.22, f32[1,768,48]{1,2,0:T(8,128)S(1)} %copy-done.6), kind=kOutput, calls=%fused_computation.19 | convolution fusion | flops 452984832 | bytes 3489792 | tf_op jit(solution)/shard_map/lr,plyx->pryx/dot_general | solution.py:48
  198.8 0.0 all-reduce.5.cloned.1.call-update
  198.9 0.3 all-reduce.7.cloned.1.call-start
  199.2 2.4 fusion.37
  201.6 29.7 %all-reduce.5.cloned.1.call-done = f32[48,32,32]{0,2,1:T(8,128)} async-done(((f32[48,32,32]{0,2,1:T(8,128)}), f32[48,32,32]{0,2,1:T(8,128)}) %all-reduce.5.cloned.1.call-update) | async-done | bytes 196624 | tf_op jit(solution)/shard_map/psum | solution.py:50
  231.3 1.5 multiply_divide_fusion
  232.8 0.0 copy-start.3
  232.8 0.8 copy-done.3
  233.6 4.8 %convolution_bitcast_fusion.3 = f32[768,48]{0,1:T(8,128)} fusion(f32[768,32,32]{0,2,1:T(8,128)} %squeeze.22, f32[48,32,32]{0,2,1:T(8,128)S(1)} %multiply_divide_fusion), kind=kOutput, calls=%fused_computation.23 | convolution fusion | flops 452984832 | bytes 3489792 | tf_op jit(solution)/shard_map/lyx,ryx->lr/dot_general | solution.py:54
  238.4 0.0 all-reduce.7.cloned.1.call-update
  238.4 2.2 convolution_bitcast_fusion.4
  240.6 37.1 %psum.31 = f32[48,48]{1,0:T(8,128)S(1)} all-reduce(f32[48,48]{1,0:T(8,128)S(1)} %convolution_bitcast_fusion.4), channel_id=1, replica_groups=mesh['sp'=8,'bd'=4] {'sp'}, use_global_device_ids=true, to_apply=%region_5.0 | all-reduce | flops 2304 | bytes 18432 | tf_op jit(solution)/shard_map/psum | solution.py:55
  277.7 30.7 %all-reduce.7.cloned.1.call-done = f32[768,48]{0,1:T(8,128)} async-done(((f32[768,48]{0,1:T(8,128)}), f32[768,48]{0,1:T(8,128)}) %all-reduce.7.cloned.1.call-update) | async-done | bytes 147472 | tf_op jit(solution)/shard_map/psum | solution.py:55
  308.4 1.9 fusion.15
  (1 shorter events, 0.0 us)
Async XLA Ops:
  7.2 6.2 %copy-start = (f32[1,96,32,256]{3,2,1,0:T(8,128)S(1)}, f32[1,96,32,256]{3,2,1,0:T(8,128)}, u32[]{:S(2)}) copy-start(f32[1,96,32,256]{3,2,1,0:T(8,128)} %param.5) | copy-start | bytes 9437188
  18.2 1.7 copy-start.1
  19.9 2.0 copy-start.7
  22.0 7.9 %copy-start.2 = (f32[96,4,2,8,128]{4,3,1,2,0:T(8,128)S(1)}, f32[96,4,2,8,128]{4,3,1,2,0:T(8,128)}, u32[]{:S(2)}) copy-start(f32[96,4,2,8,128]{4,3,1,2,0:T(8,128)} %copy-done.1) | copy-start | bytes 9437188
  22.0 7.9 %copy-start.4 = (f32[96,32,1,128]{3,1,2,0:T(8,128)S(1)}, f32[96,32,1,128]{3,1,2,0:T(8,128)}, u32[]{:S(2)}) copy-start(f32[96,32,1,128]{3,1,2,0:T(8,128)} %get-tuple-element.2) | copy-start | bytes 4718596
  22.0 7.9 %copy-start.5 = (f32[96,32,1,128]{3,1,2,0:T(8,128)S(1)}, f32[96,32,1,128]{3,1,2,0:T(8,128)}, u32[]{:S(2)}) copy-start(f32[96,32,1,128]{3,1,2,0:T(8,128)} %get-tuple-element.3) | copy-start | bytes 4718596
  77.4 7.4 %copy-start.6 = (f32[1,768,48]{1,2,0:T(8,128)S(1)}, f32[1,768,48]{1,2,0:T(8,128)}, u32[]{:S(2)}) copy-start(f32[1,768,48]{1,2,0:T(8,128)} %param.8) | copy-start | bytes 442372
  77.4 100.7 %all-to-all-start = ((f32[1,96,32,256]{1,2,0,3:T(8,128)}), f32[1,96,32,256]{1,2,0,3:T(8,128)}, u32[]{:S(2)}, u32[]{:S(2)}) async-start(f32[1,96,32,256]{1,2,0,3:T(8,128)} %bitcast.76), calls=%async_computation | async-start | bytes 8388608 | tf_op jit(solution)/shard_map/all_to_all | solution.py:47
  84.8 146.5 %all-reduce.5.cloned.1.call-start = ((), (), s32[]{:S(2)}) async-start(), calls=%async_computation.1 | async-start | bytes 1048576 | tf_op jit(solution)/shard_map/psum | solution.py:50
  198.9 109.6 %all-reduce.7.cloned.1.call-start = ((), (), s32[]{:S(2)}) async-start(), calls=%async_computation.2 | async-start | bytes 294912 | tf_op jit(solution)/shard_map/psum | solution.py:55
  232.8 0.8 copy-start.3
Sparse Core Ops, SparseCore 0:
  199.0 32.2 all-reduce.4
  238.5 69.8 all-reduce.6
where the time goes:
time: 320 us; the launch traced here: 318 us
  waiting for transfers between devices  142 us (44%)
  matrix products  73.1 us (23%)
  blocking collectives  48.7 us (15%)
  local copies, waits for them, and re-layouts  29.2 us (9%)
  between operations  14.6 us (5%)
  starting transfers between devices  7.72 us (2%)
    all_to_all x1, waiting for transfers between devices, local(): lax.all_to_all(blurred, 'sp', split_axis=3, concat_axis=1, tiled=True)  81.4 us
    dot_general x1, matrix products, blur_columns(): jnp.einsum('pybi,pio->pybo', window, band_table, precision=lax.Precision....  42 us
    psum x1, blocking collectives, local(): numer_w, gram_h = lax.psum((numer_w_part, gram_h_part), 'sp')  37.1 us
    psum x1, waiting for transfers between devices, local(): numer_w, gram_h = lax.psum((numer_w_part, gram_h_part), 'sp')  30.7 us
    psum x1, waiting for transfers between devices, local(): numer_h, gram_w = lax.psum((numer_part[0], gram_part), 'bd')  29.7 us
    psum x1, blocking collectives, local(): numer_h, gram_w = lax.psum((numer_part[0], gram_part), 'bd')  11.6 us
    all_to_all x2, local copies, waits for them, and re-layouts, local(): lax.all_to_all(blurred, 'sp', split_axis=3, concat_axis=1, tiled=True)  10.3 us
    dot_general x2, matrix products, band_weights(): jnp.einsum('pk,iok->pio', kernel, select, precision=lax.Precision.HIGHEST)  9.77 us
  transfers between devices with their start and end apart: 3, of which 3 were waited for; matrix products, arithmetic and copies ran while one was open for 2% of the time, Pallas kernels for 0%

commit v1 on v0

--- a/solution.py
+++ b/solution.py
@@ -1,7 +1,359 @@
+import functools
+
 import jax
 import jax.numpy as jnp
 from jax import lax
+from jax.experimental import pallas as pl
+from jax.experimental.pallas import tpu as pltpu
 from jax.sharding import PartitionSpec as P
+
+F32 = jnp.float32
+BF16 = jnp.bfloat16
+LANES = 128
+GROUP = 16
+VMEM_LIMIT = 48 * 1024 * 1024
+
+
+def split(value):
+    high = value.astype(BF16)
+    low = (value - high.astype(F32)).astype(BF16)
+    return high, low
+
+
+def dot(left, right):
+    return lax.dot_general(left, right, (((1,), (0,)), ((), ())), preferred_element_type=F32)
+
+
+def dot_nt(left, right):
+    return lax.dot_general(left, right, (((1,), (1,)), ((), ())), preferred_element_type=F32)
+
+
+def dot_exact(left, right):
+    return lax.dot_general(
+        left, right, (((1,), (0,)), ((), ())),
+        precision=lax.Precision.HIGHEST, preferred_element_type=F32,
+    )
+
+
+def exchange_blocks(rows, block):
+    lane = lax.broadcasted_iota(jnp.int32, rows[0].shape, 1)
+    first_half = lane < 2 * block
+    even = (lane // block) % 2 == 0
+    v0, v1, v2, v3 = rows
+    u0 = jnp.where(first_half, v0, pltpu.roll(v2, 2 * block, 1))
+    u2 = jnp.where(first_half, pltpu.roll(v0, 2 * block, 1), v2)
+    u1 = jnp.where(first_half, v1, pltpu.roll(v3, 2 * block, 1))
+    u3 = jnp.where(first_half, pltpu.roll(v1, 2 * block, 1), v3)
+    w0 = jnp.where(even, u0, pltpu.roll(u1, block, 1))
+    w1 = jnp.where(even, pltpu.roll(u0, 3 * block, 1), u1)
+    w2 = jnp.where(even, u2, pltpu.roll(u3, block, 1))
+    w3 = jnp.where(even, pltpu.roll(u2, 3 * block, 1), u3)
+    return w0, w1, w2, w3
+
+
+def normalized_taps(taps_ref, reverse, work_ref, out_ref):
+    taps = taps_ref.shape[0]
+    planes = taps_ref.shape[2]
+    work_ref[...] = jnp.zeros_like(work_ref)
+    for tap in range(taps):
+        row = taps - 1 - tap if reverse else tap
+        work_ref[row:row + 1, 0:planes] = taps_ref[tap]
+    values = work_ref[...]
+    total = jnp.sum(values, axis=0, keepdims=True)
+    total = jnp.where(total == 0.0, 1.0, total)
+    out_ref[...] = jnp.transpose(values / total)
+
+
+def column_table(row, margin):
+    circulant = pltpu.roll(jnp.broadcast_to(row, (LANES, LANES)), 0, 1, stride=1, stride_axis=0)
+    high = circulant.astype(BF16).astype(F32)
+    low = circulant - high
+    src = lax.broadcasted_iota(jnp.int32, (LANES, LANES), 0)
+    dst = lax.broadcasted_iota(jnp.int32, (LANES, LANES), 1)
+    near = jnp.abs(dst - src) <= margin
+    edge = GROUP
+    wraps_up = (src - dst)[LANES - edge:] > LANES // 2
+    wraps_down = (dst - src)[:edge] > LANES // 2
+    empty = jnp.zeros((LANES - edge, LANES), BF16)
+
+    def table(part):
+        middle = jnp.where(near, part, 0.0).astype(BF16)
+        upper = jnp.where(wraps_up, part[LANES - edge:], 0.0).astype(BF16)
+        lower = jnp.where(wraps_down, part[:edge], 0.0).astype(BF16)
+        top = jnp.concatenate([middle, jnp.concatenate([empty, upper], axis=0)], axis=1)
+        bottom = jnp.concatenate([jnp.concatenate([lower, empty], axis=0), middle], axis=1)
+        return jnp.concatenate([top, bottom], axis=0)
+
+    return table(high), table(low)
+
+
+def row_table(base, margin, height):
+    high = base.astype(BF16).astype(F32)
+    low = base - high
+    plane = lax.broadcasted_iota(jnp.int32, (8, LANES), 0)
+    lane = lax.broadcasted_iota(jnp.int32, (8, LANES), 1)
+    per_vector = LANES // height
+    own = lane // height == plane % per_vector
+    masks = [own & (plane // per_vector == part) for part in range(8 * height // LANES)]
+
+    def table(part):
+        strips = []
+        for row in range(height):
+            rolled = pltpu.roll(part, (row - margin) % LANES, 1)
+            strips.append(jnp.concatenate([jnp.where(mask, rolled, 0.0) for mask in masks], axis=1))
+        return jnp.concatenate(strips, axis=0).astype(BF16)
+
+    return table(high), table(low)
+
+
+def blur_kernel(cube_ref, taps_x_ref, taps_y_ref, w_ref, xh_ref, xl_ref, *rest):
+    part_refs = rest[:8]
+    work_ref, kx_ref, ky_ref = rest[8:]
+    step = pl.program_id(0)
+    taps = taps_x_ref.shape[0]
+    margin = (taps - 1) // 2
+    height = cube_ref.shape[1]
+
+    @pl.when(step == 0)
+    def _():
+        normalized_taps(taps_x_ref, True, work_ref, kx_ref)
+        normalized_taps(taps_y_ref, False, work_ref, ky_ref)
+        kx_ref[...] = pltpu.roll(kx_ref[...], LANES - margin, 1)
+        per_vector = LANES // height
+        place = lax.broadcasted_iota(jnp.int32, (LANES, LANES), 0) % per_vector
+        values = ky_ref[...]
+        placed = values
+        for k in range(1, per_vector):
+            placed = jnp.where(place == k, pltpu.roll(values, k * height, 1), placed)
+        ky_ref[...] = placed
+
+    halves = []
+    for half in range(GROUP // 8):
+        done = []
+        for plane in range(8 * half, 8 * half + 8):
+            row = kx_ref[pl.ds(step * GROUP + plane, 1), :]
+            table_high, table_low = column_table(row, margin)
+            high, low = split(cube_ref[plane])
+            both = dot(jnp.concatenate([high, low], axis=0), table_high)
+            done.append(both[:height] + (both[height:] + dot(high, table_low)))
+        high, low = split(jnp.concatenate(done, axis=0))
+        rows = ky_ref[pl.ds(pl.multiple_of(step * GROUP + 8 * half, 8), 8), :]
+        table_high, table_low = row_table(rows, margin, height)
+        result = dot(table_high, high) + (dot(table_low, high) + dot(table_high, low))
+        halves.append(result.reshape(height, 8, result.shape[1]))
+    high, low = split(jnp.concatenate(halves, axis=1))
+    planes_here = pl.ds(pl.multiple_of(step * GROUP, GROUP), GROUP)
+    xh_ref[:, planes_here, :] = high
+    xl_ref[:, planes_here, :] = low
+
+    @pl.when(step == pl.num_programs(0) - 1)
+    def _():
+        planes = xh_ref.shape[1]
+        rank, band = w_ref.shape
+        me_sp = lax.axis_index("sp")
+        me_bd = lax.axis_index("bd")
+        bands = lax.axis_size("bd")
+        pieces = lax.axis_size("sp")
+        tall = height // bands
+        wide = xh_ref.shape[2] // pieces
+        shift = lax.rem(band - me_sp * planes, band)
+        w_high, w_low = split(pltpu.roll(w_ref[...], shift, 1)[:, :planes])
+        w_both = jnp.concatenate([w_high, w_low], axis=0)
+        for rel_bd in (1, 3, 0, 2):
+            first_row = lax.bitwise_xor(me_bd, rel_bd) * tall
+            sums = []
+            for row in range(tall):
+                both = dot(w_both, xh_ref[first_row + row])
+                sums.append(both[:rank] + (both[rank:] + dot(w_high, xl_ref[first_row + row])))
+            for column in range(2):
+                vectors = []
+                for quarter in range(2):
+                    vectors.append(exchange_blocks(
+                        [sums[4 * quarter + k][:, column * LANES:(column + 1) * LANES] for k in range(4)], wide))
+                for k in range(4):
+                    piece = jnp.concatenate([vectors[0][k], vectors[1][k]], axis=1)
+                    owner = column * 4 + k
+                    rel_sp = lax.bitwise_xor(me_sp, owner)
+                    inner = rel_sp // 2
+                    low_bit = rel_sp % 2
+                    base = (rel_bd % 2) * 4 + (rel_bd // 2) * 2
+
+                    @pl.when(low_bit == 0)
+                    def _():
+                        part_refs[base][inner] = piece
+
+                    @pl.when(low_bit == 1)
+                    def _():
+                        part_refs[base + 1][inner] = piece
+
+
+def blur_call(cube, taps_x, taps_y, w_rows):
+    planes, height, length = cube.shape
+    rank = w_rows.shape[0]
+    taps = taps_x.shape[0]
+    part = jax.ShapeDtypeStruct((4, rank, 256), F32)
+    whole = lambda shape: pl.BlockSpec(shape, lambda i: (0,) * len(shape))
+    return pl.pallas_call(
+        blur_kernel,
+        grid=(planes // GROUP,),
+        out_shape=[jax.ShapeDtypeStruct((height, planes, length), BF16)] * 2 + [part] * 8,
+        in_specs=[
+            pl.BlockSpec((GROUP, height, length), lambda i: (i, 0, 0)),
+            whole(taps_x.shape), whole(taps_y.shape), whole(w_rows.shape),
+        ],
+        out_specs=[whole((height, planes, length))] * 2 + [whole(part.shape)] * 8,
+        scratch_shapes=[pltpu.VMEM((LANES, LANES), F32)] * 3,
+        compiler_params=pltpu.CompilerParams(
+            dimension_semantics=("arbitrary",), vmem_limit_bytes=VMEM_LIMIT),
+    )(cube, taps_x, taps_y, w_rows)
+
+
+def gram_kernel(w_ref, out_ref):
+    high, low = split(w_ref[...])
+    both = jnp.concatenate([high, low], axis=0)
+    rank = w_ref.shape[0]
+    total = dot_nt(both, both)
+    out_ref[...] = total[:rank, :rank] + (total[rank:, :rank] + total[:rank, rank:]) + total[rank:, rank:]
+
+
+def gram_call(w_rows):
+    rank = w_rows.shape[0]
+    return pl.pallas_call(
+        gram_kernel,
+        out_shape=jax.ShapeDtypeStruct((rank, rank), F32),
+    )(w_rows)
+
+
+def update_h_kernel(n0, n1, n2, n3, g0, g1, g2, g3, h_ref, out_ref):
+    tall = h_ref.shape[0] // lax.axis_size("bd")
+    first = pl.multiple_of(lax.axis_index("bd") * tall, tall)
+    here = h_ref[pl.ds(first, tall)]
+    here = jnp.transpose(here.reshape(-1, here.shape[2]))
+    gram = (g0[...] + g1[...]) + (g2[...] + g3[...])
+    numer = (n0[...] + n1[...]) + (n2[...] + n3[...])
+    out_ref[...] = here * numer / dot_exact(gram, here)
+
+
+def update_h_call(numer, gram, h_columns):
+    return pl.pallas_call(
+        update_h_kernel,
+        out_shape=jax.ShapeDtypeStruct(numer[0].shape, F32),
+    )(*numer, *gram, h_columns)
+
+
+def update_w_kernel(xh_ref, xl_ref, w_ref, *rest):
+    part_refs = rest[:8]
+    w_out, h_out, all_ref = rest[8:]
+    height, planes, length = xh_ref.shape
+    rank, band = w_ref.shape
+    me_sp = lax.axis_index("sp")
+    me_bd = lax.axis_index("bd")
+    bands = lax.axis_size("bd")
+    pieces = lax.axis_size("sp")
+    tall = height // bands
+    wide = length // pieces
+    for rel in range(bands * pieces):
+        slot, inner = rel // 4, rel % 4
+        rel_bd = (slot // 4) + 2 * ((slot // 2) % 2)
+        rel_sp = slot % 2 + 2 * inner
+        owner = lax.bitwise_xor(me_bd, rel_bd) * pieces + lax.bitwise_xor(me_sp, rel_sp)
+        all_ref[owner] = part_refs[slot][inner]
+    for part in range(bands):
+        mine = jnp.transpose(all_ref[part * pieces + me_sp])
+        h_out[part * tall:(part + 1) * tall] = mine.reshape(tall, wide, rank)
+    numer = jnp.zeros((rank, planes), F32)
+    gram = jnp.zeros((rank, rank), F32)
+    for part in range(bands):
+        rows = [[None, None] for _ in range(tall)]
+        for column in range(2):
+            for quarter in range(2):
+                vectors = exchange_blocks(
+                    [all_ref[part * pieces + column * 4 + k][:, quarter * LANES:(quarter + 1) * LANES]
+                     for k in range(4)], wide)
+                for k in range(4):
+                    rows[4 * quarter + k][column] = vectors[k]
+        for row in range(tall):
+            high, low = split(jnp.concatenate(rows[row], axis=1))
+            both = jnp.concatenate([high, low], axis=0)
+            product = dot_nt(both, xh_ref[part * tall + row])
+            numer = numer + (product[:rank] + (product[rank:] + dot_nt(high, xl_ref[part * tall + row])))
+            product = dot_nt(both, high)
+            gram = gram + (product[:rank] + (product[rank:] + dot_nt(high, low)))
+    shift = lax.rem(band - me_sp * planes, band)
+    w_here = pltpu.roll(w_ref[...], shift, 1)[:, :planes]
+    w_out[...] = w_here * numer / dot_exact(gram, w_here)
+
+
+def update_w_call(x_high, x_low, w_rows, parts):
+    height, planes, length = x_high.shape
+    rank = w_rows.shape[0]
+    wide = length // lax.axis_size("sp")
+    return pl.pallas_call(
+        update_w_kernel,
+        out_shape=[
+            jax.ShapeDtypeStruct((rank, planes), F32),
+            jax.ShapeDtypeStruct((height, wide, rank), F32),
+        ],
+        scratch_shapes=[pltpu.VMEM((4 * len(parts),) + parts[0].shape[1:], F32)],
+        compiler_params=pltpu.CompilerParams(vmem_limit_bytes=VMEM_LIMIT),
+    )(x_high, x_low, w_rows, *parts)
+
+
+def gather_w_kernel(*refs):
+    part_refs = refs[:-2]
+    out_ref, all_ref = refs[-2:]
+    planes = part_refs[0].shape[1]
+    me_sp = lax.axis_index("sp")
+    for rel, part in enumerate(part_refs):
+        all_ref[lax.bitwise_xor(me_sp, rel), :, 0:planes] = part[...]
+    for owner in range(len(part_refs)):
+        out_ref[:, owner * planes:(owner + 1) * planes] = all_ref[owner][:, :planes]
+
+
+def gather_w_call(parts):
+    rank, planes = parts[0].shape
+    return pl.pallas_call(
+        gather_w_kernel,
+        out_shape=jax.ShapeDtypeStruct((rank, planes * len(parts)), F32),
+        scratch_shapes=[pltpu.VMEM((len(parts), rank, LANES), F32)],
+    )(*parts)
+
+
+def send(value, mask_sp, mask_bd):
+    bands = lax.axis_size("bd")
+    pieces = lax.axis_size("sp")
+    pairs = []
+    for s in range(pieces):
+        for b in range(bands):
+            pairs.append((s * bands + b, (s ^ mask_sp) * bands + (b ^ mask_bd)))
+    return lax.ppermute(value, ("sp", "bd"), pairs)
+
+
+def local(cube, taps_x, taps_y, factor_w, factor_h):
+    bands = lax.axis_size("bd")
+    pieces = lax.axis_size("sp")
+    w_rows = jnp.transpose(factor_w[0])
+    taps_x = jnp.transpose(taps_x, (2, 0, 1))
+    taps_y = jnp.transpose(taps_y, (2, 0, 1))
+    h_columns = jnp.transpose(factor_h, (1, 2, 0))
+    gram = gram_call(w_rows)
+    grams = [gram] + [send(gram, 0, mask) for mask in range(1, bands)]
+    x_high, x_low, *parts = blur_call(cube[0], taps_x, taps_y, w_rows)
+    keep, give = parts[:4], parts[4:]
+    taken = [send(value, 0, 1) for value in give]
+    chip = [mine + other for mine, other in zip(keep, taken)]
+    around = [chip[0]] + [send(chip[k], k % 2, 2 * (k // 2)) for k in range(1, 4)]
+    square = [(around[0][k] + around[1][k]) + (around[2][k] + around[3][k]) for k in range(4)]
+    line = [square[0]] + [send(square[k], 2 * k, 0) for k in range(1, 4)]
+    h_piece = update_h_call(line, grams, h_columns)
+    h_line = [h_piece] + [send(h_piece, 2 * k, 0) for k in range(1, 4)]
+    h_line = jnp.stack(h_line)
+    h_parts = [h_line] + [send(h_line, k % 2, 2 * (k // 2)) for k in range(1, 4)]
+    h_parts = h_parts + [send(value, 0, 1) for value in h_parts]
+    w_piece, h_next = update_w_call(x_high, x_low, w_rows, h_parts)
+    w_pieces = [w_piece] + [send(w_piece, mask, 0) for mask in range(1, pieces)]
+    w_next = gather_w_call(w_pieces)
+    return jnp.transpose(w_next)[None], jnp.transpose(h_next, (2, 0, 1))
 
 
 def normalized(kernel):
@@ -37,7 +389,7 @@
     return result.reshape(count, height, length)
 
 
-def local(cube, taps_x, taps_y, factor_w, factor_h):
+def local_any(cube, taps_x, taps_y, factor_w, factor_h):
     highest = lax.Precision.HIGHEST
     kernel_x = normalized(taps_x[0])
     kernel_y = normalized(taps_y[0])
@@ -66,4 +418,9 @@
         P(None, None, "sp"),
     )
     out_specs = (P("bd", None, None), P(None, None, "sp"))
-    return jax.shard_map(local, mesh=mesh, in_specs=in_specs, out_specs=out_specs, check_vma=False)
+
+    def body(cube, *rest):
+        suits = lax.axis_size("sp") == 8 and lax.axis_size("bd") == 4 and cube.shape[1] % GROUP == 0
+        return (local if suits else local_any)(cube, *rest)
+
+    return jax.shard_map(body, mesh=mesh, in_specs=in_specs, out_specs=out_specs, check_vma=False)

time: 320 us -> 88 us (0.28)
  waiting for transfers between devices: 142 us -> 28.7 us
  matrix products: 73.1 us -> 0 us
  blocking collectives: 48.7 us -> 0 us
  local copies, waits for them, and re-layouts: 29.2 us -> 3.55 us
  starting transfers between devices: 7.72 us -> 31.5 us
  Pallas kernels: 0 us -> 21.5 us
  between operations: 14.6 us -> 0.8 us
    all_to_all x1 -> x0, waiting for transfers between devices: 81.4 us -> none  [local(): lax.all_to_all(blurred, 'sp', split_axis=3, concat_axis=1, tiled=True)]
    dot_general x9 -> x0, matrix products: 70.7 us -> none  [the longest x1 42 us: blur_columns(): jnp.einsum('pybi,pio->pybo', window, band_table, precision=lax.Precision....]
    psum x2 -> x0, waiting for transfers between devices: 60.5 us -> none  [the longest x1 30.7 us: local(): numer_w, gram_h = lax.psum((numer_w_part, gram_h_part), 'sp')]
    psum x2 -> x0, blocking collectives: 48.7 us -> none  [the longest x1 37.1 us: local(): numer_w, gram_h = lax.psum((numer_w_part, gram_h_part), 'sp')]
    ppermute x0 -> x30, starting transfers between devices: none -> 31.5 us  [send(): return lax.ppermute(value, ('sp', 'bd'), pairs)]
    ppermute x0 -> x30, waiting for transfers between devices: none -> 28.7 us  [send(): return lax.ppermute(value, ('sp', 'bd'), pairs)]
    pallas_call x0 -> x5, Pallas kernels: none -> 21.5 us  [the longest x1 12.4 us: blur_call(): pl.pallas_call(blur_kernel, grid=(planes // GROUP,), out_shape=[jax.Shape...]
    all_to_all x2 -> x0, local copies, waits for them, and re-layouts: 10.3 us -> none  [local(): lax.all_to_all(blurred, 'sp', split_axis=3, concat_axis=1, tiled=True)]
  transfers between devices with their start and end apart: 3 -> 30, of which waited for: 3 -> 15; matrix products, arithmetic and copies ran while one was open for 2% -> 0% of each run, Pallas kernels for 0% -> 2%
where the time goes in v1:
time: 88 us; the launch traced here: 87.6 us
  starting transfers between devices  31.5 us (36%)
  waiting for transfers between devices  28.7 us (33%)
  Pallas kernels  21.5 us (24%)
  local copies, waits for them, and re-layouts  3.55 us (4%)
  other arithmetic  1.6 us (2%)
    ppermute x30, starting transfers between devices, send(): return lax.ppermute(value, ('sp', 'bd'), pairs)  31.5 us
    ppermute x30, waiting for transfers between devices, send(): return lax.ppermute(value, ('sp', 'bd'), pairs)  28.7 us
    pallas_call x1, Pallas kernels, blur_call(): pl.pallas_call(blur_kernel, grid=(planes // GROUP,), out_shape=[jax.Shape...  12.4 us
    unnamed x34, local copies, waits for them, and re-layouts  3.55 us
    pallas_call x1, Pallas kernels, update_w_call(): pl.pallas_call(update_w_kernel, out_shape=[jax.ShapeDtypeStruct((rank, pl...  3.54 us
    pallas_call x1, Pallas kernels, update_h_call(): pl.pallas_call(update_h_kernel, out_shape=jax.ShapeDtypeStruct(numer[0].s...  2.11 us
    pallas_call x1, Pallas kernels, gram_call(): pl.pallas_call(gram_kernel, out_shape=jax.ShapeDtypeStruct((rank, rank),...  1.77 us
  transfers between devices with their start and end apart: 30, of which 15 were waited for; matrix products, arithmetic and copies ran while one was open for 0% of the time, Pallas kernels for 2%

profile of v1, /device:TPU:0, one launch (start us, length us, event | category | flops | bytes accessed | tf_op | source)
XLA Modules:
  0.0 87.6 jit_solution(5341815142809047877)
XLA Ops:
  0.6 0.0 copy-start
  0.6 0.9 %copy-done = f32[1,768,48]{1,2,0:T(8,128)S(1)} copy-done((f32[1,768,48]{1,2,0:T(8,128)S(1)}, f32[1,768,48]{1,2,0:T(8,128)}, u32[]{:S(2)}) %copy-start) | copy-done | bytes 147480
  1.5 0.7 copy-done.3
  2.3 0.7 copy-done.4
  3.0 12.4 %shard_map.68 = (bf16[32,96,256]{2,1,0:T(8,128)(2,1)S(1)}, bf16[32,96,256]{2,1,0:T(8,128)(2,1)S(1)}, f32[4,48,256]{2,1,0:T(8,128)S(1)}, f32[4,48,256]{2,1,0:T(8,...) custom-call(f32[96,32,256]{2,1,0:T(8,128)} %bitcast.28, ...), custom_call_target="tpu_custom_call" | custom-call | tf_op jit(solution)/shard_map/pallas_call | solution.py:196
  15.4 0.5 collective-permute-start.1
  15.9 0.1 collective-permute-start.3
  16.0 0.4 collective-permute-start.5
  16.4 0.1 collective-permute-start
  16.5 0.5 collective-permute-done.1
  17.0 2.9 %collective-permute-start.2 = (f32[4,48,256]{2,1,0:T(8,128)S(1)}, f32[4,48,256]{2,1,0:T(8,128)S(1)}, u32[]{:S(2)}, u32[]{:S(2)}) collective-permute-start(f32[4,48,256]{2,1,0:T(8,128)S(1)} %add.68), channel_id=1, source_target_pairs={{0,4},{1,5},{2,6},{3,7},{4,0},{5,1},{6,2},{7,3},{8,12},{9,13},{10,... | collective-permute-start | bytes 589832 | tf_op jit(solution)/shard_map/ppermute | solution.py:329
  19.9 0.0 collective-permute-done.3
  20.0 1.6 %collective-permute-start.4 = (f32[4,48,256]{2,1,0:T(8,128)S(1)}, f32[4,48,256]{2,1,0:T(8,128)S(1)}, u32[]{:S(2)}, u32[]{:S(2)}) collective-permute-start(f32[4,48,256]{2,1,0:T(8,128)S(1)} %add.70), channel_id=1, source_target_pairs={{0,2},{1,3},{2,0},{3,1},{4,6},{5,7},{6,4},{7,5},{8,10},{9,11},{10,... | collective-permute-start | bytes 589832 | tf_op jit(solution)/shard_map/ppermute | solution.py:329
  21.6 0.0 copy-start.1
  21.6 0.2 collective-permute-start.6
  21.8 3.8 %collective-permute-done.2 = f32[4,48,256]{2,1,0:T(8,128)S(1)} collective-permute-done((f32[4,48,256]{2,1,0:T(8,128)S(1)}, f32[4,48,256]{2,1,0:T(8,128)S(1)}, u32[]{:S(2)}, u32[]{:S(2)}) %collective-permute-start.2) | collective-permute-done | bytes 196640 | tf_op jit(solution)/shard_map/ppermute | solution.py:329
  25.6 5.3 %collective-permute-done.4 = f32[4,48,256]{2,1,0:T(8,128)S(1)} collective-permute-done((f32[4,48,256]{2,1,0:T(8,128)S(1)}, f32[4,48,256]{2,1,0:T(8,128)S(1)}, u32[]{:S(2)}, u32[]{:S(2)}) %collective-permute-start.4) | collective-permute-done | bytes 196640 | tf_op jit(solution)/shard_map/ppermute | solution.py:329
  30.9 0.7 fusion.1
  31.6 3.6 %collective-permute-start.9 = (f32[48,256]{1,0:T(8,128)S(1)}, f32[48,256]{1,0:T(8,128)S(1)}, u32[]{:S(2)}, u32[]{:S(2)}) collective-permute-start(f32[48,256]{1,0:T(8,128)S(1)} %get-tuple-element.26), channel_id=1, source_target_pairs={{0,24},{1,25},{2,26},{3,27},{4,28},{5,29},{6,30},{7,31},{8,16},{9,... | collective-permute-start | bytes 147464 | tf_op jit(solution)/shard_map/ppermute | solution.py:329
  35.2 0.8 collective-permute-start.7
  36.0 1.8 %shard_map.69.g0 = f32[48,48]{1,0:T(8,128)} custom-call(f32[48,768]{1,0:T(8,128)} %bitcast.23), custom_call_target="tpu_custom_call" | custom-call | tf_op jit(solution)/shard_map/pallas_call | solution.py:221
  37.8 0.0 collective-permute-start.12
  37.8 1.5 %collective-permute-start.11 = (f32[48,48]{1,0:T(8,128)}, f32[48,48]{1,0:T(8,128)S(1)}, u32[]{:S(2)}, u32[]{:S(2)}) collective-permute-start(f32[48,48]{1,0:T(8,128)} %shard_map.69.g0), channel_id=1, source_target_pairs={{0,2},{1,3},{2,0},{3,1},{4,6},{5,7},{6,4},{7,5},{8,10},{9,11},{10,... | collective-permute-start | bytes 27656 | tf_op jit(solution)/shard_map/ppermute | solution.py:329
  39.3 2.1 %collective-permute-done.12.g3 = f32[48,48]{1,0:T(8,128)S(1)} collective-permute-done((f32[48,48]{1,0:T(8,128)}, f32[48,48]{1,0:T(8,128)S(1)}, u32[]{:S(2)}, u32[]{:S(2)}) %collective-permute-start.12) | collective-permute-done | bytes 9248 | tf_op jit(solution)/shard_map/ppermute | solution.py:329
  41.4 0.1 collective-permute-start.10
  41.5 0.3 collective-permute-done.11.g2
  41.8 1.0 %collective-permute-done.10.g1 = f32[48,48]{1,0:T(8,128)S(1)} collective-permute-done((f32[48,48]{1,0:T(8,128)}, f32[48,48]{1,0:T(8,128)S(1)}, u32[]{:S(2)}, u32[]{:S(2)}) %collective-permute-start.10) | collective-permute-done | bytes 9248 | tf_op jit(solution)/shard_map/ppermute | solution.py:329
  42.8 0.0 collective-permute-done.9.n3
  42.8 0.0 collective-permute-done.8.n2
  42.8 0.0 copy-start.6
  42.9 0.0 collective-permute-done.7.n1
  42.9 0.6 copy-done.15
  43.4 0.0 copy-done.5
  43.5 0.0 copy-done.6
  43.5 2.1 %shard_map.70 = f32[48,256]{1,0:T(8,128)} custom-call(f32[48,256]{1,0:T(8,128)} %get-tuple-element.29.n0, f32[48,256]{1,0:T(8,128)} %collective-permute-done.7.n1, f32[48,256]{1,0:T(8,128)} %copy-done.6, f32[48,256]{1,0:T(8,128)} %copy-done.5, f32[48,48]{1,0:T(8,128)} %shard_map.69.g0, f32[48,48]{1,0:T(8,128)} %copy-done.15, f32[48,48]{1,0:T(8,128)} %copy-done.13, ...), custom_call_target="tpu_custom_call" | custom-call | tf_op jit(solution)/shard_map/pallas_call | solution.py:238
  45.6 3.6 %collective-permute-start.15 = (f32[48,256]{1,0:T(8,128)}, f32[48,256]{1,0:T(8,128)S(1)}, u32[]{:S(2)}, u32[]{:S(2)}) collective-permute-start(f32[48,256]{1,0:T(8,128)} %shard_map.70), channel_id=1, source_target_pairs={{0,24},{1,25},{2,26},{3,27},{4,28},{5,29},{6,30},{7,31},{8,16},{9,... | collective-permute-start | bytes 147464 | tf_op jit(solution)/shard_map/ppermute | solution.py:329
  49.2 0.0 collective-permute-start.14
  49.2 0.8 collective-permute-start.13
  50.0 2.1 %collective-permute-done.15 = f32[48,256]{1,0:T(8,128)S(1)} collective-permute-done((f32[48,256]{1,0:T(8,128)}, f32[48,256]{1,0:T(8,128)S(1)}, u32[]{:S(2)}, u32[]{:S(2)}) %collective-permute-start.15) | collective-permute-done | bytes 49184 | tf_op jit(solution)/shard_map/ppermute | solution.py:329
  52.0 2.4 %collective-permute-done.14 = f32[48,256]{1,0:T(8,128)S(1)} collective-permute-done((f32[48,256]{1,0:T(8,128)}, f32[48,256]{1,0:T(8,128)S(1)}, u32[]{:S(2)}, u32[]{:S(2)}) %collective-permute-start.14) | collective-permute-done | bytes 49184 | tf_op jit(solution)/shard_map/ppermute | solution.py:329
  54.4 0.1 collective-permute-done.13
  54.5 0.8 pad_maximum_fusion.rest_0_
  55.3 1.4 %collective-permute-start.18 = (f32[4,48,256]{2,1,0:T(8,128)S(1)}, f32[4,48,256]{2,1,0:T(8,128)S(1)}, u32[]{:S(2)}, u32[]{:S(2)}) collective-permute-start(f32[4,48,256]{2,1,0:T(8,128)S(1)} %pad_maximum_fusion.rest_0_), channel_id=1, source_target_pairs={{0,6},{1,7},{2,4},{3,5},{4,2},{5,3},{6,0},{7,1},{8,14},{9,15},{10,... | collective-permute-start | bytes 589832 | tf_op jit(solution)/shard_map/ppermute | solution.py:329
  56.7 1.1 %collective-permute-start.17 = (f32[4,48,256]{2,1,0:T(8,128)S(1)}, f32[4,48,256]{2,1,0:T(8,128)S(1)}, u32[]{:S(2)}, u32[]{:S(2)}) collective-permute-start(f32[4,48,256]{2,1,0:T(8,128)S(1)} %pad_maximum_fusion.rest_0_), channel_id=1, source_target_pairs={{0,2},{1,3},{2,0},{3,1},{4,6},{5,7},{6,4},{7,5},{8,10},{9,11},{10,... | collective-permute-start | bytes 589832 | tf_op jit(solution)/shard_map/ppermute | solution.py:329
  57.8 1.1 %collective-permute-start.16 = (f32[4,48,256]{2,1,0:T(8,128)S(1)}, f32[4,48,256]{2,1,0:T(8,128)S(1)}, u32[]{:S(2)}, u32[]{:S(2)}) collective-permute-start(f32[4,48,256]{2,1,0:T(8,128)S(1)} %pad_maximum_fusion.rest_0_), channel_id=1, source_target_pairs={{0,4},{1,5},{2,6},{3,7},{4,0},{5,1},{6,2},{7,3},{8,12},{9,13},{10,... | collective-permute-start | bytes 589832 | tf_op jit(solution)/shard_map/ppermute | solution.py:329
  58.9 5.2 %collective-permute-done.18.rest_3_ = f32[4,48,256]{2,1,0:T(8,128)S(1)} collective-permute-done((f32[4,48,256]{2,1,0:T(8,128)S(1)}, f32[4,48,256]{2,1,0:T(8,128)S(1)}, u32[]{:S(2)}, u32[]{:S(2)}) %collective-permute-start.18) | collective-permute-done | bytes 196640 | tf_op jit(solution)/shard_map/ppermute | solution.py:329
  64.1 2.1 %collective-permute-done.17.rest_2_ = f32[4,48,256]{2,1,0:T(8,128)S(1)} collective-permute-done((f32[4,48,256]{2,1,0:T(8,128)S(1)}, f32[4,48,256]{2,1,0:T(8,128)S(1)}, u32[]{:S(2)}, u32[]{:S(2)}) %collective-permute-start.17) | collective-permute-done | bytes 196640 | tf_op jit(solution)/shard_map/ppermute | solution.py:329
  66.1 0.0 collective-permute-start.21
  66.1 0.5 collective-permute-start.20
  66.6 0.9 %collective-permute-done.21.rest_6_ = f32[4,48,256]{2,1,0:T(8,128)S(1)} collective-permute-done((f32[4,48,256]{2,1,0:T(8,128)S(1)}, f32[4,48,256]{2,1,0:T(8,128)S(1)}, u32[]{:S(2)}, u32[]{:S(2)}) %collective-permute-start.21) | collective-permute-done | bytes 196640 | tf_op jit(solution)/shard_map/ppermute | solution.py:329
  67.6 0.3 collective-permute-done.20.rest_5_
  67.9 3.5 %shard_map.71 = (f32[48,96]{1,0:T(8,128)S(1)}, f32[32,32,48]{2,1,0:T(8,128)}) custom-call(bf16[32,96,256]{2,1,0:T(8,128)(2,1)S(1)} %get-tuple-element.14.xh_ref, bf16[32,96,256]{2,1,0:T(8,128)(2,1)S(1)} %get-tuple-element.15.xl_ref, f32[48,768]{1,0:T(8,128)S(1)} %bitcast.25, f32[4,48,256]{2,1,0:T(8,128)S(1)} %pad_maximum_fusion.rest_0_, ...), custom_call_target="tpu_custom_call" | custom-call | tf_op jit(solution)/shard_map/pallas_call | solution.py:291
  71.4 2.5 %collective-permute-start.29 = (f32[48,96]{1,0:T(8,128)S(1)}, f32[48,96]{1,0:T(8,128)S(1)}, u32[]{:S(2)}, u32[]{:S(2)}) collective-permute-start(f32[48,96]{1,0:T(8,128)S(1)} %get-tuple-element.24.refs_0_), channel_id=1, source_target_pairs={{0,28},{1,29},{2,30},{3,31},{4,24},{5,25},{6,26},{7,27},{8,20},{9,... | collective-permute-start | bytes 55304 | tf_op jit(solution)/shard_map/ppermute | solution.py:329
  73.9 1.7 %collective-permute-start.28 = (f32[48,96]{1,0:T(8,128)S(1)}, f32[48,96]{1,0:T(8,128)S(1)}, u32[]{:S(2)}, u32[]{:S(2)}) collective-permute-start(f32[48,96]{1,0:T(8,128)S(1)} %get-tuple-element.24.refs_0_), channel_id=1, source_target_pairs={{0,24},{1,25},{2,26},{3,27},{4,28},{5,29},{6,30},{7,31},{8,16},{9,... | collective-permute-start | bytes 55304 | tf_op jit(solution)/shard_map/ppermute | solution.py:329
  75.6 0.6 collective-permute-start.27
  76.2 2.9 %collective-permute-start.26 = (f32[48,96]{1,0:T(8,128)S(1)}, f32[48,96]{1,0:T(8,128)S(1)}, u32[]{:S(2)}, u32[]{:S(2)}) collective-permute-start(f32[48,96]{1,0:T(8,128)S(1)} %get-tuple-element.24.refs_0_), channel_id=1, source_target_pairs={{0,16},{1,17},{2,18},{3,19},{4,20},{5,21},{6,22},{7,23},{8,24},{9,... | collective-permute-start | bytes 55304 | tf_op jit(solution)/shard_map/ppermute | solution.py:329
  79.0 0.2 collective-permute-start.25
  79.2 0.0 collective-permute-done.29.refs_7_
  79.2 2.2 %collective-permute-start.24 = (f32[48,96]{1,0:T(8,128)S(1)}, f32[48,96]{1,0:T(8,128)S(1)}, u32[]{:S(2)}, u32[]{:S(2)}) collective-permute-start(f32[48,96]{1,0:T(8,128)S(1)} %get-tuple-element.24.refs_0_), channel_id=1, source_target_pairs={{0,8},{1,9},{2,10},{3,11},{4,12},{5,13},{6,14},{7,15},{8,0},{9,1},... | collective-permute-start | bytes 55304 | tf_op jit(solution)/shard_map/ppermute | solution.py:329
  81.5 1.1 %collective-permute-start.23 = (f32[48,96]{1,0:T(8,128)S(1)}, f32[48,96]{1,0:T(8,128)S(1)}, u32[]{:S(2)}, u32[]{:S(2)}) collective-permute-start(f32[48,96]{1,0:T(8,128)S(1)} %get-tuple-element.24.refs_0_), channel_id=1, source_target_pairs={{0,4},{1,5},{2,6},{3,7},{4,0},{5,1},{6,2},{7,3},{8,12},{9,13},{10,... | collective-permute-start | bytes 55304 | tf_op jit(solution)/shard_map/ppermute | solution.py:329
  82.6 1.2 %collective-permute-done.25.refs_3_ = f32[48,96]{1,0:T(8,128)S(1)} collective-permute-done((f32[48,96]{1,0:T(8,128)S(1)}, f32[48,96]{1,0:T(8,128)S(1)}, u32[]{:S(2)}, u32[]{:S(2)}) %collective-permute-start.25) | collective-permute-done | bytes 18464 | tf_op jit(solution)/shard_map/ppermute | solution.py:329
  83.8 1.5 %collective-permute-done.23.refs_1_ = f32[48,96]{1,0:T(8,128)S(1)} collective-permute-done((f32[48,96]{1,0:T(8,128)S(1)}, f32[48,96]{1,0:T(8,128)S(1)}, u32[]{:S(2)}, u32[]{:S(2)}) %collective-permute-start.23) | collective-permute-done | bytes 18464 | tf_op jit(solution)/shard_map/ppermute | solution.py:329
  85.3 0.6 copy-done.16
  85.9 1.6 %shard_map.72 = f32[48,768]{1,0:T(8,128)} custom-call(f32[48,96]{1,0:T(8,128)} %copy-done.2, f32[48,96]{1,0:T(8,128)} %copy-done.16, f32[48,96]{1,0:T(8,128)} %copy-done.14, f32[48,96]{1,0:T(8,128)} %copy-done.12, f32[48,96]{1,0:T(8,128)} %copy-done.10, f32[48,96]{1,0:T(8,128)} %copy-done.9, f32[48,96]{1,0:T(8,128)} %copy-done.8, f32[48,96]{1,0:T(8,128)} %copy-done.7), custom_call_target="tpu_custom_call" | custom-call | tf_op jit(solution)/shard_map/pallas_call | solution.py:315
  (41 shorter events, 0.2 us)
Async XLA Ops:
  0.6 0.9 %copy-start = (f32[1,768,48]{1,2,0:T(8,128)S(1)}, f32[1,768,48]{1,2,0:T(8,128)}, u32[]{:S(2)}) copy-start(f32[1,768,48]{1,2,0:T(8,128)} %param.8) | copy-start | bytes 442372
  1.5 0.7 copy-start.3
  2.3 0.7 copy-start.4
  15.4 1.6 %collective-permute-start.1 = (f32[4,48,256]{2,1,0:T(8,128)S(1)}, f32[4,48,256]{2,1,0:T(8,128)S(1)}, u32[]{:S(2)}, u32[]{:S(2)}) collective-permute-start(f32[4,48,256]{2,1,0:T(8,128)S(1)} %get-tuple-element.19), channel_id=1, source_target_pairs={{0,1},{1,0},{2,3},{3,2},{4,5},{5,4},{6,7},{7,6},{8,9},{9,8},{10,11... | collective-permute-start | bytes 589832 | tf_op jit(solution)/shard_map/ppermute | solution.py:329
  15.9 4.0 %collective-permute-start.3 = (f32[4,48,256]{2,1,0:T(8,128)S(1)}, f32[4,48,256]{2,1,0:T(8,128)S(1)}, u32[]{:S(2)}, u32[]{:S(2)}) collective-permute-start(f32[4,48,256]{2,1,0:T(8,128)S(1)} %get-tuple-element.21), channel_id=1, source_target_pairs={{0,1},{1,0},{2,3},{3,2},{4,5},{5,4},{6,7},{7,6},{8,9},{9,8},{10,11... | collective-permute-start | bytes 589832 | tf_op jit(solution)/shard_map/ppermute | solution.py:329
  16.0 5.6 %collective-permute-start.5 = (f32[4,48,256]{2,1,0:T(8,128)S(1)}, f32[4,48,256]{2,1,0:T(8,128)S(1)}, u32[]{:S(2)}, u32[]{:S(2)}) collective-permute-start(f32[4,48,256]{2,1,0:T(8,128)S(1)} %get-tuple-element.23), channel_id=1, source_target_pairs={{0,1},{1,0},{2,3},{3,2},{4,5},{5,4},{6,7},{7,6},{8,9},{9,8},{10,11... | collective-permute-start | bytes 589832 | tf_op jit(solution)/shard_map/ppermute | solution.py:329
  16.4 5.4 %collective-permute-start = (f32[4,48,256]{2,1,0:T(8,128)S(1)}, f32[4,48,256]{2,1,0:T(8,128)S(1)}, u32[]{:S(2)}, u32[]{:S(2)}) collective-permute-start(f32[4,48,256]{2,1,0:T(8,128)S(1)} %get-tuple-element.17), channel_id=1, source_target_pairs={{0,1},{1,0},{2,3},{3,2},{4,5},{5,4},{6,7},{7,6},{8,9},{9,8},{10,11... | collective-permute-start | bytes 589832 | tf_op jit(solution)/shard_map/ppermute | solution.py:329
  17.0 8.6 %collective-permute-start.2 = (f32[4,48,256]{2,1,0:T(8,128)S(1)}, f32[4,48,256]{2,1,0:T(8,128)S(1)}, u32[]{:S(2)}, u32[]{:S(2)}) collective-permute-start(f32[4,48,256]{2,1,0:T(8,128)S(1)} %add.68), channel_id=1, source_target_pairs={{0,4},{1,5},{2,6},{3,7},{4,0},{5,1},{6,2},{7,3},{8,12},{9,13},{10,... | collective-permute-start | bytes 589832 | tf_op jit(solution)/shard_map/ppermute | solution.py:329
  20.0 10.9 %collective-permute-start.4 = (f32[4,48,256]{2,1,0:T(8,128)S(1)}, f32[4,48,256]{2,1,0:T(8,128)S(1)}, u32[]{:S(2)}, u32[]{:S(2)}) collective-permute-start(f32[4,48,256]{2,1,0:T(8,128)S(1)} %add.70), channel_id=1, source_target_pairs={{0,2},{1,3},{2,0},{3,1},{4,6},{5,7},{6,4},{7,5},{8,10},{9,11},{10,... | collective-permute-start | bytes 589832 | tf_op jit(solution)/shard_map/ppermute | solution.py:329
  21.6 46.2 %copy-start.1 = (f32[1,768,48]{1,2,0:T(8,128)S(1)}, f32[1,768,48]{1,2,0:T(8,128)}, u32[]{:S(2)}) copy-start(f32[1,768,48]{1,2,0:T(8,128)} %param.8) | copy-start | bytes 442372
  21.6 9.3 %collective-permute-start.6 = (f32[4,48,256]{2,1,0:T(8,128)S(1)}, f32[4,48,256]{2,1,0:T(8,128)S(1)}, u32[]{:S(2)}, u32[]{:S(2)}) collective-permute-start(f32[4,48,256]{2,1,0:T(8,128)S(1)} %add.71), channel_id=1, source_target_pairs={{0,6},{1,7},{2,4},{3,5},{4,2},{5,3},{6,0},{7,1},{8,14},{9,15},{10,... | collective-permute-start | bytes 589832 | tf_op jit(solution)/shard_map/ppermute | solution.py:329
  31.6 11.2 %collective-permute-start.9 = (f32[48,256]{1,0:T(8,128)S(1)}, f32[48,256]{1,0:T(8,128)S(1)}, u32[]{:S(2)}, u32[]{:S(2)}) collective-permute-start(f32[48,256]{1,0:T(8,128)S(1)} %get-tuple-element.26), channel_id=1, source_target_pairs={{0,24},{1,25},{2,26},{3,27},{4,28},{5,29},{6,30},{7,31},{8,16},{9,... | collective-permute-start | bytes 147464 | tf_op jit(solution)/shard_map/ppermute | solution.py:329
  35.2 7.6 %collective-permute-start.8 = (f32[48,256]{1,0:T(8,128)S(1)}, f32[48,256]{1,0:T(8,128)S(1)}, u32[]{:S(2)}, u32[]{:S(2)}) collective-permute-start(f32[48,256]{1,0:T(8,128)S(1)} %get-tuple-element.27), channel_id=1, source_target_pairs={{0,16},{1,17},{2,18},{3,19},{4,20},{5,21},{6,22},{7,23},{8,24},{9,... | collective-permute-start | bytes 147464 | tf_op jit(solution)/shard_map/ppermute | solution.py:329
  35.2 7.6 %collective-permute-start.7 = (f32[48,256]{1,0:T(8,128)S(1)}, f32[48,256]{1,0:T(8,128)}, u32[]{:S(2)}, u32[]{:S(2)}) collective-permute-start(f32[48,256]{1,0:T(8,128)S(1)} %get-tuple-element.28), channel_id=1, source_target_pairs={{0,8},{1,9},{2,10},{3,11},{4,12},{5,13},{6,14},{7,15},{8,0},{9,1},... | collective-permute-start | bytes 147464 | tf_op jit(solution)/shard_map/ppermute | solution.py:329
  37.8 3.7 %collective-permute-start.12 = (f32[48,48]{1,0:T(8,128)}, f32[48,48]{1,0:T(8,128)S(1)}, u32[]{:S(2)}, u32[]{:S(2)}) collective-permute-start(f32[48,48]{1,0:T(8,128)} %shard_map.69.g0), channel_id=1, source_target_pairs={{0,3},{1,2},{2,1},{3,0},{4,7},{5,6},{6,5},{7,4},{8,11},{9,10},{10,... | collective-permute-start | bytes 27656 | tf_op jit(solution)/shard_map/ppermute | solution.py:329
  37.8 4.1 %collective-permute-start.11 = (f32[48,48]{1,0:T(8,128)}, f32[48,48]{1,0:T(8,128)S(1)}, u32[]{:S(2)}, u32[]{:S(2)}) collective-permute-start(f32[48,48]{1,0:T(8,128)} %shard_map.69.g0), channel_id=1, source_target_pairs={{0,2},{1,3},{2,0},{3,1},{4,6},{5,7},{6,4},{7,5},{8,10},{9,11},{10,... | collective-permute-start | bytes 27656 | tf_op jit(solution)/shard_map/ppermute | solution.py:329
  41.4 1.4 %copy-start.11 = (f32[48,48]{1,0:T(8,128)}, f32[48,48]{1,0:T(8,128)S(1)}, u32[]{:S(2)}) copy-start(f32[48,48]{1,0:T(8,128)S(1)} %collective-permute-done.12.g3) | copy-start | bytes 27652
  41.4 1.4 %collective-permute-start.10 = (f32[48,48]{1,0:T(8,128)}, f32[48,48]{1,0:T(8,128)S(1)}, u32[]{:S(2)}, u32[]{:S(2)}) collective-permute-start(f32[48,48]{1,0:T(8,128)} %shard_map.69.g0), channel_id=1, source_target_pairs={{0,1},{1,0},{2,3},{3,2},{4,5},{5,4},{6,7},{7,6},{8,9},{9,8},{10,11... | collective-permute-start | bytes 27656 | tf_op jit(solution)/shard_map/ppermute | solution.py:329
  41.8 1.0 %copy-start.13 = (f32[48,48]{1,0:T(8,128)}, f32[48,48]{1,0:T(8,128)S(1)}, u32[]{:S(2)}) copy-start(f32[48,48]{1,0:T(8,128)S(1)} %collective-permute-done.11.g2) | copy-start | bytes 27652
  42.8 0.6 copy-start.15
  42.8 0.6 copy-start.5
  42.8 0.6 copy-start.6
  45.6 6.5 %collective-permute-start.15 = (f32[48,256]{1,0:T(8,128)}, f32[48,256]{1,0:T(8,128)S(1)}, u32[]{:S(2)}, u32[]{:S(2)}) collective-permute-start(f32[48,256]{1,0:T(8,128)} %shard_map.70), channel_id=1, source_target_pairs={{0,24},{1,25},{2,26},{3,27},{4,28},{5,29},{6,30},{7,31},{8,16},{9,... | collective-permute-start | bytes 147464 | tf_op jit(solution)/shard_map/ppermute | solution.py:329
  49.2 5.3 %collective-permute-start.14 = (f32[48,256]{1,0:T(8,128)}, f32[48,256]{1,0:T(8,128)S(1)}, u32[]{:S(2)}, u32[]{:S(2)}) collective-permute-start(f32[48,256]{1,0:T(8,128)} %shard_map.70), channel_id=1, source_target_pairs={{0,16},{1,17},{2,18},{3,19},{4,20},{5,21},{6,22},{7,23},{8,24},{9,... | collective-permute-start | bytes 147464 | tf_op jit(solution)/shard_map/ppermute | solution.py:329
  49.2 5.3 %collective-permute-start.13 = (f32[48,256]{1,0:T(8,128)}, f32[48,256]{1,0:T(8,128)S(1)}, u32[]{:S(2)}, u32[]{:S(2)}) collective-permute-start(f32[48,256]{1,0:T(8,128)} %shard_map.70), channel_id=1, source_target_pairs={{0,8},{1,9},{2,10},{3,11},{4,12},{5,13},{6,14},{7,15},{8,0},{9,1},... | collective-permute-start | bytes 147464 | tf_op jit(solution)/shard_map/ppermute | solution.py:329
  55.3 8.7 %collective-permute-start.18 = (f32[4,48,256]{2,1,0:T(8,128)S(1)}, f32[4,48,256]{2,1,0:T(8,128)S(1)}, u32[]{:S(2)}, u32[]{:S(2)}) collective-permute-start(f32[4,48,256]{2,1,0:T(8,128)S(1)} %pad_maximum_fusion.rest_0_), channel_id=1, source_target_pairs={{0,6},{1,7},{2,4},{3,5},{4,2},{5,3},{6,0},{7,1},{8,14},{9,15},{10,... | collective-permute-start | bytes 589832 | tf_op jit(solution)/shard_map/ppermute | solution.py:329
  56.7 9.4 %collective-permute-start.17 = (f32[4,48,256]{2,1,0:T(8,128)S(1)}, f32[4,48,256]{2,1,0:T(8,128)S(1)}, u32[]{:S(2)}, u32[]{:S(2)}) collective-permute-start(f32[4,48,256]{2,1,0:T(8,128)S(1)} %pad_maximum_fusion.rest_0_), channel_id=1, source_target_pairs={{0,2},{1,3},{2,0},{3,1},{4,6},{5,7},{6,4},{7,5},{8,10},{9,11},{10,... | collective-permute-start | bytes 589832 | tf_op jit(solution)/shard_map/ppermute | solution.py:329
  57.8 8.3 %collective-permute-start.16 = (f32[4,48,256]{2,1,0:T(8,128)S(1)}, f32[4,48,256]{2,1,0:T(8,128)S(1)}, u32[]{:S(2)}, u32[]{:S(2)}) collective-permute-start(f32[4,48,256]{2,1,0:T(8,128)S(1)} %pad_maximum_fusion.rest_0_), channel_id=1, source_target_pairs={{0,4},{1,5},{2,6},{3,7},{4,0},{5,1},{6,2},{7,3},{8,12},{9,13},{10,... | collective-permute-start | bytes 589832 | tf_op jit(solution)/shard_map/ppermute | solution.py:329
  58.9 7.8 %collective-permute-start.19 = (f32[4,48,256]{2,1,0:T(8,128)S(1)}, f32[4,48,256]{2,1,0:T(8,128)S(1)}, u32[]{:S(2)}, u32[]{:S(2)}) collective-permute-start(f32[4,48,256]{2,1,0:T(8,128)S(1)} %pad_maximum_fusion.rest_0_), channel_id=1, source_target_pairs={{0,1},{1,0},{2,3},{3,2},{4,5},{5,4},{6,7},{7,6},{8,9},{9,8},{10,11... | collective-permute-start | bytes 589832 | tf_op jit(solution)/shard_map/ppermute | solution.py:329
  64.1 2.6 %collective-permute-start.22 = (f32[4,48,256]{2,1,0:T(8,128)S(1)}, f32[4,48,256]{2,1,0:T(8,128)S(1)}, u32[]{:S(2)}, u32[]{:S(2)}) collective-permute-start(f32[4,48,256]{2,1,0:T(8,128)S(1)} %collective-permute-done.18.rest_3_), channel_id=1, source_target_pairs={{0,1},{1,0},{2,3},{3,2},{4,5},{5,4},{6,7},{7,6},{8,9},{9,8},{10,11... | collective-permute-start | bytes 589832 | tf_op jit(solution)/shard_map/ppermute | solution.py:329
  66.1 1.4 %collective-permute-start.21 = (f32[4,48,256]{2,1,0:T(8,128)S(1)}, f32[4,48,256]{2,1,0:T(8,128)S(1)}, u32[]{:S(2)}, u32[]{:S(2)}) collective-permute-start(f32[4,48,256]{2,1,0:T(8,128)S(1)} %collective-permute-done.17.rest_2_), channel_id=1, source_target_pairs={{0,1},{1,0},{2,3},{3,2},{4,5},{5,4},{6,7},{7,6},{8,9},{9,8},{10,11... | collective-permute-start | bytes 589832 | tf_op jit(solution)/shard_map/ppermute | solution.py:329
  66.1 1.7 %collective-permute-start.20 = (f32[4,48,256]{2,1,0:T(8,128)S(1)}, f32[4,48,256]{2,1,0:T(8,128)S(1)}, u32[]{:S(2)}, u32[]{:S(2)}) collective-permute-start(f32[4,48,256]{2,1,0:T(8,128)S(1)} %collective-permute-done.16.rest_1_), channel_id=1, source_target_pairs={{0,1},{1,0},{2,3},{3,2},{4,5},{5,4},{6,7},{7,6},{8,9},{9,8},{10,11... | collective-permute-start | bytes 589832 | tf_op jit(solution)/shard_map/ppermute | solution.py:329
  71.4 13.9 %copy-start.2 = (f32[48,96]{1,0:T(8,128)}, f32[48,96]{1,0:T(8,128)S(1)}, u32[]{:S(2)}) copy-start(f32[48,96]{1,0:T(8,128)S(1)} %get-tuple-element.24.refs_0_) | copy-start | bytes 55300
  71.4 7.8 %collective-permute-start.29 = (f32[48,96]{1,0:T(8,128)S(1)}, f32[48,96]{1,0:T(8,128)S(1)}, u32[]{:S(2)}, u32[]{:S(2)}) collective-permute-start(f32[48,96]{1,0:T(8,128)S(1)} %get-tuple-element.24.refs_0_), channel_id=1, source_target_pairs={{0,28},{1,29},{2,30},{3,31},{4,24},{5,25},{6,26},{7,27},{8,20},{9,... | collective-permute-start | bytes 55304 | tf_op jit(solution)/shard_map/ppermute | solution.py:329
  73.9 7.5 %collective-permute-start.28 = (f32[48,96]{1,0:T(8,128)S(1)}, f32[48,96]{1,0:T(8,128)S(1)}, u32[]{:S(2)}, u32[]{:S(2)}) collective-permute-start(f32[48,96]{1,0:T(8,128)S(1)} %get-tuple-element.24.refs_0_), channel_id=1, source_target_pairs={{0,24},{1,25},{2,26},{3,27},{4,28},{5,29},{6,30},{7,31},{8,16},{9,... | collective-permute-start | bytes 55304 | tf_op jit(solution)/shard_map/ppermute | solution.py:329
  75.6 7.0 %collective-permute-start.27 = (f32[48,96]{1,0:T(8,128)S(1)}, f32[48,96]{1,0:T(8,128)S(1)}, u32[]{:S(2)}, u32[]{:S(2)}) collective-permute-start(f32[48,96]{1,0:T(8,128)S(1)} %get-tuple-element.24.refs_0_), channel_id=1, source_target_pairs={{0,20},{1,21},{2,22},{3,23},{4,16},{5,17},{6,18},{7,19},{8,28},{9,... | collective-permute-start | bytes 55304 | tf_op jit(solution)/shard_map/ppermute | solution.py:329
  76.2 6.4 %collective-permute-start.26 = (f32[48,96]{1,0:T(8,128)S(1)}, f32[48,96]{1,0:T(8,128)S(1)}, u32[]{:S(2)}, u32[]{:S(2)}) collective-permute-start(f32[48,96]{1,0:T(8,128)S(1)} %get-tuple-element.24.refs_0_), channel_id=1, source_target_pairs={{0,16},{1,17},{2,18},{3,19},{4,20},{5,21},{6,22},{7,23},{8,24},{9,... | collective-permute-start | bytes 55304 | tf_op jit(solution)/shard_map/ppermute | solution.py:329
  79.0 4.7 %collective-permute-start.25 = (f32[48,96]{1,0:T(8,128)S(1)}, f32[48,96]{1,0:T(8,128)S(1)}, u32[]{:S(2)}, u32[]{:S(2)}) collective-permute-start(f32[48,96]{1,0:T(8,128)S(1)} %get-tuple-element.24.refs_0_), channel_id=1, source_target_pairs={{0,12},{1,13},{2,14},{3,15},{4,8},{5,9},{6,10},{7,11},{8,4},{9,5},... | collective-permute-start | bytes 55304 | tf_op jit(solution)/shard_map/ppermute | solution.py:329
  79.2 6.1 %copy-start.7 = (f32[48,96]{1,0:T(8,128)}, f32[48,96]{1,0:T(8,128)S(1)}, u32[]{:S(2)}) copy-start(f32[48,96]{1,0:T(8,128)S(1)} %collective-permute-done.29.refs_7_) | copy-start | bytes 55300
  79.2 4.6 %collective-permute-start.24 = (f32[48,96]{1,0:T(8,128)S(1)}, f32[48,96]{1,0:T(8,128)S(1)}, u32[]{:S(2)}, u32[]{:S(2)}) collective-permute-start(f32[48,96]{1,0:T(8,128)S(1)} %get-tuple-element.24.refs_0_), channel_id=1, source_target_pairs={{0,8},{1,9},{2,10},{3,11},{4,12},{5,13},{6,14},{7,15},{8,0},{9,1},... | collective-permute-start | bytes 55304 | tf_op jit(solution)/shard_map/ppermute | solution.py:329
  81.5 3.8 %copy-start.8 = (f32[48,96]{1,0:T(8,128)}, f32[48,96]{1,0:T(8,128)S(1)}, u32[]{:S(2)}) copy-start(f32[48,96]{1,0:T(8,128)S(1)} %collective-permute-done.28.refs_6_) | copy-start | bytes 55300
  81.5 3.8 %collective-permute-start.23 = (f32[48,96]{1,0:T(8,128)S(1)}, f32[48,96]{1,0:T(8,128)S(1)}, u32[]{:S(2)}, u32[]{:S(2)}) collective-permute-start(f32[48,96]{1,0:T(8,128)S(1)} %get-tuple-element.24.refs_0_), channel_id=1, source_target_pairs={{0,4},{1,5},{2,6},{3,7},{4,0},{5,1},{6,2},{7,3},{8,12},{9,13},{10,... | collective-permute-start | bytes 55304 | tf_op jit(solution)/shard_map/ppermute | solution.py:329
  82.5 2.7 %copy-start.9 = (f32[48,96]{1,0:T(8,128)}, f32[48,96]{1,0:T(8,128)S(1)}, u32[]{:S(2)}) copy-start(f32[48,96]{1,0:T(8,128)S(1)} %collective-permute-done.27.refs_5_) | copy-start | bytes 55300
  82.6 2.8 %copy-start.10 = (f32[48,96]{1,0:T(8,128)}, f32[48,96]{1,0:T(8,128)S(1)}, u32[]{:S(2)}) copy-start(f32[48,96]{1,0:T(8,128)S(1)} %collective-permute-done.26.refs_4_) | copy-start | bytes 55300
  83.8 1.5 %copy-start.12 = (f32[48,96]{1,0:T(8,128)}, f32[48,96]{1,0:T(8,128)S(1)}, u32[]{:S(2)}) copy-start(f32[48,96]{1,0:T(8,128)S(1)} %collective-permute-done.25.refs_3_) | copy-start | bytes 55300
  83.8 1.6 %copy-start.14 = (f32[48,96]{1,0:T(8,128)}, f32[48,96]{1,0:T(8,128)S(1)}, u32[]{:S(2)}) copy-start(f32[48,96]{1,0:T(8,128)S(1)} %collective-permute-done.24.refs_2_) | copy-start | bytes 55300
  85.3 0.6 copy-start.16

commit v2 on v1

--- a/solution.py
+++ b/solution.py
@@ -106,9 +106,17 @@
     return table(high), table(low)
 
 
-def blur_kernel(cube_ref, taps_x_ref, taps_y_ref, w_ref, xh_ref, xl_ref, *rest):
-    part_refs = rest[:8]
-    work_ref, kx_ref, ky_ref = rest[8:]
+def band_gram(w_rows):
+    high, low = split(w_rows)
+    rank = w_rows.shape[0]
+    padded = jnp.concatenate([high, jnp.zeros((2 * LANES - rank, high.shape[1]), BF16)], axis=0)
+    padded_low = jnp.concatenate([low, jnp.zeros((2 * LANES - rank, low.shape[1]), BF16)], axis=0)
+    both = dot_nt(jnp.concatenate([high, low], axis=0), padded)
+    return both[:rank] + (both[rank:] + dot_nt(high, padded_low))
+
+
+def blur_kernel(cube_ref, taps_x_hbm, taps_y_hbm, w_hbm, xh_ref, xl_ref, far_keep, far_give, near_keep, near_give,
+                taps_x_ref, taps_y_ref, w_ref, sems, work_ref, kx_ref, ky_ref):
     step = pl.program_id(0)
     taps = taps_x_ref.shape[0]
     margin = (taps - 1) // 2
@@ -116,6 +124,18 @@
 
     @pl.when(step == 0)
     def _():
+        copies = [
+            pltpu.make_async_copy(taps_x_hbm, taps_x_ref, sems.at[0]),
+            pltpu.make_async_copy(taps_y_hbm, taps_y_ref, sems.at[1]),
+            pltpu.make_async_copy(w_hbm, w_ref, sems.at[2]),
+        ]
+        for copy in copies:
+            copy.start()
+        for copy in copies:
+            copy.wait()
+        gram = band_gram(w_ref[...])
+        near_keep[8] = gram
+        near_give[8] = gram
         normalized_taps(taps_x_ref, True, work_ref, kx_ref)
         normalized_taps(taps_y_ref, False, work_ref, ky_ref)
         kx_ref[...] = pltpu.roll(kx_ref[...], LANES - margin, 1)
@@ -143,180 +163,192 @@
         halves.append(result.reshape(height, 8, result.shape[1]))
     high, low = split(jnp.concatenate(halves, axis=1))
     planes_here = pl.ds(pl.multiple_of(step * GROUP, GROUP), GROUP)
-    xh_ref[:, planes_here, :] = high
-    xl_ref[:, planes_here, :] = low
+    for column in range(2):
+        xh_ref[column, :, planes_here, :] = high[:, :, column * LANES:(column + 1) * LANES]
+        xl_ref[column, :, planes_here, :] = low[:, :, column * LANES:(column + 1) * LANES]
 
     @pl.when(step == pl.num_programs(0) - 1)
     def _():
-        planes = xh_ref.shape[1]
+        planes = xh_ref.shape[2]
         rank, band = w_ref.shape
         me_sp = lax.axis_index("sp")
         me_bd = lax.axis_index("bd")
-        bands = lax.axis_size("bd")
-        pieces = lax.axis_size("sp")
-        tall = height // bands
-        wide = xh_ref.shape[2] // pieces
+        tall = height // lax.axis_size("bd")
+        wide = 2 * LANES // lax.axis_size("sp")
         shift = lax.rem(band - me_sp * planes, band)
         w_high, w_low = split(pltpu.roll(w_ref[...], shift, 1)[:, :planes])
         w_both = jnp.concatenate([w_high, w_low], axis=0)
-        for rel_bd in (1, 3, 0, 2):
+        for rel_bd in range(4):
             first_row = lax.bitwise_xor(me_bd, rel_bd) * tall
             sums = []
             for row in range(tall):
-                both = dot(w_both, xh_ref[first_row + row])
-                sums.append(both[:rank] + (both[rank:] + dot(w_high, xl_ref[first_row + row])))
+                x_high = jnp.concatenate([xh_ref[0, first_row + row], xh_ref[1, first_row + row]], axis=1)
+                x_low = jnp.concatenate([xl_ref[0, first_row + row], xl_ref[1, first_row + row]], axis=1)
+                both = dot(w_both, x_high)
+                sums.append(both[:rank] + (both[rank:] + dot(w_high, x_low)))
+            far_ref, near_ref = (far_keep, near_keep) if rel_bd % 2 == 0 else (far_give, near_give)
             for column in range(2):
-                vectors = []
-                for quarter in range(2):
-                    vectors.append(exchange_blocks(
-                        [sums[4 * quarter + k][:, column * LANES:(column + 1) * LANES] for k in range(4)], wide))
+                quarters = [
+                    exchange_blocks(
+                        [sums[4 * quarter + k][:, column * LANES:(column + 1) * LANES] for k in range(4)], wide)
+                    for quarter in range(2)]
                 for k in range(4):
-                    piece = jnp.concatenate([vectors[0][k], vectors[1][k]], axis=1)
-                    owner = column * 4 + k
-                    rel_sp = lax.bitwise_xor(me_sp, owner)
-                    inner = rel_sp // 2
-                    low_bit = rel_sp % 2
-                    base = (rel_bd % 2) * 4 + (rel_bd // 2) * 2
-
-                    @pl.when(low_bit == 0)
+                    piece = jnp.concatenate([quarters[0][k], quarters[1][k]], axis=1)
+                    rel_sp = lax.bitwise_xor(me_sp, column * 4 + k)
+                    place = (rel_bd // 2) * 4 + (rel_sp % 2) * 2 + (rel_sp // 2) % 2
+
+                    @pl.when(rel_sp >= 4)
                     def _():
-                        part_refs[base][inner] = piece
-
-                    @pl.when(low_bit == 1)
+                        far_ref[place] = piece
+
+                    @pl.when(rel_sp < 4)
                     def _():
-                        part_refs[base + 1][inner] = piece
+                        near_ref[place] = piece
 
 
 def blur_call(cube, taps_x, taps_y, w_rows):
     planes, height, length = cube.shape
     rank = w_rows.shape[0]
-    taps = taps_x.shape[0]
-    part = jax.ShapeDtypeStruct((4, rank, 256), F32)
+    far = jax.ShapeDtypeStruct((8, rank, 2 * LANES), F32)
+    near = jax.ShapeDtypeStruct((9, rank, 2 * LANES), F32)
+    image = (2, height, planes, LANES)
     whole = lambda shape: pl.BlockSpec(shape, lambda i: (0,) * len(shape))
     return pl.pallas_call(
         blur_kernel,
         grid=(planes // GROUP,),
-        out_shape=[jax.ShapeDtypeStruct((height, planes, length), BF16)] * 2 + [part] * 8,
-        in_specs=[
-            pl.BlockSpec((GROUP, height, length), lambda i: (i, 0, 0)),
-            whole(taps_x.shape), whole(taps_y.shape), whole(w_rows.shape),
-        ],
-        out_specs=[whole((height, planes, length))] * 2 + [whole(part.shape)] * 8,
-        scratch_shapes=[pltpu.VMEM((LANES, LANES), F32)] * 3,
+        out_shape=[jax.ShapeDtypeStruct(image, BF16)] * 2 + [far, far, near, near],
+        in_specs=[pl.BlockSpec((GROUP, height, length), lambda i: (i, 0, 0))]
+        + [pl.BlockSpec(memory_space=pltpu.HBM)] * 3,
+        out_specs=[whole(image)] * 2 + [whole(far.shape)] * 2 + [whole(near.shape)] * 2,
+        scratch_shapes=[pltpu.VMEM(value.shape, F32) for value in (taps_x, taps_y, w_rows)]
+        + [pltpu.SemaphoreType.DMA((3,))] + [pltpu.VMEM((LANES, LANES), F32)] * 3,
         compiler_params=pltpu.CompilerParams(
             dimension_semantics=("arbitrary",), vmem_limit_bytes=VMEM_LIMIT),
     )(cube, taps_x, taps_y, w_rows)
 
 
-def gram_kernel(w_ref, out_ref):
-    high, low = split(w_ref[...])
-    both = jnp.concatenate([high, low], axis=0)
-    rank = w_ref.shape[0]
-    total = dot_nt(both, both)
-    out_ref[...] = total[:rank, :rank] + (total[rank:, :rank] + total[:rank, rank:]) + total[rank:, rank:]
-
-
-def gram_call(w_rows):
-    rank = w_rows.shape[0]
-    return pl.pallas_call(
-        gram_kernel,
-        out_shape=jax.ShapeDtypeStruct((rank, rank), F32),
-    )(w_rows)
-
-
-def update_h_kernel(n0, n1, n2, n3, g0, g1, g2, g3, h_ref, out_ref):
+def ratio_kernel(gram_ref, other_ref, h_ref, out_ref):
     tall = h_ref.shape[0] // lax.axis_size("bd")
     first = pl.multiple_of(lax.axis_index("bd") * tall, tall)
     here = h_ref[pl.ds(first, tall)]
     here = jnp.transpose(here.reshape(-1, here.shape[2]))
-    gram = (g0[...] + g1[...]) + (g2[...] + g3[...])
-    numer = (n0[...] + n1[...]) + (n2[...] + n3[...])
-    out_ref[...] = here * numer / dot_exact(gram, here)
-
-
-def update_h_call(numer, gram, h_columns):
+    gram = gram_ref[...] + other_ref[...]
+    out_ref[...] = here / dot_exact(gram, here)
+
+
+def ratio_call(gram, gram_other, h_columns):
+    rank = h_columns.shape[2]
+    columns = h_columns.shape[0] * h_columns.shape[1] // lax.axis_size("bd")
     return pl.pallas_call(
-        update_h_kernel,
-        out_shape=jax.ShapeDtypeStruct(numer[0].shape, F32),
-    )(*numer, *gram, h_columns)
-
-
-def update_w_kernel(xh_ref, xl_ref, w_ref, *rest):
-    part_refs = rest[:8]
-    w_out, h_out, all_ref = rest[8:]
-    height, planes, length = xh_ref.shape
-    rank, band = w_ref.shape
+        ratio_kernel,
+        out_shape=jax.ShapeDtypeStruct((rank, columns), F32),
+    )(gram, gram_other, h_columns)
+
+
+def accumulate(xh_ref, xl_ref, part_refs, all_ref, column, numer, gram):
+    height, rank = xh_ref.shape[1], all_ref.shape[1]
     me_sp = lax.axis_index("sp")
     me_bd = lax.axis_index("bd")
     bands = lax.axis_size("bd")
-    pieces = lax.axis_size("sp")
     tall = height // bands
-    wide = length // pieces
-    for rel in range(bands * pieces):
-        slot, inner = rel // 4, rel % 4
-        rel_bd = (slot // 4) + 2 * ((slot // 2) % 2)
-        rel_sp = slot % 2 + 2 * inner
-        owner = lax.bitwise_xor(me_bd, rel_bd) * pieces + lax.bitwise_xor(me_sp, rel_sp)
-        all_ref[owner] = part_refs[slot][inner]
+    wide = 2 * LANES // lax.axis_size("sp")
+    for slot in range(8):
+        rel_bd = slot // 4 + 2 * ((slot // 2) % 2)
+        for inner in range(2):
+            owner_sp = lax.bitwise_xor(me_sp, slot % 2 + 2 * inner) % 4
+            all_ref[lax.bitwise_xor(me_bd, rel_bd) * 4 + owner_sp] = part_refs[slot][inner]
     for part in range(bands):
-        mine = jnp.transpose(all_ref[part * pieces + me_sp])
-        h_out[part * tall:(part + 1) * tall] = mine.reshape(tall, wide, rank)
-    numer = jnp.zeros((rank, planes), F32)
-    gram = jnp.zeros((rank, rank), F32)
-    for part in range(bands):
-        rows = [[None, None] for _ in range(tall)]
-        for column in range(2):
-            for quarter in range(2):
-                vectors = exchange_blocks(
-                    [all_ref[part * pieces + column * 4 + k][:, quarter * LANES:(quarter + 1) * LANES]
-                     for k in range(4)], wide)
-                for k in range(4):
-                    rows[4 * quarter + k][column] = vectors[k]
-        for row in range(tall):
-            high, low = split(jnp.concatenate(rows[row], axis=1))
+        rows = []
+        for quarter in range(2):
+            rows += exchange_blocks(
+                [all_ref[part * 4 + k][:, quarter * LANES:(quarter + 1) * LANES] for k in range(4)], wide)
+        for row in range(0, tall, 2):
+            high, low = split(jnp.concatenate([rows[row], rows[row + 1]], axis=1))
             both = jnp.concatenate([high, low], axis=0)
-            product = dot_nt(both, xh_ref[part * tall + row])
-            numer = numer + (product[:rank] + (product[rank:] + dot_nt(high, xl_ref[part * tall + row])))
+            y = part * tall + row
+            x_high = jnp.concatenate([xh_ref[column, y], xh_ref[column, y + 1]], axis=1)
+            x_low = jnp.concatenate([xl_ref[column, y], xl_ref[column, y + 1]], axis=1)
+            product = dot_nt(both, x_high)
+            numer = numer + (product[:rank] + (product[rank:] + dot_nt(high, x_low)))
             product = dot_nt(both, high)
             gram = gram + (product[:rank] + (product[rank:] + dot_nt(high, low)))
+    return numer, gram
+
+
+def near_kernel(xh_ref, xl_ref, *rest):
+    part_refs = rest[:8]
+    numer_out, gram_out, h_out, all_ref = rest[8:]
+    planes = xh_ref.shape[2]
+    rank = all_ref.shape[1]
+    bands = lax.axis_size("bd")
+    tall = xh_ref.shape[1] // bands
+    wide = 2 * LANES // lax.axis_size("sp")
+    me_sp = lax.axis_index("sp")
+    numer, gram = accumulate(
+        xh_ref, xl_ref, part_refs, all_ref, me_sp // 4,
+        jnp.zeros((rank, planes), F32), jnp.zeros((rank, rank), F32))
+    numer_out[...] = numer
+    gram_out[...] = gram
+    for part in range(bands):
+        mine = jnp.transpose(all_ref[part * 4 + me_sp % 4])
+        h_out[part * tall:(part + 1) * tall] = mine.reshape(tall, wide, rank)
+
+
+def near_call(x_high, x_low, parts):
+    _, height, planes, _ = x_high.shape
+    rank = parts[0].shape[1]
+    wide = 2 * LANES // lax.axis_size("sp")
+    return pl.pallas_call(
+        near_kernel,
+        out_shape=[
+            jax.ShapeDtypeStruct((rank, planes), F32),
+            jax.ShapeDtypeStruct((rank, rank), F32),
+            jax.ShapeDtypeStruct((height, wide, rank), F32),
+        ],
+        scratch_shapes=[pltpu.VMEM((16,) + parts[0].shape[1:], F32)],
+        compiler_params=pltpu.CompilerParams(vmem_limit_bytes=VMEM_LIMIT),
+    )(x_high, x_low, *parts)
+
+
+def far_kernel(xh_ref, xl_ref, w_ref, numer_ref, gram_ref, *rest):
+    part_refs = rest[:8]
+    w_out, all_ref = rest[8:]
+    planes = xh_ref.shape[2]
+    band = w_ref.shape[1]
+    me_sp = lax.axis_index("sp")
+    numer, gram = accumulate(
+        xh_ref, xl_ref, part_refs, all_ref, 1 - me_sp // 4, numer_ref[...], gram_ref[...])
     shift = lax.rem(band - me_sp * planes, band)
     w_here = pltpu.roll(w_ref[...], shift, 1)[:, :planes]
     w_out[...] = w_here * numer / dot_exact(gram, w_here)
 
 
-def update_w_call(x_high, x_low, w_rows, parts):
-    height, planes, length = x_high.shape
-    rank = w_rows.shape[0]
-    wide = length // lax.axis_size("sp")
+def far_call(x_high, x_low, w_rows, numer, gram, parts):
     return pl.pallas_call(
-        update_w_kernel,
-        out_shape=[
-            jax.ShapeDtypeStruct((rank, planes), F32),
-            jax.ShapeDtypeStruct((height, wide, rank), F32),
-        ],
-        scratch_shapes=[pltpu.VMEM((4 * len(parts),) + parts[0].shape[1:], F32)],
+        far_kernel,
+        out_shape=jax.ShapeDtypeStruct(numer.shape, F32),
+        scratch_shapes=[pltpu.VMEM((16,) + parts[0].shape[1:], F32)],
         compiler_params=pltpu.CompilerParams(vmem_limit_bytes=VMEM_LIMIT),
-    )(x_high, x_low, w_rows, *parts)
-
-
-def gather_w_kernel(*refs):
-    part_refs = refs[:-2]
-    out_ref, all_ref = refs[-2:]
-    planes = part_refs[0].shape[1]
+    )(x_high, x_low, w_rows, numer, gram, *parts)
+
+
+def gather_w_kernel(mine_ref, other_ref, out_ref, all_ref):
+    planes = mine_ref.shape[2]
     me_sp = lax.axis_index("sp")
-    for rel, part in enumerate(part_refs):
-        all_ref[lax.bitwise_xor(me_sp, rel), :, 0:planes] = part[...]
-    for owner in range(len(part_refs)):
+    for rel in range(8):
+        part = mine_ref if rel < 4 else other_ref
+        all_ref[lax.bitwise_xor(me_sp, rel), :, 0:planes] = part[rel % 4]
+    for owner in range(8):
         out_ref[:, owner * planes:(owner + 1) * planes] = all_ref[owner][:, :planes]
 
 
-def gather_w_call(parts):
-    rank, planes = parts[0].shape
+def gather_w_call(mine, other):
+    _, rank, planes = mine.shape
     return pl.pallas_call(
         gather_w_kernel,
-        out_shape=jax.ShapeDtypeStruct((rank, planes * len(parts)), F32),
-        scratch_shapes=[pltpu.VMEM((len(parts), rank, LANES), F32)],
-    )(*parts)
+        out_shape=jax.ShapeDtypeStruct((rank, planes * 8), F32),
+        scratch_shapes=[pltpu.VMEM((8, rank, LANES), F32)],
+    )(mine, other)
 
 
 def send(value, mask_sp, mask_bd):
@@ -329,30 +361,43 @@
     return lax.ppermute(value, ("sp", "bd"), pairs)
 
 
+def around(values):
+    return [send(values[k], k % 2, 2 * (k // 2)) for k in range(1, 4)]
+
+
 def local(cube, taps_x, taps_y, factor_w, factor_h):
-    bands = lax.axis_size("bd")
-    pieces = lax.axis_size("sp")
     w_rows = jnp.transpose(factor_w[0])
     taps_x = jnp.transpose(taps_x, (2, 0, 1))
     taps_y = jnp.transpose(taps_y, (2, 0, 1))
     h_columns = jnp.transpose(factor_h, (1, 2, 0))
-    gram = gram_call(w_rows)
-    grams = [gram] + [send(gram, 0, mask) for mask in range(1, bands)]
-    x_high, x_low, *parts = blur_call(cube[0], taps_x, taps_y, w_rows)
-    keep, give = parts[:4], parts[4:]
-    taken = [send(value, 0, 1) for value in give]
-    chip = [mine + other for mine, other in zip(keep, taken)]
-    around = [chip[0]] + [send(chip[k], k % 2, 2 * (k // 2)) for k in range(1, 4)]
-    square = [(around[0][k] + around[1][k]) + (around[2][k] + around[3][k]) for k in range(4)]
-    line = [square[0]] + [send(square[k], 2 * k, 0) for k in range(1, 4)]
-    h_piece = update_h_call(line, grams, h_columns)
-    h_line = [h_piece] + [send(h_piece, 2 * k, 0) for k in range(1, 4)]
-    h_line = jnp.stack(h_line)
-    h_parts = [h_line] + [send(h_line, k % 2, 2 * (k // 2)) for k in range(1, 4)]
-    h_parts = h_parts + [send(value, 0, 1) for value in h_parts]
-    w_piece, h_next = update_w_call(x_high, x_low, w_rows, h_parts)
-    w_pieces = [w_piece] + [send(w_piece, mask, 0) for mask in range(1, pieces)]
-    w_next = gather_w_call(w_pieces)
+    x_high, x_low, far_keep, far_give, near_keep, near_give = blur_call(cube[0], taps_x, taps_y, w_rows)
+    far_taken = send(far_give, 0, 1)
+    near_taken = send(near_give, 0, 1)
+    far = [far_keep[2 * k:2 * k + 2] + far_taken[2 * k:2 * k + 2] for k in range(4)]
+    near = [near_keep[2 * k:2 * k + 2] + near_taken[2 * k:2 * k + 2] for k in range(4)]
+    rank = w_rows.shape[0]
+    gram = near_keep[8, :, :rank] + near_taken[8, :, :rank]
+    gram_other = send(gram, 0, 2)
+    far_round = around(far)
+    near_round = around(near)
+    far_sum = (far[0] + far_round[0]) + (far_round[1] + far_round[2])
+    ratio = ratio_call(gram, gram_other, h_columns)
+    far_other = send(far_sum, 4, 0)
+    far_other, ratio = lax.optimization_barrier((far_other, ratio))
+    line = [(near[0][k] + near_round[0][k]) + (near_round[1][k] + near_round[2][k]) + far_other[k] for k in range(2)]
+    h_piece = ratio * (line[0] + send(line[1], 2, 0))
+    h_near = jnp.stack([h_piece, send(h_piece, 2, 0)])
+    h_far = send(h_near, 4, 0)
+    near_parts = [h_near] + around([h_near] * 4)
+    near_parts = near_parts + [send(value, 0, 1) for value in near_parts]
+    numer, gram_h, h_next = near_call(x_high, x_low, near_parts)
+    far_parts = [h_far] + around([h_far] * 4)
+    numer, *far_parts = lax.optimization_barrier((numer, *far_parts))
+    far_parts = far_parts + [send(value, 0, 1) for value in far_parts]
+    w_piece = far_call(x_high, x_low, w_rows, numer, gram_h, far_parts)
+    w_two = jnp.stack([w_piece, send(w_piece, 1, 0)])
+    w_four = jnp.concatenate([w_two, send(w_two, 2, 0)])
+    w_next = gather_w_call(w_four, send(w_four, 4, 0))
     return jnp.transpose(w_next)[None], jnp.transpose(h_next, (2, 0, 1))
 
 

time: 88 us -> 84.8 us (0.964)
  starting transfers between devices: 31.5 us -> 28.8 us
  other arithmetic: 1.6 us -> 3.16 us
  waiting for transfers between devices: 28.7 us -> 27.5 us
  Pallas kernels: 21.5 us -> 20.6 us
    ppermute x30, starting transfers between devices: 31.5 us -> 28.8 us  [send(): return lax.ppermute(value, ('sp', 'bd'), pairs)]
    add x5, other arithmetic: 0.79 us -> 2.26 us  [the longest x1 0.84 us: local(): near[0][k] + near_round[0][k] + (near_round[1][k] + near_round[2][k])]
    pallas_call x3, Pallas kernels: 7.41 us -> 6.11 us  [the longest x1 2.34 us: near_call(): pl.pallas_call(near_kernel, out_shape=[jax.ShapeDtypeStruct((rank, planes...]
    ppermute x30, waiting for transfers between devices: 28.7 us -> 27.5 us  [send(): return lax.ppermute(value, ('sp', 'bd'), pairs)]
    unnamed x34 -> x16, local copies, waits for them, and re-layouts: 3.55 us -> 3.57 us
  transfers between devices with their start and end apart: 30 -> 30, of which waited for: 15 -> 19; matrix products, arithmetic and copies ran while one was open for 0% -> 2% of each run, Pallas kernels for 2% -> 5%
where the time goes in v2:
time: 84.8 us; the launch traced here: 84.3 us
  starting transfers between devices  28.8 us (34%)
  waiting for transfers between devices  27.5 us (32%)
  Pallas kernels  20.6 us (24%)
  local copies, waits for them, and re-layouts  3.57 us (4%)
  other arithmetic  3.16 us (4%)
    ppermute x30, starting transfers between devices, send(): return lax.ppermute(value, ('sp', 'bd'), pairs)  28.8 us
    ppermute x30, waiting for transfers between devices, send(): return lax.ppermute(value, ('sp', 'bd'), pairs)  27.5 us
    pallas_call x1, Pallas kernels, blur_call(): pl.pallas_call(blur_kernel, grid=(planes // GROUP,), out_shape=[jax.Shape...  12.7 us
    unnamed x16, local copies, waits for them, and re-layouts  3.57 us
    pallas_call x1, Pallas kernels, near_call(): pl.pallas_call(near_kernel, out_shape=[jax.ShapeDtypeStruct((rank, planes...  2.34 us
    pallas_call x1, Pallas kernels, ratio_call(): pl.pallas_call(ratio_kernel, out_shape=jax.ShapeDtypeStruct((rank, column...  1.97 us
    pallas_call x1, Pallas kernels, far_call(): pl.pallas_call(far_kernel, out_shape=jax.ShapeDtypeStruct(numer.shape, F3...  1.8 us
    pallas_call x1, Pallas kernels, gather_w_call(): pl.pallas_call(gather_w_kernel, out_shape=jax.ShapeDtypeStruct((rank, pla...  1.73 us
  transfers between devices with their start and end apart: 30, of which 19 were waited for; matrix products, arithmetic and copies ran while one was open for 2% of the time, Pallas kernels for 5%

profile of v2, /device:TPU:0, one launch (start us, length us, event | category | flops | bytes accessed | tf_op | source)
XLA Modules:
  0.0 84.3 jit_solution(5887846379629621687)
XLA Ops:
  0.6 0.0 copy-start
  0.6 0.9 %copy-done = f32[1,768,48]{1,2,0:T(8,128)S(1)} copy-done((f32[1,768,48]{1,2,0:T(8,128)S(1)}, f32[1,768,48]{1,2,0:T(8,128)}, u32[]{:S(2)}) %copy-start) | copy-done | bytes 147480
  1.5 0.7 copy-done.2
  2.3 0.7 copy-done.3
  3.0 12.7 %shard_map.68 = (bf16[2,32,96,128]{3,2,1,0:T(8,128)(2,1)S(1)}, bf16[2,32,96,128]{3,2,1,0:T(8,128)(2,1)S(1)}, f32[8,48,256]{2,1,0:T(8,128)S(1)}, f32[8,48,256]{2,...) custom-call(f32[96,32,256]{2,1,0:T(8,128)} %bitcast.31, f32[25,1,96]{2,1,0:T(1,128)S(1)} %bitcast.29, ...), custom_call_target="tpu_custom_call" | custom-call | tf_op jit(solution)/shard_map/pallas_call | solution.py:216
  15.7 0.5 collective-permute-start
  16.2 0.1 collective-permute-start.5
  16.3 1.3 %collective-permute-done = f32[8,48,256]{2,1,0:T(8,128)S(1)} collective-permute-done((f32[8,48,256]{2,1,0:T(8,128)S(1)}, f32[8,48,256]{2,1,0:T(8,128)S(1)}, u32[]{:S(2)}, u32[]{:S(2)}) %collective-permute-start) | collective-permute-done | bytes 393248 | tf_op jit(solution)/shard_map/ppermute | solution.py:361
  17.6 3.9 %collective-permute-start.3 = (f32[2,48,256]{2,1,0:T(8,128)S(1)}, f32[2,48,256]{2,1,0:T(8,128)S(1)}, u32[]{:S(2)}, u32[]{:S(2)}) collective-permute-start(f32[2,48,256]{2,1,0:T(8,128)S(1)} %get-tuple-element.38), channel_id=1, source_target_pairs={{0,6},{1,7},{2,4},{3,5},{4,2},{5,3},{6,0},{7,1},{8,14},{9,15},{10,... | collective-permute-start | bytes 294920 | tf_op jit(solution)/shard_map/ppermute | solution.py:361
  21.5 0.5 collective-permute-start.2
  22.0 0.1 collective-permute-start.1
  22.1 0.0 collective-permute-done.5
  22.1 0.7 slice_add_fusion.3
  22.8 2.8 %collective-permute-start.9 = (f32[2,48,256]{2,1,0:T(8,128)}, f32[2,48,256]{2,1,0:T(8,128)S(1)}, u32[]{:S(2)}, u32[]{:S(2)}) collective-permute-start(f32[2,48,256]{2,1,0:T(8,128)} %get-tuple-element.35), channel_id=1, source_target_pairs={{0,6},{1,7},{2,4},{3,5},{4,2},{5,3},{6,0},{7,1},{8,14},{9,15},{10,... | collective-permute-start | bytes 294920 | tf_op jit(solution)/shard_map/ppermute | solution.py:361
  25.7 0.5 collective-permute-start.8
  26.2 0.7 collective-permute-start.7
  26.9 0.7 collective-permute-done.2
  27.6 0.7 fusion.1
  28.3 3.0 %collective-permute-start.4 = (f32[2,48,256]{2,1,0:T(8,128)}, f32[2,48,256]{2,1,0:T(8,128)}, u32[]{:S(2)}, u32[]{:S(2)}) collective-permute-start(f32[2,48,256]{2,1,0:T(8,128)} %fusion.1), channel_id=1, source_target_pairs={{0,16},{1,17},{2,18},{3,19},{4,20},{5,21},{6,22},{7,23},{8,24},{9,... | collective-permute-start | bytes 294920 | tf_op jit(solution)/shard_map/ppermute | solution.py:361
  31.2 1.6 %collective-permute-start.6 = (f32[48,48]{1,0:T(8,128)S(1)}, f32[48,48]{1,0:T(8,128)S(1)}, u32[]{:S(2)}, u32[]{:S(2)}) collective-permute-start(f32[48,48]{1,0:T(8,128)S(1)} %fusion.10.gram_ref), channel_id=1, source_target_pairs={{0,2},{1,3},{2,0},{3,1},{4,6},{5,7},{6,4},{7,5},{8,10},{9,11},{10,... | collective-permute-start | bytes 27656 | tf_op jit(solution)/shard_map/ppermute | solution.py:361
  32.9 2.2 %collective-permute-done.6.other_ref = f32[48,48]{1,0:T(8,128)S(1)} collective-permute-done((f32[48,48]{1,0:T(8,128)S(1)}, f32[48,48]{1,0:T(8,128)S(1)}, u32[]{:S(2)}, u32[]{:S(2)}) %collective-permute-start.6) | collective-permute-done | bytes 9248 | tf_op jit(solution)/shard_map/ppermute | solution.py:361
  35.1 0.6 copy-done.7
  35.7 2.0 %shard_map.69 = f32[48,256]{1,0:T(8,128)} custom-call(f32[48,48]{1,0:T(8,128)} %copy-done.5, f32[48,48]{1,0:T(8,128)} %copy-done.7, f32[32,32,48]{2,1,0:T(8,128)} %bitcast.32), custom_call_target="tpu_custom_call" | custom-call | tf_op jit(solution)/shard_map/pallas_call | solution.py:242
  37.6 0.0 collective-permute-done.4
  37.6 0.0 collective-permute-done.9
  37.7 0.0 collective-permute-done.7
  37.7 0.8 %fusion.4 = f32[48,256]{1,0:T(8,128)S(1)} fusion(f32[2,48,256]{2,1,0:T(8,128)S(1)} %collective-permute-done.9, f32[2,48,256]{2,1,0:T(8,128)S(1)} %collective-permute-done.8, f32[2,48,256]{2,1,0:T(8,128)} %collective-permute-done.7, f32[2,48,256]{2,1,0:T(8,128)S(1)} %get-tuple-element.34, f32[2,48,256]{2,1,0:T(8,128)} %collective-permute-done.4), kind=kLoop, calls=%fused_computation.15 | loop fusion | flops 49152 | bytes 294912 | tf_op jit(solution)/shard_map/add | solution.py:387
  38.5 1.7 %collective-permute-start.10 = (f32[48,256]{1,0:T(8,128)S(1)}, f32[48,256]{1,0:T(8,128)S(1)}, u32[]{:S(2)}, u32[]{:S(2)}) collective-permute-start(f32[48,256]{1,0:T(8,128)S(1)} %fusion.4), channel_id=1, source_target_pairs={{0,8},{1,9},{2,10},{3,11},{4,12},{5,13},{6,14},{7,15},{8,0},{9,1},... | collective-permute-start | bytes 147464 | tf_op jit(solution)/shard_map/ppermute | solution.py:361
  40.2 2.5 %collective-permute-done.10 = f32[48,256]{1,0:T(8,128)S(1)} collective-permute-done((f32[48,256]{1,0:T(8,128)S(1)}, f32[48,256]{1,0:T(8,128)S(1)}, u32[]{:S(2)}, u32[]{:S(2)}) %collective-permute-start.10) | collective-permute-done | bytes 49184 | tf_op jit(solution)/shard_map/ppermute | solution.py:361
  42.7 0.9 %fusion.9 = f32[48,256]{1,0:T(8,128)S(1)} fusion(f32[48,256]{1,0:T(8,128)} %shard_map.69, f32[48,256]{1,0:T(8,128)S(1)} %collective-permute-done.10, f32[2,48,256]{2,1,0:T(8,128)S(1)} %collective-permute-done.9, f32[2,48,256]{2,1,0:T(8,128)S(1)} %collective-permute-done.8, f32[2,48,256]{2,1,0:T(8,128)} %collective-permute-done.7, ...), kind=kLoop, calls=%fused_computation.22 | loop fusion | flops 73728 | bytes 393216 | tf_op jit(solution)/shard_map/mul | solution.py:388
  43.5 1.7 %collective-permute-start.11 = (f32[48,256]{1,0:T(8,128)S(1)}, f32[48,256]{1,0:T(8,128)S(1)}, u32[]{:S(2)}, u32[]{:S(2)}) collective-permute-start(f32[48,256]{1,0:T(8,128)S(1)} %fusion.9), channel_id=1, source_target_pairs={{0,8},{1,9},{2,10},{3,11},{4,12},{5,13},{6,14},{7,15},{8,0},{9,1},... | collective-permute-start | bytes 147464 | tf_op jit(solution)/shard_map/ppermute | solution.py:361
  45.2 2.5 %collective-permute-done.11 = f32[48,256]{1,0:T(8,128)S(1)} collective-permute-done((f32[48,256]{1,0:T(8,128)S(1)}, f32[48,256]{1,0:T(8,128)S(1)}, u32[]{:S(2)}, u32[]{:S(2)}) %collective-permute-start.11) | collective-permute-done | bytes 49184 | tf_op jit(solution)/shard_map/ppermute | solution.py:361
  47.7 1.6 %collective-permute-start.14 = (f32[2,48,256]{2,1,0:T(8,128)S(1)}, f32[2,48,256]{2,1,0:T(8,128)S(1)}, u32[]{:S(2)}, u32[]{:S(2)}) collective-permute-start(f32[2,48,256]{2,1,0:T(8,128)S(1)} %pad_maximum_fusion.rest_0_), channel_id=1, source_target_pairs={{0,6},{1,7},{2,4},{3,5},{4,2},{5,3},{6,0},{7,1},{8,14},{9,15},{10,... | collective-permute-start | bytes 294920 | tf_op jit(solution)/shard_map/ppermute | solution.py:361
  49.4 1.5 %collective-permute-start.13 = (f32[2,48,256]{2,1,0:T(8,128)S(1)}, f32[2,48,256]{2,1,0:T(8,128)S(1)}, u32[]{:S(2)}, u32[]{:S(2)}) collective-permute-start(f32[2,48,256]{2,1,0:T(8,128)S(1)} %pad_maximum_fusion.rest_0_), channel_id=1, source_target_pairs={{0,2},{1,3},{2,0},{3,1},{4,6},{5,7},{6,4},{7,5},{8,10},{9,11},{10,... | collective-permute-start | bytes 294920 | tf_op jit(solution)/shard_map/ppermute | solution.py:361
  50.9 0.4 collective-permute-start.12
  51.3 0.4 collective-permute-start.19
  51.7 0.0 collective-permute-start.15
  51.7 1.6 %collective-permute-done.14.rest_3_ = f32[2,48,256]{2,1,0:T(8,128)S(1)} collective-permute-done((f32[2,48,256]{2,1,0:T(8,128)S(1)}, f32[2,48,256]{2,1,0:T(8,128)S(1)}, u32[]{:S(2)}, u32[]{:S(2)}) %collective-permute-start.14) | collective-permute-done | bytes 98336 | tf_op jit(solution)/shard_map/ppermute | solution.py:361
  53.3 1.0 %collective-permute-done.13.rest_2_ = f32[2,48,256]{2,1,0:T(8,128)S(1)} collective-permute-done((f32[2,48,256]{2,1,0:T(8,128)S(1)}, f32[2,48,256]{2,1,0:T(8,128)S(1)}, u32[]{:S(2)}, u32[]{:S(2)}) %collective-permute-start.13) | collective-permute-done | bytes 98336 | tf_op jit(solution)/shard_map/ppermute | solution.py:361
  54.3 1.1 %collective-permute-done.12.rest_1_ = f32[2,48,256]{2,1,0:T(8,128)S(1)} collective-permute-done((f32[2,48,256]{2,1,0:T(8,128)S(1)}, f32[2,48,256]{2,1,0:T(8,128)S(1)}, u32[]{:S(2)}, u32[]{:S(2)}) %collective-permute-start.12) | collective-permute-done | bytes 98336 | tf_op jit(solution)/shard_map/ppermute | solution.py:361
  55.5 1.3 %collective-permute-done.19.rest_0_ = f32[2,48,256]{2,1,0:T(8,128)S(1)} collective-permute-done((f32[2,48,256]{2,1,0:T(8,128)S(1)}, f32[2,48,256]{2,1,0:T(8,128)S(1)}, u32[]{:S(2)}, u32[]{:S(2)}) %collective-permute-start.19) | collective-permute-done | bytes 98336 | tf_op jit(solution)/shard_map/ppermute | solution.py:361
  56.8 1.6 %collective-permute-start.22 = (f32[2,48,256]{2,1,0:T(8,128)S(1)}, f32[2,48,256]{2,1,0:T(8,128)S(1)}, u32[]{:S(2)}, u32[]{:S(2)}) collective-permute-start(f32[2,48,256]{2,1,0:T(8,128)S(1)} %collective-permute-done.19.rest_0_), channel_id=1, source_target_pairs={{0,6},{1,7},{2,4},{3,5},{4,2},{5,3},{6,0},{7,1},{8,14},{9,15},{10,... | collective-permute-start | bytes 294920 | tf_op jit(solution)/shard_map/ppermute | solution.py:361
  58.4 1.5 %collective-permute-start.21 = (f32[2,48,256]{2,1,0:T(8,128)S(1)}, f32[2,48,256]{2,1,0:T(8,128)S(1)}, u32[]{:S(2)}, u32[]{:S(2)}) collective-permute-start(f32[2,48,256]{2,1,0:T(8,128)S(1)} %collective-permute-done.19.rest_0_), channel_id=1, source_target_pairs={{0,2},{1,3},{2,0},{3,1},{4,6},{5,7},{6,4},{7,5},{8,10},{9,11},{10,... | collective-permute-start | bytes 294920 | tf_op jit(solution)/shard_map/ppermute | solution.py:361
  59.9 0.4 collective-permute-start.20
  60.3 2.3 %shard_map.70 = (f32[48,96]{1,0:T(8,128)S(1)}, f32[48,48]{1,0:T(8,128)S(1)}, f32[32,32,48]{2,1,0:T(8,128)}) custom-call(bf16[2,32,96,128]{3,2,1,0:T(8,128)(2,1)S(1)} %get-tuple-element.18.xh_ref, bf16[2,32,96,128]{3,2,1,0:T(8,128)(2,1)S(1)} %get-tuple-element.19.xl_ref, f32[2,48,256]{2,1,0:T(8,128)S(1)} %pad_maximum_fusion.rest_0_, ...), custom_call_target="tpu_custom_call" | custom-call | tf_op jit(solution)/shard_map/pallas_call | solution.py:301
  62.6 0.5 collective-permute-done.22.rest_3_
  63.2 0.5 collective-permute-done.21.rest_2_
  63.7 0.8 collective-permute-done.20.rest_1_
  64.5 0.5 collective-permute-start.24
  65.0 0.0 collective-permute-start.25
  65.0 0.5 collective-permute-start.26
  65.5 0.3 collective-permute-done.23.rest_4_
  65.8 0.2 collective-permute-done.24.rest_5_
  65.9 0.4 collective-permute-done.25.rest_6_
  66.3 0.2 collective-permute-done.26.rest_7_
  66.5 1.8 %shard_map.71 = f32[48,96]{1,0:T(8,128)S(1)} custom-call(bf16[2,32,96,128]{3,2,1,0:T(8,128)(2,1)S(1)} %get-tuple-element.18.xh_ref, bf16[2,32,96,128]{3,2,1,0:T(8,128)(2,1)S(1)} %get-tuple-element.19.xl_ref, f32[48,768]{1,0:T(8,128)S(1)} %bitcast.26, f32[48,96]{1,0:T(8,128)S(1)} %get-tuple-element.27.numer_ref, f32[48,48]{1,0:T(8,128)S(1)} %get-tuple-element.28.gram_ref, ...), custom_call_target="tpu_custom_call" | custom-call | tf_op jit(solution)/shard_map/pallas_call | solution.py:327
  68.3 0.6 collective-permute-start.27
  68.9 3.3 %collective-permute-done.27 = f32[48,96]{1,0:T(8,128)S(1)} collective-permute-done((f32[48,96]{1,0:T(8,128)S(1)}, f32[48,96]{1,0:T(8,128)S(1)}, u32[]{:S(2)}, u32[]{:S(2)}) %collective-permute-start.27) | collective-permute-done | bytes 18464 | tf_op jit(solution)/shard_map/ppermute | solution.py:361
  72.2 1.6 %collective-permute-start.28 = (f32[2,48,96]{2,1,0:T(8,128)S(1)}, f32[2,48,96]{2,1,0:T(8,128)S(1)}, u32[]{:S(2)}, u32[]{:S(2)}) collective-permute-start(f32[2,48,96]{2,1,0:T(8,128)S(1)} %pad_maximum_fusion.2), channel_id=1, source_target_pairs={{0,8},{1,9},{2,10},{3,11},{4,12},{5,13},{6,14},{7,15},{8,0},{9,1},... | collective-permute-start | bytes 110600 | tf_op jit(solution)/shard_map/ppermute | solution.py:361
  73.8 2.5 %collective-permute-done.28 = f32[2,48,96]{2,1,0:T(8,128)S(1)} collective-permute-done((f32[2,48,96]{2,1,0:T(8,128)S(1)}, f32[2,48,96]{2,1,0:T(8,128)S(1)}, u32[]{:S(2)}, u32[]{:S(2)}) %collective-permute-start.28) | collective-permute-done | bytes 36896 | tf_op jit(solution)/shard_map/ppermute | solution.py:361
  76.4 1.0 %collective-permute-start.29 = (f32[4,48,96]{2,1,0:T(8,128)S(1)}, f32[4,48,96]{2,1,0:T(8,128)S(1)}, u32[]{:S(2)}, u32[]{:S(2)}) collective-permute-start(f32[4,48,96]{2,1,0:T(8,128)S(1)} %pad_maximum_fusion.1.mine_ref), channel_id=1, source_target_pairs={{0,16},{1,17},{2,18},{3,19},{4,20},{5,21},{6,22},{7,23},{8,24},{9,... | collective-permute-start | bytes 221192 | tf_op jit(solution)/shard_map/ppermute | solution.py:361
  77.4 4.6 %collective-permute-done.29.other_ref = f32[4,48,96]{2,1,0:T(8,128)S(1)} collective-permute-done((f32[4,48,96]{2,1,0:T(8,128)S(1)}, f32[4,48,96]{2,1,0:T(8,128)S(1)}, u32[]{:S(2)}, u32[]{:S(2)}) %collective-permute-start.29) | collective-permute-done | bytes 73760 | tf_op jit(solution)/shard_map/ppermute | solution.py:361
  82.0 0.6 copy-done.6
  82.6 1.7 %shard_map.72 = f32[48,768]{1,0:T(8,128)} custom-call(f32[4,48,96]{2,1,0:T(8,128)} %copy-done.4, f32[4,48,96]{2,1,0:T(8,128)} %copy-done.6), custom_call_target="tpu_custom_call" | custom-call | tf_op jit(solution)/shard_map/pallas_call | solution.py:347
  (26 shorter events, 0.1 us)
Async XLA Ops:
  0.6 0.9 %copy-start = (f32[1,768,48]{1,2,0:T(8,128)S(1)}, f32[1,768,48]{1,2,0:T(8,128)}, u32[]{:S(2)}) copy-start(f32[1,768,48]{1,2,0:T(8,128)} %param.8) | copy-start | bytes 442372
  1.5 0.7 copy-start.2
  2.3 0.7 copy-start.3
  15.7 1.9 %collective-permute-start = (f32[8,48,256]{2,1,0:T(8,128)S(1)}, f32[8,48,256]{2,1,0:T(8,128)S(1)}, u32[]{:S(2)}, u32[]{:S(2)}) collective-permute-start(f32[8,48,256]{2,1,0:T(8,128)S(1)} %get-tuple-element.21), channel_id=1, source_target_pairs={{0,1},{1,0},{2,3},{3,2},{4,5},{5,4},{6,7},{7,6},{8,9},{9,8},{10,11... | collective-permute-start | bytes 1179656 | tf_op jit(solution)/shard_map/ppermute | solution.py:361
  16.2 5.9 %collective-permute-start.5 = (f32[9,48,256]{2,1,0:T(8,128)S(1)}, f32[9,48,256]{2,1,0:T(8,128)S(1)}, u32[]{:S(2)}, u32[]{:S(2)}) collective-permute-start(f32[9,48,256]{2,1,0:T(8,128)S(1)} %get-tuple-element.23), channel_id=1, source_target_pairs={{0,1},{1,0},{2,3},{3,2},{4,5},{5,4},{6,7},{7,6},{8,9},{9,8},{10,11... | collective-permute-start | bytes 1327112 | tf_op jit(solution)/shard_map/ppermute | solution.py:361
  17.6 8.6 %collective-permute-start.3 = (f32[2,48,256]{2,1,0:T(8,128)S(1)}, f32[2,48,256]{2,1,0:T(8,128)S(1)}, u32[]{:S(2)}, u32[]{:S(2)}) collective-permute-start(f32[2,48,256]{2,1,0:T(8,128)S(1)} %get-tuple-element.38), channel_id=1, source_target_pairs={{0,6},{1,7},{2,4},{3,5},{4,2},{5,3},{6,0},{7,1},{8,14},{9,15},{10,... | collective-permute-start | bytes 294920 | tf_op jit(solution)/shard_map/ppermute | solution.py:361
  21.5 6.1 %collective-permute-start.2 = (f32[2,48,256]{2,1,0:T(8,128)S(1)}, f32[2,48,256]{2,1,0:T(8,128)S(1)}, u32[]{:S(2)}, u32[]{:S(2)}) collective-permute-start(f32[2,48,256]{2,1,0:T(8,128)S(1)} %get-tuple-element.39), channel_id=1, source_target_pairs={{0,2},{1,3},{2,0},{3,1},{4,6},{5,7},{6,4},{7,5},{8,10},{9,11},{10,... | collective-permute-start | bytes 294920 | tf_op jit(solution)/shard_map/ppermute | solution.py:361
  22.0 5.6 %collective-permute-start.1 = (f32[2,48,256]{2,1,0:T(8,128)S(1)}, f32[2,48,256]{2,1,0:T(8,128)S(1)}, u32[]{:S(2)}, u32[]{:S(2)}) collective-permute-start(f32[2,48,256]{2,1,0:T(8,128)S(1)} %get-tuple-element.40), channel_id=1, source_target_pairs={{0,4},{1,5},{2,6},{3,7},{4,0},{5,1},{6,2},{7,3},{8,12},{9,13},{10,... | collective-permute-start | bytes 294920 | tf_op jit(solution)/shard_map/ppermute | solution.py:361
  22.8 14.8 %collective-permute-start.9 = (f32[2,48,256]{2,1,0:T(8,128)}, f32[2,48,256]{2,1,0:T(8,128)S(1)}, u32[]{:S(2)}, u32[]{:S(2)}) collective-permute-start(f32[2,48,256]{2,1,0:T(8,128)} %get-tuple-element.35), channel_id=1, source_target_pairs={{0,6},{1,7},{2,4},{3,5},{4,2},{5,3},{6,0},{7,1},{8,14},{9,15},{10,... | collective-permute-start | bytes 294920 | tf_op jit(solution)/shard_map/ppermute | solution.py:361
  25.7 12.0 %collective-permute-start.8 = (f32[2,48,256]{2,1,0:T(8,128)}, f32[2,48,256]{2,1,0:T(8,128)S(1)}, u32[]{:S(2)}, u32[]{:S(2)}) collective-permute-start(f32[2,48,256]{2,1,0:T(8,128)} %get-tuple-element.36), channel_id=1, source_target_pairs={{0,2},{1,3},{2,0},{3,1},{4,6},{5,7},{6,4},{7,5},{8,10},{9,11},{10,... | collective-permute-start | bytes 294920 | tf_op jit(solution)/shard_map/ppermute | solution.py:361
  26.2 11.5 %collective-permute-start.7 = (f32[2,48,256]{2,1,0:T(8,128)}, f32[2,48,256]{2,1,0:T(8,128)}, u32[]{:S(2)}, u32[]{:S(2)}) collective-permute-start(f32[2,48,256]{2,1,0:T(8,128)} %get-tuple-element.37), channel_id=1, source_target_pairs={{0,4},{1,5},{2,6},{3,7},{4,0},{5,1},{6,2},{7,3},{8,12},{9,13},{10,... | collective-permute-start | bytes 294920 | tf_op jit(solution)/shard_map/ppermute | solution.py:361
  28.3 9.4 %collective-permute-start.4 = (f32[2,48,256]{2,1,0:T(8,128)}, f32[2,48,256]{2,1,0:T(8,128)}, u32[]{:S(2)}, u32[]{:S(2)}) collective-permute-start(f32[2,48,256]{2,1,0:T(8,128)} %fusion.1), channel_id=1, source_target_pairs={{0,16},{1,17},{2,18},{3,19},{4,20},{5,21},{6,22},{7,23},{8,24},{9,... | collective-permute-start | bytes 294920 | tf_op jit(solution)/shard_map/ppermute | solution.py:361
  31.2 3.8 %copy-start.5 = (f32[48,48]{1,0:T(8,128)}, f32[48,48]{1,0:T(8,128)S(1)}, u32[]{:S(2)}) copy-start(f32[48,48]{1,0:T(8,128)S(1)} %fusion.10.gram_ref) | copy-start | bytes 27652
  31.2 3.8 %collective-permute-start.6 = (f32[48,48]{1,0:T(8,128)S(1)}, f32[48,48]{1,0:T(8,128)S(1)}, u32[]{:S(2)}, u32[]{:S(2)}) collective-permute-start(f32[48,48]{1,0:T(8,128)S(1)} %fusion.10.gram_ref), channel_id=1, source_target_pairs={{0,2},{1,3},{2,0},{3,1},{4,6},{5,7},{6,4},{7,5},{8,10},{9,11},{10,... | collective-permute-start | bytes 27656 | tf_op jit(solution)/shard_map/ppermute | solution.py:361
  35.1 0.6 copy-start.7
  38.5 4.2 %collective-permute-start.10 = (f32[48,256]{1,0:T(8,128)S(1)}, f32[48,256]{1,0:T(8,128)S(1)}, u32[]{:S(2)}, u32[]{:S(2)}) collective-permute-start(f32[48,256]{1,0:T(8,128)S(1)} %fusion.4), channel_id=1, source_target_pairs={{0,8},{1,9},{2,10},{3,11},{4,12},{5,13},{6,14},{7,15},{8,0},{9,1},... | collective-permute-start | bytes 147464 | tf_op jit(solution)/shard_map/ppermute | solution.py:361
  43.5 4.2 %collective-permute-start.11 = (f32[48,256]{1,0:T(8,128)S(1)}, f32[48,256]{1,0:T(8,128)S(1)}, u32[]{:S(2)}, u32[]{:S(2)}) collective-permute-start(f32[48,256]{1,0:T(8,128)S(1)} %fusion.9), channel_id=1, source_target_pairs={{0,8},{1,9},{2,10},{3,11},{4,12},{5,13},{6,14},{7,15},{8,0},{9,1},... | collective-permute-start | bytes 147464 | tf_op jit(solution)/shard_map/ppermute | solution.py:361
  47.7 5.6 %collective-permute-start.14 = (f32[2,48,256]{2,1,0:T(8,128)S(1)}, f32[2,48,256]{2,1,0:T(8,128)S(1)}, u32[]{:S(2)}, u32[]{:S(2)}) collective-permute-start(f32[2,48,256]{2,1,0:T(8,128)S(1)} %pad_maximum_fusion.rest_0_), channel_id=1, source_target_pairs={{0,6},{1,7},{2,4},{3,5},{4,2},{5,3},{6,0},{7,1},{8,14},{9,15},{10,... | collective-permute-start | bytes 294920 | tf_op jit(solution)/shard_map/ppermute | solution.py:361
  49.4 5.0 %collective-permute-start.13 = (f32[2,48,256]{2,1,0:T(8,128)S(1)}, f32[2,48,256]{2,1,0:T(8,128)S(1)}, u32[]{:S(2)}, u32[]{:S(2)}) collective-permute-start(f32[2,48,256]{2,1,0:T(8,128)S(1)} %pad_maximum_fusion.rest_0_), channel_id=1, source_target_pairs={{0,2},{1,3},{2,0},{3,1},{4,6},{5,7},{6,4},{7,5},{8,10},{9,11},{10,... | collective-permute-start | bytes 294920 | tf_op jit(solution)/shard_map/ppermute | solution.py:361
  50.9 4.6 %collective-permute-start.12 = (f32[2,48,256]{2,1,0:T(8,128)S(1)}, f32[2,48,256]{2,1,0:T(8,128)S(1)}, u32[]{:S(2)}, u32[]{:S(2)}) collective-permute-start(f32[2,48,256]{2,1,0:T(8,128)S(1)} %pad_maximum_fusion.rest_0_), channel_id=1, source_target_pairs={{0,4},{1,5},{2,6},{3,7},{4,0},{5,1},{6,2},{7,3},{8,12},{9,13},{10,... | collective-permute-start | bytes 294920 | tf_op jit(solution)/shard_map/ppermute | solution.py:361
  51.3 5.5 %collective-permute-start.19 = (f32[2,48,256]{2,1,0:T(8,128)S(1)}, f32[2,48,256]{2,1,0:T(8,128)S(1)}, u32[]{:S(2)}, u32[]{:S(2)}) collective-permute-start(f32[2,48,256]{2,1,0:T(8,128)S(1)} %pad_maximum_fusion.rest_0_), channel_id=1, source_target_pairs={{0,16},{1,17},{2,18},{3,19},{4,20},{5,21},{6,22},{7,23},{8,24},{9,... | collective-permute-start | bytes 294920 | tf_op jit(solution)/shard_map/ppermute | solution.py:361
  51.7 6.7 %collective-permute-start.15 = (f32[2,48,256]{2,1,0:T(8,128)S(1)}, f32[2,48,256]{2,1,0:T(8,128)S(1)}, u32[]{:S(2)}, u32[]{:S(2)}) collective-permute-start(f32[2,48,256]{2,1,0:T(8,128)S(1)} %pad_maximum_fusion.rest_0_), channel_id=1, source_target_pairs={{0,1},{1,0},{2,3},{3,2},{4,5},{5,4},{6,7},{7,6},{8,9},{9,8},{10,11... | collective-permute-start | bytes 294920 | tf_op jit(solution)/shard_map/ppermute | solution.py:361
  53.3 6.5 %collective-permute-start.18 = (f32[2,48,256]{2,1,0:T(8,128)S(1)}, f32[2,48,256]{2,1,0:T(8,128)S(1)}, u32[]{:S(2)}, u32[]{:S(2)}) collective-permute-start(f32[2,48,256]{2,1,0:T(8,128)S(1)} %collective-permute-done.14.rest_3_), channel_id=1, source_target_pairs={{0,1},{1,0},{2,3},{3,2},{4,5},{5,4},{6,7},{7,6},{8,9},{9,8},{10,11... | collective-permute-start | bytes 294920 | tf_op jit(solution)/shard_map/ppermute | solution.py:361
  54.3 5.9 %collective-permute-start.17 = (f32[2,48,256]{2,1,0:T(8,128)S(1)}, f32[2,48,256]{2,1,0:T(8,128)S(1)}, u32[]{:S(2)}, u32[]{:S(2)}) collective-permute-start(f32[2,48,256]{2,1,0:T(8,128)S(1)} %collective-permute-done.13.rest_2_), channel_id=1, source_target_pairs={{0,1},{1,0},{2,3},{3,2},{4,5},{5,4},{6,7},{7,6},{8,9},{9,8},{10,11... | collective-permute-start | bytes 294920 | tf_op jit(solution)/shard_map/ppermute | solution.py:361
  55.5 4.8 %collective-permute-start.16 = (f32[2,48,256]{2,1,0:T(8,128)S(1)}, f32[2,48,256]{2,1,0:T(8,128)S(1)}, u32[]{:S(2)}, u32[]{:S(2)}) collective-permute-start(f32[2,48,256]{2,1,0:T(8,128)S(1)} %collective-permute-done.12.rest_1_), channel_id=1, source_target_pairs={{0,1},{1,0},{2,3},{3,2},{4,5},{5,4},{6,7},{7,6},{8,9},{9,8},{10,11... | collective-permute-start | bytes 294920 | tf_op jit(solution)/shard_map/ppermute | solution.py:361
  56.8 6.4 %collective-permute-start.22 = (f32[2,48,256]{2,1,0:T(8,128)S(1)}, f32[2,48,256]{2,1,0:T(8,128)S(1)}, u32[]{:S(2)}, u32[]{:S(2)}) collective-permute-start(f32[2,48,256]{2,1,0:T(8,128)S(1)} %collective-permute-done.19.rest_0_), channel_id=1, source_target_pairs={{0,6},{1,7},{2,4},{3,5},{4,2},{5,3},{6,0},{7,1},{8,14},{9,15},{10,... | collective-permute-start | bytes 294920 | tf_op jit(solution)/shard_map/ppermute | solution.py:361
  58.4 5.3 %collective-permute-start.21 = (f32[2,48,256]{2,1,0:T(8,128)S(1)}, f32[2,48,256]{2,1,0:T(8,128)S(1)}, u32[]{:S(2)}, u32[]{:S(2)}) collective-permute-start(f32[2,48,256]{2,1,0:T(8,128)S(1)} %collective-permute-done.19.rest_0_), channel_id=1, source_target_pairs={{0,2},{1,3},{2,0},{3,1},{4,6},{5,7},{6,4},{7,5},{8,10},{9,11},{10,... | collective-permute-start | bytes 294920 | tf_op jit(solution)/shard_map/ppermute | solution.py:361
  59.9 4.6 %collective-permute-start.20 = (f32[2,48,256]{2,1,0:T(8,128)S(1)}, f32[2,48,256]{2,1,0:T(8,128)S(1)}, u32[]{:S(2)}, u32[]{:S(2)}) collective-permute-start(f32[2,48,256]{2,1,0:T(8,128)S(1)} %collective-permute-done.19.rest_0_), channel_id=1, source_target_pairs={{0,4},{1,5},{2,6},{3,7},{4,0},{5,1},{6,2},{7,3},{8,12},{9,13},{10,... | collective-permute-start | bytes 294920 | tf_op jit(solution)/shard_map/ppermute | solution.py:361
  60.3 6.2 %copy-start.1 = (f32[1,768,48]{1,2,0:T(8,128)S(1)}, f32[1,768,48]{1,2,0:T(8,128)}, u32[]{:S(2)}) copy-start(f32[1,768,48]{1,2,0:T(8,128)} %param.8) | copy-start | bytes 442372
  64.5 1.3 %collective-permute-start.23 = (f32[2,48,256]{2,1,0:T(8,128)S(1)}, f32[2,48,256]{2,1,0:T(8,128)S(1)}, u32[]{:S(2)}, u32[]{:S(2)}) collective-permute-start(f32[2,48,256]{2,1,0:T(8,128)S(1)} %collective-permute-done.19.rest_0_), channel_id=1, source_target_pairs={{0,1},{1,0},{2,3},{3,2},{4,5},{5,4},{6,7},{7,6},{8,9},{9,8},{10,11... | collective-permute-start | bytes 294920 | tf_op jit(solution)/shard_map/ppermute | solution.py:361
  64.5 1.5 %collective-permute-start.24 = (f32[2,48,256]{2,1,0:T(8,128)S(1)}, f32[2,48,256]{2,1,0:T(8,128)S(1)}, u32[]{:S(2)}, u32[]{:S(2)}) collective-permute-start(f32[2,48,256]{2,1,0:T(8,128)S(1)} %collective-permute-done.20.rest_1_), channel_id=1, source_target_pairs={{0,1},{1,0},{2,3},{3,2},{4,5},{5,4},{6,7},{7,6},{8,9},{9,8},{10,11... | collective-permute-start | bytes 294920 | tf_op jit(solution)/shard_map/ppermute | solution.py:361
  65.0 1.3 %collective-permute-start.25 = (f32[2,48,256]{2,1,0:T(8,128)S(1)}, f32[2,48,256]{2,1,0:T(8,128)S(1)}, u32[]{:S(2)}, u32[]{:S(2)}) collective-permute-start(f32[2,48,256]{2,1,0:T(8,128)S(1)} %collective-permute-done.21.rest_2_), channel_id=1, source_target_pairs={{0,1},{1,0},{2,3},{3,2},{4,5},{5,4},{6,7},{7,6},{8,9},{9,8},{10,11... | collective-permute-start | bytes 294920 | tf_op jit(solution)/shard_map/ppermute | solution.py:361
  65.0 1.5 %collective-permute-start.26 = (f32[2,48,256]{2,1,0:T(8,128)S(1)}, f32[2,48,256]{2,1,0:T(8,128)S(1)}, u32[]{:S(2)}, u32[]{:S(2)}) collective-permute-start(f32[2,48,256]{2,1,0:T(8,128)S(1)} %collective-permute-done.22.rest_3_), channel_id=1, source_target_pairs={{0,1},{1,0},{2,3},{3,2},{4,5},{5,4},{6,7},{7,6},{8,9},{9,8},{10,11... | collective-permute-start | bytes 294920 | tf_op jit(solution)/shard_map/ppermute | solution.py:361
  68.3 3.9 %collective-permute-start.27 = (f32[48,96]{1,0:T(8,128)S(1)}, f32[48,96]{1,0:T(8,128)S(1)}, u32[]{:S(2)}, u32[]{:S(2)}) collective-permute-start(f32[48,96]{1,0:T(8,128)S(1)} %shard_map.71), channel_id=1, source_target_pairs={{0,4},{1,5},{2,6},{3,7},{4,0},{5,1},{6,2},{7,3},{8,12},{9,13},{10,... | collective-permute-start | bytes 55304 | tf_op jit(solution)/shard_map/ppermute | solution.py:361
  72.2 4.2 %collective-permute-start.28 = (f32[2,48,96]{2,1,0:T(8,128)S(1)}, f32[2,48,96]{2,1,0:T(8,128)S(1)}, u32[]{:S(2)}, u32[]{:S(2)}) collective-permute-start(f32[2,48,96]{2,1,0:T(8,128)S(1)} %pad_maximum_fusion.2), channel_id=1, source_target_pairs={{0,8},{1,9},{2,10},{3,11},{4,12},{5,13},{6,14},{7,15},{8,0},{9,1},... | collective-permute-start | bytes 110600 | tf_op jit(solution)/shard_map/ppermute | solution.py:361
  76.4 5.6 %copy-start.4 = (f32[4,48,96]{2,1,0:T(8,128)}, f32[4,48,96]{2,1,0:T(8,128)S(1)}, u32[]{:S(2)}) copy-start(f32[4,48,96]{2,1,0:T(8,128)S(1)} %pad_maximum_fusion.1.mine_ref) | copy-start | bytes 221188
  76.4 5.6 %collective-permute-start.29 = (f32[4,48,96]{2,1,0:T(8,128)S(1)}, f32[4,48,96]{2,1,0:T(8,128)S(1)}, u32[]{:S(2)}, u32[]{:S(2)}) collective-permute-start(f32[4,48,96]{2,1,0:T(8,128)S(1)} %pad_maximum_fusion.1.mine_ref), channel_id=1, source_target_pairs={{0,16},{1,17},{2,18},{3,19},{4,20},{5,21},{6,22},{7,23},{8,24},{9,... | collective-permute-start | bytes 221192 | tf_op jit(solution)/shard_map/ppermute | solution.py:361
  82.0 0.6 copy-start.6

commit v3 on v2

--- a/solution.py
+++ b/solution.py
@@ -106,6 +106,29 @@
     return table(high), table(low)
 
 
+def fold(square):
+    side = square.shape[0]
+    across = 2 * LANES // side
+    blocks = [square[first:first + 8] for first in range(0, side, 8)]
+    blocks += [jnp.zeros_like(blocks[0])] * (2 * across - len(blocks))
+    rest = jnp.zeros((8, 2 * LANES - across * side), F32)
+    return jnp.concatenate(
+        [jnp.concatenate(blocks[first:first + across] + [rest], axis=1) for first in (0, across)], axis=0)
+
+
+def unfold(folded, side):
+    across = 2 * LANES // side
+    blocks = []
+    for block in range(side // 8):
+        row, lane = 8 * (block // across), side * (block % across)
+        blocks.append(folded[row:row + 8, lane:lane + side])
+    return jnp.concatenate(blocks, axis=0)
+
+
+def in_vmem(count):
+    return [pl.BlockSpec(memory_space=pltpu.VMEM)] * count
+
+
 def band_gram(w_rows):
     high, low = split(w_rows)
     rank = w_rows.shape[0]
@@ -121,6 +144,7 @@
     taps = taps_x_ref.shape[0]
     margin = (taps - 1) // 2
     height = cube_ref.shape[1]
+    rank = w_ref.shape[0]
 
     @pl.when(step == 0)
     def _():
@@ -133,9 +157,9 @@
             copy.start()
         for copy in copies:
             copy.wait()
-        gram = band_gram(w_ref[...])
-        near_keep[8] = gram
-        near_give[8] = gram
+        gram = fold(band_gram(w_ref[...])[:, :rank])
+        far_keep[8 * rank:] = gram
+        far_give[8 * rank:] = gram
         normalized_taps(taps_x_ref, True, work_ref, kx_ref)
         normalized_taps(taps_y_ref, False, work_ref, ky_ref)
         kx_ref[...] = pltpu.roll(kx_ref[...], LANES - margin, 1)
@@ -170,7 +194,7 @@
     @pl.when(step == pl.num_programs(0) - 1)
     def _():
         planes = xh_ref.shape[2]
-        rank, band = w_ref.shape
+        band = w_ref.shape[1]
         me_sp = lax.axis_index("sp")
         me_bd = lax.axis_index("bd")
         tall = height // lax.axis_size("bd")
@@ -195,22 +219,26 @@
                 for k in range(4):
                     piece = jnp.concatenate([quarters[0][k], quarters[1][k]], axis=1)
                     rel_sp = lax.bitwise_xor(me_sp, column * 4 + k)
-                    place = (rel_bd // 2) * 4 + (rel_sp % 2) * 2 + (rel_sp // 2) % 2
+                    near_side = rel_sp % 2
+                    if rel_bd // 2:
+                        near_side = 1 - near_side
+                    place = (rel_bd // 2) * 4 + near_side * 2 + (rel_sp // 2) % 2
+                    first = pl.multiple_of(place * rank, 8)
 
                     @pl.when(rel_sp >= 4)
                     def _():
-                        far_ref[place] = piece
+                        far_ref[pl.ds(first, rank)] = piece
 
                     @pl.when(rel_sp < 4)
                     def _():
-                        near_ref[place] = piece
+                        near_ref[pl.ds(first, rank)] = piece
 
 
 def blur_call(cube, taps_x, taps_y, w_rows):
     planes, height, length = cube.shape
     rank = w_rows.shape[0]
-    far = jax.ShapeDtypeStruct((8, rank, 2 * LANES), F32)
-    near = jax.ShapeDtypeStruct((9, rank, 2 * LANES), F32)
+    far = jax.ShapeDtypeStruct((8 * rank + 16, 2 * LANES), F32)
+    near = jax.ShapeDtypeStruct((8 * rank, 2 * LANES), F32)
     image = (2, height, planes, LANES)
     whole = lambda shape: pl.BlockSpec(shape, lambda i: (0,) * len(shape))
     return pl.pallas_call(
@@ -232,7 +260,7 @@
     first = pl.multiple_of(lax.axis_index("bd") * tall, tall)
     here = h_ref[pl.ds(first, tall)]
     here = jnp.transpose(here.reshape(-1, here.shape[2]))
-    gram = gram_ref[...] + other_ref[...]
+    gram = unfold(gram_ref[...] + other_ref[...], here.shape[0])
     out_ref[...] = here / dot_exact(gram, here)
 
 
@@ -242,6 +270,7 @@
     return pl.pallas_call(
         ratio_kernel,
         out_shape=jax.ShapeDtypeStruct((rank, columns), F32),
+        in_specs=in_vmem(3),
     )(gram, gram_other, h_columns)
 
 
@@ -305,6 +334,7 @@
             jax.ShapeDtypeStruct((rank, rank), F32),
             jax.ShapeDtypeStruct((height, wide, rank), F32),
         ],
+        in_specs=in_vmem(len(parts) + 2),
         scratch_shapes=[pltpu.VMEM((16,) + parts[0].shape[1:], F32)],
         compiler_params=pltpu.CompilerParams(vmem_limit_bytes=VMEM_LIMIT),
     )(x_high, x_low, *parts)
@@ -327,28 +357,37 @@
     return pl.pallas_call(
         far_kernel,
         out_shape=jax.ShapeDtypeStruct(numer.shape, F32),
+        in_specs=in_vmem(len(parts) + 5),
         scratch_shapes=[pltpu.VMEM((16,) + parts[0].shape[1:], F32)],
         compiler_params=pltpu.CompilerParams(vmem_limit_bytes=VMEM_LIMIT),
     )(x_high, x_low, w_rows, numer, gram, *parts)
 
 
-def gather_w_kernel(mine_ref, other_ref, out_ref, all_ref):
-    planes = mine_ref.shape[2]
+def gather_w_kernel(*refs):
+    part_refs = refs[:-2]
+    out_ref, all_ref = refs[-2:]
+    planes = out_ref.shape[1] // 8
     me_sp = lax.axis_index("sp")
-    for rel in range(8):
-        part = mine_ref if rel < 4 else other_ref
-        all_ref[lax.bitwise_xor(me_sp, rel), :, 0:planes] = part[rel % 4]
+    rel = 0
+    for part_ref in part_refs:
+        for inner in range(part_ref.shape[0]):
+            all_ref[lax.bitwise_xor(me_sp, RING[rel]), :, 0:planes] = part_ref[inner]
+            rel += 1
     for owner in range(8):
         out_ref[:, owner * planes:(owner + 1) * planes] = all_ref[owner][:, :planes]
 
 
-def gather_w_call(mine, other):
-    _, rank, planes = mine.shape
+RING = (0, 1, 2, 4, 6, 3, 5, 7)
+
+
+def gather_w_call(parts):
+    _, rank, planes = parts[0].shape
     return pl.pallas_call(
         gather_w_kernel,
         out_shape=jax.ShapeDtypeStruct((rank, planes * 8), F32),
+        in_specs=in_vmem(len(parts)),
         scratch_shapes=[pltpu.VMEM((8, rank, LANES), F32)],
-    )(mine, other)
+    )(*parts)
 
 
 def send(value, mask_sp, mask_bd):
@@ -370,34 +409,38 @@
     taps_x = jnp.transpose(taps_x, (2, 0, 1))
     taps_y = jnp.transpose(taps_y, (2, 0, 1))
     h_columns = jnp.transpose(factor_h, (1, 2, 0))
+    rank = w_rows.shape[0]
     x_high, x_low, far_keep, far_give, near_keep, near_give = blur_call(cube[0], taps_x, taps_y, w_rows)
     far_taken = send(far_give, 0, 1)
     near_taken = send(near_give, 0, 1)
-    far = [far_keep[2 * k:2 * k + 2] + far_taken[2 * k:2 * k + 2] for k in range(4)]
-    near = [near_keep[2 * k:2 * k + 2] + near_taken[2 * k:2 * k + 2] for k in range(4)]
-    rank = w_rows.shape[0]
-    gram = near_keep[8, :, :rank] + near_taken[8, :, :rank]
-    gram_other = send(gram, 0, 2)
+    spans = [(0, 2), (2, 4), (6, 8), (4, 6)]
+    rows = [(first * rank, last * rank) for first, last in spans]
+    near = [near_keep[first:last] + near_taken[first:last] for first, last in rows]
+    rows[2] = (rows[2][0], far_keep.shape[0])
+    far = [far_keep[first:last] + far_taken[first:last] for first, last in rows]
+    gram = far[2][2 * rank:]
     far_round = around(far)
     near_round = around(near)
-    far_sum = (far[0] + far_round[0]) + (far_round[1] + far_round[2])
-    ratio = ratio_call(gram, gram_other, h_columns)
-    far_other = send(far_sum, 4, 0)
-    far_other, ratio = lax.optimization_barrier((far_other, ratio))
-    line = [(near[0][k] + near_round[0][k]) + (near_round[1][k] + near_round[2][k]) + far_other[k] for k in range(2)]
-    h_piece = ratio * (line[0] + send(line[1], 2, 0))
+    ratio = ratio_call(gram, far_round[1][2 * rank:], h_columns)
+
+    def total(first, others, k):
+        part = slice(k * rank, (k + 1) * rank)
+        return (first[part] + others[0][part]) + (others[1][part] + others[2][part])
+
+    across = [send(total(far[0], far_round, 0), 4, 0), send(total(far[0], far_round, 1), 6, 0)]
+    along = send(total(near[0], near_round, 1), 2, 0)
+    h_piece = ratio * ((total(near[0], near_round, 0) + along) + (across[0] + across[1]))
     h_near = jnp.stack([h_piece, send(h_piece, 2, 0)])
-    h_far = send(h_near, 4, 0)
+    h_far = jnp.stack([send(h_piece, 4, 0), send(h_piece, 6, 0)])
     near_parts = [h_near] + around([h_near] * 4)
     near_parts = near_parts + [send(value, 0, 1) for value in near_parts]
     numer, gram_h, h_next = near_call(x_high, x_low, near_parts)
     far_parts = [h_far] + around([h_far] * 4)
     numer, *far_parts = lax.optimization_barrier((numer, *far_parts))
     far_parts = far_parts + [send(value, 0, 1) for value in far_parts]
-    w_piece = far_call(x_high, x_low, w_rows, numer, gram_h, far_parts)
-    w_two = jnp.stack([w_piece, send(w_piece, 1, 0)])
-    w_four = jnp.concatenate([w_two, send(w_two, 2, 0)])
-    w_next = gather_w_call(w_four, send(w_four, 4, 0))
+    w_piece = far_call(x_high, x_low, w_rows, numer, gram_h, far_parts)[None]
+    w_line = jnp.concatenate([send(w_piece, mask, 0) for mask in (2, 4, 6)])
+    w_next = gather_w_call([w_piece, send(w_piece, 1, 0), w_line, send(w_line, 1, 0)])
     return jnp.transpose(w_next)[None], jnp.transpose(h_next, (2, 0, 1))
 
 

time: 84.8 us -> 83.6 us (0.986)
  waiting for transfers between devices: 27.5 us -> 22.7 us
  starting transfers between devices: 28.8 us -> 32.1 us
  local copies, waits for them, and re-layouts: 3.57 us -> 4.77 us
  other arithmetic: 3.16 us -> 2.31 us
    ppermute x30 -> x33, waiting for transfers between devices: 27.5 us -> 22.7 us  [send(): return lax.ppermute(value, ('sp', 'bd'), pairs)]
    ppermute x30 -> x33, starting transfers between devices: 28.8 us -> 32.1 us  [send(): return lax.ppermute(value, ('sp', 'bd'), pairs)]
    slice x0 -> x2, local copies, waits for them, and re-layouts: none -> 1.22 us  [the longest x1 0.62 us: local(): gram = far[2][2 * rank:]]
    add x5, other arithmetic: 2.26 us -> 1.4 us  [the longest x2 1.3 us: total(): return first[part] + others[0][part] + (others[1][part] + others[2][part])]
    unnamed x16 -> x18, local copies, waits for them, and re-layouts: 3.57 us -> 3.55 us
  transfers between devices with their start and end apart: 30 -> 33, of which waited for: 19 -> 17; matrix products, arithmetic and copies ran while one was open for 2% -> 3% of each run, Pallas kernels for 5% -> 5%
where the time goes in v3:
time: 83.6 us; the launch traced here: 83.2 us
  starting transfers between devices  32.1 us (38%)
  waiting for transfers between devices  22.7 us (27%)
  Pallas kernels  20.6 us (25%)
  local copies, waits for them, and re-layouts  4.77 us (6%)
  other arithmetic  2.31 us (3%)
    ppermute x33, starting transfers between devices, send(): return lax.ppermute(value, ('sp', 'bd'), pairs)  32.1 us
    ppermute x33, waiting for transfers between devices, send(): return lax.ppermute(value, ('sp', 'bd'), pairs)  22.7 us
    pallas_call x1, Pallas kernels, blur_call(): pl.pallas_call(blur_kernel, grid=(planes // GROUP,), out_shape=[jax.Shape...  12.8 us
    unnamed x18, local copies, waits for them, and re-layouts  3.55 us
    pallas_call x1, Pallas kernels, near_call(): pl.pallas_call(near_kernel, out_shape=[jax.ShapeDtypeStruct((rank, planes...  2.33 us
    pallas_call x1, Pallas kernels, ratio_call(): pl.pallas_call(ratio_kernel, out_shape=jax.ShapeDtypeStruct((rank, column...  1.97 us
    pallas_call x1, Pallas kernels, far_call(): pl.pallas_call(far_kernel, out_shape=jax.ShapeDtypeStruct(numer.shape, F3...  1.81 us
    pallas_call x1, Pallas kernels, gather_w_call(): pl.pallas_call(gather_w_kernel, out_shape=jax.ShapeDtypeStruct((rank, pla...  1.74 us
  transfers between devices with their start and end apart: 33, of which 17 were waited for; matrix products, arithmetic and copies ran while one was open for 3% of the time, Pallas kernels for 5%

profile of v3, /device:TPU:0, one launch (start us, length us, event | category | flops | bytes accessed | tf_op | source)
XLA Modules:
  0.0 83.2 jit_solution(2217200433989289858)
XLA Ops:
  0.6 0.0 copy-start
  0.6 0.9 %copy-done = f32[1,768,48]{1,2,0:T(8,128)S(1)} copy-done((f32[1,768,48]{1,2,0:T(8,128)S(1)}, f32[1,768,48]{1,2,0:T(8,128)}, u32[]{:S(2)}) %copy-start) | copy-done | bytes 147480
  1.5 0.7 copy-done.3
  2.3 0.7 copy-done.4
  3.0 12.8 %shard_map.68 = (bf16[2,32,96,128]{3,2,1,0:T(8,128)(2,1)S(1)}, bf16[2,32,96,128]{3,2,1,0:T(8,128)(2,1)S(1)}, f32[400,256]{1,0:T(8,128)S(1)}, f32[400,256]{1,0:T(...) custom-call(f32[96,32,256]{2,1,0:T(8,128)} %bitcast.25, f32[25,1,96]{2,1,0:T(1,128)S(1)} %bitcast.23, ...), custom_call_target="tpu_custom_call" | custom-call | tf_op jit(solution)/shard_map/pallas_call | solution.py:244
  15.7 0.5 collective-permute-start.2
  16.2 0.1 collective-permute-start
  16.3 1.3 %collective-permute-done.2 = f32[384,256]{1,0:T(8,128)S(1)} collective-permute-done((f32[384,256]{1,0:T(8,128)S(1)}, f32[384,256]{1,0:T(8,128)S(1)}, u32[]{:S(2)}, u32[]{:S(2)}) %collective-permute-start.2) | collective-permute-done | bytes 393248 | tf_op jit(solution)/shard_map/ppermute | solution.py:400
  17.6 0.1 slice_add_fusion.7
  17.7 3.9 %collective-permute-start.5 = (f32[96,256]{1,0:T(8,128)S(1)}, f32[96,256]{1,0:T(8,128)S(1)}, u32[]{:S(2)}, u32[]{:S(2)}) collective-permute-start(f32[96,256]{1,0:T(8,128)S(1)} %get-tuple-element.34), channel_id=1, source_target_pairs={{0,6},{1,7},{2,4},{3,5},{4,2},{5,3},{6,0},{7,1},{8,14},{9,15},{10,... | collective-permute-start | bytes 294920 | tf_op jit(solution)/shard_map/ppermute | solution.py:400
  21.5 0.5 collective-permute-start.4
  22.0 0.1 collective-permute-start.3
  22.2 2.9 %collective-permute-start.8 = (f32[96,256]{1,0:T(8,128)S(1)}, f32[96,256]{1,0:T(8,128)S(1)}, u32[]{:S(2)}, u32[]{:S(2)}) collective-permute-start(f32[96,256]{1,0:T(8,128)S(1)} %get-tuple-element.31), channel_id=1, source_target_pairs={{0,6},{1,7},{2,4},{3,5},{4,2},{5,3},{6,0},{7,1},{8,14},{9,15},{10,... | collective-permute-start | bytes 294920 | tf_op jit(solution)/shard_map/ppermute | solution.py:400
  25.1 0.5 collective-permute-start.7
  25.7 1.4 %collective-permute-start.1 = (f32[112,256]{1,0:T(8,128)S(1)}, f32[112,256]{1,0:T(8,128)S(1)}, u32[]{:S(2)}, u32[]{:S(2)}) collective-permute-start(f32[112,256]{1,0:T(8,128)S(1)} %slice_add_fusion), channel_id=1, source_target_pairs={{0,2},{1,3},{2,0},{3,1},{4,6},{5,7},{6,4},{7,5},{8,10},{9,11},{10,... | collective-permute-start | bytes 344072 | tf_op jit(solution)/shard_map/ppermute | solution.py:400
  27.1 0.9 %collective-permute-done.4 = f32[96,256]{1,0:T(8,128)S(1)} collective-permute-done((f32[96,256]{1,0:T(8,128)S(1)}, f32[96,256]{1,0:T(8,128)S(1)}, u32[]{:S(2)}, u32[]{:S(2)}) %collective-permute-start.4) | collective-permute-done | bytes 98336 | tf_op jit(solution)/shard_map/ppermute | solution.py:400
  28.0 0.6 fusion.2
  28.6 1.8 %collective-permute-start.6 = (f32[48,256]{1,0:T(8,128)}, f32[48,256]{1,0:T(8,128)}, u32[]{:S(2)}, u32[]{:S(2)}) collective-permute-start(f32[48,256]{1,0:T(8,128)} %fusion.2), channel_id=1, source_target_pairs={{0,8},{1,9},{2,10},{3,11},{4,12},{5,13},{6,14},{7,15},{8,0},{9,1},... | collective-permute-start | bytes 147464 | tf_op jit(solution)/shard_map/ppermute | solution.py:400
  30.5 0.1 collective-permute-done.8
  30.5 0.7 collective-permute-done.7
  31.2 0.1 collective-permute-done.1
  31.3 0.7 fusion
  32.0 3.8 %collective-permute-start.10 = (f32[48,256]{1,0:T(8,128)}, f32[48,256]{1,0:T(8,128)}, u32[]{:S(2)}, u32[]{:S(2)}) collective-permute-start(f32[48,256]{1,0:T(8,128)} %get-tuple-element.37), channel_id=1, source_target_pairs={{0,24},{1,25},{2,26},{3,27},{4,28},{5,29},{6,30},{7,31},{8,16},{9,... | collective-permute-start | bytes 147464 | tf_op jit(solution)/shard_map/ppermute | solution.py:400
  35.8 0.6 slice.137.gram_ref
  36.4 0.6 slice.138.other_ref
  37.0 2.0 %shard_map.69 = f32[48,256]{1,0:T(8,128)} custom-call(f32[16,256]{1,0:T(8,128)} %slice.137.gram_ref, f32[16,256]{1,0:T(8,128)} %slice.138.other_ref, f32[32,32,48]{2,1,0:T(8,128)} %bitcast.26), custom_call_target="tpu_custom_call" | custom-call | tf_op jit(solution)/shard_map/pallas_call | solution.py:270
  39.0 2.1 %collective-permute-done.9 = f32[48,256]{1,0:T(8,128)} collective-permute-done((f32[48,256]{1,0:T(8,128)}, f32[48,256]{1,0:T(8,128)}, u32[]{:S(2)}, u32[]{:S(2)}) %collective-permute-start.9) | collective-permute-done | bytes 49184 | tf_op jit(solution)/shard_map/ppermute | solution.py:400
  41.1 0.9 %fusion.6 = f32[48,256]{1,0:T(8,128)S(1)} fusion(f32[48,256]{1,0:T(8,128)} %shard_map.69, f32[48,256]{1,0:T(8,128)} %collective-permute-done.6, f32[96,256]{1,0:T(8,128)S(1)} %collective-permute-done.5, f32[96,256]{1,0:T(8,128)S(1)} %collective-permute-done.4, f32[96,256]{1,0:T(8,128)S(1)} %collective-permute-done.3, f32[96,256]{1,0:T(8,128)S(1)} %get-tuple-element.33, ...), kind=kLoop, calls=%fused_computation.23 | loop fusion | flops 86016 | bytes 442368 | tf_op jit(solution)/shard_map/mul | solution.py:432
  42.0 0.1 collective-permute-start.11
  42.0 4.1 %collective-permute-done.11 = f32[48,256]{1,0:T(8,128)S(1)} collective-permute-done((f32[48,256]{1,0:T(8,128)S(1)}, f32[48,256]{1,0:T(8,128)S(1)}, u32[]{:S(2)}, u32[]{:S(2)}) %collective-permute-start.11) | collective-permute-done | bytes 49184 | tf_op jit(solution)/shard_map/ppermute | solution.py:400
  46.1 2.1 %collective-permute-start.14 = (f32[2,48,256]{2,1,0:T(8,128)S(1)}, f32[2,48,256]{2,1,0:T(8,128)S(1)}, u32[]{:S(2)}, u32[]{:S(2)}) collective-permute-start(f32[2,48,256]{2,1,0:T(8,128)S(1)} %pad_maximum_fusion.rest_0_), channel_id=1, source_target_pairs={{0,6},{1,7},{2,4},{3,5},{4,2},{5,3},{6,0},{7,1},{8,14},{9,15},{10,... | collective-permute-start | bytes 294920 | tf_op jit(solution)/shard_map/ppermute | solution.py:400
  48.2 1.0 %collective-permute-start.13 = (f32[2,48,256]{2,1,0:T(8,128)S(1)}, f32[2,48,256]{2,1,0:T(8,128)S(1)}, u32[]{:S(2)}, u32[]{:S(2)}) collective-permute-start(f32[2,48,256]{2,1,0:T(8,128)S(1)} %pad_maximum_fusion.rest_0_), channel_id=1, source_target_pairs={{0,2},{1,3},{2,0},{3,1},{4,6},{5,7},{6,4},{7,5},{8,10},{9,11},{10,... | collective-permute-start | bytes 294920 | tf_op jit(solution)/shard_map/ppermute | solution.py:400
  49.1 0.5 collective-permute-start.12
  49.7 1.6 %collective-permute-start.20 = (f32[48,256]{1,0:T(8,128)S(1)}, f32[48,256]{1,0:T(8,128)S(1)}, u32[]{:S(2)}, u32[]{:S(2)}) collective-permute-start(f32[48,256]{1,0:T(8,128)S(1)} %fusion.6), channel_id=1, source_target_pairs={{0,24},{1,25},{2,26},{3,27},{4,28},{5,29},{6,30},{7,31},{8,16},{9,... | collective-permute-start | bytes 147464 | tf_op jit(solution)/shard_map/ppermute | solution.py:400
  51.3 4.3 %collective-permute-done.20 = f32[48,256]{1,0:T(8,128)S(1)} collective-permute-done((f32[48,256]{1,0:T(8,128)S(1)}, f32[48,256]{1,0:T(8,128)S(1)}, u32[]{:S(2)}, u32[]{:S(2)}) %collective-permute-start.20) | collective-permute-done | bytes 49184 | tf_op jit(solution)/shard_map/ppermute | solution.py:400
  55.6 0.5 collective-permute-start.18
  56.1 0.1 collective-permute-start.17
  56.2 0.4 collective-permute-start.16
  56.6 0.0 collective-permute-done.19
  56.6 2.1 %collective-permute-start.23 = (f32[2,48,256]{2,1,0:T(8,128)S(1)}, f32[2,48,256]{2,1,0:T(8,128)S(1)}, u32[]{:S(2)}, u32[]{:S(2)}) collective-permute-start(f32[2,48,256]{2,1,0:T(8,128)S(1)} %pad_maximum_fusion.1.rest_0_), channel_id=1, source_target_pairs={{0,6},{1,7},{2,4},{3,5},{4,2},{5,3},{6,0},{7,1},{8,14},{9,15},{10,... | collective-permute-start | bytes 294920 | tf_op jit(solution)/shard_map/ppermute | solution.py:400
  58.7 1.0 %collective-permute-start.22 = (f32[2,48,256]{2,1,0:T(8,128)S(1)}, f32[2,48,256]{2,1,0:T(8,128)S(1)}, u32[]{:S(2)}, u32[]{:S(2)}) collective-permute-start(f32[2,48,256]{2,1,0:T(8,128)S(1)} %pad_maximum_fusion.1.rest_0_), channel_id=1, source_target_pairs={{0,2},{1,3},{2,0},{3,1},{4,6},{5,7},{6,4},{7,5},{8,10},{9,11},{10,... | collective-permute-start | bytes 294920 | tf_op jit(solution)/shard_map/ppermute | solution.py:400
  59.7 0.5 collective-permute-start.21
  60.2 2.3 %shard_map.70 = (f32[48,96]{1,0:T(8,128)S(1)}, f32[48,48]{1,0:T(8,128)S(1)}, f32[32,32,48]{2,1,0:T(8,128)}) custom-call(bf16[2,32,96,128]{3,2,1,0:T(8,128)(2,1)S(1)} %get-tuple-element.16.xh_ref, bf16[2,32,96,128]{3,2,1,0:T(8,128)(2,1)S(1)} %get-tuple-element.17.xl_ref, f32[2,48,256]{2,1,0:T(8,128)S(1)} %pad_maximum_fusion.rest_0_, ...), custom_call_target="tpu_custom_call" | custom-call | tf_op jit(solution)/shard_map/pallas_call | solution.py:330
  62.5 1.9 %collective-permute-done.22.rest_2_ = f32[2,48,256]{2,1,0:T(8,128)S(1)} collective-permute-done((f32[2,48,256]{2,1,0:T(8,128)S(1)}, f32[2,48,256]{2,1,0:T(8,128)S(1)}, u32[]{:S(2)}, u32[]{:S(2)}) %collective-permute-start.22) | collective-permute-done | bytes 98336 | tf_op jit(solution)/shard_map/ppermute | solution.py:400
  64.5 0.1 collective-permute-done.21.rest_1_
  64.5 0.5 collective-permute-start.25
  65.0 0.0 collective-permute-start.26
  65.0 0.5 collective-permute-start.27
  65.5 0.3 collective-permute-done.24.rest_4_
  65.8 0.2 collective-permute-done.25.rest_5_
  66.0 0.4 collective-permute-done.26.rest_6_
  66.3 0.2 collective-permute-done.27.rest_7_
  66.5 1.8 %shard_map.71 = f32[48,96]{1,0:T(8,128)S(1)} custom-call(bf16[2,32,96,128]{3,2,1,0:T(8,128)(2,1)S(1)} %get-tuple-element.16.xh_ref, bf16[2,32,96,128]{3,2,1,0:T(8,128)(2,1)S(1)} %get-tuple-element.17.xl_ref, f32[48,768]{1,0:T(8,128)S(1)} %bitcast.17, f32[48,96]{1,0:T(8,128)S(1)} %get-tuple-element.23.numer_ref, f32[48,48]{1,0:T(8,128)S(1)} %get-tuple-element.24.gram_ref, ...), custom_call_target="tpu_custom_call" | custom-call | tf_op jit(solution)/shard_map/pallas_call | solution.py:357
  68.3 0.1 collective-permute-start.29
  68.4 1.9 %collective-permute-start.31 = (f32[1,48,96]{2,1,0:T(8,128)S(1)}, f32[1,48,96]{2,1,0:T(8,128)S(1)}, u32[]{:S(2)}, u32[]{:S(2)}) collective-permute-start(f32[1,48,96]{2,1,0:T(8,128)S(1)} %bitcast.19), channel_id=1, source_target_pairs={{0,24},{1,25},{2,26},{3,27},{4,28},{5,29},{6,30},{7,31},{8,16},{9,... | collective-permute-start | bytes 55304 | tf_op jit(solution)/shard_map/ppermute | solution.py:400
  70.3 1.6 %collective-permute-start.30 = (f32[1,48,96]{2,1,0:T(8,128)S(1)}, f32[1,48,96]{2,1,0:T(8,128)S(1)}, u32[]{:S(2)}, u32[]{:S(2)}) collective-permute-start(f32[1,48,96]{2,1,0:T(8,128)S(1)} %bitcast.20), channel_id=1, source_target_pairs={{0,16},{1,17},{2,18},{3,19},{4,20},{5,21},{6,22},{7,23},{8,24},{9,... | collective-permute-start | bytes 55304 | tf_op jit(solution)/shard_map/ppermute | solution.py:400
  71.9 0.3 collective-permute-done.29
  72.2 2.8 %collective-permute-done.30 = f32[1,48,96]{2,1,0:T(8,128)S(1)} collective-permute-done((f32[1,48,96]{2,1,0:T(8,128)S(1)}, f32[1,48,96]{2,1,0:T(8,128)S(1)}, u32[]{:S(2)}, u32[]{:S(2)}) %collective-permute-start.30) | collective-permute-done | bytes 18464 | tf_op jit(solution)/shard_map/ppermute | solution.py:400
  75.1 1.3 %collective-permute-start.32 = (f32[3,48,96]{2,1,0:T(8,128)S(1)}, f32[3,48,96]{2,1,0:T(8,128)S(1)}, u32[]{:S(2)}, u32[]{:S(2)}) collective-permute-start(f32[3,48,96]{2,1,0:T(8,128)S(1)} %constant_dynamic-update-slice_fusion.refs_2_), channel_id=1, source_target_pairs={{0,4},{1,5},{2,6},{3,7},{4,0},{5,1},{6,2},{7,3},{8,12},{9,13},{10,... | collective-permute-start | bytes 165896 | tf_op jit(solution)/shard_map/ppermute | solution.py:400
  76.4 0.8 collective-permute-start.28
  77.1 3.1 %collective-permute-done.28.refs_1_ = f32[1,48,96]{2,1,0:T(8,128)S(1)} collective-permute-done((f32[1,48,96]{2,1,0:T(8,128)S(1)}, f32[1,48,96]{2,1,0:T(8,128)S(1)}, u32[]{:S(2)}, u32[]{:S(2)}) %collective-permute-start.28) | collective-permute-done | bytes 18464 | tf_op jit(solution)/shard_map/ppermute | solution.py:400
  80.2 0.6 copy-done.7
  80.8 0.6 copy-done.6
  81.4 1.7 %shard_map.72 = f32[48,768]{1,0:T(8,128)} custom-call(f32[1,48,96]{2,1,0:T(8,128)} %bitcast.22, f32[1,48,96]{2,1,0:T(8,128)} %copy-done.7, f32[3,48,96]{2,1,0:T(8,128)} %copy-done.5, f32[3,48,96]{2,1,0:T(8,128)} %copy-done.6), custom_call_target="tpu_custom_call" | custom-call | tf_op jit(solution)/shard_map/pallas_call | solution.py:385
  (36 shorter events, 0.1 us)
Async XLA Ops:
  0.6 0.9 %copy-start = (f32[1,768,48]{1,2,0:T(8,128)S(1)}, f32[1,768,48]{1,2,0:T(8,128)}, u32[]{:S(2)}) copy-start(f32[1,768,48]{1,2,0:T(8,128)} %param.8) | copy-start | bytes 442372
  1.5 0.7 copy-start.3
  2.3 0.7 copy-start.4
  15.7 1.9 %collective-permute-start.2 = (f32[384,256]{1,0:T(8,128)S(1)}, f32[384,256]{1,0:T(8,128)S(1)}, u32[]{:S(2)}, u32[]{:S(2)}) collective-permute-start(f32[384,256]{1,0:T(8,128)S(1)} %get-tuple-element.21), channel_id=1, source_target_pairs={{0,1},{1,0},{2,3},{3,2},{4,5},{5,4},{6,7},{7,6},{8,9},{9,8},{10,11... | collective-permute-start | bytes 1179656 | tf_op jit(solution)/shard_map/ppermute | solution.py:400
  16.2 5.9 %collective-permute-start = (f32[400,256]{1,0:T(8,128)S(1)}, f32[400,256]{1,0:T(8,128)S(1)}, u32[]{:S(2)}, u32[]{:S(2)}) collective-permute-start(f32[400,256]{1,0:T(8,128)S(1)} %get-tuple-element.19), channel_id=1, source_target_pairs={{0,1},{1,0},{2,3},{3,2},{4,5},{5,4},{6,7},{7,6},{8,9},{9,8},{10,11... | collective-permute-start | bytes 1228808 | tf_op jit(solution)/shard_map/ppermute | solution.py:400
  17.7 8.0 %collective-permute-start.5 = (f32[96,256]{1,0:T(8,128)S(1)}, f32[96,256]{1,0:T(8,128)S(1)}, u32[]{:S(2)}, u32[]{:S(2)}) collective-permute-start(f32[96,256]{1,0:T(8,128)S(1)} %get-tuple-element.34), channel_id=1, source_target_pairs={{0,6},{1,7},{2,4},{3,5},{4,2},{5,3},{6,0},{7,1},{8,14},{9,15},{10,... | collective-permute-start | bytes 294920 | tf_op jit(solution)/shard_map/ppermute | solution.py:400
  21.5 6.5 %collective-permute-start.4 = (f32[96,256]{1,0:T(8,128)S(1)}, f32[96,256]{1,0:T(8,128)S(1)}, u32[]{:S(2)}, u32[]{:S(2)}) collective-permute-start(f32[96,256]{1,0:T(8,128)S(1)} %get-tuple-element.35), channel_id=1, source_target_pairs={{0,2},{1,3},{2,0},{3,1},{4,6},{5,7},{6,4},{7,5},{8,10},{9,11},{10,... | collective-permute-start | bytes 294920 | tf_op jit(solution)/shard_map/ppermute | solution.py:400
  22.0 6.0 %collective-permute-start.3 = (f32[96,256]{1,0:T(8,128)S(1)}, f32[96,256]{1,0:T(8,128)S(1)}, u32[]{:S(2)}, u32[]{:S(2)}) collective-permute-start(f32[96,256]{1,0:T(8,128)S(1)} %get-tuple-element.36), channel_id=1, source_target_pairs={{0,4},{1,5},{2,6},{3,7},{4,0},{5,1},{6,2},{7,3},{8,12},{9,13},{10,... | collective-permute-start | bytes 294920 | tf_op jit(solution)/shard_map/ppermute | solution.py:400
  22.2 8.3 %collective-permute-start.8 = (f32[96,256]{1,0:T(8,128)S(1)}, f32[96,256]{1,0:T(8,128)S(1)}, u32[]{:S(2)}, u32[]{:S(2)}) collective-permute-start(f32[96,256]{1,0:T(8,128)S(1)} %get-tuple-element.31), channel_id=1, source_target_pairs={{0,6},{1,7},{2,4},{3,5},{4,2},{5,3},{6,0},{7,1},{8,14},{9,15},{10,... | collective-permute-start | bytes 294920 | tf_op jit(solution)/shard_map/ppermute | solution.py:400
  25.1 6.1 %collective-permute-start.7 = (f32[96,256]{1,0:T(8,128)S(1)}, f32[96,256]{1,0:T(8,128)S(1)}, u32[]{:S(2)}, u32[]{:S(2)}) collective-permute-start(f32[96,256]{1,0:T(8,128)S(1)} %get-tuple-element.32), channel_id=1, source_target_pairs={{0,4},{1,5},{2,6},{3,7},{4,0},{5,1},{6,2},{7,3},{8,12},{9,13},{10,... | collective-permute-start | bytes 294920 | tf_op jit(solution)/shard_map/ppermute | solution.py:400
  25.7 5.6 %collective-permute-start.1 = (f32[112,256]{1,0:T(8,128)S(1)}, f32[112,256]{1,0:T(8,128)S(1)}, u32[]{:S(2)}, u32[]{:S(2)}) collective-permute-start(f32[112,256]{1,0:T(8,128)S(1)} %slice_add_fusion), channel_id=1, source_target_pairs={{0,2},{1,3},{2,0},{3,1},{4,6},{5,7},{6,4},{7,5},{8,10},{9,11},{10,... | collective-permute-start | bytes 344072 | tf_op jit(solution)/shard_map/ppermute | solution.py:400
  28.6 10.3 %collective-permute-start.6 = (f32[48,256]{1,0:T(8,128)}, f32[48,256]{1,0:T(8,128)}, u32[]{:S(2)}, u32[]{:S(2)}) collective-permute-start(f32[48,256]{1,0:T(8,128)} %fusion.2), channel_id=1, source_target_pairs={{0,8},{1,9},{2,10},{3,11},{4,12},{5,13},{6,14},{7,15},{8,0},{9,1},... | collective-permute-start | bytes 147464 | tf_op jit(solution)/shard_map/ppermute | solution.py:400
  32.0 7.0 %collective-permute-start.10 = (f32[48,256]{1,0:T(8,128)}, f32[48,256]{1,0:T(8,128)}, u32[]{:S(2)}, u32[]{:S(2)}) collective-permute-start(f32[48,256]{1,0:T(8,128)} %get-tuple-element.37), channel_id=1, source_target_pairs={{0,24},{1,25},{2,26},{3,27},{4,28},{5,29},{6,30},{7,31},{8,16},{9,... | collective-permute-start | bytes 147464 | tf_op jit(solution)/shard_map/ppermute | solution.py:400
  35.8 5.3 %collective-permute-start.9 = (f32[48,256]{1,0:T(8,128)}, f32[48,256]{1,0:T(8,128)}, u32[]{:S(2)}, u32[]{:S(2)}) collective-permute-start(f32[48,256]{1,0:T(8,128)} %get-tuple-element.38), channel_id=1, source_target_pairs={{0,16},{1,17},{2,18},{3,19},{4,20},{5,21},{6,22},{7,23},{8,24},{9,... | collective-permute-start | bytes 147464 | tf_op jit(solution)/shard_map/ppermute | solution.py:400
  42.0 4.2 %collective-permute-start.11 = (f32[48,256]{1,0:T(8,128)S(1)}, f32[48,256]{1,0:T(8,128)S(1)}, u32[]{:S(2)}, u32[]{:S(2)}) collective-permute-start(f32[48,256]{1,0:T(8,128)S(1)} %fusion.6), channel_id=1, source_target_pairs={{0,8},{1,9},{2,10},{3,11},{4,12},{5,13},{6,14},{7,15},{8,0},{9,1},... | collective-permute-start | bytes 147464 | tf_op jit(solution)/shard_map/ppermute | solution.py:400
  46.1 9.4 %collective-permute-start.14 = (f32[2,48,256]{2,1,0:T(8,128)S(1)}, f32[2,48,256]{2,1,0:T(8,128)S(1)}, u32[]{:S(2)}, u32[]{:S(2)}) collective-permute-start(f32[2,48,256]{2,1,0:T(8,128)S(1)} %pad_maximum_fusion.rest_0_), channel_id=1, source_target_pairs={{0,6},{1,7},{2,4},{3,5},{4,2},{5,3},{6,0},{7,1},{8,14},{9,15},{10,... | collective-permute-start | bytes 294920 | tf_op jit(solution)/shard_map/ppermute | solution.py:400
  48.2 7.9 %collective-permute-start.13 = (f32[2,48,256]{2,1,0:T(8,128)S(1)}, f32[2,48,256]{2,1,0:T(8,128)S(1)}, u32[]{:S(2)}, u32[]{:S(2)}) collective-permute-start(f32[2,48,256]{2,1,0:T(8,128)S(1)} %pad_maximum_fusion.rest_0_), channel_id=1, source_target_pairs={{0,2},{1,3},{2,0},{3,1},{4,6},{5,7},{6,4},{7,5},{8,10},{9,11},{10,... | collective-permute-start | bytes 294920 | tf_op jit(solution)/shard_map/ppermute | solution.py:400
  49.1 7.0 %collective-permute-start.12 = (f32[2,48,256]{2,1,0:T(8,128)S(1)}, f32[2,48,256]{2,1,0:T(8,128)S(1)}, u32[]{:S(2)}, u32[]{:S(2)}) collective-permute-start(f32[2,48,256]{2,1,0:T(8,128)S(1)} %pad_maximum_fusion.rest_0_), channel_id=1, source_target_pairs={{0,4},{1,5},{2,6},{3,7},{4,0},{5,1},{6,2},{7,3},{8,12},{9,13},{10,... | collective-permute-start | bytes 294920 | tf_op jit(solution)/shard_map/ppermute | solution.py:400
  49.7 5.9 %collective-permute-start.20 = (f32[48,256]{1,0:T(8,128)S(1)}, f32[48,256]{1,0:T(8,128)S(1)}, u32[]{:S(2)}, u32[]{:S(2)}) collective-permute-start(f32[48,256]{1,0:T(8,128)S(1)} %fusion.6), channel_id=1, source_target_pairs={{0,24},{1,25},{2,26},{3,27},{4,28},{5,29},{6,30},{7,31},{8,16},{9,... | collective-permute-start | bytes 147464 | tf_op jit(solution)/shard_map/ppermute | solution.py:400
  51.3 5.3 %collective-permute-start.19 = (f32[48,256]{1,0:T(8,128)S(1)}, f32[48,256]{1,0:T(8,128)S(1)}, u32[]{:S(2)}, u32[]{:S(2)}) collective-permute-start(f32[48,256]{1,0:T(8,128)S(1)} %fusion.6), channel_id=1, source_target_pairs={{0,16},{1,17},{2,18},{3,19},{4,20},{5,21},{6,22},{7,23},{8,24},{9,... | collective-permute-start | bytes 147464 | tf_op jit(solution)/shard_map/ppermute | solution.py:400
  55.6 3.1 %collective-permute-start.15 = (f32[2,48,256]{2,1,0:T(8,128)S(1)}, f32[2,48,256]{2,1,0:T(8,128)S(1)}, u32[]{:S(2)}, u32[]{:S(2)}) collective-permute-start(f32[2,48,256]{2,1,0:T(8,128)S(1)} %pad_maximum_fusion.rest_0_), channel_id=1, source_target_pairs={{0,1},{1,0},{2,3},{3,2},{4,5},{5,4},{6,7},{7,6},{8,9},{9,8},{10,11... | collective-permute-start | bytes 294920 | tf_op jit(solution)/shard_map/ppermute | solution.py:400
  55.6 4.1 %collective-permute-start.18 = (f32[2,48,256]{2,1,0:T(8,128)S(1)}, f32[2,48,256]{2,1,0:T(8,128)S(1)}, u32[]{:S(2)}, u32[]{:S(2)}) collective-permute-start(f32[2,48,256]{2,1,0:T(8,128)S(1)} %collective-permute-done.14.rest_3_), channel_id=1, source_target_pairs={{0,1},{1,0},{2,3},{3,2},{4,5},{5,4},{6,7},{7,6},{8,9},{9,8},{10,11... | collective-permute-start | bytes 294920 | tf_op jit(solution)/shard_map/ppermute | solution.py:400
  56.1 4.1 %collective-permute-start.17 = (f32[2,48,256]{2,1,0:T(8,128)S(1)}, f32[2,48,256]{2,1,0:T(8,128)S(1)}, u32[]{:S(2)}, u32[]{:S(2)}) collective-permute-start(f32[2,48,256]{2,1,0:T(8,128)S(1)} %collective-permute-done.13.rest_2_), channel_id=1, source_target_pairs={{0,1},{1,0},{2,3},{3,2},{4,5},{5,4},{6,7},{7,6},{8,9},{9,8},{10,11... | collective-permute-start | bytes 294920 | tf_op jit(solution)/shard_map/ppermute | solution.py:400
  56.2 4.0 %collective-permute-start.16 = (f32[2,48,256]{2,1,0:T(8,128)S(1)}, f32[2,48,256]{2,1,0:T(8,128)S(1)}, u32[]{:S(2)}, u32[]{:S(2)}) collective-permute-start(f32[2,48,256]{2,1,0:T(8,128)S(1)} %collective-permute-done.12.rest_1_), channel_id=1, source_target_pairs={{0,1},{1,0},{2,3},{3,2},{4,5},{5,4},{6,7},{7,6},{8,9},{9,8},{10,11... | collective-permute-start | bytes 294920 | tf_op jit(solution)/shard_map/ppermute | solution.py:400
  56.6 5.9 %collective-permute-start.23 = (f32[2,48,256]{2,1,0:T(8,128)S(1)}, f32[2,48,256]{2,1,0:T(8,128)S(1)}, u32[]{:S(2)}, u32[]{:S(2)}) collective-permute-start(f32[2,48,256]{2,1,0:T(8,128)S(1)} %pad_maximum_fusion.1.rest_0_), channel_id=1, source_target_pairs={{0,6},{1,7},{2,4},{3,5},{4,2},{5,3},{6,0},{7,1},{8,14},{9,15},{10,... | collective-permute-start | bytes 294920 | tf_op jit(solution)/shard_map/ppermute | solution.py:400
  58.7 5.8 %collective-permute-start.22 = (f32[2,48,256]{2,1,0:T(8,128)S(1)}, f32[2,48,256]{2,1,0:T(8,128)S(1)}, u32[]{:S(2)}, u32[]{:S(2)}) collective-permute-start(f32[2,48,256]{2,1,0:T(8,128)S(1)} %pad_maximum_fusion.1.rest_0_), channel_id=1, source_target_pairs={{0,2},{1,3},{2,0},{3,1},{4,6},{5,7},{6,4},{7,5},{8,10},{9,11},{10,... | collective-permute-start | bytes 294920 | tf_op jit(solution)/shard_map/ppermute | solution.py:400
  59.7 4.9 %collective-permute-start.21 = (f32[2,48,256]{2,1,0:T(8,128)S(1)}, f32[2,48,256]{2,1,0:T(8,128)S(1)}, u32[]{:S(2)}, u32[]{:S(2)}) collective-permute-start(f32[2,48,256]{2,1,0:T(8,128)S(1)} %pad_maximum_fusion.1.rest_0_), channel_id=1, source_target_pairs={{0,4},{1,5},{2,6},{3,7},{4,0},{5,1},{6,2},{7,3},{8,12},{9,13},{10,... | collective-permute-start | bytes 294920 | tf_op jit(solution)/shard_map/ppermute | solution.py:400
  60.2 6.3 %copy-start.1 = (f32[1,768,48]{1,2,0:T(8,128)S(1)}, f32[1,768,48]{1,2,0:T(8,128)}, u32[]{:S(2)}) copy-start(f32[1,768,48]{1,2,0:T(8,128)} %param.8) | copy-start | bytes 442372
  64.5 1.3 %collective-permute-start.24 = (f32[2,48,256]{2,1,0:T(8,128)S(1)}, f32[2,48,256]{2,1,0:T(8,128)S(1)}, u32[]{:S(2)}, u32[]{:S(2)}) collective-permute-start(f32[2,48,256]{2,1,0:T(8,128)S(1)} %pad_maximum_fusion.1.rest_0_), channel_id=1, source_target_pairs={{0,1},{1,0},{2,3},{3,2},{4,5},{5,4},{6,7},{7,6},{8,9},{9,8},{10,11... | collective-permute-start | bytes 294920 | tf_op jit(solution)/shard_map/ppermute | solution.py:400
  64.5 1.5 %collective-permute-start.25 = (f32[2,48,256]{2,1,0:T(8,128)S(1)}, f32[2,48,256]{2,1,0:T(8,128)S(1)}, u32[]{:S(2)}, u32[]{:S(2)}) collective-permute-start(f32[2,48,256]{2,1,0:T(8,128)S(1)} %collective-permute-done.21.rest_1_), channel_id=1, source_target_pairs={{0,1},{1,0},{2,3},{3,2},{4,5},{5,4},{6,7},{7,6},{8,9},{9,8},{10,11... | collective-permute-start | bytes 294920 | tf_op jit(solution)/shard_map/ppermute | solution.py:400
  65.0 1.3 %collective-permute-start.26 = (f32[2,48,256]{2,1,0:T(8,128)S(1)}, f32[2,48,256]{2,1,0:T(8,128)S(1)}, u32[]{:S(2)}, u32[]{:S(2)}) collective-permute-start(f32[2,48,256]{2,1,0:T(8,128)S(1)} %collective-permute-done.22.rest_2_), channel_id=1, source_target_pairs={{0,1},{1,0},{2,3},{3,2},{4,5},{5,4},{6,7},{7,6},{8,9},{9,8},{10,11... | collective-permute-start | bytes 294920 | tf_op jit(solution)/shard_map/ppermute | solution.py:400
  65.0 1.5 %collective-permute-start.27 = (f32[2,48,256]{2,1,0:T(8,128)S(1)}, f32[2,48,256]{2,1,0:T(8,128)S(1)}, u32[]{:S(2)}, u32[]{:S(2)}) collective-permute-start(f32[2,48,256]{2,1,0:T(8,128)S(1)} %collective-permute-done.23.rest_3_), channel_id=1, source_target_pairs={{0,1},{1,0},{2,3},{3,2},{4,5},{5,4},{6,7},{7,6},{8,9},{9,8},{10,11... | collective-permute-start | bytes 294920 | tf_op jit(solution)/shard_map/ppermute | solution.py:400
  68.3 11.9 %copy-start.2 = (f32[48,96]{1,0:T(8,128)}, f32[48,96]{1,0:T(8,128)S(1)}, u32[]{:S(2)}) copy-start(f32[48,96]{1,0:T(8,128)S(1)} %shard_map.71) | copy-start | bytes 55300
  68.3 3.9 %collective-permute-start.29 = (f32[1,48,96]{2,1,0:T(8,128)S(1)}, f32[1,48,96]{2,1,0:T(8,128)S(1)}, u32[]{:S(2)}, u32[]{:S(2)}) collective-permute-start(f32[1,48,96]{2,1,0:T(8,128)S(1)} %bitcast.18), channel_id=1, source_target_pairs={{0,8},{1,9},{2,10},{3,11},{4,12},{5,13},{6,14},{7,15},{8,0},{9,1},... | collective-permute-start | bytes 55304 | tf_op jit(solution)/shard_map/ppermute | solution.py:400
  68.4 6.6 %collective-permute-start.31 = (f32[1,48,96]{2,1,0:T(8,128)S(1)}, f32[1,48,96]{2,1,0:T(8,128)S(1)}, u32[]{:S(2)}, u32[]{:S(2)}) collective-permute-start(f32[1,48,96]{2,1,0:T(8,128)S(1)} %bitcast.19), channel_id=1, source_target_pairs={{0,24},{1,25},{2,26},{3,27},{4,28},{5,29},{6,30},{7,31},{8,16},{9,... | collective-permute-start | bytes 55304 | tf_op jit(solution)/shard_map/ppermute | solution.py:400
  70.3 4.7 %collective-permute-start.30 = (f32[1,48,96]{2,1,0:T(8,128)S(1)}, f32[1,48,96]{2,1,0:T(8,128)S(1)}, u32[]{:S(2)}, u32[]{:S(2)}) collective-permute-start(f32[1,48,96]{2,1,0:T(8,128)S(1)} %bitcast.20), channel_id=1, source_target_pairs={{0,16},{1,17},{2,18},{3,19},{4,20},{5,21},{6,22},{7,23},{8,24},{9,... | collective-permute-start | bytes 55304 | tf_op jit(solution)/shard_map/ppermute | solution.py:400
  75.0 5.2 %copy-start.5 = (f32[3,48,96]{2,1,0:T(8,128)}, f32[3,48,96]{2,1,0:T(8,128)S(1)}, u32[]{:S(2)}) copy-start(f32[3,48,96]{2,1,0:T(8,128)S(1)} %constant_dynamic-update-slice_fusion.refs_2_) | copy-start | bytes 165892
  75.1 5.2 %collective-permute-start.32 = (f32[3,48,96]{2,1,0:T(8,128)S(1)}, f32[3,48,96]{2,1,0:T(8,128)S(1)}, u32[]{:S(2)}, u32[]{:S(2)}) collective-permute-start(f32[3,48,96]{2,1,0:T(8,128)S(1)} %constant_dynamic-update-slice_fusion.refs_2_), channel_id=1, source_target_pairs={{0,4},{1,5},{2,6},{3,7},{4,0},{5,1},{6,2},{7,3},{8,12},{9,13},{10,... | collective-permute-start | bytes 165896 | tf_op jit(solution)/shard_map/ppermute | solution.py:400
  76.4 3.8 %collective-permute-start.28 = (f32[1,48,96]{2,1,0:T(8,128)S(1)}, f32[1,48,96]{2,1,0:T(8,128)S(1)}, u32[]{:S(2)}, u32[]{:S(2)}) collective-permute-start(f32[1,48,96]{2,1,0:T(8,128)S(1)} %bitcast.21), channel_id=1, source_target_pairs={{0,4},{1,5},{2,6},{3,7},{4,0},{5,1},{6,2},{7,3},{8,12},{9,13},{10,... | collective-permute-start | bytes 55304 | tf_op jit(solution)/shard_map/ppermute | solution.py:400
  80.2 0.6 copy-start.7
  80.8 0.6 copy-start.6

commit v4 on v3

--- a/solution.py
+++ b/solution.py
@@ -11,6 +11,8 @@
 BF16 = jnp.bfloat16
 LANES = 128
 GROUP = 16
+PIECES = 16
+FOLDED = 24
 VMEM_LIMIT = 48 * 1024 * 1024
 
 
@@ -108,20 +110,16 @@
 
 def fold(square):
     side = square.shape[0]
-    across = 2 * LANES // side
-    blocks = [square[first:first + 8] for first in range(0, side, 8)]
-    blocks += [jnp.zeros_like(blocks[0])] * (2 * across - len(blocks))
-    rest = jnp.zeros((8, 2 * LANES - across * side), F32)
+    rest = jnp.zeros((8, LANES - 2 * side), F32)
     return jnp.concatenate(
-        [jnp.concatenate(blocks[first:first + across] + [rest], axis=1) for first in (0, across)], axis=0)
+        [jnp.concatenate([square[first:first + 8], square[first + 8:first + 16], rest], axis=1)
+         for first in range(0, side, 16)], axis=0)
 
 
 def unfold(folded, side):
-    across = 2 * LANES // side
     blocks = []
-    for block in range(side // 8):
-        row, lane = 8 * (block // across), side * (block % across)
-        blocks.append(folded[row:row + 8, lane:lane + side])
+    for first in range(0, folded.shape[0], 8):
+        blocks += [folded[first:first + 8, :side], folded[first:first + 8, side:2 * side]]
     return jnp.concatenate(blocks, axis=0)
 
 
@@ -138,7 +136,7 @@
     return both[:rank] + (both[rank:] + dot_nt(high, padded_low))
 
 
-def blur_kernel(cube_ref, taps_x_hbm, taps_y_hbm, w_hbm, xh_ref, xl_ref, far_keep, far_give, near_keep, near_give,
+def blur_kernel(cube_ref, taps_x_hbm, taps_y_hbm, w_hbm, xh_ref, xl_ref, keep_0, give_0, keep_1, give_1,
                 taps_x_ref, taps_y_ref, w_ref, sems, work_ref, kx_ref, ky_ref):
     step = pl.program_id(0)
     taps = taps_x_ref.shape[0]
@@ -158,8 +156,8 @@
         for copy in copies:
             copy.wait()
         gram = fold(band_gram(w_ref[...])[:, :rank])
-        far_keep[8 * rank:] = gram
-        far_give[8 * rank:] = gram
+        keep_0[PIECES * rank:] = gram
+        give_0[PIECES * rank:] = gram
         normalized_taps(taps_x_ref, True, work_ref, kx_ref)
         normalized_taps(taps_y_ref, False, work_ref, ky_ref)
         kx_ref[...] = pltpu.roll(kx_ref[...], LANES - margin, 1)
@@ -187,13 +185,12 @@
         halves.append(result.reshape(height, 8, result.shape[1]))
     high, low = split(jnp.concatenate(halves, axis=1))
     planes_here = pl.ds(pl.multiple_of(step * GROUP, GROUP), GROUP)
-    for column in range(2):
-        xh_ref[column, :, planes_here, :] = high[:, :, column * LANES:(column + 1) * LANES]
-        xl_ref[column, :, planes_here, :] = low[:, :, column * LANES:(column + 1) * LANES]
+    xh_ref[:, planes_here, :] = high
+    xl_ref[:, planes_here, :] = low
 
     @pl.when(step == pl.num_programs(0) - 1)
     def _():
-        planes = xh_ref.shape[2]
+        planes = xh_ref.shape[1]
         band = w_ref.shape[1]
         me_sp = lax.axis_index("sp")
         me_bd = lax.axis_index("bd")
@@ -202,52 +199,38 @@
         shift = lax.rem(band - me_sp * planes, band)
         w_high, w_low = split(pltpu.roll(w_ref[...], shift, 1)[:, :planes])
         w_both = jnp.concatenate([w_high, w_low], axis=0)
-        for rel_bd in range(4):
-            first_row = lax.bitwise_xor(me_bd, rel_bd) * tall
-            sums = []
-            for row in range(tall):
-                x_high = jnp.concatenate([xh_ref[0, first_row + row], xh_ref[1, first_row + row]], axis=1)
-                x_low = jnp.concatenate([xl_ref[0, first_row + row], xl_ref[1, first_row + row]], axis=1)
-                both = dot(w_both, x_high)
-                sums.append(both[:rank] + (both[rank:] + dot(w_high, x_low)))
-            far_ref, near_ref = (far_keep, near_keep) if rel_bd % 2 == 0 else (far_give, near_give)
-            for column in range(2):
-                quarters = [
-                    exchange_blocks(
-                        [sums[4 * quarter + k][:, column * LANES:(column + 1) * LANES] for k in range(4)], wide)
-                    for quarter in range(2)]
-                for k in range(4):
-                    piece = jnp.concatenate([quarters[0][k], quarters[1][k]], axis=1)
-                    rel_sp = lax.bitwise_xor(me_sp, column * 4 + k)
-                    near_side = rel_sp % 2
-                    if rel_bd // 2:
-                        near_side = 1 - near_side
-                    place = (rel_bd // 2) * 4 + near_side * 2 + (rel_sp // 2) % 2
-                    first = pl.multiple_of(place * rank, 8)
-
-                    @pl.when(rel_sp >= 4)
-                    def _():
-                        far_ref[pl.ds(first, rank)] = piece
-
-                    @pl.when(rel_sp < 4)
-                    def _():
-                        near_ref[pl.ds(first, rank)] = piece
+        for chain in range(2):
+            for rel_bd in (1, 3, 0, 2):
+                first_row = lax.bitwise_xor(me_bd, rel_bd) * tall + 4 * chain
+                sums = []
+                for row in range(4):
+                    both = dot(w_both, xh_ref[first_row + row])
+                    sums.append(both[:rank] + (both[rank:] + dot(w_high, xl_ref[first_row + row])))
+                refs = ((keep_0, give_0), (keep_1, give_1))[chain]
+                for column in range(2):
+                    pieces = exchange_blocks(
+                        [value[:, column * LANES:(column + 1) * LANES] for value in sums], wide)
+                    for k in range(4):
+                        rel_sp = lax.bitwise_xor(me_sp, column * 4 + k)
+                        side = 3 - rel_sp % 2 if rel_bd // 2 else rel_sp % 2
+                        first = pl.multiple_of((side * 4 + rel_sp // 2) * rank, 8)
+                        refs[rel_bd % 2][pl.ds(first, rank)] = pieces[k]
 
 
 def blur_call(cube, taps_x, taps_y, w_rows):
     planes, height, length = cube.shape
     rank = w_rows.shape[0]
-    far = jax.ShapeDtypeStruct((8 * rank + 16, 2 * LANES), F32)
-    near = jax.ShapeDtypeStruct((8 * rank, 2 * LANES), F32)
-    image = (2, height, planes, LANES)
+    first = jax.ShapeDtypeStruct((PIECES * rank + FOLDED, LANES), F32)
+    second = jax.ShapeDtypeStruct((PIECES * rank, LANES), F32)
+    image = (height, planes, length)
     whole = lambda shape: pl.BlockSpec(shape, lambda i: (0,) * len(shape))
     return pl.pallas_call(
         blur_kernel,
         grid=(planes // GROUP,),
-        out_shape=[jax.ShapeDtypeStruct(image, BF16)] * 2 + [far, far, near, near],
+        out_shape=[jax.ShapeDtypeStruct(image, BF16)] * 2 + [first, first, second, second],
         in_specs=[pl.BlockSpec((GROUP, height, length), lambda i: (i, 0, 0))]
         + [pl.BlockSpec(memory_space=pltpu.HBM)] * 3,
-        out_specs=[whole(image)] * 2 + [whole(far.shape)] * 2 + [whole(near.shape)] * 2,
+        out_specs=[whole(image)] * 2 + [whole(first.shape)] * 2 + [whole(second.shape)] * 2,
         scratch_shapes=[pltpu.VMEM(value.shape, F32) for value in (taps_x, taps_y, w_rows)]
         + [pltpu.SemaphoreType.DMA((3,))] + [pltpu.VMEM((LANES, LANES), F32)] * 3,
         compiler_params=pltpu.CompilerParams(
@@ -255,112 +238,114 @@
     )(cube, taps_x, taps_y, w_rows)
 
 
-def ratio_kernel(gram_ref, other_ref, h_ref, out_ref):
+def ratio_kernel(mine_ref, other_ref, h_ref, out_0, out_1):
     tall = h_ref.shape[0] // lax.axis_size("bd")
     first = pl.multiple_of(lax.axis_index("bd") * tall, tall)
     here = h_ref[pl.ds(first, tall)]
     here = jnp.transpose(here.reshape(-1, here.shape[2]))
-    gram = unfold(gram_ref[...] + other_ref[...], here.shape[0])
-    out_ref[...] = here / dot_exact(gram, here)
-
-
-def ratio_call(gram, gram_other, h_columns):
-    rank = h_columns.shape[2]
-    columns = h_columns.shape[0] * h_columns.shape[1] // lax.axis_size("bd")
+    rows = mine_ref.shape[0]
+    gram = unfold(mine_ref[rows - FOLDED:rows] + other_ref[rows - FOLDED:rows], here.shape[0])
+    ratio = here / dot_exact(gram, here)
+    out_0[...] = ratio[:, :LANES]
+    out_1[...] = ratio[:, LANES:]
+
+
+def ratio_call(mine, other, h_columns):
+    piece = jax.ShapeDtypeStruct((h_columns.shape[2], LANES), F32)
     return pl.pallas_call(
         ratio_kernel,
-        out_shape=jax.ShapeDtypeStruct((rank, columns), F32),
+        out_shape=[piece, piece],
         in_specs=in_vmem(3),
-    )(gram, gram_other, h_columns)
-
-
-def accumulate(xh_ref, xl_ref, part_refs, all_ref, column, numer, gram):
-    height, rank = xh_ref.shape[1], all_ref.shape[1]
+        compiler_params=pltpu.CompilerParams(vmem_limit_bytes=VMEM_LIMIT),
+    )(mine, other, h_columns)
+
+
+def accumulate(xh_ref, xl_ref, part_refs, all_ref, h_out, chain, numer, gram):
+    height, rank = xh_ref.shape[0], all_ref.shape[1]
     me_sp = lax.axis_index("sp")
     me_bd = lax.axis_index("bd")
     bands = lax.axis_size("bd")
+    pieces = lax.axis_size("sp")
     tall = height // bands
-    wide = 2 * LANES // lax.axis_size("sp")
-    for slot in range(8):
+    wide = 2 * LANES // pieces
+    for slot, part_ref in enumerate(part_refs):
         rel_bd = slot // 4 + 2 * ((slot // 2) % 2)
-        for inner in range(2):
-            owner_sp = lax.bitwise_xor(me_sp, slot % 2 + 2 * inner) % 4
-            all_ref[lax.bitwise_xor(me_bd, rel_bd) * 4 + owner_sp] = part_refs[slot][inner]
+        for inner in range(4):
+            rel_sp = slot % 2 + 2 * inner
+            owner = lax.bitwise_xor(me_bd, rel_bd) * pieces + lax.bitwise_xor(me_sp, rel_sp)
+            all_ref[owner] = part_ref[inner]
     for part in range(bands):
-        rows = []
-        for quarter in range(2):
-            rows += exchange_blocks(
-                [all_ref[part * 4 + k][:, quarter * LANES:(quarter + 1) * LANES] for k in range(4)], wide)
-        for row in range(0, tall, 2):
-            high, low = split(jnp.concatenate([rows[row], rows[row + 1]], axis=1))
+        first_row = part * tall + 4 * chain
+        halves = [
+            exchange_blocks([all_ref[part * pieces + column * 4 + k] for k in range(4)], wide)
+            for column in range(2)]
+        for row in range(4):
+            high, low = split(jnp.concatenate([halves[0][row], halves[1][row]], axis=1))
             both = jnp.concatenate([high, low], axis=0)
-            y = part * tall + row
-            x_high = jnp.concatenate([xh_ref[column, y], xh_ref[column, y + 1]], axis=1)
-            x_low = jnp.concatenate([xl_ref[column, y], xl_ref[column, y + 1]], axis=1)
-            product = dot_nt(both, x_high)
-            numer = numer + (product[:rank] + (product[rank:] + dot_nt(high, x_low)))
+            product = dot_nt(both, xh_ref[first_row + row])
+            numer = numer + (product[:rank] + (product[rank:] + dot_nt(high, xl_ref[first_row + row])))
             product = dot_nt(both, high)
             gram = gram + (product[:rank] + (product[rank:] + dot_nt(high, low)))
+        mine = jnp.transpose(all_ref[part * pieces + me_sp])
+        h_out[first_row:first_row + 4] = mine.reshape(4, wide, rank)
     return numer, gram
 
 
-def near_kernel(xh_ref, xl_ref, *rest):
+def first_kernel(xh_ref, xl_ref, *rest):
     part_refs = rest[:8]
     numer_out, gram_out, h_out, all_ref = rest[8:]
-    planes = xh_ref.shape[2]
-    rank = all_ref.shape[1]
-    bands = lax.axis_size("bd")
-    tall = xh_ref.shape[1] // bands
-    wide = 2 * LANES // lax.axis_size("sp")
-    me_sp = lax.axis_index("sp")
+    planes, rank = xh_ref.shape[1], all_ref.shape[1]
     numer, gram = accumulate(
-        xh_ref, xl_ref, part_refs, all_ref, me_sp // 4,
+        xh_ref, xl_ref, part_refs, all_ref, h_out, 0,
         jnp.zeros((rank, planes), F32), jnp.zeros((rank, rank), F32))
     numer_out[...] = numer
     gram_out[...] = gram
-    for part in range(bands):
-        mine = jnp.transpose(all_ref[part * 4 + me_sp % 4])
-        h_out[part * tall:(part + 1) * tall] = mine.reshape(tall, wide, rank)
-
-
-def near_call(x_high, x_low, parts):
-    _, height, planes, _ = x_high.shape
+    tall = xh_ref.shape[0] // lax.axis_size("bd")
+    for part in range(lax.axis_size("bd")):
+        h_out[part * tall + 4:(part + 1) * tall] = jnp.zeros((tall - 4,) + h_out.shape[1:], F32)
+
+
+def first_call(x_high, x_low, parts):
+    height, planes, length = x_high.shape
     rank = parts[0].shape[1]
-    wide = 2 * LANES // lax.axis_size("sp")
     return pl.pallas_call(
-        near_kernel,
+        first_kernel,
         out_shape=[
             jax.ShapeDtypeStruct((rank, planes), F32),
             jax.ShapeDtypeStruct((rank, rank), F32),
-            jax.ShapeDtypeStruct((height, wide, rank), F32),
+            jax.ShapeDtypeStruct((height, length // lax.axis_size("sp"), rank), F32),
         ],
-        in_specs=in_vmem(len(parts) + 2),
-        scratch_shapes=[pltpu.VMEM((16,) + parts[0].shape[1:], F32)],
+        in_specs=in_vmem(2 + len(parts)),
+        scratch_shapes=[pltpu.VMEM((32,) + parts[0].shape[1:], F32)],
         compiler_params=pltpu.CompilerParams(vmem_limit_bytes=VMEM_LIMIT),
     )(x_high, x_low, *parts)
 
 
-def far_kernel(xh_ref, xl_ref, w_ref, numer_ref, gram_ref, *rest):
+def second_kernel(xh_ref, xl_ref, w_ref, numer_ref, gram_ref, h_ref, *rest):
     part_refs = rest[:8]
-    w_out, all_ref = rest[8:]
-    planes = xh_ref.shape[2]
+    w_out, h_out, all_ref = rest[8:]
+    planes = xh_ref.shape[1]
     band = w_ref.shape[1]
     me_sp = lax.axis_index("sp")
+    h_out[...] = h_ref[...]
     numer, gram = accumulate(
-        xh_ref, xl_ref, part_refs, all_ref, 1 - me_sp // 4, numer_ref[...], gram_ref[...])
+        xh_ref, xl_ref, part_refs, all_ref, h_out, 1, numer_ref[...], gram_ref[...])
     shift = lax.rem(band - me_sp * planes, band)
     w_here = pltpu.roll(w_ref[...], shift, 1)[:, :planes]
     w_out[...] = w_here * numer / dot_exact(gram, w_here)
 
 
-def far_call(x_high, x_low, w_rows, numer, gram, parts):
+def second_call(x_high, x_low, w_rows, numer, gram, h_half, parts):
     return pl.pallas_call(
-        far_kernel,
-        out_shape=jax.ShapeDtypeStruct(numer.shape, F32),
-        in_specs=in_vmem(len(parts) + 5),
-        scratch_shapes=[pltpu.VMEM((16,) + parts[0].shape[1:], F32)],
+        second_kernel,
+        out_shape=[
+            jax.ShapeDtypeStruct(numer.shape, F32),
+            jax.ShapeDtypeStruct(h_half.shape, F32),
+        ],
+        in_specs=in_vmem(6 + len(parts)),
+        scratch_shapes=[pltpu.VMEM((32,) + parts[0].shape[1:], F32)],
         compiler_params=pltpu.CompilerParams(vmem_limit_bytes=VMEM_LIMIT),
-    )(x_high, x_low, w_rows, numer, gram, *parts)
+    )(x_high, x_low, w_rows, numer, gram, h_half, *parts)
 
 
 def gather_w_kernel(*refs):
@@ -387,6 +372,7 @@
         out_shape=jax.ShapeDtypeStruct((rank, planes * 8), F32),
         in_specs=in_vmem(len(parts)),
         scratch_shapes=[pltpu.VMEM((8, rank, LANES), F32)],
+        compiler_params=pltpu.CompilerParams(vmem_limit_bytes=VMEM_LIMIT),
     )(*parts)
 
 
@@ -410,35 +396,31 @@
     taps_y = jnp.transpose(taps_y, (2, 0, 1))
     h_columns = jnp.transpose(factor_h, (1, 2, 0))
     rank = w_rows.shape[0]
-    x_high, x_low, far_keep, far_give, near_keep, near_give = blur_call(cube[0], taps_x, taps_y, w_rows)
-    far_taken = send(far_give, 0, 1)
-    near_taken = send(near_give, 0, 1)
-    spans = [(0, 2), (2, 4), (6, 8), (4, 6)]
-    rows = [(first * rank, last * rank) for first, last in spans]
-    near = [near_keep[first:last] + near_taken[first:last] for first, last in rows]
-    rows[2] = (rows[2][0], far_keep.shape[0])
-    far = [far_keep[first:last] + far_taken[first:last] for first, last in rows]
-    gram = far[2][2 * rank:]
-    far_round = around(far)
-    near_round = around(near)
-    ratio = ratio_call(gram, far_round[1][2 * rank:], h_columns)
-
-    def total(first, others, k):
-        part = slice(k * rank, (k + 1) * rank)
-        return (first[part] + others[0][part]) + (others[1][part] + others[2][part])
-
-    across = [send(total(far[0], far_round, 0), 4, 0), send(total(far[0], far_round, 1), 6, 0)]
-    along = send(total(near[0], near_round, 1), 2, 0)
-    h_piece = ratio * ((total(near[0], near_round, 0) + along) + (across[0] + across[1]))
-    h_near = jnp.stack([h_piece, send(h_piece, 2, 0)])
-    h_far = jnp.stack([send(h_piece, 4, 0), send(h_piece, 6, 0)])
-    near_parts = [h_near] + around([h_near] * 4)
-    near_parts = near_parts + [send(value, 0, 1) for value in near_parts]
-    numer, gram_h, h_next = near_call(x_high, x_low, near_parts)
-    far_parts = [h_far] + around([h_far] * 4)
-    numer, *far_parts = lax.optimization_barrier((numer, *far_parts))
-    far_parts = far_parts + [send(value, 0, 1) for value in far_parts]
-    w_piece = far_call(x_high, x_low, w_rows, numer, gram_h, far_parts)[None]
+    x_high, x_low, keep_0, give_0, keep_1, give_1 = blur_call(cube[0], taps_x, taps_y, w_rows)
+    chains = []
+    for keep, give in ((keep_0, give_0), (keep_1, give_1)):
+        taken = send(give, 0, 1)
+        bounds = [place * 4 * rank for place in (0, 1, 3, 2)]
+        sides = []
+        for first in bounds:
+            last = keep.shape[0] if first == max(bounds) else first + 4 * rank
+            sides.append(keep[first:last] + taken[first:last])
+        chains.append((sides, around(sides)))
+    ratios = ratio_call(chains[0][0][2], chains[0][1][1], h_columns)
+    rounds = []
+    for (sides, others), ratio in zip(chains, ratios):
+        line = []
+        for k in range(4):
+            part = slice(k * rank, (k + 1) * rank)
+            line.append((sides[0][part] + others[0][part]) + (others[1][part] + others[2][part]))
+        line = [line[0]] + [send(line[k], 2 * k, 0) for k in range(1, 4)]
+        h_piece = ratio * ((line[0] + line[1]) + (line[2] + line[3]))
+        h_line = jnp.stack([h_piece] + [send(h_piece, 2 * k, 0) for k in range(1, 4)])
+        parts = [h_line] + around([h_line] * 4)
+        rounds.append(parts + [send(value, 0, 1) for value in parts])
+    numer, gram_h, h_half = first_call(x_high, x_low, rounds[0])
+    w_piece, h_next = second_call(x_high, x_low, w_rows, numer, gram_h, h_half, rounds[1])
+    w_piece = w_piece[None]
     w_line = jnp.concatenate([send(w_piece, mask, 0) for mask in (2, 4, 6)])
     w_next = gather_w_call([w_piece, send(w_piece, 1, 0), w_line, send(w_line, 1, 0)])
     return jnp.transpose(w_next)[None], jnp.transpose(h_next, (2, 0, 1))

time: 83.6 us -> 76 us (0.909)
  starting transfers between devices: 32.1 us -> 42 us
  waiting for transfers between devices: 22.7 us -> 14.7 us
  Pallas kernels: 20.6 us -> 15.7 us
  local copies, waits for them, and re-layouts: 4.77 us -> 2.34 us
  other arithmetic: 2.31 us -> 0.18 us
    ppermute x33 -> x39, starting transfers between devices: 32.1 us -> 42 us  [send(): return lax.ppermute(value, ('sp', 'bd'), pairs)]
    ppermute x33 -> x39, waiting for transfers between devices: 22.7 us -> 14.7 us  [send(): return lax.ppermute(value, ('sp', 'bd'), pairs)]
    pallas_call x3, Pallas kernels: 6.12 us -> 3.98 us  [the longest x1 2.28 us: second_call(): pl.pallas_call(second_kernel, out_shape=[jax.ShapeDtypeStruct(numer.shape...]
    pallas_call x1, Pallas kernels: 12.8 us -> 11 us  [blur_call(): pl.pallas_call(blur_kernel, grid=(planes // GROUP,), out_shape=[jax.Shape...]
    add x5, other arithmetic: 1.4 us -> 0.13 us  [the longest x3 0.1 us: local(): sides.append(keep[first:last] + taken[first:last])]
    slice x2 -> x0, local copies, waits for them, and re-layouts: 1.22 us -> none  [the longest x1 0.62 us: local(): gram = far[2][2 * rank:]]
    unnamed x18 -> x12, local copies, waits for them, and re-layouts: 3.55 us -> 2.33 us
    pallas_call x1, Pallas kernels: 1.74 us -> 0.78 us  [gather_w_call(): pl.pallas_call(gather_w_kernel, out_shape=jax.ShapeDtypeStruct((rank, pla...]
  transfers between devices with their start and end apart: 33 -> 39, of which waited for: 17 -> 10; matrix products, arithmetic and copies ran while one was open for 3% -> 0% of each run, Pallas kernels for 5% -> 2%
where the time goes in v4:
time: 76 us; the launch traced here: 75.7 us
  starting transfers between devices  42 us (55%)
  Pallas kernels  15.7 us (21%)
  waiting for transfers between devices  14.7 us (19%)
  local copies, waits for them, and re-layouts  2.34 us (3%)
  between operations  0.79 us (1%)
    ppermute x39, starting transfers between devices, send(): return lax.ppermute(value, ('sp', 'bd'), pairs)  42 us
    ppermute x39, waiting for transfers between devices, send(): return lax.ppermute(value, ('sp', 'bd'), pairs)  14.7 us
    pallas_call x1, Pallas kernels, blur_call(): pl.pallas_call(blur_kernel, grid=(planes // GROUP,), out_shape=[jax.Shape...  11 us
    unnamed x12, local copies, waits for them, and re-layouts  2.33 us
    pallas_call x1, Pallas kernels, second_call(): pl.pallas_call(second_kernel, out_shape=[jax.ShapeDtypeStruct(numer.shape...  2.28 us
  transfers between devices with their start and end apart: 39, of which 10 were waited for; matrix products, arithmetic and copies ran while one was open for 0% of the time, Pallas kernels for 2%

profile of v4, /device:TPU:0, one launch (start us, length us, event | category | flops | bytes accessed | tf_op | source)
XLA Modules:
  0.0 75.7 jit_solution(7231019837454442317)
XLA Ops:
  0.6 0.0 copy-start
  0.6 0.9 %copy-done = f32[1,768,48]{1,2,0:T(8,128)S(1)} copy-done((f32[1,768,48]{1,2,0:T(8,128)S(1)}, f32[1,768,48]{1,2,0:T(8,128)}, u32[]{:S(2)}) %copy-start) | copy-done | bytes 147480
  1.5 0.7 copy-done.3
  2.3 0.7 copy-done.4
  3.0 11.0 %shard_map.68 = (bf16[32,96,256]{2,1,0:T(8,128)(2,1)S(1)}, bf16[32,96,256]{2,1,0:T(8,128)(2,1)S(1)}, f32[792,128]{1,0:T(8,128)S(1)}, f32[792,128]{1,0:T(8,128)S(...) custom-call(f32[96,32,256]{2,1,0:T(8,128)} %bitcast.30, f32[25,1,96]{2,1,0:T(1,128)S(1)} %bitcast.28, ...), custom_call_target="tpu_custom_call" | custom-call | tf_op jit(solution)/shard_map/pallas_call | solution.py:227
  14.0 0.5 collective-permute-start.17
  14.5 0.1 collective-permute-start
  14.5 1.3 %collective-permute-done.17 = f32[768,128]{1,0:T(8,128)S(1)} collective-permute-done((f32[768,128]{1,0:T(8,128)S(1)}, f32[768,128]{1,0:T(8,128)S(1)}, u32[]{:S(2)}, u32[]{:S(2)}) %collective-permute-start.17) | collective-permute-done | bytes 393248 | tf_op jit(solution)/shard_map/ppermute | solution.py:386
  15.9 3.9 %collective-permute-start.20 = (f32[192,128]{1,0:T(8,128)S(1)}, f32[192,128]{1,0:T(8,128)S(1)}, u32[]{:S(2)}, u32[]{:S(2)}) collective-permute-start(f32[192,128]{1,0:T(8,128)S(1)} %get-tuple-element.32), channel_id=1, source_target_pairs={{0,6},{1,7},{2,4},{3,5},{4,2},{5,3},{6,0},{7,1},{8,14},{9,15},{10,... | collective-permute-start | bytes 294920 | tf_op jit(solution)/shard_map/ppermute | solution.py:386
  19.8 0.5 collective-permute-start.19
  20.3 0.1 collective-permute-start.18
  20.4 0.0 collective-permute-done
  20.4 2.9 %collective-permute-start.3 = (f32[192,128]{1,0:T(8,128)S(1)}, f32[192,128]{1,0:T(8,128)S(1)}, u32[]{:S(2)}, u32[]{:S(2)}) collective-permute-start(f32[192,128]{1,0:T(8,128)S(1)} %get-tuple-element.29), channel_id=1, source_target_pairs={{0,6},{1,7},{2,4},{3,5},{4,2},{5,3},{6,0},{7,1},{8,14},{9,15},{10,... | collective-permute-start | bytes 294920 | tf_op jit(solution)/shard_map/ppermute | solution.py:386
  23.4 0.5 collective-permute-start.2
  23.9 0.0 collective-permute-done.20
  23.9 1.4 %collective-permute-start.1 = (f32[216,128]{1,0:T(8,128)S(1)}, f32[216,128]{1,0:T(8,128)S(1)}, u32[]{:S(2)}, u32[]{:S(2)}) collective-permute-start(f32[216,128]{1,0:T(8,128)S(1)} %slice_add_fusion.mine_ref), channel_id=1, source_target_pairs={{0,2},{1,3},{2,0},{3,1},{4,6},{5,7},{6,4},{7,5},{8,10},{9,11},{10,... | collective-permute-start | bytes 331784 | tf_op jit(solution)/shard_map/ppermute | solution.py:386
  25.3 0.9 %collective-permute-done.19 = f32[192,128]{1,0:T(8,128)S(1)} collective-permute-done((f32[192,128]{1,0:T(8,128)S(1)}, f32[192,128]{1,0:T(8,128)S(1)}, u32[]{:S(2)}, u32[]{:S(2)}) %collective-permute-start.19) | collective-permute-done | bytes 98336 | tf_op jit(solution)/shard_map/ppermute | solution.py:386
  26.2 0.0 collective-permute-done.18
  26.2 3.9 %collective-permute-start.23 = (f32[48,128]{1,0:T(8,128)S(1)}, f32[48,128]{1,0:T(8,128)S(1)}, u32[]{:S(2)}, u32[]{:S(2)}) collective-permute-start(f32[48,128]{1,0:T(8,128)S(1)} %get-tuple-element.38), channel_id=1, source_target_pairs={{0,24},{1,25},{2,26},{3,27},{4,28},{5,29},{6,30},{7,31},{8,16},{9,... | collective-permute-start | bytes 73736 | tf_op jit(solution)/shard_map/ppermute | solution.py:386
  30.2 0.6 collective-permute-start.21
  30.8 3.8 %collective-permute-start.6 = (f32[48,128]{1,0:T(8,128)S(1)}, f32[48,128]{1,0:T(8,128)S(1)}, u32[]{:S(2)}, u32[]{:S(2)}) collective-permute-start(f32[48,128]{1,0:T(8,128)S(1)} %get-tuple-element.35), channel_id=1, source_target_pairs={{0,24},{1,25},{2,26},{3,27},{4,28},{5,29},{6,30},{7,31},{8,16},{9,... | collective-permute-start | bytes 73736 | tf_op jit(solution)/shard_map/ppermute | solution.py:386
  34.7 0.3 shard_map.69
  34.9 0.0 collective-permute-done.23
  34.9 0.7 collective-permute-start.4
  35.7 3.8 %collective-permute-start.26 = (f32[48,128]{1,0:T(8,128)S(1)}, f32[48,128]{1,0:T(8,128)S(1)}, u32[]{:S(2)}, u32[]{:S(2)}) collective-permute-start(f32[48,128]{1,0:T(8,128)S(1)} %fusion.6), channel_id=1, source_target_pairs={{0,24},{1,25},{2,26},{3,27},{4,28},{5,29},{6,30},{7,31},{8,16},{9,... | collective-permute-start | bytes 73736 | tf_op jit(solution)/shard_map/ppermute | solution.py:386
  39.5 0.6 collective-permute-start.24
  40.1 0.0 collective-permute-done.5
  40.2 3.8 %collective-permute-start.9 = (f32[48,128]{1,0:T(8,128)S(1)}, f32[48,128]{1,0:T(8,128)S(1)}, u32[]{:S(2)}, u32[]{:S(2)}) collective-permute-start(f32[48,128]{1,0:T(8,128)S(1)} %fusion.13), channel_id=1, source_target_pairs={{0,24},{1,25},{2,26},{3,27},{4,28},{5,29},{6,30},{7,31},{8,16},{9,... | collective-permute-start | bytes 73736 | tf_op jit(solution)/shard_map/ppermute | solution.py:386
  44.0 0.0 collective-permute-done.26
  44.0 0.6 collective-permute-start.7
  44.6 0.0 collective-permute-done.25
  44.6 0.0 collective-permute-done.24
  44.6 1.4 %collective-permute-start.29 = (f32[4,48,128]{2,1,0:T(8,128)S(1)}, f32[4,48,128]{2,1,0:T(8,128)S(1)}, u32[]{:S(2)}, u32[]{:S(2)}) collective-permute-start(f32[4,48,128]{2,1,0:T(8,128)S(1)} %pad_maximum_fusion.1.rest_0_), channel_id=1, source_target_pairs={{0,6},{1,7},{2,4},{3,5},{4,2},{5,3},{6,0},{7,1},{8,14},{9,15},{10,... | collective-permute-start | bytes 294920 | tf_op jit(solution)/shard_map/ppermute | solution.py:386
  46.0 1.4 %collective-permute-start.28 = (f32[4,48,128]{2,1,0:T(8,128)S(1)}, f32[4,48,128]{2,1,0:T(8,128)S(1)}, u32[]{:S(2)}, u32[]{:S(2)}) collective-permute-start(f32[4,48,128]{2,1,0:T(8,128)S(1)} %pad_maximum_fusion.1.rest_0_), channel_id=1, source_target_pairs={{0,2},{1,3},{2,0},{3,1},{4,6},{5,7},{6,4},{7,5},{8,10},{9,11},{10,... | collective-permute-start | bytes 294920 | tf_op jit(solution)/shard_map/ppermute | solution.py:386
  47.4 0.0 collective-permute-done.9
  47.4 1.3 %collective-permute-done.8 = f32[48,128]{1,0:T(8,128)S(1)} collective-permute-done((f32[48,128]{1,0:T(8,128)S(1)}, f32[48,128]{1,0:T(8,128)S(1)}, u32[]{:S(2)}, u32[]{:S(2)}) %collective-permute-start.8) | collective-permute-done | bytes 24608 | tf_op jit(solution)/shard_map/ppermute | solution.py:386
  48.7 0.0 collective-permute-done.7
  48.7 1.1 %collective-permute-start.12 = (f32[4,48,128]{2,1,0:T(8,128)S(1)}, f32[4,48,128]{2,1,0:T(8,128)S(1)}, u32[]{:S(2)}, u32[]{:S(2)}) collective-permute-start(f32[4,48,128]{2,1,0:T(8,128)S(1)} %pad_maximum_fusion.rest_0_), channel_id=1, source_target_pairs={{0,6},{1,7},{2,4},{3,5},{4,2},{5,3},{6,0},{7,1},{8,14},{9,15},{10,... | collective-permute-start | bytes 294920 | tf_op jit(solution)/shard_map/ppermute | solution.py:386
  49.8 1.6 %collective-permute-start.11 = (f32[4,48,128]{2,1,0:T(8,128)S(1)}, f32[4,48,128]{2,1,0:T(8,128)S(1)}, u32[]{:S(2)}, u32[]{:S(2)}) collective-permute-start(f32[4,48,128]{2,1,0:T(8,128)S(1)} %pad_maximum_fusion.rest_0_), channel_id=1, source_target_pairs={{0,2},{1,3},{2,0},{3,1},{4,6},{5,7},{6,4},{7,5},{8,10},{9,11},{10,... | collective-permute-start | bytes 294920 | tf_op jit(solution)/shard_map/ppermute | solution.py:386
  51.3 0.9 %collective-permute-start.10 = (f32[4,48,128]{2,1,0:T(8,128)S(1)}, f32[4,48,128]{2,1,0:T(8,128)S(1)}, u32[]{:S(2)}, u32[]{:S(2)}) collective-permute-start(f32[4,48,128]{2,1,0:T(8,128)S(1)} %pad_maximum_fusion.rest_0_), channel_id=1, source_target_pairs={{0,4},{1,5},{2,6},{3,7},{4,0},{5,1},{6,2},{7,3},{8,12},{9,13},{10,... | collective-permute-start | bytes 294920 | tf_op jit(solution)/shard_map/ppermute | solution.py:386
  52.3 0.0 collective-permute-done.29.rest_3_
  52.3 1.1 %collective-permute-start.27 = (f32[4,48,128]{2,1,0:T(8,128)S(1)}, f32[4,48,128]{2,1,0:T(8,128)S(1)}, u32[]{:S(2)}, u32[]{:S(2)}) collective-permute-start(f32[4,48,128]{2,1,0:T(8,128)S(1)} %pad_maximum_fusion.1.rest_0_), channel_id=1, source_target_pairs={{0,4},{1,5},{2,6},{3,7},{4,0},{5,1},{6,2},{7,3},{8,12},{9,13},{10,... | collective-permute-start | bytes 294920 | tf_op jit(solution)/shard_map/ppermute | solution.py:386
  53.4 0.0 collective-permute-done.28.rest_2_
  53.4 1.0 %collective-permute-done.12.rest_3_ = f32[4,48,128]{2,1,0:T(8,128)S(1)} collective-permute-done((f32[4,48,128]{2,1,0:T(8,128)S(1)}, f32[4,48,128]{2,1,0:T(8,128)S(1)}, u32[]{:S(2)}, u32[]{:S(2)}) %collective-permute-start.12) | collective-permute-done | bytes 98336 | tf_op jit(solution)/shard_map/ppermute | solution.py:386
  54.4 0.9 %collective-permute-done.11.rest_2_ = f32[4,48,128]{2,1,0:T(8,128)S(1)} collective-permute-done((f32[4,48,128]{2,1,0:T(8,128)S(1)}, f32[4,48,128]{2,1,0:T(8,128)S(1)}, u32[]{:S(2)}, u32[]{:S(2)}) %collective-permute-start.11) | collective-permute-done | bytes 98336 | tf_op jit(solution)/shard_map/ppermute | solution.py:386
  55.3 0.0 collective-permute-start.15
  55.3 0.6 collective-permute-done.10.rest_1_
  56.0 0.0 collective-permute-start.14
  56.0 1.0 %collective-permute-done.27.rest_1_ = f32[4,48,128]{2,1,0:T(8,128)S(1)} collective-permute-done((f32[4,48,128]{2,1,0:T(8,128)S(1)}, f32[4,48,128]{2,1,0:T(8,128)S(1)}, u32[]{:S(2)}, u32[]{:S(2)}) %collective-permute-start.27) | collective-permute-done | bytes 98336 | tf_op jit(solution)/shard_map/ppermute | solution.py:386
  57.0 0.0 collective-permute-start.30
  57.0 0.5 collective-permute-start.33
  57.5 0.1 collective-permute-start.32
  57.6 0.0 collective-permute-done.15.rest_6_
  57.6 0.4 collective-permute-start.31
  58.1 1.4 %shard_map.70 = (f32[48,96]{1,0:T(8,128)S(1)}, f32[48,48]{1,0:T(8,128)S(1)}, f32[32,32,48]{2,1,0:T(8,128)S(1)}) custom-call(bf16[32,96,256]{2,1,0:T(8,128)(2,1)S(1)} %get-tuple-element.15.xh_ref, bf16[32,96,256]{2,1,0:T(8,128)(2,1)S(1)} %get-tuple-element.16.xl_ref, f32[4,48,128]{2,1,0:T(8,128)S(1)} %pad_maximum_fusion.rest_0_, ...), custom_call_target="tpu_custom_call" | custom-call | tf_op jit(solution)/shard_map/pallas_call | solution.py:311
  59.5 2.3 %shard_map.71 = (f32[48,96]{1,0:T(8,128)S(1)}, f32[32,32,48]{2,1,0:T(8,128)}) custom-call(bf16[32,96,256]{2,1,0:T(8,128)(2,1)S(1)} %get-tuple-element.15.xh_ref, bf16[32,96,256]{2,1,0:T(8,128)(2,1)S(1)} %get-tuple-element.16.xl_ref, f32[48,768]{1,0:T(8,128)S(1)} %bitcast.21, f32[48,96]{1,0:T(8,128)S(1)} %get-tuple-element.20.numer_ref, ...), custom_call_target="tpu_custom_call" | custom-call | tf_op jit(solution)/shard_map/pallas_call | solution.py:339
  61.8 0.2 collective-permute-start.35
  62.0 3.3 %collective-permute-start.37 = (f32[1,48,96]{2,1,0:T(8,128)S(1)}, f32[1,48,96]{2,1,0:T(8,128)S(1)}, u32[]{:S(2)}, u32[]{:S(2)}) collective-permute-start(f32[1,48,96]{2,1,0:T(8,128)S(1)} %bitcast.24), channel_id=1, source_target_pairs={{0,24},{1,25},{2,26},{3,27},{4,28},{5,29},{6,30},{7,31},{8,16},{9,... | collective-permute-start | bytes 55304 | tf_op jit(solution)/shard_map/ppermute | solution.py:386
  65.3 0.3 collective-permute-done.35
  65.6 4.4 %collective-permute-done.36 = f32[1,48,96]{2,1,0:T(8,128)S(1)} collective-permute-done((f32[1,48,96]{2,1,0:T(8,128)S(1)}, f32[1,48,96]{2,1,0:T(8,128)S(1)}, u32[]{:S(2)}, u32[]{:S(2)}) %collective-permute-start.36) | collective-permute-done | bytes 18464 | tf_op jit(solution)/shard_map/ppermute | solution.py:386
  70.0 1.0 %collective-permute-start.38 = (f32[3,48,96]{2,1,0:T(8,128)S(1)}, f32[3,48,96]{2,1,0:T(8,128)S(1)}, u32[]{:S(2)}, u32[]{:S(2)}) collective-permute-start(f32[3,48,96]{2,1,0:T(8,128)S(1)} %constant_dynamic-update-slice_fusion.refs_2_), channel_id=1, source_target_pairs={{0,4},{1,5},{2,6},{3,7},{4,0},{5,1},{6,2},{7,3},{8,12},{9,13},{10,... | collective-permute-start | bytes 165896 | tf_op jit(solution)/shard_map/ppermute | solution.py:386
  71.1 1.0 %collective-permute-start.34 = (f32[1,48,96]{2,1,0:T(8,128)S(1)}, f32[1,48,96]{2,1,0:T(8,128)S(1)}, u32[]{:S(2)}, u32[]{:S(2)}) collective-permute-start(f32[1,48,96]{2,1,0:T(8,128)S(1)} %bitcast.26), channel_id=1, source_target_pairs={{0,4},{1,5},{2,6},{3,7},{4,0},{5,1},{6,2},{7,3},{8,12},{9,13},{10,... | collective-permute-start | bytes 55304 | tf_op jit(solution)/shard_map/ppermute | solution.py:386
  72.1 2.8 %collective-permute-done.34.refs_1_ = f32[1,48,96]{2,1,0:T(8,128)S(1)} collective-permute-done((f32[1,48,96]{2,1,0:T(8,128)S(1)}, f32[1,48,96]{2,1,0:T(8,128)S(1)}, u32[]{:S(2)}, u32[]{:S(2)}) %collective-permute-start.34) | collective-permute-done | bytes 18464 | tf_op jit(solution)/shard_map/ppermute | solution.py:386
  74.9 0.8 %shard_map.72 = f32[48,768]{1,0:T(8,128)} custom-call(f32[1,48,96]{2,1,0:T(8,128)S(1)} %bitcast.27, f32[1,48,96]{2,1,0:T(8,128)S(1)} %collective-permute-done.34.refs_1_, f32[3,48,96]{2,1,0:T(8,128)S(1)} %constant_dynamic-update-slice_fusion.refs_2_, f32[3,48,96]{2,1,0:T(8,128)S(1)} %collective-permute-done.38.refs_3_), custom_call_target="tpu_custom_call" | custom-call | tf_op jit(solution)/shard_map/pallas_call | solution.py:370
  (41 shorter events, 0.3 us)
Async XLA Ops:
  0.6 0.9 %copy-start = (f32[1,768,48]{1,2,0:T(8,128)S(1)}, f32[1,768,48]{1,2,0:T(8,128)}, u32[]{:S(2)}) copy-start(f32[1,768,48]{1,2,0:T(8,128)} %param.8) | copy-start | bytes 442372
  1.5 0.7 copy-start.3
  2.3 0.7 copy-start.4
  14.0 1.9 %collective-permute-start.17 = (f32[768,128]{1,0:T(8,128)S(1)}, f32[768,128]{1,0:T(8,128)S(1)}, u32[]{:S(2)}, u32[]{:S(2)}) collective-permute-start(f32[768,128]{1,0:T(8,128)S(1)} %get-tuple-element.25), channel_id=1, source_target_pairs={{0,1},{1,0},{2,3},{3,2},{4,5},{5,4},{6,7},{7,6},{8,9},{9,8},{10,11... | collective-permute-start | bytes 1179656 | tf_op jit(solution)/shard_map/ppermute | solution.py:386
  14.5 5.9 %collective-permute-start = (f32[792,128]{1,0:T(8,128)S(1)}, f32[792,128]{1,0:T(8,128)S(1)}, u32[]{:S(2)}, u32[]{:S(2)}) collective-permute-start(f32[792,128]{1,0:T(8,128)S(1)} %get-tuple-element.18), channel_id=1, source_target_pairs={{0,1},{1,0},{2,3},{3,2},{4,5},{5,4},{6,7},{7,6},{8,9},{9,8},{10,11... | collective-permute-start | bytes 1216520 | tf_op jit(solution)/shard_map/ppermute | solution.py:386
  15.8 18.8 %copy-start.2 = (f32[48,32,32]{0,2,1:T(8,128)S(1)}, f32[48,32,32]{0,2,1:T(8,128)}, u32[]{:S(2)}) copy-start(f32[48,32,32]{0,2,1:T(8,128)} %param.9) | copy-start | bytes 589828
  15.9 8.0 %collective-permute-start.20 = (f32[192,128]{1,0:T(8,128)S(1)}, f32[192,128]{1,0:T(8,128)S(1)}, u32[]{:S(2)}, u32[]{:S(2)}) collective-permute-start(f32[192,128]{1,0:T(8,128)S(1)} %get-tuple-element.32), channel_id=1, source_target_pairs={{0,6},{1,7},{2,4},{3,5},{4,2},{5,3},{6,0},{7,1},{8,14},{9,15},{10,... | collective-permute-start | bytes 294920 | tf_op jit(solution)/shard_map/ppermute | solution.py:386
  19.8 6.5 %collective-permute-start.19 = (f32[192,128]{1,0:T(8,128)S(1)}, f32[192,128]{1,0:T(8,128)S(1)}, u32[]{:S(2)}, u32[]{:S(2)}) collective-permute-start(f32[192,128]{1,0:T(8,128)S(1)} %get-tuple-element.33), channel_id=1, source_target_pairs={{0,2},{1,3},{2,0},{3,1},{4,6},{5,7},{6,4},{7,5},{8,10},{9,11},{10,... | collective-permute-start | bytes 294920 | tf_op jit(solution)/shard_map/ppermute | solution.py:386
  20.3 6.0 %collective-permute-start.18 = (f32[192,128]{1,0:T(8,128)S(1)}, f32[192,128]{1,0:T(8,128)S(1)}, u32[]{:S(2)}, u32[]{:S(2)}) collective-permute-start(f32[192,128]{1,0:T(8,128)S(1)} %get-tuple-element.34), channel_id=1, source_target_pairs={{0,4},{1,5},{2,6},{3,7},{4,0},{5,1},{6,2},{7,3},{8,12},{9,13},{10,... | collective-permute-start | bytes 294920 | tf_op jit(solution)/shard_map/ppermute | solution.py:386
  20.4 9.7 %collective-permute-start.3 = (f32[192,128]{1,0:T(8,128)S(1)}, f32[192,128]{1,0:T(8,128)S(1)}, u32[]{:S(2)}, u32[]{:S(2)}) collective-permute-start(f32[192,128]{1,0:T(8,128)S(1)} %get-tuple-element.29), channel_id=1, source_target_pairs={{0,6},{1,7},{2,4},{3,5},{4,2},{5,3},{6,0},{7,1},{8,14},{9,15},{10,... | collective-permute-start | bytes 294920 | tf_op jit(solution)/shard_map/ppermute | solution.py:386
  23.4 7.5 %collective-permute-start.2 = (f32[192,128]{1,0:T(8,128)S(1)}, f32[192,128]{1,0:T(8,128)S(1)}, u32[]{:S(2)}, u32[]{:S(2)}) collective-permute-start(f32[192,128]{1,0:T(8,128)S(1)} %get-tuple-element.30), channel_id=1, source_target_pairs={{0,4},{1,5},{2,6},{3,7},{4,0},{5,1},{6,2},{7,3},{8,12},{9,13},{10,... | collective-permute-start | bytes 294920 | tf_op jit(solution)/shard_map/ppermute | solution.py:386
  23.9 6.9 %collective-permute-start.1 = (f32[216,128]{1,0:T(8,128)S(1)}, f32[216,128]{1,0:T(8,128)S(1)}, u32[]{:S(2)}, u32[]{:S(2)}) collective-permute-start(f32[216,128]{1,0:T(8,128)S(1)} %slice_add_fusion.mine_ref), channel_id=1, source_target_pairs={{0,2},{1,3},{2,0},{3,1},{4,6},{5,7},{6,4},{7,5},{8,10},{9,11},{10,... | collective-permute-start | bytes 331784 | tf_op jit(solution)/shard_map/ppermute | solution.py:386
  26.2 8.7 %collective-permute-start.23 = (f32[48,128]{1,0:T(8,128)S(1)}, f32[48,128]{1,0:T(8,128)S(1)}, u32[]{:S(2)}, u32[]{:S(2)}) collective-permute-start(f32[48,128]{1,0:T(8,128)S(1)} %get-tuple-element.38), channel_id=1, source_target_pairs={{0,24},{1,25},{2,26},{3,27},{4,28},{5,29},{6,30},{7,31},{8,16},{9,... | collective-permute-start | bytes 73736 | tf_op jit(solution)/shard_map/ppermute | solution.py:386
  30.2 5.5 %collective-permute-start.22 = (f32[48,128]{1,0:T(8,128)S(1)}, f32[48,128]{1,0:T(8,128)S(1)}, u32[]{:S(2)}, u32[]{:S(2)}) collective-permute-start(f32[48,128]{1,0:T(8,128)S(1)} %get-tuple-element.39), channel_id=1, source_target_pairs={{0,16},{1,17},{2,18},{3,19},{4,20},{5,21},{6,22},{7,23},{8,24},{9,... | collective-permute-start | bytes 73736 | tf_op jit(solution)/shard_map/ppermute | solution.py:386
  30.2 5.5 %collective-permute-start.21 = (f32[48,128]{1,0:T(8,128)S(1)}, f32[48,128]{1,0:T(8,128)S(1)}, u32[]{:S(2)}, u32[]{:S(2)}) collective-permute-start(f32[48,128]{1,0:T(8,128)S(1)} %get-tuple-element.40), channel_id=1, source_target_pairs={{0,8},{1,9},{2,10},{3,11},{4,12},{5,13},{6,14},{7,15},{8,0},{9,1},... | collective-permute-start | bytes 73736 | tf_op jit(solution)/shard_map/ppermute | solution.py:386
  30.8 8.7 %collective-permute-start.6 = (f32[48,128]{1,0:T(8,128)S(1)}, f32[48,128]{1,0:T(8,128)S(1)}, u32[]{:S(2)}, u32[]{:S(2)}) collective-permute-start(f32[48,128]{1,0:T(8,128)S(1)} %get-tuple-element.35), channel_id=1, source_target_pairs={{0,24},{1,25},{2,26},{3,27},{4,28},{5,29},{6,30},{7,31},{8,16},{9,... | collective-permute-start | bytes 73736 | tf_op jit(solution)/shard_map/ppermute | solution.py:386
  34.6 5.5 %collective-permute-start.5 = (f32[48,128]{1,0:T(8,128)S(1)}, f32[48,128]{1,0:T(8,128)S(1)}, u32[]{:S(2)}, u32[]{:S(2)}) collective-permute-start(f32[48,128]{1,0:T(8,128)S(1)} %get-tuple-element.36), channel_id=1, source_target_pairs={{0,16},{1,17},{2,18},{3,19},{4,20},{5,21},{6,22},{7,23},{8,24},{9,... | collective-permute-start | bytes 73736 | tf_op jit(solution)/shard_map/ppermute | solution.py:386
  34.9 5.2 %collective-permute-start.4 = (f32[48,128]{1,0:T(8,128)S(1)}, f32[48,128]{1,0:T(8,128)S(1)}, u32[]{:S(2)}, u32[]{:S(2)}) collective-permute-start(f32[48,128]{1,0:T(8,128)S(1)} %get-tuple-element.37), channel_id=1, source_target_pairs={{0,8},{1,9},{2,10},{3,11},{4,12},{5,13},{6,14},{7,15},{8,0},{9,1},... | collective-permute-start | bytes 73736 | tf_op jit(solution)/shard_map/ppermute | solution.py:386
  35.7 8.3 %collective-permute-start.26 = (f32[48,128]{1,0:T(8,128)S(1)}, f32[48,128]{1,0:T(8,128)S(1)}, u32[]{:S(2)}, u32[]{:S(2)}) collective-permute-start(f32[48,128]{1,0:T(8,128)S(1)} %fusion.6), channel_id=1, source_target_pairs={{0,24},{1,25},{2,26},{3,27},{4,28},{5,29},{6,30},{7,31},{8,16},{9,... | collective-permute-start | bytes 73736 | tf_op jit(solution)/shard_map/ppermute | solution.py:386
  39.5 5.1 %collective-permute-start.25 = (f32[48,128]{1,0:T(8,128)S(1)}, f32[48,128]{1,0:T(8,128)S(1)}, u32[]{:S(2)}, u32[]{:S(2)}) collective-permute-start(f32[48,128]{1,0:T(8,128)S(1)} %fusion.6), channel_id=1, source_target_pairs={{0,16},{1,17},{2,18},{3,19},{4,20},{5,21},{6,22},{7,23},{8,24},{9,... | collective-permute-start | bytes 73736 | tf_op jit(solution)/shard_map/ppermute | solution.py:386
  39.5 5.1 %collective-permute-start.24 = (f32[48,128]{1,0:T(8,128)S(1)}, f32[48,128]{1,0:T(8,128)S(1)}, u32[]{:S(2)}, u32[]{:S(2)}) collective-permute-start(f32[48,128]{1,0:T(8,128)S(1)} %fusion.6), channel_id=1, source_target_pairs={{0,8},{1,9},{2,10},{3,11},{4,12},{5,13},{6,14},{7,15},{8,0},{9,1},... | collective-permute-start | bytes 73736 | tf_op jit(solution)/shard_map/ppermute | solution.py:386
  40.2 7.3 %collective-permute-start.9 = (f32[48,128]{1,0:T(8,128)S(1)}, f32[48,128]{1,0:T(8,128)S(1)}, u32[]{:S(2)}, u32[]{:S(2)}) collective-permute-start(f32[48,128]{1,0:T(8,128)S(1)} %fusion.13), channel_id=1, source_target_pairs={{0,24},{1,25},{2,26},{3,27},{4,28},{5,29},{6,30},{7,31},{8,16},{9,... | collective-permute-start | bytes 73736 | tf_op jit(solution)/shard_map/ppermute | solution.py:386
  44.0 4.7 %collective-permute-start.8 = (f32[48,128]{1,0:T(8,128)S(1)}, f32[48,128]{1,0:T(8,128)S(1)}, u32[]{:S(2)}, u32[]{:S(2)}) collective-permute-start(f32[48,128]{1,0:T(8,128)S(1)} %fusion.13), channel_id=1, source_target_pairs={{0,16},{1,17},{2,18},{3,19},{4,20},{5,21},{6,22},{7,23},{8,24},{9,... | collective-permute-start | bytes 73736 | tf_op jit(solution)/shard_map/ppermute | solution.py:386
  44.0 4.7 %collective-permute-start.7 = (f32[48,128]{1,0:T(8,128)S(1)}, f32[48,128]{1,0:T(8,128)S(1)}, u32[]{:S(2)}, u32[]{:S(2)}) collective-permute-start(f32[48,128]{1,0:T(8,128)S(1)} %fusion.13), channel_id=1, source_target_pairs={{0,8},{1,9},{2,10},{3,11},{4,12},{5,13},{6,14},{7,15},{8,0},{9,1},... | collective-permute-start | bytes 73736 | tf_op jit(solution)/shard_map/ppermute | solution.py:386
  44.6 7.6 %collective-permute-start.29 = (f32[4,48,128]{2,1,0:T(8,128)S(1)}, f32[4,48,128]{2,1,0:T(8,128)S(1)}, u32[]{:S(2)}, u32[]{:S(2)}) collective-permute-start(f32[4,48,128]{2,1,0:T(8,128)S(1)} %pad_maximum_fusion.1.rest_0_), channel_id=1, source_target_pairs={{0,6},{1,7},{2,4},{3,5},{4,2},{5,3},{6,0},{7,1},{8,14},{9,15},{10,... | collective-permute-start | bytes 294920 | tf_op jit(solution)/shard_map/ppermute | solution.py:386
  46.0 7.4 %collective-permute-start.28 = (f32[4,48,128]{2,1,0:T(8,128)S(1)}, f32[4,48,128]{2,1,0:T(8,128)S(1)}, u32[]{:S(2)}, u32[]{:S(2)}) collective-permute-start(f32[4,48,128]{2,1,0:T(8,128)S(1)} %pad_maximum_fusion.1.rest_0_), channel_id=1, source_target_pairs={{0,2},{1,3},{2,0},{3,1},{4,6},{5,7},{6,4},{7,5},{8,10},{9,11},{10,... | collective-permute-start | bytes 294920 | tf_op jit(solution)/shard_map/ppermute | solution.py:386
  48.7 5.7 %collective-permute-start.12 = (f32[4,48,128]{2,1,0:T(8,128)S(1)}, f32[4,48,128]{2,1,0:T(8,128)S(1)}, u32[]{:S(2)}, u32[]{:S(2)}) collective-permute-start(f32[4,48,128]{2,1,0:T(8,128)S(1)} %pad_maximum_fusion.rest_0_), channel_id=1, source_target_pairs={{0,6},{1,7},{2,4},{3,5},{4,2},{5,3},{6,0},{7,1},{8,14},{9,15},{10,... | collective-permute-start | bytes 294920 | tf_op jit(solution)/shard_map/ppermute | solution.py:386
  49.8 5.6 %collective-permute-start.11 = (f32[4,48,128]{2,1,0:T(8,128)S(1)}, f32[4,48,128]{2,1,0:T(8,128)S(1)}, u32[]{:S(2)}, u32[]{:S(2)}) collective-permute-start(f32[4,48,128]{2,1,0:T(8,128)S(1)} %pad_maximum_fusion.rest_0_), channel_id=1, source_target_pairs={{0,2},{1,3},{2,0},{3,1},{4,6},{5,7},{6,4},{7,5},{8,10},{9,11},{10,... | collective-permute-start | bytes 294920 | tf_op jit(solution)/shard_map/ppermute | solution.py:386
  51.3 4.6 %collective-permute-start.10 = (f32[4,48,128]{2,1,0:T(8,128)S(1)}, f32[4,48,128]{2,1,0:T(8,128)S(1)}, u32[]{:S(2)}, u32[]{:S(2)}) collective-permute-start(f32[4,48,128]{2,1,0:T(8,128)S(1)} %pad_maximum_fusion.rest_0_), channel_id=1, source_target_pairs={{0,4},{1,5},{2,6},{3,7},{4,0},{5,1},{6,2},{7,3},{8,12},{9,13},{10,... | collective-permute-start | bytes 294920 | tf_op jit(solution)/shard_map/ppermute | solution.py:386
  52.3 4.7 %collective-permute-start.27 = (f32[4,48,128]{2,1,0:T(8,128)S(1)}, f32[4,48,128]{2,1,0:T(8,128)S(1)}, u32[]{:S(2)}, u32[]{:S(2)}) collective-permute-start(f32[4,48,128]{2,1,0:T(8,128)S(1)} %pad_maximum_fusion.1.rest_0_), channel_id=1, source_target_pairs={{0,4},{1,5},{2,6},{3,7},{4,0},{5,1},{6,2},{7,3},{8,12},{9,13},{10,... | collective-permute-start | bytes 294920 | tf_op jit(solution)/shard_map/ppermute | solution.py:386
  53.4 3.6 %collective-permute-start.13 = (f32[4,48,128]{2,1,0:T(8,128)S(1)}, f32[4,48,128]{2,1,0:T(8,128)S(1)}, u32[]{:S(2)}, u32[]{:S(2)}) collective-permute-start(f32[4,48,128]{2,1,0:T(8,128)S(1)} %pad_maximum_fusion.rest_0_), channel_id=1, source_target_pairs={{0,1},{1,0},{2,3},{3,2},{4,5},{5,4},{6,7},{7,6},{8,9},{9,8},{10,11... | collective-permute-start | bytes 294920 | tf_op jit(solution)/shard_map/ppermute | solution.py:386
  54.4 3.1 %collective-permute-start.16 = (f32[4,48,128]{2,1,0:T(8,128)S(1)}, f32[4,48,128]{2,1,0:T(8,128)S(1)}, u32[]{:S(2)}, u32[]{:S(2)}) collective-permute-start(f32[4,48,128]{2,1,0:T(8,128)S(1)} %collective-permute-done.12.rest_3_), channel_id=1, source_target_pairs={{0,1},{1,0},{2,3},{3,2},{4,5},{5,4},{6,7},{7,6},{8,9},{9,8},{10,11... | collective-permute-start | bytes 294920 | tf_op jit(solution)/shard_map/ppermute | solution.py:386
  55.3 2.3 %collective-permute-start.15 = (f32[4,48,128]{2,1,0:T(8,128)S(1)}, f32[4,48,128]{2,1,0:T(8,128)S(1)}, u32[]{:S(2)}, u32[]{:S(2)}) collective-permute-start(f32[4,48,128]{2,1,0:T(8,128)S(1)} %collective-permute-done.11.rest_2_), channel_id=1, source_target_pairs={{0,1},{1,0},{2,3},{3,2},{4,5},{5,4},{6,7},{7,6},{8,9},{9,8},{10,11... | collective-permute-start | bytes 294920 | tf_op jit(solution)/shard_map/ppermute | solution.py:386
  56.0 2.1 %collective-permute-start.14 = (f32[4,48,128]{2,1,0:T(8,128)S(1)}, f32[4,48,128]{2,1,0:T(8,128)S(1)}, u32[]{:S(2)}, u32[]{:S(2)}) collective-permute-start(f32[4,48,128]{2,1,0:T(8,128)S(1)} %collective-permute-done.10.rest_1_), channel_id=1, source_target_pairs={{0,1},{1,0},{2,3},{3,2},{4,5},{5,4},{6,7},{7,6},{8,9},{9,8},{10,11... | collective-permute-start | bytes 294920 | tf_op jit(solution)/shard_map/ppermute | solution.py:386
  57.0 2.5 %collective-permute-start.30 = (f32[4,48,128]{2,1,0:T(8,128)S(1)}, f32[4,48,128]{2,1,0:T(8,128)S(1)}, u32[]{:S(2)}, u32[]{:S(2)}) collective-permute-start(f32[4,48,128]{2,1,0:T(8,128)S(1)} %pad_maximum_fusion.1.rest_0_), channel_id=1, source_target_pairs={{0,1},{1,0},{2,3},{3,2},{4,5},{5,4},{6,7},{7,6},{8,9},{9,8},{10,11... | collective-permute-start | bytes 294920 | tf_op jit(solution)/shard_map/ppermute | solution.py:386
  57.0 2.5 %collective-permute-start.33 = (f32[4,48,128]{2,1,0:T(8,128)S(1)}, f32[4,48,128]{2,1,0:T(8,128)S(1)}, u32[]{:S(2)}, u32[]{:S(2)}) collective-permute-start(f32[4,48,128]{2,1,0:T(8,128)S(1)} %collective-permute-done.29.rest_3_), channel_id=1, source_target_pairs={{0,1},{1,0},{2,3},{3,2},{4,5},{5,4},{6,7},{7,6},{8,9},{9,8},{10,11... | collective-permute-start | bytes 294920 | tf_op jit(solution)/shard_map/ppermute | solution.py:386
  57.5 2.0 %collective-permute-start.32 = (f32[4,48,128]{2,1,0:T(8,128)S(1)}, f32[4,48,128]{2,1,0:T(8,128)S(1)}, u32[]{:S(2)}, u32[]{:S(2)}) collective-permute-start(f32[4,48,128]{2,1,0:T(8,128)S(1)} %collective-permute-done.28.rest_2_), channel_id=1, source_target_pairs={{0,1},{1,0},{2,3},{3,2},{4,5},{5,4},{6,7},{7,6},{8,9},{9,8},{10,11... | collective-permute-start | bytes 294920 | tf_op jit(solution)/shard_map/ppermute | solution.py:386
  57.6 1.9 %collective-permute-start.31 = (f32[4,48,128]{2,1,0:T(8,128)S(1)}, f32[4,48,128]{2,1,0:T(8,128)S(1)}, u32[]{:S(2)}, u32[]{:S(2)}) collective-permute-start(f32[4,48,128]{2,1,0:T(8,128)S(1)} %collective-permute-done.27.rest_1_), channel_id=1, source_target_pairs={{0,1},{1,0},{2,3},{3,2},{4,5},{5,4},{6,7},{7,6},{8,9},{9,8},{10,11... | collective-permute-start | bytes 294920 | tf_op jit(solution)/shard_map/ppermute | solution.py:386
  58.1 1.5 %copy-start.1 = (f32[1,768,48]{1,2,0:T(8,128)S(1)}, f32[1,768,48]{1,2,0:T(8,128)}, u32[]{:S(2)}) copy-start(f32[1,768,48]{1,2,0:T(8,128)} %param.8) | copy-start | bytes 442372
  61.8 3.8 %collective-permute-start.35 = (f32[1,48,96]{2,1,0:T(8,128)S(1)}, f32[1,48,96]{2,1,0:T(8,128)S(1)}, u32[]{:S(2)}, u32[]{:S(2)}) collective-permute-start(f32[1,48,96]{2,1,0:T(8,128)S(1)} %bitcast.23), channel_id=1, source_target_pairs={{0,8},{1,9},{2,10},{3,11},{4,12},{5,13},{6,14},{7,15},{8,0},{9,1},... | collective-permute-start | bytes 55304 | tf_op jit(solution)/shard_map/ppermute | solution.py:386
  62.0 8.0 %collective-permute-start.37 = (f32[1,48,96]{2,1,0:T(8,128)S(1)}, f32[1,48,96]{2,1,0:T(8,128)S(1)}, u32[]{:S(2)}, u32[]{:S(2)}) collective-permute-start(f32[1,48,96]{2,1,0:T(8,128)S(1)} %bitcast.24), channel_id=1, source_target_pairs={{0,24},{1,25},{2,26},{3,27},{4,28},{5,29},{6,30},{7,31},{8,16},{9,... | collective-permute-start | bytes 55304 | tf_op jit(solution)/shard_map/ppermute | solution.py:386
  65.3 4.7 %collective-permute-start.36 = (f32[1,48,96]{2,1,0:T(8,128)S(1)}, f32[1,48,96]{2,1,0:T(8,128)S(1)}, u32[]{:S(2)}, u32[]{:S(2)}) collective-permute-start(f32[1,48,96]{2,1,0:T(8,128)S(1)} %bitcast.25), channel_id=1, source_target_pairs={{0,16},{1,17},{2,18},{3,19},{4,20},{5,21},{6,22},{7,23},{8,24},{9,... | collective-permute-start | bytes 55304 | tf_op jit(solution)/shard_map/ppermute | solution.py:386
  70.0 4.9 %collective-permute-start.38 = (f32[3,48,96]{2,1,0:T(8,128)S(1)}, f32[3,48,96]{2,1,0:T(8,128)S(1)}, u32[]{:S(2)}, u32[]{:S(2)}) collective-permute-start(f32[3,48,96]{2,1,0:T(8,128)S(1)} %constant_dynamic-update-slice_fusion.refs_2_), channel_id=1, source_target_pairs={{0,4},{1,5},{2,6},{3,7},{4,0},{5,1},{6,2},{7,3},{8,12},{9,13},{10,... | collective-permute-start | bytes 165896 | tf_op jit(solution)/shard_map/ppermute | solution.py:386
  71.1 3.8 %collective-permute-start.34 = (f32[1,48,96]{2,1,0:T(8,128)S(1)}, f32[1,48,96]{2,1,0:T(8,128)S(1)}, u32[]{:S(2)}, u32[]{:S(2)}) collective-permute-start(f32[1,48,96]{2,1,0:T(8,128)S(1)} %bitcast.26), channel_id=1, source_target_pairs={{0,4},{1,5},{2,6},{3,7},{4,0},{5,1},{6,2},{7,3},{8,12},{9,13},{10,... | collective-permute-start | bytes 55304 | tf_op jit(solution)/shard_map/ppermute | solution.py:386

commit v5 on v1

--- a/solution.py
+++ b/solution.py
@@ -11,6 +11,7 @@
 BF16 = jnp.bfloat16
 LANES = 128
 GROUP = 16
+FOLDED = 16
 VMEM_LIMIT = 48 * 1024 * 1024
 
 
@@ -106,16 +107,61 @@
     return table(high), table(low)
 
 
-def blur_kernel(cube_ref, taps_x_ref, taps_y_ref, w_ref, xh_ref, xl_ref, *rest):
-    part_refs = rest[:8]
-    work_ref, kx_ref, ky_ref = rest[8:]
+def fold(square):
+    side = square.shape[0]
+    across = 2 * LANES // side
+    blocks = [square[first:first + 8] for first in range(0, side, 8)]
+    blocks += [jnp.zeros_like(blocks[0])] * (2 * across - len(blocks))
+    rest = jnp.zeros((8, 2 * LANES - across * side), F32)
+    return jnp.concatenate(
+        [jnp.concatenate(blocks[first:first + across] + [rest], axis=1) for first in (0, across)], axis=0)
+
+
+def unfold(folded, side):
+    across = 2 * LANES // side
+    blocks = []
+    for block in range(side // 8):
+        row, lane = 8 * (block // across), side * (block % across)
+        blocks.append(folded[row:row + 8, lane:lane + side])
+    return jnp.concatenate(blocks, axis=0)
+
+
+def in_vmem(count):
+    return [pl.BlockSpec(memory_space=pltpu.VMEM)] * count
+
+
+def band_gram(w_rows):
+    high, low = split(w_rows)
+    rank = w_rows.shape[0]
+    padded = jnp.concatenate([high, jnp.zeros((2 * LANES - rank, high.shape[1]), BF16)], axis=0)
+    padded_low = jnp.concatenate([low, jnp.zeros((2 * LANES - rank, low.shape[1]), BF16)], axis=0)
+    both = dot_nt(jnp.concatenate([high, low], axis=0), padded)
+    return both[:rank] + (both[rank:] + dot_nt(high, padded_low))
+
+
+def blur_kernel(cube_ref, taps_x_hbm, taps_y_hbm, w_hbm, xh_ref, xl_ref, keep_ref, give_ref,
+                taps_x_ref, taps_y_ref, w_ref, sems, work_ref, kx_ref, ky_ref):
     step = pl.program_id(0)
     taps = taps_x_ref.shape[0]
     margin = (taps - 1) // 2
     height = cube_ref.shape[1]
+    rank = w_ref.shape[0]
 
     @pl.when(step == 0)
     def _():
+        copies = [
+            pltpu.make_async_copy(taps_x_hbm, taps_x_ref, sems.at[0]),
+            pltpu.make_async_copy(taps_y_hbm, taps_y_ref, sems.at[1]),
+            pltpu.make_async_copy(w_hbm, w_ref, sems.at[2]),
+        ]
+        for copy in copies:
+            copy.start()
+        for copy in copies:
+            copy.wait()
+        gram = fold(band_gram(w_ref[...])[:, :rank])
+        for side in range(4):
+            keep_ref[side, 4 * rank:] = gram
+            give_ref[side, 4 * rank:] = gram
         normalized_taps(taps_x_ref, True, work_ref, kx_ref)
         normalized_taps(taps_y_ref, False, work_ref, ky_ref)
         kx_ref[...] = pltpu.roll(kx_ref[...], LANES - margin, 1)
@@ -149,118 +195,80 @@
     @pl.when(step == pl.num_programs(0) - 1)
     def _():
         planes = xh_ref.shape[1]
-        rank, band = w_ref.shape
+        band = w_ref.shape[1]
         me_sp = lax.axis_index("sp")
         me_bd = lax.axis_index("bd")
-        bands = lax.axis_size("bd")
-        pieces = lax.axis_size("sp")
-        tall = height // bands
-        wide = xh_ref.shape[2] // pieces
+        tall = height // lax.axis_size("bd")
+        wide = 2 * LANES // lax.axis_size("sp")
         shift = lax.rem(band - me_sp * planes, band)
         w_high, w_low = split(pltpu.roll(w_ref[...], shift, 1)[:, :planes])
         w_both = jnp.concatenate([w_high, w_low], axis=0)
-        for rel_bd in (1, 3, 0, 2):
-            first_row = lax.bitwise_xor(me_bd, rel_bd) * tall
-            sums = []
-            for row in range(tall):
-                both = dot(w_both, xh_ref[first_row + row])
-                sums.append(both[:rank] + (both[rank:] + dot(w_high, xl_ref[first_row + row])))
-            for column in range(2):
-                vectors = []
-                for quarter in range(2):
-                    vectors.append(exchange_blocks(
-                        [sums[4 * quarter + k][:, column * LANES:(column + 1) * LANES] for k in range(4)], wide))
-                for k in range(4):
-                    piece = jnp.concatenate([vectors[0][k], vectors[1][k]], axis=1)
-                    owner = column * 4 + k
-                    rel_sp = lax.bitwise_xor(me_sp, owner)
-                    inner = rel_sp // 2
-                    low_bit = rel_sp % 2
-                    base = (rel_bd % 2) * 4 + (rel_bd // 2) * 2
-
-                    @pl.when(low_bit == 0)
-                    def _():
-                        part_refs[base][inner] = piece
-
-                    @pl.when(low_bit == 1)
-                    def _():
-                        part_refs[base + 1][inner] = piece
+        for rel, part_ref in ((1, give_ref), (0, keep_ref)):
+            for row_side in range(2):
+                first_row = (2 * row_side + lax.bitwise_xor(me_bd % 2, rel)) * tall
+                sums = []
+                for row in range(tall):
+                    both = dot(w_both, xh_ref[first_row + row])
+                    sums.append(both[:rank] + (both[rank:] + dot(w_high, xl_ref[first_row + row])))
+                for column in range(2):
+                    quarters = [
+                        exchange_blocks(
+                            [value[:, column * LANES:(column + 1) * LANES] for value in sums[first:first + 4]], wide)
+                        for first in (0, 4)]
+                    for k in range(4):
+                        owner = column * 4 + k
+                        first = (owner // 2) * rank
+                        part_ref[2 * row_side + owner % 2, first:first + rank] = jnp.concatenate(
+                            [quarters[0][k], quarters[1][k]], axis=1)
 
 
 def blur_call(cube, taps_x, taps_y, w_rows):
     planes, height, length = cube.shape
     rank = w_rows.shape[0]
-    taps = taps_x.shape[0]
-    part = jax.ShapeDtypeStruct((4, rank, 256), F32)
+    part = jax.ShapeDtypeStruct((4, 4 * rank + FOLDED, 2 * LANES), F32)
+    image = (height, planes, length)
     whole = lambda shape: pl.BlockSpec(shape, lambda i: (0,) * len(shape))
     return pl.pallas_call(
         blur_kernel,
         grid=(planes // GROUP,),
-        out_shape=[jax.ShapeDtypeStruct((height, planes, length), BF16)] * 2 + [part] * 8,
-        in_specs=[
-            pl.BlockSpec((GROUP, height, length), lambda i: (i, 0, 0)),
-            whole(taps_x.shape), whole(taps_y.shape), whole(w_rows.shape),
-        ],
-        out_specs=[whole((height, planes, length))] * 2 + [whole(part.shape)] * 8,
-        scratch_shapes=[pltpu.VMEM((LANES, LANES), F32)] * 3,
+        out_shape=[jax.ShapeDtypeStruct(image, BF16)] * 2 + [part, part],
+        in_specs=[pl.BlockSpec((GROUP, height, length), lambda i: (i, 0, 0))]
+        + [pl.BlockSpec(memory_space=pltpu.HBM)] * 3,
+        out_specs=[whole(image)] * 2 + [whole(part.shape)] * 2,
+        scratch_shapes=[pltpu.VMEM(value.shape, F32) for value in (taps_x, taps_y, w_rows)]
+        + [pltpu.SemaphoreType.DMA((3,))] + [pltpu.VMEM((LANES, LANES), F32)] * 3,
         compiler_params=pltpu.CompilerParams(
             dimension_semantics=("arbitrary",), vmem_limit_bytes=VMEM_LIMIT),
     )(cube, taps_x, taps_y, w_rows)
 
 
-def gram_kernel(w_ref, out_ref):
-    high, low = split(w_ref[...])
-    both = jnp.concatenate([high, low], axis=0)
-    rank = w_ref.shape[0]
-    total = dot_nt(both, both)
-    out_ref[...] = total[:rank, :rank] + (total[rank:, :rank] + total[:rank, rank:]) + total[rank:, rank:]
-
-
-def gram_call(w_rows):
-    rank = w_rows.shape[0]
-    return pl.pallas_call(
-        gram_kernel,
-        out_shape=jax.ShapeDtypeStruct((rank, rank), F32),
-    )(w_rows)
-
-
-def update_h_kernel(n0, n1, n2, n3, g0, g1, g2, g3, h_ref, out_ref):
+def ratio_kernel(parts_ref, h_ref, out_ref):
     tall = h_ref.shape[0] // lax.axis_size("bd")
     first = pl.multiple_of(lax.axis_index("bd") * tall, tall)
     here = h_ref[pl.ds(first, tall)]
     here = jnp.transpose(here.reshape(-1, here.shape[2]))
-    gram = (g0[...] + g1[...]) + (g2[...] + g3[...])
-    numer = (n0[...] + n1[...]) + (n2[...] + n3[...])
-    out_ref[...] = here * numer / dot_exact(gram, here)
-
-
-def update_h_call(numer, gram, h_columns):
+    rows = parts_ref.shape[1]
+    folded = [parts_ref[k, rows - FOLDED:rows] for k in range(4)]
+    gram = 0.5 * unfold((folded[0] + folded[1]) + (folded[2] + folded[3]), here.shape[0])
+    out_ref[...] = here / dot_exact(gram, here)
+
+
+def ratio_call(parts, h_columns):
     return pl.pallas_call(
-        update_h_kernel,
-        out_shape=jax.ShapeDtypeStruct(numer[0].shape, F32),
-    )(*numer, *gram, h_columns)
-
-
-def update_w_kernel(xh_ref, xl_ref, w_ref, *rest):
-    part_refs = rest[:8]
-    w_out, h_out, all_ref = rest[8:]
-    height, planes, length = xh_ref.shape
+        ratio_kernel,
+        out_shape=jax.ShapeDtypeStruct((h_columns.shape[2], 2 * LANES), F32),
+        in_specs=in_vmem(2),
+        compiler_params=pltpu.CompilerParams(vmem_limit_bytes=VMEM_LIMIT),
+    )(parts, h_columns)
+
+
+def update_w_kernel(xh_ref, xl_ref, w_ref, all_ref, w_out, h_out):
+    height, planes, _ = xh_ref.shape
     rank, band = w_ref.shape
     me_sp = lax.axis_index("sp")
-    me_bd = lax.axis_index("bd")
     bands = lax.axis_size("bd")
-    pieces = lax.axis_size("sp")
     tall = height // bands
-    wide = length // pieces
-    for rel in range(bands * pieces):
-        slot, inner = rel // 4, rel % 4
-        rel_bd = (slot // 4) + 2 * ((slot // 2) % 2)
-        rel_sp = slot % 2 + 2 * inner
-        owner = lax.bitwise_xor(me_bd, rel_bd) * pieces + lax.bitwise_xor(me_sp, rel_sp)
-        all_ref[owner] = part_refs[slot][inner]
-    for part in range(bands):
-        mine = jnp.transpose(all_ref[part * pieces + me_sp])
-        h_out[part * tall:(part + 1) * tall] = mine.reshape(tall, wide, rank)
+    wide = 2 * LANES // lax.axis_size("sp")
     numer = jnp.zeros((rank, planes), F32)
     gram = jnp.zeros((rank, rank), F32)
     for part in range(bands):
@@ -268,7 +276,7 @@
         for column in range(2):
             for quarter in range(2):
                 vectors = exchange_blocks(
-                    [all_ref[part * pieces + column * 4 + k][:, quarter * LANES:(quarter + 1) * LANES]
+                    [all_ref[(column * 4 + k) * bands + part][:, quarter * LANES:(quarter + 1) * LANES]
                      for k in range(4)], wide)
                 for k in range(4):
                     rows[4 * quarter + k][column] = vectors[k]
@@ -279,44 +287,44 @@
             numer = numer + (product[:rank] + (product[rank:] + dot_nt(high, xl_ref[part * tall + row])))
             product = dot_nt(both, high)
             gram = gram + (product[:rank] + (product[rank:] + dot_nt(high, low)))
+        mine = jnp.transpose(all_ref[me_sp * bands + part])
+        h_out[part * tall:(part + 1) * tall] = mine.reshape(tall, wide, rank)
     shift = lax.rem(band - me_sp * planes, band)
     w_here = pltpu.roll(w_ref[...], shift, 1)[:, :planes]
-    w_out[...] = w_here * numer / dot_exact(gram, w_here)
-
-
-def update_w_call(x_high, x_low, w_rows, parts):
+    w_here = w_here * numer / dot_exact(gram, w_here)
+    for owner in range(w_out.shape[0]):
+        w_out[owner] = w_here
+
+
+def update_w_call(x_high, x_low, w_rows, gathered):
     height, planes, length = x_high.shape
     rank = w_rows.shape[0]
-    wide = length // lax.axis_size("sp")
+    pieces = lax.axis_size("sp")
     return pl.pallas_call(
         update_w_kernel,
         out_shape=[
-            jax.ShapeDtypeStruct((rank, planes), F32),
-            jax.ShapeDtypeStruct((height, wide, rank), F32),
+            jax.ShapeDtypeStruct((pieces, rank, planes), F32),
+            jax.ShapeDtypeStruct((height, length // pieces, rank), F32),
         ],
-        scratch_shapes=[pltpu.VMEM((4 * len(parts),) + parts[0].shape[1:], F32)],
+        in_specs=in_vmem(4),
         compiler_params=pltpu.CompilerParams(vmem_limit_bytes=VMEM_LIMIT),
-    )(x_high, x_low, w_rows, *parts)
-
-
-def gather_w_kernel(*refs):
-    part_refs = refs[:-2]
-    out_ref, all_ref = refs[-2:]
-    planes = part_refs[0].shape[1]
-    me_sp = lax.axis_index("sp")
-    for rel, part in enumerate(part_refs):
-        all_ref[lax.bitwise_xor(me_sp, rel), :, 0:planes] = part[...]
-    for owner in range(len(part_refs)):
-        out_ref[:, owner * planes:(owner + 1) * planes] = all_ref[owner][:, :planes]
-
-
-def gather_w_call(parts):
-    rank, planes = parts[0].shape
+    )(x_high, x_low, w_rows, gathered)
+
+
+def join_w_kernel(parts_ref, out_ref):
+    planes = parts_ref.shape[2]
+    for owner in range(parts_ref.shape[0]):
+        out_ref[:, owner * planes:(owner + 1) * planes] = parts_ref[owner]
+
+
+def join_w_call(parts):
+    pieces, rank, planes = parts.shape
     return pl.pallas_call(
-        gather_w_kernel,
-        out_shape=jax.ShapeDtypeStruct((rank, planes * len(parts)), F32),
-        scratch_shapes=[pltpu.VMEM((len(parts), rank, LANES), F32)],
-    )(*parts)
+        join_w_kernel,
+        out_shape=jax.ShapeDtypeStruct((rank, planes * pieces), F32),
+        in_specs=in_vmem(1),
+        compiler_params=pltpu.CompilerParams(vmem_limit_bytes=VMEM_LIMIT),
+    )(parts)
 
 
 def send(value, mask_sp, mask_bd):
@@ -329,30 +337,30 @@
     return lax.ppermute(value, ("sp", "bd"), pairs)
 
 
+def exchange(value, square):
+    pieces, bands = lax.axis_size("sp"), lax.axis_size("bd")
+    if square:
+        groups = [[(2 * z + s) * bands + 2 * b + core for b in range(2) for s in range(2)]
+                  for z in range(pieces // 2) for core in range(2)]
+    else:
+        groups = [[(2 * z + s) * bands + b for z in range(pieces // 2)] for s in range(2) for b in range(bands)]
+    return lax.all_to_all(value, ("sp", "bd"), 0, 0, axis_index_groups=groups, tiled=True)
+
+
 def local(cube, taps_x, taps_y, factor_w, factor_h):
-    bands = lax.axis_size("bd")
-    pieces = lax.axis_size("sp")
     w_rows = jnp.transpose(factor_w[0])
     taps_x = jnp.transpose(taps_x, (2, 0, 1))
     taps_y = jnp.transpose(taps_y, (2, 0, 1))
     h_columns = jnp.transpose(factor_h, (1, 2, 0))
-    gram = gram_call(w_rows)
-    grams = [gram] + [send(gram, 0, mask) for mask in range(1, bands)]
-    x_high, x_low, *parts = blur_call(cube[0], taps_x, taps_y, w_rows)
-    keep, give = parts[:4], parts[4:]
-    taken = [send(value, 0, 1) for value in give]
-    chip = [mine + other for mine, other in zip(keep, taken)]
-    around = [chip[0]] + [send(chip[k], k % 2, 2 * (k // 2)) for k in range(1, 4)]
-    square = [(around[0][k] + around[1][k]) + (around[2][k] + around[3][k]) for k in range(4)]
-    line = [square[0]] + [send(square[k], 2 * k, 0) for k in range(1, 4)]
-    h_piece = update_h_call(line, grams, h_columns)
-    h_line = [h_piece] + [send(h_piece, 2 * k, 0) for k in range(1, 4)]
-    h_line = jnp.stack(h_line)
-    h_parts = [h_line] + [send(h_line, k % 2, 2 * (k // 2)) for k in range(1, 4)]
-    h_parts = h_parts + [send(value, 0, 1) for value in h_parts]
-    w_piece, h_next = update_w_call(x_high, x_low, w_rows, h_parts)
-    w_pieces = [w_piece] + [send(w_piece, mask, 0) for mask in range(1, pieces)]
-    w_next = gather_w_call(w_pieces)
+    rank = w_rows.shape[0]
+    x_high, x_low, keep, give = blur_call(cube[0], taps_x, taps_y, w_rows)
+    square = exchange(keep + send(give, 0, 1), True)
+    line = jnp.sum(square[:, :4 * rank], axis=0).reshape(4, rank, 2 * LANES)
+    numer = jnp.sum(exchange(line, False), axis=0)
+    h_piece = ratio_call(square, h_columns) * numer
+    gathered = lax.all_gather(h_piece, ("sp", "bd"))
+    w_piece, h_next = update_w_call(x_high, x_low, w_rows, gathered)
+    w_next = join_w_call(lax.all_to_all(w_piece, "sp", 0, 0, tiled=True))
     return jnp.transpose(w_next)[None], jnp.transpose(h_next, (2, 0, 1))
 
 

time: 88 us -> 133 us (1.51)
  waiting for transfers between devices: 28.7 us -> 61.1 us
  blocking collectives: 0 us -> 30 us
  starting transfers between devices: 31.5 us -> 5.39 us
  between operations: 0.8 us -> 14.1 us
  Pallas kernels: 21.5 us -> 15.4 us
  local copies, waits for them, and re-layouts: 3.55 us -> 5.15 us
    all_gather x0 -> x1, waiting for transfers between devices: none -> 53.1 us  [local(): gathered = lax.all_gather(h_piece, ('sp', 'bd'))]
    ppermute x30 -> x1, starting transfers between devices: 31.5 us -> 0.52 us  [send(): return lax.ppermute(value, ('sp', 'bd'), pairs)]
    all_to_all x0 -> x2, blocking collectives: none -> 30 us  [the longest x1 17.5 us: exchange(): lax.all_to_all(value, ('sp', 'bd'), 0, 0, axis_index_groups=groups, tiled...]
    ppermute x30 -> x1, waiting for transfers between devices: 28.7 us -> 2.01 us  [send(): return lax.ppermute(value, ('sp', 'bd'), pairs)]
    all_to_all x0 -> x1, waiting for transfers between devices: none -> 5.96 us  [exchange(): lax.all_to_all(value, ('sp', 'bd'), 0, 0, axis_index_groups=groups, tiled...]
    all_to_all x0 -> x1, starting transfers between devices: none -> 4.87 us  [exchange(): lax.all_to_all(value, ('sp', 'bd'), 0, 0, axis_index_groups=groups, tiled...]
    pallas_call x4 -> x3, Pallas kernels: 9.06 us -> 4.47 us  [the longest x1 3.42 us: update_w_call(): pl.pallas_call(update_w_kernel, out_shape=[jax.ShapeDtypeStruct((pieces,...]
    unnamed x34 -> x16, local copies, waits for them, and re-layouts: 3.55 us -> 5.15 us
  transfers between devices with their start and end apart: 30 -> 3, of which waited for: 15 -> 3; matrix products, arithmetic and copies ran while one was open for 0% -> 0% of each run, Pallas kernels for 2% -> 0%
where the time goes in v5:
time: 133 us
  waiting for transfers between devices  61.1 us (46%)
  blocking collectives  30 us (23%)
  Pallas kernels  15.4 us (12%)
  between operations  14.1 us (11%)
  starting transfers between devices  5.39 us (4%)
  local copies, waits for them, and re-layouts  5.15 us (4%)
  other arithmetic  1.48 us (1%)
    all_gather x1, waiting for transfers between devices, local(): gathered = lax.all_gather(h_piece, ('sp', 'bd'))  53.1 us
    all_to_all x1, blocking collectives, exchange(): lax.all_to_all(value, ('sp', 'bd'), 0, 0, axis_index_groups=groups, tiled...  17.5 us
    all_to_all x1, blocking collectives, local(): w_next = join_w_call(lax.all_to_all(w_piece, 'sp', 0, 0, tiled=True))  12.5 us
    pallas_call x1, Pallas kernels, blur_call(): pl.pallas_call(blur_kernel, grid=(planes // GROUP,), out_shape=[jax.Shape...  10.9 us
    all_to_all x1, waiting for transfers between devices, exchange(): lax.all_to_all(value, ('sp', 'bd'), 0, 0, axis_index_groups=groups, tiled...  5.96 us
    unnamed x16, local copies, waits for them, and re-layouts  5.15 us
    all_to_all x1, starting transfers between devices, exchange(): lax.all_to_all(value, ('sp', 'bd'), 0, 0, axis_index_groups=groups, tiled...  4.87 us
    pallas_call x1, Pallas kernels, update_w_call(): pl.pallas_call(update_w_kernel, out_shape=[jax.ShapeDtypeStruct((pieces,...  3.42 us
  transfers between devices with their start and end apart: 3, of which 3 were waited for; matrix products, arithmetic and copies ran while one was open for 0% of the time, Pallas kernels for 0%

profile of v5, /device:TPU:0, one launch (start us, length us, event | category | flops | bytes accessed | tf_op | source)
XLA Modules:
  0.0 132.6 jit_solution(5052386832289396711)
XLA Ops:
  7.2 0.0 copy-start.3
  7.2 0.9 copy-done.3
  8.1 0.0 copy-start.6
  8.1 0.7 copy-done.6
  8.8 0.0 copy-start.7
  8.8 0.7 copy-done.7
  9.5 10.9 %shard_map.68 = (bf16[32,96,256]{2,1,0:T(8,128)(2,1)S(1)}, bf16[32,96,256]{2,1,0:T(8,128)(2,1)S(1)}, f32[4,208,256]{2,1,0:T(8,128)S(1)}, f32[4,208,256]{2,1,0:T(8,128)S(1)}) custom-call(f32[96,32,256]{2,1,0:T(8,128)} %bitcast.19, f32[25,1,96]{2,1,0:T(1,128)S(1)} %bitcast.17, f32[25,1,96]{2,1,0:T(1,128)S(1)} %bitcast.18, f32[48,768]{1,0:T(8,128)S(1)} %bitcast.14), custom_call_target="tpu_custom_call" | custom-call | tf_op jit(solution)/shard_map/pallas_call | solution.py:231
  20.4 0.0 copy-start
  20.4 0.5 collective-permute-start
  21.0 2.0 %collective-permute-done = f32[4,208,256]{2,1,0:T(8,128)S(1)} collective-permute-done((f32[4,208,256]{2,1,0:T(8,128)S(1)}, f32[4,208,256]{2,1,0:T(8,128)S(1)}, u32[]{:S(2)}, u32[]{:S(2)}) %collective-permute-start) | collective-permute-done | bytes 852000 | tf_op jit(solution)/shard_map/ppermute | solution.py:337
  23.0 0.1 add.3
  23.1 0.0 copy-start.5
  23.1 17.5 %all_to_all.15.parts_ref = f32[4,208,256]{2,1,0:T(8,128)S(1)} all-to-all(f32[4,208,256]{2,1,0:T(8,128)S(1)} %add.3), channel_id=1, replica_groups={{0,4,2,6},{1,5,3,7},{8,12,10,14},{9,13,11,15},{16,20,18,22},{17,21,19,2..., dimensions={0} | all-to-all | bytes 1703936 | tf_op jit(solution)/shard_map/all_to_all | solution.py:347
  40.6 0.0 copy-done
  40.6 0.0 copy-start.4
  40.6 0.7 slice_reduce_fusion
  41.4 4.9 %all-to-all-start.1 = ((f32[4,48,256]{2,1,0:T(8,128)}), f32[4,48,256]{2,1,0:T(8,128)S(1)}, u32[]{:S(2)}, u32[]{:S(2)}) async-start(f32[4,48,256]{2,1,0:T(8,128)} %bitcast.6), calls=%async_computation.1 | async-start | bytes 393216 | tf_op jit(solution)/shard_map/all_to_all | solution.py:347
  46.2 0.0 all-gather.3.cloned.1.call-start
  46.2 0.0 copy-done.5
  46.2 0.3 shard_map.69
  46.5 6.0 %all-to-all-done.1 = f32[4,48,256]{2,1,0:T(8,128)S(1)} async-done(((f32[4,48,256]{2,1,0:T(8,128)}), f32[4,48,256]{2,1,0:T(8,128)S(1)}, u32[]{:S(2)}, u32[]{:S(2)}) %all-to-all-start.1) | async-done | bytes 196640 | tf_op jit(solution)/shard_map/all_to_all | solution.py:347
  52.5 0.6 mul.3
  53.1 0.0 all-gather.3.cloned.1.call-update
  53.1 53.1 %all-gather.3.cloned.1.call-done = f32[1536,256]{1,0:T(8,128)} async-done(((f32[48,256]{1,0:T(8,128)}), f32[1536,256]{1,0:T(8,128)}) %all-gather.3.cloned.1.call-update) | async-done | bytes 1572880 | tf_op jit(solution)/shard_map/all_gather | solution.py:361
  106.2 0.0 copy-done.4
  106.2 0.0 copy-start.1
  106.2 1.4 %copy-done.1 = bf16[32,96,256]{2,1,0:T(8,128)(2,1)S(1)} copy-done((bf16[32,96,256]{2,1,0:T(8,128)(2,1)S(1)}, bf16[32,96,256]{2,1,0:T(8,128)(2,1)}, u32[]{:S(2)}) %copy-start.1) | copy-done | bytes 1572888
  107.6 0.0 copy-start.2
  107.6 1.4 %copy-done.2 = f32[1536,256]{1,0:T(8,128)S(1)} copy-done((f32[1536,256]{1,0:T(8,128)S(1)}, f32[1536,256]{1,0:T(8,128)}, u32[]{:S(2)}) %copy-start.2) | copy-done | bytes 1572888
  109.1 3.4 %shard_map.70 = (f32[8,48,96]{2,1,0:T(8,128)S(1)}, f32[32,32,48]{2,1,0:T(8,128)}) custom-call(bf16[32,96,256]{2,1,0:T(8,128)(2,1)S(1)} %get-tuple-element.8.xh_ref, bf16[32,96,256]{2,1,0:T(8,128)(2,1)S(1)} %copy-done.1, f32[48,768]{1,0:T(8,128)S(1)} %bitcast.15, f32[32,48,256]{2,1,0:T(8,128)S(1)} %bitcast.13), custom_call_target="tpu_custom_call" | custom-call | tf_op jit(solution)/shard_map/pallas_call | solution.py:303
  112.5 12.5 %all_to_all.16.parts_ref = f32[8,48,96]{2,1,0:T(8,128)S(1)} all-to-all(f32[8,48,96]{2,1,0:T(8,128)S(1)} %get-tuple-element.12), channel_id=1, replica_groups=mesh['sp'=8,'bd'=4] {'sp'}, dimensions={0} | all-to-all | bytes 294912 | tf_op jit(solution)/shard_map/all_to_all | solution.py:363
  125.0 0.8 shard_map.71
  (1 shorter events, 0.0 us)
Async XLA Ops:
  7.2 0.9 copy-start.3
  8.1 0.7 copy-start.6
  8.8 0.7 copy-start.7
  20.4 20.2 %copy-start = (bf16[32,96,256]{2,1,0:T(8,128)(2,1)}, bf16[32,96,256]{2,1,0:T(8,128)(2,1)S(1)}, u32[]{:S(2)}) copy-start(bf16[32,96,256]{2,1,0:T(8,128)(2,1)S(1)} %get-tuple-element.9.xl_ref) | copy-start | bytes 4718596
  20.4 2.5 %collective-permute-start = (f32[4,208,256]{2,1,0:T(8,128)S(1)}, f32[4,208,256]{2,1,0:T(8,128)S(1)}, u32[]{:S(2)}, u32[]{:S(2)}) collective-permute-start(f32[4,208,256]{2,1,0:T(8,128)S(1)} %get-tuple-element.11), channel_id=1, source_target_pairs={{0,1},{1,0},{2,3},{3,2},{4,5},{5,4},{6,7},{7,6},{8,9},{9,8},{10,11... | collective-permute-start | bytes 2555912 | tf_op jit(solution)/shard_map/ppermute | solution.py:337
  23.1 23.1 %copy-start.5 = (f32[48,32,32]{0,2,1:T(8,128)S(1)}, f32[48,32,32]{0,2,1:T(8,128)}, u32[]{:S(2)}) copy-start(f32[48,32,32]{0,2,1:T(8,128)} %param.9) | copy-start | bytes 589828
  40.6 65.6 %copy-start.4 = (f32[1,768,48]{1,2,0:T(8,128)S(1)}, f32[1,768,48]{1,2,0:T(8,128)}, u32[]{:S(2)}) copy-start(f32[1,768,48]{1,2,0:T(8,128)} %param.8) | copy-start | bytes 442372
  41.4 11.1 %all-to-all-start.1 = ((f32[4,48,256]{2,1,0:T(8,128)}), f32[4,48,256]{2,1,0:T(8,128)S(1)}, u32[]{:S(2)}, u32[]{:S(2)}) async-start(f32[4,48,256]{2,1,0:T(8,128)} %bitcast.6), calls=%async_computation.1 | async-start | bytes 393216 | tf_op jit(solution)/shard_map/all_to_all | solution.py:347
  46.2 60.0 %all-gather.3.cloned.1.call-start = ((), (), s32[]{:S(2)}) async-start(), calls=%async_computation.3 | async-start | bytes 1622016 | tf_op jit(solution)/shard_map/all_gather | solution.py:361
  106.2 1.4 %copy-start.1 = (bf16[32,96,256]{2,1,0:T(8,128)(2,1)S(1)}, bf16[32,96,256]{2,1,0:T(8,128)(2,1)}, u32[]{:S(2)}) copy-start(bf16[32,96,256]{2,1,0:T(8,128)(2,1)} %copy-done) | copy-start | bytes 4718596
  107.6 1.4 %copy-start.2 = (f32[1536,256]{1,0:T(8,128)S(1)}, f32[1536,256]{1,0:T(8,128)}, u32[]{:S(2)}) copy-start(f32[1536,256]{1,0:T(8,128)} %all-gather.3.cloned.1.call-done) | copy-start | bytes 4718596
Sparse Core Ops, SparseCore 0:
  53.3 52.9 all-gather.2

commit v6 on v4

--- a/solution.py
+++ b/solution.py
@@ -66,27 +66,29 @@
     out_ref[...] = jnp.transpose(values / total)
 
 
-def column_table(row, margin):
-    circulant = pltpu.roll(jnp.broadcast_to(row, (LANES, LANES)), 0, 1, stride=1, stride_axis=0)
-    high = circulant.astype(BF16).astype(F32)
-    low = circulant - high
-    src = lax.broadcasted_iota(jnp.int32, (LANES, LANES), 0)
-    dst = lax.broadcasted_iota(jnp.int32, (LANES, LANES), 1)
-    near = jnp.abs(dst - src) <= margin
-    edge = GROUP
-    wraps_up = (src - dst)[LANES - edge:] > LANES // 2
-    wraps_down = (dst - src)[:edge] > LANES // 2
-    empty = jnp.zeros((LANES - edge, LANES), BF16)
-
-    def table(part):
-        middle = jnp.where(near, part, 0.0).astype(BF16)
-        upper = jnp.where(wraps_up, part[LANES - edge:], 0.0).astype(BF16)
-        lower = jnp.where(wraps_down, part[:edge], 0.0).astype(BF16)
-        top = jnp.concatenate([middle, jnp.concatenate([empty, upper], axis=0)], axis=1)
-        bottom = jnp.concatenate([jnp.concatenate([lower, empty], axis=0), middle], axis=1)
-        return jnp.concatenate([top, bottom], axis=0)
-
-    return table(high), table(low)
+def blur_plane(plane, row, taps):
+    margin = (taps - 1) // 2
+    step = LANES - 2 * margin
+    table = pltpu.roll(jnp.broadcast_to(row, (LANES, LANES)), 0, 1, stride=1, stride_axis=0)
+    table = jnp.concatenate(split(table), axis=1)
+    left, right = plane[:, :LANES], plane[:, LANES:]
+    lane = lax.broadcasted_iota(jnp.int32, left.shape, 1)
+    zero = jnp.zeros_like(left)
+    windows = [
+        jnp.where(lane >= margin, pltpu.roll(left, margin, 1), zero),
+        jnp.where(lane < 3 * margin, pltpu.roll(left, 3 * margin, 1), pltpu.roll(right, 3 * margin, 1)),
+        jnp.where(lane < 5 * margin, pltpu.roll(right, 5 * margin, 1), zero),
+    ]
+    high, low = split(jnp.concatenate(windows, axis=0))
+    product = dot(jnp.concatenate([high, low], axis=0), table)
+    rows = high.shape[0]
+    blocks = product[:rows, :LANES] + (product[:rows, LANES:] + product[rows:, :LANES])
+    height = plane.shape[0]
+    first, second, third = [blocks[k * height:(k + 1) * height] for k in range(3)]
+    second = pltpu.roll(second, step, 1)
+    third = pltpu.roll(third, 2 * step - LANES, 1)
+    return jnp.concatenate(
+        [jnp.where(lane < step, first, second), jnp.where(lane < 2 * step - LANES, second, third)], axis=1)
 
 
 def row_table(base, margin, height):
@@ -160,7 +162,7 @@
         give_0[PIECES * rank:] = gram
         normalized_taps(taps_x_ref, True, work_ref, kx_ref)
         normalized_taps(taps_y_ref, False, work_ref, ky_ref)
-        kx_ref[...] = pltpu.roll(kx_ref[...], LANES - margin, 1)
+        kx_ref[...] = pltpu.roll(kx_ref[...], LANES - 2 * margin, 1)
         per_vector = LANES // height
         place = lax.broadcasted_iota(jnp.int32, (LANES, LANES), 0) % per_vector
         values = ky_ref[...]
@@ -174,10 +176,7 @@
         done = []
         for plane in range(8 * half, 8 * half + 8):
             row = kx_ref[pl.ds(step * GROUP + plane, 1), :]
-            table_high, table_low = column_table(row, margin)
-            high, low = split(cube_ref[plane])
-            both = dot(jnp.concatenate([high, low], axis=0), table_high)
-            done.append(both[:height] + (both[height:] + dot(high, table_low)))
+            done.append(blur_plane(cube_ref[plane], row, taps))
         high, low = split(jnp.concatenate(done, axis=0))
         rows = ky_ref[pl.ds(pl.multiple_of(step * GROUP + 8 * half, 8), 8), :]
         table_high, table_low = row_table(rows, margin, height)
@@ -197,15 +196,20 @@
         tall = height // lax.axis_size("bd")
         wide = 2 * LANES // lax.axis_size("sp")
         shift = lax.rem(band - me_sp * planes, band)
-        w_high, w_low = split(pltpu.roll(w_ref[...], shift, 1)[:, :planes])
-        w_both = jnp.concatenate([w_high, w_low], axis=0)
+        w_here = pltpu.roll(w_ref[...], shift, 1)[:, :2 * LANES]
+        lane = lax.broadcasted_iota(jnp.int32, w_here.shape, 1)
+        w_here = jnp.where(lane < planes, w_here, 0.0)
+        w_high = w_here.astype(BF16).astype(F32)
+        w_both = jnp.concatenate([w_high + pltpu.roll(w_high, planes, 1), w_here - w_high], axis=0)
+        w_both = w_both.astype(BF16)[:, :2 * planes]
         for chain in range(2):
             for rel_bd in (1, 3, 0, 2):
                 first_row = lax.bitwise_xor(me_bd, rel_bd) * tall + 4 * chain
                 sums = []
                 for row in range(4):
-                    both = dot(w_both, xh_ref[first_row + row])
-                    sums.append(both[:rank] + (both[rank:] + dot(w_high, xl_ref[first_row + row])))
+                    image = jnp.concatenate([xh_ref[first_row + row], xl_ref[first_row + row]], axis=0)
+                    both = dot(w_both, image)
+                    sums.append(both[:rank] + both[rank:])
                 refs = ((keep_0, give_0), (keep_1, give_1))[chain]
                 for column in range(2):
                     pieces = exchange_blocks(
@@ -260,8 +264,9 @@
     )(mine, other, h_columns)
 
 
-def accumulate(xh_ref, xl_ref, part_refs, all_ref, h_out, chain, numer, gram):
-    height, rank = xh_ref.shape[0], all_ref.shape[1]
+def accumulate(xh_ref, xl_ref, part_refs, all_ref, h_out, chain, total):
+    height, planes, _ = xh_ref.shape
+    rank = all_ref.shape[1]
     me_sp = lax.axis_index("sp")
     me_bd = lax.axis_index("bd")
     bands = lax.axis_size("bd")
@@ -279,27 +284,22 @@
         halves = [
             exchange_blocks([all_ref[part * pieces + column * 4 + k] for k in range(4)], wide)
             for column in range(2)]
-        for row in range(4):
-            high, low = split(jnp.concatenate([halves[0][row], halves[1][row]], axis=1))
-            both = jnp.concatenate([high, low], axis=0)
-            product = dot_nt(both, xh_ref[first_row + row])
-            numer = numer + (product[:rank] + (product[rank:] + dot_nt(high, xl_ref[first_row + row])))
-            product = dot_nt(both, high)
-            gram = gram + (product[:rank] + (product[rank:] + dot_nt(high, low)))
+        rows = jnp.concatenate([halves[column][row] for row in range(4) for column in range(2)], axis=1)
+        high, low = split(rows)
+        here = jnp.concatenate([high, low], axis=0)
+        image = [
+            jnp.concatenate([ref[first_row + row] for row in range(4)], axis=1) for ref in (xh_ref, xl_ref)]
+        total = total + dot_nt(jnp.concatenate(image + [here], axis=0), here)
         mine = jnp.transpose(all_ref[part * pieces + me_sp])
         h_out[first_row:first_row + 4] = mine.reshape(4, wide, rank)
-    return numer, gram
+    return total
 
 
 def first_kernel(xh_ref, xl_ref, *rest):
     part_refs = rest[:8]
-    numer_out, gram_out, h_out, all_ref = rest[8:]
-    planes, rank = xh_ref.shape[1], all_ref.shape[1]
-    numer, gram = accumulate(
-        xh_ref, xl_ref, part_refs, all_ref, h_out, 0,
-        jnp.zeros((rank, planes), F32), jnp.zeros((rank, rank), F32))
-    numer_out[...] = numer
-    gram_out[...] = gram
+    total_out, h_out, all_ref = rest[8:]
+    total_out[...] = accumulate(
+        xh_ref, xl_ref, part_refs, all_ref, h_out, 0, jnp.zeros(total_out.shape, F32))
     tall = xh_ref.shape[0] // lax.axis_size("bd")
     for part in range(lax.axis_size("bd")):
         h_out[part * tall + 4:(part + 1) * tall] = jnp.zeros((tall - 4,) + h_out.shape[1:], F32)
@@ -311,8 +311,7 @@
     return pl.pallas_call(
         first_kernel,
         out_shape=[
-            jax.ShapeDtypeStruct((rank, planes), F32),
-            jax.ShapeDtypeStruct((rank, rank), F32),
+            jax.ShapeDtypeStruct((2 * (planes + rank), 2 * rank), F32),
             jax.ShapeDtypeStruct((height, length // lax.axis_size("sp"), rank), F32),
         ],
         in_specs=in_vmem(2 + len(parts)),
@@ -321,31 +320,34 @@
     )(x_high, x_low, *parts)
 
 
-def second_kernel(xh_ref, xl_ref, w_ref, numer_ref, gram_ref, h_ref, *rest):
+def second_kernel(xh_ref, xl_ref, w_ref, total_ref, h_ref, *rest):
     part_refs = rest[:8]
     w_out, h_out, all_ref = rest[8:]
     planes = xh_ref.shape[1]
-    band = w_ref.shape[1]
+    rank, band = w_ref.shape
     me_sp = lax.axis_index("sp")
     h_out[...] = h_ref[...]
-    numer, gram = accumulate(
-        xh_ref, xl_ref, part_refs, all_ref, h_out, 1, numer_ref[...], gram_ref[...])
+    total = accumulate(xh_ref, xl_ref, part_refs, all_ref, h_out, 1, total_ref[...])
+    numer = total[:planes, :rank] + (total[:planes, rank:] + total[planes:2 * planes, :rank])
+    gram = total[2 * planes:]
+    gram = gram[:rank, :rank] + (gram[:rank, rank:] + gram[rank:, :rank])
     shift = lax.rem(band - me_sp * planes, band)
     w_here = pltpu.roll(w_ref[...], shift, 1)[:, :planes]
-    w_out[...] = w_here * numer / dot_exact(gram, w_here)
-
-
-def second_call(x_high, x_low, w_rows, numer, gram, h_half, parts):
+    w_out[...] = w_here * jnp.transpose(numer) / dot_exact(gram, w_here)
+
+
+def second_call(x_high, x_low, w_rows, total, h_half, parts):
+    planes, rank = x_high.shape[1], w_rows.shape[0]
     return pl.pallas_call(
         second_kernel,
         out_shape=[
-            jax.ShapeDtypeStruct(numer.shape, F32),
+            jax.ShapeDtypeStruct((rank, planes), F32),
             jax.ShapeDtypeStruct(h_half.shape, F32),
         ],
-        in_specs=in_vmem(6 + len(parts)),
+        in_specs=in_vmem(5 + len(parts)),
         scratch_shapes=[pltpu.VMEM((32,) + parts[0].shape[1:], F32)],
         compiler_params=pltpu.CompilerParams(vmem_limit_bytes=VMEM_LIMIT),
-    )(x_high, x_low, w_rows, numer, gram, h_half, *parts)
+    )(x_high, x_low, w_rows, total, h_half, *parts)
 
 
 def gather_w_kernel(*refs):
@@ -362,7 +364,7 @@
         out_ref[:, owner * planes:(owner + 1) * planes] = all_ref[owner][:, :planes]
 
 
-RING = (0, 1, 2, 4, 6, 3, 5, 7)
+RING = (0, 1, 2, 3, 4, 5, 6, 7)
 
 
 def gather_w_call(parts):
@@ -418,11 +420,10 @@
         h_line = jnp.stack([h_piece] + [send(h_piece, 2 * k, 0) for k in range(1, 4)])
         parts = [h_line] + around([h_line] * 4)
         rounds.append(parts + [send(value, 0, 1) for value in parts])
-    numer, gram_h, h_half = first_call(x_high, x_low, rounds[0])
-    w_piece, h_next = second_call(x_high, x_low, w_rows, numer, gram_h, h_half, rounds[1])
-    w_piece = w_piece[None]
-    w_line = jnp.concatenate([send(w_piece, mask, 0) for mask in (2, 4, 6)])
-    w_next = gather_w_call([w_piece, send(w_piece, 1, 0), w_line, send(w_line, 1, 0)])
+    total, h_half = first_call(x_high, x_low, rounds[0])
+    w_piece, h_next = second_call(x_high, x_low, w_rows, total, h_half, rounds[1])
+    w_pair = jnp.stack([w_piece, send(w_piece, 1, 0)])
+    w_next = gather_w_call([w_pair] + [send(w_pair, 2 * k, 0) for k in range(1, 4)])
     return jnp.transpose(w_next)[None], jnp.transpose(h_next, (2, 0, 1))
 
 

time: 76 us -> 75.3 us (level)
  waiting for transfers between devices: 14.7 us -> 13.2 us
  Pallas kernels: 15.7 us -> 16.6 us
    ppermute x39 -> x38, waiting for transfers between devices: 14.7 us -> 13.2 us  [send(): return lax.ppermute(value, ('sp', 'bd'), pairs)]
    pallas_call x1, Pallas kernels: 11 us -> 12.2 us  [blur_call(): pl.pallas_call(blur_kernel, grid=(planes // GROUP,), out_shape=[jax.Shape...]
    ppermute x39 -> x38, starting transfers between devices: 42 us -> 41.8 us  [send(): return lax.ppermute(value, ('sp', 'bd'), pairs)]
    unnamed x12 -> x10, local copies, waits for them, and re-layouts: 2.33 us -> 2.33 us
  transfers between devices with their start and end apart: 39 -> 38, of which waited for: 10 -> 10; matrix products, arithmetic and copies ran while one was open for 0% -> 0% of each run, Pallas kernels for 2% -> 2%
where the time goes in v6:
time: 75.3 us; the launch traced here: 75 us
  starting transfers between devices  41.8 us (56%)
  Pallas kernels  16.6 us (22%)
  waiting for transfers between devices  13.2 us (18%)
  local copies, waits for them, and re-layouts  2.33 us (3%)
  between operations  0.78 us (1%)
    ppermute x38, starting transfers between devices, send(): return lax.ppermute(value, ('sp', 'bd'), pairs)  41.8 us
    ppermute x38, waiting for transfers between devices, send(): return lax.ppermute(value, ('sp', 'bd'), pairs)  13.2 us
    pallas_call x1, Pallas kernels, blur_call(): pl.pallas_call(blur_kernel, grid=(planes // GROUP,), out_shape=[jax.Shape...  12.2 us
    unnamed x10, local copies, waits for them, and re-layouts  2.33 us
    pallas_call x1, Pallas kernels, second_call(): pl.pallas_call(second_kernel, out_shape=[jax.ShapeDtypeStruct((rank, plan...  2.27 us
  transfers between devices with their start and end apart: 38, of which 10 were waited for; matrix products, arithmetic and copies ran while one was open for 0% of the time, Pallas kernels for 2%

profile of v6, /device:TPU:0, one launch (start us, length us, event | category | flops | bytes accessed | tf_op | source)
XLA Modules:
  0.0 75.0 jit_solution(7398199674051859983)
XLA Ops:
  0.6 0.0 copy-start
  0.6 0.9 %copy-done = f32[1,768,48]{1,2,0:T(8,128)S(1)} copy-done((f32[1,768,48]{1,2,0:T(8,128)S(1)}, f32[1,768,48]{1,2,0:T(8,128)}, u32[]{:S(2)}) %copy-start) | copy-done | bytes 147480
  1.5 0.7 copy-done.3
  2.3 0.7 copy-done.4
  3.0 12.2 %shard_map.68 = (bf16[32,96,256]{2,1,0:T(8,128)(2,1)S(1)}, bf16[32,96,256]{2,1,0:T(8,128)(2,1)S(1)}, f32[792,128]{1,0:T(8,128)S(1)}, f32[792,128]{1,0:T(8,128)S(...) custom-call(f32[96,32,256]{2,1,0:T(8,128)} %bitcast.27, f32[25,1,96]{2,1,0:T(1,128)S(1)} %bitcast.25, ...), custom_call_target="tpu_custom_call" | custom-call | tf_op jit(solution)/shard_map/pallas_call | solution.py:231
  15.2 0.5 collective-permute-start.17
  15.7 0.1 collective-permute-start
  15.8 1.3 %collective-permute-done.17 = f32[768,128]{1,0:T(8,128)S(1)} collective-permute-done((f32[768,128]{1,0:T(8,128)S(1)}, f32[768,128]{1,0:T(8,128)S(1)}, u32[]{:S(2)}, u32[]{:S(2)}) %collective-permute-start.17) | collective-permute-done | bytes 393248 | tf_op jit(solution)/shard_map/ppermute | solution.py:388
  17.1 3.9 %collective-permute-start.20 = (f32[192,128]{1,0:T(8,128)S(1)}, f32[192,128]{1,0:T(8,128)S(1)}, u32[]{:S(2)}, u32[]{:S(2)}) collective-permute-start(f32[192,128]{1,0:T(8,128)S(1)} %get-tuple-element.30), channel_id=1, source_target_pairs={{0,6},{1,7},{2,4},{3,5},{4,2},{5,3},{6,0},{7,1},{8,14},{9,15},{10,... | collective-permute-start | bytes 294920 | tf_op jit(solution)/shard_map/ppermute | solution.py:388
  21.0 0.5 collective-permute-start.19
  21.5 0.1 collective-permute-start.18
  21.6 0.0 collective-permute-done
  21.7 2.9 %collective-permute-start.3 = (f32[192,128]{1,0:T(8,128)S(1)}, f32[192,128]{1,0:T(8,128)S(1)}, u32[]{:S(2)}, u32[]{:S(2)}) collective-permute-start(f32[192,128]{1,0:T(8,128)S(1)} %get-tuple-element.27), channel_id=1, source_target_pairs={{0,6},{1,7},{2,4},{3,5},{4,2},{5,3},{6,0},{7,1},{8,14},{9,15},{10,... | collective-permute-start | bytes 294920 | tf_op jit(solution)/shard_map/ppermute | solution.py:388
  24.6 0.5 collective-permute-start.2
  25.1 0.0 collective-permute-done.20
  25.2 1.4 %collective-permute-start.1 = (f32[216,128]{1,0:T(8,128)S(1)}, f32[216,128]{1,0:T(8,128)S(1)}, u32[]{:S(2)}, u32[]{:S(2)}) collective-permute-start(f32[216,128]{1,0:T(8,128)S(1)} %slice_add_fusion.mine_ref), channel_id=1, source_target_pairs={{0,2},{1,3},{2,0},{3,1},{4,6},{5,7},{6,4},{7,5},{8,10},{9,11},{10,... | collective-permute-start | bytes 331784 | tf_op jit(solution)/shard_map/ppermute | solution.py:388
  26.5 0.9 %collective-permute-done.19 = f32[192,128]{1,0:T(8,128)S(1)} collective-permute-done((f32[192,128]{1,0:T(8,128)S(1)}, f32[192,128]{1,0:T(8,128)S(1)}, u32[]{:S(2)}, u32[]{:S(2)}) %collective-permute-start.19) | collective-permute-done | bytes 98336 | tf_op jit(solution)/shard_map/ppermute | solution.py:388
  27.5 0.0 collective-permute-done.18
  27.5 3.9 %collective-permute-start.23 = (f32[48,128]{1,0:T(8,128)S(1)}, f32[48,128]{1,0:T(8,128)S(1)}, u32[]{:S(2)}, u32[]{:S(2)}) collective-permute-start(f32[48,128]{1,0:T(8,128)S(1)} %get-tuple-element.36), channel_id=1, source_target_pairs={{0,24},{1,25},{2,26},{3,27},{4,28},{5,29},{6,30},{7,31},{8,16},{9,... | collective-permute-start | bytes 73736 | tf_op jit(solution)/shard_map/ppermute | solution.py:388
  31.4 0.6 collective-permute-start.21
  32.1 0.0 collective-permute-done.2
  32.1 3.8 %collective-permute-start.6 = (f32[48,128]{1,0:T(8,128)S(1)}, f32[48,128]{1,0:T(8,128)S(1)}, u32[]{:S(2)}, u32[]{:S(2)}) collective-permute-start(f32[48,128]{1,0:T(8,128)S(1)} %get-tuple-element.33), channel_id=1, source_target_pairs={{0,24},{1,25},{2,26},{3,27},{4,28},{5,29},{6,30},{7,31},{8,16},{9,... | collective-permute-start | bytes 73736 | tf_op jit(solution)/shard_map/ppermute | solution.py:388
  35.9 0.3 shard_map.69
  36.2 0.0 collective-permute-done.23
  36.2 0.7 collective-permute-start.4
  36.9 0.0 collective-permute-done.22
  36.9 0.0 collective-permute-done.21
  36.9 3.8 %collective-permute-start.26 = (f32[48,128]{1,0:T(8,128)S(1)}, f32[48,128]{1,0:T(8,128)S(1)}, u32[]{:S(2)}, u32[]{:S(2)}) collective-permute-start(f32[48,128]{1,0:T(8,128)S(1)} %fusion.6), channel_id=1, source_target_pairs={{0,24},{1,25},{2,26},{3,27},{4,28},{5,29},{6,30},{7,31},{8,16},{9,... | collective-permute-start | bytes 73736 | tf_op jit(solution)/shard_map/ppermute | solution.py:388
  40.7 0.6 collective-permute-start.24
  41.4 0.0 collective-permute-done.4
  41.4 3.8 %collective-permute-start.9 = (f32[48,128]{1,0:T(8,128)S(1)}, f32[48,128]{1,0:T(8,128)S(1)}, u32[]{:S(2)}, u32[]{:S(2)}) collective-permute-start(f32[48,128]{1,0:T(8,128)S(1)} %fusion.13), channel_id=1, source_target_pairs={{0,24},{1,25},{2,26},{3,27},{4,28},{5,29},{6,30},{7,31},{8,16},{9,... | collective-permute-start | bytes 73736 | tf_op jit(solution)/shard_map/ppermute | solution.py:388
  45.2 0.0 collective-permute-start.8
  45.2 0.0 collective-permute-done.26
  45.2 0.6 collective-permute-start.7
  45.9 0.0 collective-permute-done.25
  45.9 0.0 collective-permute-done.24
  45.9 1.4 %collective-permute-start.29 = (f32[4,48,128]{2,1,0:T(8,128)S(1)}, f32[4,48,128]{2,1,0:T(8,128)S(1)}, u32[]{:S(2)}, u32[]{:S(2)}) collective-permute-start(f32[4,48,128]{2,1,0:T(8,128)S(1)} %pad_maximum_fusion.1.rest_0_), channel_id=1, source_target_pairs={{0,6},{1,7},{2,4},{3,5},{4,2},{5,3},{6,0},{7,1},{8,14},{9,15},{10,... | collective-permute-start | bytes 294920 | tf_op jit(solution)/shard_map/ppermute | solution.py:388
  47.3 1.4 %collective-permute-start.28 = (f32[4,48,128]{2,1,0:T(8,128)S(1)}, f32[4,48,128]{2,1,0:T(8,128)S(1)}, u32[]{:S(2)}, u32[]{:S(2)}) collective-permute-start(f32[4,48,128]{2,1,0:T(8,128)S(1)} %pad_maximum_fusion.1.rest_0_), channel_id=1, source_target_pairs={{0,2},{1,3},{2,0},{3,1},{4,6},{5,7},{6,4},{7,5},{8,10},{9,11},{10,... | collective-permute-start | bytes 294920 | tf_op jit(solution)/shard_map/ppermute | solution.py:388
  48.7 0.0 collective-permute-done.9
  48.7 1.3 %collective-permute-done.8 = f32[48,128]{1,0:T(8,128)S(1)} collective-permute-done((f32[48,128]{1,0:T(8,128)S(1)}, f32[48,128]{1,0:T(8,128)S(1)}, u32[]{:S(2)}, u32[]{:S(2)}) %collective-permute-start.8) | collective-permute-done | bytes 24608 | tf_op jit(solution)/shard_map/ppermute | solution.py:388
  50.0 1.1 %collective-permute-start.12 = (f32[4,48,128]{2,1,0:T(8,128)S(1)}, f32[4,48,128]{2,1,0:T(8,128)S(1)}, u32[]{:S(2)}, u32[]{:S(2)}) collective-permute-start(f32[4,48,128]{2,1,0:T(8,128)S(1)} %pad_maximum_fusion.rest_0_), channel_id=1, source_target_pairs={{0,6},{1,7},{2,4},{3,5},{4,2},{5,3},{6,0},{7,1},{8,14},{9,15},{10,... | collective-permute-start | bytes 294920 | tf_op jit(solution)/shard_map/ppermute | solution.py:388
  51.0 1.6 %collective-permute-start.11 = (f32[4,48,128]{2,1,0:T(8,128)S(1)}, f32[4,48,128]{2,1,0:T(8,128)S(1)}, u32[]{:S(2)}, u32[]{:S(2)}) collective-permute-start(f32[4,48,128]{2,1,0:T(8,128)S(1)} %pad_maximum_fusion.rest_0_), channel_id=1, source_target_pairs={{0,2},{1,3},{2,0},{3,1},{4,6},{5,7},{6,4},{7,5},{8,10},{9,11},{10,... | collective-permute-start | bytes 294920 | tf_op jit(solution)/shard_map/ppermute | solution.py:388
  52.6 0.9 %collective-permute-start.10 = (f32[4,48,128]{2,1,0:T(8,128)S(1)}, f32[4,48,128]{2,1,0:T(8,128)S(1)}, u32[]{:S(2)}, u32[]{:S(2)}) collective-permute-start(f32[4,48,128]{2,1,0:T(8,128)S(1)} %pad_maximum_fusion.rest_0_), channel_id=1, source_target_pairs={{0,4},{1,5},{2,6},{3,7},{4,0},{5,1},{6,2},{7,3},{8,12},{9,13},{10,... | collective-permute-start | bytes 294920 | tf_op jit(solution)/shard_map/ppermute | solution.py:388
  53.5 1.1 %collective-permute-start.27 = (f32[4,48,128]{2,1,0:T(8,128)S(1)}, f32[4,48,128]{2,1,0:T(8,128)S(1)}, u32[]{:S(2)}, u32[]{:S(2)}) collective-permute-start(f32[4,48,128]{2,1,0:T(8,128)S(1)} %pad_maximum_fusion.1.rest_0_), channel_id=1, source_target_pairs={{0,4},{1,5},{2,6},{3,7},{4,0},{5,1},{6,2},{7,3},{8,12},{9,13},{10,... | collective-permute-start | bytes 294920 | tf_op jit(solution)/shard_map/ppermute | solution.py:388
  54.6 1.0 %collective-permute-done.12.rest_3_ = f32[4,48,128]{2,1,0:T(8,128)S(1)} collective-permute-done((f32[4,48,128]{2,1,0:T(8,128)S(1)}, f32[4,48,128]{2,1,0:T(8,128)S(1)}, u32[]{:S(2)}, u32[]{:S(2)}) %collective-permute-start.12) | collective-permute-done | bytes 98336 | tf_op jit(solution)/shard_map/ppermute | solution.py:388
  55.6 0.0 collective-permute-start.16
  55.6 0.9 %collective-permute-done.11.rest_2_ = f32[4,48,128]{2,1,0:T(8,128)S(1)} collective-permute-done((f32[4,48,128]{2,1,0:T(8,128)S(1)}, f32[4,48,128]{2,1,0:T(8,128)S(1)}, u32[]{:S(2)}, u32[]{:S(2)}) %collective-permute-start.11) | collective-permute-done | bytes 98336 | tf_op jit(solution)/shard_map/ppermute | solution.py:388
  56.6 0.6 collective-permute-done.10.rest_1_
  57.2 0.0 collective-permute-start.14
  57.2 1.0 %collective-permute-done.27.rest_1_ = f32[4,48,128]{2,1,0:T(8,128)S(1)} collective-permute-done((f32[4,48,128]{2,1,0:T(8,128)S(1)}, f32[4,48,128]{2,1,0:T(8,128)S(1)}, u32[]{:S(2)}, u32[]{:S(2)}) %collective-permute-start.27) | collective-permute-done | bytes 98336 | tf_op jit(solution)/shard_map/ppermute | solution.py:388
  58.3 0.5 collective-permute-start.33
  58.8 0.1 collective-permute-start.32
  58.8 0.0 collective-permute-done.15.rest_6_
  58.9 0.4 collective-permute-start.31
  59.3 1.1 %shard_map.70 = (f32[288,96]{1,0:T(8,128)S(1)}, f32[32,32,48]{2,1,0:T(8,128)S(1)}) custom-call(bf16[32,96,256]{2,1,0:T(8,128)(2,1)S(1)} %get-tuple-element.14.xh_ref, bf16[32,96,256]{2,1,0:T(8,128)(2,1)S(1)} %get-tuple-element.15.xl_ref, f32[4,48,128]{2,1,0:T(8,128)S(1)} %pad_maximum_fusion.rest_0_, f32[4,48,128]{2,1,0:T(8,128)S(1)} %collective-permute-done.10.rest_1_, ...), custom_call_target="tpu_custom_call" | custom-call | tf_op jit(solution)/shard_map/pallas_call | solution.py:311
  60.4 0.0 collective-permute-done.33.rest_7_
  60.4 2.3 %shard_map.71 = (f32[48,96]{1,0:T(8,128)S(1)}, f32[32,32,48]{2,1,0:T(8,128)}) custom-call(bf16[32,96,256]{2,1,0:T(8,128)(2,1)S(1)} %get-tuple-element.14.xh_ref, bf16[32,96,256]{2,1,0:T(8,128)(2,1)S(1)} %get-tuple-element.15.xl_ref, f32[48,768]{1,0:T(8,128)S(1)} %bitcast.22, f32[288,96]{1,0:T(8,128)S(1)} %get-tuple-element.19.total_ref, ...), custom_call_target="tpu_custom_call" | custom-call | tf_op jit(solution)/shard_map/pallas_call | solution.py:341
  62.7 1.0 %collective-permute-start.34 = (f32[48,96]{1,0:T(8,128)S(1)}, f32[48,96]{1,0:T(8,128)S(1)}, u32[]{:S(2)}, u32[]{:S(2)}) collective-permute-start(f32[48,96]{1,0:T(8,128)S(1)} %get-tuple-element.24), channel_id=1, source_target_pairs={{0,4},{1,5},{2,6},{3,7},{4,0},{5,1},{6,2},{7,3},{8,12},{9,13},{10,... | collective-permute-start | bytes 55304 | tf_op jit(solution)/shard_map/ppermute | solution.py:388
  63.7 2.8 %collective-permute-done.34 = f32[48,96]{1,0:T(8,128)S(1)} collective-permute-done((f32[48,96]{1,0:T(8,128)S(1)}, f32[48,96]{1,0:T(8,128)S(1)}, u32[]{:S(2)}, u32[]{:S(2)}) %collective-permute-start.34) | collective-permute-done | bytes 18464 | tf_op jit(solution)/shard_map/ppermute | solution.py:388
  66.5 2.7 %collective-permute-start.37 = (f32[2,48,96]{2,1,0:T(8,128)S(1)}, f32[2,48,96]{2,1,0:T(8,128)S(1)}, u32[]{:S(2)}, u32[]{:S(2)}) collective-permute-start(f32[2,48,96]{2,1,0:T(8,128)S(1)} %pad_maximum_fusion.2.refs_0_), channel_id=1, source_target_pairs={{0,24},{1,25},{2,26},{3,27},{4,28},{5,29},{6,30},{7,31},{8,16},{9,... | collective-permute-start | bytes 110600 | tf_op jit(solution)/shard_map/ppermute | solution.py:388
  69.2 1.8 %collective-permute-start.35 = (f32[2,48,96]{2,1,0:T(8,128)S(1)}, f32[2,48,96]{2,1,0:T(8,128)S(1)}, u32[]{:S(2)}, u32[]{:S(2)}) collective-permute-start(f32[2,48,96]{2,1,0:T(8,128)S(1)} %pad_maximum_fusion.2.refs_0_), channel_id=1, source_target_pairs={{0,8},{1,9},{2,10},{3,11},{4,12},{5,13},{6,14},{7,15},{8,0},{9,1},... | collective-permute-start | bytes 110600 | tf_op jit(solution)/shard_map/ppermute | solution.py:388
  71.0 1.6 %collective-permute-done.37.refs_3_ = f32[2,48,96]{2,1,0:T(8,128)S(1)} collective-permute-done((f32[2,48,96]{2,1,0:T(8,128)S(1)}, f32[2,48,96]{2,1,0:T(8,128)S(1)}, u32[]{:S(2)}, u32[]{:S(2)}) %collective-permute-start.37) | collective-permute-done | bytes 36896 | tf_op jit(solution)/shard_map/ppermute | solution.py:388
  72.6 1.6 %collective-permute-done.36.refs_2_ = f32[2,48,96]{2,1,0:T(8,128)S(1)} collective-permute-done((f32[2,48,96]{2,1,0:T(8,128)S(1)}, f32[2,48,96]{2,1,0:T(8,128)S(1)}, u32[]{:S(2)}, u32[]{:S(2)}) %collective-permute-start.36) | collective-permute-done | bytes 36896 | tf_op jit(solution)/shard_map/ppermute | solution.py:388
  74.2 0.8 %shard_map.72 = f32[48,768]{1,0:T(8,128)} custom-call(f32[2,48,96]{2,1,0:T(8,128)S(1)} %pad_maximum_fusion.2.refs_0_, f32[2,48,96]{2,1,0:T(8,128)S(1)} %collective-permute-done.35.refs_1_, f32[2,48,96]{2,1,0:T(8,128)S(1)} %collective-permute-done.36.refs_2_, f32[2,48,96]{2,1,0:T(8,128)S(1)} %collective-permute-done.37.refs_3_), custom_call_target="tpu_custom_call" | custom-call | tf_op jit(solution)/shard_map/pallas_call | solution.py:372
  (37 shorter events, 0.3 us)
Async XLA Ops:
  0.6 0.9 %copy-start = (f32[1,768,48]{1,2,0:T(8,128)S(1)}, f32[1,768,48]{1,2,0:T(8,128)}, u32[]{:S(2)}) copy-start(f32[1,768,48]{1,2,0:T(8,128)} %param.8) | copy-start | bytes 442372
  1.5 0.7 copy-start.3
  2.3 0.7 copy-start.4
  15.2 1.9 %collective-permute-start.17 = (f32[768,128]{1,0:T(8,128)S(1)}, f32[768,128]{1,0:T(8,128)S(1)}, u32[]{:S(2)}, u32[]{:S(2)}) collective-permute-start(f32[768,128]{1,0:T(8,128)S(1)} %get-tuple-element.23), channel_id=1, source_target_pairs={{0,1},{1,0},{2,3},{3,2},{4,5},{5,4},{6,7},{7,6},{8,9},{9,8},{10,11... | collective-permute-start | bytes 1179656 | tf_op jit(solution)/shard_map/ppermute | solution.py:388
  15.7 5.9 %collective-permute-start = (f32[792,128]{1,0:T(8,128)S(1)}, f32[792,128]{1,0:T(8,128)S(1)}, u32[]{:S(2)}, u32[]{:S(2)}) collective-permute-start(f32[792,128]{1,0:T(8,128)S(1)} %get-tuple-element.17), channel_id=1, source_target_pairs={{0,1},{1,0},{2,3},{3,2},{4,5},{5,4},{6,7},{7,6},{8,9},{9,8},{10,11... | collective-permute-start | bytes 1216520 | tf_op jit(solution)/shard_map/ppermute | solution.py:388
  17.1 18.8 %copy-start.2 = (f32[48,32,32]{0,2,1:T(8,128)S(1)}, f32[48,32,32]{0,2,1:T(8,128)}, u32[]{:S(2)}) copy-start(f32[48,32,32]{0,2,1:T(8,128)} %param.9) | copy-start | bytes 589828
  17.1 8.0 %collective-permute-start.20 = (f32[192,128]{1,0:T(8,128)S(1)}, f32[192,128]{1,0:T(8,128)S(1)}, u32[]{:S(2)}, u32[]{:S(2)}) collective-permute-start(f32[192,128]{1,0:T(8,128)S(1)} %get-tuple-element.30), channel_id=1, source_target_pairs={{0,6},{1,7},{2,4},{3,5},{4,2},{5,3},{6,0},{7,1},{8,14},{9,15},{10,... | collective-permute-start | bytes 294920 | tf_op jit(solution)/shard_map/ppermute | solution.py:388
  21.0 6.5 %collective-permute-start.19 = (f32[192,128]{1,0:T(8,128)S(1)}, f32[192,128]{1,0:T(8,128)S(1)}, u32[]{:S(2)}, u32[]{:S(2)}) collective-permute-start(f32[192,128]{1,0:T(8,128)S(1)} %get-tuple-element.31), channel_id=1, source_target_pairs={{0,2},{1,3},{2,0},{3,1},{4,6},{5,7},{6,4},{7,5},{8,10},{9,11},{10,... | collective-permute-start | bytes 294920 | tf_op jit(solution)/shard_map/ppermute | solution.py:388
  21.5 6.0 %collective-permute-start.18 = (f32[192,128]{1,0:T(8,128)S(1)}, f32[192,128]{1,0:T(8,128)S(1)}, u32[]{:S(2)}, u32[]{:S(2)}) collective-permute-start(f32[192,128]{1,0:T(8,128)S(1)} %get-tuple-element.32), channel_id=1, source_target_pairs={{0,4},{1,5},{2,6},{3,7},{4,0},{5,1},{6,2},{7,3},{8,12},{9,13},{10,... | collective-permute-start | bytes 294920 | tf_op jit(solution)/shard_map/ppermute | solution.py:388
  21.7 9.7 %collective-permute-start.3 = (f32[192,128]{1,0:T(8,128)S(1)}, f32[192,128]{1,0:T(8,128)S(1)}, u32[]{:S(2)}, u32[]{:S(2)}) collective-permute-start(f32[192,128]{1,0:T(8,128)S(1)} %get-tuple-element.27), channel_id=1, source_target_pairs={{0,6},{1,7},{2,4},{3,5},{4,2},{5,3},{6,0},{7,1},{8,14},{9,15},{10,... | collective-permute-start | bytes 294920 | tf_op jit(solution)/shard_map/ppermute | solution.py:388
  24.6 7.5 %collective-permute-start.2 = (f32[192,128]{1,0:T(8,128)S(1)}, f32[192,128]{1,0:T(8,128)S(1)}, u32[]{:S(2)}, u32[]{:S(2)}) collective-permute-start(f32[192,128]{1,0:T(8,128)S(1)} %get-tuple-element.28), channel_id=1, source_target_pairs={{0,4},{1,5},{2,6},{3,7},{4,0},{5,1},{6,2},{7,3},{8,12},{9,13},{10,... | collective-permute-start | bytes 294920 | tf_op jit(solution)/shard_map/ppermute | solution.py:388
  25.2 6.9 %collective-permute-start.1 = (f32[216,128]{1,0:T(8,128)S(1)}, f32[216,128]{1,0:T(8,128)S(1)}, u32[]{:S(2)}, u32[]{:S(2)}) collective-permute-start(f32[216,128]{1,0:T(8,128)S(1)} %slice_add_fusion.mine_ref), channel_id=1, source_target_pairs={{0,2},{1,3},{2,0},{3,1},{4,6},{5,7},{6,4},{7,5},{8,10},{9,11},{10,... | collective-permute-start | bytes 331784 | tf_op jit(solution)/shard_map/ppermute | solution.py:388
  27.5 8.7 %collective-permute-start.23 = (f32[48,128]{1,0:T(8,128)S(1)}, f32[48,128]{1,0:T(8,128)S(1)}, u32[]{:S(2)}, u32[]{:S(2)}) collective-permute-start(f32[48,128]{1,0:T(8,128)S(1)} %get-tuple-element.36), channel_id=1, source_target_pairs={{0,24},{1,25},{2,26},{3,27},{4,28},{5,29},{6,30},{7,31},{8,16},{9,... | collective-permute-start | bytes 73736 | tf_op jit(solution)/shard_map/ppermute | solution.py:388
  31.4 5.5 %collective-permute-start.22 = (f32[48,128]{1,0:T(8,128)S(1)}, f32[48,128]{1,0:T(8,128)S(1)}, u32[]{:S(2)}, u32[]{:S(2)}) collective-permute-start(f32[48,128]{1,0:T(8,128)S(1)} %get-tuple-element.37), channel_id=1, source_target_pairs={{0,16},{1,17},{2,18},{3,19},{4,20},{5,21},{6,22},{7,23},{8,24},{9,... | collective-permute-start | bytes 73736 | tf_op jit(solution)/shard_map/ppermute | solution.py:388
  31.4 5.5 %collective-permute-start.21 = (f32[48,128]{1,0:T(8,128)S(1)}, f32[48,128]{1,0:T(8,128)S(1)}, u32[]{:S(2)}, u32[]{:S(2)}) collective-permute-start(f32[48,128]{1,0:T(8,128)S(1)} %get-tuple-element.38), channel_id=1, source_target_pairs={{0,8},{1,9},{2,10},{3,11},{4,12},{5,13},{6,14},{7,15},{8,0},{9,1},... | collective-permute-start | bytes 73736 | tf_op jit(solution)/shard_map/ppermute | solution.py:388
  32.1 8.7 %collective-permute-start.6 = (f32[48,128]{1,0:T(8,128)S(1)}, f32[48,128]{1,0:T(8,128)S(1)}, u32[]{:S(2)}, u32[]{:S(2)}) collective-permute-start(f32[48,128]{1,0:T(8,128)S(1)} %get-tuple-element.33), channel_id=1, source_target_pairs={{0,24},{1,25},{2,26},{3,27},{4,28},{5,29},{6,30},{7,31},{8,16},{9,... | collective-permute-start | bytes 73736 | tf_op jit(solution)/shard_map/ppermute | solution.py:388
  35.9 5.5 %collective-permute-start.5 = (f32[48,128]{1,0:T(8,128)S(1)}, f32[48,128]{1,0:T(8,128)S(1)}, u32[]{:S(2)}, u32[]{:S(2)}) collective-permute-start(f32[48,128]{1,0:T(8,128)S(1)} %get-tuple-element.34), channel_id=1, source_target_pairs={{0,16},{1,17},{2,18},{3,19},{4,20},{5,21},{6,22},{7,23},{8,24},{9,... | collective-permute-start | bytes 73736 | tf_op jit(solution)/shard_map/ppermute | solution.py:388
  36.2 5.2 %collective-permute-start.4 = (f32[48,128]{1,0:T(8,128)S(1)}, f32[48,128]{1,0:T(8,128)S(1)}, u32[]{:S(2)}, u32[]{:S(2)}) collective-permute-start(f32[48,128]{1,0:T(8,128)S(1)} %get-tuple-element.35), channel_id=1, source_target_pairs={{0,8},{1,9},{2,10},{3,11},{4,12},{5,13},{6,14},{7,15},{8,0},{9,1},... | collective-permute-start | bytes 73736 | tf_op jit(solution)/shard_map/ppermute | solution.py:388
  36.9 8.3 %collective-permute-start.26 = (f32[48,128]{1,0:T(8,128)S(1)}, f32[48,128]{1,0:T(8,128)S(1)}, u32[]{:S(2)}, u32[]{:S(2)}) collective-permute-start(f32[48,128]{1,0:T(8,128)S(1)} %fusion.6), channel_id=1, source_target_pairs={{0,24},{1,25},{2,26},{3,27},{4,28},{5,29},{6,30},{7,31},{8,16},{9,... | collective-permute-start | bytes 73736 | tf_op jit(solution)/shard_map/ppermute | solution.py:388
  40.7 5.1 %collective-permute-start.25 = (f32[48,128]{1,0:T(8,128)S(1)}, f32[48,128]{1,0:T(8,128)S(1)}, u32[]{:S(2)}, u32[]{:S(2)}) collective-permute-start(f32[48,128]{1,0:T(8,128)S(1)} %fusion.6), channel_id=1, source_target_pairs={{0,16},{1,17},{2,18},{3,19},{4,20},{5,21},{6,22},{7,23},{8,24},{9,... | collective-permute-start | bytes 73736 | tf_op jit(solution)/shard_map/ppermute | solution.py:388
  40.7 5.1 %collective-permute-start.24 = (f32[48,128]{1,0:T(8,128)S(1)}, f32[48,128]{1,0:T(8,128)S(1)}, u32[]{:S(2)}, u32[]{:S(2)}) collective-permute-start(f32[48,128]{1,0:T(8,128)S(1)} %fusion.6), channel_id=1, source_target_pairs={{0,8},{1,9},{2,10},{3,11},{4,12},{5,13},{6,14},{7,15},{8,0},{9,1},... | collective-permute-start | bytes 73736 | tf_op jit(solution)/shard_map/ppermute | solution.py:388
  41.4 7.3 %collective-permute-start.9 = (f32[48,128]{1,0:T(8,128)S(1)}, f32[48,128]{1,0:T(8,128)S(1)}, u32[]{:S(2)}, u32[]{:S(2)}) collective-permute-start(f32[48,128]{1,0:T(8,128)S(1)} %fusion.13), channel_id=1, source_target_pairs={{0,24},{1,25},{2,26},{3,27},{4,28},{5,29},{6,30},{7,31},{8,16},{9,... | collective-permute-start | bytes 73736 | tf_op jit(solution)/shard_map/ppermute | solution.py:388
  45.2 4.7 %collective-permute-start.8 = (f32[48,128]{1,0:T(8,128)S(1)}, f32[48,128]{1,0:T(8,128)S(1)}, u32[]{:S(2)}, u32[]{:S(2)}) collective-permute-start(f32[48,128]{1,0:T(8,128)S(1)} %fusion.13), channel_id=1, source_target_pairs={{0,16},{1,17},{2,18},{3,19},{4,20},{5,21},{6,22},{7,23},{8,24},{9,... | collective-permute-start | bytes 73736 | tf_op jit(solution)/shard_map/ppermute | solution.py:388
  45.2 4.7 %collective-permute-start.7 = (f32[48,128]{1,0:T(8,128)S(1)}, f32[48,128]{1,0:T(8,128)S(1)}, u32[]{:S(2)}, u32[]{:S(2)}) collective-permute-start(f32[48,128]{1,0:T(8,128)S(1)} %fusion.13), channel_id=1, source_target_pairs={{0,8},{1,9},{2,10},{3,11},{4,12},{5,13},{6,14},{7,15},{8,0},{9,1},... | collective-permute-start | bytes 73736 | tf_op jit(solution)/shard_map/ppermute | solution.py:388
  45.9 7.6 %collective-permute-start.29 = (f32[4,48,128]{2,1,0:T(8,128)S(1)}, f32[4,48,128]{2,1,0:T(8,128)S(1)}, u32[]{:S(2)}, u32[]{:S(2)}) collective-permute-start(f32[4,48,128]{2,1,0:T(8,128)S(1)} %pad_maximum_fusion.1.rest_0_), channel_id=1, source_target_pairs={{0,6},{1,7},{2,4},{3,5},{4,2},{5,3},{6,0},{7,1},{8,14},{9,15},{10,... | collective-permute-start | bytes 294920 | tf_op jit(solution)/shard_map/ppermute | solution.py:388
  47.3 7.4 %collective-permute-start.28 = (f32[4,48,128]{2,1,0:T(8,128)S(1)}, f32[4,48,128]{2,1,0:T(8,128)S(1)}, u32[]{:S(2)}, u32[]{:S(2)}) collective-permute-start(f32[4,48,128]{2,1,0:T(8,128)S(1)} %pad_maximum_fusion.1.rest_0_), channel_id=1, source_target_pairs={{0,2},{1,3},{2,0},{3,1},{4,6},{5,7},{6,4},{7,5},{8,10},{9,11},{10,... | collective-permute-start | bytes 294920 | tf_op jit(solution)/shard_map/ppermute | solution.py:388
  50.0 5.7 %collective-permute-start.12 = (f32[4,48,128]{2,1,0:T(8,128)S(1)}, f32[4,48,128]{2,1,0:T(8,128)S(1)}, u32[]{:S(2)}, u32[]{:S(2)}) collective-permute-start(f32[4,48,128]{2,1,0:T(8,128)S(1)} %pad_maximum_fusion.rest_0_), channel_id=1, source_target_pairs={{0,6},{1,7},{2,4},{3,5},{4,2},{5,3},{6,0},{7,1},{8,14},{9,15},{10,... | collective-permute-start | bytes 294920 | tf_op jit(solution)/shard_map/ppermute | solution.py:388
  51.0 5.6 %collective-permute-start.11 = (f32[4,48,128]{2,1,0:T(8,128)S(1)}, f32[4,48,128]{2,1,0:T(8,128)S(1)}, u32[]{:S(2)}, u32[]{:S(2)}) collective-permute-start(f32[4,48,128]{2,1,0:T(8,128)S(1)} %pad_maximum_fusion.rest_0_), channel_id=1, source_target_pairs={{0,2},{1,3},{2,0},{3,1},{4,6},{5,7},{6,4},{7,5},{8,10},{9,11},{10,... | collective-permute-start | bytes 294920 | tf_op jit(solution)/shard_map/ppermute | solution.py:388
  52.6 4.6 %collective-permute-start.10 = (f32[4,48,128]{2,1,0:T(8,128)S(1)}, f32[4,48,128]{2,1,0:T(8,128)S(1)}, u32[]{:S(2)}, u32[]{:S(2)}) collective-permute-start(f32[4,48,128]{2,1,0:T(8,128)S(1)} %pad_maximum_fusion.rest_0_), channel_id=1, source_target_pairs={{0,4},{1,5},{2,6},{3,7},{4,0},{5,1},{6,2},{7,3},{8,12},{9,13},{10,... | collective-permute-start | bytes 294920 | tf_op jit(solution)/shard_map/ppermute | solution.py:388
  53.5 4.7 %collective-permute-start.27 = (f32[4,48,128]{2,1,0:T(8,128)S(1)}, f32[4,48,128]{2,1,0:T(8,128)S(1)}, u32[]{:S(2)}, u32[]{:S(2)}) collective-permute-start(f32[4,48,128]{2,1,0:T(8,128)S(1)} %pad_maximum_fusion.1.rest_0_), channel_id=1, source_target_pairs={{0,4},{1,5},{2,6},{3,7},{4,0},{5,1},{6,2},{7,3},{8,12},{9,13},{10,... | collective-permute-start | bytes 294920 | tf_op jit(solution)/shard_map/ppermute | solution.py:388
  54.6 3.6 %collective-permute-start.13 = (f32[4,48,128]{2,1,0:T(8,128)S(1)}, f32[4,48,128]{2,1,0:T(8,128)S(1)}, u32[]{:S(2)}, u32[]{:S(2)}) collective-permute-start(f32[4,48,128]{2,1,0:T(8,128)S(1)} %pad_maximum_fusion.rest_0_), channel_id=1, source_target_pairs={{0,1},{1,0},{2,3},{3,2},{4,5},{5,4},{6,7},{7,6},{8,9},{9,8},{10,11... | collective-permute-start | bytes 294920 | tf_op jit(solution)/shard_map/ppermute | solution.py:388
  55.6 3.1 %collective-permute-start.16 = (f32[4,48,128]{2,1,0:T(8,128)S(1)}, f32[4,48,128]{2,1,0:T(8,128)S(1)}, u32[]{:S(2)}, u32[]{:S(2)}) collective-permute-start(f32[4,48,128]{2,1,0:T(8,128)S(1)} %collective-permute-done.12.rest_3_), channel_id=1, source_target_pairs={{0,1},{1,0},{2,3},{3,2},{4,5},{5,4},{6,7},{7,6},{8,9},{9,8},{10,11... | collective-permute-start | bytes 294920 | tf_op jit(solution)/shard_map/ppermute | solution.py:388
  56.6 2.3 %collective-permute-start.15 = (f32[4,48,128]{2,1,0:T(8,128)S(1)}, f32[4,48,128]{2,1,0:T(8,128)S(1)}, u32[]{:S(2)}, u32[]{:S(2)}) collective-permute-start(f32[4,48,128]{2,1,0:T(8,128)S(1)} %collective-permute-done.11.rest_2_), channel_id=1, source_target_pairs={{0,1},{1,0},{2,3},{3,2},{4,5},{5,4},{6,7},{7,6},{8,9},{9,8},{10,11... | collective-permute-start | bytes 294920 | tf_op jit(solution)/shard_map/ppermute | solution.py:388
  57.2 2.1 %collective-permute-start.14 = (f32[4,48,128]{2,1,0:T(8,128)S(1)}, f32[4,48,128]{2,1,0:T(8,128)S(1)}, u32[]{:S(2)}, u32[]{:S(2)}) collective-permute-start(f32[4,48,128]{2,1,0:T(8,128)S(1)} %collective-permute-done.10.rest_1_), channel_id=1, source_target_pairs={{0,1},{1,0},{2,3},{3,2},{4,5},{5,4},{6,7},{7,6},{8,9},{9,8},{10,11... | collective-permute-start | bytes 294920 | tf_op jit(solution)/shard_map/ppermute | solution.py:388
  58.3 2.1 %collective-permute-start.30 = (f32[4,48,128]{2,1,0:T(8,128)S(1)}, f32[4,48,128]{2,1,0:T(8,128)S(1)}, u32[]{:S(2)}, u32[]{:S(2)}) collective-permute-start(f32[4,48,128]{2,1,0:T(8,128)S(1)} %pad_maximum_fusion.1.rest_0_), channel_id=1, source_target_pairs={{0,1},{1,0},{2,3},{3,2},{4,5},{5,4},{6,7},{7,6},{8,9},{9,8},{10,11... | collective-permute-start | bytes 294920 | tf_op jit(solution)/shard_map/ppermute | solution.py:388
  58.3 2.1 %collective-permute-start.33 = (f32[4,48,128]{2,1,0:T(8,128)S(1)}, f32[4,48,128]{2,1,0:T(8,128)S(1)}, u32[]{:S(2)}, u32[]{:S(2)}) collective-permute-start(f32[4,48,128]{2,1,0:T(8,128)S(1)} %collective-permute-done.29.rest_3_), channel_id=1, source_target_pairs={{0,1},{1,0},{2,3},{3,2},{4,5},{5,4},{6,7},{7,6},{8,9},{9,8},{10,11... | collective-permute-start | bytes 294920 | tf_op jit(solution)/shard_map/ppermute | solution.py:388
  58.8 1.6 %collective-permute-start.32 = (f32[4,48,128]{2,1,0:T(8,128)S(1)}, f32[4,48,128]{2,1,0:T(8,128)S(1)}, u32[]{:S(2)}, u32[]{:S(2)}) collective-permute-start(f32[4,48,128]{2,1,0:T(8,128)S(1)} %collective-permute-done.28.rest_2_), channel_id=1, source_target_pairs={{0,1},{1,0},{2,3},{3,2},{4,5},{5,4},{6,7},{7,6},{8,9},{9,8},{10,11... | collective-permute-start | bytes 294920 | tf_op jit(solution)/shard_map/ppermute | solution.py:388
  58.9 1.6 %collective-permute-start.31 = (f32[4,48,128]{2,1,0:T(8,128)S(1)}, f32[4,48,128]{2,1,0:T(8,128)S(1)}, u32[]{:S(2)}, u32[]{:S(2)}) collective-permute-start(f32[4,48,128]{2,1,0:T(8,128)S(1)} %collective-permute-done.27.rest_1_), channel_id=1, source_target_pairs={{0,1},{1,0},{2,3},{3,2},{4,5},{5,4},{6,7},{7,6},{8,9},{9,8},{10,11... | collective-permute-start | bytes 294920 | tf_op jit(solution)/shard_map/ppermute | solution.py:388
  59.3 1.1 %copy-start.1 = (f32[1,768,48]{1,2,0:T(8,128)S(1)}, f32[1,768,48]{1,2,0:T(8,128)}, u32[]{:S(2)}) copy-start(f32[1,768,48]{1,2,0:T(8,128)} %param.8) | copy-start | bytes 442372
  62.7 3.8 %collective-permute-start.34 = (f32[48,96]{1,0:T(8,128)S(1)}, f32[48,96]{1,0:T(8,128)S(1)}, u32[]{:S(2)}, u32[]{:S(2)}) collective-permute-start(f32[48,96]{1,0:T(8,128)S(1)} %get-tuple-element.24), channel_id=1, source_target_pairs={{0,4},{1,5},{2,6},{3,7},{4,0},{5,1},{6,2},{7,3},{8,12},{9,13},{10,... | collective-permute-start | bytes 55304 | tf_op jit(solution)/shard_map/ppermute | solution.py:388
  66.5 6.1 %collective-permute-start.37 = (f32[2,48,96]{2,1,0:T(8,128)S(1)}, f32[2,48,96]{2,1,0:T(8,128)S(1)}, u32[]{:S(2)}, u32[]{:S(2)}) collective-permute-start(f32[2,48,96]{2,1,0:T(8,128)S(1)} %pad_maximum_fusion.2.refs_0_), channel_id=1, source_target_pairs={{0,24},{1,25},{2,26},{3,27},{4,28},{5,29},{6,30},{7,31},{8,16},{9,... | collective-permute-start | bytes 110600 | tf_op jit(solution)/shard_map/ppermute | solution.py:388
  69.2 5.0 %collective-permute-start.36 = (f32[2,48,96]{2,1,0:T(8,128)S(1)}, f32[2,48,96]{2,1,0:T(8,128)S(1)}, u32[]{:S(2)}, u32[]{:S(2)}) collective-permute-start(f32[2,48,96]{2,1,0:T(8,128)S(1)} %pad_maximum_fusion.2.refs_0_), channel_id=1, source_target_pairs={{0,16},{1,17},{2,18},{3,19},{4,20},{5,21},{6,22},{7,23},{8,24},{9,... | collective-permute-start | bytes 110600 | tf_op jit(solution)/shard_map/ppermute | solution.py:388
  69.2 5.0 %collective-permute-start.35 = (f32[2,48,96]{2,1,0:T(8,128)S(1)}, f32[2,48,96]{2,1,0:T(8,128)S(1)}, u32[]{:S(2)}, u32[]{:S(2)}) collective-permute-start(f32[2,48,96]{2,1,0:T(8,128)S(1)} %pad_maximum_fusion.2.refs_0_), channel_id=1, source_target_pairs={{0,8},{1,9},{2,10},{3,11},{4,12},{5,13},{6,14},{7,15},{8,0},{9,1},... | collective-permute-start | bytes 110600 | tf_op jit(solution)/shard_map/ppermute | solution.py:388

commit v7 on v6

--- a/solution.py
+++ b/solution.py
@@ -66,29 +66,39 @@
     out_ref[...] = jnp.transpose(values / total)
 
 
-def blur_plane(plane, row, taps):
-    margin = (taps - 1) // 2
-    step = LANES - 2 * margin
+def column_table(row, margin):
     table = pltpu.roll(jnp.broadcast_to(row, (LANES, LANES)), 0, 1, stride=1, stride_axis=0)
-    table = jnp.concatenate(split(table), axis=1)
+    high = table.astype(BF16).astype(F32)
+    src = lax.broadcasted_iota(jnp.int32, (GROUP, LANES), 0)
+    dst = lax.broadcasted_iota(jnp.int32, (GROUP, LANES), 1)
+    first, last = slice(0, GROUP), slice(LANES - GROUP, LANES)
+    above = dst - src <= LANES // 2
+    below = src + LANES - GROUP - dst <= LANES // 2
+    empty = jnp.zeros((LANES - 2 * GROUP, LANES), F32)
+    main, edge = [], []
+    for part in (high, table - high):
+        main.append(jnp.concatenate(
+            [jnp.where(above, part[first], 0.0), part[GROUP:LANES - GROUP], jnp.where(below, part[last], 0.0)],
+            axis=0).astype(BF16))
+        edge.append(jnp.concatenate(
+            [jnp.where(above, 0.0, part[first]), empty, jnp.where(below, 0.0, part[last])],
+            axis=0).astype(BF16))
+    return jnp.concatenate([jnp.concatenate(main, axis=1), jnp.concatenate(edge, axis=1)], axis=0)
+
+
+def blur_plane(plane, row, margin):
+    height = plane.shape[0]
+    table = column_table(row, margin)
     left, right = plane[:, :LANES], plane[:, LANES:]
     lane = lax.broadcasted_iota(jnp.int32, left.shape, 1)
-    zero = jnp.zeros_like(left)
-    windows = [
-        jnp.where(lane >= margin, pltpu.roll(left, margin, 1), zero),
-        jnp.where(lane < 3 * margin, pltpu.roll(left, 3 * margin, 1), pltpu.roll(right, 3 * margin, 1)),
-        jnp.where(lane < 5 * margin, pltpu.roll(right, 5 * margin, 1), zero),
-    ]
-    high, low = split(jnp.concatenate(windows, axis=0))
+    main = jnp.concatenate([left, right], axis=0)
+    edge = jnp.concatenate(
+        [jnp.where(lane < LANES // 2, right, 0.0), jnp.where(lane < LANES // 2, 0.0, left)], axis=0)
+    high, low = split(jnp.concatenate([main, edge], axis=1))
     product = dot(jnp.concatenate([high, low], axis=0), table)
-    rows = high.shape[0]
+    rows = 2 * height
     blocks = product[:rows, :LANES] + (product[:rows, LANES:] + product[rows:, :LANES])
-    height = plane.shape[0]
-    first, second, third = [blocks[k * height:(k + 1) * height] for k in range(3)]
-    second = pltpu.roll(second, step, 1)
-    third = pltpu.roll(third, 2 * step - LANES, 1)
-    return jnp.concatenate(
-        [jnp.where(lane < step, first, second), jnp.where(lane < 2 * step - LANES, second, third)], axis=1)
+    return jnp.concatenate([blocks[:height], blocks[height:]], axis=1)
 
 
 def row_table(base, margin, height):
@@ -138,7 +148,7 @@
     return both[:rank] + (both[rank:] + dot_nt(high, padded_low))
 
 
-def blur_kernel(cube_ref, taps_x_hbm, taps_y_hbm, w_hbm, xh_ref, xl_ref, keep_0, give_0, keep_1, give_1,
+def blur_kernel(cube_ref, taps_x_hbm, taps_y_hbm, w_hbm, xh_ref, xl_ref, w_here_ref, keep_0, give_0, keep_1, give_1,
                 taps_x_ref, taps_y_ref, w_ref, sems, work_ref, kx_ref, ky_ref):
     step = pl.program_id(0)
     taps = taps_x_ref.shape[0]
@@ -162,7 +172,7 @@
         give_0[PIECES * rank:] = gram
         normalized_taps(taps_x_ref, True, work_ref, kx_ref)
         normalized_taps(taps_y_ref, False, work_ref, ky_ref)
-        kx_ref[...] = pltpu.roll(kx_ref[...], LANES - 2 * margin, 1)
+        kx_ref[...] = pltpu.roll(kx_ref[...], LANES - margin, 1)
         per_vector = LANES // height
         place = lax.broadcasted_iota(jnp.int32, (LANES, LANES), 0) % per_vector
         values = ky_ref[...]
@@ -176,7 +186,7 @@
         done = []
         for plane in range(8 * half, 8 * half + 8):
             row = kx_ref[pl.ds(step * GROUP + plane, 1), :]
-            done.append(blur_plane(cube_ref[plane], row, taps))
+            done.append(blur_plane(cube_ref[plane], row, margin))
         high, low = split(jnp.concatenate(done, axis=0))
         rows = ky_ref[pl.ds(pl.multiple_of(step * GROUP + 8 * half, 8), 8), :]
         table_high, table_low = row_table(rows, margin, height)
@@ -197,6 +207,7 @@
         wide = 2 * LANES // lax.axis_size("sp")
         shift = lax.rem(band - me_sp * planes, band)
         w_here = pltpu.roll(w_ref[...], shift, 1)[:, :2 * LANES]
+        w_here_ref[...] = w_here[:, :planes]
         lane = lax.broadcasted_iota(jnp.int32, w_here.shape, 1)
         w_here = jnp.where(lane < planes, w_here, 0.0)
         w_high = w_here.astype(BF16).astype(F32)
@@ -227,14 +238,15 @@
     first = jax.ShapeDtypeStruct((PIECES * rank + FOLDED, LANES), F32)
     second = jax.ShapeDtypeStruct((PIECES * rank, LANES), F32)
     image = (height, planes, length)
+    mine = jax.ShapeDtypeStruct((rank, planes), F32)
     whole = lambda shape: pl.BlockSpec(shape, lambda i: (0,) * len(shape))
     return pl.pallas_call(
         blur_kernel,
         grid=(planes // GROUP,),
-        out_shape=[jax.ShapeDtypeStruct(image, BF16)] * 2 + [first, first, second, second],
+        out_shape=[jax.ShapeDtypeStruct(image, BF16)] * 2 + [mine, first, first, second, second],
         in_specs=[pl.BlockSpec((GROUP, height, length), lambda i: (i, 0, 0))]
         + [pl.BlockSpec(memory_space=pltpu.HBM)] * 3,
-        out_specs=[whole(image)] * 2 + [whole(first.shape)] * 2 + [whole(second.shape)] * 2,
+        out_specs=[whole(image)] * 2 + [whole(mine.shape)] + [whole(first.shape)] * 2 + [whole(second.shape)] * 2,
         scratch_shapes=[pltpu.VMEM(value.shape, F32) for value in (taps_x, taps_y, w_rows)]
         + [pltpu.SemaphoreType.DMA((3,))] + [pltpu.VMEM((LANES, LANES), F32)] * 3,
         compiler_params=pltpu.CompilerParams(
@@ -242,23 +254,21 @@
     )(cube, taps_x, taps_y, w_rows)
 
 
-def ratio_kernel(mine_ref, other_ref, h_ref, out_0, out_1):
+def ratio_kernel(mine_ref, other_ref, h_ref, out_ref):
     tall = h_ref.shape[0] // lax.axis_size("bd")
     first = pl.multiple_of(lax.axis_index("bd") * tall, tall)
     here = h_ref[pl.ds(first, tall)]
     here = jnp.transpose(here.reshape(-1, here.shape[2]))
     rows = mine_ref.shape[0]
     gram = unfold(mine_ref[rows - FOLDED:rows] + other_ref[rows - FOLDED:rows], here.shape[0])
-    ratio = here / dot_exact(gram, here)
-    out_0[...] = ratio[:, :LANES]
-    out_1[...] = ratio[:, LANES:]
+    out_ref[...] = here / dot_exact(gram, here)
 
 
 def ratio_call(mine, other, h_columns):
-    piece = jax.ShapeDtypeStruct((h_columns.shape[2], LANES), F32)
+    piece = jax.ShapeDtypeStruct((h_columns.shape[2], 2 * LANES), F32)
     return pl.pallas_call(
         ratio_kernel,
-        out_shape=[piece, piece],
+        out_shape=piece,
         in_specs=in_vmem(3),
         compiler_params=pltpu.CompilerParams(vmem_limit_bytes=VMEM_LIMIT),
     )(mine, other, h_columns)
@@ -324,30 +334,27 @@
     part_refs = rest[:8]
     w_out, h_out, all_ref = rest[8:]
     planes = xh_ref.shape[1]
-    rank, band = w_ref.shape
-    me_sp = lax.axis_index("sp")
+    rank = w_ref.shape[0]
     h_out[...] = h_ref[...]
     total = accumulate(xh_ref, xl_ref, part_refs, all_ref, h_out, 1, total_ref[...])
     numer = total[:planes, :rank] + (total[:planes, rank:] + total[planes:2 * planes, :rank])
     gram = total[2 * planes:]
     gram = gram[:rank, :rank] + (gram[:rank, rank:] + gram[rank:, :rank])
-    shift = lax.rem(band - me_sp * planes, band)
-    w_here = pltpu.roll(w_ref[...], shift, 1)[:, :planes]
+    w_here = w_ref[...]
     w_out[...] = w_here * jnp.transpose(numer) / dot_exact(gram, w_here)
 
 
-def second_call(x_high, x_low, w_rows, total, h_half, parts):
-    planes, rank = x_high.shape[1], w_rows.shape[0]
+def second_call(x_high, x_low, w_here, total, h_half, parts):
     return pl.pallas_call(
         second_kernel,
         out_shape=[
-            jax.ShapeDtypeStruct((rank, planes), F32),
+            jax.ShapeDtypeStruct(w_here.shape, F32),
             jax.ShapeDtypeStruct(h_half.shape, F32),
         ],
         in_specs=in_vmem(5 + len(parts)),
         scratch_shapes=[pltpu.VMEM((32,) + parts[0].shape[1:], F32)],
         compiler_params=pltpu.CompilerParams(vmem_limit_bytes=VMEM_LIMIT),
-    )(x_high, x_low, w_rows, total, h_half, *parts)
+    )(x_high, x_low, w_here, total, h_half, *parts)
 
 
 def gather_w_kernel(*refs):
@@ -398,7 +405,7 @@
     taps_y = jnp.transpose(taps_y, (2, 0, 1))
     h_columns = jnp.transpose(factor_h, (1, 2, 0))
     rank = w_rows.shape[0]
-    x_high, x_low, keep_0, give_0, keep_1, give_1 = blur_call(cube[0], taps_x, taps_y, w_rows)
+    x_high, x_low, w_here, keep_0, give_0, keep_1, give_1 = blur_call(cube[0], taps_x, taps_y, w_rows)
     chains = []
     for keep, give in ((keep_0, give_0), (keep_1, give_1)):
         taken = send(give, 0, 1)
@@ -408,20 +415,23 @@
             last = keep.shape[0] if first == max(bounds) else first + 4 * rank
             sides.append(keep[first:last] + taken[first:last])
         chains.append((sides, around(sides)))
-    ratios = ratio_call(chains[0][0][2], chains[0][1][1], h_columns)
+    ratio = ratio_call(chains[0][0][2], chains[0][1][1], h_columns)
+    line = []
+    for k in range(4):
+        part = slice(k * rank, (k + 1) * rank)
+        line.append(jnp.concatenate(
+            [(sides[0][part] + others[0][part]) + (others[1][part] + others[2][part]) for sides, others in chains],
+            axis=1))
+    line = [line[0]] + [send(line[k], 2 * k, 0) for k in range(1, 4)]
+    h_piece = ratio * ((line[0] + line[1]) + (line[2] + line[3]))
+    h_line = [h_piece] + [send(h_piece, 2 * k, 0) for k in range(1, 4)]
     rounds = []
-    for (sides, others), ratio in zip(chains, ratios):
-        line = []
-        for k in range(4):
-            part = slice(k * rank, (k + 1) * rank)
-            line.append((sides[0][part] + others[0][part]) + (others[1][part] + others[2][part]))
-        line = [line[0]] + [send(line[k], 2 * k, 0) for k in range(1, 4)]
-        h_piece = ratio * ((line[0] + line[1]) + (line[2] + line[3]))
-        h_line = jnp.stack([h_piece] + [send(h_piece, 2 * k, 0) for k in range(1, 4)])
-        parts = [h_line] + around([h_line] * 4)
+    for first in (0, LANES):
+        mine = jnp.stack([value[:, first:first + LANES] for value in h_line])
+        parts = [mine] + around([mine] * 4)
         rounds.append(parts + [send(value, 0, 1) for value in parts])
     total, h_half = first_call(x_high, x_low, rounds[0])
-    w_piece, h_next = second_call(x_high, x_low, w_rows, total, h_half, rounds[1])
+    w_piece, h_next = second_call(x_high, x_low, w_here, total, h_half, rounds[1])
     w_pair = jnp.stack([w_piece, send(w_piece, 1, 0)])
     w_next = gather_w_call([w_pair] + [send(w_pair, 2 * k, 0) for k in range(1, 4)])
     return jnp.transpose(w_next)[None], jnp.transpose(h_next, (2, 0, 1))

time: 75.3 us -> 75.6 us (level)
  waiting for transfers between devices: 13.2 us -> 23 us
  starting transfers between devices: 41.8 us -> 34.4 us
  Pallas kernels: 16.6 us -> 14.7 us
    ppermute x38 -> x32, waiting for transfers between devices: 13.2 us -> 23 us  [send(): return lax.ppermute(value, ('sp', 'bd'), pairs)]
    ppermute x38 -> x32, starting transfers between devices: 41.8 us -> 34.4 us  [send(): return lax.ppermute(value, ('sp', 'bd'), pairs)]
    pallas_call x1, Pallas kernels: 12.2 us -> 10.3 us  [blur_call(): pl.pallas_call(blur_kernel, grid=(planes // GROUP,), out_shape=[jax.Shape...]
    unnamed x10 -> x8, local copies, waits for them, and re-layouts: 2.33 us -> 2.32 us
  transfers between devices with their start and end apart: 38 -> 32, of which waited for: 10 -> 17; matrix products, arithmetic and copies ran while one was open for 0% -> 0% of each run, Pallas kernels for 2% -> 2%
where the time goes in v7:
time: 75.6 us; the launch traced here: 75.3 us
  starting transfers between devices  34.4 us (46%)
  waiting for transfers between devices  23 us (30%)
  Pallas kernels  14.7 us (19%)
  local copies, waits for them, and re-layouts  2.34 us (3%)
  between operations  0.79 us (1%)
    ppermute x32, starting transfers between devices, send(): return lax.ppermute(value, ('sp', 'bd'), pairs)  34.4 us
    ppermute x32, waiting for transfers between devices, send(): return lax.ppermute(value, ('sp', 'bd'), pairs)  23 us
    pallas_call x1, Pallas kernels, blur_call(): pl.pallas_call(blur_kernel, grid=(planes // GROUP,), out_shape=[jax.Shape...  10.3 us
    unnamed x8, local copies, waits for them, and re-layouts  2.32 us
    pallas_call x1, Pallas kernels, second_call(): pl.pallas_call(second_kernel, out_shape=[jax.ShapeDtypeStruct(w_here.shap...  2.24 us
  transfers between devices with their start and end apart: 32, of which 17 were waited for; matrix products, arithmetic and copies ran while one was open for 0% of the time, Pallas kernels for 2%

profile of v7, /device:TPU:0, one launch (start us, length us, event | category | flops | bytes accessed | tf_op | source)
XLA Modules:
  0.0 75.3 jit_solution(17509939959811875587)
XLA Ops:
  0.6 0.9 %copy-done.1 = f32[1,768,48]{1,2,0:T(8,128)S(1)} copy-done((f32[1,768,48]{1,2,0:T(8,128)S(1)}, f32[1,768,48]{1,2,0:T(8,128)}, u32[]{:S(2)}) %copy-start.1) | copy-done | bytes 147480
  1.5 0.7 copy-done.2
  2.3 0.7 copy-done.3
  3.0 10.3 %shard_map.68 = (bf16[32,96,256]{2,1,0:T(8,128)(2,1)S(1)}, bf16[32,96,256]{2,1,0:T(8,128)(2,1)S(1)}, f32[48,96]{1,0:T(8,128)S(1)}, f32[792,128]{1,0:T(8,128)S(1)...) custom-call(f32[96,32,256]{2,1,0:T(8,128)} %bitcast.34, f32[25,1,96]{2,1,0:T(1,128)S(1)} %bitcast.32, ...), custom_call_target="tpu_custom_call" | custom-call | tf_op jit(solution)/shard_map/pallas_call | solution.py:243
  13.3 0.5 collective-permute-start.4
  13.8 0.1 collective-permute-start
  13.9 1.3 %collective-permute-done.4 = f32[768,128]{1,0:T(8,128)S(1)} collective-permute-done((f32[768,128]{1,0:T(8,128)S(1)}, f32[768,128]{1,0:T(8,128)S(1)}, u32[]{:S(2)}, u32[]{:S(2)}) %collective-permute-start.4) | collective-permute-done | bytes 393248 | tf_op jit(solution)/shard_map/ppermute | solution.py:395
  15.2 3.9 %collective-permute-start.7 = (f32[192,128]{1,0:T(8,128)S(1)}, f32[192,128]{1,0:T(8,128)S(1)}, u32[]{:S(2)}, u32[]{:S(2)}) collective-permute-start(f32[192,128]{1,0:T(8,128)S(1)} %get-tuple-element.28), channel_id=1, source_target_pairs={{0,6},{1,7},{2,4},{3,5},{4,2},{5,3},{6,0},{7,1},{8,14},{9,15},{10,... | collective-permute-start | bytes 294920 | tf_op jit(solution)/shard_map/ppermute | solution.py:395
  19.1 0.5 collective-permute-start.6
  19.6 0.1 collective-permute-start.5
  19.8 2.9 %collective-permute-start.3 = (f32[192,128]{1,0:T(8,128)S(1)}, f32[192,128]{1,0:T(8,128)S(1)}, u32[]{:S(2)}, u32[]{:S(2)}) collective-permute-start(f32[192,128]{1,0:T(8,128)S(1)} %get-tuple-element.25), channel_id=1, source_target_pairs={{0,6},{1,7},{2,4},{3,5},{4,2},{5,3},{6,0},{7,1},{8,14},{9,15},{10,... | collective-permute-start | bytes 294920 | tf_op jit(solution)/shard_map/ppermute | solution.py:395
  22.7 0.5 collective-permute-start.2
  23.2 1.4 %collective-permute-start.1 = (f32[216,128]{1,0:T(8,128)S(1)}, f32[216,128]{1,0:T(8,128)S(1)}, u32[]{:S(2)}, u32[]{:S(2)}) collective-permute-start(f32[216,128]{1,0:T(8,128)S(1)} %slice_add_fusion.mine_ref), channel_id=1, source_target_pairs={{0,2},{1,3},{2,0},{3,1},{4,6},{5,7},{6,4},{7,5},{8,10},{9,11},{10,... | collective-permute-start | bytes 331784 | tf_op jit(solution)/shard_map/ppermute | solution.py:395
  24.6 0.9 %collective-permute-done.6 = f32[192,128]{1,0:T(8,128)S(1)} collective-permute-done((f32[192,128]{1,0:T(8,128)S(1)}, f32[192,128]{1,0:T(8,128)S(1)}, u32[]{:S(2)}, u32[]{:S(2)}) %collective-permute-start.6) | collective-permute-done | bytes 98336 | tf_op jit(solution)/shard_map/ppermute | solution.py:395
  25.6 2.5 %collective-permute-done.3 = f32[192,128]{1,0:T(8,128)S(1)} collective-permute-done((f32[192,128]{1,0:T(8,128)S(1)}, f32[192,128]{1,0:T(8,128)S(1)}, u32[]{:S(2)}, u32[]{:S(2)}) %collective-permute-start.3) | collective-permute-done | bytes 98336 | tf_op jit(solution)/shard_map/ppermute | solution.py:395
  28.1 0.7 collective-permute-done.2
  28.7 0.1 collective-permute-done.1.other_ref
  28.8 1.8 %collective-permute-start.8 = (f32[48,256]{1,0:T(8,128)S(1)}, f32[48,256]{1,0:T(8,128)S(1)}, u32[]{:S(2)}, u32[]{:S(2)}) collective-permute-start(f32[48,256]{1,0:T(8,128)S(1)} %pad_maximum_fusion.2), channel_id=1, source_target_pairs={{0,8},{1,9},{2,10},{3,11},{4,12},{5,13},{6,14},{7,15},{8,0},{9,1},... | collective-permute-start | bytes 147464 | tf_op jit(solution)/shard_map/ppermute | solution.py:395
  30.6 2.6 %collective-permute-start.9 = (f32[48,256]{1,0:T(8,128)S(1)}, f32[48,256]{1,0:T(8,128)S(1)}, u32[]{:S(2)}, u32[]{:S(2)}) collective-permute-start(f32[48,256]{1,0:T(8,128)S(1)} %pad_maximum_fusion.3), channel_id=1, source_target_pairs={{0,16},{1,17},{2,18},{3,19},{4,20},{5,21},{6,22},{7,23},{8,24},{9,... | collective-permute-start | bytes 147464 | tf_op jit(solution)/shard_map/ppermute | solution.py:395
  33.2 0.1 collective-permute-start.10
  33.3 0.3 shard_map.69
  33.6 0.0 collective-permute-done.8
  33.6 2.6 %collective-permute-done.9 = f32[48,256]{1,0:T(8,128)S(1)} collective-permute-done((f32[48,256]{1,0:T(8,128)S(1)}, f32[48,256]{1,0:T(8,128)S(1)}, u32[]{:S(2)}, u32[]{:S(2)}) %collective-permute-start.9) | collective-permute-done | bytes 49184 | tf_op jit(solution)/shard_map/ppermute | solution.py:395
  36.2 3.0 %collective-permute-done.10 = f32[48,256]{1,0:T(8,128)S(1)} collective-permute-done((f32[48,256]{1,0:T(8,128)S(1)}, f32[48,256]{1,0:T(8,128)S(1)}, u32[]{:S(2)}, u32[]{:S(2)}) %collective-permute-start.10) | collective-permute-done | bytes 49184 | tf_op jit(solution)/shard_map/ppermute | solution.py:395
  39.1 0.7 collective-permute-start.13
  39.8 0.0 collective-permute-start.12
  39.8 3.8 %collective-permute-start.11 = (f32[48,256]{1,0:T(8,128)S(1)}, f32[48,256]{1,0:T(8,128)S(1)}, u32[]{:S(2)}, u32[]{:S(2)}) collective-permute-start(f32[48,256]{1,0:T(8,128)S(1)} %fusion.1), channel_id=1, source_target_pairs={{0,8},{1,9},{2,10},{3,11},{4,12},{5,13},{6,14},{7,15},{8,0},{9,1},... | collective-permute-start | bytes 147464 | tf_op jit(solution)/shard_map/ppermute | solution.py:395
  43.6 1.6 %collective-permute-done.13 = f32[48,256]{1,0:T(8,128)S(1)} collective-permute-done((f32[48,256]{1,0:T(8,128)S(1)}, f32[48,256]{1,0:T(8,128)S(1)}, u32[]{:S(2)}, u32[]{:S(2)}) %collective-permute-start.13) | collective-permute-done | bytes 49184 | tf_op jit(solution)/shard_map/ppermute | solution.py:395
  45.2 0.7 collective-permute-done.12
  45.9 0.0 collective-permute-done.11
  45.9 0.1 collective-permute-start.17
  46.0 2.0 %collective-permute-start.16 = (f32[4,48,128]{2,1,0:T(8,128)S(1)}, f32[4,48,128]{2,1,0:T(8,128)S(1)}, u32[]{:S(2)}, u32[]{:S(2)}) collective-permute-start(f32[4,48,128]{2,1,0:T(8,128)S(1)} %pad_maximum_fusion.rest_0_), channel_id=1, source_target_pairs={{0,6},{1,7},{2,4},{3,5},{4,2},{5,3},{6,0},{7,1},{8,14},{9,15},{10,... | collective-permute-start | bytes 294920 | tf_op jit(solution)/shard_map/ppermute | solution.py:395
  48.0 1.0 %collective-permute-start.15 = (f32[4,48,128]{2,1,0:T(8,128)S(1)}, f32[4,48,128]{2,1,0:T(8,128)S(1)}, u32[]{:S(2)}, u32[]{:S(2)}) collective-permute-start(f32[4,48,128]{2,1,0:T(8,128)S(1)} %pad_maximum_fusion.rest_0_), channel_id=1, source_target_pairs={{0,2},{1,3},{2,0},{3,1},{4,6},{5,7},{6,4},{7,5},{8,10},{9,11},{10,... | collective-permute-start | bytes 294920 | tf_op jit(solution)/shard_map/ppermute | solution.py:395
  49.0 0.5 collective-permute-start.14
  49.5 2.0 %collective-permute-start.23 = (f32[4,48,128]{2,1,0:T(8,128)S(1)}, f32[4,48,128]{2,1,0:T(8,128)S(1)}, u32[]{:S(2)}, u32[]{:S(2)}) collective-permute-start(f32[4,48,128]{2,1,0:T(8,128)S(1)} %pad_maximum_fusion.1.rest_0_), channel_id=1, source_target_pairs={{0,6},{1,7},{2,4},{3,5},{4,2},{5,3},{6,0},{7,1},{8,14},{9,15},{10,... | collective-permute-start | bytes 294920 | tf_op jit(solution)/shard_map/ppermute | solution.py:395
  51.6 0.0 collective-permute-done.17.rest_4_
  51.6 1.0 %collective-permute-start.22 = (f32[4,48,128]{2,1,0:T(8,128)S(1)}, f32[4,48,128]{2,1,0:T(8,128)S(1)}, u32[]{:S(2)}, u32[]{:S(2)}) collective-permute-start(f32[4,48,128]{2,1,0:T(8,128)S(1)} %pad_maximum_fusion.1.rest_0_), channel_id=1, source_target_pairs={{0,2},{1,3},{2,0},{3,1},{4,6},{5,7},{6,4},{7,5},{8,10},{9,11},{10,... | collective-permute-start | bytes 294920 | tf_op jit(solution)/shard_map/ppermute | solution.py:395
  52.6 0.0 collective-permute-done.16.rest_3_
  52.6 1.5 %collective-permute-start.21 = (f32[4,48,128]{2,1,0:T(8,128)S(1)}, f32[4,48,128]{2,1,0:T(8,128)S(1)}, u32[]{:S(2)}, u32[]{:S(2)}) collective-permute-start(f32[4,48,128]{2,1,0:T(8,128)S(1)} %pad_maximum_fusion.1.rest_0_), channel_id=1, source_target_pairs={{0,4},{1,5},{2,6},{3,7},{4,0},{5,1},{6,2},{7,3},{8,12},{9,13},{10,... | collective-permute-start | bytes 294920 | tf_op jit(solution)/shard_map/ppermute | solution.py:395
  54.1 1.2 %collective-permute-done.15.rest_2_ = f32[4,48,128]{2,1,0:T(8,128)S(1)} collective-permute-done((f32[4,48,128]{2,1,0:T(8,128)S(1)}, f32[4,48,128]{2,1,0:T(8,128)S(1)}, u32[]{:S(2)}, u32[]{:S(2)}) %collective-permute-start.15) | collective-permute-done | bytes 98336 | tf_op jit(solution)/shard_map/ppermute | solution.py:395
  55.2 0.0 collective-permute-start.20
  55.2 0.0 collective-permute-done.14.rest_1_
  55.2 0.5 collective-permute-start.19
  55.7 1.5 %collective-permute-done.23.rest_3_ = f32[4,48,128]{2,1,0:T(8,128)S(1)} collective-permute-done((f32[4,48,128]{2,1,0:T(8,128)S(1)}, f32[4,48,128]{2,1,0:T(8,128)S(1)}, u32[]{:S(2)}, u32[]{:S(2)}) %collective-permute-start.23) | collective-permute-done | bytes 98336 | tf_op jit(solution)/shard_map/ppermute | solution.py:395
  57.2 0.0 collective-permute-start.18
  57.2 1.2 %collective-permute-done.22.rest_2_ = f32[4,48,128]{2,1,0:T(8,128)S(1)} collective-permute-done((f32[4,48,128]{2,1,0:T(8,128)S(1)}, f32[4,48,128]{2,1,0:T(8,128)S(1)}, u32[]{:S(2)}, u32[]{:S(2)}) %collective-permute-start.22) | collective-permute-done | bytes 98336 | tf_op jit(solution)/shard_map/ppermute | solution.py:395
  58.4 0.0 collective-permute-start.24
  58.5 0.1 collective-permute-done.21.rest_1_
  58.5 0.4 collective-permute-start.27
  58.9 0.0 collective-permute-done.20.rest_7_
  58.9 0.1 collective-permute-start.26
  59.1 0.4 collective-permute-start.25
  59.4 0.0 collective-permute-done.18.rest_5_
  59.4 1.1 %shard_map.70 = (f32[288,96]{1,0:T(8,128)S(1)}, f32[32,32,48]{2,1,0:T(8,128)S(1)}) custom-call(bf16[32,96,256]{2,1,0:T(8,128)(2,1)S(1)} %get-tuple-element.13.xh_ref, bf16[32,96,256]{2,1,0:T(8,128)(2,1)S(1)} %get-tuple-element.14.xl_ref, f32[4,48,128]{2,1,0:T(8,128)S(1)} %pad_maximum_fusion.rest_0_, f32[4,48,128]{2,1,0:T(8,128)S(1)} %collective-permute-done.14.rest_1_, ...), custom_call_target="tpu_custom_call" | custom-call | tf_op jit(solution)/shard_map/pallas_call | solution.py:321
  60.5 2.2 %shard_map.71 = (f32[48,96]{1,0:T(8,128)S(1)}, f32[32,32,48]{2,1,0:T(8,128)}) custom-call(bf16[32,96,256]{2,1,0:T(8,128)(2,1)S(1)} %get-tuple-element.13.xh_ref, bf16[32,96,256]{2,1,0:T(8,128)(2,1)S(1)} %get-tuple-element.14.xl_ref, f32[48,96]{1,0:T(8,128)S(1)} %get-tuple-element.15.w_ref, f32[288,96]{1,0:T(8,128)S(1)} %get-tuple-element.20.total_ref, ...), custom_call_target="tpu_custom_call" | custom-call | tf_op jit(solution)/shard_map/pallas_call | solution.py:348
  62.8 1.5 %collective-permute-start.28 = (f32[48,96]{1,0:T(8,128)S(1)}, f32[48,96]{1,0:T(8,128)S(1)}, u32[]{:S(2)}, u32[]{:S(2)}) collective-permute-start(f32[48,96]{1,0:T(8,128)S(1)} %get-tuple-element.22), channel_id=1, source_target_pairs={{0,4},{1,5},{2,6},{3,7},{4,0},{5,1},{6,2},{7,3},{8,12},{9,13},{10,... | collective-permute-start | bytes 55304 | tf_op jit(solution)/shard_map/ppermute | solution.py:395
  64.3 2.3 %collective-permute-done.28 = f32[48,96]{1,0:T(8,128)S(1)} collective-permute-done((f32[48,96]{1,0:T(8,128)S(1)}, f32[48,96]{1,0:T(8,128)S(1)}, u32[]{:S(2)}, u32[]{:S(2)}) %collective-permute-start.28) | collective-permute-done | bytes 18464 | tf_op jit(solution)/shard_map/ppermute | solution.py:395
  66.6 2.2 %collective-permute-start.31 = (f32[2,48,96]{2,1,0:T(8,128)S(1)}, f32[2,48,96]{2,1,0:T(8,128)S(1)}, u32[]{:S(2)}, u32[]{:S(2)}) collective-permute-start(f32[2,48,96]{2,1,0:T(8,128)S(1)} %pad_maximum_fusion.5.refs_0_), channel_id=1, source_target_pairs={{0,24},{1,25},{2,26},{3,27},{4,28},{5,29},{6,30},{7,31},{8,16},{9,... | collective-permute-start | bytes 110600 | tf_op jit(solution)/shard_map/ppermute | solution.py:395
  68.8 1.1 %collective-permute-start.30 = (f32[2,48,96]{2,1,0:T(8,128)S(1)}, f32[2,48,96]{2,1,0:T(8,128)S(1)}, u32[]{:S(2)}, u32[]{:S(2)}) collective-permute-start(f32[2,48,96]{2,1,0:T(8,128)S(1)} %pad_maximum_fusion.5.refs_0_), channel_id=1, source_target_pairs={{0,16},{1,17},{2,18},{3,19},{4,20},{5,21},{6,22},{7,23},{8,24},{9,... | collective-permute-start | bytes 110600 | tf_op jit(solution)/shard_map/ppermute | solution.py:395
  69.9 1.1 %collective-permute-start.29 = (f32[2,48,96]{2,1,0:T(8,128)S(1)}, f32[2,48,96]{2,1,0:T(8,128)S(1)}, u32[]{:S(2)}, u32[]{:S(2)}) collective-permute-start(f32[2,48,96]{2,1,0:T(8,128)S(1)} %pad_maximum_fusion.5.refs_0_), channel_id=1, source_target_pairs={{0,8},{1,9},{2,10},{3,11},{4,12},{5,13},{6,14},{7,15},{8,0},{9,1},... | collective-permute-start | bytes 110600 | tf_op jit(solution)/shard_map/ppermute | solution.py:395
  71.1 1.8 %collective-permute-done.31.refs_3_ = f32[2,48,96]{2,1,0:T(8,128)S(1)} collective-permute-done((f32[2,48,96]{2,1,0:T(8,128)S(1)}, f32[2,48,96]{2,1,0:T(8,128)S(1)}, u32[]{:S(2)}, u32[]{:S(2)}) %collective-permute-start.31) | collective-permute-done | bytes 36896 | tf_op jit(solution)/shard_map/ppermute | solution.py:395
  72.9 1.4 %collective-permute-done.30.refs_2_ = f32[2,48,96]{2,1,0:T(8,128)S(1)} collective-permute-done((f32[2,48,96]{2,1,0:T(8,128)S(1)}, f32[2,48,96]{2,1,0:T(8,128)S(1)}, u32[]{:S(2)}, u32[]{:S(2)}) %collective-permute-start.30) | collective-permute-done | bytes 36896 | tf_op jit(solution)/shard_map/ppermute | solution.py:395
  74.2 0.3 collective-permute-done.29.refs_1_
  74.5 0.8 %shard_map.72 = f32[48,768]{1,0:T(8,128)} custom-call(f32[2,48,96]{2,1,0:T(8,128)S(1)} %pad_maximum_fusion.5.refs_0_, f32[2,48,96]{2,1,0:T(8,128)S(1)} %collective-permute-done.29.refs_1_, f32[2,48,96]{2,1,0:T(8,128)S(1)} %collective-permute-done.30.refs_2_, f32[2,48,96]{2,1,0:T(8,128)S(1)} %collective-permute-done.31.refs_3_), custom_call_target="tpu_custom_call" | custom-call | tf_op jit(solution)/shard_map/pallas_call | solution.py:379
  (29 shorter events, 0.3 us)
Async XLA Ops:
  0.6 0.9 %copy-start.1 = (f32[1,768,48]{1,2,0:T(8,128)S(1)}, f32[1,768,48]{1,2,0:T(8,128)}, u32[]{:S(2)}) copy-start(f32[1,768,48]{1,2,0:T(8,128)} %param.8) | copy-start | bytes 442372
  1.5 0.7 copy-start.2
  2.3 0.7 copy-start.3
  13.3 1.9 %collective-permute-start.4 = (f32[768,128]{1,0:T(8,128)S(1)}, f32[768,128]{1,0:T(8,128)S(1)}, u32[]{:S(2)}, u32[]{:S(2)}) collective-permute-start(f32[768,128]{1,0:T(8,128)S(1)} %get-tuple-element.19), channel_id=1, source_target_pairs={{0,1},{1,0},{2,3},{3,2},{4,5},{5,4},{6,7},{7,6},{8,9},{9,8},{10,11... | collective-permute-start | bytes 1179656 | tf_op jit(solution)/shard_map/ppermute | solution.py:395
  13.8 5.9 %collective-permute-start = (f32[792,128]{1,0:T(8,128)S(1)}, f32[792,128]{1,0:T(8,128)S(1)}, u32[]{:S(2)}, u32[]{:S(2)}) collective-permute-start(f32[792,128]{1,0:T(8,128)S(1)} %get-tuple-element.17), channel_id=1, source_target_pairs={{0,1},{1,0},{2,3},{3,2},{4,5},{5,4},{6,7},{7,6},{8,9},{9,8},{10,11... | collective-permute-start | bytes 1216520 | tf_op jit(solution)/shard_map/ppermute | solution.py:395
  15.1 18.2 %copy-start = (f32[48,32,32]{0,2,1:T(8,128)S(1)}, f32[48,32,32]{0,2,1:T(8,128)}, u32[]{:S(2)}) copy-start(f32[48,32,32]{0,2,1:T(8,128)} %param.9) | copy-start | bytes 589828
  15.2 8.0 %collective-permute-start.7 = (f32[192,128]{1,0:T(8,128)S(1)}, f32[192,128]{1,0:T(8,128)S(1)}, u32[]{:S(2)}, u32[]{:S(2)}) collective-permute-start(f32[192,128]{1,0:T(8,128)S(1)} %get-tuple-element.28), channel_id=1, source_target_pairs={{0,6},{1,7},{2,4},{3,5},{4,2},{5,3},{6,0},{7,1},{8,14},{9,15},{10,... | collective-permute-start | bytes 294920 | tf_op jit(solution)/shard_map/ppermute | solution.py:395
  19.1 6.5 %collective-permute-start.6 = (f32[192,128]{1,0:T(8,128)S(1)}, f32[192,128]{1,0:T(8,128)S(1)}, u32[]{:S(2)}, u32[]{:S(2)}) collective-permute-start(f32[192,128]{1,0:T(8,128)S(1)} %get-tuple-element.29), channel_id=1, source_target_pairs={{0,2},{1,3},{2,0},{3,1},{4,6},{5,7},{6,4},{7,5},{8,10},{9,11},{10,... | collective-permute-start | bytes 294920 | tf_op jit(solution)/shard_map/ppermute | solution.py:395
  19.6 6.0 %collective-permute-start.5 = (f32[192,128]{1,0:T(8,128)S(1)}, f32[192,128]{1,0:T(8,128)S(1)}, u32[]{:S(2)}, u32[]{:S(2)}) collective-permute-start(f32[192,128]{1,0:T(8,128)S(1)} %get-tuple-element.30), channel_id=1, source_target_pairs={{0,4},{1,5},{2,6},{3,7},{4,0},{5,1},{6,2},{7,3},{8,12},{9,13},{10,... | collective-permute-start | bytes 294920 | tf_op jit(solution)/shard_map/ppermute | solution.py:395
  19.8 8.3 %collective-permute-start.3 = (f32[192,128]{1,0:T(8,128)S(1)}, f32[192,128]{1,0:T(8,128)S(1)}, u32[]{:S(2)}, u32[]{:S(2)}) collective-permute-start(f32[192,128]{1,0:T(8,128)S(1)} %get-tuple-element.25), channel_id=1, source_target_pairs={{0,6},{1,7},{2,4},{3,5},{4,2},{5,3},{6,0},{7,1},{8,14},{9,15},{10,... | collective-permute-start | bytes 294920 | tf_op jit(solution)/shard_map/ppermute | solution.py:395
  22.7 6.1 %collective-permute-start.2 = (f32[192,128]{1,0:T(8,128)S(1)}, f32[192,128]{1,0:T(8,128)S(1)}, u32[]{:S(2)}, u32[]{:S(2)}) collective-permute-start(f32[192,128]{1,0:T(8,128)S(1)} %get-tuple-element.26), channel_id=1, source_target_pairs={{0,4},{1,5},{2,6},{3,7},{4,0},{5,1},{6,2},{7,3},{8,12},{9,13},{10,... | collective-permute-start | bytes 294920 | tf_op jit(solution)/shard_map/ppermute | solution.py:395
  23.2 5.6 %collective-permute-start.1 = (f32[216,128]{1,0:T(8,128)S(1)}, f32[216,128]{1,0:T(8,128)S(1)}, u32[]{:S(2)}, u32[]{:S(2)}) collective-permute-start(f32[216,128]{1,0:T(8,128)S(1)} %slice_add_fusion.mine_ref), channel_id=1, source_target_pairs={{0,2},{1,3},{2,0},{3,1},{4,6},{5,7},{6,4},{7,5},{8,10},{9,11},{10,... | collective-permute-start | bytes 331784 | tf_op jit(solution)/shard_map/ppermute | solution.py:395
  28.8 4.7 %collective-permute-start.8 = (f32[48,256]{1,0:T(8,128)S(1)}, f32[48,256]{1,0:T(8,128)S(1)}, u32[]{:S(2)}, u32[]{:S(2)}) collective-permute-start(f32[48,256]{1,0:T(8,128)S(1)} %pad_maximum_fusion.2), channel_id=1, source_target_pairs={{0,8},{1,9},{2,10},{3,11},{4,12},{5,13},{6,14},{7,15},{8,0},{9,1},... | collective-permute-start | bytes 147464 | tf_op jit(solution)/shard_map/ppermute | solution.py:395
  30.6 5.5 %collective-permute-start.9 = (f32[48,256]{1,0:T(8,128)S(1)}, f32[48,256]{1,0:T(8,128)S(1)}, u32[]{:S(2)}, u32[]{:S(2)}) collective-permute-start(f32[48,256]{1,0:T(8,128)S(1)} %pad_maximum_fusion.3), channel_id=1, source_target_pairs={{0,16},{1,17},{2,18},{3,19},{4,20},{5,21},{6,22},{7,23},{8,24},{9,... | collective-permute-start | bytes 147464 | tf_op jit(solution)/shard_map/ppermute | solution.py:395
  33.2 5.9 %collective-permute-start.10 = (f32[48,256]{1,0:T(8,128)S(1)}, f32[48,256]{1,0:T(8,128)S(1)}, u32[]{:S(2)}, u32[]{:S(2)}) collective-permute-start(f32[48,256]{1,0:T(8,128)S(1)} %pad_maximum_fusion.4), channel_id=1, source_target_pairs={{0,24},{1,25},{2,26},{3,27},{4,28},{5,29},{6,30},{7,31},{8,16},{9,... | collective-permute-start | bytes 147464 | tf_op jit(solution)/shard_map/ppermute | solution.py:395
  39.1 6.1 %collective-permute-start.13 = (f32[48,256]{1,0:T(8,128)S(1)}, f32[48,256]{1,0:T(8,128)S(1)}, u32[]{:S(2)}, u32[]{:S(2)}) collective-permute-start(f32[48,256]{1,0:T(8,128)S(1)} %fusion.1), channel_id=1, source_target_pairs={{0,24},{1,25},{2,26},{3,27},{4,28},{5,29},{6,30},{7,31},{8,16},{9,... | collective-permute-start | bytes 147464 | tf_op jit(solution)/shard_map/ppermute | solution.py:395
  39.8 6.0 %collective-permute-start.12 = (f32[48,256]{1,0:T(8,128)S(1)}, f32[48,256]{1,0:T(8,128)S(1)}, u32[]{:S(2)}, u32[]{:S(2)}) collective-permute-start(f32[48,256]{1,0:T(8,128)S(1)} %fusion.1), channel_id=1, source_target_pairs={{0,16},{1,17},{2,18},{3,19},{4,20},{5,21},{6,22},{7,23},{8,24},{9,... | collective-permute-start | bytes 147464 | tf_op jit(solution)/shard_map/ppermute | solution.py:395
  39.8 6.0 %collective-permute-start.11 = (f32[48,256]{1,0:T(8,128)S(1)}, f32[48,256]{1,0:T(8,128)S(1)}, u32[]{:S(2)}, u32[]{:S(2)}) collective-permute-start(f32[48,256]{1,0:T(8,128)S(1)} %fusion.1), channel_id=1, source_target_pairs={{0,8},{1,9},{2,10},{3,11},{4,12},{5,13},{6,14},{7,15},{8,0},{9,1},... | collective-permute-start | bytes 147464 | tf_op jit(solution)/shard_map/ppermute | solution.py:395
  45.9 5.7 %collective-permute-start.17 = (f32[4,48,128]{2,1,0:T(8,128)S(1)}, f32[4,48,128]{2,1,0:T(8,128)S(1)}, u32[]{:S(2)}, u32[]{:S(2)}) collective-permute-start(f32[4,48,128]{2,1,0:T(8,128)S(1)} %pad_maximum_fusion.rest_0_), channel_id=1, source_target_pairs={{0,1},{1,0},{2,3},{3,2},{4,5},{5,4},{6,7},{7,6},{8,9},{9,8},{10,11... | collective-permute-start | bytes 294920 | tf_op jit(solution)/shard_map/ppermute | solution.py:395
  46.0 6.6 %collective-permute-start.16 = (f32[4,48,128]{2,1,0:T(8,128)S(1)}, f32[4,48,128]{2,1,0:T(8,128)S(1)}, u32[]{:S(2)}, u32[]{:S(2)}) collective-permute-start(f32[4,48,128]{2,1,0:T(8,128)S(1)} %pad_maximum_fusion.rest_0_), channel_id=1, source_target_pairs={{0,6},{1,7},{2,4},{3,5},{4,2},{5,3},{6,0},{7,1},{8,14},{9,15},{10,... | collective-permute-start | bytes 294920 | tf_op jit(solution)/shard_map/ppermute | solution.py:395
  48.0 7.2 %collective-permute-start.15 = (f32[4,48,128]{2,1,0:T(8,128)S(1)}, f32[4,48,128]{2,1,0:T(8,128)S(1)}, u32[]{:S(2)}, u32[]{:S(2)}) collective-permute-start(f32[4,48,128]{2,1,0:T(8,128)S(1)} %pad_maximum_fusion.rest_0_), channel_id=1, source_target_pairs={{0,2},{1,3},{2,0},{3,1},{4,6},{5,7},{6,4},{7,5},{8,10},{9,11},{10,... | collective-permute-start | bytes 294920 | tf_op jit(solution)/shard_map/ppermute | solution.py:395
  49.0 6.2 %collective-permute-start.14 = (f32[4,48,128]{2,1,0:T(8,128)S(1)}, f32[4,48,128]{2,1,0:T(8,128)S(1)}, u32[]{:S(2)}, u32[]{:S(2)}) collective-permute-start(f32[4,48,128]{2,1,0:T(8,128)S(1)} %pad_maximum_fusion.rest_0_), channel_id=1, source_target_pairs={{0,4},{1,5},{2,6},{3,7},{4,0},{5,1},{6,2},{7,3},{8,12},{9,13},{10,... | collective-permute-start | bytes 294920 | tf_op jit(solution)/shard_map/ppermute | solution.py:395
  49.5 7.7 %collective-permute-start.23 = (f32[4,48,128]{2,1,0:T(8,128)S(1)}, f32[4,48,128]{2,1,0:T(8,128)S(1)}, u32[]{:S(2)}, u32[]{:S(2)}) collective-permute-start(f32[4,48,128]{2,1,0:T(8,128)S(1)} %pad_maximum_fusion.1.rest_0_), channel_id=1, source_target_pairs={{0,6},{1,7},{2,4},{3,5},{4,2},{5,3},{6,0},{7,1},{8,14},{9,15},{10,... | collective-permute-start | bytes 294920 | tf_op jit(solution)/shard_map/ppermute | solution.py:395
  51.6 6.9 %collective-permute-start.22 = (f32[4,48,128]{2,1,0:T(8,128)S(1)}, f32[4,48,128]{2,1,0:T(8,128)S(1)}, u32[]{:S(2)}, u32[]{:S(2)}) collective-permute-start(f32[4,48,128]{2,1,0:T(8,128)S(1)} %pad_maximum_fusion.1.rest_0_), channel_id=1, source_target_pairs={{0,2},{1,3},{2,0},{3,1},{4,6},{5,7},{6,4},{7,5},{8,10},{9,11},{10,... | collective-permute-start | bytes 294920 | tf_op jit(solution)/shard_map/ppermute | solution.py:395
  52.6 5.9 %collective-permute-start.21 = (f32[4,48,128]{2,1,0:T(8,128)S(1)}, f32[4,48,128]{2,1,0:T(8,128)S(1)}, u32[]{:S(2)}, u32[]{:S(2)}) collective-permute-start(f32[4,48,128]{2,1,0:T(8,128)S(1)} %pad_maximum_fusion.1.rest_0_), channel_id=1, source_target_pairs={{0,4},{1,5},{2,6},{3,7},{4,0},{5,1},{6,2},{7,3},{8,12},{9,13},{10,... | collective-permute-start | bytes 294920 | tf_op jit(solution)/shard_map/ppermute | solution.py:395
  55.2 3.7 %collective-permute-start.20 = (f32[4,48,128]{2,1,0:T(8,128)S(1)}, f32[4,48,128]{2,1,0:T(8,128)S(1)}, u32[]{:S(2)}, u32[]{:S(2)}) collective-permute-start(f32[4,48,128]{2,1,0:T(8,128)S(1)} %collective-permute-done.16.rest_3_), channel_id=1, source_target_pairs={{0,1},{1,0},{2,3},{3,2},{4,5},{5,4},{6,7},{7,6},{8,9},{9,8},{10,11... | collective-permute-start | bytes 294920 | tf_op jit(solution)/shard_map/ppermute | solution.py:395
  55.2 3.8 %collective-permute-start.19 = (f32[4,48,128]{2,1,0:T(8,128)S(1)}, f32[4,48,128]{2,1,0:T(8,128)S(1)}, u32[]{:S(2)}, u32[]{:S(2)}) collective-permute-start(f32[4,48,128]{2,1,0:T(8,128)S(1)} %collective-permute-done.15.rest_2_), channel_id=1, source_target_pairs={{0,1},{1,0},{2,3},{3,2},{4,5},{5,4},{6,7},{7,6},{8,9},{9,8},{10,11... | collective-permute-start | bytes 294920 | tf_op jit(solution)/shard_map/ppermute | solution.py:395
  57.2 2.2 %collective-permute-start.18 = (f32[4,48,128]{2,1,0:T(8,128)S(1)}, f32[4,48,128]{2,1,0:T(8,128)S(1)}, u32[]{:S(2)}, u32[]{:S(2)}) collective-permute-start(f32[4,48,128]{2,1,0:T(8,128)S(1)} %collective-permute-done.14.rest_1_), channel_id=1, source_target_pairs={{0,1},{1,0},{2,3},{3,2},{4,5},{5,4},{6,7},{7,6},{8,9},{9,8},{10,11... | collective-permute-start | bytes 294920 | tf_op jit(solution)/shard_map/ppermute | solution.py:395
  58.4 2.1 %collective-permute-start.24 = (f32[4,48,128]{2,1,0:T(8,128)S(1)}, f32[4,48,128]{2,1,0:T(8,128)S(1)}, u32[]{:S(2)}, u32[]{:S(2)}) collective-permute-start(f32[4,48,128]{2,1,0:T(8,128)S(1)} %pad_maximum_fusion.1.rest_0_), channel_id=1, source_target_pairs={{0,1},{1,0},{2,3},{3,2},{4,5},{5,4},{6,7},{7,6},{8,9},{9,8},{10,11... | collective-permute-start | bytes 294920 | tf_op jit(solution)/shard_map/ppermute | solution.py:395
  58.5 2.0 %collective-permute-start.27 = (f32[4,48,128]{2,1,0:T(8,128)S(1)}, f32[4,48,128]{2,1,0:T(8,128)S(1)}, u32[]{:S(2)}, u32[]{:S(2)}) collective-permute-start(f32[4,48,128]{2,1,0:T(8,128)S(1)} %collective-permute-done.23.rest_3_), channel_id=1, source_target_pairs={{0,1},{1,0},{2,3},{3,2},{4,5},{5,4},{6,7},{7,6},{8,9},{9,8},{10,11... | collective-permute-start | bytes 294920 | tf_op jit(solution)/shard_map/ppermute | solution.py:395
  58.9 1.6 %collective-permute-start.26 = (f32[4,48,128]{2,1,0:T(8,128)S(1)}, f32[4,48,128]{2,1,0:T(8,128)S(1)}, u32[]{:S(2)}, u32[]{:S(2)}) collective-permute-start(f32[4,48,128]{2,1,0:T(8,128)S(1)} %collective-permute-done.22.rest_2_), channel_id=1, source_target_pairs={{0,1},{1,0},{2,3},{3,2},{4,5},{5,4},{6,7},{7,6},{8,9},{9,8},{10,11... | collective-permute-start | bytes 294920 | tf_op jit(solution)/shard_map/ppermute | solution.py:395
  59.1 1.5 %collective-permute-start.25 = (f32[4,48,128]{2,1,0:T(8,128)S(1)}, f32[4,48,128]{2,1,0:T(8,128)S(1)}, u32[]{:S(2)}, u32[]{:S(2)}) collective-permute-start(f32[4,48,128]{2,1,0:T(8,128)S(1)} %collective-permute-done.21.rest_1_), channel_id=1, source_target_pairs={{0,1},{1,0},{2,3},{3,2},{4,5},{5,4},{6,7},{7,6},{8,9},{9,8},{10,11... | collective-permute-start | bytes 294920 | tf_op jit(solution)/shard_map/ppermute | solution.py:395
  62.8 3.8 %collective-permute-start.28 = (f32[48,96]{1,0:T(8,128)S(1)}, f32[48,96]{1,0:T(8,128)S(1)}, u32[]{:S(2)}, u32[]{:S(2)}) collective-permute-start(f32[48,96]{1,0:T(8,128)S(1)} %get-tuple-element.22), channel_id=1, source_target_pairs={{0,4},{1,5},{2,6},{3,7},{4,0},{5,1},{6,2},{7,3},{8,12},{9,13},{10,... | collective-permute-start | bytes 55304 | tf_op jit(solution)/shard_map/ppermute | solution.py:395
  66.6 6.2 %collective-permute-start.31 = (f32[2,48,96]{2,1,0:T(8,128)S(1)}, f32[2,48,96]{2,1,0:T(8,128)S(1)}, u32[]{:S(2)}, u32[]{:S(2)}) collective-permute-start(f32[2,48,96]{2,1,0:T(8,128)S(1)} %pad_maximum_fusion.5.refs_0_), channel_id=1, source_target_pairs={{0,24},{1,25},{2,26},{3,27},{4,28},{5,29},{6,30},{7,31},{8,16},{9,... | collective-permute-start | bytes 110600 | tf_op jit(solution)/shard_map/ppermute | solution.py:395
  68.8 5.4 %collective-permute-start.30 = (f32[2,48,96]{2,1,0:T(8,128)S(1)}, f32[2,48,96]{2,1,0:T(8,128)S(1)}, u32[]{:S(2)}, u32[]{:S(2)}) collective-permute-start(f32[2,48,96]{2,1,0:T(8,128)S(1)} %pad_maximum_fusion.5.refs_0_), channel_id=1, source_target_pairs={{0,16},{1,17},{2,18},{3,19},{4,20},{5,21},{6,22},{7,23},{8,24},{9,... | collective-permute-start | bytes 110600 | tf_op jit(solution)/shard_map/ppermute | solution.py:395
  69.9 4.6 %collective-permute-start.29 = (f32[2,48,96]{2,1,0:T(8,128)S(1)}, f32[2,48,96]{2,1,0:T(8,128)S(1)}, u32[]{:S(2)}, u32[]{:S(2)}) collective-permute-start(f32[2,48,96]{2,1,0:T(8,128)S(1)} %pad_maximum_fusion.5.refs_0_), channel_id=1, source_target_pairs={{0,8},{1,9},{2,10},{3,11},{4,12},{5,13},{6,14},{7,15},{8,0},{9,1},... | collective-permute-start | bytes 110600 | tf_op jit(solution)/shard_map/ppermute | solution.py:395

commit v8 on v7

--- a/solution.py
+++ b/solution.py
@@ -148,45 +148,14 @@
     return both[:rank] + (both[rank:] + dot_nt(high, padded_low))
 
 
-def blur_kernel(cube_ref, taps_x_hbm, taps_y_hbm, w_hbm, xh_ref, xl_ref, w_here_ref, keep_0, give_0, keep_1, give_1,
-                taps_x_ref, taps_y_ref, w_ref, sems, work_ref, kx_ref, ky_ref):
-    step = pl.program_id(0)
-    taps = taps_x_ref.shape[0]
-    margin = (taps - 1) // 2
+def blur_group(step, cube_ref, kx_ref, ky_ref, xh_ref, xl_ref, margin):
     height = cube_ref.shape[1]
-    rank = w_ref.shape[0]
-
-    @pl.when(step == 0)
-    def _():
-        copies = [
-            pltpu.make_async_copy(taps_x_hbm, taps_x_ref, sems.at[0]),
-            pltpu.make_async_copy(taps_y_hbm, taps_y_ref, sems.at[1]),
-            pltpu.make_async_copy(w_hbm, w_ref, sems.at[2]),
-        ]
-        for copy in copies:
-            copy.start()
-        for copy in copies:
-            copy.wait()
-        gram = fold(band_gram(w_ref[...])[:, :rank])
-        keep_0[PIECES * rank:] = gram
-        give_0[PIECES * rank:] = gram
-        normalized_taps(taps_x_ref, True, work_ref, kx_ref)
-        normalized_taps(taps_y_ref, False, work_ref, ky_ref)
-        kx_ref[...] = pltpu.roll(kx_ref[...], LANES - margin, 1)
-        per_vector = LANES // height
-        place = lax.broadcasted_iota(jnp.int32, (LANES, LANES), 0) % per_vector
-        values = ky_ref[...]
-        placed = values
-        for k in range(1, per_vector):
-            placed = jnp.where(place == k, pltpu.roll(values, k * height, 1), placed)
-        ky_ref[...] = placed
-
     halves = []
     for half in range(GROUP // 8):
         done = []
-        for plane in range(8 * half, 8 * half + 8):
-            row = kx_ref[pl.ds(step * GROUP + plane, 1), :]
-            done.append(blur_plane(cube_ref[plane], row, margin))
+        for k in range(8 * half, 8 * half + 8):
+            plane = step * GROUP + k
+            done.append(blur_plane(cube_ref[plane], kx_ref[pl.ds(plane, 1), :], margin))
         high, low = split(jnp.concatenate(done, axis=0))
         rows = ky_ref[pl.ds(pl.multiple_of(step * GROUP + 8 * half, 8), 8), :]
         table_high, table_low = row_table(rows, margin, height)
@@ -197,39 +166,82 @@
     xh_ref[:, planes_here, :] = high
     xl_ref[:, planes_here, :] = low
 
-    @pl.when(step == pl.num_programs(0) - 1)
-    def _():
-        planes = xh_ref.shape[1]
-        band = w_ref.shape[1]
-        me_sp = lax.axis_index("sp")
-        me_bd = lax.axis_index("bd")
-        tall = height // lax.axis_size("bd")
-        wide = 2 * LANES // lax.axis_size("sp")
-        shift = lax.rem(band - me_sp * planes, band)
-        w_here = pltpu.roll(w_ref[...], shift, 1)[:, :2 * LANES]
-        w_here_ref[...] = w_here[:, :planes]
-        lane = lax.broadcasted_iota(jnp.int32, w_here.shape, 1)
-        w_here = jnp.where(lane < planes, w_here, 0.0)
-        w_high = w_here.astype(BF16).astype(F32)
-        w_both = jnp.concatenate([w_high + pltpu.roll(w_high, planes, 1), w_here - w_high], axis=0)
-        w_both = w_both.astype(BF16)[:, :2 * planes]
-        for chain in range(2):
-            for rel_bd in (1, 3, 0, 2):
-                first_row = lax.bitwise_xor(me_bd, rel_bd) * tall + 4 * chain
-                sums = []
-                for row in range(4):
-                    image = jnp.concatenate([xh_ref[first_row + row], xl_ref[first_row + row]], axis=0)
-                    both = dot(w_both, image)
-                    sums.append(both[:rank] + both[rank:])
-                refs = ((keep_0, give_0), (keep_1, give_1))[chain]
-                for column in range(2):
-                    pieces = exchange_blocks(
-                        [value[:, column * LANES:(column + 1) * LANES] for value in sums], wide)
-                    for k in range(4):
-                        rel_sp = lax.bitwise_xor(me_sp, column * 4 + k)
-                        side = 3 - rel_sp % 2 if rel_bd // 2 else rel_sp % 2
-                        first = pl.multiple_of((side * 4 + rel_sp // 2) * rank, 8)
-                        refs[rel_bd % 2][pl.ds(first, rank)] = pieces[k]
+
+def blur_kernel(cube_hbm, taps_x_hbm, taps_y_hbm, w_hbm, xh_ref, xl_ref, w_here_ref, keep_0, give_0, keep_1, give_1,
+                cube_ref, taps_x_ref, taps_y_ref, w_ref, sems, chunk_sems, work_ref, kx_ref, ky_ref):
+    taps = taps_x_ref.shape[0]
+    margin = (taps - 1) // 2
+    height = cube_ref.shape[1]
+    rank = w_ref.shape[0]
+    groups = cube_ref.shape[0] // GROUP
+
+    def chunk(step):
+        here = pl.ds(step * GROUP, GROUP)
+        return pltpu.make_async_copy(cube_hbm.at[here], cube_ref.at[here], chunk_sems.at[step])
+
+    copies = [
+        pltpu.make_async_copy(taps_x_hbm, taps_x_ref, sems.at[0]),
+        pltpu.make_async_copy(taps_y_hbm, taps_y_ref, sems.at[1]),
+        pltpu.make_async_copy(w_hbm, w_ref, sems.at[2]),
+    ]
+    for copy in copies:
+        copy.start()
+    for step in range(groups):
+        chunk(step).start()
+    copies[0].wait()
+    normalized_taps(taps_x_ref, True, work_ref, kx_ref)
+    kx_ref[...] = pltpu.roll(kx_ref[...], LANES - margin, 1)
+    copies[1].wait()
+    normalized_taps(taps_y_ref, False, work_ref, ky_ref)
+    per_vector = LANES // height
+    place = lax.broadcasted_iota(jnp.int32, (LANES, LANES), 0) % per_vector
+    values = ky_ref[...]
+    placed = values
+    for k in range(1, per_vector):
+        placed = jnp.where(place == k, pltpu.roll(values, k * height, 1), placed)
+    ky_ref[...] = placed
+    copies[2].wait()
+
+    def body(step, carry):
+        chunk(step).wait()
+        blur_group(step, cube_ref, kx_ref, ky_ref, xh_ref, xl_ref, margin)
+        return carry
+
+    lax.fori_loop(0, groups, body, 0)
+    gram = fold(band_gram(w_ref[...])[:, :rank])
+    keep_0[PIECES * rank:] = gram
+    give_0[PIECES * rank:] = gram
+    planes = xh_ref.shape[1]
+    band = w_ref.shape[1]
+    me_sp = lax.axis_index("sp")
+    me_bd = lax.axis_index("bd")
+    tall = height // lax.axis_size("bd")
+    wide = 2 * LANES // lax.axis_size("sp")
+    shift = lax.rem(band - me_sp * planes, band)
+    w_here = pltpu.roll(w_ref[...], shift, 1)[:, :2 * LANES]
+    w_here_ref[...] = w_here[:, :planes]
+    lane = lax.broadcasted_iota(jnp.int32, w_here.shape, 1)
+    w_here = jnp.where(lane < planes, w_here, 0.0)
+    w_high = w_here.astype(BF16).astype(F32)
+    w_both = jnp.concatenate([w_high + pltpu.roll(w_high, planes, 1), w_here - w_high], axis=0)
+    w_both = w_both.astype(BF16)[:, :2 * planes]
+    for chain in range(2):
+        for rel_bd in (1, 3, 0, 2):
+            first_row = lax.bitwise_xor(me_bd, rel_bd) * tall + 4 * chain
+            sums = []
+            for row in range(4):
+                image = jnp.concatenate([xh_ref[first_row + row], xl_ref[first_row + row]], axis=0)
+                both = dot(w_both, image)
+                sums.append(both[:rank] + both[rank:])
+            refs = ((keep_0, give_0), (keep_1, give_1))[chain]
+            for column in range(2):
+                pieces = exchange_blocks(
+                    [value[:, column * LANES:(column + 1) * LANES] for value in sums], wide)
+                for k in range(4):
+                    rel_sp = lax.bitwise_xor(me_sp, column * 4 + k)
+                    side = 3 - rel_sp % 2 if rel_bd // 2 else rel_sp % 2
+                    first = pl.multiple_of((side * 4 + rel_sp // 2) * rank, 8)
+                    refs[rel_bd % 2][pl.ds(first, rank)] = pieces[k]
 
 
 def blur_call(cube, taps_x, taps_y, w_rows):
@@ -239,19 +251,17 @@
     second = jax.ShapeDtypeStruct((PIECES * rank, LANES), F32)
     image = (height, planes, length)
     mine = jax.ShapeDtypeStruct((rank, planes), F32)
-    whole = lambda shape: pl.BlockSpec(shape, lambda i: (0,) * len(shape))
+    in_hbm = [pltpu.with_memory_space_constraint(value, pltpu.HBM) for value in (cube, taps_x, taps_y, w_rows)]
     return pl.pallas_call(
         blur_kernel,
-        grid=(planes // GROUP,),
         out_shape=[jax.ShapeDtypeStruct(image, BF16)] * 2 + [mine, first, first, second, second],
-        in_specs=[pl.BlockSpec((GROUP, height, length), lambda i: (i, 0, 0))]
-        + [pl.BlockSpec(memory_space=pltpu.HBM)] * 3,
-        out_specs=[whole(image)] * 2 + [whole(mine.shape)] + [whole(first.shape)] * 2 + [whole(second.shape)] * 2,
-        scratch_shapes=[pltpu.VMEM(value.shape, F32) for value in (taps_x, taps_y, w_rows)]
-        + [pltpu.SemaphoreType.DMA((3,))] + [pltpu.VMEM((LANES, LANES), F32)] * 3,
-        compiler_params=pltpu.CompilerParams(
-            dimension_semantics=("arbitrary",), vmem_limit_bytes=VMEM_LIMIT),
-    )(cube, taps_x, taps_y, w_rows)
+        in_specs=[pl.BlockSpec(memory_space=pltpu.HBM)] * 4,
+        out_specs=in_vmem(7),
+        scratch_shapes=[pltpu.VMEM(value.shape, F32) for value in (cube, taps_x, taps_y, w_rows)]
+        + [pltpu.SemaphoreType.DMA((3,)), pltpu.SemaphoreType.DMA((planes // GROUP,))]
+        + [pltpu.VMEM((LANES, LANES), F32)] * 3,
+        compiler_params=pltpu.CompilerParams(vmem_limit_bytes=VMEM_LIMIT),
+    )(*in_hbm)
 
 
 def ratio_kernel(mine_ref, other_ref, h_ref, out_ref):

time: 75.6 us -> 73.1 us (0.967)
  local copies, waits for them, and re-layouts: 2.34 us -> 0.02 us
    unnamed x8 -> x2, local copies, waits for them, and re-layouts: 2.32 us -> 0.01 us
where the time goes in v8:
time: 73.1 us; the launch traced here: 73 us
  starting transfers between devices  34.4 us (47%)
  waiting for transfers between devices  23 us (31%)
  Pallas kernels  14.6 us (20%)
  between operations  0.77 us (1%)
    ppermute x32, starting transfers between devices, send(): return lax.ppermute(value, ('sp', 'bd'), pairs)  34.4 us
    ppermute x32, waiting for transfers between devices, send(): return lax.ppermute(value, ('sp', 'bd'), pairs)  23 us
    pallas_call x1, Pallas kernels, blur_call(): pl.pallas_call(blur_kernel, out_shape=[jax.ShapeDtypeStruct(image, BF16)]...  10.3 us
    pallas_call x1, Pallas kernels, second_call(): pl.pallas_call(second_kernel, out_shape=[jax.ShapeDtypeStruct(w_here.shap...  2.24 us
  transfers between devices with their start and end apart: 32, of which 17 were waited for; matrix products, arithmetic and copies ran while one was open for 0% of the time, Pallas kernels for 2%

profile of v8, /device:TPU:0, one launch (start us, length us, event | category | flops | bytes accessed | tf_op | source)
XLA Modules:
  0.0 73.0 jit_solution(12234894728156482482)
XLA Ops:
  0.6 10.3 %shard_map.68 = (bf16[32,96,256]{2,1,0:T(8,128)(2,1)S(1)}, bf16[32,96,256]{2,1,0:T(8,128)(2,1)S(1)}, f32[48,96]{1,0:T(8,128)S(1)}, f32[792,128]{1,0:T(8,128)S(1)...) custom-call(f32[96,32,256]{2,1,0:T(8,128)} %bitcast.31, f32[25,1,96]{2,1,0:T(1,128)} %bitcast.35, ...), custom_call_target="tpu_custom_call" | custom-call | tf_op jit(solution)/shard_map/pallas_call | solution.py:255
  10.9 0.5 collective-permute-start.4
  11.5 0.1 collective-permute-start
  11.6 1.3 %collective-permute-done.4 = f32[768,128]{1,0:T(8,128)S(1)} collective-permute-done((f32[768,128]{1,0:T(8,128)S(1)}, f32[768,128]{1,0:T(8,128)S(1)}, u32[]{:S(2)}, u32[]{:S(2)}) %collective-permute-start.4) | collective-permute-done | bytes 393248 | tf_op jit(solution)/shard_map/ppermute | solution.py:405
  12.8 0.1 slice_add_fusion.4
  12.9 3.9 %collective-permute-start.7 = (f32[192,128]{1,0:T(8,128)S(1)}, f32[192,128]{1,0:T(8,128)S(1)}, u32[]{:S(2)}, u32[]{:S(2)}) collective-permute-start(f32[192,128]{1,0:T(8,128)S(1)} %get-tuple-element.28), channel_id=1, source_target_pairs={{0,6},{1,7},{2,4},{3,5},{4,2},{5,3},{6,0},{7,1},{8,14},{9,15},{10,... | collective-permute-start | bytes 294920 | tf_op jit(solution)/shard_map/ppermute | solution.py:405
  16.8 0.5 collective-permute-start.6
  17.3 0.1 collective-permute-start.5
  17.4 0.0 collective-permute-done
  17.4 2.9 %collective-permute-start.3 = (f32[192,128]{1,0:T(8,128)S(1)}, f32[192,128]{1,0:T(8,128)S(1)}, u32[]{:S(2)}, u32[]{:S(2)}) collective-permute-start(f32[192,128]{1,0:T(8,128)S(1)} %get-tuple-element.25), channel_id=1, source_target_pairs={{0,6},{1,7},{2,4},{3,5},{4,2},{5,3},{6,0},{7,1},{8,14},{9,15},{10,... | collective-permute-start | bytes 294920 | tf_op jit(solution)/shard_map/ppermute | solution.py:405
  20.4 0.5 collective-permute-start.2
  20.9 0.0 collective-permute-done.7
  20.9 1.4 %collective-permute-start.1 = (f32[216,128]{1,0:T(8,128)S(1)}, f32[216,128]{1,0:T(8,128)S(1)}, u32[]{:S(2)}, u32[]{:S(2)}) collective-permute-start(f32[216,128]{1,0:T(8,128)S(1)} %slice_add_fusion.mine_ref), channel_id=1, source_target_pairs={{0,2},{1,3},{2,0},{3,1},{4,6},{5,7},{6,4},{7,5},{8,10},{9,11},{10,... | collective-permute-start | bytes 331784 | tf_op jit(solution)/shard_map/ppermute | solution.py:405
  22.3 1.0 %collective-permute-done.6 = f32[192,128]{1,0:T(8,128)S(1)} collective-permute-done((f32[192,128]{1,0:T(8,128)S(1)}, f32[192,128]{1,0:T(8,128)S(1)}, u32[]{:S(2)}, u32[]{:S(2)}) %collective-permute-start.6) | collective-permute-done | bytes 98336 | tf_op jit(solution)/shard_map/ppermute | solution.py:405
  23.2 0.0 collective-permute-done.5
  23.3 2.5 %collective-permute-done.3 = f32[192,128]{1,0:T(8,128)S(1)} collective-permute-done((f32[192,128]{1,0:T(8,128)S(1)}, f32[192,128]{1,0:T(8,128)S(1)}, u32[]{:S(2)}, u32[]{:S(2)}) %collective-permute-start.3) | collective-permute-done | bytes 98336 | tf_op jit(solution)/shard_map/ppermute | solution.py:405
  25.8 0.7 collective-permute-done.2
  26.4 0.1 collective-permute-done.1.other_ref
  26.5 1.8 %collective-permute-start.8 = (f32[48,256]{1,0:T(8,128)S(1)}, f32[48,256]{1,0:T(8,128)S(1)}, u32[]{:S(2)}, u32[]{:S(2)}) collective-permute-start(f32[48,256]{1,0:T(8,128)S(1)} %pad_maximum_fusion.2), channel_id=1, source_target_pairs={{0,8},{1,9},{2,10},{3,11},{4,12},{5,13},{6,14},{7,15},{8,0},{9,1},... | collective-permute-start | bytes 147464 | tf_op jit(solution)/shard_map/ppermute | solution.py:405
  28.3 2.6 %collective-permute-start.9 = (f32[48,256]{1,0:T(8,128)S(1)}, f32[48,256]{1,0:T(8,128)S(1)}, u32[]{:S(2)}, u32[]{:S(2)}) collective-permute-start(f32[48,256]{1,0:T(8,128)S(1)} %pad_maximum_fusion.3), channel_id=1, source_target_pairs={{0,16},{1,17},{2,18},{3,19},{4,20},{5,21},{6,22},{7,23},{8,24},{9,... | collective-permute-start | bytes 147464 | tf_op jit(solution)/shard_map/ppermute | solution.py:405
  30.9 0.1 collective-permute-start.10
  31.0 0.3 shard_map.69
  31.3 0.0 collective-permute-done.8
  31.3 2.5 %collective-permute-done.9 = f32[48,256]{1,0:T(8,128)S(1)} collective-permute-done((f32[48,256]{1,0:T(8,128)S(1)}, f32[48,256]{1,0:T(8,128)S(1)}, u32[]{:S(2)}, u32[]{:S(2)}) %collective-permute-start.9) | collective-permute-done | bytes 49184 | tf_op jit(solution)/shard_map/ppermute | solution.py:405
  33.8 3.0 %collective-permute-done.10 = f32[48,256]{1,0:T(8,128)S(1)} collective-permute-done((f32[48,256]{1,0:T(8,128)S(1)}, f32[48,256]{1,0:T(8,128)S(1)}, u32[]{:S(2)}, u32[]{:S(2)}) %collective-permute-start.10) | collective-permute-done | bytes 49184 | tf_op jit(solution)/shard_map/ppermute | solution.py:405
  36.8 0.7 collective-permute-start.13
  37.5 0.0 collective-permute-start.12
  37.5 3.8 %collective-permute-start.11 = (f32[48,256]{1,0:T(8,128)S(1)}, f32[48,256]{1,0:T(8,128)S(1)}, u32[]{:S(2)}, u32[]{:S(2)}) collective-permute-start(f32[48,256]{1,0:T(8,128)S(1)} %fusion.1), channel_id=1, source_target_pairs={{0,8},{1,9},{2,10},{3,11},{4,12},{5,13},{6,14},{7,15},{8,0},{9,1},... | collective-permute-start | bytes 147464 | tf_op jit(solution)/shard_map/ppermute | solution.py:405
  41.3 1.6 %collective-permute-done.13 = f32[48,256]{1,0:T(8,128)S(1)} collective-permute-done((f32[48,256]{1,0:T(8,128)S(1)}, f32[48,256]{1,0:T(8,128)S(1)}, u32[]{:S(2)}, u32[]{:S(2)}) %collective-permute-start.13) | collective-permute-done | bytes 49184 | tf_op jit(solution)/shard_map/ppermute | solution.py:405
  42.9 0.7 collective-permute-done.12
  43.6 0.1 collective-permute-start.17
  43.7 2.0 %collective-permute-start.16 = (f32[4,48,128]{2,1,0:T(8,128)S(1)}, f32[4,48,128]{2,1,0:T(8,128)S(1)}, u32[]{:S(2)}, u32[]{:S(2)}) collective-permute-start(f32[4,48,128]{2,1,0:T(8,128)S(1)} %pad_maximum_fusion.rest_0_), channel_id=1, source_target_pairs={{0,6},{1,7},{2,4},{3,5},{4,2},{5,3},{6,0},{7,1},{8,14},{9,15},{10,... | collective-permute-start | bytes 294920 | tf_op jit(solution)/shard_map/ppermute | solution.py:405
  45.7 1.0 %collective-permute-start.15 = (f32[4,48,128]{2,1,0:T(8,128)S(1)}, f32[4,48,128]{2,1,0:T(8,128)S(1)}, u32[]{:S(2)}, u32[]{:S(2)}) collective-permute-start(f32[4,48,128]{2,1,0:T(8,128)S(1)} %pad_maximum_fusion.rest_0_), channel_id=1, source_target_pairs={{0,2},{1,3},{2,0},{3,1},{4,6},{5,7},{6,4},{7,5},{8,10},{9,11},{10,... | collective-permute-start | bytes 294920 | tf_op jit(solution)/shard_map/ppermute | solution.py:405
  46.7 0.5 collective-permute-start.14
  47.2 2.0 %collective-permute-start.23 = (f32[4,48,128]{2,1,0:T(8,128)S(1)}, f32[4,48,128]{2,1,0:T(8,128)S(1)}, u32[]{:S(2)}, u32[]{:S(2)}) collective-permute-start(f32[4,48,128]{2,1,0:T(8,128)S(1)} %pad_maximum_fusion.1.rest_0_), channel_id=1, source_target_pairs={{0,6},{1,7},{2,4},{3,5},{4,2},{5,3},{6,0},{7,1},{8,14},{9,15},{10,... | collective-permute-start | bytes 294920 | tf_op jit(solution)/shard_map/ppermute | solution.py:405
  49.2 0.0 collective-permute-done.17.rest_4_
  49.2 1.0 %collective-permute-start.22 = (f32[4,48,128]{2,1,0:T(8,128)S(1)}, f32[4,48,128]{2,1,0:T(8,128)S(1)}, u32[]{:S(2)}, u32[]{:S(2)}) collective-permute-start(f32[4,48,128]{2,1,0:T(8,128)S(1)} %pad_maximum_fusion.1.rest_0_), channel_id=1, source_target_pairs={{0,2},{1,3},{2,0},{3,1},{4,6},{5,7},{6,4},{7,5},{8,10},{9,11},{10,... | collective-permute-start | bytes 294920 | tf_op jit(solution)/shard_map/ppermute | solution.py:405
  50.3 1.5 %collective-permute-start.21 = (f32[4,48,128]{2,1,0:T(8,128)S(1)}, f32[4,48,128]{2,1,0:T(8,128)S(1)}, u32[]{:S(2)}, u32[]{:S(2)}) collective-permute-start(f32[4,48,128]{2,1,0:T(8,128)S(1)} %pad_maximum_fusion.1.rest_0_), channel_id=1, source_target_pairs={{0,4},{1,5},{2,6},{3,7},{4,0},{5,1},{6,2},{7,3},{8,12},{9,13},{10,... | collective-permute-start | bytes 294920 | tf_op jit(solution)/shard_map/ppermute | solution.py:405
  51.7 1.2 %collective-permute-done.15.rest_2_ = f32[4,48,128]{2,1,0:T(8,128)S(1)} collective-permute-done((f32[4,48,128]{2,1,0:T(8,128)S(1)}, f32[4,48,128]{2,1,0:T(8,128)S(1)}, u32[]{:S(2)}, u32[]{:S(2)}) %collective-permute-start.15) | collective-permute-done | bytes 98336 | tf_op jit(solution)/shard_map/ppermute | solution.py:405
  52.9 0.0 collective-permute-start.20
  52.9 0.5 collective-permute-start.19
  53.4 1.5 %collective-permute-done.23.rest_3_ = f32[4,48,128]{2,1,0:T(8,128)S(1)} collective-permute-done((f32[4,48,128]{2,1,0:T(8,128)S(1)}, f32[4,48,128]{2,1,0:T(8,128)S(1)}, u32[]{:S(2)}, u32[]{:S(2)}) %collective-permute-start.23) | collective-permute-done | bytes 98336 | tf_op jit(solution)/shard_map/ppermute | solution.py:405
  54.9 1.2 %collective-permute-done.22.rest_2_ = f32[4,48,128]{2,1,0:T(8,128)S(1)} collective-permute-done((f32[4,48,128]{2,1,0:T(8,128)S(1)}, f32[4,48,128]{2,1,0:T(8,128)S(1)}, u32[]{:S(2)}, u32[]{:S(2)}) %collective-permute-start.22) | collective-permute-done | bytes 98336 | tf_op jit(solution)/shard_map/ppermute | solution.py:405
  56.1 0.0 collective-permute-start.24
  56.1 0.1 collective-permute-done.21.rest_1_
  56.2 0.4 collective-permute-start.27
  56.6 0.0 collective-permute-done.20.rest_7_
  56.6 0.1 collective-permute-start.26
  56.7 0.4 collective-permute-start.25
  57.1 0.0 collective-permute-done.18.rest_5_
  57.1 1.0 %shard_map.70 = (f32[288,96]{1,0:T(8,128)S(1)}, f32[32,32,48]{2,1,0:T(8,128)S(1)}) custom-call(bf16[32,96,256]{2,1,0:T(8,128)(2,1)S(1)} %get-tuple-element.13.xh_ref, bf16[32,96,256]{2,1,0:T(8,128)(2,1)S(1)} %get-tuple-element.14.xl_ref, f32[4,48,128]{2,1,0:T(8,128)S(1)} %pad_maximum_fusion.rest_0_, f32[4,48,128]{2,1,0:T(8,128)S(1)} %collective-permute-done.14.rest_1_, ...), custom_call_target="tpu_custom_call" | custom-call | tf_op jit(solution)/shard_map/pallas_call | solution.py:331
  58.2 0.0 collective-permute-done.24.rest_4_
  58.2 0.0 collective-permute-done.26.rest_6_
  58.2 0.0 collective-permute-done.25.rest_5_
  58.2 2.2 %shard_map.71 = (f32[48,96]{1,0:T(8,128)S(1)}, f32[32,32,48]{2,1,0:T(8,128)}) custom-call(bf16[32,96,256]{2,1,0:T(8,128)(2,1)S(1)} %get-tuple-element.13.xh_ref, bf16[32,96,256]{2,1,0:T(8,128)(2,1)S(1)} %get-tuple-element.14.xl_ref, f32[48,96]{1,0:T(8,128)S(1)} %get-tuple-element.15.w_ref, f32[288,96]{1,0:T(8,128)S(1)} %get-tuple-element.20.total_ref, ...), custom_call_target="tpu_custom_call" | custom-call | tf_op jit(solution)/shard_map/pallas_call | solution.py:358
  60.5 1.5 %collective-permute-start.28 = (f32[48,96]{1,0:T(8,128)S(1)}, f32[48,96]{1,0:T(8,128)S(1)}, u32[]{:S(2)}, u32[]{:S(2)}) collective-permute-start(f32[48,96]{1,0:T(8,128)S(1)} %get-tuple-element.22), channel_id=1, source_target_pairs={{0,4},{1,5},{2,6},{3,7},{4,0},{5,1},{6,2},{7,3},{8,12},{9,13},{10,... | collective-permute-start | bytes 55304 | tf_op jit(solution)/shard_map/ppermute | solution.py:405
  62.0 2.3 %collective-permute-done.28 = f32[48,96]{1,0:T(8,128)S(1)} collective-permute-done((f32[48,96]{1,0:T(8,128)S(1)}, f32[48,96]{1,0:T(8,128)S(1)}, u32[]{:S(2)}, u32[]{:S(2)}) %collective-permute-start.28) | collective-permute-done | bytes 18464 | tf_op jit(solution)/shard_map/ppermute | solution.py:405
  64.3 2.2 %collective-permute-start.31 = (f32[2,48,96]{2,1,0:T(8,128)S(1)}, f32[2,48,96]{2,1,0:T(8,128)S(1)}, u32[]{:S(2)}, u32[]{:S(2)}) collective-permute-start(f32[2,48,96]{2,1,0:T(8,128)S(1)} %pad_maximum_fusion.5.refs_0_), channel_id=1, source_target_pairs={{0,24},{1,25},{2,26},{3,27},{4,28},{5,29},{6,30},{7,31},{8,16},{9,... | collective-permute-start | bytes 110600 | tf_op jit(solution)/shard_map/ppermute | solution.py:405
  66.5 1.1 %collective-permute-start.30 = (f32[2,48,96]{2,1,0:T(8,128)S(1)}, f32[2,48,96]{2,1,0:T(8,128)S(1)}, u32[]{:S(2)}, u32[]{:S(2)}) collective-permute-start(f32[2,48,96]{2,1,0:T(8,128)S(1)} %pad_maximum_fusion.5.refs_0_), channel_id=1, source_target_pairs={{0,16},{1,17},{2,18},{3,19},{4,20},{5,21},{6,22},{7,23},{8,24},{9,... | collective-permute-start | bytes 110600 | tf_op jit(solution)/shard_map/ppermute | solution.py:405
  67.6 1.1 %collective-permute-start.29 = (f32[2,48,96]{2,1,0:T(8,128)S(1)}, f32[2,48,96]{2,1,0:T(8,128)S(1)}, u32[]{:S(2)}, u32[]{:S(2)}) collective-permute-start(f32[2,48,96]{2,1,0:T(8,128)S(1)} %pad_maximum_fusion.5.refs_0_), channel_id=1, source_target_pairs={{0,8},{1,9},{2,10},{3,11},{4,12},{5,13},{6,14},{7,15},{8,0},{9,1},... | collective-permute-start | bytes 110600 | tf_op jit(solution)/shard_map/ppermute | solution.py:405
  68.7 1.8 %collective-permute-done.31.refs_3_ = f32[2,48,96]{2,1,0:T(8,128)S(1)} collective-permute-done((f32[2,48,96]{2,1,0:T(8,128)S(1)}, f32[2,48,96]{2,1,0:T(8,128)S(1)}, u32[]{:S(2)}, u32[]{:S(2)}) %collective-permute-start.31) | collective-permute-done | bytes 36896 | tf_op jit(solution)/shard_map/ppermute | solution.py:405
  70.5 1.4 %collective-permute-done.30.refs_2_ = f32[2,48,96]{2,1,0:T(8,128)S(1)} collective-permute-done((f32[2,48,96]{2,1,0:T(8,128)S(1)}, f32[2,48,96]{2,1,0:T(8,128)S(1)}, u32[]{:S(2)}, u32[]{:S(2)}) %collective-permute-start.30) | collective-permute-done | bytes 36896 | tf_op jit(solution)/shard_map/ppermute | solution.py:405
  71.9 0.3 collective-permute-done.29.refs_1_
  72.2 0.8 %shard_map.72 = f32[48,768]{1,0:T(8,128)} custom-call(f32[2,48,96]{2,1,0:T(8,128)S(1)} %pad_maximum_fusion.5.refs_0_, f32[2,48,96]{2,1,0:T(8,128)S(1)} %collective-permute-done.29.refs_1_, f32[2,48,96]{2,1,0:T(8,128)S(1)} %collective-permute-done.30.refs_2_, f32[2,48,96]{2,1,0:T(8,128)S(1)} %collective-permute-done.31.refs_3_), custom_call_target="tpu_custom_call" | custom-call | tf_op jit(solution)/shard_map/pallas_call | solution.py:389
  (23 shorter events, 0.2 us)
Async XLA Ops:
  10.9 1.9 %collective-permute-start.4 = (f32[768,128]{1,0:T(8,128)S(1)}, f32[768,128]{1,0:T(8,128)S(1)}, u32[]{:S(2)}, u32[]{:S(2)}) collective-permute-start(f32[768,128]{1,0:T(8,128)S(1)} %get-tuple-element.19), channel_id=1, source_target_pairs={{0,1},{1,0},{2,3},{3,2},{4,5},{5,4},{6,7},{7,6},{8,9},{9,8},{10,11... | collective-permute-start | bytes 1179656 | tf_op jit(solution)/shard_map/ppermute | solution.py:405
  11.5 5.9 %collective-permute-start = (f32[792,128]{1,0:T(8,128)S(1)}, f32[792,128]{1,0:T(8,128)S(1)}, u32[]{:S(2)}, u32[]{:S(2)}) collective-permute-start(f32[792,128]{1,0:T(8,128)S(1)} %get-tuple-element.17), channel_id=1, source_target_pairs={{0,1},{1,0},{2,3},{3,2},{4,5},{5,4},{6,7},{7,6},{8,9},{9,8},{10,11... | collective-permute-start | bytes 1216520 | tf_op jit(solution)/shard_map/ppermute | solution.py:405
  12.8 18.2 %copy-start = (f32[48,32,32]{0,2,1:T(8,128)S(1)}, f32[48,32,32]{0,2,1:T(8,128)}, u32[]{:S(2)}) copy-start(f32[48,32,32]{0,2,1:T(8,128)} %param.9) | copy-start | bytes 589828
  12.9 8.0 %collective-permute-start.7 = (f32[192,128]{1,0:T(8,128)S(1)}, f32[192,128]{1,0:T(8,128)S(1)}, u32[]{:S(2)}, u32[]{:S(2)}) collective-permute-start(f32[192,128]{1,0:T(8,128)S(1)} %get-tuple-element.28), channel_id=1, source_target_pairs={{0,6},{1,7},{2,4},{3,5},{4,2},{5,3},{6,0},{7,1},{8,14},{9,15},{10,... | collective-permute-start | bytes 294920 | tf_op jit(solution)/shard_map/ppermute | solution.py:405
  16.8 6.5 %collective-permute-start.6 = (f32[192,128]{1,0:T(8,128)S(1)}, f32[192,128]{1,0:T(8,128)S(1)}, u32[]{:S(2)}, u32[]{:S(2)}) collective-permute-start(f32[192,128]{1,0:T(8,128)S(1)} %get-tuple-element.29), channel_id=1, source_target_pairs={{0,2},{1,3},{2,0},{3,1},{4,6},{5,7},{6,4},{7,5},{8,10},{9,11},{10,... | collective-permute-start | bytes 294920 | tf_op jit(solution)/shard_map/ppermute | solution.py:405
  17.3 6.0 %collective-permute-start.5 = (f32[192,128]{1,0:T(8,128)S(1)}, f32[192,128]{1,0:T(8,128)S(1)}, u32[]{:S(2)}, u32[]{:S(2)}) collective-permute-start(f32[192,128]{1,0:T(8,128)S(1)} %get-tuple-element.30), channel_id=1, source_target_pairs={{0,4},{1,5},{2,6},{3,7},{4,0},{5,1},{6,2},{7,3},{8,12},{9,13},{10,... | collective-permute-start | bytes 294920 | tf_op jit(solution)/shard_map/ppermute | solution.py:405
  17.4 8.3 %collective-permute-start.3 = (f32[192,128]{1,0:T(8,128)S(1)}, f32[192,128]{1,0:T(8,128)S(1)}, u32[]{:S(2)}, u32[]{:S(2)}) collective-permute-start(f32[192,128]{1,0:T(8,128)S(1)} %get-tuple-element.25), channel_id=1, source_target_pairs={{0,6},{1,7},{2,4},{3,5},{4,2},{5,3},{6,0},{7,1},{8,14},{9,15},{10,... | collective-permute-start | bytes 294920 | tf_op jit(solution)/shard_map/ppermute | solution.py:405
  20.4 6.1 %collective-permute-start.2 = (f32[192,128]{1,0:T(8,128)S(1)}, f32[192,128]{1,0:T(8,128)S(1)}, u32[]{:S(2)}, u32[]{:S(2)}) collective-permute-start(f32[192,128]{1,0:T(8,128)S(1)} %get-tuple-element.26), channel_id=1, source_target_pairs={{0,4},{1,5},{2,6},{3,7},{4,0},{5,1},{6,2},{7,3},{8,12},{9,13},{10,... | collective-permute-start | bytes 294920 | tf_op jit(solution)/shard_map/ppermute | solution.py:405
  20.9 5.6 %collective-permute-start.1 = (f32[216,128]{1,0:T(8,128)S(1)}, f32[216,128]{1,0:T(8,128)S(1)}, u32[]{:S(2)}, u32[]{:S(2)}) collective-permute-start(f32[216,128]{1,0:T(8,128)S(1)} %slice_add_fusion.mine_ref), channel_id=1, source_target_pairs={{0,2},{1,3},{2,0},{3,1},{4,6},{5,7},{6,4},{7,5},{8,10},{9,11},{10,... | collective-permute-start | bytes 331784 | tf_op jit(solution)/shard_map/ppermute | solution.py:405
  26.5 4.7 %collective-permute-start.8 = (f32[48,256]{1,0:T(8,128)S(1)}, f32[48,256]{1,0:T(8,128)S(1)}, u32[]{:S(2)}, u32[]{:S(2)}) collective-permute-start(f32[48,256]{1,0:T(8,128)S(1)} %pad_maximum_fusion.2), channel_id=1, source_target_pairs={{0,8},{1,9},{2,10},{3,11},{4,12},{5,13},{6,14},{7,15},{8,0},{9,1},... | collective-permute-start | bytes 147464 | tf_op jit(solution)/shard_map/ppermute | solution.py:405
  28.3 5.5 %collective-permute-start.9 = (f32[48,256]{1,0:T(8,128)S(1)}, f32[48,256]{1,0:T(8,128)S(1)}, u32[]{:S(2)}, u32[]{:S(2)}) collective-permute-start(f32[48,256]{1,0:T(8,128)S(1)} %pad_maximum_fusion.3), channel_id=1, source_target_pairs={{0,16},{1,17},{2,18},{3,19},{4,20},{5,21},{6,22},{7,23},{8,24},{9,... | collective-permute-start | bytes 147464 | tf_op jit(solution)/shard_map/ppermute | solution.py:405
  30.9 5.9 %collective-permute-start.10 = (f32[48,256]{1,0:T(8,128)S(1)}, f32[48,256]{1,0:T(8,128)S(1)}, u32[]{:S(2)}, u32[]{:S(2)}) collective-permute-start(f32[48,256]{1,0:T(8,128)S(1)} %pad_maximum_fusion.4), channel_id=1, source_target_pairs={{0,24},{1,25},{2,26},{3,27},{4,28},{5,29},{6,30},{7,31},{8,16},{9,... | collective-permute-start | bytes 147464 | tf_op jit(solution)/shard_map/ppermute | solution.py:405
  36.8 6.1 %collective-permute-start.13 = (f32[48,256]{1,0:T(8,128)S(1)}, f32[48,256]{1,0:T(8,128)S(1)}, u32[]{:S(2)}, u32[]{:S(2)}) collective-permute-start(f32[48,256]{1,0:T(8,128)S(1)} %fusion.1), channel_id=1, source_target_pairs={{0,24},{1,25},{2,26},{3,27},{4,28},{5,29},{6,30},{7,31},{8,16},{9,... | collective-permute-start | bytes 147464 | tf_op jit(solution)/shard_map/ppermute | solution.py:405
  37.5 6.0 %collective-permute-start.12 = (f32[48,256]{1,0:T(8,128)S(1)}, f32[48,256]{1,0:T(8,128)S(1)}, u32[]{:S(2)}, u32[]{:S(2)}) collective-permute-start(f32[48,256]{1,0:T(8,128)S(1)} %fusion.1), channel_id=1, source_target_pairs={{0,16},{1,17},{2,18},{3,19},{4,20},{5,21},{6,22},{7,23},{8,24},{9,... | collective-permute-start | bytes 147464 | tf_op jit(solution)/shard_map/ppermute | solution.py:405
  37.5 6.0 %collective-permute-start.11 = (f32[48,256]{1,0:T(8,128)S(1)}, f32[48,256]{1,0:T(8,128)S(1)}, u32[]{:S(2)}, u32[]{:S(2)}) collective-permute-start(f32[48,256]{1,0:T(8,128)S(1)} %fusion.1), channel_id=1, source_target_pairs={{0,8},{1,9},{2,10},{3,11},{4,12},{5,13},{6,14},{7,15},{8,0},{9,1},... | collective-permute-start | bytes 147464 | tf_op jit(solution)/shard_map/ppermute | solution.py:405
  43.6 5.7 %collective-permute-start.17 = (f32[4,48,128]{2,1,0:T(8,128)S(1)}, f32[4,48,128]{2,1,0:T(8,128)S(1)}, u32[]{:S(2)}, u32[]{:S(2)}) collective-permute-start(f32[4,48,128]{2,1,0:T(8,128)S(1)} %pad_maximum_fusion.rest_0_), channel_id=1, source_target_pairs={{0,1},{1,0},{2,3},{3,2},{4,5},{5,4},{6,7},{7,6},{8,9},{9,8},{10,11... | collective-permute-start | bytes 294920 | tf_op jit(solution)/shard_map/ppermute | solution.py:405
  43.7 6.6 %collective-permute-start.16 = (f32[4,48,128]{2,1,0:T(8,128)S(1)}, f32[4,48,128]{2,1,0:T(8,128)S(1)}, u32[]{:S(2)}, u32[]{:S(2)}) collective-permute-start(f32[4,48,128]{2,1,0:T(8,128)S(1)} %pad_maximum_fusion.rest_0_), channel_id=1, source_target_pairs={{0,6},{1,7},{2,4},{3,5},{4,2},{5,3},{6,0},{7,1},{8,14},{9,15},{10,... | collective-permute-start | bytes 294920 | tf_op jit(solution)/shard_map/ppermute | solution.py:405
  45.7 7.2 %collective-permute-start.15 = (f32[4,48,128]{2,1,0:T(8,128)S(1)}, f32[4,48,128]{2,1,0:T(8,128)S(1)}, u32[]{:S(2)}, u32[]{:S(2)}) collective-permute-start(f32[4,48,128]{2,1,0:T(8,128)S(1)} %pad_maximum_fusion.rest_0_), channel_id=1, source_target_pairs={{0,2},{1,3},{2,0},{3,1},{4,6},{5,7},{6,4},{7,5},{8,10},{9,11},{10,... | collective-permute-start | bytes 294920 | tf_op jit(solution)/shard_map/ppermute | solution.py:405
  46.7 6.2 %collective-permute-start.14 = (f32[4,48,128]{2,1,0:T(8,128)S(1)}, f32[4,48,128]{2,1,0:T(8,128)S(1)}, u32[]{:S(2)}, u32[]{:S(2)}) collective-permute-start(f32[4,48,128]{2,1,0:T(8,128)S(1)} %pad_maximum_fusion.rest_0_), channel_id=1, source_target_pairs={{0,4},{1,5},{2,6},{3,7},{4,0},{5,1},{6,2},{7,3},{8,12},{9,13},{10,... | collective-permute-start | bytes 294920 | tf_op jit(solution)/shard_map/ppermute | solution.py:405
  47.2 7.7 %collective-permute-start.23 = (f32[4,48,128]{2,1,0:T(8,128)S(1)}, f32[4,48,128]{2,1,0:T(8,128)S(1)}, u32[]{:S(2)}, u32[]{:S(2)}) collective-permute-start(f32[4,48,128]{2,1,0:T(8,128)S(1)} %pad_maximum_fusion.1.rest_0_), channel_id=1, source_target_pairs={{0,6},{1,7},{2,4},{3,5},{4,2},{5,3},{6,0},{7,1},{8,14},{9,15},{10,... | collective-permute-start | bytes 294920 | tf_op jit(solution)/shard_map/ppermute | solution.py:405
  49.2 6.8 %collective-permute-start.22 = (f32[4,48,128]{2,1,0:T(8,128)S(1)}, f32[4,48,128]{2,1,0:T(8,128)S(1)}, u32[]{:S(2)}, u32[]{:S(2)}) collective-permute-start(f32[4,48,128]{2,1,0:T(8,128)S(1)} %pad_maximum_fusion.1.rest_0_), channel_id=1, source_target_pairs={{0,2},{1,3},{2,0},{3,1},{4,6},{5,7},{6,4},{7,5},{8,10},{9,11},{10,... | collective-permute-start | bytes 294920 | tf_op jit(solution)/shard_map/ppermute | solution.py:405
  50.3 6.0 %collective-permute-start.21 = (f32[4,48,128]{2,1,0:T(8,128)S(1)}, f32[4,48,128]{2,1,0:T(8,128)S(1)}, u32[]{:S(2)}, u32[]{:S(2)}) collective-permute-start(f32[4,48,128]{2,1,0:T(8,128)S(1)} %pad_maximum_fusion.1.rest_0_), channel_id=1, source_target_pairs={{0,4},{1,5},{2,6},{3,7},{4,0},{5,1},{6,2},{7,3},{8,12},{9,13},{10,... | collective-permute-start | bytes 294920 | tf_op jit(solution)/shard_map/ppermute | solution.py:405
  52.9 3.7 %collective-permute-start.20 = (f32[4,48,128]{2,1,0:T(8,128)S(1)}, f32[4,48,128]{2,1,0:T(8,128)S(1)}, u32[]{:S(2)}, u32[]{:S(2)}) collective-permute-start(f32[4,48,128]{2,1,0:T(8,128)S(1)} %collective-permute-done.16.rest_3_), channel_id=1, source_target_pairs={{0,1},{1,0},{2,3},{3,2},{4,5},{5,4},{6,7},{7,6},{8,9},{9,8},{10,11... | collective-permute-start | bytes 294920 | tf_op jit(solution)/shard_map/ppermute | solution.py:405
  52.9 3.8 %collective-permute-start.19 = (f32[4,48,128]{2,1,0:T(8,128)S(1)}, f32[4,48,128]{2,1,0:T(8,128)S(1)}, u32[]{:S(2)}, u32[]{:S(2)}) collective-permute-start(f32[4,48,128]{2,1,0:T(8,128)S(1)} %collective-permute-done.15.rest_2_), channel_id=1, source_target_pairs={{0,1},{1,0},{2,3},{3,2},{4,5},{5,4},{6,7},{7,6},{8,9},{9,8},{10,11... | collective-permute-start | bytes 294920 | tf_op jit(solution)/shard_map/ppermute | solution.py:405
  54.9 2.2 %collective-permute-start.18 = (f32[4,48,128]{2,1,0:T(8,128)S(1)}, f32[4,48,128]{2,1,0:T(8,128)S(1)}, u32[]{:S(2)}, u32[]{:S(2)}) collective-permute-start(f32[4,48,128]{2,1,0:T(8,128)S(1)} %collective-permute-done.14.rest_1_), channel_id=1, source_target_pairs={{0,1},{1,0},{2,3},{3,2},{4,5},{5,4},{6,7},{7,6},{8,9},{9,8},{10,11... | collective-permute-start | bytes 294920 | tf_op jit(solution)/shard_map/ppermute | solution.py:405
  56.1 2.1 %collective-permute-start.24 = (f32[4,48,128]{2,1,0:T(8,128)S(1)}, f32[4,48,128]{2,1,0:T(8,128)S(1)}, u32[]{:S(2)}, u32[]{:S(2)}) collective-permute-start(f32[4,48,128]{2,1,0:T(8,128)S(1)} %pad_maximum_fusion.1.rest_0_), channel_id=1, source_target_pairs={{0,1},{1,0},{2,3},{3,2},{4,5},{5,4},{6,7},{7,6},{8,9},{9,8},{10,11... | collective-permute-start | bytes 294920 | tf_op jit(solution)/shard_map/ppermute | solution.py:405
  56.2 2.0 %collective-permute-start.27 = (f32[4,48,128]{2,1,0:T(8,128)S(1)}, f32[4,48,128]{2,1,0:T(8,128)S(1)}, u32[]{:S(2)}, u32[]{:S(2)}) collective-permute-start(f32[4,48,128]{2,1,0:T(8,128)S(1)} %collective-permute-done.23.rest_3_), channel_id=1, source_target_pairs={{0,1},{1,0},{2,3},{3,2},{4,5},{5,4},{6,7},{7,6},{8,9},{9,8},{10,11... | collective-permute-start | bytes 294920 | tf_op jit(solution)/shard_map/ppermute | solution.py:405
  56.6 1.6 %collective-permute-start.26 = (f32[4,48,128]{2,1,0:T(8,128)S(1)}, f32[4,48,128]{2,1,0:T(8,128)S(1)}, u32[]{:S(2)}, u32[]{:S(2)}) collective-permute-start(f32[4,48,128]{2,1,0:T(8,128)S(1)} %collective-permute-done.22.rest_2_), channel_id=1, source_target_pairs={{0,1},{1,0},{2,3},{3,2},{4,5},{5,4},{6,7},{7,6},{8,9},{9,8},{10,11... | collective-permute-start | bytes 294920 | tf_op jit(solution)/shard_map/ppermute | solution.py:405
  56.7 1.5 %collective-permute-start.25 = (f32[4,48,128]{2,1,0:T(8,128)S(1)}, f32[4,48,128]{2,1,0:T(8,128)S(1)}, u32[]{:S(2)}, u32[]{:S(2)}) collective-permute-start(f32[4,48,128]{2,1,0:T(8,128)S(1)} %collective-permute-done.21.rest_1_), channel_id=1, source_target_pairs={{0,1},{1,0},{2,3},{3,2},{4,5},{5,4},{6,7},{7,6},{8,9},{9,8},{10,11... | collective-permute-start | bytes 294920 | tf_op jit(solution)/shard_map/ppermute | solution.py:405
  60.5 3.8 %collective-permute-start.28 = (f32[48,96]{1,0:T(8,128)S(1)}, f32[48,96]{1,0:T(8,128)S(1)}, u32[]{:S(2)}, u32[]{:S(2)}) collective-permute-start(f32[48,96]{1,0:T(8,128)S(1)} %get-tuple-element.22), channel_id=1, source_target_pairs={{0,4},{1,5},{2,6},{3,7},{4,0},{5,1},{6,2},{7,3},{8,12},{9,13},{10,... | collective-permute-start | bytes 55304 | tf_op jit(solution)/shard_map/ppermute | solution.py:405
  64.3 6.2 %collective-permute-start.31 = (f32[2,48,96]{2,1,0:T(8,128)S(1)}, f32[2,48,96]{2,1,0:T(8,128)S(1)}, u32[]{:S(2)}, u32[]{:S(2)}) collective-permute-start(f32[2,48,96]{2,1,0:T(8,128)S(1)} %pad_maximum_fusion.5.refs_0_), channel_id=1, source_target_pairs={{0,24},{1,25},{2,26},{3,27},{4,28},{5,29},{6,30},{7,31},{8,16},{9,... | collective-permute-start | bytes 110600 | tf_op jit(solution)/shard_map/ppermute | solution.py:405
  66.5 5.4 %collective-permute-start.30 = (f32[2,48,96]{2,1,0:T(8,128)S(1)}, f32[2,48,96]{2,1,0:T(8,128)S(1)}, u32[]{:S(2)}, u32[]{:S(2)}) collective-permute-start(f32[2,48,96]{2,1,0:T(8,128)S(1)} %pad_maximum_fusion.5.refs_0_), channel_id=1, source_target_pairs={{0,16},{1,17},{2,18},{3,19},{4,20},{5,21},{6,22},{7,23},{8,24},{9,... | collective-permute-start | bytes 110600 | tf_op jit(solution)/shard_map/ppermute | solution.py:405
  67.6 4.6 %collective-permute-start.29 = (f32[2,48,96]{2,1,0:T(8,128)S(1)}, f32[2,48,96]{2,1,0:T(8,128)S(1)}, u32[]{:S(2)}, u32[]{:S(2)}) collective-permute-start(f32[2,48,96]{2,1,0:T(8,128)S(1)} %pad_maximum_fusion.5.refs_0_), channel_id=1, source_target_pairs={{0,8},{1,9},{2,10},{3,11},{4,12},{5,13},{6,14},{7,15},{8,0},{9,1},... | collective-permute-start | bytes 110600 | tf_op jit(solution)/shard_map/ppermute | solution.py:405

commit v9 on v8

--- a/solution.py
+++ b/solution.py
@@ -137,6 +137,10 @@
 
 def in_vmem(count):
     return [pl.BlockSpec(memory_space=pltpu.VMEM)] * count
+
+
+def stage_bits(row, column, swapped):
+    return row + swapped * (column - row), column + swapped * (row - column)
 
 
 def band_gram(w_rows):
@@ -209,8 +213,10 @@
 
     lax.fori_loop(0, groups, body, 0)
     gram = fold(band_gram(w_ref[...])[:, :rank])
-    keep_0[PIECES * rank:] = gram
-    give_0[PIECES * rank:] = gram
+    span = PIECES // 2 * rank
+    for ref in (keep_0, give_0):
+        ref[span:span + FOLDED] = gram
+        ref[2 * span + FOLDED:] = gram
     planes = xh_ref.shape[1]
     band = w_ref.shape[1]
     me_sp = lax.axis_index("sp")
@@ -239,15 +245,16 @@
                     [value[:, column * LANES:(column + 1) * LANES] for value in sums], wide)
                 for k in range(4):
                     rel_sp = lax.bitwise_xor(me_sp, column * 4 + k)
-                    side = 3 - rel_sp % 2 if rel_bd // 2 else rel_sp % 2
-                    first = pl.multiple_of((side * 4 + rel_sp // 2) * rank, 8)
-                    refs[rel_bd % 2][pl.ds(first, rank)] = pieces[k]
+                    outer, inner = stage_bits(rel_bd // 2, rel_sp % 2, (me_bd + rel_bd + chain) % 2)
+                    first = ((outer * 2 + inner) * 4 + rel_sp // 2) * rank
+                    first = first + outer * FOLDED if chain == 0 else first
+                    refs[rel_bd % 2][pl.ds(pl.multiple_of(first, 8), rank)] = pieces[k]
 
 
 def blur_call(cube, taps_x, taps_y, w_rows):
     planes, height, length = cube.shape
     rank = w_rows.shape[0]
-    first = jax.ShapeDtypeStruct((PIECES * rank + FOLDED, LANES), F32)
+    first = jax.ShapeDtypeStruct((PIECES * rank + 2 * FOLDED, LANES), F32)
     second = jax.ShapeDtypeStruct((PIECES * rank, LANES), F32)
     image = (height, planes, length)
     mine = jax.ShapeDtypeStruct((rank, planes), F32)
@@ -270,7 +277,7 @@
     here = h_ref[pl.ds(first, tall)]
     here = jnp.transpose(here.reshape(-1, here.shape[2]))
     rows = mine_ref.shape[0]
-    gram = unfold(mine_ref[rows - FOLDED:rows] + other_ref[rows - FOLDED:rows], here.shape[0])
+    gram = 0.5 * unfold(mine_ref[rows - FOLDED:rows] + other_ref[rows - FOLDED:rows], here.shape[0])
     out_ref[...] = here / dot_exact(gram, here)
 
 
@@ -284,9 +291,8 @@
     )(mine, other, h_columns)
 
 
-def accumulate(xh_ref, xl_ref, part_refs, all_ref, h_out, chain, total):
+def accumulate(xh_ref, xl_ref, part_refs, all_ref, chain, total):
     height, planes, _ = xh_ref.shape
-    rank = all_ref.shape[1]
     me_sp = lax.axis_index("sp")
     me_bd = lax.axis_index("bd")
     bands = lax.axis_size("bd")
@@ -294,11 +300,13 @@
     tall = height // bands
     wide = 2 * LANES // pieces
     for slot, part_ref in enumerate(part_refs):
-        rel_bd = slot // 4 + 2 * ((slot // 2) % 2)
-        for inner in range(4):
-            rel_sp = slot % 2 + 2 * inner
-            owner = lax.bitwise_xor(me_bd, rel_bd) * pieces + lax.bitwise_xor(me_sp, rel_sp)
-            all_ref[owner] = part_ref[inner]
+        core, outer = slot // 2, slot % 2
+        for inner in range(2):
+            row, column = stage_bits(outer, inner, (me_bd + core + chain) % 2)
+            for step in range(4):
+                owner_bd = lax.bitwise_xor(me_bd, core + 2 * row)
+                owner_sp = lax.bitwise_xor(me_sp, column + 2 * step)
+                all_ref[owner_bd * pieces + owner_sp] = part_ref[inner, step]
     for part in range(bands):
         first_row = part * tall + 4 * chain
         halves = [
@@ -310,43 +318,33 @@
         image = [
             jnp.concatenate([ref[first_row + row] for row in range(4)], axis=1) for ref in (xh_ref, xl_ref)]
         total = total + dot_nt(jnp.concatenate(image + [here], axis=0), here)
-        mine = jnp.transpose(all_ref[part * pieces + me_sp])
-        h_out[first_row:first_row + 4] = mine.reshape(4, wide, rank)
     return total
 
 
 def first_kernel(xh_ref, xl_ref, *rest):
-    part_refs = rest[:8]
-    total_out, h_out, all_ref = rest[8:]
-    total_out[...] = accumulate(
-        xh_ref, xl_ref, part_refs, all_ref, h_out, 0, jnp.zeros(total_out.shape, F32))
-    tall = xh_ref.shape[0] // lax.axis_size("bd")
-    for part in range(lax.axis_size("bd")):
-        h_out[part * tall + 4:(part + 1) * tall] = jnp.zeros((tall - 4,) + h_out.shape[1:], F32)
+    part_refs = rest[:4]
+    total_out, all_ref = rest[4:]
+    total_out[...] = accumulate(xh_ref, xl_ref, part_refs, all_ref, 0, jnp.zeros(total_out.shape, F32))
 
 
 def first_call(x_high, x_low, parts):
-    height, planes, length = x_high.shape
-    rank = parts[0].shape[1]
+    _, planes, _ = x_high.shape
+    rank = parts[0].shape[2]
     return pl.pallas_call(
         first_kernel,
-        out_shape=[
-            jax.ShapeDtypeStruct((2 * (planes + rank), 2 * rank), F32),
-            jax.ShapeDtypeStruct((height, length // lax.axis_size("sp"), rank), F32),
-        ],
+        out_shape=jax.ShapeDtypeStruct((2 * (planes + rank), 2 * rank), F32),
         in_specs=in_vmem(2 + len(parts)),
-        scratch_shapes=[pltpu.VMEM((32,) + parts[0].shape[1:], F32)],
+        scratch_shapes=[pltpu.VMEM((32, rank, LANES), F32)],
         compiler_params=pltpu.CompilerParams(vmem_limit_bytes=VMEM_LIMIT),
     )(x_high, x_low, *parts)
 
 
-def second_kernel(xh_ref, xl_ref, w_ref, total_ref, h_ref, *rest):
-    part_refs = rest[:8]
-    w_out, h_out, all_ref = rest[8:]
+def second_kernel(xh_ref, xl_ref, w_ref, total_ref, *rest):
+    part_refs = rest[:4]
+    w_out, all_ref = rest[4:]
     planes = xh_ref.shape[1]
     rank = w_ref.shape[0]
-    h_out[...] = h_ref[...]
-    total = accumulate(xh_ref, xl_ref, part_refs, all_ref, h_out, 1, total_ref[...])
+    total = accumulate(xh_ref, xl_ref, part_refs, all_ref, 1, total_ref[...])
     numer = total[:planes, :rank] + (total[:planes, rank:] + total[planes:2 * planes, :rank])
     gram = total[2 * planes:]
     gram = gram[:rank, :rank] + (gram[:rank, rank:] + gram[rank:, :rank])
@@ -354,17 +352,38 @@
     w_out[...] = w_here * jnp.transpose(numer) / dot_exact(gram, w_here)
 
 
-def second_call(x_high, x_low, w_here, total, h_half, parts):
+def second_call(x_high, x_low, w_here, total, parts):
+    rank = w_here.shape[0]
     return pl.pallas_call(
         second_kernel,
-        out_shape=[
-            jax.ShapeDtypeStruct(w_here.shape, F32),
-            jax.ShapeDtypeStruct(h_half.shape, F32),
-        ],
-        in_specs=in_vmem(5 + len(parts)),
-        scratch_shapes=[pltpu.VMEM((32,) + parts[0].shape[1:], F32)],
+        out_shape=jax.ShapeDtypeStruct(w_here.shape, F32),
+        in_specs=in_vmem(4 + len(parts)),
+        scratch_shapes=[pltpu.VMEM((32, rank, LANES), F32)],
         compiler_params=pltpu.CompilerParams(vmem_limit_bytes=VMEM_LIMIT),
-    )(x_high, x_low, w_here, total, h_half, *parts)
+    )(x_high, x_low, w_here, total, *parts)
+
+
+def place_h_kernel(*refs):
+    h_out = refs[-1]
+    me_bd = lax.axis_index("bd")
+    tall = h_out.shape[0] // lax.axis_size("bd")
+    for chain in range(2):
+        for core in range(2):
+            near_ref, far_ref = refs[4 * chain + 2 * core:4 * chain + 2 * core + 2]
+            swapped = (me_bd + core + chain) % 2
+            across = jnp.where(swapped == 0, far_ref[0, 0], near_ref[1, 0])
+            for row, piece in ((0, near_ref[0, 0]), (1, across)):
+                first = lax.bitwise_xor(me_bd, core + 2 * row) * tall + 4 * chain
+                h_out[pl.ds(first, 4)] = jnp.transpose(piece).reshape((4,) + h_out.shape[1:])
+
+
+def place_h_call(parts, shape):
+    return pl.pallas_call(
+        place_h_kernel,
+        out_shape=jax.ShapeDtypeStruct(shape, F32),
+        in_specs=in_vmem(len(parts)),
+        compiler_params=pltpu.CompilerParams(vmem_limit_bytes=VMEM_LIMIT),
+    )(*parts)
 
 
 def gather_w_kernel(*refs):
@@ -381,6 +400,7 @@
         out_ref[:, owner * planes:(owner + 1) * planes] = all_ref[owner][:, :planes]
 
 
+ORDER = (3, 2, 1)
 RING = (0, 1, 2, 3, 4, 5, 6, 7)
 
 
@@ -405,8 +425,18 @@
     return lax.ppermute(value, ("sp", "bd"), pairs)
 
 
-def around(values):
-    return [send(values[k], k % 2, 2 * (k // 2)) for k in range(1, 4)]
+def send_across(value, chain, outer):
+    bands = lax.axis_size("bd")
+    pieces = lax.axis_size("sp")
+    pairs = []
+    for s in range(pieces):
+        for b in range(bands):
+            if (b + chain + outer) % 2:
+                target = s * bands + (b ^ 2)
+            else:
+                target = (s ^ 1) * bands + b
+            pairs.append((s * bands + b, target))
+    return lax.ppermute(value, ("sp", "bd"), pairs)
 
 
 def local(cube, taps_x, taps_y, factor_w, factor_h):
@@ -416,32 +446,34 @@
     h_columns = jnp.transpose(factor_h, (1, 2, 0))
     rank = w_rows.shape[0]
     x_high, x_low, w_here, keep_0, give_0, keep_1, give_1 = blur_call(cube[0], taps_x, taps_y, w_rows)
-    chains = []
-    for keep, give in ((keep_0, give_0), (keep_1, give_1)):
+    sums = []
+    for chain, (keep, give) in enumerate(((keep_0, give_0), (keep_1, give_1))):
         taken = send(give, 0, 1)
-        bounds = [place * 4 * rank for place in (0, 1, 3, 2)]
-        sides = []
-        for first in bounds:
-            last = keep.shape[0] if first == max(bounds) else first + 4 * rank
-            sides.append(keep[first:last] + taken[first:last])
-        chains.append((sides, around(sides)))
-    ratio = ratio_call(chains[0][0][2], chains[0][1][1], h_columns)
-    line = []
-    for k in range(4):
-        part = slice(k * rank, (k + 1) * rank)
-        line.append(jnp.concatenate(
-            [(sides[0][part] + others[0][part]) + (others[1][part] + others[2][part]) for sides, others in chains],
-            axis=1))
-    line = [line[0]] + [send(line[k], 2 * k, 0) for k in range(1, 4)]
+        half = keep.shape[0] // 2
+        outer = send_across(keep[half:] + taken[half:], chain, 1)
+        near = keep[:half] + taken[:half] + outer
+        quarter = 4 * rank
+        across = near[quarter:]
+        inner = send_across(across, chain, 0)
+        if chain == 0:
+            ratio = ratio_call(across, inner, h_columns)
+        sums.append(near[:quarter] + inner[:quarter])
+    line = [jnp.concatenate([value[k * rank:(k + 1) * rank] for value in sums], axis=1) for k in range(4)]
+    line = [line[0]] + [send(line[k], 2 * k, 0) for k in ORDER]
     h_piece = ratio * ((line[0] + line[1]) + (line[2] + line[3]))
     h_line = [h_piece] + [send(h_piece, 2 * k, 0) for k in range(1, 4)]
-    rounds = []
-    for first in (0, LANES):
+    chains = []
+    for chain, first in enumerate((0, LANES)):
         mine = jnp.stack([value[:, first:first + LANES] for value in h_line])
-        parts = [mine] + around([mine] * 4)
-        rounds.append(parts + [send(value, 0, 1) for value in parts])
-    total, h_half = first_call(x_high, x_low, rounds[0])
-    w_piece, h_next = second_call(x_high, x_low, w_here, total, h_half, rounds[1])
+        near = jnp.stack([mine, send_across(mine, chain, 0)])
+        chains.append([near, send_across(near, chain, 1)])
+    first_parts = chains[0] + [send(value, 0, 1) for value in chains[0]]
+    total = first_call(x_high, x_low, first_parts)
+    total, far = lax.optimization_barrier((total, chains[1][1]))
+    second_parts = [chains[1][0], far]
+    second_parts = second_parts + [send(value, 0, 1) for value in second_parts]
+    w_piece = second_call(x_high, x_low, w_here, total, second_parts)
+    h_next = place_h_call(first_parts + second_parts, h_columns.shape)
     w_pair = jnp.stack([w_piece, send(w_piece, 1, 0)])
     w_next = gather_w_call([w_pair] + [send(w_pair, 2 * k, 0) for k in range(1, 4)])
     return jnp.transpose(w_next)[None], jnp.transpose(h_next, (2, 0, 1))

time: 73.1 us -> 78.4 us (1.073)
  waiting for transfers between devices: 23 us -> 32.4 us
  starting transfers between devices: 34.4 us -> 29.8 us
    ppermute x32 -> x16, starting transfers between devices: 34.4 us -> 15.5 us  [send(): return lax.ppermute(value, ('sp', 'bd'), pairs)]
    ppermute x0 -> x8, waiting for transfers between devices: none -> 18.3 us  [send_across(): return lax.ppermute(value, ('sp', 'bd'), pairs)]
    ppermute x0 -> x8, starting transfers between devices: none -> 14.3 us  [send_across(): return lax.ppermute(value, ('sp', 'bd'), pairs)]
    ppermute x32 -> x16, waiting for transfers between devices: 23 us -> 14.1 us  [send(): return lax.ppermute(value, ('sp', 'bd'), pairs)]
    pallas_call x2 -> x3, Pallas kernels: 3.29 us -> 3.5 us  [the longest x1 1.41 us: second_call(): pl.pallas_call(second_kernel, out_shape=jax.ShapeDtypeStruct(w_here.shape...]
  transfers between devices with their start and end apart: 32 -> 24, of which waited for: 17 -> 16; matrix products, arithmetic and copies ran while one was open for 0% -> 0% of each run, Pallas kernels for 2% -> 3%
where the time goes in v9:
time: 78.4 us; the launch traced here: 78.3 us
  waiting for transfers between devices  32.4 us (41%)
  starting transfers between devices  29.8 us (38%)
  Pallas kernels  14.9 us (19%)
  between operations  0.8 us (1%)
    ppermute x8, waiting for transfers between devices, send_across(): return lax.ppermute(value, ('sp', 'bd'), pairs)  18.3 us
    ppermute x16, starting transfers between devices, send(): return lax.ppermute(value, ('sp', 'bd'), pairs)  15.5 us
    ppermute x8, starting transfers between devices, send_across(): return lax.ppermute(value, ('sp', 'bd'), pairs)  14.3 us
    ppermute x16, waiting for transfers between devices, send(): return lax.ppermute(value, ('sp', 'bd'), pairs)  14.1 us
    pallas_call x1, Pallas kernels, blur_call(): pl.pallas_call(blur_kernel, out_shape=[jax.ShapeDtypeStruct(image, BF16)]...  10.3 us
  transfers between devices with their start and end apart: 24, of which 16 were waited for; matrix products, arithmetic and copies ran while one was open for 0% of the time, Pallas kernels for 3%

profile of v9, /device:TPU:0, one launch (start us, length us, event | category | flops | bytes accessed | tf_op | source)
XLA Modules:
  0.0 78.3 jit_solution(18025416487744609906)
XLA Ops:
  0.6 10.3 %shard_map.68 = (bf16[32,96,256]{2,1,0:T(8,128)(2,1)S(1)}, bf16[32,96,256]{2,1,0:T(8,128)(2,1)S(1)}, f32[48,96]{1,0:T(8,128)S(1)}, f32[816,128]{1,0:T(8,128)S(1)...) custom-call(f32[96,32,256]{2,1,0:T(8,128)} %bitcast.37, f32[25,1,96]{2,1,0:T(1,128)} %bitcast.44, ...), custom_call_target="tpu_custom_call" | custom-call | tf_op jit(solution)/shard_map/pallas_call | solution.py:262
  11.0 0.5 collective-permute-start.3
  11.5 0.1 collective-permute-start
  11.6 1.3 %collective-permute-done.3 = f32[768,128]{1,0:T(8,128)S(1)} collective-permute-done((f32[768,128]{1,0:T(8,128)S(1)}, f32[768,128]{1,0:T(8,128)S(1)}, u32[]{:S(2)}, u32[]{:S(2)}) %collective-permute-start.3) | collective-permute-done | bytes 393248 | tf_op jit(solution)/shard_map/ppermute | solution.py:425
  12.9 2.9 %collective-permute-start.4 = (f32[384,128]{1,0:T(8,128)S(1)}, f32[384,128]{1,0:T(8,128)S(1)}, u32[]{:S(2)}, u32[]{:S(2)}) collective-permute-start(f32[384,128]{1,0:T(8,128)S(1)} %slice_add_fusion.2), channel_id=1, source_target_pairs={{0,4},{1,3},{2,6},{3,1},{4,0},{5,7},{6,2},{7,5},{8,12},{9,11},{10,... | collective-permute-start | bytes 589832 | tf_op jit(solution)/shard_map/ppermute | solution.py:439
  15.8 0.0 collective-permute-done
  15.8 0.0 copy-start
  15.8 1.6 %collective-permute-start.1 = (f32[408,128]{1,0:T(8,128)S(1)}, f32[408,128]{1,0:T(8,128)S(1)}, u32[]{:S(2)}, u32[]{:S(2)}) collective-permute-start(f32[408,128]{1,0:T(8,128)S(1)} %slice_add_fusion), channel_id=1, source_target_pairs={{0,2},{1,5},{2,0},{3,7},{4,6},{5,1},{6,4},{7,3},{8,10},{9,13},{10,... | collective-permute-start | bytes 626696 | tf_op jit(solution)/shard_map/ppermute | solution.py:439
  17.4 3.2 %collective-permute-done.4 = f32[384,128]{1,0:T(8,128)S(1)} collective-permute-done((f32[384,128]{1,0:T(8,128)S(1)}, f32[384,128]{1,0:T(8,128)S(1)}, u32[]{:S(2)}, u32[]{:S(2)}) %collective-permute-start.4) | collective-permute-done | bytes 196640 | tf_op jit(solution)/shard_map/ppermute | solution.py:439
  20.7 2.9 %collective-permute-start.5 = (f32[192,128]{1,0:T(8,128)S(1)}, f32[192,128]{1,0:T(8,128)S(1)}, u32[]{:S(2)}, u32[]{:S(2)}) collective-permute-start(f32[192,128]{1,0:T(8,128)S(1)} %slice.125), channel_id=1, source_target_pairs={{0,2},{1,5},{2,0},{3,7},{4,6},{5,1},{6,4},{7,3},{8,10},{9,13},{10,... | collective-permute-start | bytes 294920 | tf_op jit(solution)/shard_map/ppermute | solution.py:439
  23.6 0.0 collective-permute-done.1
  23.7 1.6 %collective-permute-start.2 = (f32[216,128]{1,0:T(8,128)S(1)}, f32[216,128]{1,0:T(8,128)S(1)}, u32[]{:S(2)}, u32[]{:S(2)}) collective-permute-start(f32[216,128]{1,0:T(8,128)S(1)} %slice.118.mine_ref), channel_id=1, source_target_pairs={{0,4},{1,3},{2,6},{3,1},{4,0},{5,7},{6,2},{7,5},{8,12},{9,11},{10,... | collective-permute-start | bytes 331784 | tf_op jit(solution)/shard_map/ppermute | solution.py:439
  25.2 1.5 %collective-permute-done.5 = f32[192,128]{1,0:T(8,128)S(1)} collective-permute-done((f32[192,128]{1,0:T(8,128)S(1)}, f32[192,128]{1,0:T(8,128)S(1)}, u32[]{:S(2)}, u32[]{:S(2)}) %collective-permute-start.5) | collective-permute-done | bytes 98336 | tf_op jit(solution)/shard_map/ppermute | solution.py:439
  26.8 1.7 %collective-permute-done.2.other_ref = f32[216,128]{1,0:T(8,128)S(1)} collective-permute-done((f32[216,128]{1,0:T(8,128)S(1)}, f32[216,128]{1,0:T(8,128)S(1)}, u32[]{:S(2)}, u32[]{:S(2)}) %collective-permute-start.2) | collective-permute-done | bytes 110624 | tf_op jit(solution)/shard_map/ppermute | solution.py:439
  28.5 3.7 %collective-permute-start.6 = (f32[48,256]{1,0:T(8,128)S(1)}, f32[48,256]{1,0:T(8,128)S(1)}, u32[]{:S(2)}, u32[]{:S(2)}) collective-permute-start(f32[48,256]{1,0:T(8,128)S(1)} %pad_maximum_fusion.4), channel_id=1, source_target_pairs={{0,24},{1,25},{2,26},{3,27},{4,28},{5,29},{6,30},{7,31},{8,16},{9,... | collective-permute-start | bytes 147464 | tf_op jit(solution)/shard_map/ppermute | solution.py:425
  32.2 0.0 collective-permute-start.7
  32.2 0.8 %collective-permute-start.8 = (f32[48,256]{1,0:T(8,128)S(1)}, f32[48,256]{1,0:T(8,128)S(1)}, u32[]{:S(2)}, u32[]{:S(2)}) collective-permute-start(f32[48,256]{1,0:T(8,128)S(1)} %pad_maximum_fusion.6), channel_id=1, source_target_pairs={{0,8},{1,9},{2,10},{3,11},{4,12},{5,13},{6,14},{7,15},{8,0},{9,1},... | collective-permute-start | bytes 147464 | tf_op jit(solution)/shard_map/ppermute | solution.py:425
  33.0 0.0 copy-done
  33.0 0.3 shard_map.69
  33.3 1.3 %collective-permute-done.6 = f32[48,256]{1,0:T(8,128)S(1)} collective-permute-done((f32[48,256]{1,0:T(8,128)S(1)}, f32[48,256]{1,0:T(8,128)S(1)}, u32[]{:S(2)}, u32[]{:S(2)}) %collective-permute-start.6) | collective-permute-done | bytes 49184 | tf_op jit(solution)/shard_map/ppermute | solution.py:425
  34.6 3.0 %collective-permute-done.7 = f32[48,256]{1,0:T(8,128)S(1)} collective-permute-done((f32[48,256]{1,0:T(8,128)S(1)}, f32[48,256]{1,0:T(8,128)S(1)}, u32[]{:S(2)}, u32[]{:S(2)}) %collective-permute-start.7) | collective-permute-done | bytes 49184 | tf_op jit(solution)/shard_map/ppermute | solution.py:425
  37.6 0.0 collective-permute-done.8
  37.7 1.1 %collective-permute-start.11 = (f32[48,256]{1,0:T(8,128)S(1)}, f32[48,256]{1,0:T(8,128)S(1)}, u32[]{:S(2)}, u32[]{:S(2)}) collective-permute-start(f32[48,256]{1,0:T(8,128)S(1)} %fusion.3), channel_id=1, source_target_pairs={{0,24},{1,25},{2,26},{3,27},{4,28},{5,29},{6,30},{7,31},{8,16},{9,... | collective-permute-start | bytes 147464 | tf_op jit(solution)/shard_map/ppermute | solution.py:425
  38.8 0.6 collective-permute-start.10
  39.4 2.7 %collective-permute-start.9 = (f32[48,256]{1,0:T(8,128)S(1)}, f32[48,256]{1,0:T(8,128)S(1)}, u32[]{:S(2)}, u32[]{:S(2)}) collective-permute-start(f32[48,256]{1,0:T(8,128)S(1)} %fusion.3), channel_id=1, source_target_pairs={{0,8},{1,9},{2,10},{3,11},{4,12},{5,13},{6,14},{7,15},{8,0},{9,1},... | collective-permute-start | bytes 147464 | tf_op jit(solution)/shard_map/ppermute | solution.py:425
  42.1 1.5 %collective-permute-done.11 = f32[48,256]{1,0:T(8,128)S(1)} collective-permute-done((f32[48,256]{1,0:T(8,128)S(1)}, f32[48,256]{1,0:T(8,128)S(1)}, u32[]{:S(2)}, u32[]{:S(2)}) %collective-permute-start.11) | collective-permute-done | bytes 49184 | tf_op jit(solution)/shard_map/ppermute | solution.py:425
  43.7 1.0 %collective-permute-done.10 = f32[48,256]{1,0:T(8,128)S(1)} collective-permute-done((f32[48,256]{1,0:T(8,128)S(1)}, f32[48,256]{1,0:T(8,128)S(1)}, u32[]{:S(2)}, u32[]{:S(2)}) %collective-permute-start.10) | collective-permute-done | bytes 49184 | tf_op jit(solution)/shard_map/ppermute | solution.py:425
  44.7 0.0 collective-permute-done.9
  44.7 1.6 %collective-permute-start.12 = (f32[4,48,128]{2,1,0:T(8,128)S(1)}, f32[4,48,128]{2,1,0:T(8,128)S(1)}, u32[]{:S(2)}, u32[]{:S(2)}) collective-permute-start(f32[4,48,128]{2,1,0:T(8,128)S(1)} %get-tuple-element.23), channel_id=1, source_target_pairs={{0,4},{1,3},{2,6},{3,1},{4,0},{5,7},{6,2},{7,5},{8,12},{9,11},{10,... | collective-permute-start | bytes 294920 | tf_op jit(solution)/shard_map/ppermute | solution.py:439
  46.3 4.2 %collective-permute-done.12 = f32[4,48,128]{2,1,0:T(8,128)S(1)} collective-permute-done((f32[4,48,128]{2,1,0:T(8,128)S(1)}, f32[4,48,128]{2,1,0:T(8,128)S(1)}, u32[]{:S(2)}, u32[]{:S(2)}) %collective-permute-start.12) | collective-permute-done | bytes 98336 | tf_op jit(solution)/shard_map/ppermute | solution.py:439
  50.5 0.1 collective-permute-start.13
  50.6 2.1 %collective-permute-start.16 = (f32[4,48,128]{2,1,0:T(8,128)S(1)}, f32[4,48,128]{2,1,0:T(8,128)S(1)}, u32[]{:S(2)}, u32[]{:S(2)}) collective-permute-start(f32[4,48,128]{2,1,0:T(8,128)S(1)} %get-tuple-element.21), channel_id=1, source_target_pairs={{0,2},{1,5},{2,0},{3,7},{4,6},{5,1},{6,4},{7,3},{8,10},{9,13},{10,... | collective-permute-start | bytes 294920 | tf_op jit(solution)/shard_map/ppermute | solution.py:439
  52.7 0.0 collective-permute-start.14
  52.7 3.6 %collective-permute-done.13.rest_1_.refs_1_ = f32[2,4,48,128]{3,2,1,0:T(8,128)S(1)} collective-permute-done((f32[2,4,48,128]{3,2,1,0:T(8,128)S(1)}, f32[2,4,48,128]{3,2,1,0:T(8,128)S(1)}, u32[]{:S(2)}, u32[]{:S(2)}) %collective-permute-start.13) | collective-permute-done | bytes 196640 | tf_op jit(solution)/shard_map/ppermute | solution.py:439
  56.3 0.0 collective-permute-start.15
  56.3 1.0 %collective-permute-done.16 = f32[4,48,128]{2,1,0:T(8,128)S(1)} collective-permute-done((f32[4,48,128]{2,1,0:T(8,128)S(1)}, f32[4,48,128]{2,1,0:T(8,128)S(1)}, u32[]{:S(2)}, u32[]{:S(2)}) %collective-permute-start.16) | collective-permute-done | bytes 98336 | tf_op jit(solution)/shard_map/ppermute | solution.py:439
  57.3 1.6 %collective-permute-start.17 = (f32[2,4,48,128]{3,2,1,0:T(8,128)S(1)}, f32[2,4,48,128]{3,2,1,0:T(8,128)S(1)}, u32[]{:S(2)}, u32[]{:S(2)}) collective-permute-start(f32[2,4,48,128]{3,2,1,0:T(8,128)S(1)} %pad_maximum_fusion.1.rest_0_.refs_4_), channel_id=1, source_target_pairs={{0,4},{1,3},{2,6},{3,1},{4,0},{5,7},{6,2},{7,5},{8,12},{9,11},{10,... | collective-permute-start | bytes 589832 | tf_op jit(solution)/shard_map/ppermute | solution.py:439
  58.9 0.0 collective-permute-start.18
  58.9 0.0 collective-permute-done.14.rest_2_.refs_2_
  58.9 0.0 collective-permute-done.15.rest_3_.refs_3_
  58.9 1.1 %shard_map.70.total_ref = f32[288,96]{1,0:T(8,128)S(1)} custom-call(bf16[32,96,256]{2,1,0:T(8,128)(2,1)S(1)} %get-tuple-element.11.xh_ref, bf16[32,96,256]{2,1,0:T(8,128)(2,1)S(1)} %get-tuple-element.12.xl_ref, f32[2,4,48,128]{3,2,1,0:T(8,128)S(1)} %pad_maximum_fusion.rest_0_.refs_0_, f32[2,4,48,128]{3,2,1,0:T(8,128)S(1)} %collective-permute-done.13.rest_1_.refs_1_, ...), custom_call_target="tpu_custom_call" | custom-call | tf_op jit(solution)/shard_map/pallas_call | solution.py:333
  60.0 3.1 %collective-permute-done.17.rest_1_.refs_5_ = f32[2,4,48,128]{3,2,1,0:T(8,128)S(1)} collective-permute-done((f32[2,4,48,128]{3,2,1,0:T(8,128)S(1)}, f32[2,4,48,128]{3,2,1,0:T(8,128)S(1)}, u32[]{:S(2)}, u32[]{:S(2)}) %collective-permute-start.17) | collective-permute-done | bytes 196640 | tf_op jit(solution)/shard_map/ppermute | solution.py:439
  63.1 0.0 collective-permute-start.19
  63.1 0.0 collective-permute-done.18.rest_2_.refs_6_
  63.1 1.4 %collective-permute-done.19.rest_3_.refs_7_ = f32[2,4,48,128]{3,2,1,0:T(8,128)S(1)} collective-permute-done((f32[2,4,48,128]{3,2,1,0:T(8,128)S(1)}, f32[2,4,48,128]{3,2,1,0:T(8,128)S(1)}, u32[]{:S(2)}, u32[]{:S(2)}) %collective-permute-start.19) | collective-permute-done | bytes 196640 | tf_op jit(solution)/shard_map/ppermute | solution.py:425
  64.5 1.4 %shard_map.71 = f32[48,96]{1,0:T(8,128)S(1)} custom-call(bf16[32,96,256]{2,1,0:T(8,128)(2,1)S(1)} %get-tuple-element.11.xh_ref, bf16[32,96,256]{2,1,0:T(8,128)(2,1)S(1)} %get-tuple-element.12.xl_ref, f32[48,96]{1,0:T(8,128)S(1)} %get-tuple-element.13.w_ref, f32[288,96]{1,0:T(8,128)S(1)} %shard_map.70.total_ref, ...), custom_call_target="tpu_custom_call" | custom-call | tf_op jit(solution)/shard_map/pallas_call | solution.py:357
  65.9 1.6 %collective-permute-start.20 = (f32[48,96]{1,0:T(8,128)S(1)}, f32[48,96]{1,0:T(8,128)S(1)}, u32[]{:S(2)}, u32[]{:S(2)}) collective-permute-start(f32[48,96]{1,0:T(8,128)S(1)} %shard_map.71), channel_id=1, source_target_pairs={{0,4},{1,5},{2,6},{3,7},{4,0},{5,1},{6,2},{7,3},{8,12},{9,13},{10,... | collective-permute-start | bytes 55304 | tf_op jit(solution)/shard_map/ppermute | solution.py:425
  67.5 2.3 %collective-permute-done.20 = f32[48,96]{1,0:T(8,128)S(1)} collective-permute-done((f32[48,96]{1,0:T(8,128)S(1)}, f32[48,96]{1,0:T(8,128)S(1)}, u32[]{:S(2)}, u32[]{:S(2)}) %collective-permute-start.20) | collective-permute-done | bytes 18464 | tf_op jit(solution)/shard_map/ppermute | solution.py:425
  69.8 2.3 %collective-permute-start.23 = (f32[2,48,96]{2,1,0:T(8,128)S(1)}, f32[2,48,96]{2,1,0:T(8,128)S(1)}, u32[]{:S(2)}, u32[]{:S(2)}) collective-permute-start(f32[2,48,96]{2,1,0:T(8,128)S(1)} %pad_maximum_fusion.7.refs_0_), channel_id=1, source_target_pairs={{0,24},{1,25},{2,26},{3,27},{4,28},{5,29},{6,30},{7,31},{8,16},{9,... | collective-permute-start | bytes 110600 | tf_op jit(solution)/shard_map/ppermute | solution.py:425
  72.1 0.8 %collective-permute-start.22 = (f32[2,48,96]{2,1,0:T(8,128)S(1)}, f32[2,48,96]{2,1,0:T(8,128)S(1)}, u32[]{:S(2)}, u32[]{:S(2)}) collective-permute-start(f32[2,48,96]{2,1,0:T(8,128)S(1)} %pad_maximum_fusion.7.refs_0_), channel_id=1, source_target_pairs={{0,16},{1,17},{2,18},{3,19},{4,20},{5,21},{6,22},{7,23},{8,24},{9,... | collective-permute-start | bytes 110600 | tf_op jit(solution)/shard_map/ppermute | solution.py:425
  72.9 1.4 %collective-permute-start.21 = (f32[2,48,96]{2,1,0:T(8,128)S(1)}, f32[2,48,96]{2,1,0:T(8,128)S(1)}, u32[]{:S(2)}, u32[]{:S(2)}) collective-permute-start(f32[2,48,96]{2,1,0:T(8,128)S(1)} %pad_maximum_fusion.7.refs_0_), channel_id=1, source_target_pairs={{0,8},{1,9},{2,10},{3,11},{4,12},{5,13},{6,14},{7,15},{8,0},{9,1},... | collective-permute-start | bytes 110600 | tf_op jit(solution)/shard_map/ppermute | solution.py:425
  74.3 1.0 %shard_map.73 = f32[32,32,48]{2,1,0:T(8,128)} custom-call(f32[2,4,48,128]{3,2,1,0:T(8,128)S(1)} %pad_maximum_fusion.rest_0_.refs_0_, f32[2,4,48,128]{3,2,1,0:T(8,128)S(1)} %collective-permute-done.13.rest_1_.refs_1_, f32[2,4,48,128]{3,2,1,0:T(8,128)S(1)} %collective-permute-done.14.rest_2_.refs_2_, ...), custom_call_target="tpu_custom_call" | custom-call | tf_op jit(solution)/shard_map/pallas_call | solution.py:381
  75.3 0.8 %collective-permute-done.23.refs_3_ = f32[2,48,96]{2,1,0:T(8,128)S(1)} collective-permute-done((f32[2,48,96]{2,1,0:T(8,128)S(1)}, f32[2,48,96]{2,1,0:T(8,128)S(1)}, u32[]{:S(2)}, u32[]{:S(2)}) %collective-permute-start.23) | collective-permute-done | bytes 36896 | tf_op jit(solution)/shard_map/ppermute | solution.py:425
  76.1 1.4 %collective-permute-done.22.refs_2_ = f32[2,48,96]{2,1,0:T(8,128)S(1)} collective-permute-done((f32[2,48,96]{2,1,0:T(8,128)S(1)}, f32[2,48,96]{2,1,0:T(8,128)S(1)}, u32[]{:S(2)}, u32[]{:S(2)}) %collective-permute-start.22) | collective-permute-done | bytes 36896 | tf_op jit(solution)/shard_map/ppermute | solution.py:425
  77.5 0.0 collective-permute-done.21.refs_1_
  77.5 0.8 shard_map.72
  (23 shorter events, 0.3 us)
Async XLA Ops:
  11.0 1.9 %collective-permute-start.3 = (f32[768,128]{1,0:T(8,128)S(1)}, f32[768,128]{1,0:T(8,128)S(1)}, u32[]{:S(2)}, u32[]{:S(2)}) collective-permute-start(f32[768,128]{1,0:T(8,128)S(1)} %get-tuple-element.17), channel_id=1, source_target_pairs={{0,1},{1,0},{2,3},{3,2},{4,5},{5,4},{6,7},{7,6},{8,9},{9,8},{10,11... | collective-permute-start | bytes 1179656 | tf_op jit(solution)/shard_map/ppermute | solution.py:425
  11.5 4.3 %collective-permute-start = (f32[816,128]{1,0:T(8,128)S(1)}, f32[816,128]{1,0:T(8,128)S(1)}, u32[]{:S(2)}, u32[]{:S(2)}) collective-permute-start(f32[816,128]{1,0:T(8,128)S(1)} %get-tuple-element.15), channel_id=1, source_target_pairs={{0,1},{1,0},{2,3},{3,2},{4,5},{5,4},{6,7},{7,6},{8,9},{9,8},{10,11... | collective-permute-start | bytes 1253384 | tf_op jit(solution)/shard_map/ppermute | solution.py:425
  12.9 7.8 %collective-permute-start.4 = (f32[384,128]{1,0:T(8,128)S(1)}, f32[384,128]{1,0:T(8,128)S(1)}, u32[]{:S(2)}, u32[]{:S(2)}) collective-permute-start(f32[384,128]{1,0:T(8,128)S(1)} %slice_add_fusion.2), channel_id=1, source_target_pairs={{0,4},{1,3},{2,6},{3,1},{4,0},{5,7},{6,2},{7,5},{8,12},{9,11},{10,... | collective-permute-start | bytes 589832 | tf_op jit(solution)/shard_map/ppermute | solution.py:439
  15.8 17.2 %copy-start = (f32[48,32,32]{0,2,1:T(8,128)S(1)}, f32[48,32,32]{0,2,1:T(8,128)}, u32[]{:S(2)}) copy-start(f32[48,32,32]{0,2,1:T(8,128)} %param.9) | copy-start | bytes 589828
  15.8 7.8 %collective-permute-start.1 = (f32[408,128]{1,0:T(8,128)S(1)}, f32[408,128]{1,0:T(8,128)S(1)}, u32[]{:S(2)}, u32[]{:S(2)}) collective-permute-start(f32[408,128]{1,0:T(8,128)S(1)} %slice_add_fusion), channel_id=1, source_target_pairs={{0,2},{1,5},{2,0},{3,7},{4,6},{5,1},{6,4},{7,3},{8,10},{9,13},{10,... | collective-permute-start | bytes 626696 | tf_op jit(solution)/shard_map/ppermute | solution.py:439
  20.7 6.1 %collective-permute-start.5 = (f32[192,128]{1,0:T(8,128)S(1)}, f32[192,128]{1,0:T(8,128)S(1)}, u32[]{:S(2)}, u32[]{:S(2)}) collective-permute-start(f32[192,128]{1,0:T(8,128)S(1)} %slice.125), channel_id=1, source_target_pairs={{0,2},{1,5},{2,0},{3,7},{4,6},{5,1},{6,4},{7,3},{8,10},{9,13},{10,... | collective-permute-start | bytes 294920 | tf_op jit(solution)/shard_map/ppermute | solution.py:439
  23.7 4.8 %collective-permute-start.2 = (f32[216,128]{1,0:T(8,128)S(1)}, f32[216,128]{1,0:T(8,128)S(1)}, u32[]{:S(2)}, u32[]{:S(2)}) collective-permute-start(f32[216,128]{1,0:T(8,128)S(1)} %slice.118.mine_ref), channel_id=1, source_target_pairs={{0,4},{1,3},{2,6},{3,1},{4,0},{5,7},{6,2},{7,5},{8,12},{9,11},{10,... | collective-permute-start | bytes 331784 | tf_op jit(solution)/shard_map/ppermute | solution.py:439
  28.5 6.1 %collective-permute-start.6 = (f32[48,256]{1,0:T(8,128)S(1)}, f32[48,256]{1,0:T(8,128)S(1)}, u32[]{:S(2)}, u32[]{:S(2)}) collective-permute-start(f32[48,256]{1,0:T(8,128)S(1)} %pad_maximum_fusion.4), channel_id=1, source_target_pairs={{0,24},{1,25},{2,26},{3,27},{4,28},{5,29},{6,30},{7,31},{8,16},{9,... | collective-permute-start | bytes 147464 | tf_op jit(solution)/shard_map/ppermute | solution.py:425
  32.2 5.4 %collective-permute-start.7 = (f32[48,256]{1,0:T(8,128)S(1)}, f32[48,256]{1,0:T(8,128)S(1)}, u32[]{:S(2)}, u32[]{:S(2)}) collective-permute-start(f32[48,256]{1,0:T(8,128)S(1)} %pad_maximum_fusion.5), channel_id=1, source_target_pairs={{0,16},{1,17},{2,18},{3,19},{4,20},{5,21},{6,22},{7,23},{8,24},{9,... | collective-permute-start | bytes 147464 | tf_op jit(solution)/shard_map/ppermute | solution.py:425
  32.2 5.4 %collective-permute-start.8 = (f32[48,256]{1,0:T(8,128)S(1)}, f32[48,256]{1,0:T(8,128)S(1)}, u32[]{:S(2)}, u32[]{:S(2)}) collective-permute-start(f32[48,256]{1,0:T(8,128)S(1)} %pad_maximum_fusion.6), channel_id=1, source_target_pairs={{0,8},{1,9},{2,10},{3,11},{4,12},{5,13},{6,14},{7,15},{8,0},{9,1},... | collective-permute-start | bytes 147464 | tf_op jit(solution)/shard_map/ppermute | solution.py:425
  37.7 6.0 %collective-permute-start.11 = (f32[48,256]{1,0:T(8,128)S(1)}, f32[48,256]{1,0:T(8,128)S(1)}, u32[]{:S(2)}, u32[]{:S(2)}) collective-permute-start(f32[48,256]{1,0:T(8,128)S(1)} %fusion.3), channel_id=1, source_target_pairs={{0,24},{1,25},{2,26},{3,27},{4,28},{5,29},{6,30},{7,31},{8,16},{9,... | collective-permute-start | bytes 147464 | tf_op jit(solution)/shard_map/ppermute | solution.py:425
  38.8 5.9 %collective-permute-start.10 = (f32[48,256]{1,0:T(8,128)S(1)}, f32[48,256]{1,0:T(8,128)S(1)}, u32[]{:S(2)}, u32[]{:S(2)}) collective-permute-start(f32[48,256]{1,0:T(8,128)S(1)} %fusion.3), channel_id=1, source_target_pairs={{0,16},{1,17},{2,18},{3,19},{4,20},{5,21},{6,22},{7,23},{8,24},{9,... | collective-permute-start | bytes 147464 | tf_op jit(solution)/shard_map/ppermute | solution.py:425
  39.4 5.3 %collective-permute-start.9 = (f32[48,256]{1,0:T(8,128)S(1)}, f32[48,256]{1,0:T(8,128)S(1)}, u32[]{:S(2)}, u32[]{:S(2)}) collective-permute-start(f32[48,256]{1,0:T(8,128)S(1)} %fusion.3), channel_id=1, source_target_pairs={{0,8},{1,9},{2,10},{3,11},{4,12},{5,13},{6,14},{7,15},{8,0},{9,1},... | collective-permute-start | bytes 147464 | tf_op jit(solution)/shard_map/ppermute | solution.py:425
  44.7 5.8 %collective-permute-start.12 = (f32[4,48,128]{2,1,0:T(8,128)S(1)}, f32[4,48,128]{2,1,0:T(8,128)S(1)}, u32[]{:S(2)}, u32[]{:S(2)}) collective-permute-start(f32[4,48,128]{2,1,0:T(8,128)S(1)} %get-tuple-element.23), channel_id=1, source_target_pairs={{0,4},{1,3},{2,6},{3,1},{4,0},{5,7},{6,2},{7,5},{8,12},{9,11},{10,... | collective-permute-start | bytes 294920 | tf_op jit(solution)/shard_map/ppermute | solution.py:439
  50.5 5.7 %collective-permute-start.13 = (f32[2,4,48,128]{3,2,1,0:T(8,128)S(1)}, f32[2,4,48,128]{3,2,1,0:T(8,128)S(1)}, u32[]{:S(2)}, u32[]{:S(2)}) collective-permute-start(f32[2,4,48,128]{3,2,1,0:T(8,128)S(1)} %pad_maximum_fusion.rest_0_.refs_0_), channel_id=1, source_target_pairs={{0,2},{1,5},{2,0},{3,7},{4,6},{5,1},{6,4},{7,3},{8,10},{9,13},{10,... | collective-permute-start | bytes 589832 | tf_op jit(solution)/shard_map/ppermute | solution.py:439
  50.6 6.7 %collective-permute-start.16 = (f32[4,48,128]{2,1,0:T(8,128)S(1)}, f32[4,48,128]{2,1,0:T(8,128)S(1)}, u32[]{:S(2)}, u32[]{:S(2)}) collective-permute-start(f32[4,48,128]{2,1,0:T(8,128)S(1)} %get-tuple-element.21), channel_id=1, source_target_pairs={{0,2},{1,5},{2,0},{3,7},{4,6},{5,1},{6,4},{7,3},{8,10},{9,13},{10,... | collective-permute-start | bytes 294920 | tf_op jit(solution)/shard_map/ppermute | solution.py:439
  52.7 6.2 %collective-permute-start.14 = (f32[2,4,48,128]{3,2,1,0:T(8,128)S(1)}, f32[2,4,48,128]{3,2,1,0:T(8,128)S(1)}, u32[]{:S(2)}, u32[]{:S(2)}) collective-permute-start(f32[2,4,48,128]{3,2,1,0:T(8,128)S(1)} %pad_maximum_fusion.rest_0_.refs_0_), channel_id=1, source_target_pairs={{0,1},{1,0},{2,3},{3,2},{4,5},{5,4},{6,7},{7,6},{8,9},{9,8},{10,11... | collective-permute-start | bytes 589832 | tf_op jit(solution)/shard_map/ppermute | solution.py:425
  56.3 2.7 %collective-permute-start.15 = (f32[2,4,48,128]{3,2,1,0:T(8,128)S(1)}, f32[2,4,48,128]{3,2,1,0:T(8,128)S(1)}, u32[]{:S(2)}, u32[]{:S(2)}) collective-permute-start(f32[2,4,48,128]{3,2,1,0:T(8,128)S(1)} %collective-permute-done.13.rest_1_.refs_1_), channel_id=1, source_target_pairs={{0,1},{1,0},{2,3},{3,2},{4,5},{5,4},{6,7},{7,6},{8,9},{9,8},{10,11... | collective-permute-start | bytes 589832 | tf_op jit(solution)/shard_map/ppermute | solution.py:425
  57.3 5.7 %collective-permute-start.17 = (f32[2,4,48,128]{3,2,1,0:T(8,128)S(1)}, f32[2,4,48,128]{3,2,1,0:T(8,128)S(1)}, u32[]{:S(2)}, u32[]{:S(2)}) collective-permute-start(f32[2,4,48,128]{3,2,1,0:T(8,128)S(1)} %pad_maximum_fusion.1.rest_0_.refs_4_), channel_id=1, source_target_pairs={{0,4},{1,3},{2,6},{3,1},{4,0},{5,7},{6,2},{7,5},{8,12},{9,11},{10,... | collective-permute-start | bytes 589832 | tf_op jit(solution)/shard_map/ppermute | solution.py:439
  58.9 4.2 %collective-permute-start.18 = (f32[2,4,48,128]{3,2,1,0:T(8,128)S(1)}, f32[2,4,48,128]{3,2,1,0:T(8,128)S(1)}, u32[]{:S(2)}, u32[]{:S(2)}) collective-permute-start(f32[2,4,48,128]{3,2,1,0:T(8,128)S(1)} %pad_maximum_fusion.1.rest_0_.refs_4_), channel_id=1, source_target_pairs={{0,1},{1,0},{2,3},{3,2},{4,5},{5,4},{6,7},{7,6},{8,9},{9,8},{10,11... | collective-permute-start | bytes 589832 | tf_op jit(solution)/shard_map/ppermute | solution.py:425
  63.1 1.4 %collective-permute-start.19 = (f32[2,4,48,128]{3,2,1,0:T(8,128)S(1)}, f32[2,4,48,128]{3,2,1,0:T(8,128)S(1)}, u32[]{:S(2)}, u32[]{:S(2)}) collective-permute-start(f32[2,4,48,128]{3,2,1,0:T(8,128)S(1)} %collective-permute-done.17.rest_1_.refs_5_), channel_id=1, source_target_pairs={{0,1},{1,0},{2,3},{3,2},{4,5},{5,4},{6,7},{7,6},{8,9},{9,8},{10,11... | collective-permute-start | bytes 589832 | tf_op jit(solution)/shard_map/ppermute | solution.py:425
  65.9 3.9 %collective-permute-start.20 = (f32[48,96]{1,0:T(8,128)S(1)}, f32[48,96]{1,0:T(8,128)S(1)}, u32[]{:S(2)}, u32[]{:S(2)}) collective-permute-start(f32[48,96]{1,0:T(8,128)S(1)} %shard_map.71), channel_id=1, source_target_pairs={{0,4},{1,5},{2,6},{3,7},{4,0},{5,1},{6,2},{7,3},{8,12},{9,13},{10,... | collective-permute-start | bytes 55304 | tf_op jit(solution)/shard_map/ppermute | solution.py:425
  69.8 6.3 %collective-permute-start.23 = (f32[2,48,96]{2,1,0:T(8,128)S(1)}, f32[2,48,96]{2,1,0:T(8,128)S(1)}, u32[]{:S(2)}, u32[]{:S(2)}) collective-permute-start(f32[2,48,96]{2,1,0:T(8,128)S(1)} %pad_maximum_fusion.7.refs_0_), channel_id=1, source_target_pairs={{0,24},{1,25},{2,26},{3,27},{4,28},{5,29},{6,30},{7,31},{8,16},{9,... | collective-permute-start | bytes 110600 | tf_op jit(solution)/shard_map/ppermute | solution.py:425
  72.1 5.4 %collective-permute-start.22 = (f32[2,48,96]{2,1,0:T(8,128)S(1)}, f32[2,48,96]{2,1,0:T(8,128)S(1)}, u32[]{:S(2)}, u32[]{:S(2)}) collective-permute-start(f32[2,48,96]{2,1,0:T(8,128)S(1)} %pad_maximum_fusion.7.refs_0_), channel_id=1, source_target_pairs={{0,16},{1,17},{2,18},{3,19},{4,20},{5,21},{6,22},{7,23},{8,24},{9,... | collective-permute-start | bytes 110600 | tf_op jit(solution)/shard_map/ppermute | solution.py:425
  72.9 4.6 %collective-permute-start.21 = (f32[2,48,96]{2,1,0:T(8,128)S(1)}, f32[2,48,96]{2,1,0:T(8,128)S(1)}, u32[]{:S(2)}, u32[]{:S(2)}) collective-permute-start(f32[2,48,96]{2,1,0:T(8,128)S(1)} %pad_maximum_fusion.7.refs_0_), channel_id=1, source_target_pairs={{0,8},{1,9},{2,10},{3,11},{4,12},{5,13},{6,14},{7,15},{8,0},{9,1},... | collective-permute-start | bytes 110600 | tf_op jit(solution)/shard_map/ppermute | solution.py:425

commit v10 on v8

--- a/solution.py
+++ b/solution.py
@@ -284,9 +284,8 @@
     )(mine, other, h_columns)
 
 
-def accumulate(xh_ref, xl_ref, part_refs, all_ref, h_out, chain, total):
+def accumulate(xh_ref, xl_ref, part_refs, all_ref, chain, total):
     height, planes, _ = xh_ref.shape
-    rank = all_ref.shape[1]
     me_sp = lax.axis_index("sp")
     me_bd = lax.axis_index("bd")
     bands = lax.axis_size("bd")
@@ -310,43 +309,33 @@
         image = [
             jnp.concatenate([ref[first_row + row] for row in range(4)], axis=1) for ref in (xh_ref, xl_ref)]
         total = total + dot_nt(jnp.concatenate(image + [here], axis=0), here)
-        mine = jnp.transpose(all_ref[part * pieces + me_sp])
-        h_out[first_row:first_row + 4] = mine.reshape(4, wide, rank)
     return total
 
 
 def first_kernel(xh_ref, xl_ref, *rest):
     part_refs = rest[:8]
-    total_out, h_out, all_ref = rest[8:]
-    total_out[...] = accumulate(
-        xh_ref, xl_ref, part_refs, all_ref, h_out, 0, jnp.zeros(total_out.shape, F32))
-    tall = xh_ref.shape[0] // lax.axis_size("bd")
-    for part in range(lax.axis_size("bd")):
-        h_out[part * tall + 4:(part + 1) * tall] = jnp.zeros((tall - 4,) + h_out.shape[1:], F32)
+    total_out, all_ref = rest[8:]
+    total_out[...] = accumulate(xh_ref, xl_ref, part_refs, all_ref, 0, jnp.zeros(total_out.shape, F32))
 
 
 def first_call(x_high, x_low, parts):
-    height, planes, length = x_high.shape
+    _, planes, _ = x_high.shape
     rank = parts[0].shape[1]
     return pl.pallas_call(
         first_kernel,
-        out_shape=[
-            jax.ShapeDtypeStruct((2 * (planes + rank), 2 * rank), F32),
-            jax.ShapeDtypeStruct((height, length // lax.axis_size("sp"), rank), F32),
-        ],
+        out_shape=jax.ShapeDtypeStruct((2 * (planes + rank), 2 * rank), F32),
         in_specs=in_vmem(2 + len(parts)),
-        scratch_shapes=[pltpu.VMEM((32,) + parts[0].shape[1:], F32)],
+        scratch_shapes=[pltpu.VMEM((32, rank, LANES), F32)],
         compiler_params=pltpu.CompilerParams(vmem_limit_bytes=VMEM_LIMIT),
     )(x_high, x_low, *parts)
 
 
-def second_kernel(xh_ref, xl_ref, w_ref, total_ref, h_ref, *rest):
+def second_kernel(xh_ref, xl_ref, w_ref, total_ref, *rest):
     part_refs = rest[:8]
-    w_out, h_out, all_ref = rest[8:]
+    w_out, all_ref = rest[8:]
     planes = xh_ref.shape[1]
     rank = w_ref.shape[0]
-    h_out[...] = h_ref[...]
-    total = accumulate(xh_ref, xl_ref, part_refs, all_ref, h_out, 1, total_ref[...])
+    total = accumulate(xh_ref, xl_ref, part_refs, all_ref, 1, total_ref[...])
     numer = total[:planes, :rank] + (total[:planes, rank:] + total[planes:2 * planes, :rank])
     gram = total[2 * planes:]
     gram = gram[:rank, :rank] + (gram[:rank, rank:] + gram[rank:, :rank])
@@ -354,17 +343,35 @@
     w_out[...] = w_here * jnp.transpose(numer) / dot_exact(gram, w_here)
 
 
-def second_call(x_high, x_low, w_here, total, h_half, parts):
+def second_call(x_high, x_low, w_here, total, parts):
+    rank = w_here.shape[0]
     return pl.pallas_call(
         second_kernel,
-        out_shape=[
-            jax.ShapeDtypeStruct(w_here.shape, F32),
-            jax.ShapeDtypeStruct(h_half.shape, F32),
-        ],
-        in_specs=in_vmem(5 + len(parts)),
-        scratch_shapes=[pltpu.VMEM((32,) + parts[0].shape[1:], F32)],
+        out_shape=jax.ShapeDtypeStruct(w_here.shape, F32),
+        in_specs=in_vmem(4 + len(parts)),
+        scratch_shapes=[pltpu.VMEM((32, rank, LANES), F32)],
         compiler_params=pltpu.CompilerParams(vmem_limit_bytes=VMEM_LIMIT),
-    )(x_high, x_low, w_here, total, h_half, *parts)
+    )(x_high, x_low, w_here, total, *parts)
+
+
+def place_h_kernel(*refs):
+    h_out = refs[-1]
+    me_bd = lax.axis_index("bd")
+    tall = h_out.shape[0] // lax.axis_size("bd")
+    for chain in range(2):
+        for rel_bd in range(4):
+            piece = refs[4 * chain + rel_bd][0]
+            first = lax.bitwise_xor(me_bd, rel_bd) * tall + 4 * chain
+            h_out[pl.ds(first, 4)] = jnp.transpose(piece).reshape((4,) + h_out.shape[1:])
+
+
+def place_h_call(parts, shape):
+    return pl.pallas_call(
+        place_h_kernel,
+        out_shape=jax.ShapeDtypeStruct(shape, F32),
+        in_specs=in_vmem(len(parts)),
+        compiler_params=pltpu.CompilerParams(vmem_limit_bytes=VMEM_LIMIT),
+    )(*parts)
 
 
 def gather_w_kernel(*refs):
@@ -432,16 +439,19 @@
         line.append(jnp.concatenate(
             [(sides[0][part] + others[0][part]) + (others[1][part] + others[2][part]) for sides, others in chains],
             axis=1))
-    line = [line[0]] + [send(line[k], 2 * k, 0) for k in range(1, 4)]
+    line = [line[0]] + [send(line[k], 2 * k, 0) for k in (3, 2, 1)]
     h_piece = ratio * ((line[0] + line[1]) + (line[2] + line[3]))
     h_line = [h_piece] + [send(h_piece, 2 * k, 0) for k in range(1, 4)]
-    rounds = []
+    chains = []
     for first in (0, LANES):
         mine = jnp.stack([value[:, first:first + LANES] for value in h_line])
-        parts = [mine] + around([mine] * 4)
-        rounds.append(parts + [send(value, 0, 1) for value in parts])
-    total, h_half = first_call(x_high, x_low, rounds[0])
-    w_piece, h_next = second_call(x_high, x_low, w_here, total, h_half, rounds[1])
+        chains.append([mine] + around([mine] * 4))
+    first_parts = chains[0] + [send(value, 0, 1) for value in chains[0]]
+    total = first_call(x_high, x_low, first_parts)
+    second_parts = chains[1] + [send(value, 0, 1) for value in chains[1]]
+    w_piece = second_call(x_high, x_low, w_here, total, second_parts)
+    own = [parts[k] for parts in (first_parts, second_parts) for k in (0, 4, 2, 6)]
+    h_next = place_h_call(own, h_columns.shape)
     w_pair = jnp.stack([w_piece, send(w_piece, 1, 0)])
     w_next = gather_w_call([w_pair] + [send(w_pair, 2 * k, 0) for k in range(1, 4)])
     return jnp.transpose(w_next)[None], jnp.transpose(h_next, (2, 0, 1))

time: 73.1 us -> 71.1 us (0.973)
  waiting for transfers between devices: 23 us -> 20.9 us
    ppermute x32, waiting for transfers between devices: 23 us -> 20.9 us  [send(): return lax.ppermute(value, ('sp', 'bd'), pairs)]
    pallas_call x2 -> x3, Pallas kernels: 3.29 us -> 3.45 us  [the longest x1 1.41 us: second_call(): pl.pallas_call(second_kernel, out_shape=jax.ShapeDtypeStruct(w_here.shape...]
  transfers between devices with their start and end apart: 32 -> 32, of which waited for: 17 -> 17; matrix products, arithmetic and copies ran while one was open for 0% -> 0% of each run, Pallas kernels for 2% -> 3%
where the time goes in v10:
time: 71.1 us; the launch traced here: 71 us
  starting transfers between devices  34.2 us (48%)
  waiting for transfers between devices  20.9 us (29%)
  Pallas kernels  14.8 us (21%)
  between operations  0.77 us (1%)
    ppermute x32, starting transfers between devices, send(): return lax.ppermute(value, ('sp', 'bd'), pairs)  34.2 us
    ppermute x32, waiting for transfers between devices, send(): return lax.ppermute(value, ('sp', 'bd'), pairs)  20.9 us
    pallas_call x1, Pallas kernels, blur_call(): pl.pallas_call(blur_kernel, out_shape=[jax.ShapeDtypeStruct(image, BF16)]...  10.3 us
  transfers between devices with their start and end apart: 32, of which 17 were waited for; matrix products, arithmetic and copies ran while one was open for 0% of the time, Pallas kernels for 3%

profile of v10, /device:TPU:0, one launch (start us, length us, event | category | flops | bytes accessed | tf_op | source)
XLA Modules:
  0.0 71.0 jit_solution(13449218022809508952)
XLA Ops:
  0.6 10.3 %shard_map.68 = (bf16[32,96,256]{2,1,0:T(8,128)(2,1)S(1)}, bf16[32,96,256]{2,1,0:T(8,128)(2,1)S(1)}, f32[48,96]{1,0:T(8,128)S(1)}, f32[792,128]{1,0:T(8,128)S(1)...) custom-call(f32[96,32,256]{2,1,0:T(8,128)} %bitcast.31, f32[25,1,96]{2,1,0:T(1,128)} %bitcast.36, ...), custom_call_target="tpu_custom_call" | custom-call | tf_op jit(solution)/shard_map/pallas_call | solution.py:255
  10.9 0.5 collective-permute-start.4
  11.5 0.1 collective-permute-start
  11.6 1.3 %collective-permute-done.4 = f32[768,128]{1,0:T(8,128)S(1)} collective-permute-done((f32[768,128]{1,0:T(8,128)S(1)}, f32[768,128]{1,0:T(8,128)S(1)}, u32[]{:S(2)}, u32[]{:S(2)}) %collective-permute-start.4) | collective-permute-done | bytes 393248 | tf_op jit(solution)/shard_map/ppermute | solution.py:412
  12.8 0.1 slice_add_fusion.4
  12.9 3.9 %collective-permute-start.7 = (f32[192,128]{1,0:T(8,128)S(1)}, f32[192,128]{1,0:T(8,128)S(1)}, u32[]{:S(2)}, u32[]{:S(2)}) collective-permute-start(f32[192,128]{1,0:T(8,128)S(1)} %get-tuple-element.20), channel_id=1, source_target_pairs={{0,6},{1,7},{2,4},{3,5},{4,2},{5,3},{6,0},{7,1},{8,14},{9,15},{10,... | collective-permute-start | bytes 294920 | tf_op jit(solution)/shard_map/ppermute | solution.py:412
  16.8 0.5 collective-permute-start.6
  17.3 0.1 collective-permute-start.5
  17.4 0.0 collective-permute-done
  17.4 2.9 %collective-permute-start.3 = (f32[192,128]{1,0:T(8,128)S(1)}, f32[192,128]{1,0:T(8,128)S(1)}, u32[]{:S(2)}, u32[]{:S(2)}) collective-permute-start(f32[192,128]{1,0:T(8,128)S(1)} %get-tuple-element.17), channel_id=1, source_target_pairs={{0,6},{1,7},{2,4},{3,5},{4,2},{5,3},{6,0},{7,1},{8,14},{9,15},{10,... | collective-permute-start | bytes 294920 | tf_op jit(solution)/shard_map/ppermute | solution.py:412
  20.4 0.5 collective-permute-start.2
  20.9 1.4 %collective-permute-start.1 = (f32[216,128]{1,0:T(8,128)S(1)}, f32[216,128]{1,0:T(8,128)S(1)}, u32[]{:S(2)}, u32[]{:S(2)}) collective-permute-start(f32[216,128]{1,0:T(8,128)S(1)} %slice_add_fusion.mine_ref), channel_id=1, source_target_pairs={{0,2},{1,3},{2,0},{3,1},{4,6},{5,7},{6,4},{7,5},{8,10},{9,11},{10,... | collective-permute-start | bytes 331784 | tf_op jit(solution)/shard_map/ppermute | solution.py:412
  22.3 1.0 %collective-permute-done.6 = f32[192,128]{1,0:T(8,128)S(1)} collective-permute-done((f32[192,128]{1,0:T(8,128)S(1)}, f32[192,128]{1,0:T(8,128)S(1)}, u32[]{:S(2)}, u32[]{:S(2)}) %collective-permute-start.6) | collective-permute-done | bytes 98336 | tf_op jit(solution)/shard_map/ppermute | solution.py:412
  23.3 2.5 %collective-permute-done.3 = f32[192,128]{1,0:T(8,128)S(1)} collective-permute-done((f32[192,128]{1,0:T(8,128)S(1)}, f32[192,128]{1,0:T(8,128)S(1)}, u32[]{:S(2)}, u32[]{:S(2)}) %collective-permute-start.3) | collective-permute-done | bytes 98336 | tf_op jit(solution)/shard_map/ppermute | solution.py:412
  25.8 0.7 collective-permute-done.2
  26.4 0.1 collective-permute-done.1.other_ref
  26.5 3.8 %collective-permute-start.8 = (f32[48,256]{1,0:T(8,128)S(1)}, f32[48,256]{1,0:T(8,128)S(1)}, u32[]{:S(2)}, u32[]{:S(2)}) collective-permute-start(f32[48,256]{1,0:T(8,128)S(1)} %pad_maximum_fusion.2), channel_id=1, source_target_pairs={{0,24},{1,25},{2,26},{3,27},{4,28},{5,29},{6,30},{7,31},{8,16},{9,... | collective-permute-start | bytes 147464 | tf_op jit(solution)/shard_map/ppermute | solution.py:412
  30.3 0.0 collective-permute-start.9
  30.4 0.6 collective-permute-start.10
  31.0 0.3 shard_map.69
  31.3 1.7 %collective-permute-done.8 = f32[48,256]{1,0:T(8,128)S(1)} collective-permute-done((f32[48,256]{1,0:T(8,128)S(1)}, f32[48,256]{1,0:T(8,128)S(1)}, u32[]{:S(2)}, u32[]{:S(2)}) %collective-permute-start.8) | collective-permute-done | bytes 49184 | tf_op jit(solution)/shard_map/ppermute | solution.py:412
  33.0 2.4 %collective-permute-done.9 = f32[48,256]{1,0:T(8,128)S(1)} collective-permute-done((f32[48,256]{1,0:T(8,128)S(1)}, f32[48,256]{1,0:T(8,128)S(1)}, u32[]{:S(2)}, u32[]{:S(2)}) %collective-permute-start.9) | collective-permute-done | bytes 49184 | tf_op jit(solution)/shard_map/ppermute | solution.py:412
  35.3 0.0 collective-permute-done.10
  35.4 1.7 %collective-permute-start.13 = (f32[48,256]{1,0:T(8,128)S(1)}, f32[48,256]{1,0:T(8,128)S(1)}, u32[]{:S(2)}, u32[]{:S(2)}) collective-permute-start(f32[48,256]{1,0:T(8,128)S(1)} %fusion.1), channel_id=1, source_target_pairs={{0,24},{1,25},{2,26},{3,27},{4,28},{5,29},{6,30},{7,31},{8,16},{9,... | collective-permute-start | bytes 147464 | tf_op jit(solution)/shard_map/ppermute | solution.py:412
  37.1 0.5 collective-permute-start.12
  37.5 2.3 %collective-permute-start.11 = (f32[48,256]{1,0:T(8,128)S(1)}, f32[48,256]{1,0:T(8,128)S(1)}, u32[]{:S(2)}, u32[]{:S(2)}) collective-permute-start(f32[48,256]{1,0:T(8,128)S(1)} %fusion.1), channel_id=1, source_target_pairs={{0,8},{1,9},{2,10},{3,11},{4,12},{5,13},{6,14},{7,15},{8,0},{9,1},... | collective-permute-start | bytes 147464 | tf_op jit(solution)/shard_map/ppermute | solution.py:412
  39.8 1.5 %collective-permute-done.13 = f32[48,256]{1,0:T(8,128)S(1)} collective-permute-done((f32[48,256]{1,0:T(8,128)S(1)}, f32[48,256]{1,0:T(8,128)S(1)}, u32[]{:S(2)}, u32[]{:S(2)}) %collective-permute-start.13) | collective-permute-done | bytes 49184 | tf_op jit(solution)/shard_map/ppermute | solution.py:412
  41.3 1.3 %collective-permute-done.12 = f32[48,256]{1,0:T(8,128)S(1)} collective-permute-done((f32[48,256]{1,0:T(8,128)S(1)}, f32[48,256]{1,0:T(8,128)S(1)}, u32[]{:S(2)}, u32[]{:S(2)}) %collective-permute-start.12) | collective-permute-done | bytes 49184 | tf_op jit(solution)/shard_map/ppermute | solution.py:412
  42.6 0.0 collective-permute-done.11
  42.6 0.1 collective-permute-start.17
  42.7 2.0 %collective-permute-start.16 = (f32[4,48,128]{2,1,0:T(8,128)S(1)}, f32[4,48,128]{2,1,0:T(8,128)S(1)}, u32[]{:S(2)}, u32[]{:S(2)}) collective-permute-start(f32[4,48,128]{2,1,0:T(8,128)S(1)} %pad_maximum_fusion.rest_0_.refs_0_), channel_id=1, source_target_pairs={{0,6},{1,7},{2,4},{3,5},{4,2},{5,3},{6,0},{7,1},{8,14},{9,15},{10,... | collective-permute-start | bytes 294920 | tf_op jit(solution)/shard_map/ppermute | solution.py:412
  44.7 1.1 %collective-permute-start.15 = (f32[4,48,128]{2,1,0:T(8,128)S(1)}, f32[4,48,128]{2,1,0:T(8,128)S(1)}, u32[]{:S(2)}, u32[]{:S(2)}) collective-permute-start(f32[4,48,128]{2,1,0:T(8,128)S(1)} %pad_maximum_fusion.rest_0_.refs_0_), channel_id=1, source_target_pairs={{0,2},{1,3},{2,0},{3,1},{4,6},{5,7},{6,4},{7,5},{8,10},{9,11},{10,... | collective-permute-start | bytes 294920 | tf_op jit(solution)/shard_map/ppermute | solution.py:412
  45.8 0.4 collective-permute-start.14
  46.3 2.0 %collective-permute-start.23 = (f32[4,48,128]{2,1,0:T(8,128)S(1)}, f32[4,48,128]{2,1,0:T(8,128)S(1)}, u32[]{:S(2)}, u32[]{:S(2)}) collective-permute-start(f32[4,48,128]{2,1,0:T(8,128)S(1)} %pad_maximum_fusion.1.rest_0_.refs_4_), channel_id=1, source_target_pairs={{0,6},{1,7},{2,4},{3,5},{4,2},{5,3},{6,0},{7,1},{8,14},{9,15},{10,... | collective-permute-start | bytes 294920 | tf_op jit(solution)/shard_map/ppermute | solution.py:412
  48.3 1.1 %collective-permute-start.22 = (f32[4,48,128]{2,1,0:T(8,128)S(1)}, f32[4,48,128]{2,1,0:T(8,128)S(1)}, u32[]{:S(2)}, u32[]{:S(2)}) collective-permute-start(f32[4,48,128]{2,1,0:T(8,128)S(1)} %pad_maximum_fusion.1.rest_0_.refs_4_), channel_id=1, source_target_pairs={{0,2},{1,3},{2,0},{3,1},{4,6},{5,7},{6,4},{7,5},{8,10},{9,11},{10,... | collective-permute-start | bytes 294920 | tf_op jit(solution)/shard_map/ppermute | solution.py:412
  49.4 0.0 collective-permute-done.16.rest_3_
  49.4 1.4 %collective-permute-start.21 = (f32[4,48,128]{2,1,0:T(8,128)S(1)}, f32[4,48,128]{2,1,0:T(8,128)S(1)}, u32[]{:S(2)}, u32[]{:S(2)}) collective-permute-start(f32[4,48,128]{2,1,0:T(8,128)S(1)} %pad_maximum_fusion.1.rest_0_.refs_4_), channel_id=1, source_target_pairs={{0,4},{1,5},{2,6},{3,7},{4,0},{5,1},{6,2},{7,3},{8,12},{9,13},{10,... | collective-permute-start | bytes 294920 | tf_op jit(solution)/shard_map/ppermute | solution.py:412
  50.8 1.1 %collective-permute-done.15.rest_2_.refs_2_ = f32[4,48,128]{2,1,0:T(8,128)S(1)} collective-permute-done((f32[4,48,128]{2,1,0:T(8,128)S(1)}, f32[4,48,128]{2,1,0:T(8,128)S(1)}, u32[]{:S(2)}, u32[]{:S(2)}) %collective-permute-start.15) | collective-permute-done | bytes 98336 | tf_op jit(solution)/shard_map/ppermute | solution.py:412
  52.0 0.0 collective-permute-start.20
  52.0 0.5 collective-permute-start.19
  52.5 1.2 %collective-permute-done.23.rest_3_ = f32[4,48,128]{2,1,0:T(8,128)S(1)} collective-permute-done((f32[4,48,128]{2,1,0:T(8,128)S(1)}, f32[4,48,128]{2,1,0:T(8,128)S(1)}, u32[]{:S(2)}, u32[]{:S(2)}) %collective-permute-start.23) | collective-permute-done | bytes 98336 | tf_op jit(solution)/shard_map/ppermute | solution.py:412
  53.6 0.0 collective-permute-start.18
  53.6 1.5 %collective-permute-done.22.rest_2_.refs_6_ = f32[4,48,128]{2,1,0:T(8,128)S(1)} collective-permute-done((f32[4,48,128]{2,1,0:T(8,128)S(1)}, f32[4,48,128]{2,1,0:T(8,128)S(1)}, u32[]{:S(2)}, u32[]{:S(2)}) %collective-permute-start.22) | collective-permute-done | bytes 98336 | tf_op jit(solution)/shard_map/ppermute | solution.py:412
  55.1 0.0 collective-permute-start.24
  55.2 0.4 collective-permute-done.21.rest_1_
  55.5 0.1 collective-permute-start.27
  55.6 0.0 collective-permute-done.20.rest_7_
  55.6 0.4 collective-permute-start.26
  56.0 0.1 collective-permute-start.25
  56.2 0.0 collective-permute-done.18.rest_5_
  56.2 1.0 %shard_map.70.total_ref = f32[288,96]{1,0:T(8,128)S(1)} custom-call(bf16[32,96,256]{2,1,0:T(8,128)(2,1)S(1)} %get-tuple-element.9.xh_ref, bf16[32,96,256]{2,1,0:T(8,128)(2,1)S(1)} %get-tuple-element.10.xl_ref, f32[4,48,128]{2,1,0:T(8,128)S(1)} %pad_maximum_fusion.rest_0_.refs_0_, f32[4,48,128]{2,1,0:T(8,128)S(1)} %collective-permute-done.14.rest_1_, ...), custom_call_target="tpu_custom_call" | custom-call | tf_op jit(solution)/shard_map/pallas_call | solution.py:324
  57.2 0.0 collective-permute-done.27.rest_7_
  57.2 0.0 collective-permute-done.26.rest_6_.refs_7_
  57.2 0.1 collective-permute-done.25.rest_5_
  57.4 1.4 %shard_map.71 = f32[48,96]{1,0:T(8,128)S(1)} custom-call(bf16[32,96,256]{2,1,0:T(8,128)(2,1)S(1)} %get-tuple-element.9.xh_ref, bf16[32,96,256]{2,1,0:T(8,128)(2,1)S(1)} %get-tuple-element.10.xl_ref, f32[48,96]{1,0:T(8,128)S(1)} %get-tuple-element.11.w_ref, f32[288,96]{1,0:T(8,128)S(1)} %shard_map.70.total_ref, ...), custom_call_target="tpu_custom_call" | custom-call | tf_op jit(solution)/shard_map/pallas_call | solution.py:348
  58.8 1.6 %collective-permute-start.28 = (f32[48,96]{1,0:T(8,128)S(1)}, f32[48,96]{1,0:T(8,128)S(1)}, u32[]{:S(2)}, u32[]{:S(2)}) collective-permute-start(f32[48,96]{1,0:T(8,128)S(1)} %shard_map.71), channel_id=1, source_target_pairs={{0,4},{1,5},{2,6},{3,7},{4,0},{5,1},{6,2},{7,3},{8,12},{9,13},{10,... | collective-permute-start | bytes 55304 | tf_op jit(solution)/shard_map/ppermute | solution.py:412
  60.4 2.3 %collective-permute-done.28 = f32[48,96]{1,0:T(8,128)S(1)} collective-permute-done((f32[48,96]{1,0:T(8,128)S(1)}, f32[48,96]{1,0:T(8,128)S(1)}, u32[]{:S(2)}, u32[]{:S(2)}) %collective-permute-start.28) | collective-permute-done | bytes 18464 | tf_op jit(solution)/shard_map/ppermute | solution.py:412
  62.7 2.1 %collective-permute-start.31 = (f32[2,48,96]{2,1,0:T(8,128)S(1)}, f32[2,48,96]{2,1,0:T(8,128)S(1)}, u32[]{:S(2)}, u32[]{:S(2)}) collective-permute-start(f32[2,48,96]{2,1,0:T(8,128)S(1)} %pad_maximum_fusion.5.refs_0_), channel_id=1, source_target_pairs={{0,24},{1,25},{2,26},{3,27},{4,28},{5,29},{6,30},{7,31},{8,16},{9,... | collective-permute-start | bytes 110600 | tf_op jit(solution)/shard_map/ppermute | solution.py:412
  64.8 0.6 collective-permute-start.30
  65.4 1.7 %collective-permute-start.29 = (f32[2,48,96]{2,1,0:T(8,128)S(1)}, f32[2,48,96]{2,1,0:T(8,128)S(1)}, u32[]{:S(2)}, u32[]{:S(2)}) collective-permute-start(f32[2,48,96]{2,1,0:T(8,128)S(1)} %pad_maximum_fusion.5.refs_0_), channel_id=1, source_target_pairs={{0,8},{1,9},{2,10},{3,11},{4,12},{5,13},{6,14},{7,15},{8,0},{9,1},... | collective-permute-start | bytes 110600 | tf_op jit(solution)/shard_map/ppermute | solution.py:412
  67.1 1.0 %shard_map.73 = f32[32,32,48]{2,1,0:T(8,128)} custom-call(f32[4,48,128]{2,1,0:T(8,128)S(1)} %pad_maximum_fusion.rest_0_.refs_0_, f32[4,48,128]{2,1,0:T(8,128)S(1)} %collective-permute-done.17.rest_4_.refs_1_, f32[4,48,128]{2,1,0:T(8,128)S(1)} %collective-permute-done.15.rest_2_.refs_2_, f32[4,48,128]{2,1,0:T(8,128)S(1)} %collective-permute-done.19.rest_6_.refs_3_, ...), custom_call_target="tpu_custom_call" | custom-call | tf_op jit(solution)/shard_map/pallas_call | solution.py:369
  68.1 0.9 %collective-permute-done.31.refs_3_ = f32[2,48,96]{2,1,0:T(8,128)S(1)} collective-permute-done((f32[2,48,96]{2,1,0:T(8,128)S(1)}, f32[2,48,96]{2,1,0:T(8,128)S(1)}, u32[]{:S(2)}, u32[]{:S(2)}) %collective-permute-start.31) | collective-permute-done | bytes 36896 | tf_op jit(solution)/shard_map/ppermute | solution.py:412
  69.0 1.2 %collective-permute-done.30.refs_2_ = f32[2,48,96]{2,1,0:T(8,128)S(1)} collective-permute-done((f32[2,48,96]{2,1,0:T(8,128)S(1)}, f32[2,48,96]{2,1,0:T(8,128)S(1)}, u32[]{:S(2)}, u32[]{:S(2)}) %collective-permute-start.30) | collective-permute-done | bytes 36896 | tf_op jit(solution)/shard_map/ppermute | solution.py:412
  70.2 0.8 %shard_map.72 = f32[48,768]{1,0:T(8,128)} custom-call(f32[2,48,96]{2,1,0:T(8,128)S(1)} %pad_maximum_fusion.5.refs_0_, f32[2,48,96]{2,1,0:T(8,128)S(1)} %collective-permute-done.29.refs_1_, f32[2,48,96]{2,1,0:T(8,128)S(1)} %collective-permute-done.30.refs_2_, f32[2,48,96]{2,1,0:T(8,128)S(1)} %collective-permute-done.31.refs_3_), custom_call_target="tpu_custom_call" | custom-call | tf_op jit(solution)/shard_map/pallas_call | solution.py:396
  (24 shorter events, 0.2 us)
Async XLA Ops:
  10.9 1.9 %collective-permute-start.4 = (f32[768,128]{1,0:T(8,128)S(1)}, f32[768,128]{1,0:T(8,128)S(1)}, u32[]{:S(2)}, u32[]{:S(2)}) collective-permute-start(f32[768,128]{1,0:T(8,128)S(1)} %get-tuple-element.15), channel_id=1, source_target_pairs={{0,1},{1,0},{2,3},{3,2},{4,5},{5,4},{6,7},{7,6},{8,9},{9,8},{10,11... | collective-permute-start | bytes 1179656 | tf_op jit(solution)/shard_map/ppermute | solution.py:412
  11.5 5.9 %collective-permute-start = (f32[792,128]{1,0:T(8,128)S(1)}, f32[792,128]{1,0:T(8,128)S(1)}, u32[]{:S(2)}, u32[]{:S(2)}) collective-permute-start(f32[792,128]{1,0:T(8,128)S(1)} %get-tuple-element.13), channel_id=1, source_target_pairs={{0,1},{1,0},{2,3},{3,2},{4,5},{5,4},{6,7},{7,6},{8,9},{9,8},{10,11... | collective-permute-start | bytes 1216520 | tf_op jit(solution)/shard_map/ppermute | solution.py:412
  12.8 18.2 %copy-start = (f32[48,32,32]{0,2,1:T(8,128)S(1)}, f32[48,32,32]{0,2,1:T(8,128)}, u32[]{:S(2)}) copy-start(f32[48,32,32]{0,2,1:T(8,128)} %param.9) | copy-start | bytes 589828
  12.9 8.0 %collective-permute-start.7 = (f32[192,128]{1,0:T(8,128)S(1)}, f32[192,128]{1,0:T(8,128)S(1)}, u32[]{:S(2)}, u32[]{:S(2)}) collective-permute-start(f32[192,128]{1,0:T(8,128)S(1)} %get-tuple-element.20), channel_id=1, source_target_pairs={{0,6},{1,7},{2,4},{3,5},{4,2},{5,3},{6,0},{7,1},{8,14},{9,15},{10,... | collective-permute-start | bytes 294920 | tf_op jit(solution)/shard_map/ppermute | solution.py:412
  16.8 6.5 %collective-permute-start.6 = (f32[192,128]{1,0:T(8,128)S(1)}, f32[192,128]{1,0:T(8,128)S(1)}, u32[]{:S(2)}, u32[]{:S(2)}) collective-permute-start(f32[192,128]{1,0:T(8,128)S(1)} %get-tuple-element.21), channel_id=1, source_target_pairs={{0,2},{1,3},{2,0},{3,1},{4,6},{5,7},{6,4},{7,5},{8,10},{9,11},{10,... | collective-permute-start | bytes 294920 | tf_op jit(solution)/shard_map/ppermute | solution.py:412
  17.3 6.0 %collective-permute-start.5 = (f32[192,128]{1,0:T(8,128)S(1)}, f32[192,128]{1,0:T(8,128)S(1)}, u32[]{:S(2)}, u32[]{:S(2)}) collective-permute-start(f32[192,128]{1,0:T(8,128)S(1)} %get-tuple-element.22), channel_id=1, source_target_pairs={{0,4},{1,5},{2,6},{3,7},{4,0},{5,1},{6,2},{7,3},{8,12},{9,13},{10,... | collective-permute-start | bytes 294920 | tf_op jit(solution)/shard_map/ppermute | solution.py:412
  17.4 8.3 %collective-permute-start.3 = (f32[192,128]{1,0:T(8,128)S(1)}, f32[192,128]{1,0:T(8,128)S(1)}, u32[]{:S(2)}, u32[]{:S(2)}) collective-permute-start(f32[192,128]{1,0:T(8,128)S(1)} %get-tuple-element.17), channel_id=1, source_target_pairs={{0,6},{1,7},{2,4},{3,5},{4,2},{5,3},{6,0},{7,1},{8,14},{9,15},{10,... | collective-permute-start | bytes 294920 | tf_op jit(solution)/shard_map/ppermute | solution.py:412
  20.4 6.1 %collective-permute-start.2 = (f32[192,128]{1,0:T(8,128)S(1)}, f32[192,128]{1,0:T(8,128)S(1)}, u32[]{:S(2)}, u32[]{:S(2)}) collective-permute-start(f32[192,128]{1,0:T(8,128)S(1)} %get-tuple-element.18), channel_id=1, source_target_pairs={{0,4},{1,5},{2,6},{3,7},{4,0},{5,1},{6,2},{7,3},{8,12},{9,13},{10,... | collective-permute-start | bytes 294920 | tf_op jit(solution)/shard_map/ppermute | solution.py:412
  20.9 5.6 %collective-permute-start.1 = (f32[216,128]{1,0:T(8,128)S(1)}, f32[216,128]{1,0:T(8,128)S(1)}, u32[]{:S(2)}, u32[]{:S(2)}) collective-permute-start(f32[216,128]{1,0:T(8,128)S(1)} %slice_add_fusion.mine_ref), channel_id=1, source_target_pairs={{0,2},{1,3},{2,0},{3,1},{4,6},{5,7},{6,4},{7,5},{8,10},{9,11},{10,... | collective-permute-start | bytes 331784 | tf_op jit(solution)/shard_map/ppermute | solution.py:412
  26.5 6.4 %collective-permute-start.8 = (f32[48,256]{1,0:T(8,128)S(1)}, f32[48,256]{1,0:T(8,128)S(1)}, u32[]{:S(2)}, u32[]{:S(2)}) collective-permute-start(f32[48,256]{1,0:T(8,128)S(1)} %pad_maximum_fusion.2), channel_id=1, source_target_pairs={{0,24},{1,25},{2,26},{3,27},{4,28},{5,29},{6,30},{7,31},{8,16},{9,... | collective-permute-start | bytes 147464 | tf_op jit(solution)/shard_map/ppermute | solution.py:412
  30.3 5.0 %collective-permute-start.9 = (f32[48,256]{1,0:T(8,128)S(1)}, f32[48,256]{1,0:T(8,128)S(1)}, u32[]{:S(2)}, u32[]{:S(2)}) collective-permute-start(f32[48,256]{1,0:T(8,128)S(1)} %pad_maximum_fusion.3), channel_id=1, source_target_pairs={{0,16},{1,17},{2,18},{3,19},{4,20},{5,21},{6,22},{7,23},{8,24},{9,... | collective-permute-start | bytes 147464 | tf_op jit(solution)/shard_map/ppermute | solution.py:412
  30.4 5.0 %collective-permute-start.10 = (f32[48,256]{1,0:T(8,128)S(1)}, f32[48,256]{1,0:T(8,128)S(1)}, u32[]{:S(2)}, u32[]{:S(2)}) collective-permute-start(f32[48,256]{1,0:T(8,128)S(1)} %pad_maximum_fusion.4), channel_id=1, source_target_pairs={{0,8},{1,9},{2,10},{3,11},{4,12},{5,13},{6,14},{7,15},{8,0},{9,1},... | collective-permute-start | bytes 147464 | tf_op jit(solution)/shard_map/ppermute | solution.py:412
  35.4 6.0 %collective-permute-start.13 = (f32[48,256]{1,0:T(8,128)S(1)}, f32[48,256]{1,0:T(8,128)S(1)}, u32[]{:S(2)}, u32[]{:S(2)}) collective-permute-start(f32[48,256]{1,0:T(8,128)S(1)} %fusion.1), channel_id=1, source_target_pairs={{0,24},{1,25},{2,26},{3,27},{4,28},{5,29},{6,30},{7,31},{8,16},{9,... | collective-permute-start | bytes 147464 | tf_op jit(solution)/shard_map/ppermute | solution.py:412
  37.1 5.5 %collective-permute-start.12 = (f32[48,256]{1,0:T(8,128)S(1)}, f32[48,256]{1,0:T(8,128)S(1)}, u32[]{:S(2)}, u32[]{:S(2)}) collective-permute-start(f32[48,256]{1,0:T(8,128)S(1)} %fusion.1), channel_id=1, source_target_pairs={{0,16},{1,17},{2,18},{3,19},{4,20},{5,21},{6,22},{7,23},{8,24},{9,... | collective-permute-start | bytes 147464 | tf_op jit(solution)/shard_map/ppermute | solution.py:412
  37.5 5.0 %collective-permute-start.11 = (f32[48,256]{1,0:T(8,128)S(1)}, f32[48,256]{1,0:T(8,128)S(1)}, u32[]{:S(2)}, u32[]{:S(2)}) collective-permute-start(f32[48,256]{1,0:T(8,128)S(1)} %fusion.1), channel_id=1, source_target_pairs={{0,8},{1,9},{2,10},{3,11},{4,12},{5,13},{6,14},{7,15},{8,0},{9,1},... | collective-permute-start | bytes 147464 | tf_op jit(solution)/shard_map/ppermute | solution.py:412
  42.6 5.7 %collective-permute-start.17 = (f32[4,48,128]{2,1,0:T(8,128)S(1)}, f32[4,48,128]{2,1,0:T(8,128)S(1)}, u32[]{:S(2)}, u32[]{:S(2)}) collective-permute-start(f32[4,48,128]{2,1,0:T(8,128)S(1)} %pad_maximum_fusion.rest_0_.refs_0_), channel_id=1, source_target_pairs={{0,1},{1,0},{2,3},{3,2},{4,5},{5,4},{6,7},{7,6},{8,9},{9,8},{10,11... | collective-permute-start | bytes 294920 | tf_op jit(solution)/shard_map/ppermute | solution.py:412
  42.7 6.7 %collective-permute-start.16 = (f32[4,48,128]{2,1,0:T(8,128)S(1)}, f32[4,48,128]{2,1,0:T(8,128)S(1)}, u32[]{:S(2)}, u32[]{:S(2)}) collective-permute-start(f32[4,48,128]{2,1,0:T(8,128)S(1)} %pad_maximum_fusion.rest_0_.refs_0_), channel_id=1, source_target_pairs={{0,6},{1,7},{2,4},{3,5},{4,2},{5,3},{6,0},{7,1},{8,14},{9,15},{10,... | collective-permute-start | bytes 294920 | tf_op jit(solution)/shard_map/ppermute | solution.py:412
  44.7 7.2 %collective-permute-start.15 = (f32[4,48,128]{2,1,0:T(8,128)S(1)}, f32[4,48,128]{2,1,0:T(8,128)S(1)}, u32[]{:S(2)}, u32[]{:S(2)}) collective-permute-start(f32[4,48,128]{2,1,0:T(8,128)S(1)} %pad_maximum_fusion.rest_0_.refs_0_), channel_id=1, source_target_pairs={{0,2},{1,3},{2,0},{3,1},{4,6},{5,7},{6,4},{7,5},{8,10},{9,11},{10,... | collective-permute-start | bytes 294920 | tf_op jit(solution)/shard_map/ppermute | solution.py:412
  45.8 6.1 %collective-permute-start.14 = (f32[4,48,128]{2,1,0:T(8,128)S(1)}, f32[4,48,128]{2,1,0:T(8,128)S(1)}, u32[]{:S(2)}, u32[]{:S(2)}) collective-permute-start(f32[4,48,128]{2,1,0:T(8,128)S(1)} %pad_maximum_fusion.rest_0_.refs_0_), channel_id=1, source_target_pairs={{0,4},{1,5},{2,6},{3,7},{4,0},{5,1},{6,2},{7,3},{8,12},{9,13},{10,... | collective-permute-start | bytes 294920 | tf_op jit(solution)/shard_map/ppermute | solution.py:412
  46.3 7.4 %collective-permute-start.23 = (f32[4,48,128]{2,1,0:T(8,128)S(1)}, f32[4,48,128]{2,1,0:T(8,128)S(1)}, u32[]{:S(2)}, u32[]{:S(2)}) collective-permute-start(f32[4,48,128]{2,1,0:T(8,128)S(1)} %pad_maximum_fusion.1.rest_0_.refs_4_), channel_id=1, source_target_pairs={{0,6},{1,7},{2,4},{3,5},{4,2},{5,3},{6,0},{7,1},{8,14},{9,15},{10,... | collective-permute-start | bytes 294920 | tf_op jit(solution)/shard_map/ppermute | solution.py:412
  48.3 6.8 %collective-permute-start.22 = (f32[4,48,128]{2,1,0:T(8,128)S(1)}, f32[4,48,128]{2,1,0:T(8,128)S(1)}, u32[]{:S(2)}, u32[]{:S(2)}) collective-permute-start(f32[4,48,128]{2,1,0:T(8,128)S(1)} %pad_maximum_fusion.1.rest_0_.refs_4_), channel_id=1, source_target_pairs={{0,2},{1,3},{2,0},{3,1},{4,6},{5,7},{6,4},{7,5},{8,10},{9,11},{10,... | collective-permute-start | bytes 294920 | tf_op jit(solution)/shard_map/ppermute | solution.py:412
  49.4 6.1 %collective-permute-start.21 = (f32[4,48,128]{2,1,0:T(8,128)S(1)}, f32[4,48,128]{2,1,0:T(8,128)S(1)}, u32[]{:S(2)}, u32[]{:S(2)}) collective-permute-start(f32[4,48,128]{2,1,0:T(8,128)S(1)} %pad_maximum_fusion.1.rest_0_.refs_4_), channel_id=1, source_target_pairs={{0,4},{1,5},{2,6},{3,7},{4,0},{5,1},{6,2},{7,3},{8,12},{9,13},{10,... | collective-permute-start | bytes 294920 | tf_op jit(solution)/shard_map/ppermute | solution.py:412
  52.0 3.7 %collective-permute-start.20 = (f32[4,48,128]{2,1,0:T(8,128)S(1)}, f32[4,48,128]{2,1,0:T(8,128)S(1)}, u32[]{:S(2)}, u32[]{:S(2)}) collective-permute-start(f32[4,48,128]{2,1,0:T(8,128)S(1)} %collective-permute-done.16.rest_3_), channel_id=1, source_target_pairs={{0,1},{1,0},{2,3},{3,2},{4,5},{5,4},{6,7},{7,6},{8,9},{9,8},{10,11... | collective-permute-start | bytes 294920 | tf_op jit(solution)/shard_map/ppermute | solution.py:412
  52.0 4.1 %collective-permute-start.19 = (f32[4,48,128]{2,1,0:T(8,128)S(1)}, f32[4,48,128]{2,1,0:T(8,128)S(1)}, u32[]{:S(2)}, u32[]{:S(2)}) collective-permute-start(f32[4,48,128]{2,1,0:T(8,128)S(1)} %collective-permute-done.15.rest_2_.refs_2_), channel_id=1, source_target_pairs={{0,1},{1,0},{2,3},{3,2},{4,5},{5,4},{6,7},{7,6},{8,9},{9,8},{10,11... | collective-permute-start | bytes 294920 | tf_op jit(solution)/shard_map/ppermute | solution.py:412
  53.6 2.5 %collective-permute-start.18 = (f32[4,48,128]{2,1,0:T(8,128)S(1)}, f32[4,48,128]{2,1,0:T(8,128)S(1)}, u32[]{:S(2)}, u32[]{:S(2)}) collective-permute-start(f32[4,48,128]{2,1,0:T(8,128)S(1)} %collective-permute-done.14.rest_1_), channel_id=1, source_target_pairs={{0,1},{1,0},{2,3},{3,2},{4,5},{5,4},{6,7},{7,6},{8,9},{9,8},{10,11... | collective-permute-start | bytes 294920 | tf_op jit(solution)/shard_map/ppermute | solution.py:412
  55.1 2.1 %collective-permute-start.24 = (f32[4,48,128]{2,1,0:T(8,128)S(1)}, f32[4,48,128]{2,1,0:T(8,128)S(1)}, u32[]{:S(2)}, u32[]{:S(2)}) collective-permute-start(f32[4,48,128]{2,1,0:T(8,128)S(1)} %pad_maximum_fusion.1.rest_0_.refs_4_), channel_id=1, source_target_pairs={{0,1},{1,0},{2,3},{3,2},{4,5},{5,4},{6,7},{7,6},{8,9},{9,8},{10,11... | collective-permute-start | bytes 294920 | tf_op jit(solution)/shard_map/ppermute | solution.py:412
  55.5 1.7 %collective-permute-start.27 = (f32[4,48,128]{2,1,0:T(8,128)S(1)}, f32[4,48,128]{2,1,0:T(8,128)S(1)}, u32[]{:S(2)}, u32[]{:S(2)}) collective-permute-start(f32[4,48,128]{2,1,0:T(8,128)S(1)} %collective-permute-done.23.rest_3_), channel_id=1, source_target_pairs={{0,1},{1,0},{2,3},{3,2},{4,5},{5,4},{6,7},{7,6},{8,9},{9,8},{10,11... | collective-permute-start | bytes 294920 | tf_op jit(solution)/shard_map/ppermute | solution.py:412
  55.6 1.6 %collective-permute-start.26 = (f32[4,48,128]{2,1,0:T(8,128)S(1)}, f32[4,48,128]{2,1,0:T(8,128)S(1)}, u32[]{:S(2)}, u32[]{:S(2)}) collective-permute-start(f32[4,48,128]{2,1,0:T(8,128)S(1)} %collective-permute-done.22.rest_2_.refs_6_), channel_id=1, source_target_pairs={{0,1},{1,0},{2,3},{3,2},{4,5},{5,4},{6,7},{7,6},{8,9},{9,8},{10,11... | collective-permute-start | bytes 294920 | tf_op jit(solution)/shard_map/ppermute | solution.py:412
  56.0 1.3 %collective-permute-start.25 = (f32[4,48,128]{2,1,0:T(8,128)S(1)}, f32[4,48,128]{2,1,0:T(8,128)S(1)}, u32[]{:S(2)}, u32[]{:S(2)}) collective-permute-start(f32[4,48,128]{2,1,0:T(8,128)S(1)} %collective-permute-done.21.rest_1_), channel_id=1, source_target_pairs={{0,1},{1,0},{2,3},{3,2},{4,5},{5,4},{6,7},{7,6},{8,9},{9,8},{10,11... | collective-permute-start | bytes 294920 | tf_op jit(solution)/shard_map/ppermute | solution.py:412
  58.8 3.9 %collective-permute-start.28 = (f32[48,96]{1,0:T(8,128)S(1)}, f32[48,96]{1,0:T(8,128)S(1)}, u32[]{:S(2)}, u32[]{:S(2)}) collective-permute-start(f32[48,96]{1,0:T(8,128)S(1)} %shard_map.71), channel_id=1, source_target_pairs={{0,4},{1,5},{2,6},{3,7},{4,0},{5,1},{6,2},{7,3},{8,12},{9,13},{10,... | collective-permute-start | bytes 55304 | tf_op jit(solution)/shard_map/ppermute | solution.py:412
  62.7 6.3 %collective-permute-start.31 = (f32[2,48,96]{2,1,0:T(8,128)S(1)}, f32[2,48,96]{2,1,0:T(8,128)S(1)}, u32[]{:S(2)}, u32[]{:S(2)}) collective-permute-start(f32[2,48,96]{2,1,0:T(8,128)S(1)} %pad_maximum_fusion.5.refs_0_), channel_id=1, source_target_pairs={{0,24},{1,25},{2,26},{3,27},{4,28},{5,29},{6,30},{7,31},{8,16},{9,... | collective-permute-start | bytes 110600 | tf_op jit(solution)/shard_map/ppermute | solution.py:412
  64.8 5.4 %collective-permute-start.30 = (f32[2,48,96]{2,1,0:T(8,128)S(1)}, f32[2,48,96]{2,1,0:T(8,128)S(1)}, u32[]{:S(2)}, u32[]{:S(2)}) collective-permute-start(f32[2,48,96]{2,1,0:T(8,128)S(1)} %pad_maximum_fusion.5.refs_0_), channel_id=1, source_target_pairs={{0,16},{1,17},{2,18},{3,19},{4,20},{5,21},{6,22},{7,23},{8,24},{9,... | collective-permute-start | bytes 110600 | tf_op jit(solution)/shard_map/ppermute | solution.py:412
  65.4 4.8 %collective-permute-start.29 = (f32[2,48,96]{2,1,0:T(8,128)S(1)}, f32[2,48,96]{2,1,0:T(8,128)S(1)}, u32[]{:S(2)}, u32[]{:S(2)}) collective-permute-start(f32[2,48,96]{2,1,0:T(8,128)S(1)} %pad_maximum_fusion.5.refs_0_), channel_id=1, source_target_pairs={{0,8},{1,9},{2,10},{3,11},{4,12},{5,13},{6,14},{7,15},{8,0},{9,1},... | collective-permute-start | bytes 110600 | tf_op jit(solution)/shard_map/ppermute | solution.py:412

commit v11 on v10

--- a/solution.py
+++ b/solution.py
@@ -66,58 +66,56 @@
     out_ref[...] = jnp.transpose(values / total)
 
 
-def column_table(row, margin):
+def blur_plane(plane, row, taps):
+    margin = (taps - 1) // 2
+    step = LANES - 2 * margin
+    height = plane.shape[0]
     table = pltpu.roll(jnp.broadcast_to(row, (LANES, LANES)), 0, 1, stride=1, stride_axis=0)
-    high = table.astype(BF16).astype(F32)
-    src = lax.broadcasted_iota(jnp.int32, (GROUP, LANES), 0)
-    dst = lax.broadcasted_iota(jnp.int32, (GROUP, LANES), 1)
-    first, last = slice(0, GROUP), slice(LANES - GROUP, LANES)
-    above = dst - src <= LANES // 2
-    below = src + LANES - GROUP - dst <= LANES // 2
-    empty = jnp.zeros((LANES - 2 * GROUP, LANES), F32)
-    main, edge = [], []
-    for part in (high, table - high):
-        main.append(jnp.concatenate(
-            [jnp.where(above, part[first], 0.0), part[GROUP:LANES - GROUP], jnp.where(below, part[last], 0.0)],
-            axis=0).astype(BF16))
-        edge.append(jnp.concatenate(
-            [jnp.where(above, 0.0, part[first]), empty, jnp.where(below, 0.0, part[last])],
-            axis=0).astype(BF16))
-    return jnp.concatenate([jnp.concatenate(main, axis=1), jnp.concatenate(edge, axis=1)], axis=0)
-
-
-def blur_plane(plane, row, margin):
-    height = plane.shape[0]
-    table = column_table(row, margin)
+    table = jnp.concatenate(split(table), axis=1)
     left, right = plane[:, :LANES], plane[:, LANES:]
     lane = lax.broadcasted_iota(jnp.int32, left.shape, 1)
-    main = jnp.concatenate([left, right], axis=0)
-    edge = jnp.concatenate(
-        [jnp.where(lane < LANES // 2, right, 0.0), jnp.where(lane < LANES // 2, 0.0, left)], axis=0)
-    high, low = split(jnp.concatenate([main, edge], axis=1))
-    product = dot(jnp.concatenate([high, low], axis=0), table)
-    rows = 2 * height
-    blocks = product[:rows, :LANES] + (product[:rows, LANES:] + product[rows:, :LANES])
-    return jnp.concatenate([blocks[:height], blocks[height:]], axis=1)
-
-
-def row_table(base, margin, height):
-    high = base.astype(BF16).astype(F32)
-    low = base - high
-    plane = lax.broadcasted_iota(jnp.int32, (8, LANES), 0)
+    windows = [
+        jnp.where(lane >= margin, pltpu.roll(left, margin, 1), 0.0),
+        pltpu.roll(jnp.where(lane < LANES - 3 * margin, right, left), 3 * margin, 1),
+        jnp.where(lane < 5 * margin, pltpu.roll(right, 5 * margin, 1), 0.0),
+    ]
+    image = jnp.concatenate(split(jnp.concatenate(windows, axis=0)), axis=1)
+    product = dot(image, jnp.concatenate([table, table], axis=0))
+    blocks = product[:, :LANES] + product[:, LANES:]
+    first, second, third = [blocks[k * height:(k + 1) * height] for k in range(3)]
+    second = pltpu.roll(second, step, 1)
+    third = pltpu.roll(third, 2 * step - LANES, 1)
+    return jnp.concatenate(
+        [jnp.where(lane < step, first, second), jnp.where(lane < 2 * step - LANES, second, third)], axis=1)
+
+
+def blur_rows_of(images, rows, margin):
+    height = images[0].shape[0]
+    sub = lax.broadcasted_iota(jnp.int32, (8, LANES), 0)
     lane = lax.broadcasted_iota(jnp.int32, (8, LANES), 1)
-    per_vector = LANES // height
-    own = lane // height == plane % per_vector
-    masks = [own & (plane // per_vector == part) for part in range(8 * height // LANES)]
-
-    def table(part):
-        strips = []
-        for row in range(height):
-            rolled = pltpu.roll(part, (row - margin) % LANES, 1)
-            strips.append(jnp.concatenate([jnp.where(mask, rolled, 0.0) for mask in masks], axis=1))
-        return jnp.concatenate(strips, axis=0).astype(BF16)
-
-    return table(high), table(low)
+    lower = sub < 4
+    own = lane // height == sub % 4
+    moved = pltpu.roll(pltpu.roll(rows, 4, 0), 1, 1)
+    results = []
+    for group, base in ((0, jnp.where(lower, rows, moved)), (1, jnp.where(lower, moved, rows))):
+        high = base.astype(BF16).astype(F32)
+        strips = [
+            jnp.where(own, pltpu.roll(part, (2 * pair - margin) % LANES, 1), 0.0)
+            for part in (high, base - high) for pair in range(height // 2)]
+        table = jnp.concatenate(strips, axis=0).astype(BF16)
+        table = jnp.concatenate([table, table], axis=1)
+        image = jnp.concatenate(split(jnp.concatenate(images[4 * group:4 * group + 4], axis=0)), axis=0)
+        product = dot(table, image)
+        half = product.shape[0] // 2
+        results.append(product[:half] + product[half:])
+    lower = lax.broadcasted_iota(jnp.int32, (8, results[0].shape[1]), 0) < 4
+    out = []
+    for pair in range(height // 2):
+        here = slice(8 * pair, 8 * pair + 8)
+        one, two = results[0][here], results[1][here]
+        out.append(jnp.where(lower, one, two))
+        out.append(pltpu.roll(jnp.where(lower, two, one), 4, 0))
+    return jnp.concatenate(out, axis=0).reshape(height, 8, results[0].shape[1])
 
 
 def fold(square):
@@ -148,19 +146,15 @@
     return both[:rank] + (both[rank:] + dot_nt(high, padded_low))
 
 
-def blur_group(step, cube_ref, kx_ref, ky_ref, xh_ref, xl_ref, margin):
-    height = cube_ref.shape[1]
+def blur_group(step, cube_ref, kx_ref, ky_ref, xh_ref, xl_ref, taps):
     halves = []
     for half in range(GROUP // 8):
         done = []
         for k in range(8 * half, 8 * half + 8):
             plane = step * GROUP + k
-            done.append(blur_plane(cube_ref[plane], kx_ref[pl.ds(plane, 1), :], margin))
-        high, low = split(jnp.concatenate(done, axis=0))
+            done.append(blur_plane(cube_ref[plane], kx_ref[pl.ds(plane, 1), :], taps))
         rows = ky_ref[pl.ds(pl.multiple_of(step * GROUP + 8 * half, 8), 8), :]
-        table_high, table_low = row_table(rows, margin, height)
-        result = dot(table_high, high) + (dot(table_low, high) + dot(table_high, low))
-        halves.append(result.reshape(height, 8, result.shape[1]))
+        halves.append(blur_rows_of(done, rows, (taps - 1) // 2))
     high, low = split(jnp.concatenate(halves, axis=1))
     planes_here = pl.ds(pl.multiple_of(step * GROUP, GROUP), GROUP)
     xh_ref[:, planes_here, :] = high
@@ -190,7 +184,7 @@
         chunk(step).start()
     copies[0].wait()
     normalized_taps(taps_x_ref, True, work_ref, kx_ref)
-    kx_ref[...] = pltpu.roll(kx_ref[...], LANES - margin, 1)
+    kx_ref[...] = pltpu.roll(kx_ref[...], LANES - 2 * margin, 1)
     copies[1].wait()
     normalized_taps(taps_y_ref, False, work_ref, ky_ref)
     per_vector = LANES // height
@@ -204,7 +198,7 @@
 
     def body(step, carry):
         chunk(step).wait()
-        blur_group(step, cube_ref, kx_ref, ky_ref, xh_ref, xl_ref, margin)
+        blur_group(step, cube_ref, kx_ref, ky_ref, xh_ref, xl_ref, taps)
         return carry
 
     lax.fori_loop(0, groups, body, 0)

time: 71.1 us -> 71.4 us (level)
  no operation moved by 1% of the time
where the time goes in v11:
time: 71.4 us; the launch traced here: 71.3 us
  starting transfers between devices  34.3 us (48%)
  waiting for transfers between devices  20.8 us (29%)
  Pallas kernels  15.1 us (21%)
  between operations  0.77 us (1%)
    ppermute x32, starting transfers between devices, send(): return lax.ppermute(value, ('sp', 'bd'), pairs)  34.3 us
    ppermute x32, waiting for transfers between devices, send(): return lax.ppermute(value, ('sp', 'bd'), pairs)  20.8 us
    pallas_call x1, Pallas kernels, blur_call(): pl.pallas_call(blur_kernel, out_shape=[jax.ShapeDtypeStruct(image, BF16)]...  10.6 us
  transfers between devices with their start and end apart: 32, of which 17 were waited for; matrix products, arithmetic and copies ran while one was open for 0% of the time, Pallas kernels for 3%

profile of v11, /device:TPU:0, one launch (start us, length us, event | category | flops | bytes accessed | tf_op | source)
XLA Modules:
  0.0 71.3 jit_solution(6618169337489202454)
XLA Ops:
  0.6 10.6 %shard_map.68 = (bf16[32,96,256]{2,1,0:T(8,128)(2,1)S(1)}, bf16[32,96,256]{2,1,0:T(8,128)(2,1)S(1)}, f32[48,96]{1,0:T(8,128)S(1)}, f32[792,128]{1,0:T(8,128)S(1)...) custom-call(f32[96,32,256]{2,1,0:T(8,128)} %bitcast.31, f32[25,1,96]{2,1,0:T(1,128)} %bitcast.36, ...), custom_call_target="tpu_custom_call" | custom-call | tf_op jit(solution)/shard_map/pallas_call | solution.py:249
  11.3 0.5 collective-permute-start.4
  11.8 0.1 collective-permute-start
  11.9 1.3 %collective-permute-done.4 = f32[768,128]{1,0:T(8,128)S(1)} collective-permute-done((f32[768,128]{1,0:T(8,128)S(1)}, f32[768,128]{1,0:T(8,128)S(1)}, u32[]{:S(2)}, u32[]{:S(2)}) %collective-permute-start.4) | collective-permute-done | bytes 393248 | tf_op jit(solution)/shard_map/ppermute | solution.py:406
  13.1 0.1 slice_add_fusion.4
  13.2 3.9 %collective-permute-start.7 = (f32[192,128]{1,0:T(8,128)S(1)}, f32[192,128]{1,0:T(8,128)S(1)}, u32[]{:S(2)}, u32[]{:S(2)}) collective-permute-start(f32[192,128]{1,0:T(8,128)S(1)} %get-tuple-element.20), channel_id=1, source_target_pairs={{0,6},{1,7},{2,4},{3,5},{4,2},{5,3},{6,0},{7,1},{8,14},{9,15},{10,... | collective-permute-start | bytes 294920 | tf_op jit(solution)/shard_map/ppermute | solution.py:406
  17.1 0.5 collective-permute-start.6
  17.6 0.1 collective-permute-start.5
  17.7 0.0 collective-permute-done
  17.8 2.9 %collective-permute-start.3 = (f32[192,128]{1,0:T(8,128)S(1)}, f32[192,128]{1,0:T(8,128)S(1)}, u32[]{:S(2)}, u32[]{:S(2)}) collective-permute-start(f32[192,128]{1,0:T(8,128)S(1)} %get-tuple-element.17), channel_id=1, source_target_pairs={{0,6},{1,7},{2,4},{3,5},{4,2},{5,3},{6,0},{7,1},{8,14},{9,15},{10,... | collective-permute-start | bytes 294920 | tf_op jit(solution)/shard_map/ppermute | solution.py:406
  20.7 0.5 collective-permute-start.2
  21.2 0.0 collective-permute-done.7
  21.2 1.4 %collective-permute-start.1 = (f32[216,128]{1,0:T(8,128)S(1)}, f32[216,128]{1,0:T(8,128)S(1)}, u32[]{:S(2)}, u32[]{:S(2)}) collective-permute-start(f32[216,128]{1,0:T(8,128)S(1)} %slice_add_fusion.mine_ref), channel_id=1, source_target_pairs={{0,2},{1,3},{2,0},{3,1},{4,6},{5,7},{6,4},{7,5},{8,10},{9,11},{10,... | collective-permute-start | bytes 331784 | tf_op jit(solution)/shard_map/ppermute | solution.py:406
  22.6 0.9 %collective-permute-done.6 = f32[192,128]{1,0:T(8,128)S(1)} collective-permute-done((f32[192,128]{1,0:T(8,128)S(1)}, f32[192,128]{1,0:T(8,128)S(1)}, u32[]{:S(2)}, u32[]{:S(2)}) %collective-permute-start.6) | collective-permute-done | bytes 98336 | tf_op jit(solution)/shard_map/ppermute | solution.py:406
  23.5 0.0 collective-permute-done.5
  23.6 2.5 %collective-permute-done.3 = f32[192,128]{1,0:T(8,128)S(1)} collective-permute-done((f32[192,128]{1,0:T(8,128)S(1)}, f32[192,128]{1,0:T(8,128)S(1)}, u32[]{:S(2)}, u32[]{:S(2)}) %collective-permute-start.3) | collective-permute-done | bytes 98336 | tf_op jit(solution)/shard_map/ppermute | solution.py:406
  26.1 0.7 collective-permute-done.2
  26.7 0.1 collective-permute-done.1.other_ref
  26.8 3.8 %collective-permute-start.8 = (f32[48,256]{1,0:T(8,128)S(1)}, f32[48,256]{1,0:T(8,128)S(1)}, u32[]{:S(2)}, u32[]{:S(2)}) collective-permute-start(f32[48,256]{1,0:T(8,128)S(1)} %pad_maximum_fusion.2), channel_id=1, source_target_pairs={{0,24},{1,25},{2,26},{3,27},{4,28},{5,29},{6,30},{7,31},{8,16},{9,... | collective-permute-start | bytes 147464 | tf_op jit(solution)/shard_map/ppermute | solution.py:406
  30.7 0.0 collective-permute-start.9
  30.7 0.6 collective-permute-start.10
  31.3 0.3 shard_map.69
  31.6 1.7 %collective-permute-done.8 = f32[48,256]{1,0:T(8,128)S(1)} collective-permute-done((f32[48,256]{1,0:T(8,128)S(1)}, f32[48,256]{1,0:T(8,128)S(1)}, u32[]{:S(2)}, u32[]{:S(2)}) %collective-permute-start.8) | collective-permute-done | bytes 49184 | tf_op jit(solution)/shard_map/ppermute | solution.py:406
  33.3 2.4 %collective-permute-done.9 = f32[48,256]{1,0:T(8,128)S(1)} collective-permute-done((f32[48,256]{1,0:T(8,128)S(1)}, f32[48,256]{1,0:T(8,128)S(1)}, u32[]{:S(2)}, u32[]{:S(2)}) %collective-permute-start.9) | collective-permute-done | bytes 49184 | tf_op jit(solution)/shard_map/ppermute | solution.py:406
  35.6 0.0 collective-permute-done.10
  35.7 1.7 %collective-permute-start.13 = (f32[48,256]{1,0:T(8,128)S(1)}, f32[48,256]{1,0:T(8,128)S(1)}, u32[]{:S(2)}, u32[]{:S(2)}) collective-permute-start(f32[48,256]{1,0:T(8,128)S(1)} %fusion.1), channel_id=1, source_target_pairs={{0,24},{1,25},{2,26},{3,27},{4,28},{5,29},{6,30},{7,31},{8,16},{9,... | collective-permute-start | bytes 147464 | tf_op jit(solution)/shard_map/ppermute | solution.py:406
  37.4 0.5 collective-permute-start.12
  37.9 2.3 %collective-permute-start.11 = (f32[48,256]{1,0:T(8,128)S(1)}, f32[48,256]{1,0:T(8,128)S(1)}, u32[]{:S(2)}, u32[]{:S(2)}) collective-permute-start(f32[48,256]{1,0:T(8,128)S(1)} %fusion.1), channel_id=1, source_target_pairs={{0,8},{1,9},{2,10},{3,11},{4,12},{5,13},{6,14},{7,15},{8,0},{9,1},... | collective-permute-start | bytes 147464 | tf_op jit(solution)/shard_map/ppermute | solution.py:406
  40.1 1.5 %collective-permute-done.13 = f32[48,256]{1,0:T(8,128)S(1)} collective-permute-done((f32[48,256]{1,0:T(8,128)S(1)}, f32[48,256]{1,0:T(8,128)S(1)}, u32[]{:S(2)}, u32[]{:S(2)}) %collective-permute-start.13) | collective-permute-done | bytes 49184 | tf_op jit(solution)/shard_map/ppermute | solution.py:406
  41.6 1.3 %collective-permute-done.12 = f32[48,256]{1,0:T(8,128)S(1)} collective-permute-done((f32[48,256]{1,0:T(8,128)S(1)}, f32[48,256]{1,0:T(8,128)S(1)}, u32[]{:S(2)}, u32[]{:S(2)}) %collective-permute-start.12) | collective-permute-done | bytes 49184 | tf_op jit(solution)/shard_map/ppermute | solution.py:406
  42.9 0.0 collective-permute-done.11
  42.9 0.1 collective-permute-start.17
  43.0 2.1 %collective-permute-start.16 = (f32[4,48,128]{2,1,0:T(8,128)S(1)}, f32[4,48,128]{2,1,0:T(8,128)S(1)}, u32[]{:S(2)}, u32[]{:S(2)}) collective-permute-start(f32[4,48,128]{2,1,0:T(8,128)S(1)} %pad_maximum_fusion.rest_0_.refs_0_), channel_id=1, source_target_pairs={{0,6},{1,7},{2,4},{3,5},{4,2},{5,3},{6,0},{7,1},{8,14},{9,15},{10,... | collective-permute-start | bytes 294920 | tf_op jit(solution)/shard_map/ppermute | solution.py:406
  45.1 1.1 %collective-permute-start.15 = (f32[4,48,128]{2,1,0:T(8,128)S(1)}, f32[4,48,128]{2,1,0:T(8,128)S(1)}, u32[]{:S(2)}, u32[]{:S(2)}) collective-permute-start(f32[4,48,128]{2,1,0:T(8,128)S(1)} %pad_maximum_fusion.rest_0_.refs_0_), channel_id=1, source_target_pairs={{0,2},{1,3},{2,0},{3,1},{4,6},{5,7},{6,4},{7,5},{8,10},{9,11},{10,... | collective-permute-start | bytes 294920 | tf_op jit(solution)/shard_map/ppermute | solution.py:406
  46.2 0.4 collective-permute-start.14
  46.6 2.0 %collective-permute-start.23 = (f32[4,48,128]{2,1,0:T(8,128)S(1)}, f32[4,48,128]{2,1,0:T(8,128)S(1)}, u32[]{:S(2)}, u32[]{:S(2)}) collective-permute-start(f32[4,48,128]{2,1,0:T(8,128)S(1)} %pad_maximum_fusion.1.rest_0_.refs_4_), channel_id=1, source_target_pairs={{0,6},{1,7},{2,4},{3,5},{4,2},{5,3},{6,0},{7,1},{8,14},{9,15},{10,... | collective-permute-start | bytes 294920 | tf_op jit(solution)/shard_map/ppermute | solution.py:406
  48.6 0.0 collective-permute-done.17.rest_4_.refs_1_
  48.6 1.1 %collective-permute-start.22 = (f32[4,48,128]{2,1,0:T(8,128)S(1)}, f32[4,48,128]{2,1,0:T(8,128)S(1)}, u32[]{:S(2)}, u32[]{:S(2)}) collective-permute-start(f32[4,48,128]{2,1,0:T(8,128)S(1)} %pad_maximum_fusion.1.rest_0_.refs_4_), channel_id=1, source_target_pairs={{0,2},{1,3},{2,0},{3,1},{4,6},{5,7},{6,4},{7,5},{8,10},{9,11},{10,... | collective-permute-start | bytes 294920 | tf_op jit(solution)/shard_map/ppermute | solution.py:406
  49.7 0.0 collective-permute-done.16.rest_3_
  49.7 1.5 %collective-permute-start.21 = (f32[4,48,128]{2,1,0:T(8,128)S(1)}, f32[4,48,128]{2,1,0:T(8,128)S(1)}, u32[]{:S(2)}, u32[]{:S(2)}) collective-permute-start(f32[4,48,128]{2,1,0:T(8,128)S(1)} %pad_maximum_fusion.1.rest_0_.refs_4_), channel_id=1, source_target_pairs={{0,4},{1,5},{2,6},{3,7},{4,0},{5,1},{6,2},{7,3},{8,12},{9,13},{10,... | collective-permute-start | bytes 294920 | tf_op jit(solution)/shard_map/ppermute | solution.py:406
  51.2 1.1 %collective-permute-done.15.rest_2_.refs_2_ = f32[4,48,128]{2,1,0:T(8,128)S(1)} collective-permute-done((f32[4,48,128]{2,1,0:T(8,128)S(1)}, f32[4,48,128]{2,1,0:T(8,128)S(1)}, u32[]{:S(2)}, u32[]{:S(2)}) %collective-permute-start.15) | collective-permute-done | bytes 98336 | tf_op jit(solution)/shard_map/ppermute | solution.py:406
  52.3 0.5 collective-permute-start.19
  52.8 1.2 %collective-permute-done.23.rest_3_ = f32[4,48,128]{2,1,0:T(8,128)S(1)} collective-permute-done((f32[4,48,128]{2,1,0:T(8,128)S(1)}, f32[4,48,128]{2,1,0:T(8,128)S(1)}, u32[]{:S(2)}, u32[]{:S(2)}) %collective-permute-start.23) | collective-permute-done | bytes 98336 | tf_op jit(solution)/shard_map/ppermute | solution.py:406
  54.0 1.5 %collective-permute-done.22.rest_2_.refs_6_ = f32[4,48,128]{2,1,0:T(8,128)S(1)} collective-permute-done((f32[4,48,128]{2,1,0:T(8,128)S(1)}, f32[4,48,128]{2,1,0:T(8,128)S(1)}, u32[]{:S(2)}, u32[]{:S(2)}) %collective-permute-start.22) | collective-permute-done | bytes 98336 | tf_op jit(solution)/shard_map/ppermute | solution.py:406
  55.4 0.0 collective-permute-start.24
  55.5 0.4 collective-permute-done.21.rest_1_
  55.9 0.1 collective-permute-start.27
  55.9 0.0 collective-permute-done.20.rest_7_
  56.0 0.4 collective-permute-start.26
  56.4 0.1 collective-permute-start.25
  56.5 0.0 collective-permute-done.18.rest_5_
  56.5 1.0 %shard_map.70.total_ref = f32[288,96]{1,0:T(8,128)S(1)} custom-call(bf16[32,96,256]{2,1,0:T(8,128)(2,1)S(1)} %get-tuple-element.9.xh_ref, bf16[32,96,256]{2,1,0:T(8,128)(2,1)S(1)} %get-tuple-element.10.xl_ref, f32[4,48,128]{2,1,0:T(8,128)S(1)} %pad_maximum_fusion.rest_0_.refs_0_, f32[4,48,128]{2,1,0:T(8,128)S(1)} %collective-permute-done.14.rest_1_, ...), custom_call_target="tpu_custom_call" | custom-call | tf_op jit(solution)/shard_map/pallas_call | solution.py:318
  57.5 0.0 collective-permute-done.24.rest_4_.refs_5_
  57.6 0.1 collective-permute-done.25.rest_5_
  57.7 1.4 %shard_map.71 = f32[48,96]{1,0:T(8,128)S(1)} custom-call(bf16[32,96,256]{2,1,0:T(8,128)(2,1)S(1)} %get-tuple-element.9.xh_ref, bf16[32,96,256]{2,1,0:T(8,128)(2,1)S(1)} %get-tuple-element.10.xl_ref, f32[48,96]{1,0:T(8,128)S(1)} %get-tuple-element.11.w_ref, f32[288,96]{1,0:T(8,128)S(1)} %shard_map.70.total_ref, ...), custom_call_target="tpu_custom_call" | custom-call | tf_op jit(solution)/shard_map/pallas_call | solution.py:342
  59.1 1.6 %collective-permute-start.28 = (f32[48,96]{1,0:T(8,128)S(1)}, f32[48,96]{1,0:T(8,128)S(1)}, u32[]{:S(2)}, u32[]{:S(2)}) collective-permute-start(f32[48,96]{1,0:T(8,128)S(1)} %shard_map.71), channel_id=1, source_target_pairs={{0,4},{1,5},{2,6},{3,7},{4,0},{5,1},{6,2},{7,3},{8,12},{9,13},{10,... | collective-permute-start | bytes 55304 | tf_op jit(solution)/shard_map/ppermute | solution.py:406
  60.7 2.3 %collective-permute-done.28 = f32[48,96]{1,0:T(8,128)S(1)} collective-permute-done((f32[48,96]{1,0:T(8,128)S(1)}, f32[48,96]{1,0:T(8,128)S(1)}, u32[]{:S(2)}, u32[]{:S(2)}) %collective-permute-start.28) | collective-permute-done | bytes 18464 | tf_op jit(solution)/shard_map/ppermute | solution.py:406
  63.0 2.1 %collective-permute-start.31 = (f32[2,48,96]{2,1,0:T(8,128)S(1)}, f32[2,48,96]{2,1,0:T(8,128)S(1)}, u32[]{:S(2)}, u32[]{:S(2)}) collective-permute-start(f32[2,48,96]{2,1,0:T(8,128)S(1)} %pad_maximum_fusion.5.refs_0_), channel_id=1, source_target_pairs={{0,24},{1,25},{2,26},{3,27},{4,28},{5,29},{6,30},{7,31},{8,16},{9,... | collective-permute-start | bytes 110600 | tf_op jit(solution)/shard_map/ppermute | solution.py:406
  65.1 0.6 collective-permute-start.30
  65.7 1.7 %collective-permute-start.29 = (f32[2,48,96]{2,1,0:T(8,128)S(1)}, f32[2,48,96]{2,1,0:T(8,128)S(1)}, u32[]{:S(2)}, u32[]{:S(2)}) collective-permute-start(f32[2,48,96]{2,1,0:T(8,128)S(1)} %pad_maximum_fusion.5.refs_0_), channel_id=1, source_target_pairs={{0,8},{1,9},{2,10},{3,11},{4,12},{5,13},{6,14},{7,15},{8,0},{9,1},... | collective-permute-start | bytes 110600 | tf_op jit(solution)/shard_map/ppermute | solution.py:406
  67.4 1.0 %shard_map.73 = f32[32,32,48]{2,1,0:T(8,128)} custom-call(f32[4,48,128]{2,1,0:T(8,128)S(1)} %pad_maximum_fusion.rest_0_.refs_0_, f32[4,48,128]{2,1,0:T(8,128)S(1)} %collective-permute-done.17.rest_4_.refs_1_, f32[4,48,128]{2,1,0:T(8,128)S(1)} %collective-permute-done.15.rest_2_.refs_2_, f32[4,48,128]{2,1,0:T(8,128)S(1)} %collective-permute-done.19.rest_6_.refs_3_, ...), custom_call_target="tpu_custom_call" | custom-call | tf_op jit(solution)/shard_map/pallas_call | solution.py:363
  68.4 0.9 %collective-permute-done.31.refs_3_ = f32[2,48,96]{2,1,0:T(8,128)S(1)} collective-permute-done((f32[2,48,96]{2,1,0:T(8,128)S(1)}, f32[2,48,96]{2,1,0:T(8,128)S(1)}, u32[]{:S(2)}, u32[]{:S(2)}) %collective-permute-start.31) | collective-permute-done | bytes 36896 | tf_op jit(solution)/shard_map/ppermute | solution.py:406
  69.3 1.2 %collective-permute-done.30.refs_2_ = f32[2,48,96]{2,1,0:T(8,128)S(1)} collective-permute-done((f32[2,48,96]{2,1,0:T(8,128)S(1)}, f32[2,48,96]{2,1,0:T(8,128)S(1)}, u32[]{:S(2)}, u32[]{:S(2)}) %collective-permute-start.30) | collective-permute-done | bytes 36896 | tf_op jit(solution)/shard_map/ppermute | solution.py:406
  70.5 0.8 %shard_map.72 = f32[48,768]{1,0:T(8,128)} custom-call(f32[2,48,96]{2,1,0:T(8,128)S(1)} %pad_maximum_fusion.5.refs_0_, f32[2,48,96]{2,1,0:T(8,128)S(1)} %collective-permute-done.29.refs_1_, f32[2,48,96]{2,1,0:T(8,128)S(1)} %collective-permute-done.30.refs_2_, f32[2,48,96]{2,1,0:T(8,128)S(1)} %collective-permute-done.31.refs_3_), custom_call_target="tpu_custom_call" | custom-call | tf_op jit(solution)/shard_map/pallas_call | solution.py:390
  (24 shorter events, 0.2 us)
Async XLA Ops:
  11.3 1.9 %collective-permute-start.4 = (f32[768,128]{1,0:T(8,128)S(1)}, f32[768,128]{1,0:T(8,128)S(1)}, u32[]{:S(2)}, u32[]{:S(2)}) collective-permute-start(f32[768,128]{1,0:T(8,128)S(1)} %get-tuple-element.15), channel_id=1, source_target_pairs={{0,1},{1,0},{2,3},{3,2},{4,5},{5,4},{6,7},{7,6},{8,9},{9,8},{10,11... | collective-permute-start | bytes 1179656 | tf_op jit(solution)/shard_map/ppermute | solution.py:406
  11.8 5.9 %collective-permute-start = (f32[792,128]{1,0:T(8,128)S(1)}, f32[792,128]{1,0:T(8,128)S(1)}, u32[]{:S(2)}, u32[]{:S(2)}) collective-permute-start(f32[792,128]{1,0:T(8,128)S(1)} %get-tuple-element.13), channel_id=1, source_target_pairs={{0,1},{1,0},{2,3},{3,2},{4,5},{5,4},{6,7},{7,6},{8,9},{9,8},{10,11... | collective-permute-start | bytes 1216520 | tf_op jit(solution)/shard_map/ppermute | solution.py:406
  13.1 18.2 %copy-start = (f32[48,32,32]{0,2,1:T(8,128)S(1)}, f32[48,32,32]{0,2,1:T(8,128)}, u32[]{:S(2)}) copy-start(f32[48,32,32]{0,2,1:T(8,128)} %param.9) | copy-start | bytes 589828
  13.2 8.0 %collective-permute-start.7 = (f32[192,128]{1,0:T(8,128)S(1)}, f32[192,128]{1,0:T(8,128)S(1)}, u32[]{:S(2)}, u32[]{:S(2)}) collective-permute-start(f32[192,128]{1,0:T(8,128)S(1)} %get-tuple-element.20), channel_id=1, source_target_pairs={{0,6},{1,7},{2,4},{3,5},{4,2},{5,3},{6,0},{7,1},{8,14},{9,15},{10,... | collective-permute-start | bytes 294920 | tf_op jit(solution)/shard_map/ppermute | solution.py:406
  17.1 6.5 %collective-permute-start.6 = (f32[192,128]{1,0:T(8,128)S(1)}, f32[192,128]{1,0:T(8,128)S(1)}, u32[]{:S(2)}, u32[]{:S(2)}) collective-permute-start(f32[192,128]{1,0:T(8,128)S(1)} %get-tuple-element.21), channel_id=1, source_target_pairs={{0,2},{1,3},{2,0},{3,1},{4,6},{5,7},{6,4},{7,5},{8,10},{9,11},{10,... | collective-permute-start | bytes 294920 | tf_op jit(solution)/shard_map/ppermute | solution.py:406
  17.6 6.0 %collective-permute-start.5 = (f32[192,128]{1,0:T(8,128)S(1)}, f32[192,128]{1,0:T(8,128)S(1)}, u32[]{:S(2)}, u32[]{:S(2)}) collective-permute-start(f32[192,128]{1,0:T(8,128)S(1)} %get-tuple-element.22), channel_id=1, source_target_pairs={{0,4},{1,5},{2,6},{3,7},{4,0},{5,1},{6,2},{7,3},{8,12},{9,13},{10,... | collective-permute-start | bytes 294920 | tf_op jit(solution)/shard_map/ppermute | solution.py:406
  17.8 8.3 %collective-permute-start.3 = (f32[192,128]{1,0:T(8,128)S(1)}, f32[192,128]{1,0:T(8,128)S(1)}, u32[]{:S(2)}, u32[]{:S(2)}) collective-permute-start(f32[192,128]{1,0:T(8,128)S(1)} %get-tuple-element.17), channel_id=1, source_target_pairs={{0,6},{1,7},{2,4},{3,5},{4,2},{5,3},{6,0},{7,1},{8,14},{9,15},{10,... | collective-permute-start | bytes 294920 | tf_op jit(solution)/shard_map/ppermute | solution.py:406
  20.7 6.1 %collective-permute-start.2 = (f32[192,128]{1,0:T(8,128)S(1)}, f32[192,128]{1,0:T(8,128)S(1)}, u32[]{:S(2)}, u32[]{:S(2)}) collective-permute-start(f32[192,128]{1,0:T(8,128)S(1)} %get-tuple-element.18), channel_id=1, source_target_pairs={{0,4},{1,5},{2,6},{3,7},{4,0},{5,1},{6,2},{7,3},{8,12},{9,13},{10,... | collective-permute-start | bytes 294920 | tf_op jit(solution)/shard_map/ppermute | solution.py:406
  21.2 5.6 %collective-permute-start.1 = (f32[216,128]{1,0:T(8,128)S(1)}, f32[216,128]{1,0:T(8,128)S(1)}, u32[]{:S(2)}, u32[]{:S(2)}) collective-permute-start(f32[216,128]{1,0:T(8,128)S(1)} %slice_add_fusion.mine_ref), channel_id=1, source_target_pairs={{0,2},{1,3},{2,0},{3,1},{4,6},{5,7},{6,4},{7,5},{8,10},{9,11},{10,... | collective-permute-start | bytes 331784 | tf_op jit(solution)/shard_map/ppermute | solution.py:406
  26.8 6.4 %collective-permute-start.8 = (f32[48,256]{1,0:T(8,128)S(1)}, f32[48,256]{1,0:T(8,128)S(1)}, u32[]{:S(2)}, u32[]{:S(2)}) collective-permute-start(f32[48,256]{1,0:T(8,128)S(1)} %pad_maximum_fusion.2), channel_id=1, source_target_pairs={{0,24},{1,25},{2,26},{3,27},{4,28},{5,29},{6,30},{7,31},{8,16},{9,... | collective-permute-start | bytes 147464 | tf_op jit(solution)/shard_map/ppermute | solution.py:406
  30.7 5.0 %collective-permute-start.9 = (f32[48,256]{1,0:T(8,128)S(1)}, f32[48,256]{1,0:T(8,128)S(1)}, u32[]{:S(2)}, u32[]{:S(2)}) collective-permute-start(f32[48,256]{1,0:T(8,128)S(1)} %pad_maximum_fusion.3), channel_id=1, source_target_pairs={{0,16},{1,17},{2,18},{3,19},{4,20},{5,21},{6,22},{7,23},{8,24},{9,... | collective-permute-start | bytes 147464 | tf_op jit(solution)/shard_map/ppermute | solution.py:406
  30.7 5.0 %collective-permute-start.10 = (f32[48,256]{1,0:T(8,128)S(1)}, f32[48,256]{1,0:T(8,128)S(1)}, u32[]{:S(2)}, u32[]{:S(2)}) collective-permute-start(f32[48,256]{1,0:T(8,128)S(1)} %pad_maximum_fusion.4), channel_id=1, source_target_pairs={{0,8},{1,9},{2,10},{3,11},{4,12},{5,13},{6,14},{7,15},{8,0},{9,1},... | collective-permute-start | bytes 147464 | tf_op jit(solution)/shard_map/ppermute | solution.py:406
  35.7 6.0 %collective-permute-start.13 = (f32[48,256]{1,0:T(8,128)S(1)}, f32[48,256]{1,0:T(8,128)S(1)}, u32[]{:S(2)}, u32[]{:S(2)}) collective-permute-start(f32[48,256]{1,0:T(8,128)S(1)} %fusion.1), channel_id=1, source_target_pairs={{0,24},{1,25},{2,26},{3,27},{4,28},{5,29},{6,30},{7,31},{8,16},{9,... | collective-permute-start | bytes 147464 | tf_op jit(solution)/shard_map/ppermute | solution.py:406
  37.4 5.5 %collective-permute-start.12 = (f32[48,256]{1,0:T(8,128)S(1)}, f32[48,256]{1,0:T(8,128)S(1)}, u32[]{:S(2)}, u32[]{:S(2)}) collective-permute-start(f32[48,256]{1,0:T(8,128)S(1)} %fusion.1), channel_id=1, source_target_pairs={{0,16},{1,17},{2,18},{3,19},{4,20},{5,21},{6,22},{7,23},{8,24},{9,... | collective-permute-start | bytes 147464 | tf_op jit(solution)/shard_map/ppermute | solution.py:406
  37.9 5.0 %collective-permute-start.11 = (f32[48,256]{1,0:T(8,128)S(1)}, f32[48,256]{1,0:T(8,128)S(1)}, u32[]{:S(2)}, u32[]{:S(2)}) collective-permute-start(f32[48,256]{1,0:T(8,128)S(1)} %fusion.1), channel_id=1, source_target_pairs={{0,8},{1,9},{2,10},{3,11},{4,12},{5,13},{6,14},{7,15},{8,0},{9,1},... | collective-permute-start | bytes 147464 | tf_op jit(solution)/shard_map/ppermute | solution.py:406
  42.9 5.7 %collective-permute-start.17 = (f32[4,48,128]{2,1,0:T(8,128)S(1)}, f32[4,48,128]{2,1,0:T(8,128)S(1)}, u32[]{:S(2)}, u32[]{:S(2)}) collective-permute-start(f32[4,48,128]{2,1,0:T(8,128)S(1)} %pad_maximum_fusion.rest_0_.refs_0_), channel_id=1, source_target_pairs={{0,1},{1,0},{2,3},{3,2},{4,5},{5,4},{6,7},{7,6},{8,9},{9,8},{10,11... | collective-permute-start | bytes 294920 | tf_op jit(solution)/shard_map/ppermute | solution.py:406
  43.0 6.7 %collective-permute-start.16 = (f32[4,48,128]{2,1,0:T(8,128)S(1)}, f32[4,48,128]{2,1,0:T(8,128)S(1)}, u32[]{:S(2)}, u32[]{:S(2)}) collective-permute-start(f32[4,48,128]{2,1,0:T(8,128)S(1)} %pad_maximum_fusion.rest_0_.refs_0_), channel_id=1, source_target_pairs={{0,6},{1,7},{2,4},{3,5},{4,2},{5,3},{6,0},{7,1},{8,14},{9,15},{10,... | collective-permute-start | bytes 294920 | tf_op jit(solution)/shard_map/ppermute | solution.py:406
  45.1 7.2 %collective-permute-start.15 = (f32[4,48,128]{2,1,0:T(8,128)S(1)}, f32[4,48,128]{2,1,0:T(8,128)S(1)}, u32[]{:S(2)}, u32[]{:S(2)}) collective-permute-start(f32[4,48,128]{2,1,0:T(8,128)S(1)} %pad_maximum_fusion.rest_0_.refs_0_), channel_id=1, source_target_pairs={{0,2},{1,3},{2,0},{3,1},{4,6},{5,7},{6,4},{7,5},{8,10},{9,11},{10,... | collective-permute-start | bytes 294920 | tf_op jit(solution)/shard_map/ppermute | solution.py:406
  46.2 6.1 %collective-permute-start.14 = (f32[4,48,128]{2,1,0:T(8,128)S(1)}, f32[4,48,128]{2,1,0:T(8,128)S(1)}, u32[]{:S(2)}, u32[]{:S(2)}) collective-permute-start(f32[4,48,128]{2,1,0:T(8,128)S(1)} %pad_maximum_fusion.rest_0_.refs_0_), channel_id=1, source_target_pairs={{0,4},{1,5},{2,6},{3,7},{4,0},{5,1},{6,2},{7,3},{8,12},{9,13},{10,... | collective-permute-start | bytes 294920 | tf_op jit(solution)/shard_map/ppermute | solution.py:406
  46.6 7.4 %collective-permute-start.23 = (f32[4,48,128]{2,1,0:T(8,128)S(1)}, f32[4,48,128]{2,1,0:T(8,128)S(1)}, u32[]{:S(2)}, u32[]{:S(2)}) collective-permute-start(f32[4,48,128]{2,1,0:T(8,128)S(1)} %pad_maximum_fusion.1.rest_0_.refs_4_), channel_id=1, source_target_pairs={{0,6},{1,7},{2,4},{3,5},{4,2},{5,3},{6,0},{7,1},{8,14},{9,15},{10,... | collective-permute-start | bytes 294920 | tf_op jit(solution)/shard_map/ppermute | solution.py:406
  48.6 6.8 %collective-permute-start.22 = (f32[4,48,128]{2,1,0:T(8,128)S(1)}, f32[4,48,128]{2,1,0:T(8,128)S(1)}, u32[]{:S(2)}, u32[]{:S(2)}) collective-permute-start(f32[4,48,128]{2,1,0:T(8,128)S(1)} %pad_maximum_fusion.1.rest_0_.refs_4_), channel_id=1, source_target_pairs={{0,2},{1,3},{2,0},{3,1},{4,6},{5,7},{6,4},{7,5},{8,10},{9,11},{10,... | collective-permute-start | bytes 294920 | tf_op jit(solution)/shard_map/ppermute | solution.py:406
  49.7 6.1 %collective-permute-start.21 = (f32[4,48,128]{2,1,0:T(8,128)S(1)}, f32[4,48,128]{2,1,0:T(8,128)S(1)}, u32[]{:S(2)}, u32[]{:S(2)}) collective-permute-start(f32[4,48,128]{2,1,0:T(8,128)S(1)} %pad_maximum_fusion.1.rest_0_.refs_4_), channel_id=1, source_target_pairs={{0,4},{1,5},{2,6},{3,7},{4,0},{5,1},{6,2},{7,3},{8,12},{9,13},{10,... | collective-permute-start | bytes 294920 | tf_op jit(solution)/shard_map/ppermute | solution.py:406
  52.3 3.7 %collective-permute-start.20 = (f32[4,48,128]{2,1,0:T(8,128)S(1)}, f32[4,48,128]{2,1,0:T(8,128)S(1)}, u32[]{:S(2)}, u32[]{:S(2)}) collective-permute-start(f32[4,48,128]{2,1,0:T(8,128)S(1)} %collective-permute-done.16.rest_3_), channel_id=1, source_target_pairs={{0,1},{1,0},{2,3},{3,2},{4,5},{5,4},{6,7},{7,6},{8,9},{9,8},{10,11... | collective-permute-start | bytes 294920 | tf_op jit(solution)/shard_map/ppermute | solution.py:406
  52.3 4.1 %collective-permute-start.19 = (f32[4,48,128]{2,1,0:T(8,128)S(1)}, f32[4,48,128]{2,1,0:T(8,128)S(1)}, u32[]{:S(2)}, u32[]{:S(2)}) collective-permute-start(f32[4,48,128]{2,1,0:T(8,128)S(1)} %collective-permute-done.15.rest_2_.refs_2_), channel_id=1, source_target_pairs={{0,1},{1,0},{2,3},{3,2},{4,5},{5,4},{6,7},{7,6},{8,9},{9,8},{10,11... | collective-permute-start | bytes 294920 | tf_op jit(solution)/shard_map/ppermute | solution.py:406
  54.0 2.5 %collective-permute-start.18 = (f32[4,48,128]{2,1,0:T(8,128)S(1)}, f32[4,48,128]{2,1,0:T(8,128)S(1)}, u32[]{:S(2)}, u32[]{:S(2)}) collective-permute-start(f32[4,48,128]{2,1,0:T(8,128)S(1)} %collective-permute-done.14.rest_1_), channel_id=1, source_target_pairs={{0,1},{1,0},{2,3},{3,2},{4,5},{5,4},{6,7},{7,6},{8,9},{9,8},{10,11... | collective-permute-start | bytes 294920 | tf_op jit(solution)/shard_map/ppermute | solution.py:406
  55.4 2.1 %collective-permute-start.24 = (f32[4,48,128]{2,1,0:T(8,128)S(1)}, f32[4,48,128]{2,1,0:T(8,128)S(1)}, u32[]{:S(2)}, u32[]{:S(2)}) collective-permute-start(f32[4,48,128]{2,1,0:T(8,128)S(1)} %pad_maximum_fusion.1.rest_0_.refs_4_), channel_id=1, source_target_pairs={{0,1},{1,0},{2,3},{3,2},{4,5},{5,4},{6,7},{7,6},{8,9},{9,8},{10,11... | collective-permute-start | bytes 294920 | tf_op jit(solution)/shard_map/ppermute | solution.py:406
  55.9 1.7 %collective-permute-start.27 = (f32[4,48,128]{2,1,0:T(8,128)S(1)}, f32[4,48,128]{2,1,0:T(8,128)S(1)}, u32[]{:S(2)}, u32[]{:S(2)}) collective-permute-start(f32[4,48,128]{2,1,0:T(8,128)S(1)} %collective-permute-done.23.rest_3_), channel_id=1, source_target_pairs={{0,1},{1,0},{2,3},{3,2},{4,5},{5,4},{6,7},{7,6},{8,9},{9,8},{10,11... | collective-permute-start | bytes 294920 | tf_op jit(solution)/shard_map/ppermute | solution.py:406
  56.0 1.6 %collective-permute-start.26 = (f32[4,48,128]{2,1,0:T(8,128)S(1)}, f32[4,48,128]{2,1,0:T(8,128)S(1)}, u32[]{:S(2)}, u32[]{:S(2)}) collective-permute-start(f32[4,48,128]{2,1,0:T(8,128)S(1)} %collective-permute-done.22.rest_2_.refs_6_), channel_id=1, source_target_pairs={{0,1},{1,0},{2,3},{3,2},{4,5},{5,4},{6,7},{7,6},{8,9},{9,8},{10,11... | collective-permute-start | bytes 294920 | tf_op jit(solution)/shard_map/ppermute | solution.py:406
  56.4 1.3 %collective-permute-start.25 = (f32[4,48,128]{2,1,0:T(8,128)S(1)}, f32[4,48,128]{2,1,0:T(8,128)S(1)}, u32[]{:S(2)}, u32[]{:S(2)}) collective-permute-start(f32[4,48,128]{2,1,0:T(8,128)S(1)} %collective-permute-done.21.rest_1_), channel_id=1, source_target_pairs={{0,1},{1,0},{2,3},{3,2},{4,5},{5,4},{6,7},{7,6},{8,9},{9,8},{10,11... | collective-permute-start | bytes 294920 | tf_op jit(solution)/shard_map/ppermute | solution.py:406
  59.1 3.9 %collective-permute-start.28 = (f32[48,96]{1,0:T(8,128)S(1)}, f32[48,96]{1,0:T(8,128)S(1)}, u32[]{:S(2)}, u32[]{:S(2)}) collective-permute-start(f32[48,96]{1,0:T(8,128)S(1)} %shard_map.71), channel_id=1, source_target_pairs={{0,4},{1,5},{2,6},{3,7},{4,0},{5,1},{6,2},{7,3},{8,12},{9,13},{10,... | collective-permute-start | bytes 55304 | tf_op jit(solution)/shard_map/ppermute | solution.py:406
  63.0 6.3 %collective-permute-start.31 = (f32[2,48,96]{2,1,0:T(8,128)S(1)}, f32[2,48,96]{2,1,0:T(8,128)S(1)}, u32[]{:S(2)}, u32[]{:S(2)}) collective-permute-start(f32[2,48,96]{2,1,0:T(8,128)S(1)} %pad_maximum_fusion.5.refs_0_), channel_id=1, source_target_pairs={{0,24},{1,25},{2,26},{3,27},{4,28},{5,29},{6,30},{7,31},{8,16},{9,... | collective-permute-start | bytes 110600 | tf_op jit(solution)/shard_map/ppermute | solution.py:406
  65.1 5.4 %collective-permute-start.30 = (f32[2,48,96]{2,1,0:T(8,128)S(1)}, f32[2,48,96]{2,1,0:T(8,128)S(1)}, u32[]{:S(2)}, u32[]{:S(2)}) collective-permute-start(f32[2,48,96]{2,1,0:T(8,128)S(1)} %pad_maximum_fusion.5.refs_0_), channel_id=1, source_target_pairs={{0,16},{1,17},{2,18},{3,19},{4,20},{5,21},{6,22},{7,23},{8,24},{9,... | collective-permute-start | bytes 110600 | tf_op jit(solution)/shard_map/ppermute | solution.py:406
  65.7 4.8 %collective-permute-start.29 = (f32[2,48,96]{2,1,0:T(8,128)S(1)}, f32[2,48,96]{2,1,0:T(8,128)S(1)}, u32[]{:S(2)}, u32[]{:S(2)}) collective-permute-start(f32[2,48,96]{2,1,0:T(8,128)S(1)} %pad_maximum_fusion.5.refs_0_), channel_id=1, source_target_pairs={{0,8},{1,9},{2,10},{3,11},{4,12},{5,13},{6,14},{7,15},{8,0},{9,1},... | collective-permute-start | bytes 110600 | tf_op jit(solution)/shard_map/ppermute | solution.py:406

commit v12 on v10

--- a/solution.py
+++ b/solution.py
@@ -167,7 +167,7 @@
     xl_ref[:, planes_here, :] = low
 
 
-def blur_kernel(cube_hbm, taps_x_hbm, taps_y_hbm, w_hbm, xh_ref, xl_ref, w_here_ref, keep_0, give_0, keep_1, give_1,
+def blur_kernel(cube_hbm, taps_x_hbm, taps_y_hbm, w_hbm, xh_ref, xl_ref, w_here_ref, w_both_ref, keep_ref, give_ref,
                 cube_ref, taps_x_ref, taps_y_ref, w_ref, sems, chunk_sems, work_ref, kx_ref, ky_ref):
     taps = taps_x_ref.shape[0]
     margin = (taps - 1) // 2
@@ -209,54 +209,75 @@
 
     lax.fori_loop(0, groups, body, 0)
     gram = fold(band_gram(w_ref[...])[:, :rank])
-    keep_0[PIECES * rank:] = gram
-    give_0[PIECES * rank:] = gram
+    keep_ref[PIECES * rank:] = gram
+    give_ref[PIECES * rank:] = gram
     planes = xh_ref.shape[1]
     band = w_ref.shape[1]
-    me_sp = lax.axis_index("sp")
-    me_bd = lax.axis_index("bd")
-    tall = height // lax.axis_size("bd")
-    wide = 2 * LANES // lax.axis_size("sp")
-    shift = lax.rem(band - me_sp * planes, band)
+    shift = lax.rem(band - lax.axis_index("sp") * planes, band)
     w_here = pltpu.roll(w_ref[...], shift, 1)[:, :2 * LANES]
     w_here_ref[...] = w_here[:, :planes]
     lane = lax.broadcasted_iota(jnp.int32, w_here.shape, 1)
     w_here = jnp.where(lane < planes, w_here, 0.0)
     w_high = w_here.astype(BF16).astype(F32)
-    w_both = jnp.concatenate([w_high + pltpu.roll(w_high, planes, 1), w_here - w_high], axis=0)
-    w_both = w_both.astype(BF16)[:, :2 * planes]
-    for chain in range(2):
-        for rel_bd in (1, 3, 0, 2):
-            first_row = lax.bitwise_xor(me_bd, rel_bd) * tall + 4 * chain
-            sums = []
-            for row in range(4):
-                image = jnp.concatenate([xh_ref[first_row + row], xl_ref[first_row + row]], axis=0)
-                both = dot(w_both, image)
-                sums.append(both[:rank] + both[rank:])
-            refs = ((keep_0, give_0), (keep_1, give_1))[chain]
-            for column in range(2):
-                pieces = exchange_blocks(
-                    [value[:, column * LANES:(column + 1) * LANES] for value in sums], wide)
-                for k in range(4):
-                    rel_sp = lax.bitwise_xor(me_sp, column * 4 + k)
-                    side = 3 - rel_sp % 2 if rel_bd // 2 else rel_sp % 2
-                    first = pl.multiple_of((side * 4 + rel_sp // 2) * rank, 8)
-                    refs[rel_bd % 2][pl.ds(first, rank)] = pieces[k]
+    w_both = jnp.concatenate([w_high + pltpu.roll(w_high, planes, 1), w_here - w_high], axis=0).astype(BF16)
+    w_both_ref[...] = w_both
+    project(xh_ref, xl_ref, w_both[:, :2 * planes], keep_ref, give_ref, 0)
+
+
+def project(xh_ref, xl_ref, w_both, keep_ref, give_ref, chain):
+    height = xh_ref.shape[0]
+    rank = w_both.shape[0] // 2
+    me_sp = lax.axis_index("sp")
+    me_bd = lax.axis_index("bd")
+    tall = height // lax.axis_size("bd")
+    wide = 2 * LANES // lax.axis_size("sp")
+    for rel_bd in (1, 3, 0, 2):
+        first_row = lax.bitwise_xor(me_bd, rel_bd) * tall + 4 * chain
+        sums = []
+        for row in range(4):
+            image = jnp.concatenate([xh_ref[first_row + row], xl_ref[first_row + row]], axis=0)
+            both = dot(w_both, image)
+            sums.append(both[:rank] + both[rank:])
+        part_ref = (keep_ref, give_ref)[rel_bd % 2]
+        for column in range(2):
+            pieces = exchange_blocks(
+                [value[:, column * LANES:(column + 1) * LANES] for value in sums], wide)
+            for k in range(4):
+                rel_sp = lax.bitwise_xor(me_sp, column * 4 + k)
+                side = 3 - rel_sp % 2 if rel_bd // 2 else rel_sp % 2
+                first = pl.multiple_of((side * 4 + rel_sp // 2) * rank, 8)
+                part_ref[pl.ds(first, rank)] = pieces[k]
+
+
+def project_kernel(xh_ref, xl_ref, w_both_ref, keep_ref, give_ref):
+    planes = xh_ref.shape[1]
+    project(xh_ref, xl_ref, w_both_ref[:, :2 * planes], keep_ref, give_ref, 1)
+
+
+def project_call(x_high, x_low, w_both):
+    part = jax.ShapeDtypeStruct((PIECES * w_both.shape[0] // 2, LANES), F32)
+    return pl.pallas_call(
+        project_kernel,
+        out_shape=[part, part],
+        in_specs=in_vmem(3),
+        out_specs=in_vmem(2),
+        compiler_params=pltpu.CompilerParams(vmem_limit_bytes=VMEM_LIMIT),
+    )(x_high, x_low, w_both)
 
 
 def blur_call(cube, taps_x, taps_y, w_rows):
     planes, height, length = cube.shape
     rank = w_rows.shape[0]
     first = jax.ShapeDtypeStruct((PIECES * rank + FOLDED, LANES), F32)
-    second = jax.ShapeDtypeStruct((PIECES * rank, LANES), F32)
     image = (height, planes, length)
     mine = jax.ShapeDtypeStruct((rank, planes), F32)
+    both = jax.ShapeDtypeStruct((2 * rank, 2 * LANES), BF16)
     in_hbm = [pltpu.with_memory_space_constraint(value, pltpu.HBM) for value in (cube, taps_x, taps_y, w_rows)]
     return pl.pallas_call(
         blur_kernel,
-        out_shape=[jax.ShapeDtypeStruct(image, BF16)] * 2 + [mine, first, first, second, second],
+        out_shape=[jax.ShapeDtypeStruct(image, BF16)] * 2 + [mine, both, first, first],
         in_specs=[pl.BlockSpec(memory_space=pltpu.HBM)] * 4,
-        out_specs=in_vmem(7),
+        out_specs=in_vmem(6),
         scratch_shapes=[pltpu.VMEM(value.shape, F32) for value in (cube, taps_x, taps_y, w_rows)]
         + [pltpu.SemaphoreType.DMA((3,)), pltpu.SemaphoreType.DMA((planes // GROUP,))]
         + [pltpu.VMEM((LANES, LANES), F32)] * 3,
@@ -416,16 +437,28 @@
     return [send(values[k], k % 2, 2 * (k // 2)) for k in range(1, 4)]
 
 
+def spread(value, chain):
+    if chain == 0:
+        column, row = send(value, 1, 0), send(value, 0, 2)
+        corner = send(row, 1, 0)
+    else:
+        row, column = send(value, 0, 2), send(value, 1, 0)
+        corner = send(column, 0, 2)
+    return [value, column, row, corner]
+
+
 def local(cube, taps_x, taps_y, factor_w, factor_h):
     w_rows = jnp.transpose(factor_w[0])
     taps_x = jnp.transpose(taps_x, (2, 0, 1))
     taps_y = jnp.transpose(taps_y, (2, 0, 1))
     h_columns = jnp.transpose(factor_h, (1, 2, 0))
     rank = w_rows.shape[0]
-    x_high, x_low, w_here, keep_0, give_0, keep_1, give_1 = blur_call(cube[0], taps_x, taps_y, w_rows)
+    x_high, x_low, w_here, w_both, keep_0, give_0 = blur_call(cube[0], taps_x, taps_y, w_rows)
     chains = []
-    for keep, give in ((keep_0, give_0), (keep_1, give_1)):
-        taken = send(give, 0, 1)
+    taken_0 = send(give_0, 0, 1)
+    keep_1, give_1 = project_call(x_high, x_low, w_both)
+    taken_0, keep_1, give_1 = lax.optimization_barrier((taken_0, keep_1, give_1))
+    for keep, taken in ((keep_0, taken_0), (keep_1, send(give_1, 0, 1))):
         bounds = [place * 4 * rank for place in (0, 1, 3, 2)]
         sides = []
         for first in bounds:
@@ -445,7 +478,7 @@
     chains = []
     for first in (0, LANES):
         mine = jnp.stack([value[:, first:first + LANES] for value in h_line])
-        chains.append([mine] + around([mine] * 4))
+        chains.append(spread(mine, len(chains)))
     first_parts = chains[0] + [send(value, 0, 1) for value in chains[0]]
     total = first_call(x_high, x_low, first_parts)
     second_parts = chains[1] + [send(value, 0, 1) for value in chains[1]]

time: 71.1 us -> 71.9 us (1.011)
  waiting for transfers between devices: 20.9 us -> 24.5 us
  starting transfers between devices: 34.2 us -> 31.3 us
    ppermute x32, waiting for transfers between devices: 20.9 us -> 24.5 us  [send(): return lax.ppermute(value, ('sp', 'bd'), pairs)]
    ppermute x32, starting transfers between devices: 34.2 us -> 31.3 us  [send(): return lax.ppermute(value, ('sp', 'bd'), pairs)]
  transfers between devices with their start and end apart: 32 -> 32, of which waited for: 17 -> 17; matrix products, arithmetic and copies ran while one was open for 0% -> 0% of each run, Pallas kernels for 3% -> 4%
where the time goes in v12:
time: 71.9 us; the launch traced here: 71.8 us
  starting transfers between devices  31.3 us (44%)
  waiting for transfers between devices  24.5 us (34%)
  Pallas kernels  15 us (21%)
  between operations  0.8 us (1%)
    ppermute x32, starting transfers between devices, send(): return lax.ppermute(value, ('sp', 'bd'), pairs)  31.3 us
    ppermute x32, waiting for transfers between devices, send(): return lax.ppermute(value, ('sp', 'bd'), pairs)  24.5 us
    pallas_call x1, Pallas kernels, blur_call(): pl.pallas_call(blur_kernel, out_shape=[jax.ShapeDtypeStruct(image, BF16)]...  9.78 us
  transfers between devices with their start and end apart: 32, of which 17 were waited for; matrix products, arithmetic and copies ran while one was open for 0% of the time, Pallas kernels for 4%

profile of v12, /device:TPU:0, one launch (start us, length us, event | category | flops | bytes accessed | tf_op | source)
XLA Modules:
  0.0 71.8 jit_solution(13095374777178016561)
XLA Ops:
  0.6 9.8 %shard_map.68 = (bf16[32,96,256]{2,1,0:T(8,128)(2,1)S(1)}, bf16[32,96,256]{2,1,0:T(8,128)(2,1)S(1)}, f32[48,96]{1,0:T(8,128)S(1)}, bf16[96,256]{1,0:T(8,128)(2,1...) custom-call(f32[96,32,256]{2,1,0:T(8,128)} %bitcast.31, f32[25,1,96]{2,1,0:T(1,128)} %bitcast.36, ...), custom_call_target="tpu_custom_call" | custom-call | tf_op jit(solution)/shard_map/pallas_call | solution.py:276
  10.4 0.5 collective-permute-start
  10.9 0.7 shard_map.69
  11.6 0.7 collective-permute-done
  12.3 0.4 collective-permute-start.4
  12.7 0.0 copy-start
  12.7 3.7 %collective-permute-start.3 = (f32[192,128]{1,0:T(8,128)S(1)}, f32[192,128]{1,0:T(8,128)S(1)}, u32[]{:S(2)}, u32[]{:S(2)}) collective-permute-start(f32[192,128]{1,0:T(8,128)S(1)} %get-tuple-element.25), channel_id=1, source_target_pairs={{0,6},{1,7},{2,4},{3,5},{4,2},{5,3},{6,0},{7,1},{8,14},{9,15},{10,... | collective-permute-start | bytes 294920 | tf_op jit(solution)/shard_map/ppermute | solution.py:433
  16.4 0.5 collective-permute-start.2
  16.9 0.2 collective-permute-start.1
  17.1 0.1 slice_add_fusion.4
  17.2 2.9 %collective-permute-start.7 = (f32[192,128]{1,0:T(8,128)S(1)}, f32[192,128]{1,0:T(8,128)S(1)}, u32[]{:S(2)}, u32[]{:S(2)}) collective-permute-start(f32[192,128]{1,0:T(8,128)S(1)} %get-tuple-element.28), channel_id=1, source_target_pairs={{0,6},{1,7},{2,4},{3,5},{4,2},{5,3},{6,0},{7,1},{8,14},{9,15},{10,... | collective-permute-start | bytes 294920 | tf_op jit(solution)/shard_map/ppermute | solution.py:433
  20.1 0.5 collective-permute-start.6
  20.6 1.4 %collective-permute-start.5 = (f32[192,128]{1,0:T(8,128)S(1)}, f32[192,128]{1,0:T(8,128)S(1)}, u32[]{:S(2)}, u32[]{:S(2)}) collective-permute-start(f32[192,128]{1,0:T(8,128)S(1)} %get-tuple-element.30), channel_id=1, source_target_pairs={{0,4},{1,5},{2,6},{3,7},{4,0},{5,1},{6,2},{7,3},{8,12},{9,13},{10,... | collective-permute-start | bytes 294920 | tf_op jit(solution)/shard_map/ppermute | solution.py:433
  21.9 0.7 collective-permute-done.2
  22.6 1.9 %collective-permute-done.1.other_ref = f32[216,128]{1,0:T(8,128)S(1)} collective-permute-done((f32[216,128]{1,0:T(8,128)S(1)}, f32[216,128]{1,0:T(8,128)S(1)}, u32[]{:S(2)}, u32[]{:S(2)}) %collective-permute-start.1) | collective-permute-done | bytes 110624 | tf_op jit(solution)/shard_map/ppermute | solution.py:433
  24.5 0.0 collective-permute-done.7
  24.5 1.7 %collective-permute-done.6 = f32[192,128]{1,0:T(8,128)S(1)} collective-permute-done((f32[192,128]{1,0:T(8,128)S(1)}, f32[192,128]{1,0:T(8,128)S(1)}, u32[]{:S(2)}, u32[]{:S(2)}) %collective-permute-start.6) | collective-permute-done | bytes 98336 | tf_op jit(solution)/shard_map/ppermute | solution.py:433
  26.3 0.0 collective-permute-done.5
  26.4 3.9 %collective-permute-start.8 = (f32[48,256]{1,0:T(8,128)S(1)}, f32[48,256]{1,0:T(8,128)S(1)}, u32[]{:S(2)}, u32[]{:S(2)}) collective-permute-start(f32[48,256]{1,0:T(8,128)S(1)} %pad_maximum_fusion.2), channel_id=1, source_target_pairs={{0,24},{1,25},{2,26},{3,27},{4,28},{5,29},{6,30},{7,31},{8,16},{9,... | collective-permute-start | bytes 147464 | tf_op jit(solution)/shard_map/ppermute | solution.py:433
  30.2 0.6 collective-permute-start.10
  30.9 0.3 shard_map.70
  31.2 1.5 %collective-permute-done.8 = f32[48,256]{1,0:T(8,128)S(1)} collective-permute-done((f32[48,256]{1,0:T(8,128)S(1)}, f32[48,256]{1,0:T(8,128)S(1)}, u32[]{:S(2)}, u32[]{:S(2)}) %collective-permute-start.8) | collective-permute-done | bytes 49184 | tf_op jit(solution)/shard_map/ppermute | solution.py:433
  32.7 2.6 %collective-permute-done.9 = f32[48,256]{1,0:T(8,128)S(1)} collective-permute-done((f32[48,256]{1,0:T(8,128)S(1)}, f32[48,256]{1,0:T(8,128)S(1)}, u32[]{:S(2)}, u32[]{:S(2)}) %collective-permute-start.9) | collective-permute-done | bytes 49184 | tf_op jit(solution)/shard_map/ppermute | solution.py:433
  35.2 1.9 %collective-permute-start.13 = (f32[48,256]{1,0:T(8,128)S(1)}, f32[48,256]{1,0:T(8,128)S(1)}, u32[]{:S(2)}, u32[]{:S(2)}) collective-permute-start(f32[48,256]{1,0:T(8,128)S(1)} %fusion.1), channel_id=1, source_target_pairs={{0,24},{1,25},{2,26},{3,27},{4,28},{5,29},{6,30},{7,31},{8,16},{9,... | collective-permute-start | bytes 147464 | tf_op jit(solution)/shard_map/ppermute | solution.py:433
  37.1 0.3 collective-permute-start.12
  37.4 2.3 %collective-permute-start.11 = (f32[48,256]{1,0:T(8,128)S(1)}, f32[48,256]{1,0:T(8,128)S(1)}, u32[]{:S(2)}, u32[]{:S(2)}) collective-permute-start(f32[48,256]{1,0:T(8,128)S(1)} %fusion.1), channel_id=1, source_target_pairs={{0,8},{1,9},{2,10},{3,11},{4,12},{5,13},{6,14},{7,15},{8,0},{9,1},... | collective-permute-start | bytes 147464 | tf_op jit(solution)/shard_map/ppermute | solution.py:433
  39.7 1.5 %collective-permute-done.13 = f32[48,256]{1,0:T(8,128)S(1)} collective-permute-done((f32[48,256]{1,0:T(8,128)S(1)}, f32[48,256]{1,0:T(8,128)S(1)}, u32[]{:S(2)}, u32[]{:S(2)}) %collective-permute-start.13) | collective-permute-done | bytes 49184 | tf_op jit(solution)/shard_map/ppermute | solution.py:433
  41.2 1.4 %collective-permute-done.12 = f32[48,256]{1,0:T(8,128)S(1)} collective-permute-done((f32[48,256]{1,0:T(8,128)S(1)}, f32[48,256]{1,0:T(8,128)S(1)}, u32[]{:S(2)}, u32[]{:S(2)}) %collective-permute-start.12) | collective-permute-done | bytes 49184 | tf_op jit(solution)/shard_map/ppermute | solution.py:433
  42.7 0.0 collective-permute-done.11
  42.7 0.1 collective-permute-start.17
  42.8 1.8 %collective-permute-start.15 = (f32[4,48,128]{2,1,0:T(8,128)S(1)}, f32[4,48,128]{2,1,0:T(8,128)S(1)}, u32[]{:S(2)}, u32[]{:S(2)}) collective-permute-start(f32[4,48,128]{2,1,0:T(8,128)S(1)} %pad_maximum_fusion.rest_0_.refs_0_), channel_id=1, source_target_pairs={{0,2},{1,3},{2,0},{3,1},{4,6},{5,7},{6,4},{7,5},{8,10},{9,11},{10,... | collective-permute-start | bytes 294920 | tf_op jit(solution)/shard_map/ppermute | solution.py:433
  44.5 1.5 %collective-permute-start.14 = (f32[4,48,128]{2,1,0:T(8,128)S(1)}, f32[4,48,128]{2,1,0:T(8,128)S(1)}, u32[]{:S(2)}, u32[]{:S(2)}) collective-permute-start(f32[4,48,128]{2,1,0:T(8,128)S(1)} %pad_maximum_fusion.rest_0_.refs_0_), channel_id=1, source_target_pairs={{0,4},{1,5},{2,6},{3,7},{4,0},{5,1},{6,2},{7,3},{8,12},{9,13},{10,... | collective-permute-start | bytes 294920 | tf_op jit(solution)/shard_map/ppermute | solution.py:433
  46.0 0.6 collective-permute-start.21
  46.6 0.3 collective-permute-start.22
  47.0 1.0 %collective-permute-done.15.rest_2_.refs_2_ = f32[4,48,128]{2,1,0:T(8,128)S(1)} collective-permute-done((f32[4,48,128]{2,1,0:T(8,128)S(1)}, f32[4,48,128]{2,1,0:T(8,128)S(1)}, u32[]{:S(2)}, u32[]{:S(2)}) %collective-permute-start.15) | collective-permute-done | bytes 98336 | tf_op jit(solution)/shard_map/ppermute | solution.py:433
  48.0 1.4 %collective-permute-start.16 = (f32[4,48,128]{2,1,0:T(8,128)S(1)}, f32[4,48,128]{2,1,0:T(8,128)S(1)}, u32[]{:S(2)}, u32[]{:S(2)}) collective-permute-start(f32[4,48,128]{2,1,0:T(8,128)S(1)} %collective-permute-done.15.rest_2_.refs_2_), channel_id=1, source_target_pairs={{0,4},{1,5},{2,6},{3,7},{4,0},{5,1},{6,2},{7,3},{8,12},{9,13},{10,... | collective-permute-start | bytes 294920 | tf_op jit(solution)/shard_map/ppermute | solution.py:433
  49.4 0.0 collective-permute-done.17.rest_4_.refs_1_
  49.4 0.0 collective-permute-start.19
  49.4 0.8 %collective-permute-done.14.rest_1_ = f32[4,48,128]{2,1,0:T(8,128)S(1)} collective-permute-done((f32[4,48,128]{2,1,0:T(8,128)S(1)}, f32[4,48,128]{2,1,0:T(8,128)S(1)}, u32[]{:S(2)}, u32[]{:S(2)}) %collective-permute-start.14) | collective-permute-done | bytes 98336 | tf_op jit(solution)/shard_map/ppermute | solution.py:433
  50.2 2.1 %collective-permute-done.21.rest_1_ = f32[4,48,128]{2,1,0:T(8,128)S(1)} collective-permute-done((f32[4,48,128]{2,1,0:T(8,128)S(1)}, f32[4,48,128]{2,1,0:T(8,128)S(1)}, u32[]{:S(2)}, u32[]{:S(2)}) %collective-permute-start.21) | collective-permute-done | bytes 98336 | tf_op jit(solution)/shard_map/ppermute | solution.py:433
  52.3 0.0 collective-permute-done.22.rest_2_.refs_6_
  52.3 0.0 collective-permute-start.24
  52.3 1.3 %collective-permute-done.16.rest_3_ = f32[4,48,128]{2,1,0:T(8,128)S(1)} collective-permute-done((f32[4,48,128]{2,1,0:T(8,128)S(1)}, f32[4,48,128]{2,1,0:T(8,128)S(1)}, u32[]{:S(2)}, u32[]{:S(2)}) %collective-permute-start.16) | collective-permute-done | bytes 98336 | tf_op jit(solution)/shard_map/ppermute | solution.py:433
  53.6 0.0 collective-permute-start.20
  53.6 0.0 collective-permute-done.19.rest_6_.refs_3_
  53.6 0.5 collective-permute-start.25
  54.1 0.0 collective-permute-done.18.rest_5_
  54.1 0.1 collective-permute-start.26
  54.2 2.7 %collective-permute-done.23.rest_3_ = f32[4,48,128]{2,1,0:T(8,128)S(1)} collective-permute-done((f32[4,48,128]{2,1,0:T(8,128)S(1)}, f32[4,48,128]{2,1,0:T(8,128)S(1)}, u32[]{:S(2)}, u32[]{:S(2)}) %collective-permute-start.23) | collective-permute-done | bytes 98336 | tf_op jit(solution)/shard_map/ppermute | solution.py:433
  56.9 0.0 collective-permute-start.27
  56.9 1.0 %shard_map.71.total_ref = f32[288,96]{1,0:T(8,128)S(1)} custom-call(bf16[32,96,256]{2,1,0:T(8,128)(2,1)S(1)} %get-tuple-element.13.xh_ref, bf16[32,96,256]{2,1,0:T(8,128)(2,1)S(1)} %get-tuple-element.14.xl_ref, f32[4,48,128]{2,1,0:T(8,128)S(1)} %pad_maximum_fusion.rest_0_.refs_0_, f32[4,48,128]{2,1,0:T(8,128)S(1)} %collective-permute-done.14.rest_1_, ...), custom_call_target="tpu_custom_call" | custom-call | tf_op jit(solution)/shard_map/pallas_call | solution.py:345
  58.0 0.0 collective-permute-done.26.rest_6_.refs_7_
  58.0 0.0 collective-permute-done.25.rest_5_
  58.0 0.2 collective-permute-done.27.rest_7_
  58.2 1.4 %shard_map.72 = f32[48,96]{1,0:T(8,128)S(1)} custom-call(bf16[32,96,256]{2,1,0:T(8,128)(2,1)S(1)} %get-tuple-element.13.xh_ref, bf16[32,96,256]{2,1,0:T(8,128)(2,1)S(1)} %get-tuple-element.14.xl_ref, f32[48,96]{1,0:T(8,128)S(1)} %get-tuple-element.15.w_ref, f32[288,96]{1,0:T(8,128)S(1)} %shard_map.71.total_ref, ...), custom_call_target="tpu_custom_call" | custom-call | tf_op jit(solution)/shard_map/pallas_call | solution.py:369
  59.6 1.6 %collective-permute-start.28 = (f32[48,96]{1,0:T(8,128)S(1)}, f32[48,96]{1,0:T(8,128)S(1)}, u32[]{:S(2)}, u32[]{:S(2)}) collective-permute-start(f32[48,96]{1,0:T(8,128)S(1)} %shard_map.72), channel_id=1, source_target_pairs={{0,4},{1,5},{2,6},{3,7},{4,0},{5,1},{6,2},{7,3},{8,12},{9,13},{10,... | collective-permute-start | bytes 55304 | tf_op jit(solution)/shard_map/ppermute | solution.py:433
  61.2 2.3 %collective-permute-done.28 = f32[48,96]{1,0:T(8,128)S(1)} collective-permute-done((f32[48,96]{1,0:T(8,128)S(1)}, f32[48,96]{1,0:T(8,128)S(1)}, u32[]{:S(2)}, u32[]{:S(2)}) %collective-permute-start.28) | collective-permute-done | bytes 18464 | tf_op jit(solution)/shard_map/ppermute | solution.py:433
  63.5 2.0 %collective-permute-start.31 = (f32[2,48,96]{2,1,0:T(8,128)S(1)}, f32[2,48,96]{2,1,0:T(8,128)S(1)}, u32[]{:S(2)}, u32[]{:S(2)}) collective-permute-start(f32[2,48,96]{2,1,0:T(8,128)S(1)} %pad_maximum_fusion.5.refs_0_), channel_id=1, source_target_pairs={{0,24},{1,25},{2,26},{3,27},{4,28},{5,29},{6,30},{7,31},{8,16},{9,... | collective-permute-start | bytes 110600 | tf_op jit(solution)/shard_map/ppermute | solution.py:433
  65.5 0.4 collective-permute-start.30
  66.0 2.0 %collective-permute-start.29 = (f32[2,48,96]{2,1,0:T(8,128)S(1)}, f32[2,48,96]{2,1,0:T(8,128)S(1)}, u32[]{:S(2)}, u32[]{:S(2)}) collective-permute-start(f32[2,48,96]{2,1,0:T(8,128)S(1)} %pad_maximum_fusion.5.refs_0_), channel_id=1, source_target_pairs={{0,8},{1,9},{2,10},{3,11},{4,12},{5,13},{6,14},{7,15},{8,0},{9,1},... | collective-permute-start | bytes 110600 | tf_op jit(solution)/shard_map/ppermute | solution.py:433
  68.0 1.0 %shard_map.74 = f32[32,32,48]{2,1,0:T(8,128)} custom-call(f32[4,48,128]{2,1,0:T(8,128)S(1)} %pad_maximum_fusion.rest_0_.refs_0_, f32[4,48,128]{2,1,0:T(8,128)S(1)} %collective-permute-done.17.rest_4_.refs_1_, f32[4,48,128]{2,1,0:T(8,128)S(1)} %collective-permute-done.15.rest_2_.refs_2_, f32[4,48,128]{2,1,0:T(8,128)S(1)} %collective-permute-done.19.rest_6_.refs_3_, ...), custom_call_target="tpu_custom_call" | custom-call | tf_op jit(solution)/shard_map/pallas_call | solution.py:390
  69.0 0.9 %collective-permute-done.31.refs_3_ = f32[2,48,96]{2,1,0:T(8,128)S(1)} collective-permute-done((f32[2,48,96]{2,1,0:T(8,128)S(1)}, f32[2,48,96]{2,1,0:T(8,128)S(1)}, u32[]{:S(2)}, u32[]{:S(2)}) %collective-permute-start.31) | collective-permute-done | bytes 36896 | tf_op jit(solution)/shard_map/ppermute | solution.py:433
  69.9 1.1 %collective-permute-done.30.refs_2_ = f32[2,48,96]{2,1,0:T(8,128)S(1)} collective-permute-done((f32[2,48,96]{2,1,0:T(8,128)S(1)}, f32[2,48,96]{2,1,0:T(8,128)S(1)}, u32[]{:S(2)}, u32[]{:S(2)}) %collective-permute-start.30) | collective-permute-done | bytes 36896 | tf_op jit(solution)/shard_map/ppermute | solution.py:433
  71.0 0.8 %shard_map.73 = f32[48,768]{1,0:T(8,128)} custom-call(f32[2,48,96]{2,1,0:T(8,128)S(1)} %pad_maximum_fusion.5.refs_0_, f32[2,48,96]{2,1,0:T(8,128)S(1)} %collective-permute-done.29.refs_1_, f32[2,48,96]{2,1,0:T(8,128)S(1)} %collective-permute-done.30.refs_2_, f32[2,48,96]{2,1,0:T(8,128)S(1)} %collective-permute-done.31.refs_3_), custom_call_target="tpu_custom_call" | custom-call | tf_op jit(solution)/shard_map/pallas_call | solution.py:417
  (25 shorter events, 0.2 us)
Async XLA Ops:
  10.4 1.9 %collective-permute-start = (f32[792,128]{1,0:T(8,128)S(1)}, f32[792,128]{1,0:T(8,128)S(1)}, u32[]{:S(2)}, u32[]{:S(2)}) collective-permute-start(f32[792,128]{1,0:T(8,128)S(1)} %get-tuple-element.17), channel_id=1, source_target_pairs={{0,1},{1,0},{2,3},{3,2},{4,5},{5,4},{6,7},{7,6},{8,9},{9,8},{10,11... | collective-permute-start | bytes 1216520 | tf_op jit(solution)/shard_map/ppermute | solution.py:433
  12.3 4.8 %collective-permute-start.4 = (f32[768,128]{1,0:T(8,128)S(1)}, f32[768,128]{1,0:T(8,128)S(1)}, u32[]{:S(2)}, u32[]{:S(2)}) collective-permute-start(f32[768,128]{1,0:T(8,128)S(1)} %get-tuple-element.23), channel_id=1, source_target_pairs={{0,1},{1,0},{2,3},{3,2},{4,5},{5,4},{6,7},{7,6},{8,9},{9,8},{10,11... | collective-permute-start | bytes 1179656 | tf_op jit(solution)/shard_map/ppermute | solution.py:433
  12.7 18.2 %copy-start = (f32[48,32,32]{0,2,1:T(8,128)S(1)}, f32[48,32,32]{0,2,1:T(8,128)}, u32[]{:S(2)}) copy-start(f32[48,32,32]{0,2,1:T(8,128)} %param.9) | copy-start | bytes 589828
  12.7 7.9 %collective-permute-start.3 = (f32[192,128]{1,0:T(8,128)S(1)}, f32[192,128]{1,0:T(8,128)S(1)}, u32[]{:S(2)}, u32[]{:S(2)}) collective-permute-start(f32[192,128]{1,0:T(8,128)S(1)} %get-tuple-element.25), channel_id=1, source_target_pairs={{0,6},{1,7},{2,4},{3,5},{4,2},{5,3},{6,0},{7,1},{8,14},{9,15},{10,... | collective-permute-start | bytes 294920 | tf_op jit(solution)/shard_map/ppermute | solution.py:433
  16.4 6.2 %collective-permute-start.2 = (f32[192,128]{1,0:T(8,128)S(1)}, f32[192,128]{1,0:T(8,128)S(1)}, u32[]{:S(2)}, u32[]{:S(2)}) collective-permute-start(f32[192,128]{1,0:T(8,128)S(1)} %get-tuple-element.26), channel_id=1, source_target_pairs={{0,4},{1,5},{2,6},{3,7},{4,0},{5,1},{6,2},{7,3},{8,12},{9,13},{10,... | collective-permute-start | bytes 294920 | tf_op jit(solution)/shard_map/ppermute | solution.py:433
  16.9 7.6 %collective-permute-start.1 = (f32[216,128]{1,0:T(8,128)S(1)}, f32[216,128]{1,0:T(8,128)S(1)}, u32[]{:S(2)}, u32[]{:S(2)}) collective-permute-start(f32[216,128]{1,0:T(8,128)S(1)} %slice_add_fusion.mine_ref), channel_id=1, source_target_pairs={{0,2},{1,3},{2,0},{3,1},{4,6},{5,7},{6,4},{7,5},{8,10},{9,11},{10,... | collective-permute-start | bytes 331784 | tf_op jit(solution)/shard_map/ppermute | solution.py:433
  17.2 7.4 %collective-permute-start.7 = (f32[192,128]{1,0:T(8,128)S(1)}, f32[192,128]{1,0:T(8,128)S(1)}, u32[]{:S(2)}, u32[]{:S(2)}) collective-permute-start(f32[192,128]{1,0:T(8,128)S(1)} %get-tuple-element.28), channel_id=1, source_target_pairs={{0,6},{1,7},{2,4},{3,5},{4,2},{5,3},{6,0},{7,1},{8,14},{9,15},{10,... | collective-permute-start | bytes 294920 | tf_op jit(solution)/shard_map/ppermute | solution.py:433
  20.1 6.2 %collective-permute-start.6 = (f32[192,128]{1,0:T(8,128)S(1)}, f32[192,128]{1,0:T(8,128)S(1)}, u32[]{:S(2)}, u32[]{:S(2)}) collective-permute-start(f32[192,128]{1,0:T(8,128)S(1)} %get-tuple-element.29), channel_id=1, source_target_pairs={{0,2},{1,3},{2,0},{3,1},{4,6},{5,7},{6,4},{7,5},{8,10},{9,11},{10,... | collective-permute-start | bytes 294920 | tf_op jit(solution)/shard_map/ppermute | solution.py:433
  20.6 5.7 %collective-permute-start.5 = (f32[192,128]{1,0:T(8,128)S(1)}, f32[192,128]{1,0:T(8,128)S(1)}, u32[]{:S(2)}, u32[]{:S(2)}) collective-permute-start(f32[192,128]{1,0:T(8,128)S(1)} %get-tuple-element.30), channel_id=1, source_target_pairs={{0,4},{1,5},{2,6},{3,7},{4,0},{5,1},{6,2},{7,3},{8,12},{9,13},{10,... | collective-permute-start | bytes 294920 | tf_op jit(solution)/shard_map/ppermute | solution.py:433
  26.4 6.3 %collective-permute-start.8 = (f32[48,256]{1,0:T(8,128)S(1)}, f32[48,256]{1,0:T(8,128)S(1)}, u32[]{:S(2)}, u32[]{:S(2)}) collective-permute-start(f32[48,256]{1,0:T(8,128)S(1)} %pad_maximum_fusion.2), channel_id=1, source_target_pairs={{0,24},{1,25},{2,26},{3,27},{4,28},{5,29},{6,30},{7,31},{8,16},{9,... | collective-permute-start | bytes 147464 | tf_op jit(solution)/shard_map/ppermute | solution.py:433
  30.2 5.0 %collective-permute-start.9 = (f32[48,256]{1,0:T(8,128)S(1)}, f32[48,256]{1,0:T(8,128)S(1)}, u32[]{:S(2)}, u32[]{:S(2)}) collective-permute-start(f32[48,256]{1,0:T(8,128)S(1)} %pad_maximum_fusion.3), channel_id=1, source_target_pairs={{0,16},{1,17},{2,18},{3,19},{4,20},{5,21},{6,22},{7,23},{8,24},{9,... | collective-permute-start | bytes 147464 | tf_op jit(solution)/shard_map/ppermute | solution.py:433
  30.2 5.0 %collective-permute-start.10 = (f32[48,256]{1,0:T(8,128)S(1)}, f32[48,256]{1,0:T(8,128)S(1)}, u32[]{:S(2)}, u32[]{:S(2)}) collective-permute-start(f32[48,256]{1,0:T(8,128)S(1)} %pad_maximum_fusion.4), channel_id=1, source_target_pairs={{0,8},{1,9},{2,10},{3,11},{4,12},{5,13},{6,14},{7,15},{8,0},{9,1},... | collective-permute-start | bytes 147464 | tf_op jit(solution)/shard_map/ppermute | solution.py:433
  35.2 6.0 %collective-permute-start.13 = (f32[48,256]{1,0:T(8,128)S(1)}, f32[48,256]{1,0:T(8,128)S(1)}, u32[]{:S(2)}, u32[]{:S(2)}) collective-permute-start(f32[48,256]{1,0:T(8,128)S(1)} %fusion.1), channel_id=1, source_target_pairs={{0,24},{1,25},{2,26},{3,27},{4,28},{5,29},{6,30},{7,31},{8,16},{9,... | collective-permute-start | bytes 147464 | tf_op jit(solution)/shard_map/ppermute | solution.py:433
  37.1 5.5 %collective-permute-start.12 = (f32[48,256]{1,0:T(8,128)S(1)}, f32[48,256]{1,0:T(8,128)S(1)}, u32[]{:S(2)}, u32[]{:S(2)}) collective-permute-start(f32[48,256]{1,0:T(8,128)S(1)} %fusion.1), channel_id=1, source_target_pairs={{0,16},{1,17},{2,18},{3,19},{4,20},{5,21},{6,22},{7,23},{8,24},{9,... | collective-permute-start | bytes 147464 | tf_op jit(solution)/shard_map/ppermute | solution.py:433
  37.4 5.2 %collective-permute-start.11 = (f32[48,256]{1,0:T(8,128)S(1)}, f32[48,256]{1,0:T(8,128)S(1)}, u32[]{:S(2)}, u32[]{:S(2)}) collective-permute-start(f32[48,256]{1,0:T(8,128)S(1)} %fusion.1), channel_id=1, source_target_pairs={{0,8},{1,9},{2,10},{3,11},{4,12},{5,13},{6,14},{7,15},{8,0},{9,1},... | collective-permute-start | bytes 147464 | tf_op jit(solution)/shard_map/ppermute | solution.py:433
  42.7 6.7 %collective-permute-start.17 = (f32[4,48,128]{2,1,0:T(8,128)S(1)}, f32[4,48,128]{2,1,0:T(8,128)S(1)}, u32[]{:S(2)}, u32[]{:S(2)}) collective-permute-start(f32[4,48,128]{2,1,0:T(8,128)S(1)} %pad_maximum_fusion.rest_0_.refs_0_), channel_id=1, source_target_pairs={{0,1},{1,0},{2,3},{3,2},{4,5},{5,4},{6,7},{7,6},{8,9},{9,8},{10,11... | collective-permute-start | bytes 294920 | tf_op jit(solution)/shard_map/ppermute | solution.py:433
  42.8 5.2 %collective-permute-start.15 = (f32[4,48,128]{2,1,0:T(8,128)S(1)}, f32[4,48,128]{2,1,0:T(8,128)S(1)}, u32[]{:S(2)}, u32[]{:S(2)}) collective-permute-start(f32[4,48,128]{2,1,0:T(8,128)S(1)} %pad_maximum_fusion.rest_0_.refs_0_), channel_id=1, source_target_pairs={{0,2},{1,3},{2,0},{3,1},{4,6},{5,7},{6,4},{7,5},{8,10},{9,11},{10,... | collective-permute-start | bytes 294920 | tf_op jit(solution)/shard_map/ppermute | solution.py:433
  44.5 5.6 %collective-permute-start.14 = (f32[4,48,128]{2,1,0:T(8,128)S(1)}, f32[4,48,128]{2,1,0:T(8,128)S(1)}, u32[]{:S(2)}, u32[]{:S(2)}) collective-permute-start(f32[4,48,128]{2,1,0:T(8,128)S(1)} %pad_maximum_fusion.rest_0_.refs_0_), channel_id=1, source_target_pairs={{0,4},{1,5},{2,6},{3,7},{4,0},{5,1},{6,2},{7,3},{8,12},{9,13},{10,... | collective-permute-start | bytes 294920 | tf_op jit(solution)/shard_map/ppermute | solution.py:433
  46.0 6.2 %collective-permute-start.21 = (f32[4,48,128]{2,1,0:T(8,128)S(1)}, f32[4,48,128]{2,1,0:T(8,128)S(1)}, u32[]{:S(2)}, u32[]{:S(2)}) collective-permute-start(f32[4,48,128]{2,1,0:T(8,128)S(1)} %pad_maximum_fusion.1.rest_0_.refs_4_), channel_id=1, source_target_pairs={{0,4},{1,5},{2,6},{3,7},{4,0},{5,1},{6,2},{7,3},{8,12},{9,13},{10,... | collective-permute-start | bytes 294920 | tf_op jit(solution)/shard_map/ppermute | solution.py:433
  46.6 5.7 %collective-permute-start.22 = (f32[4,48,128]{2,1,0:T(8,128)S(1)}, f32[4,48,128]{2,1,0:T(8,128)S(1)}, u32[]{:S(2)}, u32[]{:S(2)}) collective-permute-start(f32[4,48,128]{2,1,0:T(8,128)S(1)} %pad_maximum_fusion.1.rest_0_.refs_4_), channel_id=1, source_target_pairs={{0,2},{1,3},{2,0},{3,1},{4,6},{5,7},{6,4},{7,5},{8,10},{9,11},{10,... | collective-permute-start | bytes 294920 | tf_op jit(solution)/shard_map/ppermute | solution.py:433
  48.0 5.6 %collective-permute-start.16 = (f32[4,48,128]{2,1,0:T(8,128)S(1)}, f32[4,48,128]{2,1,0:T(8,128)S(1)}, u32[]{:S(2)}, u32[]{:S(2)}) collective-permute-start(f32[4,48,128]{2,1,0:T(8,128)S(1)} %collective-permute-done.15.rest_2_.refs_2_), channel_id=1, source_target_pairs={{0,4},{1,5},{2,6},{3,7},{4,0},{5,1},{6,2},{7,3},{8,12},{9,13},{10,... | collective-permute-start | bytes 294920 | tf_op jit(solution)/shard_map/ppermute | solution.py:433
  49.4 4.2 %collective-permute-start.19 = (f32[4,48,128]{2,1,0:T(8,128)S(1)}, f32[4,48,128]{2,1,0:T(8,128)S(1)}, u32[]{:S(2)}, u32[]{:S(2)}) collective-permute-start(f32[4,48,128]{2,1,0:T(8,128)S(1)} %collective-permute-done.15.rest_2_.refs_2_), channel_id=1, source_target_pairs={{0,1},{1,0},{2,3},{3,2},{4,5},{5,4},{6,7},{7,6},{8,9},{9,8},{10,11... | collective-permute-start | bytes 294920 | tf_op jit(solution)/shard_map/ppermute | solution.py:433
  50.2 4.0 %collective-permute-start.18 = (f32[4,48,128]{2,1,0:T(8,128)S(1)}, f32[4,48,128]{2,1,0:T(8,128)S(1)}, u32[]{:S(2)}, u32[]{:S(2)}) collective-permute-start(f32[4,48,128]{2,1,0:T(8,128)S(1)} %collective-permute-done.14.rest_1_), channel_id=1, source_target_pairs={{0,1},{1,0},{2,3},{3,2},{4,5},{5,4},{6,7},{7,6},{8,9},{9,8},{10,11... | collective-permute-start | bytes 294920 | tf_op jit(solution)/shard_map/ppermute | solution.py:433
  52.3 4.6 %collective-permute-start.23 = (f32[4,48,128]{2,1,0:T(8,128)S(1)}, f32[4,48,128]{2,1,0:T(8,128)S(1)}, u32[]{:S(2)}, u32[]{:S(2)}) collective-permute-start(f32[4,48,128]{2,1,0:T(8,128)S(1)} %collective-permute-done.21.rest_1_), channel_id=1, source_target_pairs={{0,2},{1,3},{2,0},{3,1},{4,6},{5,7},{6,4},{7,5},{8,10},{9,11},{10,... | collective-permute-start | bytes 294920 | tf_op jit(solution)/shard_map/ppermute | solution.py:433
  52.3 5.7 %collective-permute-start.24 = (f32[4,48,128]{2,1,0:T(8,128)S(1)}, f32[4,48,128]{2,1,0:T(8,128)S(1)}, u32[]{:S(2)}, u32[]{:S(2)}) collective-permute-start(f32[4,48,128]{2,1,0:T(8,128)S(1)} %pad_maximum_fusion.1.rest_0_.refs_4_), channel_id=1, source_target_pairs={{0,1},{1,0},{2,3},{3,2},{4,5},{5,4},{6,7},{7,6},{8,9},{9,8},{10,11... | collective-permute-start | bytes 294920 | tf_op jit(solution)/shard_map/ppermute | solution.py:433
  53.6 3.3 %collective-permute-start.20 = (f32[4,48,128]{2,1,0:T(8,128)S(1)}, f32[4,48,128]{2,1,0:T(8,128)S(1)}, u32[]{:S(2)}, u32[]{:S(2)}) collective-permute-start(f32[4,48,128]{2,1,0:T(8,128)S(1)} %collective-permute-done.16.rest_3_), channel_id=1, source_target_pairs={{0,1},{1,0},{2,3},{3,2},{4,5},{5,4},{6,7},{7,6},{8,9},{9,8},{10,11... | collective-permute-start | bytes 294920 | tf_op jit(solution)/shard_map/ppermute | solution.py:433
  53.6 4.4 %collective-permute-start.25 = (f32[4,48,128]{2,1,0:T(8,128)S(1)}, f32[4,48,128]{2,1,0:T(8,128)S(1)}, u32[]{:S(2)}, u32[]{:S(2)}) collective-permute-start(f32[4,48,128]{2,1,0:T(8,128)S(1)} %collective-permute-done.21.rest_1_), channel_id=1, source_target_pairs={{0,1},{1,0},{2,3},{3,2},{4,5},{5,4},{6,7},{7,6},{8,9},{9,8},{10,11... | collective-permute-start | bytes 294920 | tf_op jit(solution)/shard_map/ppermute | solution.py:433
  54.1 3.8 %collective-permute-start.26 = (f32[4,48,128]{2,1,0:T(8,128)S(1)}, f32[4,48,128]{2,1,0:T(8,128)S(1)}, u32[]{:S(2)}, u32[]{:S(2)}) collective-permute-start(f32[4,48,128]{2,1,0:T(8,128)S(1)} %collective-permute-done.22.rest_2_.refs_6_), channel_id=1, source_target_pairs={{0,1},{1,0},{2,3},{3,2},{4,5},{5,4},{6,7},{7,6},{8,9},{9,8},{10,11... | collective-permute-start | bytes 294920 | tf_op jit(solution)/shard_map/ppermute | solution.py:433
  56.9 1.3 %collective-permute-start.27 = (f32[4,48,128]{2,1,0:T(8,128)S(1)}, f32[4,48,128]{2,1,0:T(8,128)S(1)}, u32[]{:S(2)}, u32[]{:S(2)}) collective-permute-start(f32[4,48,128]{2,1,0:T(8,128)S(1)} %collective-permute-done.23.rest_3_), channel_id=1, source_target_pairs={{0,1},{1,0},{2,3},{3,2},{4,5},{5,4},{6,7},{7,6},{8,9},{9,8},{10,11... | collective-permute-start | bytes 294920 | tf_op jit(solution)/shard_map/ppermute | solution.py:433
  59.6 3.9 %collective-permute-start.28 = (f32[48,96]{1,0:T(8,128)S(1)}, f32[48,96]{1,0:T(8,128)S(1)}, u32[]{:S(2)}, u32[]{:S(2)}) collective-permute-start(f32[48,96]{1,0:T(8,128)S(1)} %shard_map.72), channel_id=1, source_target_pairs={{0,4},{1,5},{2,6},{3,7},{4,0},{5,1},{6,2},{7,3},{8,12},{9,13},{10,... | collective-permute-start | bytes 55304 | tf_op jit(solution)/shard_map/ppermute | solution.py:433
  63.5 6.3 %collective-permute-start.31 = (f32[2,48,96]{2,1,0:T(8,128)S(1)}, f32[2,48,96]{2,1,0:T(8,128)S(1)}, u32[]{:S(2)}, u32[]{:S(2)}) collective-permute-start(f32[2,48,96]{2,1,0:T(8,128)S(1)} %pad_maximum_fusion.5.refs_0_), channel_id=1, source_target_pairs={{0,24},{1,25},{2,26},{3,27},{4,28},{5,29},{6,30},{7,31},{8,16},{9,... | collective-permute-start | bytes 110600 | tf_op jit(solution)/shard_map/ppermute | solution.py:433
  65.5 5.5 %collective-permute-start.30 = (f32[2,48,96]{2,1,0:T(8,128)S(1)}, f32[2,48,96]{2,1,0:T(8,128)S(1)}, u32[]{:S(2)}, u32[]{:S(2)}) collective-permute-start(f32[2,48,96]{2,1,0:T(8,128)S(1)} %pad_maximum_fusion.5.refs_0_), channel_id=1, source_target_pairs={{0,16},{1,17},{2,18},{3,19},{4,20},{5,21},{6,22},{7,23},{8,24},{9,... | collective-permute-start | bytes 110600 | tf_op jit(solution)/shard_map/ppermute | solution.py:433
  66.0 5.0 %collective-permute-start.29 = (f32[2,48,96]{2,1,0:T(8,128)S(1)}, f32[2,48,96]{2,1,0:T(8,128)S(1)}, u32[]{:S(2)}, u32[]{:S(2)}) collective-permute-start(f32[2,48,96]{2,1,0:T(8,128)S(1)} %pad_maximum_fusion.5.refs_0_), channel_id=1, source_target_pairs={{0,8},{1,9},{2,10},{3,11},{4,12},{5,13},{6,14},{7,15},{8,0},{9,1},... | collective-permute-start | bytes 110600 | tf_op jit(solution)/shard_map/ppermute | solution.py:433

commit v13 on v12

--- a/solution.py
+++ b/solution.py
@@ -314,9 +314,10 @@
     tall = height // bands
     wide = 2 * LANES // pieces
     for slot, part_ref in enumerate(part_refs):
-        rel_bd = slot // 4 + 2 * ((slot // 2) % 2)
+        partner = ((0,) + PARTNERS[chain])[slot % 4]
+        rel_bd = slot // 4 + 2 * (partner // 2)
         for inner in range(4):
-            rel_sp = slot % 2 + 2 * inner
+            rel_sp = partner % 2 + 2 * inner
             owner = lax.bitwise_xor(me_bd, rel_bd) * pieces + lax.bitwise_xor(me_sp, rel_sp)
             all_ref[owner] = part_ref[inner]
     for part in range(bands):
@@ -409,6 +410,7 @@
         out_ref[:, owner * planes:(owner + 1) * planes] = all_ref[owner][:, :planes]
 
 
+PARTNERS = ((3, 1, 2), (1, 2, 3))
 RING = (0, 1, 2, 3, 4, 5, 6, 7)
 
 
@@ -435,16 +437,6 @@
 
 def around(values):
     return [send(values[k], k % 2, 2 * (k // 2)) for k in range(1, 4)]
-
-
-def spread(value, chain):
-    if chain == 0:
-        column, row = send(value, 1, 0), send(value, 0, 2)
-        corner = send(row, 1, 0)
-    else:
-        row, column = send(value, 0, 2), send(value, 1, 0)
-        corner = send(column, 0, 2)
-    return [value, column, row, corner]
 
 
 def local(cube, taps_x, taps_y, factor_w, factor_h):
@@ -469,21 +461,27 @@
     line = []
     for k in range(4):
         part = slice(k * rank, (k + 1) * rank)
-        line.append(jnp.concatenate(
-            [(sides[0][part] + others[0][part]) + (others[1][part] + others[2][part]) for sides, others in chains],
-            axis=1))
+        halves = []
+        for order, (sides, others) in zip(PARTNERS, chains):
+            one, two, three = [others[partner - 1][part] for partner in order]
+            halves.append((sides[0][part] + one) + (two + three))
+        line.append(jnp.concatenate(halves, axis=1))
     line = [line[0]] + [send(line[k], 2 * k, 0) for k in (3, 2, 1)]
     h_piece = ratio * ((line[0] + line[1]) + (line[2] + line[3]))
     h_line = [h_piece] + [send(h_piece, 2 * k, 0) for k in range(1, 4)]
     chains = []
     for first in (0, LANES):
         mine = jnp.stack([value[:, first:first + LANES] for value in h_line])
-        chains.append(spread(mine, len(chains)))
+        others = around([mine] * 4)
+        chains.append([mine] + [others[k - 1] for k in PARTNERS[len(chains)]])
     first_parts = chains[0] + [send(value, 0, 1) for value in chains[0]]
     total = first_call(x_high, x_low, first_parts)
     second_parts = chains[1] + [send(value, 0, 1) for value in chains[1]]
     w_piece = second_call(x_high, x_low, w_here, total, second_parts)
-    own = [parts[k] for parts in (first_parts, second_parts) for k in (0, 4, 2, 6)]
+    own = []
+    for order, parts in zip(PARTNERS, (first_parts, second_parts)):
+        row = 1 + order.index(2)
+        own += [parts[0], parts[4], parts[row], parts[4 + row]]
     h_next = place_h_call(own, h_columns.shape)
     w_pair = jnp.stack([w_piece, send(w_piece, 1, 0)])
     w_next = gather_w_call([w_pair] + [send(w_pair, 2 * k, 0) for k in range(1, 4)])

time: 71.9 us -> 73.1 us (1.017)
    ppermute x32, waiting for transfers between devices: 24.5 us -> 25.2 us  [send(): return lax.ppermute(value, ('sp', 'bd'), pairs)]
  transfers between devices with their start and end apart: 32 -> 32, of which waited for: 17 -> 15; matrix products, arithmetic and copies ran while one was open for 0% -> 0% of each run, Pallas kernels for 4% -> 4%
where the time goes in v13:
time: 73.1 us; the launch traced here: 72.9 us
  starting transfers between devices  31.7 us (43%)
  waiting for transfers between devices  25.2 us (34%)
  Pallas kernels  15 us (21%)
  between operations  0.8 us (1%)
    ppermute x32, starting transfers between devices, send(): return lax.ppermute(value, ('sp', 'bd'), pairs)  31.7 us
    ppermute x32, waiting for transfers between devices, send(): return lax.ppermute(value, ('sp', 'bd'), pairs)  25.2 us
    pallas_call x1, Pallas kernels, blur_call(): pl.pallas_call(blur_kernel, out_shape=[jax.ShapeDtypeStruct(image, BF16)]...  9.78 us
  transfers between devices with their start and end apart: 32, of which 15 were waited for; matrix products, arithmetic and copies ran while one was open for 0% of the time, Pallas kernels for 4%

profile of v13, /device:TPU:0, one launch (start us, length us, event | category | flops | bytes accessed | tf_op | source)
XLA Modules:
  0.0 72.9 jit_solution(18115975282600318297)
XLA Ops:
  0.6 9.8 %shard_map.68 = (bf16[32,96,256]{2,1,0:T(8,128)(2,1)S(1)}, bf16[32,96,256]{2,1,0:T(8,128)(2,1)S(1)}, f32[48,96]{1,0:T(8,128)S(1)}, bf16[96,256]{1,0:T(8,128)(2,1...) custom-call(f32[96,32,256]{2,1,0:T(8,128)} %bitcast.31, f32[25,1,96]{2,1,0:T(1,128)} %bitcast.36, ...), custom_call_target="tpu_custom_call" | custom-call | tf_op jit(solution)/shard_map/pallas_call | solution.py:276
  10.4 0.5 collective-permute-start
  10.9 0.7 shard_map.69
  11.6 0.7 collective-permute-done
  12.3 0.4 collective-permute-start.4
  12.7 0.0 copy-start
  12.7 2.7 %collective-permute-start.3 = (f32[192,128]{1,0:T(8,128)S(1)}, f32[192,128]{1,0:T(8,128)S(1)}, u32[]{:S(2)}, u32[]{:S(2)}) collective-permute-start(f32[192,128]{1,0:T(8,128)S(1)} %get-tuple-element.25), channel_id=1, source_target_pairs={{0,4},{1,5},{2,6},{3,7},{4,0},{5,1},{6,2},{7,3},{8,12},{9,13},{10,... | collective-permute-start | bytes 294920 | tf_op jit(solution)/shard_map/ppermute | solution.py:435
  15.4 1.5 %collective-permute-start.2 = (f32[192,128]{1,0:T(8,128)S(1)}, f32[192,128]{1,0:T(8,128)S(1)}, u32[]{:S(2)}, u32[]{:S(2)}) collective-permute-start(f32[192,128]{1,0:T(8,128)S(1)} %get-tuple-element.26), channel_id=1, source_target_pairs={{0,6},{1,7},{2,4},{3,5},{4,2},{5,3},{6,0},{7,1},{8,14},{9,15},{10,... | collective-permute-start | bytes 294920 | tf_op jit(solution)/shard_map/ppermute | solution.py:435
  16.9 0.1 collective-permute-start.1
  17.1 0.0 collective-permute-done.4
  17.1 0.1 slice_add_fusion.4
  17.1 3.0 %collective-permute-start.7 = (f32[192,128]{1,0:T(8,128)S(1)}, f32[192,128]{1,0:T(8,128)S(1)}, u32[]{:S(2)}, u32[]{:S(2)}) collective-permute-start(f32[192,128]{1,0:T(8,128)S(1)} %get-tuple-element.28), channel_id=1, source_target_pairs={{0,6},{1,7},{2,4},{3,5},{4,2},{5,3},{6,0},{7,1},{8,14},{9,15},{10,... | collective-permute-start | bytes 294920 | tf_op jit(solution)/shard_map/ppermute | solution.py:435
  20.1 0.5 collective-permute-start.6
  20.6 0.0 collective-permute-done.3
  20.6 0.4 collective-permute-start.5
  21.0 1.7 %collective-permute-done.2 = f32[192,128]{1,0:T(8,128)S(1)} collective-permute-done((f32[192,128]{1,0:T(8,128)S(1)}, f32[192,128]{1,0:T(8,128)S(1)}, u32[]{:S(2)}, u32[]{:S(2)}) %collective-permute-start.2) | collective-permute-done | bytes 98336 | tf_op jit(solution)/shard_map/ppermute | solution.py:435
  22.7 3.9 %collective-permute-done.1.other_ref = f32[216,128]{1,0:T(8,128)S(1)} collective-permute-done((f32[216,128]{1,0:T(8,128)S(1)}, f32[216,128]{1,0:T(8,128)S(1)}, u32[]{:S(2)}, u32[]{:S(2)}) %collective-permute-start.1) | collective-permute-done | bytes 110624 | tf_op jit(solution)/shard_map/ppermute | solution.py:435
  26.6 1.4 %collective-permute-done.6 = f32[192,128]{1,0:T(8,128)S(1)} collective-permute-done((f32[192,128]{1,0:T(8,128)S(1)}, f32[192,128]{1,0:T(8,128)S(1)}, u32[]{:S(2)}, u32[]{:S(2)}) %collective-permute-start.6) | collective-permute-done | bytes 98336 | tf_op jit(solution)/shard_map/ppermute | solution.py:435
  28.1 0.0 collective-permute-done.5
  28.1 3.7 %collective-permute-start.8 = (f32[48,256]{1,0:T(8,128)S(1)}, f32[48,256]{1,0:T(8,128)S(1)}, u32[]{:S(2)}, u32[]{:S(2)}) collective-permute-start(f32[48,256]{1,0:T(8,128)S(1)} %pad_maximum_fusion.2), channel_id=1, source_target_pairs={{0,24},{1,25},{2,26},{3,27},{4,28},{5,29},{6,30},{7,31},{8,16},{9,... | collective-permute-start | bytes 147464 | tf_op jit(solution)/shard_map/ppermute | solution.py:435
  31.8 0.8 %collective-permute-start.10 = (f32[48,256]{1,0:T(8,128)S(1)}, f32[48,256]{1,0:T(8,128)S(1)}, u32[]{:S(2)}, u32[]{:S(2)}) collective-permute-start(f32[48,256]{1,0:T(8,128)S(1)} %pad_maximum_fusion.4), channel_id=1, source_target_pairs={{0,8},{1,9},{2,10},{3,11},{4,12},{5,13},{6,14},{7,15},{8,0},{9,1},... | collective-permute-start | bytes 147464 | tf_op jit(solution)/shard_map/ppermute | solution.py:435
  32.6 0.3 shard_map.70
  32.9 1.8 %collective-permute-done.8 = f32[48,256]{1,0:T(8,128)S(1)} collective-permute-done((f32[48,256]{1,0:T(8,128)S(1)}, f32[48,256]{1,0:T(8,128)S(1)}, u32[]{:S(2)}, u32[]{:S(2)}) %collective-permute-start.8) | collective-permute-done | bytes 49184 | tf_op jit(solution)/shard_map/ppermute | solution.py:435
  34.7 2.1 %collective-permute-done.9 = f32[48,256]{1,0:T(8,128)S(1)} collective-permute-done((f32[48,256]{1,0:T(8,128)S(1)}, f32[48,256]{1,0:T(8,128)S(1)}, u32[]{:S(2)}, u32[]{:S(2)}) %collective-permute-start.9) | collective-permute-done | bytes 49184 | tf_op jit(solution)/shard_map/ppermute | solution.py:435
  36.8 0.0 collective-permute-done.10
  36.8 1.8 %collective-permute-start.13 = (f32[48,256]{1,0:T(8,128)S(1)}, f32[48,256]{1,0:T(8,128)S(1)}, u32[]{:S(2)}, u32[]{:S(2)}) collective-permute-start(f32[48,256]{1,0:T(8,128)S(1)} %fusion.1), channel_id=1, source_target_pairs={{0,24},{1,25},{2,26},{3,27},{4,28},{5,29},{6,30},{7,31},{8,16},{9,... | collective-permute-start | bytes 147464 | tf_op jit(solution)/shard_map/ppermute | solution.py:435
  38.7 0.4 collective-permute-start.12
  39.0 2.3 %collective-permute-start.11 = (f32[48,256]{1,0:T(8,128)S(1)}, f32[48,256]{1,0:T(8,128)S(1)}, u32[]{:S(2)}, u32[]{:S(2)}) collective-permute-start(f32[48,256]{1,0:T(8,128)S(1)} %fusion.1), channel_id=1, source_target_pairs={{0,8},{1,9},{2,10},{3,11},{4,12},{5,13},{6,14},{7,15},{8,0},{9,1},... | collective-permute-start | bytes 147464 | tf_op jit(solution)/shard_map/ppermute | solution.py:435
  41.3 1.5 %collective-permute-done.13 = f32[48,256]{1,0:T(8,128)S(1)} collective-permute-done((f32[48,256]{1,0:T(8,128)S(1)}, f32[48,256]{1,0:T(8,128)S(1)}, u32[]{:S(2)}, u32[]{:S(2)}) %collective-permute-start.13) | collective-permute-done | bytes 49184 | tf_op jit(solution)/shard_map/ppermute | solution.py:435
  42.8 1.4 %collective-permute-done.12 = f32[48,256]{1,0:T(8,128)S(1)} collective-permute-done((f32[48,256]{1,0:T(8,128)S(1)}, f32[48,256]{1,0:T(8,128)S(1)}, u32[]{:S(2)}, u32[]{:S(2)}) %collective-permute-start.12) | collective-permute-done | bytes 49184 | tf_op jit(solution)/shard_map/ppermute | solution.py:435
  44.2 0.0 collective-permute-done.11
  44.2 0.1 collective-permute-start.17
  44.3 0.5 collective-permute-start.16
  44.8 1.6 %collective-permute-start.15 = (f32[4,48,128]{2,1,0:T(8,128)S(1)}, f32[4,48,128]{2,1,0:T(8,128)S(1)}, u32[]{:S(2)}, u32[]{:S(2)}) collective-permute-start(f32[4,48,128]{2,1,0:T(8,128)S(1)} %pad_maximum_fusion.rest_0_.refs_0_), channel_id=1, source_target_pairs={{0,4},{1,5},{2,6},{3,7},{4,0},{5,1},{6,2},{7,3},{8,12},{9,13},{10,... | collective-permute-start | bytes 294920 | tf_op jit(solution)/shard_map/ppermute | solution.py:435
  46.4 1.5 %collective-permute-start.14 = (f32[4,48,128]{2,1,0:T(8,128)S(1)}, f32[4,48,128]{2,1,0:T(8,128)S(1)}, u32[]{:S(2)}, u32[]{:S(2)}) collective-permute-start(f32[4,48,128]{2,1,0:T(8,128)S(1)} %pad_maximum_fusion.rest_0_.refs_0_), channel_id=1, source_target_pairs={{0,6},{1,7},{2,4},{3,5},{4,2},{5,3},{6,0},{7,1},{8,14},{9,15},{10,... | collective-permute-start | bytes 294920 | tf_op jit(solution)/shard_map/ppermute | solution.py:435
  47.9 1.5 %collective-permute-start.23 = (f32[4,48,128]{2,1,0:T(8,128)S(1)}, f32[4,48,128]{2,1,0:T(8,128)S(1)}, u32[]{:S(2)}, u32[]{:S(2)}) collective-permute-start(f32[4,48,128]{2,1,0:T(8,128)S(1)} %pad_maximum_fusion.1.rest_0_.refs_4_), channel_id=1, source_target_pairs={{0,6},{1,7},{2,4},{3,5},{4,2},{5,3},{6,0},{7,1},{8,14},{9,15},{10,... | collective-permute-start | bytes 294920 | tf_op jit(solution)/shard_map/ppermute | solution.py:435
  49.4 0.0 collective-permute-done.17.rest_4_.refs_1_
  49.4 1.5 %collective-permute-start.22 = (f32[4,48,128]{2,1,0:T(8,128)S(1)}, f32[4,48,128]{2,1,0:T(8,128)S(1)}, u32[]{:S(2)}, u32[]{:S(2)}) collective-permute-start(f32[4,48,128]{2,1,0:T(8,128)S(1)} %pad_maximum_fusion.1.rest_0_.refs_4_), channel_id=1, source_target_pairs={{0,2},{1,3},{2,0},{3,1},{4,6},{5,7},{6,4},{7,5},{8,10},{9,11},{10,... | collective-permute-start | bytes 294920 | tf_op jit(solution)/shard_map/ppermute | solution.py:435
  50.9 0.5 collective-permute-start.21
  51.4 2.2 %collective-permute-done.14.rest_1_ = f32[4,48,128]{2,1,0:T(8,128)S(1)} collective-permute-done((f32[4,48,128]{2,1,0:T(8,128)S(1)}, f32[4,48,128]{2,1,0:T(8,128)S(1)}, u32[]{:S(2)}, u32[]{:S(2)}) %collective-permute-start.14) | collective-permute-done | bytes 98336 | tf_op jit(solution)/shard_map/ppermute | solution.py:435
  53.7 0.0 collective-permute-start.19
  53.7 2.0 %collective-permute-done.23.rest_3_ = f32[4,48,128]{2,1,0:T(8,128)S(1)} collective-permute-done((f32[4,48,128]{2,1,0:T(8,128)S(1)}, f32[4,48,128]{2,1,0:T(8,128)S(1)}, u32[]{:S(2)}, u32[]{:S(2)}) %collective-permute-start.23) | collective-permute-done | bytes 98336 | tf_op jit(solution)/shard_map/ppermute | solution.py:435
  55.7 0.0 collective-permute-start.24
  55.7 1.2 %collective-permute-done.22.rest_2_.refs_6_ = f32[4,48,128]{2,1,0:T(8,128)S(1)} collective-permute-done((f32[4,48,128]{2,1,0:T(8,128)S(1)}, f32[4,48,128]{2,1,0:T(8,128)S(1)}, u32[]{:S(2)}, u32[]{:S(2)}) %collective-permute-start.22) | collective-permute-done | bytes 98336 | tf_op jit(solution)/shard_map/ppermute | solution.py:435
  56.9 0.0 collective-permute-start.18
  56.9 0.0 collective-permute-done.21.rest_1_
  56.9 0.5 collective-permute-start.27
  57.4 0.0 collective-permute-done.20.rest_7_.refs_3_
  57.4 0.1 collective-permute-start.26
  57.5 0.4 collective-permute-start.25
  58.0 0.3 collective-permute-done.18.rest_5_
  58.2 1.0 %shard_map.71.total_ref = f32[288,96]{1,0:T(8,128)S(1)} custom-call(bf16[32,96,256]{2,1,0:T(8,128)(2,1)S(1)} %get-tuple-element.13.xh_ref, bf16[32,96,256]{2,1,0:T(8,128)(2,1)S(1)} %get-tuple-element.14.xl_ref, f32[4,48,128]{2,1,0:T(8,128)S(1)} %pad_maximum_fusion.rest_0_.refs_0_, f32[4,48,128]{2,1,0:T(8,128)S(1)} %collective-permute-done.14.rest_1_, ...), custom_call_target="tpu_custom_call" | custom-call | tf_op jit(solution)/shard_map/pallas_call | solution.py:346
  59.3 0.0 collective-permute-done.27.rest_7_
  59.3 0.0 collective-permute-done.26.rest_6_.refs_7_
  59.3 1.4 %shard_map.72 = f32[48,96]{1,0:T(8,128)S(1)} custom-call(bf16[32,96,256]{2,1,0:T(8,128)(2,1)S(1)} %get-tuple-element.13.xh_ref, bf16[32,96,256]{2,1,0:T(8,128)(2,1)S(1)} %get-tuple-element.14.xl_ref, f32[48,96]{1,0:T(8,128)S(1)} %get-tuple-element.15.w_ref, f32[288,96]{1,0:T(8,128)S(1)} %shard_map.71.total_ref, ...), custom_call_target="tpu_custom_call" | custom-call | tf_op jit(solution)/shard_map/pallas_call | solution.py:370
  60.7 1.0 %collective-permute-start.28 = (f32[48,96]{1,0:T(8,128)S(1)}, f32[48,96]{1,0:T(8,128)S(1)}, u32[]{:S(2)}, u32[]{:S(2)}) collective-permute-start(f32[48,96]{1,0:T(8,128)S(1)} %shard_map.72), channel_id=1, source_target_pairs={{0,4},{1,5},{2,6},{3,7},{4,0},{5,1},{6,2},{7,3},{8,12},{9,13},{10,... | collective-permute-start | bytes 55304 | tf_op jit(solution)/shard_map/ppermute | solution.py:435
  61.8 2.9 %collective-permute-done.28 = f32[48,96]{1,0:T(8,128)S(1)} collective-permute-done((f32[48,96]{1,0:T(8,128)S(1)}, f32[48,96]{1,0:T(8,128)S(1)}, u32[]{:S(2)}, u32[]{:S(2)}) %collective-permute-start.28) | collective-permute-done | bytes 18464 | tf_op jit(solution)/shard_map/ppermute | solution.py:435
  64.6 2.1 %collective-permute-start.31 = (f32[2,48,96]{2,1,0:T(8,128)S(1)}, f32[2,48,96]{2,1,0:T(8,128)S(1)}, u32[]{:S(2)}, u32[]{:S(2)}) collective-permute-start(f32[2,48,96]{2,1,0:T(8,128)S(1)} %pad_maximum_fusion.5.refs_0_), channel_id=1, source_target_pairs={{0,24},{1,25},{2,26},{3,27},{4,28},{5,29},{6,30},{7,31},{8,16},{9,... | collective-permute-start | bytes 110600 | tf_op jit(solution)/shard_map/ppermute | solution.py:435
  66.7 0.6 collective-permute-start.30
  67.3 1.7 %collective-permute-start.29 = (f32[2,48,96]{2,1,0:T(8,128)S(1)}, f32[2,48,96]{2,1,0:T(8,128)S(1)}, u32[]{:S(2)}, u32[]{:S(2)}) collective-permute-start(f32[2,48,96]{2,1,0:T(8,128)S(1)} %pad_maximum_fusion.5.refs_0_), channel_id=1, source_target_pairs={{0,8},{1,9},{2,10},{3,11},{4,12},{5,13},{6,14},{7,15},{8,0},{9,1},... | collective-permute-start | bytes 110600 | tf_op jit(solution)/shard_map/ppermute | solution.py:435
  69.1 1.0 %shard_map.74 = f32[32,32,48]{2,1,0:T(8,128)} custom-call(f32[4,48,128]{2,1,0:T(8,128)S(1)} %pad_maximum_fusion.rest_0_.refs_0_, f32[4,48,128]{2,1,0:T(8,128)S(1)} %collective-permute-done.17.rest_4_.refs_1_, f32[4,48,128]{2,1,0:T(8,128)S(1)} %collective-permute-done.16.rest_3_.refs_2_, f32[4,48,128]{2,1,0:T(8,128)S(1)} %collective-permute-done.20.rest_7_.refs_3_, ...), custom_call_target="tpu_custom_call" | custom-call | tf_op jit(solution)/shard_map/pallas_call | solution.py:391
  70.1 0.9 %collective-permute-done.31.refs_3_ = f32[2,48,96]{2,1,0:T(8,128)S(1)} collective-permute-done((f32[2,48,96]{2,1,0:T(8,128)S(1)}, f32[2,48,96]{2,1,0:T(8,128)S(1)}, u32[]{:S(2)}, u32[]{:S(2)}) %collective-permute-start.31) | collective-permute-done | bytes 36896 | tf_op jit(solution)/shard_map/ppermute | solution.py:435
  71.0 1.1 %collective-permute-done.30.refs_2_ = f32[2,48,96]{2,1,0:T(8,128)S(1)} collective-permute-done((f32[2,48,96]{2,1,0:T(8,128)S(1)}, f32[2,48,96]{2,1,0:T(8,128)S(1)}, u32[]{:S(2)}, u32[]{:S(2)}) %collective-permute-start.30) | collective-permute-done | bytes 36896 | tf_op jit(solution)/shard_map/ppermute | solution.py:435
  72.2 0.8 %shard_map.73 = f32[48,768]{1,0:T(8,128)} custom-call(f32[2,48,96]{2,1,0:T(8,128)S(1)} %pad_maximum_fusion.5.refs_0_, f32[2,48,96]{2,1,0:T(8,128)S(1)} %collective-permute-done.29.refs_1_, f32[2,48,96]{2,1,0:T(8,128)S(1)} %collective-permute-done.30.refs_2_, f32[2,48,96]{2,1,0:T(8,128)S(1)} %collective-permute-done.31.refs_3_), custom_call_target="tpu_custom_call" | custom-call | tf_op jit(solution)/shard_map/pallas_call | solution.py:419
  (25 shorter events, 0.2 us)
Async XLA Ops:
  10.4 1.9 %collective-permute-start = (f32[792,128]{1,0:T(8,128)S(1)}, f32[792,128]{1,0:T(8,128)S(1)}, u32[]{:S(2)}, u32[]{:S(2)}) collective-permute-start(f32[792,128]{1,0:T(8,128)S(1)} %get-tuple-element.17), channel_id=1, source_target_pairs={{0,1},{1,0},{2,3},{3,2},{4,5},{5,4},{6,7},{7,6},{8,9},{9,8},{10,11... | collective-permute-start | bytes 1216520 | tf_op jit(solution)/shard_map/ppermute | solution.py:435
  12.3 4.7 %collective-permute-start.4 = (f32[768,128]{1,0:T(8,128)S(1)}, f32[768,128]{1,0:T(8,128)S(1)}, u32[]{:S(2)}, u32[]{:S(2)}) collective-permute-start(f32[768,128]{1,0:T(8,128)S(1)} %get-tuple-element.23), channel_id=1, source_target_pairs={{0,1},{1,0},{2,3},{3,2},{4,5},{5,4},{6,7},{7,6},{8,9},{9,8},{10,11... | collective-permute-start | bytes 1179656 | tf_op jit(solution)/shard_map/ppermute | solution.py:435
  12.7 19.9 %copy-start = (f32[48,32,32]{0,2,1:T(8,128)S(1)}, f32[48,32,32]{0,2,1:T(8,128)}, u32[]{:S(2)}) copy-start(f32[48,32,32]{0,2,1:T(8,128)} %param.9) | copy-start | bytes 589828
  12.7 7.9 %collective-permute-start.3 = (f32[192,128]{1,0:T(8,128)S(1)}, f32[192,128]{1,0:T(8,128)S(1)}, u32[]{:S(2)}, u32[]{:S(2)}) collective-permute-start(f32[192,128]{1,0:T(8,128)S(1)} %get-tuple-element.25), channel_id=1, source_target_pairs={{0,4},{1,5},{2,6},{3,7},{4,0},{5,1},{6,2},{7,3},{8,12},{9,13},{10,... | collective-permute-start | bytes 294920 | tf_op jit(solution)/shard_map/ppermute | solution.py:435
  15.4 7.3 %collective-permute-start.2 = (f32[192,128]{1,0:T(8,128)S(1)}, f32[192,128]{1,0:T(8,128)S(1)}, u32[]{:S(2)}, u32[]{:S(2)}) collective-permute-start(f32[192,128]{1,0:T(8,128)S(1)} %get-tuple-element.26), channel_id=1, source_target_pairs={{0,6},{1,7},{2,4},{3,5},{4,2},{5,3},{6,0},{7,1},{8,14},{9,15},{10,... | collective-permute-start | bytes 294920 | tf_op jit(solution)/shard_map/ppermute | solution.py:435
  16.9 9.7 %collective-permute-start.1 = (f32[216,128]{1,0:T(8,128)S(1)}, f32[216,128]{1,0:T(8,128)S(1)}, u32[]{:S(2)}, u32[]{:S(2)}) collective-permute-start(f32[216,128]{1,0:T(8,128)S(1)} %slice_add_fusion.mine_ref), channel_id=1, source_target_pairs={{0,2},{1,3},{2,0},{3,1},{4,6},{5,7},{6,4},{7,5},{8,10},{9,11},{10,... | collective-permute-start | bytes 331784 | tf_op jit(solution)/shard_map/ppermute | solution.py:435
  17.1 9.5 %collective-permute-start.7 = (f32[192,128]{1,0:T(8,128)S(1)}, f32[192,128]{1,0:T(8,128)S(1)}, u32[]{:S(2)}, u32[]{:S(2)}) collective-permute-start(f32[192,128]{1,0:T(8,128)S(1)} %get-tuple-element.28), channel_id=1, source_target_pairs={{0,6},{1,7},{2,4},{3,5},{4,2},{5,3},{6,0},{7,1},{8,14},{9,15},{10,... | collective-permute-start | bytes 294920 | tf_op jit(solution)/shard_map/ppermute | solution.py:435
  20.1 8.0 %collective-permute-start.6 = (f32[192,128]{1,0:T(8,128)S(1)}, f32[192,128]{1,0:T(8,128)S(1)}, u32[]{:S(2)}, u32[]{:S(2)}) collective-permute-start(f32[192,128]{1,0:T(8,128)S(1)} %get-tuple-element.29), channel_id=1, source_target_pairs={{0,2},{1,3},{2,0},{3,1},{4,6},{5,7},{6,4},{7,5},{8,10},{9,11},{10,... | collective-permute-start | bytes 294920 | tf_op jit(solution)/shard_map/ppermute | solution.py:435
  20.6 7.5 %collective-permute-start.5 = (f32[192,128]{1,0:T(8,128)S(1)}, f32[192,128]{1,0:T(8,128)S(1)}, u32[]{:S(2)}, u32[]{:S(2)}) collective-permute-start(f32[192,128]{1,0:T(8,128)S(1)} %get-tuple-element.30), channel_id=1, source_target_pairs={{0,4},{1,5},{2,6},{3,7},{4,0},{5,1},{6,2},{7,3},{8,12},{9,13},{10,... | collective-permute-start | bytes 294920 | tf_op jit(solution)/shard_map/ppermute | solution.py:435
  28.1 6.5 %collective-permute-start.8 = (f32[48,256]{1,0:T(8,128)S(1)}, f32[48,256]{1,0:T(8,128)S(1)}, u32[]{:S(2)}, u32[]{:S(2)}) collective-permute-start(f32[48,256]{1,0:T(8,128)S(1)} %pad_maximum_fusion.2), channel_id=1, source_target_pairs={{0,24},{1,25},{2,26},{3,27},{4,28},{5,29},{6,30},{7,31},{8,16},{9,... | collective-permute-start | bytes 147464 | tf_op jit(solution)/shard_map/ppermute | solution.py:435
  31.8 5.0 %collective-permute-start.9 = (f32[48,256]{1,0:T(8,128)S(1)}, f32[48,256]{1,0:T(8,128)S(1)}, u32[]{:S(2)}, u32[]{:S(2)}) collective-permute-start(f32[48,256]{1,0:T(8,128)S(1)} %pad_maximum_fusion.3), channel_id=1, source_target_pairs={{0,16},{1,17},{2,18},{3,19},{4,20},{5,21},{6,22},{7,23},{8,24},{9,... | collective-permute-start | bytes 147464 | tf_op jit(solution)/shard_map/ppermute | solution.py:435
  31.8 5.0 %collective-permute-start.10 = (f32[48,256]{1,0:T(8,128)S(1)}, f32[48,256]{1,0:T(8,128)S(1)}, u32[]{:S(2)}, u32[]{:S(2)}) collective-permute-start(f32[48,256]{1,0:T(8,128)S(1)} %pad_maximum_fusion.4), channel_id=1, source_target_pairs={{0,8},{1,9},{2,10},{3,11},{4,12},{5,13},{6,14},{7,15},{8,0},{9,1},... | collective-permute-start | bytes 147464 | tf_op jit(solution)/shard_map/ppermute | solution.py:435
  36.8 6.0 %collective-permute-start.13 = (f32[48,256]{1,0:T(8,128)S(1)}, f32[48,256]{1,0:T(8,128)S(1)}, u32[]{:S(2)}, u32[]{:S(2)}) collective-permute-start(f32[48,256]{1,0:T(8,128)S(1)} %fusion.1), channel_id=1, source_target_pairs={{0,24},{1,25},{2,26},{3,27},{4,28},{5,29},{6,30},{7,31},{8,16},{9,... | collective-permute-start | bytes 147464 | tf_op jit(solution)/shard_map/ppermute | solution.py:435
  38.7 5.5 %collective-permute-start.12 = (f32[48,256]{1,0:T(8,128)S(1)}, f32[48,256]{1,0:T(8,128)S(1)}, u32[]{:S(2)}, u32[]{:S(2)}) collective-permute-start(f32[48,256]{1,0:T(8,128)S(1)} %fusion.1), channel_id=1, source_target_pairs={{0,16},{1,17},{2,18},{3,19},{4,20},{5,21},{6,22},{7,23},{8,24},{9,... | collective-permute-start | bytes 147464 | tf_op jit(solution)/shard_map/ppermute | solution.py:435
  39.0 5.2 %collective-permute-start.11 = (f32[48,256]{1,0:T(8,128)S(1)}, f32[48,256]{1,0:T(8,128)S(1)}, u32[]{:S(2)}, u32[]{:S(2)}) collective-permute-start(f32[48,256]{1,0:T(8,128)S(1)} %fusion.1), channel_id=1, source_target_pairs={{0,8},{1,9},{2,10},{3,11},{4,12},{5,13},{6,14},{7,15},{8,0},{9,1},... | collective-permute-start | bytes 147464 | tf_op jit(solution)/shard_map/ppermute | solution.py:435
  44.2 5.1 %collective-permute-start.17 = (f32[4,48,128]{2,1,0:T(8,128)S(1)}, f32[4,48,128]{2,1,0:T(8,128)S(1)}, u32[]{:S(2)}, u32[]{:S(2)}) collective-permute-start(f32[4,48,128]{2,1,0:T(8,128)S(1)} %pad_maximum_fusion.rest_0_.refs_0_), channel_id=1, source_target_pairs={{0,1},{1,0},{2,3},{3,2},{4,5},{5,4},{6,7},{7,6},{8,9},{9,8},{10,11... | collective-permute-start | bytes 294920 | tf_op jit(solution)/shard_map/ppermute | solution.py:435
  44.3 6.6 %collective-permute-start.16 = (f32[4,48,128]{2,1,0:T(8,128)S(1)}, f32[4,48,128]{2,1,0:T(8,128)S(1)}, u32[]{:S(2)}, u32[]{:S(2)}) collective-permute-start(f32[4,48,128]{2,1,0:T(8,128)S(1)} %pad_maximum_fusion.rest_0_.refs_0_), channel_id=1, source_target_pairs={{0,2},{1,3},{2,0},{3,1},{4,6},{5,7},{6,4},{7,5},{8,10},{9,11},{10,... | collective-permute-start | bytes 294920 | tf_op jit(solution)/shard_map/ppermute | solution.py:435
  44.8 6.7 %collective-permute-start.15 = (f32[4,48,128]{2,1,0:T(8,128)S(1)}, f32[4,48,128]{2,1,0:T(8,128)S(1)}, u32[]{:S(2)}, u32[]{:S(2)}) collective-permute-start(f32[4,48,128]{2,1,0:T(8,128)S(1)} %pad_maximum_fusion.rest_0_.refs_0_), channel_id=1, source_target_pairs={{0,4},{1,5},{2,6},{3,7},{4,0},{5,1},{6,2},{7,3},{8,12},{9,13},{10,... | collective-permute-start | bytes 294920 | tf_op jit(solution)/shard_map/ppermute | solution.py:435
  46.4 7.3 %collective-permute-start.14 = (f32[4,48,128]{2,1,0:T(8,128)S(1)}, f32[4,48,128]{2,1,0:T(8,128)S(1)}, u32[]{:S(2)}, u32[]{:S(2)}) collective-permute-start(f32[4,48,128]{2,1,0:T(8,128)S(1)} %pad_maximum_fusion.rest_0_.refs_0_), channel_id=1, source_target_pairs={{0,6},{1,7},{2,4},{3,5},{4,2},{5,3},{6,0},{7,1},{8,14},{9,15},{10,... | collective-permute-start | bytes 294920 | tf_op jit(solution)/shard_map/ppermute | solution.py:435
  47.9 7.9 %collective-permute-start.23 = (f32[4,48,128]{2,1,0:T(8,128)S(1)}, f32[4,48,128]{2,1,0:T(8,128)S(1)}, u32[]{:S(2)}, u32[]{:S(2)}) collective-permute-start(f32[4,48,128]{2,1,0:T(8,128)S(1)} %pad_maximum_fusion.1.rest_0_.refs_4_), channel_id=1, source_target_pairs={{0,6},{1,7},{2,4},{3,5},{4,2},{5,3},{6,0},{7,1},{8,14},{9,15},{10,... | collective-permute-start | bytes 294920 | tf_op jit(solution)/shard_map/ppermute | solution.py:435
  49.4 7.6 %collective-permute-start.22 = (f32[4,48,128]{2,1,0:T(8,128)S(1)}, f32[4,48,128]{2,1,0:T(8,128)S(1)}, u32[]{:S(2)}, u32[]{:S(2)}) collective-permute-start(f32[4,48,128]{2,1,0:T(8,128)S(1)} %pad_maximum_fusion.1.rest_0_.refs_4_), channel_id=1, source_target_pairs={{0,2},{1,3},{2,0},{3,1},{4,6},{5,7},{6,4},{7,5},{8,10},{9,11},{10,... | collective-permute-start | bytes 294920 | tf_op jit(solution)/shard_map/ppermute | solution.py:435
  50.9 6.0 %collective-permute-start.21 = (f32[4,48,128]{2,1,0:T(8,128)S(1)}, f32[4,48,128]{2,1,0:T(8,128)S(1)}, u32[]{:S(2)}, u32[]{:S(2)}) collective-permute-start(f32[4,48,128]{2,1,0:T(8,128)S(1)} %pad_maximum_fusion.1.rest_0_.refs_4_), channel_id=1, source_target_pairs={{0,4},{1,5},{2,6},{3,7},{4,0},{5,1},{6,2},{7,3},{8,12},{9,13},{10,... | collective-permute-start | bytes 294920 | tf_op jit(solution)/shard_map/ppermute | solution.py:435
  51.4 6.0 %collective-permute-start.20 = (f32[4,48,128]{2,1,0:T(8,128)S(1)}, f32[4,48,128]{2,1,0:T(8,128)S(1)}, u32[]{:S(2)}, u32[]{:S(2)}) collective-permute-start(f32[4,48,128]{2,1,0:T(8,128)S(1)} %collective-permute-done.16.rest_3_.refs_2_), channel_id=1, source_target_pairs={{0,1},{1,0},{2,3},{3,2},{4,5},{5,4},{6,7},{7,6},{8,9},{9,8},{10,11... | collective-permute-start | bytes 294920 | tf_op jit(solution)/shard_map/ppermute | solution.py:435
  53.7 3.8 %collective-permute-start.19 = (f32[4,48,128]{2,1,0:T(8,128)S(1)}, f32[4,48,128]{2,1,0:T(8,128)S(1)}, u32[]{:S(2)}, u32[]{:S(2)}) collective-permute-start(f32[4,48,128]{2,1,0:T(8,128)S(1)} %collective-permute-done.15.rest_2_), channel_id=1, source_target_pairs={{0,1},{1,0},{2,3},{3,2},{4,5},{5,4},{6,7},{7,6},{8,9},{9,8},{10,11... | collective-permute-start | bytes 294920 | tf_op jit(solution)/shard_map/ppermute | solution.py:435
  55.7 3.6 %collective-permute-start.24 = (f32[4,48,128]{2,1,0:T(8,128)S(1)}, f32[4,48,128]{2,1,0:T(8,128)S(1)}, u32[]{:S(2)}, u32[]{:S(2)}) collective-permute-start(f32[4,48,128]{2,1,0:T(8,128)S(1)} %pad_maximum_fusion.1.rest_0_.refs_4_), channel_id=1, source_target_pairs={{0,1},{1,0},{2,3},{3,2},{4,5},{5,4},{6,7},{7,6},{8,9},{9,8},{10,11... | collective-permute-start | bytes 294920 | tf_op jit(solution)/shard_map/ppermute | solution.py:435
  56.9 1.3 %collective-permute-start.18 = (f32[4,48,128]{2,1,0:T(8,128)S(1)}, f32[4,48,128]{2,1,0:T(8,128)S(1)}, u32[]{:S(2)}, u32[]{:S(2)}) collective-permute-start(f32[4,48,128]{2,1,0:T(8,128)S(1)} %collective-permute-done.14.rest_1_), channel_id=1, source_target_pairs={{0,1},{1,0},{2,3},{3,2},{4,5},{5,4},{6,7},{7,6},{8,9},{9,8},{10,11... | collective-permute-start | bytes 294920 | tf_op jit(solution)/shard_map/ppermute | solution.py:435
  56.9 2.4 %collective-permute-start.27 = (f32[4,48,128]{2,1,0:T(8,128)S(1)}, f32[4,48,128]{2,1,0:T(8,128)S(1)}, u32[]{:S(2)}, u32[]{:S(2)}) collective-permute-start(f32[4,48,128]{2,1,0:T(8,128)S(1)} %collective-permute-done.23.rest_3_), channel_id=1, source_target_pairs={{0,1},{1,0},{2,3},{3,2},{4,5},{5,4},{6,7},{7,6},{8,9},{9,8},{10,11... | collective-permute-start | bytes 294920 | tf_op jit(solution)/shard_map/ppermute | solution.py:435
  57.4 1.9 %collective-permute-start.26 = (f32[4,48,128]{2,1,0:T(8,128)S(1)}, f32[4,48,128]{2,1,0:T(8,128)S(1)}, u32[]{:S(2)}, u32[]{:S(2)}) collective-permute-start(f32[4,48,128]{2,1,0:T(8,128)S(1)} %collective-permute-done.22.rest_2_.refs_6_), channel_id=1, source_target_pairs={{0,1},{1,0},{2,3},{3,2},{4,5},{5,4},{6,7},{7,6},{8,9},{9,8},{10,11... | collective-permute-start | bytes 294920 | tf_op jit(solution)/shard_map/ppermute | solution.py:435
  57.5 1.8 %collective-permute-start.25 = (f32[4,48,128]{2,1,0:T(8,128)S(1)}, f32[4,48,128]{2,1,0:T(8,128)S(1)}, u32[]{:S(2)}, u32[]{:S(2)}) collective-permute-start(f32[4,48,128]{2,1,0:T(8,128)S(1)} %collective-permute-done.21.rest_1_), channel_id=1, source_target_pairs={{0,1},{1,0},{2,3},{3,2},{4,5},{5,4},{6,7},{7,6},{8,9},{9,8},{10,11... | collective-permute-start | bytes 294920 | tf_op jit(solution)/shard_map/ppermute | solution.py:435
  60.7 3.9 %collective-permute-start.28 = (f32[48,96]{1,0:T(8,128)S(1)}, f32[48,96]{1,0:T(8,128)S(1)}, u32[]{:S(2)}, u32[]{:S(2)}) collective-permute-start(f32[48,96]{1,0:T(8,128)S(1)} %shard_map.72), channel_id=1, source_target_pairs={{0,4},{1,5},{2,6},{3,7},{4,0},{5,1},{6,2},{7,3},{8,12},{9,13},{10,... | collective-permute-start | bytes 55304 | tf_op jit(solution)/shard_map/ppermute | solution.py:435
  64.6 6.4 %collective-permute-start.31 = (f32[2,48,96]{2,1,0:T(8,128)S(1)}, f32[2,48,96]{2,1,0:T(8,128)S(1)}, u32[]{:S(2)}, u32[]{:S(2)}) collective-permute-start(f32[2,48,96]{2,1,0:T(8,128)S(1)} %pad_maximum_fusion.5.refs_0_), channel_id=1, source_target_pairs={{0,24},{1,25},{2,26},{3,27},{4,28},{5,29},{6,30},{7,31},{8,16},{9,... | collective-permute-start | bytes 110600 | tf_op jit(solution)/shard_map/ppermute | solution.py:435
  66.7 5.4 %collective-permute-start.30 = (f32[2,48,96]{2,1,0:T(8,128)S(1)}, f32[2,48,96]{2,1,0:T(8,128)S(1)}, u32[]{:S(2)}, u32[]{:S(2)}) collective-permute-start(f32[2,48,96]{2,1,0:T(8,128)S(1)} %pad_maximum_fusion.5.refs_0_), channel_id=1, source_target_pairs={{0,16},{1,17},{2,18},{3,19},{4,20},{5,21},{6,22},{7,23},{8,24},{9,... | collective-permute-start | bytes 110600 | tf_op jit(solution)/shard_map/ppermute | solution.py:435
  67.3 4.8 %collective-permute-start.29 = (f32[2,48,96]{2,1,0:T(8,128)S(1)}, f32[2,48,96]{2,1,0:T(8,128)S(1)}, u32[]{:S(2)}, u32[]{:S(2)}) collective-permute-start(f32[2,48,96]{2,1,0:T(8,128)S(1)} %pad_maximum_fusion.5.refs_0_), channel_id=1, source_target_pairs={{0,8},{1,9},{2,10},{3,11},{4,12},{5,13},{6,14},{7,15},{8,0},{9,1},... | collective-permute-start | bytes 110600 | tf_op jit(solution)/shard_map/ppermute | solution.py:435

commit v14 on v12

--- a/solution.py
+++ b/solution.py
@@ -437,16 +437,6 @@
     return [send(values[k], k % 2, 2 * (k // 2)) for k in range(1, 4)]
 
 
-def spread(value, chain):
-    if chain == 0:
-        column, row = send(value, 1, 0), send(value, 0, 2)
-        corner = send(row, 1, 0)
-    else:
-        row, column = send(value, 0, 2), send(value, 1, 0)
-        corner = send(column, 0, 2)
-    return [value, column, row, corner]
-
-
 def local(cube, taps_x, taps_y, factor_w, factor_h):
     w_rows = jnp.transpose(factor_w[0])
     taps_x = jnp.transpose(taps_x, (2, 0, 1))
@@ -466,19 +456,20 @@
             sides.append(keep[first:last] + taken[first:last])
         chains.append((sides, around(sides)))
     ratio = ratio_call(chains[0][0][2], chains[0][1][1], h_columns)
-    line = []
-    for k in range(4):
-        part = slice(k * rank, (k + 1) * rank)
-        line.append(jnp.concatenate(
-            [(sides[0][part] + others[0][part]) + (others[1][part] + others[2][part]) for sides, others in chains],
-            axis=1))
-    line = [line[0]] + [send(line[k], 2 * k, 0) for k in (3, 2, 1)]
-    h_piece = ratio * ((line[0] + line[1]) + (line[2] + line[3]))
+    numer = []
+    for sides, others in chains:
+        line = []
+        for k in range(4):
+            part = slice(k * rank, (k + 1) * rank)
+            line.append((sides[0][part] + others[0][part]) + (others[1][part] + others[2][part]))
+        line = [line[0]] + [send(line[k], 2 * k, 0) for k in range(1, 4)]
+        numer.append((line[0] + line[1]) + (line[2] + line[3]))
+    h_piece = ratio * jnp.concatenate(numer, axis=1)
     h_line = [h_piece] + [send(h_piece, 2 * k, 0) for k in range(1, 4)]
     chains = []
     for first in (0, LANES):
         mine = jnp.stack([value[:, first:first + LANES] for value in h_line])
-        chains.append(spread(mine, len(chains)))
+        chains.append([mine] + around([mine] * 4))
     first_parts = chains[0] + [send(value, 0, 1) for value in chains[0]]
     total = first_call(x_high, x_low, first_parts)
     second_parts = chains[1] + [send(value, 0, 1) for value in chains[1]]

time: 71.9 us -> 75 us (1.043)
  starting transfers between devices: 31.3 us -> 38.4 us
  waiting for transfers between devices: 24.5 us -> 20.5 us
    ppermute x32 -> x35, starting transfers between devices: 31.3 us -> 38.4 us  [send(): return lax.ppermute(value, ('sp', 'bd'), pairs)]
    ppermute x32 -> x35, waiting for transfers between devices: 24.5 us -> 20.5 us  [send(): return lax.ppermute(value, ('sp', 'bd'), pairs)]
  transfers between devices with their start and end apart: 32 -> 35, of which waited for: 17 -> 15; matrix products, arithmetic and copies ran while one was open for 0% -> 0% of each run, Pallas kernels for 4% -> 4%
where the time goes in v14:
time: 75 us; the launch traced here: 74.9 us
  starting transfers between devices  38.4 us (51%)
  waiting for transfers between devices  20.5 us (27%)
  Pallas kernels  15 us (20%)
  between operations  0.8 us (1%)
    ppermute x35, starting transfers between devices, send(): return lax.ppermute(value, ('sp', 'bd'), pairs)  38.4 us
    ppermute x35, waiting for transfers between devices, send(): return lax.ppermute(value, ('sp', 'bd'), pairs)  20.5 us
    pallas_call x1, Pallas kernels, blur_call(): pl.pallas_call(blur_kernel, out_shape=[jax.ShapeDtypeStruct(image, BF16)]...  9.78 us
  transfers between devices with their start and end apart: 35, of which 15 were waited for; matrix products, arithmetic and copies ran while one was open for 0% of the time, Pallas kernels for 4%

profile of v14, /device:TPU:0, one launch (start us, length us, event | category | flops | bytes accessed | tf_op | source)
XLA Modules:
  0.0 74.9 jit_solution(17307871727719585663)
XLA Ops:
  0.6 9.8 %shard_map.68 = (bf16[32,96,256]{2,1,0:T(8,128)(2,1)S(1)}, bf16[32,96,256]{2,1,0:T(8,128)(2,1)S(1)}, f32[48,96]{1,0:T(8,128)S(1)}, bf16[96,256]{1,0:T(8,128)(2,1...) custom-call(f32[96,32,256]{2,1,0:T(8,128)} %bitcast.31, f32[25,1,96]{2,1,0:T(1,128)} %bitcast.36, ...), custom_call_target="tpu_custom_call" | custom-call | tf_op jit(solution)/shard_map/pallas_call | solution.py:276
  10.4 0.5 collective-permute-start
  10.9 0.7 shard_map.69
  11.6 0.0 copy-start
  11.6 0.7 collective-permute-done
  12.3 0.4 collective-permute-start.7
  12.7 3.7 %collective-permute-start.3 = (f32[192,128]{1,0:T(8,128)S(1)}, f32[192,128]{1,0:T(8,128)S(1)}, u32[]{:S(2)}, u32[]{:S(2)}) collective-permute-start(f32[192,128]{1,0:T(8,128)S(1)} %get-tuple-element.25), channel_id=1, source_target_pairs={{0,6},{1,7},{2,4},{3,5},{4,2},{5,3},{6,0},{7,1},{8,14},{9,15},{10,... | collective-permute-start | bytes 294920 | tf_op jit(solution)/shard_map/ppermute | solution.py:433
  16.4 0.5 collective-permute-start.2
  16.9 0.2 collective-permute-start.1
  17.1 0.0 collective-permute-done.7
  17.2 2.9 %collective-permute-start.10 = (f32[192,128]{1,0:T(8,128)S(1)}, f32[192,128]{1,0:T(8,128)S(1)}, u32[]{:S(2)}, u32[]{:S(2)}) collective-permute-start(f32[192,128]{1,0:T(8,128)S(1)} %get-tuple-element.28), channel_id=1, source_target_pairs={{0,6},{1,7},{2,4},{3,5},{4,2},{5,3},{6,0},{7,1},{8,14},{9,15},{10,... | collective-permute-start | bytes 294920 | tf_op jit(solution)/shard_map/ppermute | solution.py:433
  20.1 0.5 collective-permute-start.9
  20.6 0.0 collective-permute-done.3
  20.6 1.4 %collective-permute-start.8 = (f32[192,128]{1,0:T(8,128)S(1)}, f32[192,128]{1,0:T(8,128)S(1)}, u32[]{:S(2)}, u32[]{:S(2)}) collective-permute-start(f32[192,128]{1,0:T(8,128)S(1)} %get-tuple-element.30), channel_id=1, source_target_pairs={{0,4},{1,5},{2,6},{3,7},{4,0},{5,1},{6,2},{7,3},{8,12},{9,13},{10,... | collective-permute-start | bytes 294920 | tf_op jit(solution)/shard_map/ppermute | solution.py:433
  21.9 0.7 collective-permute-done.2
  22.6 1.9 %collective-permute-done.1.other_ref = f32[216,128]{1,0:T(8,128)S(1)} collective-permute-done((f32[216,128]{1,0:T(8,128)S(1)}, f32[216,128]{1,0:T(8,128)S(1)}, u32[]{:S(2)}, u32[]{:S(2)}) %collective-permute-start.1) | collective-permute-done | bytes 110624 | tf_op jit(solution)/shard_map/ppermute | solution.py:433
  24.5 4.1 %collective-permute-start.6 = (f32[48,128]{1,0:T(8,128)S(1)}, f32[48,128]{1,0:T(8,128)S(1)}, u32[]{:S(2)}, u32[]{:S(2)}) collective-permute-start(f32[48,128]{1,0:T(8,128)S(1)} %get-tuple-element.31), channel_id=1, source_target_pairs={{0,24},{1,25},{2,26},{3,27},{4,28},{5,29},{6,30},{7,31},{8,16},{9,... | collective-permute-start | bytes 73736 | tf_op jit(solution)/shard_map/ppermute | solution.py:433
  28.7 0.0 collective-permute-start.5
  28.7 0.3 shard_map.70
  28.9 0.0 collective-permute-done.10
  29.0 0.7 collective-permute-start.4
  29.7 0.0 collective-permute-done.8
  29.7 3.8 %collective-permute-start.13 = (f32[48,128]{1,0:T(8,128)S(1)}, f32[48,128]{1,0:T(8,128)S(1)}, u32[]{:S(2)}, u32[]{:S(2)}) collective-permute-start(f32[48,128]{1,0:T(8,128)S(1)} %get-tuple-element.34), channel_id=1, source_target_pairs={{0,24},{1,25},{2,26},{3,27},{4,28},{5,29},{6,30},{7,31},{8,16},{9,... | collective-permute-start | bytes 73736 | tf_op jit(solution)/shard_map/ppermute | solution.py:433
  33.5 0.0 collective-permute-start.12
  33.5 0.6 collective-permute-start.11
  34.2 1.3 %collective-permute-done.13 = f32[48,128]{1,0:T(8,128)S(1)} collective-permute-done((f32[48,128]{1,0:T(8,128)S(1)}, f32[48,128]{1,0:T(8,128)S(1)}, u32[]{:S(2)}, u32[]{:S(2)}) %collective-permute-start.13) | collective-permute-done | bytes 24608 | tf_op jit(solution)/shard_map/ppermute | solution.py:433
  35.5 4.0 %collective-permute-done.12 = f32[48,128]{1,0:T(8,128)S(1)} collective-permute-done((f32[48,128]{1,0:T(8,128)S(1)}, f32[48,128]{1,0:T(8,128)S(1)}, u32[]{:S(2)}, u32[]{:S(2)}) %collective-permute-start.12) | collective-permute-done | bytes 24608 | tf_op jit(solution)/shard_map/ppermute | solution.py:433
  39.5 0.0 collective-permute-done.11
  39.5 0.7 collective-permute-start.16
  40.2 0.5 collective-permute-start.15
  40.7 3.3 %collective-permute-start.14 = (f32[48,256]{1,0:T(8,128)S(1)}, f32[48,256]{1,0:T(8,128)S(1)}, u32[]{:S(2)}, u32[]{:S(2)}) collective-permute-start(f32[48,256]{1,0:T(8,128)S(1)} %maximum_multiply_fusion), channel_id=1, source_target_pairs={{0,8},{1,9},{2,10},{3,11},{4,12},{5,13},{6,14},{7,15},{8,0},{9,1},... | collective-permute-start | bytes 147464 | tf_op jit(solution)/shard_map/ppermute | solution.py:433
  44.0 1.6 %collective-permute-done.16 = f32[48,256]{1,0:T(8,128)S(1)} collective-permute-done((f32[48,256]{1,0:T(8,128)S(1)}, f32[48,256]{1,0:T(8,128)S(1)}, u32[]{:S(2)}, u32[]{:S(2)}) %collective-permute-start.16) | collective-permute-done | bytes 49184 | tf_op jit(solution)/shard_map/ppermute | solution.py:433
  45.6 0.6 collective-permute-done.15
  46.2 0.1 collective-permute-start.20
  46.3 0.9 %collective-permute-start.19 = (f32[4,48,128]{2,1,0:T(8,128)S(1)}, f32[4,48,128]{2,1,0:T(8,128)S(1)}, u32[]{:S(2)}, u32[]{:S(2)}) collective-permute-start(f32[4,48,128]{2,1,0:T(8,128)S(1)} %pad_maximum_fusion.rest_0_.refs_0_), channel_id=1, source_target_pairs={{0,6},{1,7},{2,4},{3,5},{4,2},{5,3},{6,0},{7,1},{8,14},{9,15},{10,... | collective-permute-start | bytes 294920 | tf_op jit(solution)/shard_map/ppermute | solution.py:433
  47.2 2.1 %collective-permute-start.18 = (f32[4,48,128]{2,1,0:T(8,128)S(1)}, f32[4,48,128]{2,1,0:T(8,128)S(1)}, u32[]{:S(2)}, u32[]{:S(2)}) collective-permute-start(f32[4,48,128]{2,1,0:T(8,128)S(1)} %pad_maximum_fusion.rest_0_.refs_0_), channel_id=1, source_target_pairs={{0,2},{1,3},{2,0},{3,1},{4,6},{5,7},{6,4},{7,5},{8,10},{9,11},{10,... | collective-permute-start | bytes 294920 | tf_op jit(solution)/shard_map/ppermute | solution.py:433
  49.3 0.6 collective-permute-start.17
  49.9 0.9 %collective-permute-start.26 = (f32[4,48,128]{2,1,0:T(8,128)S(1)}, f32[4,48,128]{2,1,0:T(8,128)S(1)}, u32[]{:S(2)}, u32[]{:S(2)}) collective-permute-start(f32[4,48,128]{2,1,0:T(8,128)S(1)} %pad_maximum_fusion.1.rest_0_.refs_4_), channel_id=1, source_target_pairs={{0,6},{1,7},{2,4},{3,5},{4,2},{5,3},{6,0},{7,1},{8,14},{9,15},{10,... | collective-permute-start | bytes 294920 | tf_op jit(solution)/shard_map/ppermute | solution.py:433
  50.8 2.0 %collective-permute-start.25 = (f32[4,48,128]{2,1,0:T(8,128)S(1)}, f32[4,48,128]{2,1,0:T(8,128)S(1)}, u32[]{:S(2)}, u32[]{:S(2)}) collective-permute-start(f32[4,48,128]{2,1,0:T(8,128)S(1)} %pad_maximum_fusion.1.rest_0_.refs_4_), channel_id=1, source_target_pairs={{0,2},{1,3},{2,0},{3,1},{4,6},{5,7},{6,4},{7,5},{8,10},{9,11},{10,... | collective-permute-start | bytes 294920 | tf_op jit(solution)/shard_map/ppermute | solution.py:433
  52.8 0.1 collective-permute-done.19.rest_3_
  52.9 1.4 %collective-permute-start.24 = (f32[4,48,128]{2,1,0:T(8,128)S(1)}, f32[4,48,128]{2,1,0:T(8,128)S(1)}, u32[]{:S(2)}, u32[]{:S(2)}) collective-permute-start(f32[4,48,128]{2,1,0:T(8,128)S(1)} %pad_maximum_fusion.1.rest_0_.refs_4_), channel_id=1, source_target_pairs={{0,4},{1,5},{2,6},{3,7},{4,0},{5,1},{6,2},{7,3},{8,12},{9,13},{10,... | collective-permute-start | bytes 294920 | tf_op jit(solution)/shard_map/ppermute | solution.py:433
  54.3 0.8 %collective-permute-done.18.rest_2_.refs_2_ = f32[4,48,128]{2,1,0:T(8,128)S(1)} collective-permute-done((f32[4,48,128]{2,1,0:T(8,128)S(1)}, f32[4,48,128]{2,1,0:T(8,128)S(1)}, u32[]{:S(2)}, u32[]{:S(2)}) %collective-permute-start.18) | collective-permute-done | bytes 98336 | tf_op jit(solution)/shard_map/ppermute | solution.py:433
  55.1 0.0 collective-permute-start.23
  55.1 0.0 collective-permute-done.17.rest_1_
  55.1 0.5 collective-permute-start.22
  55.6 1.6 %collective-permute-done.26.rest_3_ = f32[4,48,128]{2,1,0:T(8,128)S(1)} collective-permute-done((f32[4,48,128]{2,1,0:T(8,128)S(1)}, f32[4,48,128]{2,1,0:T(8,128)S(1)}, u32[]{:S(2)}, u32[]{:S(2)}) %collective-permute-start.26) | collective-permute-done | bytes 98336 | tf_op jit(solution)/shard_map/ppermute | solution.py:433
  57.2 0.0 collective-permute-start.27
  57.2 1.5 %collective-permute-done.25.rest_2_.refs_6_ = f32[4,48,128]{2,1,0:T(8,128)S(1)} collective-permute-done((f32[4,48,128]{2,1,0:T(8,128)S(1)}, f32[4,48,128]{2,1,0:T(8,128)S(1)}, u32[]{:S(2)}, u32[]{:S(2)}) %collective-permute-start.25) | collective-permute-done | bytes 98336 | tf_op jit(solution)/shard_map/ppermute | solution.py:433
  58.7 0.5 collective-permute-start.30
  59.2 0.1 collective-permute-start.29
  59.3 0.4 collective-permute-start.28
  59.7 0.3 collective-permute-done.21.rest_5_
  60.0 1.0 %shard_map.71.total_ref = f32[288,96]{1,0:T(8,128)S(1)} custom-call(bf16[32,96,256]{2,1,0:T(8,128)(2,1)S(1)} %get-tuple-element.13.xh_ref, bf16[32,96,256]{2,1,0:T(8,128)(2,1)S(1)} %get-tuple-element.14.xl_ref, f32[4,48,128]{2,1,0:T(8,128)S(1)} %pad_maximum_fusion.rest_0_.refs_0_, f32[4,48,128]{2,1,0:T(8,128)S(1)} %collective-permute-done.17.rest_1_, ...), custom_call_target="tpu_custom_call" | custom-call | tf_op jit(solution)/shard_map/pallas_call | solution.py:345
  61.1 1.4 %shard_map.72 = f32[48,96]{1,0:T(8,128)S(1)} custom-call(bf16[32,96,256]{2,1,0:T(8,128)(2,1)S(1)} %get-tuple-element.13.xh_ref, bf16[32,96,256]{2,1,0:T(8,128)(2,1)S(1)} %get-tuple-element.14.xl_ref, f32[48,96]{1,0:T(8,128)S(1)} %get-tuple-element.15.w_ref, f32[288,96]{1,0:T(8,128)S(1)} %shard_map.71.total_ref, ...), custom_call_target="tpu_custom_call" | custom-call | tf_op jit(solution)/shard_map/pallas_call | solution.py:369
  62.5 0.7 collective-permute-start.31
  63.2 3.2 %collective-permute-done.31 = f32[48,96]{1,0:T(8,128)S(1)} collective-permute-done((f32[48,96]{1,0:T(8,128)S(1)}, f32[48,96]{1,0:T(8,128)S(1)}, u32[]{:S(2)}, u32[]{:S(2)}) %collective-permute-start.31) | collective-permute-done | bytes 18464 | tf_op jit(solution)/shard_map/ppermute | solution.py:433
  66.4 2.1 %collective-permute-start.34 = (f32[2,48,96]{2,1,0:T(8,128)S(1)}, f32[2,48,96]{2,1,0:T(8,128)S(1)}, u32[]{:S(2)}, u32[]{:S(2)}) collective-permute-start(f32[2,48,96]{2,1,0:T(8,128)S(1)} %pad_maximum_fusion.2.refs_0_), channel_id=1, source_target_pairs={{0,24},{1,25},{2,26},{3,27},{4,28},{5,29},{6,30},{7,31},{8,16},{9,... | collective-permute-start | bytes 110600 | tf_op jit(solution)/shard_map/ppermute | solution.py:433
  68.6 0.9 %collective-permute-start.33 = (f32[2,48,96]{2,1,0:T(8,128)S(1)}, f32[2,48,96]{2,1,0:T(8,128)S(1)}, u32[]{:S(2)}, u32[]{:S(2)}) collective-permute-start(f32[2,48,96]{2,1,0:T(8,128)S(1)} %pad_maximum_fusion.2.refs_0_), channel_id=1, source_target_pairs={{0,16},{1,17},{2,18},{3,19},{4,20},{5,21},{6,22},{7,23},{8,24},{9,... | collective-permute-start | bytes 110600 | tf_op jit(solution)/shard_map/ppermute | solution.py:433
  69.5 1.4 %collective-permute-start.32 = (f32[2,48,96]{2,1,0:T(8,128)S(1)}, f32[2,48,96]{2,1,0:T(8,128)S(1)}, u32[]{:S(2)}, u32[]{:S(2)}) collective-permute-start(f32[2,48,96]{2,1,0:T(8,128)S(1)} %pad_maximum_fusion.2.refs_0_), channel_id=1, source_target_pairs={{0,8},{1,9},{2,10},{3,11},{4,12},{5,13},{6,14},{7,15},{8,0},{9,1},... | collective-permute-start | bytes 110600 | tf_op jit(solution)/shard_map/ppermute | solution.py:433
  70.9 1.0 %shard_map.74 = f32[32,32,48]{2,1,0:T(8,128)} custom-call(f32[4,48,128]{2,1,0:T(8,128)S(1)} %pad_maximum_fusion.rest_0_.refs_0_, f32[4,48,128]{2,1,0:T(8,128)S(1)} %collective-permute-done.20.rest_4_.refs_1_, f32[4,48,128]{2,1,0:T(8,128)S(1)} %collective-permute-done.18.rest_2_.refs_2_, f32[4,48,128]{2,1,0:T(8,128)S(1)} %collective-permute-done.22.rest_6_.refs_3_, ...), custom_call_target="tpu_custom_call" | custom-call | tf_op jit(solution)/shard_map/pallas_call | solution.py:390
  71.9 0.9 %collective-permute-done.34.refs_3_ = f32[2,48,96]{2,1,0:T(8,128)S(1)} collective-permute-done((f32[2,48,96]{2,1,0:T(8,128)S(1)}, f32[2,48,96]{2,1,0:T(8,128)S(1)}, u32[]{:S(2)}, u32[]{:S(2)}) %collective-permute-start.34) | collective-permute-done | bytes 36896 | tf_op jit(solution)/shard_map/ppermute | solution.py:433
  72.8 1.3 %collective-permute-done.33.refs_2_ = f32[2,48,96]{2,1,0:T(8,128)S(1)} collective-permute-done((f32[2,48,96]{2,1,0:T(8,128)S(1)}, f32[2,48,96]{2,1,0:T(8,128)S(1)}, u32[]{:S(2)}, u32[]{:S(2)}) %collective-permute-start.33) | collective-permute-done | bytes 36896 | tf_op jit(solution)/shard_map/ppermute | solution.py:433
  74.1 0.0 collective-permute-done.32.refs_1_
  74.1 0.8 %shard_map.73 = f32[48,768]{1,0:T(8,128)} custom-call(f32[2,48,96]{2,1,0:T(8,128)S(1)} %pad_maximum_fusion.2.refs_0_, f32[2,48,96]{2,1,0:T(8,128)S(1)} %collective-permute-done.32.refs_1_, f32[2,48,96]{2,1,0:T(8,128)S(1)} %collective-permute-done.33.refs_2_, f32[2,48,96]{2,1,0:T(8,128)S(1)} %collective-permute-done.34.refs_3_), custom_call_target="tpu_custom_call" | custom-call | tf_op jit(solution)/shard_map/pallas_call | solution.py:417
  (30 shorter events, 0.2 us)
Async XLA Ops:
  10.4 1.9 %collective-permute-start = (f32[792,128]{1,0:T(8,128)S(1)}, f32[792,128]{1,0:T(8,128)S(1)}, u32[]{:S(2)}, u32[]{:S(2)}) collective-permute-start(f32[792,128]{1,0:T(8,128)S(1)} %get-tuple-element.17), channel_id=1, source_target_pairs={{0,1},{1,0},{2,3},{3,2},{4,5},{5,4},{6,7},{7,6},{8,9},{9,8},{10,11... | collective-permute-start | bytes 1216520 | tf_op jit(solution)/shard_map/ppermute | solution.py:433
  11.6 17.0 %copy-start = (f32[48,32,32]{0,2,1:T(8,128)S(1)}, f32[48,32,32]{0,2,1:T(8,128)}, u32[]{:S(2)}) copy-start(f32[48,32,32]{0,2,1:T(8,128)} %param.9) | copy-start | bytes 589828
  12.3 4.8 %collective-permute-start.7 = (f32[768,128]{1,0:T(8,128)S(1)}, f32[768,128]{1,0:T(8,128)S(1)}, u32[]{:S(2)}, u32[]{:S(2)}) collective-permute-start(f32[768,128]{1,0:T(8,128)S(1)} %get-tuple-element.23), channel_id=1, source_target_pairs={{0,1},{1,0},{2,3},{3,2},{4,5},{5,4},{6,7},{7,6},{8,9},{9,8},{10,11... | collective-permute-start | bytes 1179656 | tf_op jit(solution)/shard_map/ppermute | solution.py:433
  12.7 7.8 %collective-permute-start.3 = (f32[192,128]{1,0:T(8,128)S(1)}, f32[192,128]{1,0:T(8,128)S(1)}, u32[]{:S(2)}, u32[]{:S(2)}) collective-permute-start(f32[192,128]{1,0:T(8,128)S(1)} %get-tuple-element.25), channel_id=1, source_target_pairs={{0,6},{1,7},{2,4},{3,5},{4,2},{5,3},{6,0},{7,1},{8,14},{9,15},{10,... | collective-permute-start | bytes 294920 | tf_op jit(solution)/shard_map/ppermute | solution.py:433
  16.4 6.2 %collective-permute-start.2 = (f32[192,128]{1,0:T(8,128)S(1)}, f32[192,128]{1,0:T(8,128)S(1)}, u32[]{:S(2)}, u32[]{:S(2)}) collective-permute-start(f32[192,128]{1,0:T(8,128)S(1)} %get-tuple-element.26), channel_id=1, source_target_pairs={{0,4},{1,5},{2,6},{3,7},{4,0},{5,1},{6,2},{7,3},{8,12},{9,13},{10,... | collective-permute-start | bytes 294920 | tf_op jit(solution)/shard_map/ppermute | solution.py:433
  16.9 7.6 %collective-permute-start.1 = (f32[216,128]{1,0:T(8,128)S(1)}, f32[216,128]{1,0:T(8,128)S(1)}, u32[]{:S(2)}, u32[]{:S(2)}) collective-permute-start(f32[216,128]{1,0:T(8,128)S(1)} %slice_add_fusion.mine_ref), channel_id=1, source_target_pairs={{0,2},{1,3},{2,0},{3,1},{4,6},{5,7},{6,4},{7,5},{8,10},{9,11},{10,... | collective-permute-start | bytes 331784 | tf_op jit(solution)/shard_map/ppermute | solution.py:433
  17.2 11.8 %collective-permute-start.10 = (f32[192,128]{1,0:T(8,128)S(1)}, f32[192,128]{1,0:T(8,128)S(1)}, u32[]{:S(2)}, u32[]{:S(2)}) collective-permute-start(f32[192,128]{1,0:T(8,128)S(1)} %get-tuple-element.28), channel_id=1, source_target_pairs={{0,6},{1,7},{2,4},{3,5},{4,2},{5,3},{6,0},{7,1},{8,14},{9,15},{10,... | collective-permute-start | bytes 294920 | tf_op jit(solution)/shard_map/ppermute | solution.py:433
  20.1 9.6 %collective-permute-start.9 = (f32[192,128]{1,0:T(8,128)S(1)}, f32[192,128]{1,0:T(8,128)S(1)}, u32[]{:S(2)}, u32[]{:S(2)}) collective-permute-start(f32[192,128]{1,0:T(8,128)S(1)} %get-tuple-element.29), channel_id=1, source_target_pairs={{0,2},{1,3},{2,0},{3,1},{4,6},{5,7},{6,4},{7,5},{8,10},{9,11},{10,... | collective-permute-start | bytes 294920 | tf_op jit(solution)/shard_map/ppermute | solution.py:433
  20.6 9.1 %collective-permute-start.8 = (f32[192,128]{1,0:T(8,128)S(1)}, f32[192,128]{1,0:T(8,128)S(1)}, u32[]{:S(2)}, u32[]{:S(2)}) collective-permute-start(f32[192,128]{1,0:T(8,128)S(1)} %get-tuple-element.30), channel_id=1, source_target_pairs={{0,4},{1,5},{2,6},{3,7},{4,0},{5,1},{6,2},{7,3},{8,12},{9,13},{10,... | collective-permute-start | bytes 294920 | tf_op jit(solution)/shard_map/ppermute | solution.py:433
  24.5 9.0 %collective-permute-start.6 = (f32[48,128]{1,0:T(8,128)S(1)}, f32[48,128]{1,0:T(8,128)S(1)}, u32[]{:S(2)}, u32[]{:S(2)}) collective-permute-start(f32[48,128]{1,0:T(8,128)S(1)} %get-tuple-element.31), channel_id=1, source_target_pairs={{0,24},{1,25},{2,26},{3,27},{4,28},{5,29},{6,30},{7,31},{8,16},{9,... | collective-permute-start | bytes 73736 | tf_op jit(solution)/shard_map/ppermute | solution.py:433
  28.7 5.5 %collective-permute-start.5 = (f32[48,128]{1,0:T(8,128)S(1)}, f32[48,128]{1,0:T(8,128)S(1)}, u32[]{:S(2)}, u32[]{:S(2)}) collective-permute-start(f32[48,128]{1,0:T(8,128)S(1)} %get-tuple-element.32), channel_id=1, source_target_pairs={{0,16},{1,17},{2,18},{3,19},{4,20},{5,21},{6,22},{7,23},{8,24},{9,... | collective-permute-start | bytes 73736 | tf_op jit(solution)/shard_map/ppermute | solution.py:433
  29.0 5.2 %collective-permute-start.4 = (f32[48,128]{1,0:T(8,128)S(1)}, f32[48,128]{1,0:T(8,128)S(1)}, u32[]{:S(2)}, u32[]{:S(2)}) collective-permute-start(f32[48,128]{1,0:T(8,128)S(1)} %get-tuple-element.33), channel_id=1, source_target_pairs={{0,8},{1,9},{2,10},{3,11},{4,12},{5,13},{6,14},{7,15},{8,0},{9,1},... | collective-permute-start | bytes 73736 | tf_op jit(solution)/shard_map/ppermute | solution.py:433
  29.7 5.8 %collective-permute-start.13 = (f32[48,128]{1,0:T(8,128)S(1)}, f32[48,128]{1,0:T(8,128)S(1)}, u32[]{:S(2)}, u32[]{:S(2)}) collective-permute-start(f32[48,128]{1,0:T(8,128)S(1)} %get-tuple-element.34), channel_id=1, source_target_pairs={{0,24},{1,25},{2,26},{3,27},{4,28},{5,29},{6,30},{7,31},{8,16},{9,... | collective-permute-start | bytes 73736 | tf_op jit(solution)/shard_map/ppermute | solution.py:433
  33.5 6.0 %collective-permute-start.12 = (f32[48,128]{1,0:T(8,128)S(1)}, f32[48,128]{1,0:T(8,128)S(1)}, u32[]{:S(2)}, u32[]{:S(2)}) collective-permute-start(f32[48,128]{1,0:T(8,128)S(1)} %get-tuple-element.35), channel_id=1, source_target_pairs={{0,16},{1,17},{2,18},{3,19},{4,20},{5,21},{6,22},{7,23},{8,24},{9,... | collective-permute-start | bytes 73736 | tf_op jit(solution)/shard_map/ppermute | solution.py:433
  33.5 6.0 %collective-permute-start.11 = (f32[48,128]{1,0:T(8,128)S(1)}, f32[48,128]{1,0:T(8,128)S(1)}, u32[]{:S(2)}, u32[]{:S(2)}) collective-permute-start(f32[48,128]{1,0:T(8,128)S(1)} %get-tuple-element.36), channel_id=1, source_target_pairs={{0,8},{1,9},{2,10},{3,11},{4,12},{5,13},{6,14},{7,15},{8,0},{9,1},... | collective-permute-start | bytes 73736 | tf_op jit(solution)/shard_map/ppermute | solution.py:433
  39.5 6.1 %collective-permute-start.16 = (f32[48,256]{1,0:T(8,128)S(1)}, f32[48,256]{1,0:T(8,128)S(1)}, u32[]{:S(2)}, u32[]{:S(2)}) collective-permute-start(f32[48,256]{1,0:T(8,128)S(1)} %maximum_multiply_fusion), channel_id=1, source_target_pairs={{0,24},{1,25},{2,26},{3,27},{4,28},{5,29},{6,30},{7,31},{8,16},{9,... | collective-permute-start | bytes 147464 | tf_op jit(solution)/shard_map/ppermute | solution.py:433
  40.2 6.0 %collective-permute-start.15 = (f32[48,256]{1,0:T(8,128)S(1)}, f32[48,256]{1,0:T(8,128)S(1)}, u32[]{:S(2)}, u32[]{:S(2)}) collective-permute-start(f32[48,256]{1,0:T(8,128)S(1)} %maximum_multiply_fusion), channel_id=1, source_target_pairs={{0,16},{1,17},{2,18},{3,19},{4,20},{5,21},{6,22},{7,23},{8,24},{9,... | collective-permute-start | bytes 147464 | tf_op jit(solution)/shard_map/ppermute | solution.py:433
  40.7 5.5 %collective-permute-start.14 = (f32[48,256]{1,0:T(8,128)S(1)}, f32[48,256]{1,0:T(8,128)S(1)}, u32[]{:S(2)}, u32[]{:S(2)}) collective-permute-start(f32[48,256]{1,0:T(8,128)S(1)} %maximum_multiply_fusion), channel_id=1, source_target_pairs={{0,8},{1,9},{2,10},{3,11},{4,12},{5,13},{6,14},{7,15},{8,0},{9,1},... | collective-permute-start | bytes 147464 | tf_op jit(solution)/shard_map/ppermute | solution.py:433
  46.2 4.6 %collective-permute-start.20 = (f32[4,48,128]{2,1,0:T(8,128)S(1)}, f32[4,48,128]{2,1,0:T(8,128)S(1)}, u32[]{:S(2)}, u32[]{:S(2)}) collective-permute-start(f32[4,48,128]{2,1,0:T(8,128)S(1)} %pad_maximum_fusion.rest_0_.refs_0_), channel_id=1, source_target_pairs={{0,1},{1,0},{2,3},{3,2},{4,5},{5,4},{6,7},{7,6},{8,9},{9,8},{10,11... | collective-permute-start | bytes 294920 | tf_op jit(solution)/shard_map/ppermute | solution.py:433
  46.3 6.6 %collective-permute-start.19 = (f32[4,48,128]{2,1,0:T(8,128)S(1)}, f32[4,48,128]{2,1,0:T(8,128)S(1)}, u32[]{:S(2)}, u32[]{:S(2)}) collective-permute-start(f32[4,48,128]{2,1,0:T(8,128)S(1)} %pad_maximum_fusion.rest_0_.refs_0_), channel_id=1, source_target_pairs={{0,6},{1,7},{2,4},{3,5},{4,2},{5,3},{6,0},{7,1},{8,14},{9,15},{10,... | collective-permute-start | bytes 294920 | tf_op jit(solution)/shard_map/ppermute | solution.py:433
  47.2 7.9 %collective-permute-start.18 = (f32[4,48,128]{2,1,0:T(8,128)S(1)}, f32[4,48,128]{2,1,0:T(8,128)S(1)}, u32[]{:S(2)}, u32[]{:S(2)}) collective-permute-start(f32[4,48,128]{2,1,0:T(8,128)S(1)} %pad_maximum_fusion.rest_0_.refs_0_), channel_id=1, source_target_pairs={{0,2},{1,3},{2,0},{3,1},{4,6},{5,7},{6,4},{7,5},{8,10},{9,11},{10,... | collective-permute-start | bytes 294920 | tf_op jit(solution)/shard_map/ppermute | solution.py:433
  49.3 5.8 %collective-permute-start.17 = (f32[4,48,128]{2,1,0:T(8,128)S(1)}, f32[4,48,128]{2,1,0:T(8,128)S(1)}, u32[]{:S(2)}, u32[]{:S(2)}) collective-permute-start(f32[4,48,128]{2,1,0:T(8,128)S(1)} %pad_maximum_fusion.rest_0_.refs_0_), channel_id=1, source_target_pairs={{0,4},{1,5},{2,6},{3,7},{4,0},{5,1},{6,2},{7,3},{8,12},{9,13},{10,... | collective-permute-start | bytes 294920 | tf_op jit(solution)/shard_map/ppermute | solution.py:433
  49.9 7.3 %collective-permute-start.26 = (f32[4,48,128]{2,1,0:T(8,128)S(1)}, f32[4,48,128]{2,1,0:T(8,128)S(1)}, u32[]{:S(2)}, u32[]{:S(2)}) collective-permute-start(f32[4,48,128]{2,1,0:T(8,128)S(1)} %pad_maximum_fusion.1.rest_0_.refs_4_), channel_id=1, source_target_pairs={{0,6},{1,7},{2,4},{3,5},{4,2},{5,3},{6,0},{7,1},{8,14},{9,15},{10,... | collective-permute-start | bytes 294920 | tf_op jit(solution)/shard_map/ppermute | solution.py:433
  50.8 7.9 %collective-permute-start.25 = (f32[4,48,128]{2,1,0:T(8,128)S(1)}, f32[4,48,128]{2,1,0:T(8,128)S(1)}, u32[]{:S(2)}, u32[]{:S(2)}) collective-permute-start(f32[4,48,128]{2,1,0:T(8,128)S(1)} %pad_maximum_fusion.1.rest_0_.refs_4_), channel_id=1, source_target_pairs={{0,2},{1,3},{2,0},{3,1},{4,6},{5,7},{6,4},{7,5},{8,10},{9,11},{10,... | collective-permute-start | bytes 294920 | tf_op jit(solution)/shard_map/ppermute | solution.py:433
  52.9 5.8 %collective-permute-start.24 = (f32[4,48,128]{2,1,0:T(8,128)S(1)}, f32[4,48,128]{2,1,0:T(8,128)S(1)}, u32[]{:S(2)}, u32[]{:S(2)}) collective-permute-start(f32[4,48,128]{2,1,0:T(8,128)S(1)} %pad_maximum_fusion.1.rest_0_.refs_4_), channel_id=1, source_target_pairs={{0,4},{1,5},{2,6},{3,7},{4,0},{5,1},{6,2},{7,3},{8,12},{9,13},{10,... | collective-permute-start | bytes 294920 | tf_op jit(solution)/shard_map/ppermute | solution.py:433
  55.1 4.1 %collective-permute-start.23 = (f32[4,48,128]{2,1,0:T(8,128)S(1)}, f32[4,48,128]{2,1,0:T(8,128)S(1)}, u32[]{:S(2)}, u32[]{:S(2)}) collective-permute-start(f32[4,48,128]{2,1,0:T(8,128)S(1)} %collective-permute-done.19.rest_3_), channel_id=1, source_target_pairs={{0,1},{1,0},{2,3},{3,2},{4,5},{5,4},{6,7},{7,6},{8,9},{9,8},{10,11... | collective-permute-start | bytes 294920 | tf_op jit(solution)/shard_map/ppermute | solution.py:433
  55.1 4.2 %collective-permute-start.22 = (f32[4,48,128]{2,1,0:T(8,128)S(1)}, f32[4,48,128]{2,1,0:T(8,128)S(1)}, u32[]{:S(2)}, u32[]{:S(2)}) collective-permute-start(f32[4,48,128]{2,1,0:T(8,128)S(1)} %collective-permute-done.18.rest_2_.refs_2_), channel_id=1, source_target_pairs={{0,1},{1,0},{2,3},{3,2},{4,5},{5,4},{6,7},{7,6},{8,9},{9,8},{10,11... | collective-permute-start | bytes 294920 | tf_op jit(solution)/shard_map/ppermute | solution.py:433
  57.2 3.9 %collective-permute-start.27 = (f32[4,48,128]{2,1,0:T(8,128)S(1)}, f32[4,48,128]{2,1,0:T(8,128)S(1)}, u32[]{:S(2)}, u32[]{:S(2)}) collective-permute-start(f32[4,48,128]{2,1,0:T(8,128)S(1)} %pad_maximum_fusion.1.rest_0_.refs_4_), channel_id=1, source_target_pairs={{0,1},{1,0},{2,3},{3,2},{4,5},{5,4},{6,7},{7,6},{8,9},{9,8},{10,11... | collective-permute-start | bytes 294920 | tf_op jit(solution)/shard_map/ppermute | solution.py:433
  58.7 1.3 %collective-permute-start.21 = (f32[4,48,128]{2,1,0:T(8,128)S(1)}, f32[4,48,128]{2,1,0:T(8,128)S(1)}, u32[]{:S(2)}, u32[]{:S(2)}) collective-permute-start(f32[4,48,128]{2,1,0:T(8,128)S(1)} %collective-permute-done.17.rest_1_), channel_id=1, source_target_pairs={{0,1},{1,0},{2,3},{3,2},{4,5},{5,4},{6,7},{7,6},{8,9},{9,8},{10,11... | collective-permute-start | bytes 294920 | tf_op jit(solution)/shard_map/ppermute | solution.py:433
  58.7 2.4 %collective-permute-start.30 = (f32[4,48,128]{2,1,0:T(8,128)S(1)}, f32[4,48,128]{2,1,0:T(8,128)S(1)}, u32[]{:S(2)}, u32[]{:S(2)}) collective-permute-start(f32[4,48,128]{2,1,0:T(8,128)S(1)} %collective-permute-done.26.rest_3_), channel_id=1, source_target_pairs={{0,1},{1,0},{2,3},{3,2},{4,5},{5,4},{6,7},{7,6},{8,9},{9,8},{10,11... | collective-permute-start | bytes 294920 | tf_op jit(solution)/shard_map/ppermute | solution.py:433
  59.2 1.9 %collective-permute-start.29 = (f32[4,48,128]{2,1,0:T(8,128)S(1)}, f32[4,48,128]{2,1,0:T(8,128)S(1)}, u32[]{:S(2)}, u32[]{:S(2)}) collective-permute-start(f32[4,48,128]{2,1,0:T(8,128)S(1)} %collective-permute-done.25.rest_2_.refs_6_), channel_id=1, source_target_pairs={{0,1},{1,0},{2,3},{3,2},{4,5},{5,4},{6,7},{7,6},{8,9},{9,8},{10,11... | collective-permute-start | bytes 294920 | tf_op jit(solution)/shard_map/ppermute | solution.py:433
  59.3 1.8 %collective-permute-start.28 = (f32[4,48,128]{2,1,0:T(8,128)S(1)}, f32[4,48,128]{2,1,0:T(8,128)S(1)}, u32[]{:S(2)}, u32[]{:S(2)}) collective-permute-start(f32[4,48,128]{2,1,0:T(8,128)S(1)} %collective-permute-done.24.rest_1_), channel_id=1, source_target_pairs={{0,1},{1,0},{2,3},{3,2},{4,5},{5,4},{6,7},{7,6},{8,9},{9,8},{10,11... | collective-permute-start | bytes 294920 | tf_op jit(solution)/shard_map/ppermute | solution.py:433
  62.5 3.9 %collective-permute-start.31 = (f32[48,96]{1,0:T(8,128)S(1)}, f32[48,96]{1,0:T(8,128)S(1)}, u32[]{:S(2)}, u32[]{:S(2)}) collective-permute-start(f32[48,96]{1,0:T(8,128)S(1)} %shard_map.72), channel_id=1, source_target_pairs={{0,4},{1,5},{2,6},{3,7},{4,0},{5,1},{6,2},{7,3},{8,12},{9,13},{10,... | collective-permute-start | bytes 55304 | tf_op jit(solution)/shard_map/ppermute | solution.py:433
  66.4 6.3 %collective-permute-start.34 = (f32[2,48,96]{2,1,0:T(8,128)S(1)}, f32[2,48,96]{2,1,0:T(8,128)S(1)}, u32[]{:S(2)}, u32[]{:S(2)}) collective-permute-start(f32[2,48,96]{2,1,0:T(8,128)S(1)} %pad_maximum_fusion.2.refs_0_), channel_id=1, source_target_pairs={{0,24},{1,25},{2,26},{3,27},{4,28},{5,29},{6,30},{7,31},{8,16},{9,... | collective-permute-start | bytes 110600 | tf_op jit(solution)/shard_map/ppermute | solution.py:433
  68.6 5.5 %collective-permute-start.33 = (f32[2,48,96]{2,1,0:T(8,128)S(1)}, f32[2,48,96]{2,1,0:T(8,128)S(1)}, u32[]{:S(2)}, u32[]{:S(2)}) collective-permute-start(f32[2,48,96]{2,1,0:T(8,128)S(1)} %pad_maximum_fusion.2.refs_0_), channel_id=1, source_target_pairs={{0,16},{1,17},{2,18},{3,19},{4,20},{5,21},{6,22},{7,23},{8,24},{9,... | collective-permute-start | bytes 110600 | tf_op jit(solution)/shard_map/ppermute | solution.py:433
  69.5 4.6 %collective-permute-start.32 = (f32[2,48,96]{2,1,0:T(8,128)S(1)}, f32[2,48,96]{2,1,0:T(8,128)S(1)}, u32[]{:S(2)}, u32[]{:S(2)}) collective-permute-start(f32[2,48,96]{2,1,0:T(8,128)S(1)} %pad_maximum_fusion.2.refs_0_), channel_id=1, source_target_pairs={{0,8},{1,9},{2,10},{3,11},{4,12},{5,13},{6,14},{7,15},{8,0},{9,1},... | collective-permute-start | bytes 110600 | tf_op jit(solution)/shard_map/ppermute | solution.py:433

commit v15 on v12

--- a/solution.py
+++ b/solution.py
@@ -11,7 +11,7 @@
 BF16 = jnp.bfloat16
 LANES = 128
 GROUP = 16
-PIECES = 16
+PIECES = 32
 FOLDED = 24
 VMEM_LIMIT = 48 * 1024 * 1024
 
@@ -167,7 +167,7 @@
     xl_ref[:, planes_here, :] = low
 
 
-def blur_kernel(cube_hbm, taps_x_hbm, taps_y_hbm, w_hbm, xh_ref, xl_ref, w_here_ref, w_both_ref, keep_ref, give_ref,
+def blur_kernel(cube_hbm, taps_x_hbm, taps_y_hbm, w_hbm, xh_ref, xl_ref, w_here_ref, w_both_ref, part_ref,
                 cube_ref, taps_x_ref, taps_y_ref, w_ref, sems, chunk_sems, work_ref, kx_ref, ky_ref):
     taps = taps_x_ref.shape[0]
     margin = (taps - 1) // 2
@@ -209,8 +209,7 @@
 
     lax.fori_loop(0, groups, body, 0)
     gram = fold(band_gram(w_ref[...])[:, :rank])
-    keep_ref[PIECES * rank:] = gram
-    give_ref[PIECES * rank:] = gram
+    part_ref[PIECES * rank:] = gram
     planes = xh_ref.shape[1]
     band = w_ref.shape[1]
     shift = lax.rem(band - lax.axis_index("sp") * planes, band)
@@ -221,46 +220,46 @@
     w_high = w_here.astype(BF16).astype(F32)
     w_both = jnp.concatenate([w_high + pltpu.roll(w_high, planes, 1), w_here - w_high], axis=0).astype(BF16)
     w_both_ref[...] = w_both
-    project(xh_ref, xl_ref, w_both[:, :2 * planes], keep_ref, give_ref, 0)
-
-
-def project(xh_ref, xl_ref, w_both, keep_ref, give_ref, chain):
+    project(xh_ref, xl_ref, w_both[:, :2 * planes], part_ref, 0)
+
+
+def project(xh_ref, xl_ref, w_both, part_ref, chain):
     height = xh_ref.shape[0]
     rank = w_both.shape[0] // 2
     me_sp = lax.axis_index("sp")
     me_bd = lax.axis_index("bd")
     tall = height // lax.axis_size("bd")
     wide = 2 * LANES // lax.axis_size("sp")
-    for rel_bd in (1, 3, 0, 2):
-        first_row = lax.bitwise_xor(me_bd, rel_bd) * tall + 4 * chain
+    for side in range(4):
+        rel_row, core = side // 2, side % 2
+        first_row = (lax.bitwise_xor(me_bd // 2, rel_row) * 2 + core) * tall + 4 * chain
         sums = []
         for row in range(4):
             image = jnp.concatenate([xh_ref[first_row + row], xl_ref[first_row + row]], axis=0)
             both = dot(w_both, image)
             sums.append(both[:rank] + both[rank:])
-        part_ref = (keep_ref, give_ref)[rel_bd % 2]
         for column in range(2):
             pieces = exchange_blocks(
                 [value[:, column * LANES:(column + 1) * LANES] for value in sums], wide)
             for k in range(4):
                 rel_sp = lax.bitwise_xor(me_sp, column * 4 + k)
-                side = 3 - rel_sp % 2 if rel_bd // 2 else rel_sp % 2
-                first = pl.multiple_of((side * 4 + rel_sp // 2) * rank, 8)
+                place = 3 - rel_sp % 2 if rel_row else rel_sp % 2
+                first = pl.multiple_of(((place * 4 + rel_sp // 2) * 2 + core) * rank, 8)
                 part_ref[pl.ds(first, rank)] = pieces[k]
 
 
-def project_kernel(xh_ref, xl_ref, w_both_ref, keep_ref, give_ref):
+def project_kernel(xh_ref, xl_ref, w_both_ref, part_ref):
     planes = xh_ref.shape[1]
-    project(xh_ref, xl_ref, w_both_ref[:, :2 * planes], keep_ref, give_ref, 1)
+    project(xh_ref, xl_ref, w_both_ref[:, :2 * planes], part_ref, 1)
 
 
 def project_call(x_high, x_low, w_both):
     part = jax.ShapeDtypeStruct((PIECES * w_both.shape[0] // 2, LANES), F32)
     return pl.pallas_call(
         project_kernel,
-        out_shape=[part, part],
+        out_shape=part,
         in_specs=in_vmem(3),
-        out_specs=in_vmem(2),
+        out_specs=in_vmem(1)[0],
         compiler_params=pltpu.CompilerParams(vmem_limit_bytes=VMEM_LIMIT),
     )(x_high, x_low, w_both)
 
@@ -275,9 +274,9 @@
     in_hbm = [pltpu.with_memory_space_constraint(value, pltpu.HBM) for value in (cube, taps_x, taps_y, w_rows)]
     return pl.pallas_call(
         blur_kernel,
-        out_shape=[jax.ShapeDtypeStruct(image, BF16)] * 2 + [mine, both, first, first],
+        out_shape=[jax.ShapeDtypeStruct(image, BF16)] * 2 + [mine, both, first],
         in_specs=[pl.BlockSpec(memory_space=pltpu.HBM)] * 4,
-        out_specs=in_vmem(6),
+        out_specs=in_vmem(5),
         scratch_shapes=[pltpu.VMEM(value.shape, F32) for value in (cube, taps_x, taps_y, w_rows)]
         + [pltpu.SemaphoreType.DMA((3,)), pltpu.SemaphoreType.DMA((planes // GROUP,))]
         + [pltpu.VMEM((LANES, LANES), F32)] * 3,
@@ -287,22 +286,28 @@
 
 def ratio_kernel(mine_ref, other_ref, h_ref, out_ref):
     tall = h_ref.shape[0] // lax.axis_size("bd")
-    first = pl.multiple_of(lax.axis_index("bd") * tall, tall)
-    here = h_ref[pl.ds(first, tall)]
-    here = jnp.transpose(here.reshape(-1, here.shape[2]))
+    rank = h_ref.shape[2]
     rows = mine_ref.shape[0]
-    gram = unfold(mine_ref[rows - FOLDED:rows] + other_ref[rows - FOLDED:rows], here.shape[0])
-    out_ref[...] = here / dot_exact(gram, here)
+    gram = unfold(mine_ref[rows - FOLDED:rows] + other_ref[rows - FOLDED:rows], rank)
+    for core in range(2):
+        first = pl.multiple_of((lax.axis_index("bd") // 2 * 2 + core) * tall, tall)
+        here = h_ref[pl.ds(first, tall)]
+        here = jnp.transpose(here.reshape(-1, rank))
+        out_ref[core * rank:(core + 1) * rank] = here / dot_exact(gram, here)
 
 
 def ratio_call(mine, other, h_columns):
-    piece = jax.ShapeDtypeStruct((h_columns.shape[2], 2 * LANES), F32)
+    piece = jax.ShapeDtypeStruct((2 * h_columns.shape[2], 2 * LANES), F32)
     return pl.pallas_call(
         ratio_kernel,
         out_shape=piece,
         in_specs=in_vmem(3),
         compiler_params=pltpu.CompilerParams(vmem_limit_bytes=VMEM_LIMIT),
     )(mine, other, h_columns)
+
+
+def pick(own, received):
+    return jnp.where(lax.axis_index("bd") % 2 == 1, own, received)
 
 
 def accumulate(xh_ref, xl_ref, part_refs, all_ref, chain, total):
@@ -313,12 +318,14 @@
     pieces = lax.axis_size("sp")
     tall = height // bands
     wide = 2 * LANES // pieces
-    for slot, part_ref in enumerate(part_refs):
-        rel_bd = slot // 4 + 2 * ((slot // 2) % 2)
+    rank = all_ref.shape[1]
+    for partner in range(4):
+        row = lax.bitwise_xor(me_bd // 2, partner // 2)
         for inner in range(4):
-            rel_sp = slot % 2 + 2 * inner
-            owner = lax.bitwise_xor(me_bd, rel_bd) * pieces + lax.bitwise_xor(me_sp, rel_sp)
-            all_ref[owner] = part_ref[inner]
+            owner_sp = lax.bitwise_xor(me_sp, partner % 2 + 2 * inner)
+            both = pick(part_refs[partner][inner], part_refs[4 + partner][inner])
+            for core in range(2):
+                all_ref[(2 * row + core) * pieces + owner_sp] = both[core * rank:(core + 1) * rank]
     for part in range(bands):
         first_row = part * tall + 4 * chain
         halves = [
@@ -341,7 +348,7 @@
 
 def first_call(x_high, x_low, parts):
     _, planes, _ = x_high.shape
-    rank = parts[0].shape[1]
+    rank = parts[0].shape[1] // 2
     return pl.pallas_call(
         first_kernel,
         out_shape=jax.ShapeDtypeStruct((2 * (planes + rank), 2 * rank), F32),
@@ -379,11 +386,15 @@
     h_out = refs[-1]
     me_bd = lax.axis_index("bd")
     tall = h_out.shape[0] // lax.axis_size("bd")
+    rank = h_out.shape[2]
     for chain in range(2):
-        for rel_bd in range(4):
-            piece = refs[4 * chain + rel_bd][0]
-            first = lax.bitwise_xor(me_bd, rel_bd) * tall + 4 * chain
-            h_out[pl.ds(first, 4)] = jnp.transpose(piece).reshape((4,) + h_out.shape[1:])
+        for rel_row in range(2):
+            own_ref, received_ref = refs[4 * chain + 2 * rel_row:4 * chain + 2 * rel_row + 2]
+            both = pick(own_ref[0], received_ref[0])
+            for core in range(2):
+                first = (lax.bitwise_xor(me_bd // 2, rel_row) * 2 + core) * tall + 4 * chain
+                piece = jnp.transpose(both[core * rank:(core + 1) * rank])
+                h_out[pl.ds(first, 4)] = piece.reshape((4,) + h_out.shape[1:])
 
 
 def place_h_call(parts, shape):
@@ -433,18 +444,23 @@
     return lax.ppermute(value, ("sp", "bd"), pairs)
 
 
-def around(values):
-    return [send(values[k], k % 2, 2 * (k // 2)) for k in range(1, 4)]
-
-
-def spread(value, chain):
-    if chain == 0:
-        column, row = send(value, 1, 0), send(value, 0, 2)
-        corner = send(row, 1, 0)
-    else:
-        row, column = send(value, 0, 2), send(value, 1, 0)
-        corner = send(column, 0, 2)
-    return [value, column, row, corner]
+def send_odd(value, mask_sp, mask_bd):
+    bands = lax.axis_size("bd")
+    pieces = lax.axis_size("sp")
+    pairs = []
+    for s in range(pieces):
+        for b in range(1, bands, 2):
+            pairs.append((s * bands + b, (s ^ mask_sp) * bands + (b ^ mask_bd)))
+    return lax.ppermute(value, ("sp", "bd"), pairs)
+
+
+def send_core(value, source):
+    count = lax.axis_size("bd") * lax.axis_size("sp")
+    return lax.ppermute(value, ("sp", "bd"), [(d, d ^ 1) for d in range(source, count, 2)])
+
+
+def around(value):
+    return [send_odd(value[k], k % 2, 2 * (k // 2)) for k in range(1, 4)]
 
 
 def local(cube, taps_x, taps_y, factor_w, factor_h):
@@ -453,37 +469,36 @@
     taps_y = jnp.transpose(taps_y, (2, 0, 1))
     h_columns = jnp.transpose(factor_h, (1, 2, 0))
     rank = w_rows.shape[0]
-    x_high, x_low, w_here, w_both, keep_0, give_0 = blur_call(cube[0], taps_x, taps_y, w_rows)
+    x_high, x_low, w_here, w_both, part_0 = blur_call(cube[0], taps_x, taps_y, w_rows)
+    taken_0 = send_core(part_0, 0)
+    part_1 = project_call(x_high, x_low, w_both)
+    taken_0, part_1 = lax.optimization_barrier((taken_0, part_1))
     chains = []
-    taken_0 = send(give_0, 0, 1)
-    keep_1, give_1 = project_call(x_high, x_low, w_both)
-    taken_0, keep_1, give_1 = lax.optimization_barrier((taken_0, keep_1, give_1))
-    for keep, taken in ((keep_0, taken_0), (keep_1, send(give_1, 0, 1))):
-        bounds = [place * 4 * rank for place in (0, 1, 3, 2)]
+    for part, taken in ((part_0, taken_0), (part_1, send_core(part_1, 0))):
+        bounds = [place * 8 * rank for place in (0, 1, 3, 2)]
         sides = []
         for first in bounds:
-            last = keep.shape[0] if first == max(bounds) else first + 4 * rank
-            sides.append(keep[first:last] + taken[first:last])
+            last = part.shape[0] if first == max(bounds) else first + 8 * rank
+            sides.append(part[first:last] + taken[first:last])
         chains.append((sides, around(sides)))
     ratio = ratio_call(chains[0][0][2], chains[0][1][1], h_columns)
     line = []
     for k in range(4):
-        part = slice(k * rank, (k + 1) * rank)
+        here = slice(2 * k * rank, 2 * (k + 1) * rank)
         line.append(jnp.concatenate(
-            [(sides[0][part] + others[0][part]) + (others[1][part] + others[2][part]) for sides, others in chains],
+            [(sides[0][here] + others[0][here]) + (others[1][here] + others[2][here]) for sides, others in chains],
             axis=1))
-    line = [line[0]] + [send(line[k], 2 * k, 0) for k in (3, 2, 1)]
+    line = [line[0]] + [send_odd(line[k], 2 * k, 0) for k in (3, 2, 1)]
     h_piece = ratio * ((line[0] + line[1]) + (line[2] + line[3]))
-    h_line = [h_piece] + [send(h_piece, 2 * k, 0) for k in range(1, 4)]
+    h_line = [h_piece] + [send_odd(h_piece, 2 * k, 0) for k in range(1, 4)]
     chains = []
     for first in (0, LANES):
         mine = jnp.stack([value[:, first:first + LANES] for value in h_line])
-        chains.append(spread(mine, len(chains)))
-    first_parts = chains[0] + [send(value, 0, 1) for value in chains[0]]
-    total = first_call(x_high, x_low, first_parts)
-    second_parts = chains[1] + [send(value, 0, 1) for value in chains[1]]
-    w_piece = second_call(x_high, x_low, w_here, total, second_parts)
-    own = [parts[k] for parts in (first_parts, second_parts) for k in (0, 4, 2, 6)]
+        own = [mine] + around([mine] * 4)
+        chains.append(own + [send_core(value, 1) for value in own])
+    total = first_call(x_high, x_low, chains[0])
+    w_piece = second_call(x_high, x_low, w_here, total, chains[1])
+    own = [parts[k] for parts in chains for k in (0, 4, 2, 6)]
     h_next = place_h_call(own, h_columns.shape)
     w_pair = jnp.stack([w_piece, send(w_piece, 1, 0)])
     w_next = gather_w_call([w_pair] + [send(w_pair, 2 * k, 0) for k in range(1, 4)])

time: 71.9 us -> 106 us (1.47)
  waiting for transfers between devices: 24.5 us -> 56.5 us
    ppermute x0 -> x28, waiting for transfers between devices: none -> 51.1 us  [the longest x10 51.1 us: send_core(): lax.ppermute(value, ('sp', 'bd'), [(d, d ^ 1) for d in range(source, coun...]
    ppermute x0 -> x28, starting transfers between devices: none -> 27.2 us  [the longest x10 15 us: send_core(): lax.ppermute(value, ('sp', 'bd'), [(d, d ^ 1) for d in range(source, coun...]
    ppermute x32 -> x4, starting transfers between devices: 31.3 us -> 5.04 us  [send(): return lax.ppermute(value, ('sp', 'bd'), pairs)]
    ppermute x32 -> x4, waiting for transfers between devices: 24.5 us -> 5.34 us  [send(): return lax.ppermute(value, ('sp', 'bd'), pairs)]
  transfers between devices with their start and end apart: 32 -> 32, of which waited for: 17 -> 10; matrix products, arithmetic and copies ran while one was open for 0% -> 0% of each run, Pallas kernels for 4% -> 3%
where the time goes in v15:
time: 106 us; the launch traced here: 105 us
  waiting for transfers between devices  56.5 us (53%)
  starting transfers between devices  32.3 us (30%)
  Pallas kernels  15.1 us (14%)
  between operations  1.17 us (1%)
    ppermute x10, waiting for transfers between devices, send_core(): lax.ppermute(value, ('sp', 'bd'), [(d, d ^ 1) for d in range(source, coun...  51.1 us
    ppermute x10, starting transfers between devices, send_core(): lax.ppermute(value, ('sp', 'bd'), [(d, d ^ 1) for d in range(source, coun...  15 us
    ppermute x18, starting transfers between devices, send_odd(): return lax.ppermute(value, ('sp', 'bd'), pairs)  12.2 us
    pallas_call x1, Pallas kernels, blur_call(): pl.pallas_call(blur_kernel, out_shape=[jax.ShapeDtypeStruct(image, BF16)]...  9.77 us
    ppermute x4, waiting for transfers between devices, send(): return lax.ppermute(value, ('sp', 'bd'), pairs)  5.34 us
    ppermute x4, starting transfers between devices, send(): return lax.ppermute(value, ('sp', 'bd'), pairs)  5.04 us
  transfers between devices with their start and end apart: 32, of which 10 were waited for; matrix products, arithmetic and copies ran while one was open for 0% of the time, Pallas kernels for 3%

profile of v15, /device:TPU:0, one launch (start us, length us, event | category | flops | bytes accessed | tf_op | source)
XLA Modules:
  0.0 105.5 jit_solution(13385363156702274706)
XLA Ops:
  0.6 9.8 %shard_map.68 = (bf16[32,96,256]{2,1,0:T(8,128)(2,1)S(1)}, bf16[32,96,256]{2,1,0:T(8,128)(2,1)S(1)}, f32[48,96]{1,0:T(8,128)S(1)}, bf16[96,256]{1,0:T(8,128)(2,1)S(1)}, f32[1560,128]{1,0:T(8,128)S(1)}) custom-call(f32[96,32,256]{2,1,0:T(8,128)} %bitcast.31, f32[25,1,96]{2,1,0:T(1,128)} %bitcast.36, f32[25,1,96]{2,1,0:T(1,128)} %bitcast.37, f32[48,768]{1,0:T(8,128)} %bitcast.33), custom_call_target="tpu_custom_call" | custom-call | tf_op jit(solution)/shard_map/pallas_call | solution.py:275
  10.4 2.4 %collective-permute-start = (f32[1560,128]{1,0:T(8,128)S(1)}, f32[1560,128]{1,0:T(8,128)S(1)}, u32[]{:S(2)}, u32[]{:S(2)}) collective-permute-start(f32[1560,128]{1,0:T(8,128)S(1)} %get-tuple-element.12), channel_id=1, source_target_pairs={{0,1},{2,3},{4,5},{6,7},{8,9},{10,11},{12,13},{14,15},{16,17},{18,... | collective-permute-start | bytes 2396168 | tf_op jit(solution)/shard_map/ppermute | solution.py:459
  12.8 0.7 shard_map.69
  13.5 1.2 %collective-permute-done = f32[1560,128]{1,0:T(8,128)S(1)} collective-permute-done((f32[1560,128]{1,0:T(8,128)S(1)}, f32[1560,128]{1,0:T(8,128)S(1)}, u32[]{:S(2)}, u32[]{:S(2)}) %collective-permute-start) | collective-permute-done | bytes 798752 | tf_op jit(solution)/shard_map/ppermute | solution.py:459
  14.7 2.3 %collective-permute-start.4 = (f32[1536,128]{1,0:T(8,128)S(1)}, f32[1536,128]{1,0:T(8,128)S(1)}, u32[]{:S(2)}, u32[]{:S(2)}) collective-permute-start(f32[1536,128]{1,0:T(8,128)S(1)} %shard_map.69), channel_id=1, source_target_pairs={{0,1},{2,3},{4,5},{6,7},{8,9},{10,11},{12,13},{14,15},{16,17},{18,... | collective-permute-start | bytes 2359304 | tf_op jit(solution)/shard_map/ppermute | solution.py:459
  17.0 0.1 slice_add_fusion.7
  17.1 0.7 collective-permute-start.3
  17.8 0.7 collective-permute-start.2
  18.5 0.7 collective-permute-start.1
  19.2 0.1 slice_add_fusion.4
  19.3 0.0 copy-start
  19.3 0.8 collective-permute-start.7
  20.1 0.7 collective-permute-start.6
  20.8 0.0 collective-permute-done.3
  20.8 0.7 collective-permute-start.5
  21.5 0.0 collective-permute-done.2
  21.5 0.1 fusion.3
  21.6 0.0 collective-permute-done.7
  21.6 0.0 collective-permute-done.5
  21.7 0.7 collective-permute-start.8
  22.3 0.7 collective-permute-start.9
  23.0 0.7 collective-permute-start.10
  23.7 0.4 shard_map.70
  24.1 0.0 collective-permute-done.8
  24.1 0.0 collective-permute-done.10
  24.2 0.7 collective-permute-start.13
  24.9 0.7 collective-permute-start.12
  25.5 0.7 collective-permute-start.11
  26.2 0.0 collective-permute-done.12
  26.3 0.0 collective-permute-done.11
  26.3 1.3 %collective-permute-start.17 = (f32[4,96,128]{2,1,0:T(8,128)S(1)}, f32[4,96,128]{2,1,0:T(8,128)S(1)}, u32[]{:S(2)}, u32[]{:S(2)}) collective-permute-start(f32[4,96,128]{2,1,0:T(8,128)S(1)} %pad_maximum_fusion.rest_0_.refs_0_), channel_id=1, source_target_pairs={{1,0},{3,2},{5,4},{7,6},{9,8},{11,10},{13,12},{15,14},{17,16},{19,... | collective-permute-start | bytes 589832 | tf_op jit(solution)/shard_map/ppermute | solution.py:459
  27.6 0.7 collective-permute-start.16
  28.3 0.7 collective-permute-start.15
  29.0 0.7 collective-permute-start.14
  29.7 0.7 collective-permute-start.23
  30.4 35.4 %collective-permute-done.17.rest_4_.refs_1_ = f32[4,96,128]{2,1,0:T(8,128)S(1)} collective-permute-done((f32[4,96,128]{2,1,0:T(8,128)S(1)}, f32[4,96,128]{2,1,0:T(8,128)S(1)}, u32[]{:S(2)}, u32[]{:S(2)}) %collective-permute-start.17) | collective-permute-done | bytes 196640 | tf_op jit(solution)/shard_map/ppermute | solution.py:459
  65.8 0.7 collective-permute-start.22
  66.4 0.0 collective-permute-done.16.rest_3_
  66.4 0.7 collective-permute-start.21
  67.1 0.0 collective-permute-done.15.rest_2_.refs_2_
  67.1 1.3 %collective-permute-start.20 = (f32[4,96,128]{2,1,0:T(8,128)S(1)}, f32[4,96,128]{2,1,0:T(8,128)S(1)}, u32[]{:S(2)}, u32[]{:S(2)}) collective-permute-start(f32[4,96,128]{2,1,0:T(8,128)S(1)} %collective-permute-done.16.rest_3_), channel_id=1, source_target_pairs={{1,0},{3,2},{5,4},{7,6},{9,8},{11,10},{13,12},{15,14},{17,16},{19,... | collective-permute-start | bytes 589832 | tf_op jit(solution)/shard_map/ppermute | solution.py:459
  68.4 1.3 %collective-permute-start.19 = (f32[4,96,128]{2,1,0:T(8,128)S(1)}, f32[4,96,128]{2,1,0:T(8,128)S(1)}, u32[]{:S(2)}, u32[]{:S(2)}) collective-permute-start(f32[4,96,128]{2,1,0:T(8,128)S(1)} %collective-permute-done.15.rest_2_.refs_2_), channel_id=1, source_target_pairs={{1,0},{3,2},{5,4},{7,6},{9,8},{11,10},{13,12},{15,14},{17,16},{19,... | collective-permute-start | bytes 589832 | tf_op jit(solution)/shard_map/ppermute | solution.py:459
  69.8 1.3 %collective-permute-start.24 = (f32[4,96,128]{2,1,0:T(8,128)S(1)}, f32[4,96,128]{2,1,0:T(8,128)S(1)}, u32[]{:S(2)}, u32[]{:S(2)}) collective-permute-start(f32[4,96,128]{2,1,0:T(8,128)S(1)} %pad_maximum_fusion.1.rest_0_.refs_4_), channel_id=1, source_target_pairs={{1,0},{3,2},{5,4},{7,6},{9,8},{11,10},{13,12},{15,14},{17,16},{19,... | collective-permute-start | bytes 589832 | tf_op jit(solution)/shard_map/ppermute | solution.py:459
  71.1 1.3 %collective-permute-start.18 = (f32[4,96,128]{2,1,0:T(8,128)S(1)}, f32[4,96,128]{2,1,0:T(8,128)S(1)}, u32[]{:S(2)}, u32[]{:S(2)}) collective-permute-start(f32[4,96,128]{2,1,0:T(8,128)S(1)} %collective-permute-done.14.rest_1_), channel_id=1, source_target_pairs={{1,0},{3,2},{5,4},{7,6},{9,8},{11,10},{13,12},{15,14},{17,16},{19,... | collective-permute-start | bytes 589832 | tf_op jit(solution)/shard_map/ppermute | solution.py:459
  72.4 1.3 %collective-permute-start.27 = (f32[4,96,128]{2,1,0:T(8,128)S(1)}, f32[4,96,128]{2,1,0:T(8,128)S(1)}, u32[]{:S(2)}, u32[]{:S(2)}) collective-permute-start(f32[4,96,128]{2,1,0:T(8,128)S(1)} %collective-permute-done.23.rest_3_), channel_id=1, source_target_pairs={{1,0},{3,2},{5,4},{7,6},{9,8},{11,10},{13,12},{15,14},{17,16},{19,... | collective-permute-start | bytes 589832 | tf_op jit(solution)/shard_map/ppermute | solution.py:459
  73.7 10.2 %collective-permute-done.20.rest_7_ = f32[4,96,128]{2,1,0:T(8,128)S(1)} collective-permute-done((f32[4,96,128]{2,1,0:T(8,128)S(1)}, f32[4,96,128]{2,1,0:T(8,128)S(1)}, u32[]{:S(2)}, u32[]{:S(2)}) %collective-permute-start.20) | collective-permute-done | bytes 196640 | tf_op jit(solution)/shard_map/ppermute | solution.py:459
  83.9 1.3 %collective-permute-start.26 = (f32[4,96,128]{2,1,0:T(8,128)S(1)}, f32[4,96,128]{2,1,0:T(8,128)S(1)}, u32[]{:S(2)}, u32[]{:S(2)}) collective-permute-start(f32[4,96,128]{2,1,0:T(8,128)S(1)} %collective-permute-done.22.rest_2_.refs_6_), channel_id=1, source_target_pairs={{1,0},{3,2},{5,4},{7,6},{9,8},{11,10},{13,12},{15,14},{17,16},{19,... | collective-permute-start | bytes 589832 | tf_op jit(solution)/shard_map/ppermute | solution.py:459
  85.2 0.0 collective-permute-done.19.rest_6_.refs_3_
  85.2 1.3 %collective-permute-start.25 = (f32[4,96,128]{2,1,0:T(8,128)S(1)}, f32[4,96,128]{2,1,0:T(8,128)S(1)}, u32[]{:S(2)}, u32[]{:S(2)}) collective-permute-start(f32[4,96,128]{2,1,0:T(8,128)S(1)} %collective-permute-done.21.rest_1_), channel_id=1, source_target_pairs={{1,0},{3,2},{5,4},{7,6},{9,8},{11,10},{13,12},{15,14},{17,16},{19,... | collective-permute-start | bytes 589832 | tf_op jit(solution)/shard_map/ppermute | solution.py:459
  86.5 1.4 %collective-permute-done.18.rest_5_ = f32[4,96,128]{2,1,0:T(8,128)S(1)} collective-permute-done((f32[4,96,128]{2,1,0:T(8,128)S(1)}, f32[4,96,128]{2,1,0:T(8,128)S(1)}, u32[]{:S(2)}, u32[]{:S(2)}) %collective-permute-start.18) | collective-permute-done | bytes 196640 | tf_op jit(solution)/shard_map/ppermute | solution.py:459
  87.9 1.1 %shard_map.71.total_ref = f32[288,96]{1,0:T(8,128)S(1)} custom-call(bf16[32,96,256]{2,1,0:T(8,128)(2,1)S(1)} %get-tuple-element.9.xh_ref, bf16[32,96,256]{2,1,0:T(8,128)(2,1)S(1)} %get-tuple-element.10.xl_ref, f32[4,96,128]{2,1,0:T(8,128)S(1)} %pad_maximum_fusion.rest_0_.refs_0_, f32[4,96,128]{2,1,0:T(8,128)S(1)} %collective-permute-done.14.rest_1_, ...), custom_call_target="tpu_custom_call" | custom-call | tf_op jit(solution)/shard_map/pallas_call | solution.py:352
  89.0 0.2 collective-permute-done.27.rest_7_
  89.2 1.3 %collective-permute-done.26.rest_6_.refs_7_ = f32[4,96,128]{2,1,0:T(8,128)S(1)} collective-permute-done((f32[4,96,128]{2,1,0:T(8,128)S(1)}, f32[4,96,128]{2,1,0:T(8,128)S(1)}, u32[]{:S(2)}, u32[]{:S(2)}) %collective-permute-start.26) | collective-permute-done | bytes 196640 | tf_op jit(solution)/shard_map/ppermute | solution.py:459
  90.5 1.3 %collective-permute-done.25.rest_5_ = f32[4,96,128]{2,1,0:T(8,128)S(1)} collective-permute-done((f32[4,96,128]{2,1,0:T(8,128)S(1)}, f32[4,96,128]{2,1,0:T(8,128)S(1)}, u32[]{:S(2)}, u32[]{:S(2)}) %collective-permute-start.25) | collective-permute-done | bytes 196640 | tf_op jit(solution)/shard_map/ppermute | solution.py:459
  91.8 1.4 %shard_map.72 = f32[48,96]{1,0:T(8,128)S(1)} custom-call(bf16[32,96,256]{2,1,0:T(8,128)(2,1)S(1)} %get-tuple-element.9.xh_ref, bf16[32,96,256]{2,1,0:T(8,128)(2,1)S(1)} %get-tuple-element.10.xl_ref, f32[48,96]{1,0:T(8,128)S(1)} %get-tuple-element.11.w_ref, f32[288,96]{1,0:T(8,128)S(1)} %shard_map.71.total_ref, ...), custom_call_target="tpu_custom_call" | custom-call | tf_op jit(solution)/shard_map/pallas_call | solution.py:376
  93.3 0.6 collective-permute-start.28
  93.9 3.3 %collective-permute-done.28 = f32[48,96]{1,0:T(8,128)S(1)} collective-permute-done((f32[48,96]{1,0:T(8,128)S(1)}, f32[48,96]{1,0:T(8,128)S(1)}, u32[]{:S(2)}, u32[]{:S(2)}) %collective-permute-start.28) | collective-permute-done | bytes 18464 | tf_op jit(solution)/shard_map/ppermute | solution.py:444
  97.2 2.0 %collective-permute-start.31 = (f32[2,48,96]{2,1,0:T(8,128)S(1)}, f32[2,48,96]{2,1,0:T(8,128)S(1)}, u32[]{:S(2)}, u32[]{:S(2)}) collective-permute-start(f32[2,48,96]{2,1,0:T(8,128)S(1)} %pad_maximum_fusion.5.refs_0_), channel_id=1, source_target_pairs={{0,24},{1,25},{2,26},{3,27},{4,28},{5,29},{6,30},{7,31},{8,16},{9,... | collective-permute-start | bytes 110600 | tf_op jit(solution)/shard_map/ppermute | solution.py:444
  99.2 0.3 collective-permute-start.30
  99.6 2.1 %collective-permute-start.29 = (f32[2,48,96]{2,1,0:T(8,128)S(1)}, f32[2,48,96]{2,1,0:T(8,128)S(1)}, u32[]{:S(2)}, u32[]{:S(2)}) collective-permute-start(f32[2,48,96]{2,1,0:T(8,128)S(1)} %pad_maximum_fusion.5.refs_0_), channel_id=1, source_target_pairs={{0,8},{1,9},{2,10},{3,11},{4,12},{5,13},{6,14},{7,15},{8,0},{9,1},... | collective-permute-start | bytes 110600 | tf_op jit(solution)/shard_map/ppermute | solution.py:444
  101.7 1.0 shard_map.74
  102.7 0.9 collective-permute-done.31.refs_3_
  103.6 1.1 %collective-permute-done.30.refs_2_ = f32[2,48,96]{2,1,0:T(8,128)S(1)} collective-permute-done((f32[2,48,96]{2,1,0:T(8,128)S(1)}, f32[2,48,96]{2,1,0:T(8,128)S(1)}, u32[]{:S(2)}, u32[]{:S(2)}) %collective-permute-start.30) | collective-permute-done | bytes 36896 | tf_op jit(solution)/shard_map/ppermute | solution.py:444
  104.7 0.8 shard_map.73
  (25 shorter events, 0.2 us)
Async XLA Ops:
  10.4 4.3 %collective-permute-start = (f32[1560,128]{1,0:T(8,128)S(1)}, f32[1560,128]{1,0:T(8,128)S(1)}, u32[]{:S(2)}, u32[]{:S(2)}) collective-permute-start(f32[1560,128]{1,0:T(8,128)S(1)} %get-tuple-element.12), channel_id=1, source_target_pairs={{0,1},{2,3},{4,5},{6,7},{8,9},{10,11},{12,13},{14,15},{16,17},{18,... | collective-permute-start | bytes 2396168 | tf_op jit(solution)/shard_map/ppermute | solution.py:459
  14.7 4.5 %collective-permute-start.4 = (f32[1536,128]{1,0:T(8,128)S(1)}, f32[1536,128]{1,0:T(8,128)S(1)}, u32[]{:S(2)}, u32[]{:S(2)}) collective-permute-start(f32[1536,128]{1,0:T(8,128)S(1)} %shard_map.69), channel_id=1, source_target_pairs={{0,1},{2,3},{4,5},{6,7},{8,9},{10,11},{12,13},{14,15},{16,17},{18,... | collective-permute-start | bytes 2359304 | tf_op jit(solution)/shard_map/ppermute | solution.py:459
  17.1 3.7 %collective-permute-start.3 = (f32[384,128]{1,0:T(8,128)S(1)}, f32[384,128]{1,0:T(8,128)S(1)}, u32[]{:S(2)}, u32[]{:S(2)}) collective-permute-start(f32[384,128]{1,0:T(8,128)S(1)} %get-tuple-element.17), channel_id=1, source_target_pairs={{1,7},{3,5},{5,3},{7,1},{9,15},{11,13},{13,11},{15,9},{17,23},{19,... | collective-permute-start | bytes 589832 | tf_op jit(solution)/shard_map/ppermute | solution.py:454
  17.8 3.7 %collective-permute-start.2 = (f32[384,128]{1,0:T(8,128)S(1)}, f32[384,128]{1,0:T(8,128)S(1)}, u32[]{:S(2)}, u32[]{:S(2)}) collective-permute-start(f32[384,128]{1,0:T(8,128)S(1)} %get-tuple-element.18), channel_id=1, source_target_pairs={{1,5},{3,7},{5,1},{7,3},{9,13},{11,15},{13,9},{15,11},{17,21},{19,... | collective-permute-start | bytes 589832 | tf_op jit(solution)/shard_map/ppermute | solution.py:454
  18.5 3.0 %collective-permute-start.1 = (f32[408,128]{1,0:T(8,128)S(1)}, f32[408,128]{1,0:T(8,128)S(1)}, u32[]{:S(2)}, u32[]{:S(2)}) collective-permute-start(f32[408,128]{1,0:T(8,128)S(1)} %slice_add_fusion.mine_ref), channel_id=1, source_target_pairs={{1,3},{3,1},{5,7},{7,5},{9,11},{11,9},{13,15},{15,13},{17,19},{19,... | collective-permute-start | bytes 626696 | tf_op jit(solution)/shard_map/ppermute | solution.py:454
  19.3 4.4 %copy-start = (f32[48,32,32]{0,2,1:T(8,128)S(1)}, f32[48,32,32]{0,2,1:T(8,128)}, u32[]{:S(2)}) copy-start(f32[48,32,32]{0,2,1:T(8,128)} %param.9) | copy-start | bytes 589828
  19.3 2.3 %collective-permute-start.7 = (f32[384,128]{1,0:T(8,128)S(1)}, f32[384,128]{1,0:T(8,128)S(1)}, u32[]{:S(2)}, u32[]{:S(2)}) collective-permute-start(f32[384,128]{1,0:T(8,128)S(1)} %get-tuple-element.20), channel_id=1, source_target_pairs={{1,7},{3,5},{5,3},{7,1},{9,15},{11,13},{13,11},{15,9},{17,23},{19,... | collective-permute-start | bytes 589832 | tf_op jit(solution)/shard_map/ppermute | solution.py:454
  20.1 1.5 %collective-permute-start.6 = (f32[384,128]{1,0:T(8,128)S(1)}, f32[384,128]{1,0:T(8,128)S(1)}, u32[]{:S(2)}, u32[]{:S(2)}) collective-permute-start(f32[384,128]{1,0:T(8,128)S(1)} %get-tuple-element.21), channel_id=1, source_target_pairs={{1,3},{3,1},{5,7},{7,5},{9,11},{11,9},{13,15},{15,13},{17,19},{19,... | collective-permute-start | bytes 589832 | tf_op jit(solution)/shard_map/ppermute | solution.py:454
  20.8 0.8 collective-permute-start.5
  21.7 2.4 %collective-permute-start.8 = (f32[96,256]{1,0:T(8,128)S(1)}, f32[96,256]{1,0:T(8,128)S(1)}, u32[]{:S(2)}, u32[]{:S(2)}) collective-permute-start(f32[96,256]{1,0:T(8,128)S(1)} %pad_maximum_fusion.2), channel_id=1, source_target_pairs={{1,25},{3,27},{5,29},{7,31},{9,17},{11,19},{13,21},{15,23},{17,9},... | collective-permute-start | bytes 294920 | tf_op jit(solution)/shard_map/ppermute | solution.py:454
  22.3 1.8 %collective-permute-start.9 = (f32[96,256]{1,0:T(8,128)S(1)}, f32[96,256]{1,0:T(8,128)S(1)}, u32[]{:S(2)}, u32[]{:S(2)}) collective-permute-start(f32[96,256]{1,0:T(8,128)S(1)} %pad_maximum_fusion.3), channel_id=1, source_target_pairs={{1,17},{3,19},{5,21},{7,23},{9,25},{11,27},{13,29},{15,31},{17,1},... | collective-permute-start | bytes 294920 | tf_op jit(solution)/shard_map/ppermute | solution.py:454
  23.0 1.1 %collective-permute-start.10 = (f32[96,256]{1,0:T(8,128)S(1)}, f32[96,256]{1,0:T(8,128)S(1)}, u32[]{:S(2)}, u32[]{:S(2)}) collective-permute-start(f32[96,256]{1,0:T(8,128)S(1)} %pad_maximum_fusion.4), channel_id=1, source_target_pairs={{1,9},{3,11},{5,13},{7,15},{9,1},{11,3},{13,5},{15,7},{17,25},{19,... | collective-permute-start | bytes 294920 | tf_op jit(solution)/shard_map/ppermute | solution.py:454
  24.2 2.0 %collective-permute-start.13 = (f32[96,256]{1,0:T(8,128)S(1)}, f32[96,256]{1,0:T(8,128)S(1)}, u32[]{:S(2)}, u32[]{:S(2)}) collective-permute-start(f32[96,256]{1,0:T(8,128)S(1)} %fusion.1), channel_id=1, source_target_pairs={{1,25},{3,27},{5,29},{7,31},{9,17},{11,19},{13,21},{15,23},{17,9},... | collective-permute-start | bytes 294920 | tf_op jit(solution)/shard_map/ppermute | solution.py:454
  24.9 1.4 %collective-permute-start.12 = (f32[96,256]{1,0:T(8,128)S(1)}, f32[96,256]{1,0:T(8,128)S(1)}, u32[]{:S(2)}, u32[]{:S(2)}) collective-permute-start(f32[96,256]{1,0:T(8,128)S(1)} %fusion.1), channel_id=1, source_target_pairs={{1,17},{3,19},{5,21},{7,23},{9,25},{11,27},{13,29},{15,31},{17,1},... | collective-permute-start | bytes 294920 | tf_op jit(solution)/shard_map/ppermute | solution.py:454
  25.5 0.7 collective-permute-start.11
  26.3 39.5 %collective-permute-start.17 = (f32[4,96,128]{2,1,0:T(8,128)S(1)}, f32[4,96,128]{2,1,0:T(8,128)S(1)}, u32[]{:S(2)}, u32[]{:S(2)}) collective-permute-start(f32[4,96,128]{2,1,0:T(8,128)S(1)} %pad_maximum_fusion.rest_0_.refs_0_), channel_id=1, source_target_pairs={{1,0},{3,2},{5,4},{7,6},{9,8},{11,10},{13,12},{15,14},{17,16},{19,... | collective-permute-start | bytes 589832 | tf_op jit(solution)/shard_map/ppermute | solution.py:459
  27.6 38.8 %collective-permute-start.16 = (f32[4,96,128]{2,1,0:T(8,128)S(1)}, f32[4,96,128]{2,1,0:T(8,128)S(1)}, u32[]{:S(2)}, u32[]{:S(2)}) collective-permute-start(f32[4,96,128]{2,1,0:T(8,128)S(1)} %pad_maximum_fusion.rest_0_.refs_0_), channel_id=1, source_target_pairs={{1,7},{3,5},{5,3},{7,1},{9,15},{11,13},{13,11},{15,9},{17,23},{19,... | collective-permute-start | bytes 589832 | tf_op jit(solution)/shard_map/ppermute | solution.py:454
  28.3 38.8 %collective-permute-start.15 = (f32[4,96,128]{2,1,0:T(8,128)S(1)}, f32[4,96,128]{2,1,0:T(8,128)S(1)}, u32[]{:S(2)}, u32[]{:S(2)}) collective-permute-start(f32[4,96,128]{2,1,0:T(8,128)S(1)} %pad_maximum_fusion.rest_0_.refs_0_), channel_id=1, source_target_pairs={{1,3},{3,1},{5,7},{7,5},{9,11},{11,9},{13,15},{15,13},{17,19},{19,... | collective-permute-start | bytes 589832 | tf_op jit(solution)/shard_map/ppermute | solution.py:454
  29.0 39.5 %collective-permute-start.14 = (f32[4,96,128]{2,1,0:T(8,128)S(1)}, f32[4,96,128]{2,1,0:T(8,128)S(1)}, u32[]{:S(2)}, u32[]{:S(2)}) collective-permute-start(f32[4,96,128]{2,1,0:T(8,128)S(1)} %pad_maximum_fusion.rest_0_.refs_0_), channel_id=1, source_target_pairs={{1,5},{3,7},{5,1},{7,3},{9,13},{11,15},{13,9},{15,11},{17,21},{19,... | collective-permute-start | bytes 589832 | tf_op jit(solution)/shard_map/ppermute | solution.py:454
  29.7 40.1 %collective-permute-start.23 = (f32[4,96,128]{2,1,0:T(8,128)S(1)}, f32[4,96,128]{2,1,0:T(8,128)S(1)}, u32[]{:S(2)}, u32[]{:S(2)}) collective-permute-start(f32[4,96,128]{2,1,0:T(8,128)S(1)} %pad_maximum_fusion.1.rest_0_.refs_4_), channel_id=1, source_target_pairs={{1,7},{3,5},{5,3},{7,1},{9,15},{11,13},{13,11},{15,9},{17,23},{19,... | collective-permute-start | bytes 589832 | tf_op jit(solution)/shard_map/ppermute | solution.py:454
  65.8 5.3 %collective-permute-start.22 = (f32[4,96,128]{2,1,0:T(8,128)S(1)}, f32[4,96,128]{2,1,0:T(8,128)S(1)}, u32[]{:S(2)}, u32[]{:S(2)}) collective-permute-start(f32[4,96,128]{2,1,0:T(8,128)S(1)} %pad_maximum_fusion.1.rest_0_.refs_4_), channel_id=1, source_target_pairs={{1,3},{3,1},{5,7},{7,5},{9,11},{11,9},{13,15},{15,13},{17,19},{19,... | collective-permute-start | bytes 589832 | tf_op jit(solution)/shard_map/ppermute | solution.py:454
  66.4 5.9 %collective-permute-start.21 = (f32[4,96,128]{2,1,0:T(8,128)S(1)}, f32[4,96,128]{2,1,0:T(8,128)S(1)}, u32[]{:S(2)}, u32[]{:S(2)}) collective-permute-start(f32[4,96,128]{2,1,0:T(8,128)S(1)} %pad_maximum_fusion.1.rest_0_.refs_4_), channel_id=1, source_target_pairs={{1,5},{3,7},{5,1},{7,3},{9,13},{11,15},{13,9},{15,11},{17,21},{19,... | collective-permute-start | bytes 589832 | tf_op jit(solution)/shard_map/ppermute | solution.py:454
  67.1 16.8 %collective-permute-start.20 = (f32[4,96,128]{2,1,0:T(8,128)S(1)}, f32[4,96,128]{2,1,0:T(8,128)S(1)}, u32[]{:S(2)}, u32[]{:S(2)}) collective-permute-start(f32[4,96,128]{2,1,0:T(8,128)S(1)} %collective-permute-done.16.rest_3_), channel_id=1, source_target_pairs={{1,0},{3,2},{5,4},{7,6},{9,8},{11,10},{13,12},{15,14},{17,16},{19,... | collective-permute-start | bytes 589832 | tf_op jit(solution)/shard_map/ppermute | solution.py:459
  68.4 16.8 %collective-permute-start.19 = (f32[4,96,128]{2,1,0:T(8,128)S(1)}, f32[4,96,128]{2,1,0:T(8,128)S(1)}, u32[]{:S(2)}, u32[]{:S(2)}) collective-permute-start(f32[4,96,128]{2,1,0:T(8,128)S(1)} %collective-permute-done.15.rest_2_.refs_2_), channel_id=1, source_target_pairs={{1,0},{3,2},{5,4},{7,6},{9,8},{11,10},{13,12},{15,14},{17,16},{19,... | collective-permute-start | bytes 589832 | tf_op jit(solution)/shard_map/ppermute | solution.py:459
  69.8 19.2 %collective-permute-start.24 = (f32[4,96,128]{2,1,0:T(8,128)S(1)}, f32[4,96,128]{2,1,0:T(8,128)S(1)}, u32[]{:S(2)}, u32[]{:S(2)}) collective-permute-start(f32[4,96,128]{2,1,0:T(8,128)S(1)} %pad_maximum_fusion.1.rest_0_.refs_4_), channel_id=1, source_target_pairs={{1,0},{3,2},{5,4},{7,6},{9,8},{11,10},{13,12},{15,14},{17,16},{19,... | collective-permute-start | bytes 589832 | tf_op jit(solution)/shard_map/ppermute | solution.py:459
  71.1 16.8 %collective-permute-start.18 = (f32[4,96,128]{2,1,0:T(8,128)S(1)}, f32[4,96,128]{2,1,0:T(8,128)S(1)}, u32[]{:S(2)}, u32[]{:S(2)}) collective-permute-start(f32[4,96,128]{2,1,0:T(8,128)S(1)} %collective-permute-done.14.rest_1_), channel_id=1, source_target_pairs={{1,0},{3,2},{5,4},{7,6},{9,8},{11,10},{13,12},{15,14},{17,16},{19,... | collective-permute-start | bytes 589832 | tf_op jit(solution)/shard_map/ppermute | solution.py:459
  72.4 16.8 %collective-permute-start.27 = (f32[4,96,128]{2,1,0:T(8,128)S(1)}, f32[4,96,128]{2,1,0:T(8,128)S(1)}, u32[]{:S(2)}, u32[]{:S(2)}) collective-permute-start(f32[4,96,128]{2,1,0:T(8,128)S(1)} %collective-permute-done.23.rest_3_), channel_id=1, source_target_pairs={{1,0},{3,2},{5,4},{7,6},{9,8},{11,10},{13,12},{15,14},{17,16},{19,... | collective-permute-start | bytes 589832 | tf_op jit(solution)/shard_map/ppermute | solution.py:459
  83.9 6.6 %collective-permute-start.26 = (f32[4,96,128]{2,1,0:T(8,128)S(1)}, f32[4,96,128]{2,1,0:T(8,128)S(1)}, u32[]{:S(2)}, u32[]{:S(2)}) collective-permute-start(f32[4,96,128]{2,1,0:T(8,128)S(1)} %collective-permute-done.22.rest_2_.refs_6_), channel_id=1, source_target_pairs={{1,0},{3,2},{5,4},{7,6},{9,8},{11,10},{13,12},{15,14},{17,16},{19,... | collective-permute-start | bytes 589832 | tf_op jit(solution)/shard_map/ppermute | solution.py:459
  85.2 6.6 %collective-permute-start.25 = (f32[4,96,128]{2,1,0:T(8,128)S(1)}, f32[4,96,128]{2,1,0:T(8,128)S(1)}, u32[]{:S(2)}, u32[]{:S(2)}) collective-permute-start(f32[4,96,128]{2,1,0:T(8,128)S(1)} %collective-permute-done.21.rest_1_), channel_id=1, source_target_pairs={{1,0},{3,2},{5,4},{7,6},{9,8},{11,10},{13,12},{15,14},{17,16},{19,... | collective-permute-start | bytes 589832 | tf_op jit(solution)/shard_map/ppermute | solution.py:459
  93.3 3.9 %collective-permute-start.28 = (f32[48,96]{1,0:T(8,128)S(1)}, f32[48,96]{1,0:T(8,128)S(1)}, u32[]{:S(2)}, u32[]{:S(2)}) collective-permute-start(f32[48,96]{1,0:T(8,128)S(1)} %shard_map.72), channel_id=1, source_target_pairs={{0,4},{1,5},{2,6},{3,7},{4,0},{5,1},{6,2},{7,3},{8,12},{9,13},{10,... | collective-permute-start | bytes 55304 | tf_op jit(solution)/shard_map/ppermute | solution.py:444
  97.2 6.4 %collective-permute-start.31 = (f32[2,48,96]{2,1,0:T(8,128)S(1)}, f32[2,48,96]{2,1,0:T(8,128)S(1)}, u32[]{:S(2)}, u32[]{:S(2)}) collective-permute-start(f32[2,48,96]{2,1,0:T(8,128)S(1)} %pad_maximum_fusion.5.refs_0_), channel_id=1, source_target_pairs={{0,24},{1,25},{2,26},{3,27},{4,28},{5,29},{6,30},{7,31},{8,16},{9,... | collective-permute-start | bytes 110600 | tf_op jit(solution)/shard_map/ppermute | solution.py:444
  99.2 5.5 %collective-permute-start.30 = (f32[2,48,96]{2,1,0:T(8,128)S(1)}, f32[2,48,96]{2,1,0:T(8,128)S(1)}, u32[]{:S(2)}, u32[]{:S(2)}) collective-permute-start(f32[2,48,96]{2,1,0:T(8,128)S(1)} %pad_maximum_fusion.5.refs_0_), channel_id=1, source_target_pairs={{0,16},{1,17},{2,18},{3,19},{4,20},{5,21},{6,22},{7,23},{8,24},{9,... | collective-permute-start | bytes 110600 | tf_op jit(solution)/shard_map/ppermute | solution.py:444
  99.6 5.1 %collective-permute-start.29 = (f32[2,48,96]{2,1,0:T(8,128)S(1)}, f32[2,48,96]{2,1,0:T(8,128)S(1)}, u32[]{:S(2)}, u32[]{:S(2)}) collective-permute-start(f32[2,48,96]{2,1,0:T(8,128)S(1)} %pad_maximum_fusion.5.refs_0_), channel_id=1, source_target_pairs={{0,8},{1,9},{2,10},{3,11},{4,12},{5,13},{6,14},{7,15},{8,0},{9,1},... | collective-permute-start | bytes 110600 | tf_op jit(solution)/shard_map/ppermute | solution.py:444

commit v16 on v12

--- a/solution.py
+++ b/solution.py
@@ -202,12 +202,10 @@
     ky_ref[...] = placed
     copies[2].wait()
 
-    def body(step, carry):
+    for step in range(groups):
         chunk(step).wait()
+    for step in range(groups):
         blur_group(step, cube_ref, kx_ref, ky_ref, xh_ref, xl_ref, margin)
-        return carry
-
-    lax.fori_loop(0, groups, body, 0)
     gram = fold(band_gram(w_ref[...])[:, :rank])
     keep_ref[PIECES * rank:] = gram
     give_ref[PIECES * rank:] = gram
@@ -435,16 +433,6 @@
 
 def around(values):
     return [send(values[k], k % 2, 2 * (k // 2)) for k in range(1, 4)]
-
-
-def spread(value, chain):
-    if chain == 0:
-        column, row = send(value, 1, 0), send(value, 0, 2)
-        corner = send(row, 1, 0)
-    else:
-        row, column = send(value, 0, 2), send(value, 1, 0)
-        corner = send(column, 0, 2)
-    return [value, column, row, corner]
 
 
 def local(cube, taps_x, taps_y, factor_w, factor_h):
@@ -478,7 +466,7 @@
     chains = []
     for first in (0, LANES):
         mine = jnp.stack([value[:, first:first + LANES] for value in h_line])
-        chains.append(spread(mine, len(chains)))
+        chains.append([mine] + around([mine] * 4))
     first_parts = chains[0] + [send(value, 0, 1) for value in chains[0]]
     total = first_call(x_high, x_low, first_parts)
     second_parts = chains[1] + [send(value, 0, 1) for value in chains[1]]

time: 71.9 us -> 69.1 us (0.961)
  waiting for transfers between devices: 24.5 us -> 21.2 us
  starting transfers between devices: 31.3 us -> 34 us
  Pallas kernels: 15 us -> 12.7 us
    ppermute x32, waiting for transfers between devices: 24.5 us -> 21.2 us  [send(): return lax.ppermute(value, ('sp', 'bd'), pairs)]
    ppermute x32, starting transfers between devices: 31.3 us -> 34 us  [send(): return lax.ppermute(value, ('sp', 'bd'), pairs)]
    pallas_call x1, Pallas kernels: 9.78 us -> 7.47 us  [blur_call(): pl.pallas_call(blur_kernel, out_shape=[jax.ShapeDtypeStruct(image, BF16)]...]
  transfers between devices with their start and end apart: 32 -> 32, of which waited for: 17 -> 16; matrix products, arithmetic and copies ran while one was open for 0% -> 0% of each run, Pallas kernels for 4% -> 4%
where the time goes in v16:
time: 69.1 us; the launch traced here: 68.9 us
  starting transfers between devices  34 us (49%)
  waiting for transfers between devices  21.2 us (31%)
  Pallas kernels  12.7 us (18%)
  between operations  0.79 us (1%)
    ppermute x32, starting transfers between devices, send(): return lax.ppermute(value, ('sp', 'bd'), pairs)  34 us
    ppermute x32, waiting for transfers between devices, send(): return lax.ppermute(value, ('sp', 'bd'), pairs)  21.2 us
    pallas_call x1, Pallas kernels, blur_call(): pl.pallas_call(blur_kernel, out_shape=[jax.ShapeDtypeStruct(image, BF16)]...  7.47 us
    pallas_call x1, Pallas kernels, second_call(): pl.pallas_call(second_kernel, out_shape=jax.ShapeDtypeStruct(w_here.shape...  1.41 us
  transfers between devices with their start and end apart: 32, of which 16 were waited for; matrix products, arithmetic and copies ran while one was open for 0% of the time, Pallas kernels for 4%

profile of v16, /device:TPU:0, one launch (start us, length us, event | category | flops | bytes accessed | tf_op | source)
XLA Modules:
  0.0 68.9 jit_solution(14007258620197742906)
XLA Ops:
  0.6 7.5 %shard_map.68 = (bf16[32,96,256]{2,1,0:T(8,128)(2,1)S(1)}, bf16[32,96,256]{2,1,0:T(8,128)(2,1)S(1)}, f32[48,96]{1,0:T(8,128)S(1)}, bf16[96,256]{1,0:T(8,128)(2,1...) custom-call(f32[96,32,256]{2,1,0:T(8,128)} %bitcast.31, f32[25,1,96]{2,1,0:T(1,128)} %bitcast.36, ...), custom_call_target="tpu_custom_call" | custom-call | tf_op jit(solution)/shard_map/pallas_call | solution.py:274
  8.1 0.5 collective-permute-start
  8.6 0.7 shard_map.69
  9.3 0.7 collective-permute-done
  10.0 0.4 collective-permute-start.4
  10.4 0.0 copy-start
  10.4 3.7 %collective-permute-start.3 = (f32[192,128]{1,0:T(8,128)S(1)}, f32[192,128]{1,0:T(8,128)S(1)}, u32[]{:S(2)}, u32[]{:S(2)}) collective-permute-start(f32[192,128]{1,0:T(8,128)S(1)} %get-tuple-element.25), channel_id=1, source_target_pairs={{0,6},{1,7},{2,4},{3,5},{4,2},{5,3},{6,0},{7,1},{8,14},{9,15},{10,... | collective-permute-start | bytes 294920 | tf_op jit(solution)/shard_map/ppermute | solution.py:431
  14.1 0.5 collective-permute-start.2
  14.6 0.2 collective-permute-start.1
  14.8 0.0 collective-permute-done.4
  14.8 0.1 slice_add_fusion.4
  14.9 2.9 %collective-permute-start.7 = (f32[192,128]{1,0:T(8,128)S(1)}, f32[192,128]{1,0:T(8,128)S(1)}, u32[]{:S(2)}, u32[]{:S(2)}) collective-permute-start(f32[192,128]{1,0:T(8,128)S(1)} %get-tuple-element.28), channel_id=1, source_target_pairs={{0,6},{1,7},{2,4},{3,5},{4,2},{5,3},{6,0},{7,1},{8,14},{9,15},{10,... | collective-permute-start | bytes 294920 | tf_op jit(solution)/shard_map/ppermute | solution.py:431
  17.8 0.5 collective-permute-start.6
  18.3 1.3 %collective-permute-start.5 = (f32[192,128]{1,0:T(8,128)S(1)}, f32[192,128]{1,0:T(8,128)S(1)}, u32[]{:S(2)}, u32[]{:S(2)}) collective-permute-start(f32[192,128]{1,0:T(8,128)S(1)} %get-tuple-element.30), channel_id=1, source_target_pairs={{0,4},{1,5},{2,6},{3,7},{4,0},{5,1},{6,2},{7,3},{8,12},{9,13},{10,... | collective-permute-start | bytes 294920 | tf_op jit(solution)/shard_map/ppermute | solution.py:431
  19.6 0.7 collective-permute-done.2
  20.3 1.9 %collective-permute-done.1.other_ref = f32[216,128]{1,0:T(8,128)S(1)} collective-permute-done((f32[216,128]{1,0:T(8,128)S(1)}, f32[216,128]{1,0:T(8,128)S(1)}, u32[]{:S(2)}, u32[]{:S(2)}) %collective-permute-start.1) | collective-permute-done | bytes 110624 | tf_op jit(solution)/shard_map/ppermute | solution.py:431
  22.2 1.7 %collective-permute-done.6 = f32[192,128]{1,0:T(8,128)S(1)} collective-permute-done((f32[192,128]{1,0:T(8,128)S(1)}, f32[192,128]{1,0:T(8,128)S(1)}, u32[]{:S(2)}, u32[]{:S(2)}) %collective-permute-start.6) | collective-permute-done | bytes 98336 | tf_op jit(solution)/shard_map/ppermute | solution.py:431
  24.0 0.0 collective-permute-done.5
  24.1 3.9 %collective-permute-start.8 = (f32[48,256]{1,0:T(8,128)S(1)}, f32[48,256]{1,0:T(8,128)S(1)}, u32[]{:S(2)}, u32[]{:S(2)}) collective-permute-start(f32[48,256]{1,0:T(8,128)S(1)} %pad_maximum_fusion.2), channel_id=1, source_target_pairs={{0,24},{1,25},{2,26},{3,27},{4,28},{5,29},{6,30},{7,31},{8,16},{9,... | collective-permute-start | bytes 147464 | tf_op jit(solution)/shard_map/ppermute | solution.py:431
  27.9 0.6 collective-permute-start.10
  28.6 0.3 shard_map.70
  28.9 1.5 %collective-permute-done.8 = f32[48,256]{1,0:T(8,128)S(1)} collective-permute-done((f32[48,256]{1,0:T(8,128)S(1)}, f32[48,256]{1,0:T(8,128)S(1)}, u32[]{:S(2)}, u32[]{:S(2)}) %collective-permute-start.8) | collective-permute-done | bytes 49184 | tf_op jit(solution)/shard_map/ppermute | solution.py:431
  30.3 2.6 %collective-permute-done.9 = f32[48,256]{1,0:T(8,128)S(1)} collective-permute-done((f32[48,256]{1,0:T(8,128)S(1)}, f32[48,256]{1,0:T(8,128)S(1)}, u32[]{:S(2)}, u32[]{:S(2)}) %collective-permute-start.9) | collective-permute-done | bytes 49184 | tf_op jit(solution)/shard_map/ppermute | solution.py:431
  32.9 0.0 collective-permute-done.10
  32.9 1.9 %collective-permute-start.13 = (f32[48,256]{1,0:T(8,128)S(1)}, f32[48,256]{1,0:T(8,128)S(1)}, u32[]{:S(2)}, u32[]{:S(2)}) collective-permute-start(f32[48,256]{1,0:T(8,128)S(1)} %fusion.1), channel_id=1, source_target_pairs={{0,24},{1,25},{2,26},{3,27},{4,28},{5,29},{6,30},{7,31},{8,16},{9,... | collective-permute-start | bytes 147464 | tf_op jit(solution)/shard_map/ppermute | solution.py:431
  34.8 0.3 collective-permute-start.12
  35.1 2.3 %collective-permute-start.11 = (f32[48,256]{1,0:T(8,128)S(1)}, f32[48,256]{1,0:T(8,128)S(1)}, u32[]{:S(2)}, u32[]{:S(2)}) collective-permute-start(f32[48,256]{1,0:T(8,128)S(1)} %fusion.1), channel_id=1, source_target_pairs={{0,8},{1,9},{2,10},{3,11},{4,12},{5,13},{6,14},{7,15},{8,0},{9,1},... | collective-permute-start | bytes 147464 | tf_op jit(solution)/shard_map/ppermute | solution.py:431
  37.4 1.5 %collective-permute-done.13 = f32[48,256]{1,0:T(8,128)S(1)} collective-permute-done((f32[48,256]{1,0:T(8,128)S(1)}, f32[48,256]{1,0:T(8,128)S(1)}, u32[]{:S(2)}, u32[]{:S(2)}) %collective-permute-start.13) | collective-permute-done | bytes 49184 | tf_op jit(solution)/shard_map/ppermute | solution.py:431
  38.9 1.5 %collective-permute-done.12 = f32[48,256]{1,0:T(8,128)S(1)} collective-permute-done((f32[48,256]{1,0:T(8,128)S(1)}, f32[48,256]{1,0:T(8,128)S(1)}, u32[]{:S(2)}, u32[]{:S(2)}) %collective-permute-start.12) | collective-permute-done | bytes 49184 | tf_op jit(solution)/shard_map/ppermute | solution.py:431
  40.4 0.1 collective-permute-start.17
  40.5 2.7 %collective-permute-start.16 = (f32[4,48,128]{2,1,0:T(8,128)S(1)}, f32[4,48,128]{2,1,0:T(8,128)S(1)}, u32[]{:S(2)}, u32[]{:S(2)}) collective-permute-start(f32[4,48,128]{2,1,0:T(8,128)S(1)} %pad_maximum_fusion.rest_0_.refs_0_), channel_id=1, source_target_pairs={{0,6},{1,7},{2,4},{3,5},{4,2},{5,3},{6,0},{7,1},{8,14},{9,15},{10,... | collective-permute-start | bytes 294920 | tf_op jit(solution)/shard_map/ppermute | solution.py:431
  43.2 0.2 collective-permute-start.15
  43.4 0.6 collective-permute-start.14
  44.0 2.7 %collective-permute-start.23 = (f32[4,48,128]{2,1,0:T(8,128)S(1)}, f32[4,48,128]{2,1,0:T(8,128)S(1)}, u32[]{:S(2)}, u32[]{:S(2)}) collective-permute-start(f32[4,48,128]{2,1,0:T(8,128)S(1)} %pad_maximum_fusion.1.rest_0_.refs_4_), channel_id=1, source_target_pairs={{0,6},{1,7},{2,4},{3,5},{4,2},{5,3},{6,0},{7,1},{8,14},{9,15},{10,... | collective-permute-start | bytes 294920 | tf_op jit(solution)/shard_map/ppermute | solution.py:431
  46.7 0.0 collective-permute-done.17.rest_4_.refs_1_
  46.7 0.2 collective-permute-start.22
  46.9 0.0 collective-permute-done.16.rest_3_
  46.9 1.3 %collective-permute-start.21 = (f32[4,48,128]{2,1,0:T(8,128)S(1)}, f32[4,48,128]{2,1,0:T(8,128)S(1)}, u32[]{:S(2)}, u32[]{:S(2)}) collective-permute-start(f32[4,48,128]{2,1,0:T(8,128)S(1)} %pad_maximum_fusion.1.rest_0_.refs_4_), channel_id=1, source_target_pairs={{0,4},{1,5},{2,6},{3,7},{4,0},{5,1},{6,2},{7,3},{8,12},{9,13},{10,... | collective-permute-start | bytes 294920 | tf_op jit(solution)/shard_map/ppermute | solution.py:431
  48.3 1.3 %collective-permute-done.15.rest_2_.refs_2_ = f32[4,48,128]{2,1,0:T(8,128)S(1)} collective-permute-done((f32[4,48,128]{2,1,0:T(8,128)S(1)}, f32[4,48,128]{2,1,0:T(8,128)S(1)}, u32[]{:S(2)}, u32[]{:S(2)}) %collective-permute-start.15) | collective-permute-done | bytes 98336 | tf_op jit(solution)/shard_map/ppermute | solution.py:431
  49.5 0.0 collective-permute-start.20
  49.5 0.0 collective-permute-done.14.rest_1_
  49.5 0.5 collective-permute-start.19
  50.0 2.3 %collective-permute-done.23.rest_3_ = f32[4,48,128]{2,1,0:T(8,128)S(1)} collective-permute-done((f32[4,48,128]{2,1,0:T(8,128)S(1)}, f32[4,48,128]{2,1,0:T(8,128)S(1)}, u32[]{:S(2)}, u32[]{:S(2)}) %collective-permute-start.23) | collective-permute-done | bytes 98336 | tf_op jit(solution)/shard_map/ppermute | solution.py:431
  52.4 0.0 collective-permute-start.24
  52.4 0.5 collective-permute-done.22.rest_2_.refs_6_
  52.9 0.0 collective-permute-start.18
  52.9 0.3 collective-permute-done.21.rest_1_
  53.2 0.2 collective-permute-start.27
  53.4 0.0 collective-permute-done.20.rest_7_
  53.4 0.3 collective-permute-start.26
  53.7 0.0 collective-permute-done.19.rest_6_.refs_3_
  53.7 0.2 collective-permute-start.25
  53.9 0.3 collective-permute-done.18.rest_5_
  54.2 1.0 %shard_map.71.total_ref = f32[288,96]{1,0:T(8,128)S(1)} custom-call(bf16[32,96,256]{2,1,0:T(8,128)(2,1)S(1)} %get-tuple-element.13.xh_ref, bf16[32,96,256]{2,1,0:T(8,128)(2,1)S(1)} %get-tuple-element.14.xl_ref, f32[4,48,128]{2,1,0:T(8,128)S(1)} %pad_maximum_fusion.rest_0_.refs_0_, f32[4,48,128]{2,1,0:T(8,128)S(1)} %collective-permute-done.14.rest_1_, ...), custom_call_target="tpu_custom_call" | custom-call | tf_op jit(solution)/shard_map/pallas_call | solution.py:343
  55.3 1.4 %shard_map.72 = f32[48,96]{1,0:T(8,128)S(1)} custom-call(bf16[32,96,256]{2,1,0:T(8,128)(2,1)S(1)} %get-tuple-element.13.xh_ref, bf16[32,96,256]{2,1,0:T(8,128)(2,1)S(1)} %get-tuple-element.14.xl_ref, f32[48,96]{1,0:T(8,128)S(1)} %get-tuple-element.15.w_ref, f32[288,96]{1,0:T(8,128)S(1)} %shard_map.71.total_ref, ...), custom_call_target="tpu_custom_call" | custom-call | tf_op jit(solution)/shard_map/pallas_call | solution.py:367
  56.7 1.5 %collective-permute-start.28 = (f32[48,96]{1,0:T(8,128)S(1)}, f32[48,96]{1,0:T(8,128)S(1)}, u32[]{:S(2)}, u32[]{:S(2)}) collective-permute-start(f32[48,96]{1,0:T(8,128)S(1)} %shard_map.72), channel_id=1, source_target_pairs={{0,4},{1,5},{2,6},{3,7},{4,0},{5,1},{6,2},{7,3},{8,12},{9,13},{10,... | collective-permute-start | bytes 55304 | tf_op jit(solution)/shard_map/ppermute | solution.py:431
  58.2 2.4 %collective-permute-done.28 = f32[48,96]{1,0:T(8,128)S(1)} collective-permute-done((f32[48,96]{1,0:T(8,128)S(1)}, f32[48,96]{1,0:T(8,128)S(1)}, u32[]{:S(2)}, u32[]{:S(2)}) %collective-permute-start.28) | collective-permute-done | bytes 18464 | tf_op jit(solution)/shard_map/ppermute | solution.py:431
  60.6 2.0 %collective-permute-start.31 = (f32[2,48,96]{2,1,0:T(8,128)S(1)}, f32[2,48,96]{2,1,0:T(8,128)S(1)}, u32[]{:S(2)}, u32[]{:S(2)}) collective-permute-start(f32[2,48,96]{2,1,0:T(8,128)S(1)} %pad_maximum_fusion.5.refs_0_), channel_id=1, source_target_pairs={{0,24},{1,25},{2,26},{3,27},{4,28},{5,29},{6,30},{7,31},{8,16},{9,... | collective-permute-start | bytes 110600 | tf_op jit(solution)/shard_map/ppermute | solution.py:431
  62.6 0.6 collective-permute-start.30
  63.2 1.8 %collective-permute-start.29 = (f32[2,48,96]{2,1,0:T(8,128)S(1)}, f32[2,48,96]{2,1,0:T(8,128)S(1)}, u32[]{:S(2)}, u32[]{:S(2)}) collective-permute-start(f32[2,48,96]{2,1,0:T(8,128)S(1)} %pad_maximum_fusion.5.refs_0_), channel_id=1, source_target_pairs={{0,8},{1,9},{2,10},{3,11},{4,12},{5,13},{6,14},{7,15},{8,0},{9,1},... | collective-permute-start | bytes 110600 | tf_op jit(solution)/shard_map/ppermute | solution.py:431
  65.1 1.0 %shard_map.74 = f32[32,32,48]{2,1,0:T(8,128)} custom-call(f32[4,48,128]{2,1,0:T(8,128)S(1)} %pad_maximum_fusion.rest_0_.refs_0_, f32[4,48,128]{2,1,0:T(8,128)S(1)} %collective-permute-done.17.rest_4_.refs_1_, f32[4,48,128]{2,1,0:T(8,128)S(1)} %collective-permute-done.15.rest_2_.refs_2_, f32[4,48,128]{2,1,0:T(8,128)S(1)} %collective-permute-done.19.rest_6_.refs_3_, ...), custom_call_target="tpu_custom_call" | custom-call | tf_op jit(solution)/shard_map/pallas_call | solution.py:388
  66.1 1.0 %collective-permute-done.31.refs_3_ = f32[2,48,96]{2,1,0:T(8,128)S(1)} collective-permute-done((f32[2,48,96]{2,1,0:T(8,128)S(1)}, f32[2,48,96]{2,1,0:T(8,128)S(1)}, u32[]{:S(2)}, u32[]{:S(2)}) %collective-permute-start.31) | collective-permute-done | bytes 36896 | tf_op jit(solution)/shard_map/ppermute | solution.py:431
  67.1 1.1 %collective-permute-done.30.refs_2_ = f32[2,48,96]{2,1,0:T(8,128)S(1)} collective-permute-done((f32[2,48,96]{2,1,0:T(8,128)S(1)}, f32[2,48,96]{2,1,0:T(8,128)S(1)}, u32[]{:S(2)}, u32[]{:S(2)}) %collective-permute-start.30) | collective-permute-done | bytes 36896 | tf_op jit(solution)/shard_map/ppermute | solution.py:431
  68.1 0.8 %shard_map.73 = f32[48,768]{1,0:T(8,128)} custom-call(f32[2,48,96]{2,1,0:T(8,128)S(1)} %pad_maximum_fusion.5.refs_0_, f32[2,48,96]{2,1,0:T(8,128)S(1)} %collective-permute-done.29.refs_1_, f32[2,48,96]{2,1,0:T(8,128)S(1)} %collective-permute-done.30.refs_2_, f32[2,48,96]{2,1,0:T(8,128)S(1)} %collective-permute-done.31.refs_3_), custom_call_target="tpu_custom_call" | custom-call | tf_op jit(solution)/shard_map/pallas_call | solution.py:415
  (25 shorter events, 0.2 us)
Async XLA Ops:
  8.1 1.9 %collective-permute-start = (f32[792,128]{1,0:T(8,128)S(1)}, f32[792,128]{1,0:T(8,128)S(1)}, u32[]{:S(2)}, u32[]{:S(2)}) collective-permute-start(f32[792,128]{1,0:T(8,128)S(1)} %get-tuple-element.17), channel_id=1, source_target_pairs={{0,1},{1,0},{2,3},{3,2},{4,5},{5,4},{6,7},{7,6},{8,9},{9,8},{10,11... | collective-permute-start | bytes 1216520 | tf_op jit(solution)/shard_map/ppermute | solution.py:431
  10.0 4.8 %collective-permute-start.4 = (f32[768,128]{1,0:T(8,128)S(1)}, f32[768,128]{1,0:T(8,128)S(1)}, u32[]{:S(2)}, u32[]{:S(2)}) collective-permute-start(f32[768,128]{1,0:T(8,128)S(1)} %get-tuple-element.23), channel_id=1, source_target_pairs={{0,1},{1,0},{2,3},{3,2},{4,5},{5,4},{6,7},{7,6},{8,9},{9,8},{10,11... | collective-permute-start | bytes 1179656 | tf_op jit(solution)/shard_map/ppermute | solution.py:431
  10.4 18.2 %copy-start = (f32[48,32,32]{0,2,1:T(8,128)S(1)}, f32[48,32,32]{0,2,1:T(8,128)}, u32[]{:S(2)}) copy-start(f32[48,32,32]{0,2,1:T(8,128)} %param.9) | copy-start | bytes 589828
  10.4 7.9 %collective-permute-start.3 = (f32[192,128]{1,0:T(8,128)S(1)}, f32[192,128]{1,0:T(8,128)S(1)}, u32[]{:S(2)}, u32[]{:S(2)}) collective-permute-start(f32[192,128]{1,0:T(8,128)S(1)} %get-tuple-element.25), channel_id=1, source_target_pairs={{0,6},{1,7},{2,4},{3,5},{4,2},{5,3},{6,0},{7,1},{8,14},{9,15},{10,... | collective-permute-start | bytes 294920 | tf_op jit(solution)/shard_map/ppermute | solution.py:431
  14.1 6.2 %collective-permute-start.2 = (f32[192,128]{1,0:T(8,128)S(1)}, f32[192,128]{1,0:T(8,128)S(1)}, u32[]{:S(2)}, u32[]{:S(2)}) collective-permute-start(f32[192,128]{1,0:T(8,128)S(1)} %get-tuple-element.26), channel_id=1, source_target_pairs={{0,4},{1,5},{2,6},{3,7},{4,0},{5,1},{6,2},{7,3},{8,12},{9,13},{10,... | collective-permute-start | bytes 294920 | tf_op jit(solution)/shard_map/ppermute | solution.py:431
  14.6 7.6 %collective-permute-start.1 = (f32[216,128]{1,0:T(8,128)S(1)}, f32[216,128]{1,0:T(8,128)S(1)}, u32[]{:S(2)}, u32[]{:S(2)}) collective-permute-start(f32[216,128]{1,0:T(8,128)S(1)} %slice_add_fusion.mine_ref), channel_id=1, source_target_pairs={{0,2},{1,3},{2,0},{3,1},{4,6},{5,7},{6,4},{7,5},{8,10},{9,11},{10,... | collective-permute-start | bytes 331784 | tf_op jit(solution)/shard_map/ppermute | solution.py:431
  14.9 7.4 %collective-permute-start.7 = (f32[192,128]{1,0:T(8,128)S(1)}, f32[192,128]{1,0:T(8,128)S(1)}, u32[]{:S(2)}, u32[]{:S(2)}) collective-permute-start(f32[192,128]{1,0:T(8,128)S(1)} %get-tuple-element.28), channel_id=1, source_target_pairs={{0,6},{1,7},{2,4},{3,5},{4,2},{5,3},{6,0},{7,1},{8,14},{9,15},{10,... | collective-permute-start | bytes 294920 | tf_op jit(solution)/shard_map/ppermute | solution.py:431
  17.8 6.2 %collective-permute-start.6 = (f32[192,128]{1,0:T(8,128)S(1)}, f32[192,128]{1,0:T(8,128)S(1)}, u32[]{:S(2)}, u32[]{:S(2)}) collective-permute-start(f32[192,128]{1,0:T(8,128)S(1)} %get-tuple-element.29), channel_id=1, source_target_pairs={{0,2},{1,3},{2,0},{3,1},{4,6},{5,7},{6,4},{7,5},{8,10},{9,11},{10,... | collective-permute-start | bytes 294920 | tf_op jit(solution)/shard_map/ppermute | solution.py:431
  18.3 5.7 %collective-permute-start.5 = (f32[192,128]{1,0:T(8,128)S(1)}, f32[192,128]{1,0:T(8,128)S(1)}, u32[]{:S(2)}, u32[]{:S(2)}) collective-permute-start(f32[192,128]{1,0:T(8,128)S(1)} %get-tuple-element.30), channel_id=1, source_target_pairs={{0,4},{1,5},{2,6},{3,7},{4,0},{5,1},{6,2},{7,3},{8,12},{9,13},{10,... | collective-permute-start | bytes 294920 | tf_op jit(solution)/shard_map/ppermute | solution.py:431
  24.1 6.3 %collective-permute-start.8 = (f32[48,256]{1,0:T(8,128)S(1)}, f32[48,256]{1,0:T(8,128)S(1)}, u32[]{:S(2)}, u32[]{:S(2)}) collective-permute-start(f32[48,256]{1,0:T(8,128)S(1)} %pad_maximum_fusion.2), channel_id=1, source_target_pairs={{0,24},{1,25},{2,26},{3,27},{4,28},{5,29},{6,30},{7,31},{8,16},{9,... | collective-permute-start | bytes 147464 | tf_op jit(solution)/shard_map/ppermute | solution.py:431
  27.9 5.0 %collective-permute-start.9 = (f32[48,256]{1,0:T(8,128)S(1)}, f32[48,256]{1,0:T(8,128)S(1)}, u32[]{:S(2)}, u32[]{:S(2)}) collective-permute-start(f32[48,256]{1,0:T(8,128)S(1)} %pad_maximum_fusion.3), channel_id=1, source_target_pairs={{0,16},{1,17},{2,18},{3,19},{4,20},{5,21},{6,22},{7,23},{8,24},{9,... | collective-permute-start | bytes 147464 | tf_op jit(solution)/shard_map/ppermute | solution.py:431
  27.9 5.0 %collective-permute-start.10 = (f32[48,256]{1,0:T(8,128)S(1)}, f32[48,256]{1,0:T(8,128)S(1)}, u32[]{:S(2)}, u32[]{:S(2)}) collective-permute-start(f32[48,256]{1,0:T(8,128)S(1)} %pad_maximum_fusion.4), channel_id=1, source_target_pairs={{0,8},{1,9},{2,10},{3,11},{4,12},{5,13},{6,14},{7,15},{8,0},{9,1},... | collective-permute-start | bytes 147464 | tf_op jit(solution)/shard_map/ppermute | solution.py:431
  32.9 6.0 %collective-permute-start.13 = (f32[48,256]{1,0:T(8,128)S(1)}, f32[48,256]{1,0:T(8,128)S(1)}, u32[]{:S(2)}, u32[]{:S(2)}) collective-permute-start(f32[48,256]{1,0:T(8,128)S(1)} %fusion.1), channel_id=1, source_target_pairs={{0,24},{1,25},{2,26},{3,27},{4,28},{5,29},{6,30},{7,31},{8,16},{9,... | collective-permute-start | bytes 147464 | tf_op jit(solution)/shard_map/ppermute | solution.py:431
  34.8 5.5 %collective-permute-start.12 = (f32[48,256]{1,0:T(8,128)S(1)}, f32[48,256]{1,0:T(8,128)S(1)}, u32[]{:S(2)}, u32[]{:S(2)}) collective-permute-start(f32[48,256]{1,0:T(8,128)S(1)} %fusion.1), channel_id=1, source_target_pairs={{0,16},{1,17},{2,18},{3,19},{4,20},{5,21},{6,22},{7,23},{8,24},{9,... | collective-permute-start | bytes 147464 | tf_op jit(solution)/shard_map/ppermute | solution.py:431
  35.1 5.2 %collective-permute-start.11 = (f32[48,256]{1,0:T(8,128)S(1)}, f32[48,256]{1,0:T(8,128)S(1)}, u32[]{:S(2)}, u32[]{:S(2)}) collective-permute-start(f32[48,256]{1,0:T(8,128)S(1)} %fusion.1), channel_id=1, source_target_pairs={{0,8},{1,9},{2,10},{3,11},{4,12},{5,13},{6,14},{7,15},{8,0},{9,1},... | collective-permute-start | bytes 147464 | tf_op jit(solution)/shard_map/ppermute | solution.py:431
  40.4 6.3 %collective-permute-start.17 = (f32[4,48,128]{2,1,0:T(8,128)S(1)}, f32[4,48,128]{2,1,0:T(8,128)S(1)}, u32[]{:S(2)}, u32[]{:S(2)}) collective-permute-start(f32[4,48,128]{2,1,0:T(8,128)S(1)} %pad_maximum_fusion.rest_0_.refs_0_), channel_id=1, source_target_pairs={{0,1},{1,0},{2,3},{3,2},{4,5},{5,4},{6,7},{7,6},{8,9},{9,8},{10,11... | collective-permute-start | bytes 294920 | tf_op jit(solution)/shard_map/ppermute | solution.py:431
  40.5 6.5 %collective-permute-start.16 = (f32[4,48,128]{2,1,0:T(8,128)S(1)}, f32[4,48,128]{2,1,0:T(8,128)S(1)}, u32[]{:S(2)}, u32[]{:S(2)}) collective-permute-start(f32[4,48,128]{2,1,0:T(8,128)S(1)} %pad_maximum_fusion.rest_0_.refs_0_), channel_id=1, source_target_pairs={{0,6},{1,7},{2,4},{3,5},{4,2},{5,3},{6,0},{7,1},{8,14},{9,15},{10,... | collective-permute-start | bytes 294920 | tf_op jit(solution)/shard_map/ppermute | solution.py:431
  43.2 6.4 %collective-permute-start.15 = (f32[4,48,128]{2,1,0:T(8,128)S(1)}, f32[4,48,128]{2,1,0:T(8,128)S(1)}, u32[]{:S(2)}, u32[]{:S(2)}) collective-permute-start(f32[4,48,128]{2,1,0:T(8,128)S(1)} %pad_maximum_fusion.rest_0_.refs_0_), channel_id=1, source_target_pairs={{0,2},{1,3},{2,0},{3,1},{4,6},{5,7},{6,4},{7,5},{8,10},{9,11},{10,... | collective-permute-start | bytes 294920 | tf_op jit(solution)/shard_map/ppermute | solution.py:431
  43.4 6.2 %collective-permute-start.14 = (f32[4,48,128]{2,1,0:T(8,128)S(1)}, f32[4,48,128]{2,1,0:T(8,128)S(1)}, u32[]{:S(2)}, u32[]{:S(2)}) collective-permute-start(f32[4,48,128]{2,1,0:T(8,128)S(1)} %pad_maximum_fusion.rest_0_.refs_0_), channel_id=1, source_target_pairs={{0,4},{1,5},{2,6},{3,7},{4,0},{5,1},{6,2},{7,3},{8,12},{9,13},{10,... | collective-permute-start | bytes 294920 | tf_op jit(solution)/shard_map/ppermute | solution.py:431
  44.0 8.3 %collective-permute-start.23 = (f32[4,48,128]{2,1,0:T(8,128)S(1)}, f32[4,48,128]{2,1,0:T(8,128)S(1)}, u32[]{:S(2)}, u32[]{:S(2)}) collective-permute-start(f32[4,48,128]{2,1,0:T(8,128)S(1)} %pad_maximum_fusion.1.rest_0_.refs_4_), channel_id=1, source_target_pairs={{0,6},{1,7},{2,4},{3,5},{4,2},{5,3},{6,0},{7,1},{8,14},{9,15},{10,... | collective-permute-start | bytes 294920 | tf_op jit(solution)/shard_map/ppermute | solution.py:431
  46.7 6.2 %collective-permute-start.22 = (f32[4,48,128]{2,1,0:T(8,128)S(1)}, f32[4,48,128]{2,1,0:T(8,128)S(1)}, u32[]{:S(2)}, u32[]{:S(2)}) collective-permute-start(f32[4,48,128]{2,1,0:T(8,128)S(1)} %pad_maximum_fusion.1.rest_0_.refs_4_), channel_id=1, source_target_pairs={{0,2},{1,3},{2,0},{3,1},{4,6},{5,7},{6,4},{7,5},{8,10},{9,11},{10,... | collective-permute-start | bytes 294920 | tf_op jit(solution)/shard_map/ppermute | solution.py:431
  46.9 6.2 %collective-permute-start.21 = (f32[4,48,128]{2,1,0:T(8,128)S(1)}, f32[4,48,128]{2,1,0:T(8,128)S(1)}, u32[]{:S(2)}, u32[]{:S(2)}) collective-permute-start(f32[4,48,128]{2,1,0:T(8,128)S(1)} %pad_maximum_fusion.1.rest_0_.refs_4_), channel_id=1, source_target_pairs={{0,4},{1,5},{2,6},{3,7},{4,0},{5,1},{6,2},{7,3},{8,12},{9,13},{10,... | collective-permute-start | bytes 294920 | tf_op jit(solution)/shard_map/ppermute | solution.py:431
  49.5 3.9 %collective-permute-start.20 = (f32[4,48,128]{2,1,0:T(8,128)S(1)}, f32[4,48,128]{2,1,0:T(8,128)S(1)}, u32[]{:S(2)}, u32[]{:S(2)}) collective-permute-start(f32[4,48,128]{2,1,0:T(8,128)S(1)} %collective-permute-done.16.rest_3_), channel_id=1, source_target_pairs={{0,1},{1,0},{2,3},{3,2},{4,5},{5,4},{6,7},{7,6},{8,9},{9,8},{10,11... | collective-permute-start | bytes 294920 | tf_op jit(solution)/shard_map/ppermute | solution.py:431
  49.5 4.2 %collective-permute-start.19 = (f32[4,48,128]{2,1,0:T(8,128)S(1)}, f32[4,48,128]{2,1,0:T(8,128)S(1)}, u32[]{:S(2)}, u32[]{:S(2)}) collective-permute-start(f32[4,48,128]{2,1,0:T(8,128)S(1)} %collective-permute-done.15.rest_2_.refs_2_), channel_id=1, source_target_pairs={{0,1},{1,0},{2,3},{3,2},{4,5},{5,4},{6,7},{7,6},{8,9},{9,8},{10,11... | collective-permute-start | bytes 294920 | tf_op jit(solution)/shard_map/ppermute | solution.py:431
  52.4 2.9 %collective-permute-start.24 = (f32[4,48,128]{2,1,0:T(8,128)S(1)}, f32[4,48,128]{2,1,0:T(8,128)S(1)}, u32[]{:S(2)}, u32[]{:S(2)}) collective-permute-start(f32[4,48,128]{2,1,0:T(8,128)S(1)} %pad_maximum_fusion.1.rest_0_.refs_4_), channel_id=1, source_target_pairs={{0,1},{1,0},{2,3},{3,2},{4,5},{5,4},{6,7},{7,6},{8,9},{9,8},{10,11... | collective-permute-start | bytes 294920 | tf_op jit(solution)/shard_map/ppermute | solution.py:431
  52.9 1.3 %collective-permute-start.18 = (f32[4,48,128]{2,1,0:T(8,128)S(1)}, f32[4,48,128]{2,1,0:T(8,128)S(1)}, u32[]{:S(2)}, u32[]{:S(2)}) collective-permute-start(f32[4,48,128]{2,1,0:T(8,128)S(1)} %collective-permute-done.14.rest_1_), channel_id=1, source_target_pairs={{0,1},{1,0},{2,3},{3,2},{4,5},{5,4},{6,7},{7,6},{8,9},{9,8},{10,11... | collective-permute-start | bytes 294920 | tf_op jit(solution)/shard_map/ppermute | solution.py:431
  53.2 2.1 %collective-permute-start.27 = (f32[4,48,128]{2,1,0:T(8,128)S(1)}, f32[4,48,128]{2,1,0:T(8,128)S(1)}, u32[]{:S(2)}, u32[]{:S(2)}) collective-permute-start(f32[4,48,128]{2,1,0:T(8,128)S(1)} %collective-permute-done.23.rest_3_), channel_id=1, source_target_pairs={{0,1},{1,0},{2,3},{3,2},{4,5},{5,4},{6,7},{7,6},{8,9},{9,8},{10,11... | collective-permute-start | bytes 294920 | tf_op jit(solution)/shard_map/ppermute | solution.py:431
  53.4 1.9 %collective-permute-start.26 = (f32[4,48,128]{2,1,0:T(8,128)S(1)}, f32[4,48,128]{2,1,0:T(8,128)S(1)}, u32[]{:S(2)}, u32[]{:S(2)}) collective-permute-start(f32[4,48,128]{2,1,0:T(8,128)S(1)} %collective-permute-done.22.rest_2_.refs_6_), channel_id=1, source_target_pairs={{0,1},{1,0},{2,3},{3,2},{4,5},{5,4},{6,7},{7,6},{8,9},{9,8},{10,11... | collective-permute-start | bytes 294920 | tf_op jit(solution)/shard_map/ppermute | solution.py:431
  53.7 1.6 %collective-permute-start.25 = (f32[4,48,128]{2,1,0:T(8,128)S(1)}, f32[4,48,128]{2,1,0:T(8,128)S(1)}, u32[]{:S(2)}, u32[]{:S(2)}) collective-permute-start(f32[4,48,128]{2,1,0:T(8,128)S(1)} %collective-permute-done.21.rest_1_), channel_id=1, source_target_pairs={{0,1},{1,0},{2,3},{3,2},{4,5},{5,4},{6,7},{7,6},{8,9},{9,8},{10,11... | collective-permute-start | bytes 294920 | tf_op jit(solution)/shard_map/ppermute | solution.py:431
  56.7 3.9 %collective-permute-start.28 = (f32[48,96]{1,0:T(8,128)S(1)}, f32[48,96]{1,0:T(8,128)S(1)}, u32[]{:S(2)}, u32[]{:S(2)}) collective-permute-start(f32[48,96]{1,0:T(8,128)S(1)} %shard_map.72), channel_id=1, source_target_pairs={{0,4},{1,5},{2,6},{3,7},{4,0},{5,1},{6,2},{7,3},{8,12},{9,13},{10,... | collective-permute-start | bytes 55304 | tf_op jit(solution)/shard_map/ppermute | solution.py:431
  60.6 6.5 %collective-permute-start.31 = (f32[2,48,96]{2,1,0:T(8,128)S(1)}, f32[2,48,96]{2,1,0:T(8,128)S(1)}, u32[]{:S(2)}, u32[]{:S(2)}) collective-permute-start(f32[2,48,96]{2,1,0:T(8,128)S(1)} %pad_maximum_fusion.5.refs_0_), channel_id=1, source_target_pairs={{0,24},{1,25},{2,26},{3,27},{4,28},{5,29},{6,30},{7,31},{8,16},{9,... | collective-permute-start | bytes 110600 | tf_op jit(solution)/shard_map/ppermute | solution.py:431
  62.6 5.5 %collective-permute-start.30 = (f32[2,48,96]{2,1,0:T(8,128)S(1)}, f32[2,48,96]{2,1,0:T(8,128)S(1)}, u32[]{:S(2)}, u32[]{:S(2)}) collective-permute-start(f32[2,48,96]{2,1,0:T(8,128)S(1)} %pad_maximum_fusion.5.refs_0_), channel_id=1, source_target_pairs={{0,16},{1,17},{2,18},{3,19},{4,20},{5,21},{6,22},{7,23},{8,24},{9,... | collective-permute-start | bytes 110600 | tf_op jit(solution)/shard_map/ppermute | solution.py:431
  63.2 4.9 %collective-permute-start.29 = (f32[2,48,96]{2,1,0:T(8,128)S(1)}, f32[2,48,96]{2,1,0:T(8,128)S(1)}, u32[]{:S(2)}, u32[]{:S(2)}) collective-permute-start(f32[2,48,96]{2,1,0:T(8,128)S(1)} %pad_maximum_fusion.5.refs_0_), channel_id=1, source_target_pairs={{0,8},{1,9},{2,10},{3,11},{4,12},{5,13},{6,14},{7,15},{8,0},{9,1},... | collective-permute-start | bytes 110600 | tf_op jit(solution)/shard_map/ppermute | solution.py:431

commit v17 on v16

--- a/solution.py
+++ b/solution.py
@@ -303,37 +303,39 @@
     )(mine, other, h_columns)
 
 
-def accumulate(xh_ref, xl_ref, part_refs, all_ref, chain, total):
+def accumulate(xh_ref, xl_ref, part_refs, all_ref, rel_core, total):
     height, planes, _ = xh_ref.shape
     me_sp = lax.axis_index("sp")
     me_bd = lax.axis_index("bd")
-    bands = lax.axis_size("bd")
     pieces = lax.axis_size("sp")
-    tall = height // bands
+    tall = height // lax.axis_size("bd")
     wide = 2 * LANES // pieces
-    for slot, part_ref in enumerate(part_refs):
-        rel_bd = slot // 4 + 2 * ((slot // 2) % 2)
+    core = lax.bitwise_xor(me_bd % 2, rel_core)
+    for partner, part_ref in enumerate(part_refs):
+        row = lax.bitwise_xor(me_bd // 2, partner // 2)
         for inner in range(4):
-            rel_sp = slot % 2 + 2 * inner
-            owner = lax.bitwise_xor(me_bd, rel_bd) * pieces + lax.bitwise_xor(me_sp, rel_sp)
-            all_ref[owner] = part_ref[inner]
-    for part in range(bands):
-        first_row = part * tall + 4 * chain
-        halves = [
-            exchange_blocks([all_ref[part * pieces + column * 4 + k] for k in range(4)], wide)
-            for column in range(2)]
-        rows = jnp.concatenate([halves[column][row] for row in range(4) for column in range(2)], axis=1)
-        high, low = split(rows)
-        here = jnp.concatenate([high, low], axis=0)
-        image = [
-            jnp.concatenate([ref[first_row + row] for row in range(4)], axis=1) for ref in (xh_ref, xl_ref)]
-        total = total + dot_nt(jnp.concatenate(image + [here], axis=0), here)
+            column = lax.bitwise_xor(me_sp, partner % 2 + 2 * inner)
+            all_ref[row * pieces + column] = part_ref[inner]
+    for row in range(2):
+        for quarter in range(2):
+            first_row = (2 * row + core) * tall + 4 * quarter
+            halves = [
+                exchange_blocks(
+                    [all_ref[row * pieces + column * 4 + k][:, quarter * LANES:(quarter + 1) * LANES]
+                     for k in range(4)], wide)
+                for column in range(2)]
+            rows = jnp.concatenate([halves[column][k] for k in range(4) for column in range(2)], axis=1)
+            high, low = split(rows)
+            here = jnp.concatenate([high, low], axis=0)
+            image = [
+                jnp.concatenate([ref[first_row + k] for k in range(4)], axis=1) for ref in (xh_ref, xl_ref)]
+            total = total + dot_nt(jnp.concatenate(image + [here], axis=0), here)
     return total
 
 
 def first_kernel(xh_ref, xl_ref, *rest):
-    part_refs = rest[:8]
-    total_out, all_ref = rest[8:]
+    part_refs = rest[:4]
+    total_out, all_ref = rest[4:]
     total_out[...] = accumulate(xh_ref, xl_ref, part_refs, all_ref, 0, jnp.zeros(total_out.shape, F32))
 
 
@@ -344,14 +346,14 @@
         first_kernel,
         out_shape=jax.ShapeDtypeStruct((2 * (planes + rank), 2 * rank), F32),
         in_specs=in_vmem(2 + len(parts)),
-        scratch_shapes=[pltpu.VMEM((32, rank, LANES), F32)],
+        scratch_shapes=[pltpu.VMEM((16, rank, 2 * LANES), F32)],
         compiler_params=pltpu.CompilerParams(vmem_limit_bytes=VMEM_LIMIT),
     )(x_high, x_low, *parts)
 
 
 def second_kernel(xh_ref, xl_ref, w_ref, total_ref, *rest):
-    part_refs = rest[:8]
-    w_out, all_ref = rest[8:]
+    part_refs = rest[:4]
+    w_out, all_ref = rest[4:]
     planes = xh_ref.shape[1]
     rank = w_ref.shape[0]
     total = accumulate(xh_ref, xl_ref, part_refs, all_ref, 1, total_ref[...])
@@ -368,7 +370,7 @@
         second_kernel,
         out_shape=jax.ShapeDtypeStruct(w_here.shape, F32),
         in_specs=in_vmem(4 + len(parts)),
-        scratch_shapes=[pltpu.VMEM((32, rank, LANES), F32)],
+        scratch_shapes=[pltpu.VMEM((16, rank, 2 * LANES), F32)],
         compiler_params=pltpu.CompilerParams(vmem_limit_bytes=VMEM_LIMIT),
     )(x_high, x_low, w_here, total, *parts)
 
@@ -377,11 +379,10 @@
     h_out = refs[-1]
     me_bd = lax.axis_index("bd")
     tall = h_out.shape[0] // lax.axis_size("bd")
-    for chain in range(2):
-        for rel_bd in range(4):
-            piece = refs[4 * chain + rel_bd][0]
-            first = lax.bitwise_xor(me_bd, rel_bd) * tall + 4 * chain
-            h_out[pl.ds(first, 4)] = jnp.transpose(piece).reshape((4,) + h_out.shape[1:])
+    for rel_bd in range(4):
+        piece = refs[rel_bd][0]
+        first = lax.bitwise_xor(me_bd, rel_bd) * tall
+        h_out[pl.ds(first, tall)] = jnp.transpose(piece).reshape((tall,) + h_out.shape[1:])
 
 
 def place_h_call(parts, shape):
@@ -463,15 +464,12 @@
     line = [line[0]] + [send(line[k], 2 * k, 0) for k in (3, 2, 1)]
     h_piece = ratio * ((line[0] + line[1]) + (line[2] + line[3]))
     h_line = [h_piece] + [send(h_piece, 2 * k, 0) for k in range(1, 4)]
-    chains = []
-    for first in (0, LANES):
-        mine = jnp.stack([value[:, first:first + LANES] for value in h_line])
-        chains.append([mine] + around([mine] * 4))
-    first_parts = chains[0] + [send(value, 0, 1) for value in chains[0]]
+    mine = jnp.stack(h_line)
+    first_parts = [mine] + around([mine] * 4)
+    second_parts = [send(value, 0, 1) for value in first_parts]
     total = first_call(x_high, x_low, first_parts)
-    second_parts = chains[1] + [send(value, 0, 1) for value in chains[1]]
     w_piece = second_call(x_high, x_low, w_here, total, second_parts)
-    own = [parts[k] for parts in (first_parts, second_parts) for k in (0, 4, 2, 6)]
+    own = [parts[k] for k in (0, 2) for parts in (first_parts, second_parts)]
     h_next = place_h_call(own, h_columns.shape)
     w_pair = jnp.stack([w_piece, send(w_piece, 1, 0)])
     w_next = gather_w_call([w_pair] + [send(w_pair, 2 * k, 0) for k in range(1, 4)])

time: 69.1 us -> 66 us (0.955)
  starting transfers between devices: 34 us -> 28.8 us
  waiting for transfers between devices: 21.2 us -> 23.4 us
    ppermute x32 -> x25, starting transfers between devices: 34 us -> 28.8 us  [send(): return lax.ppermute(value, ('sp', 'bd'), pairs)]
    ppermute x32 -> x25, waiting for transfers between devices: 21.2 us -> 23.4 us  [send(): return lax.ppermute(value, ('sp', 'bd'), pairs)]
  transfers between devices with their start and end apart: 32 -> 25, of which waited for: 16 -> 15; matrix products, arithmetic and copies ran while one was open for 0% -> 0% of each run, Pallas kernels for 4% -> 5%
where the time goes in v17:
time: 66 us; the launch traced here: 65.8 us
  starting transfers between devices  28.8 us (44%)
  waiting for transfers between devices  23.4 us (35%)
  Pallas kernels  12.7 us (19%)
  between operations  0.75 us (1%)
    ppermute x25, starting transfers between devices, send(): return lax.ppermute(value, ('sp', 'bd'), pairs)  28.8 us
    ppermute x25, waiting for transfers between devices, send(): return lax.ppermute(value, ('sp', 'bd'), pairs)  23.4 us
    pallas_call x1, Pallas kernels, blur_call(): pl.pallas_call(blur_kernel, out_shape=[jax.ShapeDtypeStruct(image, BF16)]...  7.47 us
    pallas_call x1, Pallas kernels, second_call(): pl.pallas_call(second_kernel, out_shape=jax.ShapeDtypeStruct(w_here.shape...  1.42 us
  transfers between devices with their start and end apart: 25, of which 15 were waited for; matrix products, arithmetic and copies ran while one was open for 0% of the time, Pallas kernels for 5%

profile of v17, /device:TPU:0, one launch (start us, length us, event | category | flops | bytes accessed | tf_op | source)
XLA Modules:
  0.0 65.8 jit_solution(8719071081630159866)
XLA Ops:
  0.6 7.5 %shard_map.68 = (bf16[32,96,256]{2,1,0:T(8,128)(2,1)S(1)}, bf16[32,96,256]{2,1,0:T(8,128)(2,1)S(1)}, f32[48,96]{1,0:T(8,128)S(1)}, bf16[96,256]{1,0:T(8,128)(2,1...) custom-call(f32[96,32,256]{2,1,0:T(8,128)} %bitcast.19, f32[25,1,96]{2,1,0:T(1,128)} %bitcast.28, ...), custom_call_target="tpu_custom_call" | custom-call | tf_op jit(solution)/shard_map/pallas_call | solution.py:274
  8.1 0.5 collective-permute-start
  8.6 0.7 %shard_map.69 = (f32[768,128]{1,0:T(8,128)S(1)}, f32[768,128]{1,0:T(8,128)S(1)}) custom-call(bf16[32,96,256]{2,1,0:T(8,128)(2,1)S(1)} %get-tuple-element.13.xh_ref, bf16[32,96,256]{2,1,0:T(8,128)(2,1)S(1)} %get-tuple-element.14.xl_ref, bf16[96,256]{1,0:T(8,128)(2,1)S(1)} %get-tuple-element.18.w_both_ref), custom_call_target="tpu_custom_call" | custom-call | tf_op jit(solution)/shard_map/pallas_call | solution.py:257
  9.3 0.7 %collective-permute-done = f32[792,128]{1,0:T(8,128)S(1)} collective-permute-done((f32[792,128]{1,0:T(8,128)S(1)}, f32[792,128]{1,0:T(8,128)S(1)}, u32[]{:S(2)}, u32[]{:S(2)}) %collective-permute-start) | collective-permute-done | bytes 405536 | tf_op jit(solution)/shard_map/ppermute | solution.py:432
  10.0 0.4 collective-permute-start.4
  10.4 0.0 copy-start
  10.4 3.7 %collective-permute-start.3 = (f32[192,128]{1,0:T(8,128)S(1)}, f32[192,128]{1,0:T(8,128)S(1)}, u32[]{:S(2)}, u32[]{:S(2)}) collective-permute-start(f32[192,128]{1,0:T(8,128)S(1)} %get-tuple-element.25), channel_id=1, source_target_pairs={{0,6},{1,7},{2,4},{3,5},{4,2},{5,3},{6,0},{7,1},{8,14},{9,15},{10,... | collective-permute-start | bytes 294920 | tf_op jit(solution)/shard_map/ppermute | solution.py:432
  14.1 0.5 collective-permute-start.2
  14.6 0.2 collective-permute-start.1
  14.8 0.0 collective-permute-done.4
  14.8 0.1 slice_add_fusion.4
  14.9 2.9 %collective-permute-start.7 = (f32[192,128]{1,0:T(8,128)S(1)}, f32[192,128]{1,0:T(8,128)S(1)}, u32[]{:S(2)}, u32[]{:S(2)}) collective-permute-start(f32[192,128]{1,0:T(8,128)S(1)} %get-tuple-element.28), channel_id=1, source_target_pairs={{0,6},{1,7},{2,4},{3,5},{4,2},{5,3},{6,0},{7,1},{8,14},{9,15},{10,... | collective-permute-start | bytes 294920 | tf_op jit(solution)/shard_map/ppermute | solution.py:432
  17.8 0.5 collective-permute-start.6
  18.3 0.0 collective-permute-done.3
  18.3 1.3 %collective-permute-start.5 = (f32[192,128]{1,0:T(8,128)S(1)}, f32[192,128]{1,0:T(8,128)S(1)}, u32[]{:S(2)}, u32[]{:S(2)}) collective-permute-start(f32[192,128]{1,0:T(8,128)S(1)} %get-tuple-element.30), channel_id=1, source_target_pairs={{0,4},{1,5},{2,6},{3,7},{4,0},{5,1},{6,2},{7,3},{8,12},{9,13},{10,... | collective-permute-start | bytes 294920 | tf_op jit(solution)/shard_map/ppermute | solution.py:432
  19.6 0.7 %collective-permute-done.2 = f32[192,128]{1,0:T(8,128)S(1)} collective-permute-done((f32[192,128]{1,0:T(8,128)S(1)}, f32[192,128]{1,0:T(8,128)S(1)}, u32[]{:S(2)}, u32[]{:S(2)}) %collective-permute-start.2) | collective-permute-done | bytes 98336 | tf_op jit(solution)/shard_map/ppermute | solution.py:432
  20.3 1.9 %collective-permute-done.1.other_ref = f32[216,128]{1,0:T(8,128)S(1)} collective-permute-done((f32[216,128]{1,0:T(8,128)S(1)}, f32[216,128]{1,0:T(8,128)S(1)}, u32[]{:S(2)}, u32[]{:S(2)}) %collective-permute-start.1) | collective-permute-done | bytes 110624 | tf_op jit(solution)/shard_map/ppermute | solution.py:432
  22.2 0.0 collective-permute-done.7
  22.2 1.7 %collective-permute-done.6 = f32[192,128]{1,0:T(8,128)S(1)} collective-permute-done((f32[192,128]{1,0:T(8,128)S(1)}, f32[192,128]{1,0:T(8,128)S(1)}, u32[]{:S(2)}, u32[]{:S(2)}) %collective-permute-start.6) | collective-permute-done | bytes 98336 | tf_op jit(solution)/shard_map/ppermute | solution.py:432
  24.0 0.0 collective-permute-done.5
  24.1 3.9 %collective-permute-start.8 = (f32[48,256]{1,0:T(8,128)S(1)}, f32[48,256]{1,0:T(8,128)S(1)}, u32[]{:S(2)}, u32[]{:S(2)}) collective-permute-start(f32[48,256]{1,0:T(8,128)S(1)} %pad_maximum_fusion.1), channel_id=1, source_target_pairs={{0,24},{1,25},{2,26},{3,27},{4,28},{5,29},{6,30},{7,31},{8,16},{9,... | collective-permute-start | bytes 147464 | tf_op jit(solution)/shard_map/ppermute | solution.py:432
  27.9 0.0 collective-permute-start.9
  27.9 0.6 collective-permute-start.10
  28.6 0.0 copy-done
  28.6 0.3 shard_map.70
  28.9 1.5 %collective-permute-done.8 = f32[48,256]{1,0:T(8,128)S(1)} collective-permute-done((f32[48,256]{1,0:T(8,128)S(1)}, f32[48,256]{1,0:T(8,128)S(1)}, u32[]{:S(2)}, u32[]{:S(2)}) %collective-permute-start.8) | collective-permute-done | bytes 49184 | tf_op jit(solution)/shard_map/ppermute | solution.py:432
  30.3 2.6 %collective-permute-done.9 = f32[48,256]{1,0:T(8,128)S(1)} collective-permute-done((f32[48,256]{1,0:T(8,128)S(1)}, f32[48,256]{1,0:T(8,128)S(1)}, u32[]{:S(2)}, u32[]{:S(2)}) %collective-permute-start.9) | collective-permute-done | bytes 49184 | tf_op jit(solution)/shard_map/ppermute | solution.py:432
  32.9 0.0 collective-permute-done.10
  32.9 1.9 %collective-permute-start.13 = (f32[48,256]{1,0:T(8,128)S(1)}, f32[48,256]{1,0:T(8,128)S(1)}, u32[]{:S(2)}, u32[]{:S(2)}) collective-permute-start(f32[48,256]{1,0:T(8,128)S(1)} %fusion.1), channel_id=1, source_target_pairs={{0,24},{1,25},{2,26},{3,27},{4,28},{5,29},{6,30},{7,31},{8,16},{9,... | collective-permute-start | bytes 147464 | tf_op jit(solution)/shard_map/ppermute | solution.py:432
  34.8 0.3 collective-permute-start.12
  35.1 2.3 %collective-permute-start.11 = (f32[48,256]{1,0:T(8,128)S(1)}, f32[48,256]{1,0:T(8,128)S(1)}, u32[]{:S(2)}, u32[]{:S(2)}) collective-permute-start(f32[48,256]{1,0:T(8,128)S(1)} %fusion.1), channel_id=1, source_target_pairs={{0,8},{1,9},{2,10},{3,11},{4,12},{5,13},{6,14},{7,15},{8,0},{9,1},... | collective-permute-start | bytes 147464 | tf_op jit(solution)/shard_map/ppermute | solution.py:432
  37.4 1.5 %collective-permute-done.13 = f32[48,256]{1,0:T(8,128)S(1)} collective-permute-done((f32[48,256]{1,0:T(8,128)S(1)}, f32[48,256]{1,0:T(8,128)S(1)}, u32[]{:S(2)}, u32[]{:S(2)}) %collective-permute-start.13) | collective-permute-done | bytes 49184 | tf_op jit(solution)/shard_map/ppermute | solution.py:432
  38.9 1.5 %collective-permute-done.12 = f32[48,256]{1,0:T(8,128)S(1)} collective-permute-done((f32[48,256]{1,0:T(8,128)S(1)}, f32[48,256]{1,0:T(8,128)S(1)}, u32[]{:S(2)}, u32[]{:S(2)}) %collective-permute-start.12) | collective-permute-done | bytes 49184 | tf_op jit(solution)/shard_map/ppermute | solution.py:432
  40.3 0.0 collective-permute-done.11
  40.4 2.7 %collective-permute-start.16 = (f32[4,48,256]{2,1,0:T(8,128)S(1)}, f32[4,48,256]{2,1,0:T(8,128)S(1)}, u32[]{:S(2)}, u32[]{:S(2)}) collective-permute-start(f32[4,48,256]{2,1,0:T(8,128)S(1)} %pad_maximum_fusion.rest_0_.refs_0_), channel_id=1, source_target_pairs={{0,6},{1,7},{2,4},{3,5},{4,2},{5,3},{6,0},{7,1},{8,14},{9,15},{10,... | collective-permute-start | bytes 589832 | tf_op jit(solution)/shard_map/ppermute | solution.py:432
  43.1 0.2 collective-permute-start.15
  43.3 0.6 collective-permute-start.14
  43.9 0.0 collective-permute-start.17
  43.9 4.9 %collective-permute-done.16.rest_3_ = f32[4,48,256]{2,1,0:T(8,128)S(1)} collective-permute-done((f32[4,48,256]{2,1,0:T(8,128)S(1)}, f32[4,48,256]{2,1,0:T(8,128)S(1)}, u32[]{:S(2)}, u32[]{:S(2)}) %collective-permute-start.16) | collective-permute-done | bytes 196640 | tf_op jit(solution)/shard_map/ppermute | solution.py:432
  48.9 0.0 collective-permute-start.20
  48.9 2.1 %collective-permute-done.15.rest_2_.refs_2_ = f32[4,48,256]{2,1,0:T(8,128)S(1)} collective-permute-done((f32[4,48,256]{2,1,0:T(8,128)S(1)}, f32[4,48,256]{2,1,0:T(8,128)S(1)}, u32[]{:S(2)}, u32[]{:S(2)}) %collective-permute-start.15) | collective-permute-done | bytes 196640 | tf_op jit(solution)/shard_map/ppermute | solution.py:432
  50.9 0.0 collective-permute-start.19
  50.9 0.3 collective-permute-done.14.rest_1_
  51.2 0.2 collective-permute-start.18
  51.4 1.0 %shard_map.71.total_ref = f32[288,96]{1,0:T(8,128)S(1)} custom-call(bf16[32,96,256]{2,1,0:T(8,128)(2,1)S(1)} %get-tuple-element.13.xh_ref, bf16[32,96,256]{2,1,0:T(8,128)(2,1)S(1)} %get-tuple-element.14.xl_ref, f32[4,48,256]{2,1,0:T(8,128)S(1)} %pad_maximum_fusion.rest_0_.refs_0_, f32[4,48,256]{2,1,0:T(8,128)S(1)} %collective-permute-done.14.rest_1_, ...), custom_call_target="tpu_custom_call" | custom-call | tf_op jit(solution)/shard_map/pallas_call | solution.py:345
  52.5 0.0 collective-permute-done.17.rest_0_.refs_1_
  52.5 0.0 collective-permute-done.20.rest_3_
  52.5 0.0 collective-permute-done.19.rest_2_.refs_3_
  52.5 0.1 collective-permute-done.18.rest_1_
  52.6 1.4 %shard_map.72 = f32[48,96]{1,0:T(8,128)S(1)} custom-call(bf16[32,96,256]{2,1,0:T(8,128)(2,1)S(1)} %get-tuple-element.13.xh_ref, bf16[32,96,256]{2,1,0:T(8,128)(2,1)S(1)} %get-tuple-element.14.xl_ref, f32[48,96]{1,0:T(8,128)S(1)} %get-tuple-element.15.w_ref, f32[288,96]{1,0:T(8,128)S(1)} %shard_map.71.total_ref, ...), custom_call_target="tpu_custom_call" | custom-call | tf_op jit(solution)/shard_map/pallas_call | solution.py:369
  54.1 1.6 %collective-permute-start.21 = (f32[48,96]{1,0:T(8,128)S(1)}, f32[48,96]{1,0:T(8,128)S(1)}, u32[]{:S(2)}, u32[]{:S(2)}) collective-permute-start(f32[48,96]{1,0:T(8,128)S(1)} %shard_map.72), channel_id=1, source_target_pairs={{0,4},{1,5},{2,6},{3,7},{4,0},{5,1},{6,2},{7,3},{8,12},{9,13},{10,... | collective-permute-start | bytes 55304 | tf_op jit(solution)/shard_map/ppermute | solution.py:432
  55.6 2.3 %collective-permute-done.21 = f32[48,96]{1,0:T(8,128)S(1)} collective-permute-done((f32[48,96]{1,0:T(8,128)S(1)}, f32[48,96]{1,0:T(8,128)S(1)}, u32[]{:S(2)}, u32[]{:S(2)}) %collective-permute-start.21) | collective-permute-done | bytes 18464 | tf_op jit(solution)/shard_map/ppermute | solution.py:432
  58.0 1.1 %collective-permute-start.24 = (f32[2,48,96]{2,1,0:T(8,128)S(1)}, f32[2,48,96]{2,1,0:T(8,128)S(1)}, u32[]{:S(2)}, u32[]{:S(2)}) collective-permute-start(f32[2,48,96]{2,1,0:T(8,128)S(1)} %pad_maximum_fusion.4.refs_0_), channel_id=1, source_target_pairs={{0,24},{1,25},{2,26},{3,27},{4,28},{5,29},{6,30},{7,31},{8,16},{9,... | collective-permute-start | bytes 110600 | tf_op jit(solution)/shard_map/ppermute | solution.py:432
  59.0 1.0 %collective-permute-start.23 = (f32[2,48,96]{2,1,0:T(8,128)S(1)}, f32[2,48,96]{2,1,0:T(8,128)S(1)}, u32[]{:S(2)}, u32[]{:S(2)}) collective-permute-start(f32[2,48,96]{2,1,0:T(8,128)S(1)} %pad_maximum_fusion.4.refs_0_), channel_id=1, source_target_pairs={{0,16},{1,17},{2,18},{3,19},{4,20},{5,21},{6,22},{7,23},{8,24},{9,... | collective-permute-start | bytes 110600 | tf_op jit(solution)/shard_map/ppermute | solution.py:432
  60.0 2.4 %collective-permute-start.22 = (f32[2,48,96]{2,1,0:T(8,128)S(1)}, f32[2,48,96]{2,1,0:T(8,128)S(1)}, u32[]{:S(2)}, u32[]{:S(2)}) collective-permute-start(f32[2,48,96]{2,1,0:T(8,128)S(1)} %pad_maximum_fusion.4.refs_0_), channel_id=1, source_target_pairs={{0,8},{1,9},{2,10},{3,11},{4,12},{5,13},{6,14},{7,15},{8,0},{9,1},... | collective-permute-start | bytes 110600 | tf_op jit(solution)/shard_map/ppermute | solution.py:432
  62.4 1.0 %shard_map.74 = f32[32,32,48]{2,1,0:T(8,128)} custom-call(f32[4,48,256]{2,1,0:T(8,128)S(1)} %pad_maximum_fusion.rest_0_.refs_0_, f32[4,48,256]{2,1,0:T(8,128)S(1)} %collective-permute-done.17.rest_0_.refs_1_, f32[4,48,256]{2,1,0:T(8,128)S(1)} %collective-permute-done.15.rest_2_.refs_2_, f32[4,48,256]{2,1,0:T(8,128)S(1)} %collective-permute-done.19.rest_2_.refs_3_), custom_call_target="tpu_custom_call" | custom-call | tf_op jit(solution)/shard_map/pallas_call | solution.py:389
  63.4 0.6 collective-permute-done.24.refs_3_
  64.0 1.0 %collective-permute-done.23.refs_2_ = f32[2,48,96]{2,1,0:T(8,128)S(1)} collective-permute-done((f32[2,48,96]{2,1,0:T(8,128)S(1)}, f32[2,48,96]{2,1,0:T(8,128)S(1)}, u32[]{:S(2)}, u32[]{:S(2)}) %collective-permute-start.23) | collective-permute-done | bytes 36896 | tf_op jit(solution)/shard_map/ppermute | solution.py:432
  65.0 0.0 collective-permute-done.22.refs_1_
  65.0 0.8 %shard_map.73 = f32[48,768]{1,0:T(8,128)} custom-call(f32[2,48,96]{2,1,0:T(8,128)S(1)} %pad_maximum_fusion.4.refs_0_, f32[2,48,96]{2,1,0:T(8,128)S(1)} %collective-permute-done.22.refs_1_, f32[2,48,96]{2,1,0:T(8,128)S(1)} %collective-permute-done.23.refs_2_, f32[2,48,96]{2,1,0:T(8,128)S(1)} %collective-permute-done.24.refs_3_), custom_call_target="tpu_custom_call" | custom-call | tf_op jit(solution)/shard_map/pallas_call | solution.py:416
  (10 shorter events, 0.2 us)
Async XLA Ops:
  8.1 1.9 %collective-permute-start = (f32[792,128]{1,0:T(8,128)S(1)}, f32[792,128]{1,0:T(8,128)S(1)}, u32[]{:S(2)}, u32[]{:S(2)}) collective-permute-start(f32[792,128]{1,0:T(8,128)S(1)} %get-tuple-element.17), channel_id=1, source_target_pairs={{0,1},{1,0},{2,3},{3,2},{4,5},{5,4},{6,7},{7,6},{8,9},{9,8},{10,11... | collective-permute-start | bytes 1216520 | tf_op jit(solution)/shard_map/ppermute | solution.py:432
  10.0 4.8 %collective-permute-start.4 = (f32[768,128]{1,0:T(8,128)S(1)}, f32[768,128]{1,0:T(8,128)S(1)}, u32[]{:S(2)}, u32[]{:S(2)}) collective-permute-start(f32[768,128]{1,0:T(8,128)S(1)} %get-tuple-element.23), channel_id=1, source_target_pairs={{0,1},{1,0},{2,3},{3,2},{4,5},{5,4},{6,7},{7,6},{8,9},{9,8},{10,11... | collective-permute-start | bytes 1179656 | tf_op jit(solution)/shard_map/ppermute | solution.py:432
  10.4 18.2 %copy-start = (f32[48,32,32]{0,2,1:T(8,128)S(1)}, f32[48,32,32]{0,2,1:T(8,128)}, u32[]{:S(2)}) copy-start(f32[48,32,32]{0,2,1:T(8,128)} %param.9) | copy-start | bytes 589828
  10.4 7.9 %collective-permute-start.3 = (f32[192,128]{1,0:T(8,128)S(1)}, f32[192,128]{1,0:T(8,128)S(1)}, u32[]{:S(2)}, u32[]{:S(2)}) collective-permute-start(f32[192,128]{1,0:T(8,128)S(1)} %get-tuple-element.25), channel_id=1, source_target_pairs={{0,6},{1,7},{2,4},{3,5},{4,2},{5,3},{6,0},{7,1},{8,14},{9,15},{10,... | collective-permute-start | bytes 294920 | tf_op jit(solution)/shard_map/ppermute | solution.py:432
  14.1 6.2 %collective-permute-start.2 = (f32[192,128]{1,0:T(8,128)S(1)}, f32[192,128]{1,0:T(8,128)S(1)}, u32[]{:S(2)}, u32[]{:S(2)}) collective-permute-start(f32[192,128]{1,0:T(8,128)S(1)} %get-tuple-element.26), channel_id=1, source_target_pairs={{0,4},{1,5},{2,6},{3,7},{4,0},{5,1},{6,2},{7,3},{8,12},{9,13},{10,... | collective-permute-start | bytes 294920 | tf_op jit(solution)/shard_map/ppermute | solution.py:432
  14.6 7.6 %collective-permute-start.1 = (f32[216,128]{1,0:T(8,128)S(1)}, f32[216,128]{1,0:T(8,128)S(1)}, u32[]{:S(2)}, u32[]{:S(2)}) collective-permute-start(f32[216,128]{1,0:T(8,128)S(1)} %slice_add_fusion.mine_ref), channel_id=1, source_target_pairs={{0,2},{1,3},{2,0},{3,1},{4,6},{5,7},{6,4},{7,5},{8,10},{9,11},{10,... | collective-permute-start | bytes 331784 | tf_op jit(solution)/shard_map/ppermute | solution.py:432
  14.9 7.4 %collective-permute-start.7 = (f32[192,128]{1,0:T(8,128)S(1)}, f32[192,128]{1,0:T(8,128)S(1)}, u32[]{:S(2)}, u32[]{:S(2)}) collective-permute-start(f32[192,128]{1,0:T(8,128)S(1)} %get-tuple-element.28), channel_id=1, source_target_pairs={{0,6},{1,7},{2,4},{3,5},{4,2},{5,3},{6,0},{7,1},{8,14},{9,15},{10,... | collective-permute-start | bytes 294920 | tf_op jit(solution)/shard_map/ppermute | solution.py:432
  17.8 6.2 %collective-permute-start.6 = (f32[192,128]{1,0:T(8,128)S(1)}, f32[192,128]{1,0:T(8,128)S(1)}, u32[]{:S(2)}, u32[]{:S(2)}) collective-permute-start(f32[192,128]{1,0:T(8,128)S(1)} %get-tuple-element.29), channel_id=1, source_target_pairs={{0,2},{1,3},{2,0},{3,1},{4,6},{5,7},{6,4},{7,5},{8,10},{9,11},{10,... | collective-permute-start | bytes 294920 | tf_op jit(solution)/shard_map/ppermute | solution.py:432
  18.3 5.7 %collective-permute-start.5 = (f32[192,128]{1,0:T(8,128)S(1)}, f32[192,128]{1,0:T(8,128)S(1)}, u32[]{:S(2)}, u32[]{:S(2)}) collective-permute-start(f32[192,128]{1,0:T(8,128)S(1)} %get-tuple-element.30), channel_id=1, source_target_pairs={{0,4},{1,5},{2,6},{3,7},{4,0},{5,1},{6,2},{7,3},{8,12},{9,13},{10,... | collective-permute-start | bytes 294920 | tf_op jit(solution)/shard_map/ppermute | solution.py:432
  24.1 6.3 %collective-permute-start.8 = (f32[48,256]{1,0:T(8,128)S(1)}, f32[48,256]{1,0:T(8,128)S(1)}, u32[]{:S(2)}, u32[]{:S(2)}) collective-permute-start(f32[48,256]{1,0:T(8,128)S(1)} %pad_maximum_fusion.1), channel_id=1, source_target_pairs={{0,24},{1,25},{2,26},{3,27},{4,28},{5,29},{6,30},{7,31},{8,16},{9,... | collective-permute-start | bytes 147464 | tf_op jit(solution)/shard_map/ppermute | solution.py:432
  27.9 5.0 %collective-permute-start.9 = (f32[48,256]{1,0:T(8,128)S(1)}, f32[48,256]{1,0:T(8,128)S(1)}, u32[]{:S(2)}, u32[]{:S(2)}) collective-permute-start(f32[48,256]{1,0:T(8,128)S(1)} %pad_maximum_fusion.2), channel_id=1, source_target_pairs={{0,16},{1,17},{2,18},{3,19},{4,20},{5,21},{6,22},{7,23},{8,24},{9,... | collective-permute-start | bytes 147464 | tf_op jit(solution)/shard_map/ppermute | solution.py:432
  27.9 5.0 %collective-permute-start.10 = (f32[48,256]{1,0:T(8,128)S(1)}, f32[48,256]{1,0:T(8,128)S(1)}, u32[]{:S(2)}, u32[]{:S(2)}) collective-permute-start(f32[48,256]{1,0:T(8,128)S(1)} %pad_maximum_fusion.3), channel_id=1, source_target_pairs={{0,8},{1,9},{2,10},{3,11},{4,12},{5,13},{6,14},{7,15},{8,0},{9,1},... | collective-permute-start | bytes 147464 | tf_op jit(solution)/shard_map/ppermute | solution.py:432
  32.9 6.0 %collective-permute-start.13 = (f32[48,256]{1,0:T(8,128)S(1)}, f32[48,256]{1,0:T(8,128)S(1)}, u32[]{:S(2)}, u32[]{:S(2)}) collective-permute-start(f32[48,256]{1,0:T(8,128)S(1)} %fusion.1), channel_id=1, source_target_pairs={{0,24},{1,25},{2,26},{3,27},{4,28},{5,29},{6,30},{7,31},{8,16},{9,... | collective-permute-start | bytes 147464 | tf_op jit(solution)/shard_map/ppermute | solution.py:432
  34.8 5.5 %collective-permute-start.12 = (f32[48,256]{1,0:T(8,128)S(1)}, f32[48,256]{1,0:T(8,128)S(1)}, u32[]{:S(2)}, u32[]{:S(2)}) collective-permute-start(f32[48,256]{1,0:T(8,128)S(1)} %fusion.1), channel_id=1, source_target_pairs={{0,16},{1,17},{2,18},{3,19},{4,20},{5,21},{6,22},{7,23},{8,24},{9,... | collective-permute-start | bytes 147464 | tf_op jit(solution)/shard_map/ppermute | solution.py:432
  35.1 5.2 %collective-permute-start.11 = (f32[48,256]{1,0:T(8,128)S(1)}, f32[48,256]{1,0:T(8,128)S(1)}, u32[]{:S(2)}, u32[]{:S(2)}) collective-permute-start(f32[48,256]{1,0:T(8,128)S(1)} %fusion.1), channel_id=1, source_target_pairs={{0,8},{1,9},{2,10},{3,11},{4,12},{5,13},{6,14},{7,15},{8,0},{9,1},... | collective-permute-start | bytes 147464 | tf_op jit(solution)/shard_map/ppermute | solution.py:432
  40.4 8.5 %collective-permute-start.16 = (f32[4,48,256]{2,1,0:T(8,128)S(1)}, f32[4,48,256]{2,1,0:T(8,128)S(1)}, u32[]{:S(2)}, u32[]{:S(2)}) collective-permute-start(f32[4,48,256]{2,1,0:T(8,128)S(1)} %pad_maximum_fusion.rest_0_.refs_0_), channel_id=1, source_target_pairs={{0,6},{1,7},{2,4},{3,5},{4,2},{5,3},{6,0},{7,1},{8,14},{9,15},{10,... | collective-permute-start | bytes 589832 | tf_op jit(solution)/shard_map/ppermute | solution.py:432
  43.1 7.9 %collective-permute-start.15 = (f32[4,48,256]{2,1,0:T(8,128)S(1)}, f32[4,48,256]{2,1,0:T(8,128)S(1)}, u32[]{:S(2)}, u32[]{:S(2)}) collective-permute-start(f32[4,48,256]{2,1,0:T(8,128)S(1)} %pad_maximum_fusion.rest_0_.refs_0_), channel_id=1, source_target_pairs={{0,2},{1,3},{2,0},{3,1},{4,6},{5,7},{6,4},{7,5},{8,10},{9,11},{10,... | collective-permute-start | bytes 589832 | tf_op jit(solution)/shard_map/ppermute | solution.py:432
  43.3 7.9 %collective-permute-start.14 = (f32[4,48,256]{2,1,0:T(8,128)S(1)}, f32[4,48,256]{2,1,0:T(8,128)S(1)}, u32[]{:S(2)}, u32[]{:S(2)}) collective-permute-start(f32[4,48,256]{2,1,0:T(8,128)S(1)} %pad_maximum_fusion.rest_0_.refs_0_), channel_id=1, source_target_pairs={{0,4},{1,5},{2,6},{3,7},{4,0},{5,1},{6,2},{7,3},{8,12},{9,13},{10,... | collective-permute-start | bytes 589832 | tf_op jit(solution)/shard_map/ppermute | solution.py:432
  43.9 8.6 %collective-permute-start.17 = (f32[4,48,256]{2,1,0:T(8,128)S(1)}, f32[4,48,256]{2,1,0:T(8,128)S(1)}, u32[]{:S(2)}, u32[]{:S(2)}) collective-permute-start(f32[4,48,256]{2,1,0:T(8,128)S(1)} %pad_maximum_fusion.rest_0_.refs_0_), channel_id=1, source_target_pairs={{0,1},{1,0},{2,3},{3,2},{4,5},{5,4},{6,7},{7,6},{8,9},{9,8},{10,11... | collective-permute-start | bytes 589832 | tf_op jit(solution)/shard_map/ppermute | solution.py:432
  48.9 3.6 %collective-permute-start.20 = (f32[4,48,256]{2,1,0:T(8,128)S(1)}, f32[4,48,256]{2,1,0:T(8,128)S(1)}, u32[]{:S(2)}, u32[]{:S(2)}) collective-permute-start(f32[4,48,256]{2,1,0:T(8,128)S(1)} %collective-permute-done.16.rest_3_), channel_id=1, source_target_pairs={{0,1},{1,0},{2,3},{3,2},{4,5},{5,4},{6,7},{7,6},{8,9},{9,8},{10,11... | collective-permute-start | bytes 589832 | tf_op jit(solution)/shard_map/ppermute | solution.py:432
  50.9 1.6 %collective-permute-start.19 = (f32[4,48,256]{2,1,0:T(8,128)S(1)}, f32[4,48,256]{2,1,0:T(8,128)S(1)}, u32[]{:S(2)}, u32[]{:S(2)}) collective-permute-start(f32[4,48,256]{2,1,0:T(8,128)S(1)} %collective-permute-done.15.rest_2_.refs_2_), channel_id=1, source_target_pairs={{0,1},{1,0},{2,3},{3,2},{4,5},{5,4},{6,7},{7,6},{8,9},{9,8},{10,11... | collective-permute-start | bytes 589832 | tf_op jit(solution)/shard_map/ppermute | solution.py:432
  51.2 1.4 %collective-permute-start.18 = (f32[4,48,256]{2,1,0:T(8,128)S(1)}, f32[4,48,256]{2,1,0:T(8,128)S(1)}, u32[]{:S(2)}, u32[]{:S(2)}) collective-permute-start(f32[4,48,256]{2,1,0:T(8,128)S(1)} %collective-permute-done.14.rest_1_), channel_id=1, source_target_pairs={{0,1},{1,0},{2,3},{3,2},{4,5},{5,4},{6,7},{7,6},{8,9},{9,8},{10,11... | collective-permute-start | bytes 589832 | tf_op jit(solution)/shard_map/ppermute | solution.py:432
  54.1 3.9 %collective-permute-start.21 = (f32[48,96]{1,0:T(8,128)S(1)}, f32[48,96]{1,0:T(8,128)S(1)}, u32[]{:S(2)}, u32[]{:S(2)}) collective-permute-start(f32[48,96]{1,0:T(8,128)S(1)} %shard_map.72), channel_id=1, source_target_pairs={{0,4},{1,5},{2,6},{3,7},{4,0},{5,1},{6,2},{7,3},{8,12},{9,13},{10,... | collective-permute-start | bytes 55304 | tf_op jit(solution)/shard_map/ppermute | solution.py:432
  58.0 6.0 %collective-permute-start.24 = (f32[2,48,96]{2,1,0:T(8,128)S(1)}, f32[2,48,96]{2,1,0:T(8,128)S(1)}, u32[]{:S(2)}, u32[]{:S(2)}) collective-permute-start(f32[2,48,96]{2,1,0:T(8,128)S(1)} %pad_maximum_fusion.4.refs_0_), channel_id=1, source_target_pairs={{0,24},{1,25},{2,26},{3,27},{4,28},{5,29},{6,30},{7,31},{8,16},{9,... | collective-permute-start | bytes 110600 | tf_op jit(solution)/shard_map/ppermute | solution.py:432
  59.0 6.0 %collective-permute-start.23 = (f32[2,48,96]{2,1,0:T(8,128)S(1)}, f32[2,48,96]{2,1,0:T(8,128)S(1)}, u32[]{:S(2)}, u32[]{:S(2)}) collective-permute-start(f32[2,48,96]{2,1,0:T(8,128)S(1)} %pad_maximum_fusion.4.refs_0_), channel_id=1, source_target_pairs={{0,16},{1,17},{2,18},{3,19},{4,20},{5,21},{6,22},{7,23},{8,24},{9,... | collective-permute-start | bytes 110600 | tf_op jit(solution)/shard_map/ppermute | solution.py:432
  60.0 5.0 %collective-permute-start.22 = (f32[2,48,96]{2,1,0:T(8,128)S(1)}, f32[2,48,96]{2,1,0:T(8,128)S(1)}, u32[]{:S(2)}, u32[]{:S(2)}) collective-permute-start(f32[2,48,96]{2,1,0:T(8,128)S(1)} %pad_maximum_fusion.4.refs_0_), channel_id=1, source_target_pairs={{0,8},{1,9},{2,10},{3,11},{4,12},{5,13},{6,14},{7,15},{8,0},{9,1},... | collective-permute-start | bytes 110600 | tf_op jit(solution)/shard_map/ppermute | solution.py:432

commit v18 on v17

--- a/solution.py
+++ b/solution.py
@@ -289,7 +289,9 @@
     here = h_ref[pl.ds(first, tall)]
     here = jnp.transpose(here.reshape(-1, here.shape[2]))
     rows = mine_ref.shape[0]
-    gram = unfold(mine_ref[rows - FOLDED:rows] + other_ref[rows - FOLDED:rows], here.shape[0])
+    folded = mine_ref[rows - 16:rows] + other_ref[rows - 16:rows]
+    folded = jnp.concatenate([folded[:8, :LANES], folded[:8, LANES:], folded[8:, :LANES]], axis=0)
+    gram = unfold(folded, here.shape[0])
     out_ref[...] = here / dot_exact(gram, here)
 
 
@@ -443,25 +445,26 @@
     h_columns = jnp.transpose(factor_h, (1, 2, 0))
     rank = w_rows.shape[0]
     x_high, x_low, w_here, w_both, keep_0, give_0 = blur_call(cube[0], taps_x, taps_y, w_rows)
-    chains = []
     taken_0 = send(give_0, 0, 1)
     keep_1, give_1 = project_call(x_high, x_low, w_both)
     taken_0, keep_1, give_1 = lax.optimization_barrier((taken_0, keep_1, give_1))
-    for keep, taken in ((keep_0, taken_0), (keep_1, send(give_1, 0, 1))):
-        bounds = [place * 4 * rank for place in (0, 1, 3, 2)]
-        sides = []
-        for first in bounds:
-            last = keep.shape[0] if first == max(bounds) else first + 4 * rank
-            sides.append(keep[first:last] + taken[first:last])
-        chains.append((sides, around(sides)))
-    ratio = ratio_call(chains[0][0][2], chains[0][1][1], h_columns)
+    taken_1 = send(give_1, 0, 1)
+    sides = []
+    for place in (0, 1, 3, 2):
+        here = slice(place * 4 * rank, (place + 1) * 4 * rank)
+        sides.append(jnp.concatenate([keep_0[here] + taken_0[here], keep_1[here] + taken_1[here]], axis=1))
+    gram = keep_0[PIECES * rank:] + taken_0[PIECES * rank:]
+    gram = jnp.concatenate([gram, jnp.zeros_like(gram[:8])], axis=0)
+    gram = jnp.concatenate(
+        [jnp.concatenate([gram[first:first + 8], gram[first + 8:first + 16]], axis=1) for first in (0, 16)], axis=0)
+    sides[2] = jnp.concatenate([sides[2], gram], axis=0)
+    others = around(sides)
+    ratio = ratio_call(sides[2], others[1], h_columns)
     line = []
     for k in range(4):
         part = slice(k * rank, (k + 1) * rank)
-        line.append(jnp.concatenate(
-            [(sides[0][part] + others[0][part]) + (others[1][part] + others[2][part]) for sides, others in chains],
-            axis=1))
-    line = [line[0]] + [send(line[k], 2 * k, 0) for k in (3, 2, 1)]
+        line.append((sides[0][part] + others[0][part]) + (others[1][part] + others[2][part]))
+    line = [line[0]] + [send(line[k], 2 * k, 0) for k in range(1, 4)]
     h_piece = ratio * ((line[0] + line[1]) + (line[2] + line[3]))
     h_line = [h_piece] + [send(h_piece, 2 * k, 0) for k in range(1, 4)]
     mine = jnp.stack(h_line)

time: 66 us -> 67.4 us (1.021)
  waiting for transfers between devices: 23.4 us -> 29.1 us
  starting transfers between devices: 28.8 us -> 24.4 us
    ppermute x25 -> x22, waiting for transfers between devices: 23.4 us -> 29.1 us  [send(): return lax.ppermute(value, ('sp', 'bd'), pairs)]
    ppermute x25 -> x22, starting transfers between devices: 28.8 us -> 24.4 us  [send(): return lax.ppermute(value, ('sp', 'bd'), pairs)]
  transfers between devices with their start and end apart: 25 -> 22, of which waited for: 15 -> 16; matrix products, arithmetic and copies ran while one was open for 0% -> 0% of each run, Pallas kernels for 5% -> 4%
where the time goes in v18:
time: 67.4 us; the launch traced here: 67.3 us
  waiting for transfers between devices  29.1 us (43%)
  starting transfers between devices  24.4 us (36%)
  Pallas kernels  12.7 us (19%)
  between operations  0.75 us (1%)
    ppermute x22, waiting for transfers between devices, send(): return lax.ppermute(value, ('sp', 'bd'), pairs)  29.1 us
    ppermute x22, starting transfers between devices, send(): return lax.ppermute(value, ('sp', 'bd'), pairs)  24.4 us
    pallas_call x1, Pallas kernels, blur_call(): pl.pallas_call(blur_kernel, out_shape=[jax.ShapeDtypeStruct(image, BF16)]...  7.47 us
    pallas_call x1, Pallas kernels, second_call(): pl.pallas_call(second_kernel, out_shape=jax.ShapeDtypeStruct(w_here.shape...  1.43 us
  transfers between devices with their start and end apart: 22, of which 16 were waited for; matrix products, arithmetic and copies ran while one was open for 0% of the time, Pallas kernels for 4%

profile of v18, /device:TPU:0, one launch (start us, length us, event | category | flops | bytes accessed | tf_op | source)
XLA Modules:
  0.0 67.3 jit_solution(4488181018966090327)
XLA Ops:
  0.6 7.5 %shard_map.68 = (bf16[32,96,256]{2,1,0:T(8,128)(2,1)S(1)}, bf16[32,96,256]{2,1,0:T(8,128)(2,1)S(1)}, f32[48,96]{1,0:T(8,128)S(1)}, bf16[96,256]{1,0:T(8,128)(2,1...) custom-call(f32[96,32,256]{2,1,0:T(8,128)} %bitcast.19, f32[25,1,96]{2,1,0:T(1,128)} %bitcast.28, ...), custom_call_target="tpu_custom_call" | custom-call | tf_op jit(solution)/shard_map/pallas_call | solution.py:274
  8.1 0.5 collective-permute-start
  8.6 0.7 %shard_map.69 = (f32[768,128]{1,0:T(8,128)S(1)}, f32[768,128]{1,0:T(8,128)S(1)}) custom-call(bf16[32,96,256]{2,1,0:T(8,128)(2,1)S(1)} %get-tuple-element.13.xh_ref, bf16[32,96,256]{2,1,0:T(8,128)(2,1)S(1)} %get-tuple-element.14.xl_ref, bf16[96,256]{1,0:T(8,128)(2,1)S(1)} %get-tuple-element.18.w_both_ref), custom_call_target="tpu_custom_call" | custom-call | tf_op jit(solution)/shard_map/pallas_call | solution.py:257
  9.3 0.7 %collective-permute-done = f32[792,128]{1,0:T(8,128)S(1)} collective-permute-done((f32[792,128]{1,0:T(8,128)S(1)}, f32[792,128]{1,0:T(8,128)S(1)}, u32[]{:S(2)}, u32[]{:S(2)}) %collective-permute-start) | collective-permute-done | bytes 405536 | tf_op jit(solution)/shard_map/ppermute | solution.py:434
  10.0 0.4 collective-permute-start.1
  10.4 0.1 slice_add_fusion.5
  10.4 0.0 copy-start
  10.4 1.3 %collective-permute-done.1 = f32[768,128]{1,0:T(8,128)S(1)} collective-permute-done((f32[768,128]{1,0:T(8,128)S(1)}, f32[768,128]{1,0:T(8,128)S(1)}, u32[]{:S(2)}, u32[]{:S(2)}) %collective-permute-start.1) | collective-permute-done | bytes 393248 | tf_op jit(solution)/shard_map/ppermute | solution.py:434
  11.7 0.1 slice_add_fusion.1
  11.8 3.9 %collective-permute-start.4 = (f32[192,256]{1,0:T(8,128)S(1)}, f32[192,256]{1,0:T(8,128)S(1)}, u32[]{:S(2)}, u32[]{:S(2)}) collective-permute-start(f32[192,256]{1,0:T(8,128)S(1)} %pad_maximum_fusion.1), channel_id=1, source_target_pairs={{0,6},{1,7},{2,4},{3,5},{4,2},{5,3},{6,0},{7,1},{8,14},{9,15},{10,... | collective-permute-start | bytes 589832 | tf_op jit(solution)/shard_map/ppermute | solution.py:434
  15.7 0.6 collective-permute-start.2
  16.3 0.1 collective-permute-start.3
  16.4 5.0 %collective-permute-done.4 = f32[192,256]{1,0:T(8,128)S(1)} collective-permute-done((f32[192,256]{1,0:T(8,128)S(1)}, f32[192,256]{1,0:T(8,128)S(1)}, u32[]{:S(2)}, u32[]{:S(2)}) %collective-permute-start.4) | collective-permute-done | bytes 196640 | tf_op jit(solution)/shard_map/ppermute | solution.py:434
  21.4 4.0 %collective-permute-done.3 = f32[192,256]{1,0:T(8,128)S(1)} collective-permute-done((f32[192,256]{1,0:T(8,128)S(1)}, f32[192,256]{1,0:T(8,128)S(1)}, u32[]{:S(2)}, u32[]{:S(2)}) %collective-permute-start.3) | collective-permute-done | bytes 196640 | tf_op jit(solution)/shard_map/ppermute | solution.py:434
  25.4 0.1 collective-permute-done.2.other_ref
  25.5 3.9 %collective-permute-start.7 = (f32[48,256]{1,0:T(8,128)S(1)}, f32[48,256]{1,0:T(8,128)S(1)}, u32[]{:S(2)}, u32[]{:S(2)}) collective-permute-start(f32[48,256]{1,0:T(8,128)S(1)} %get-tuple-element.28), channel_id=1, source_target_pairs={{0,24},{1,25},{2,26},{3,27},{4,28},{5,29},{6,30},{7,31},{8,16},{9,... | collective-permute-start | bytes 147464 | tf_op jit(solution)/shard_map/ppermute | solution.py:434
  29.4 0.0 collective-permute-start.6
  29.4 0.6 collective-permute-start.5
  30.0 0.0 copy-done
  30.0 0.3 shard_map.70
  30.3 1.2 %collective-permute-done.7 = f32[48,256]{1,0:T(8,128)S(1)} collective-permute-done((f32[48,256]{1,0:T(8,128)S(1)}, f32[48,256]{1,0:T(8,128)S(1)}, u32[]{:S(2)}, u32[]{:S(2)}) %collective-permute-start.7) | collective-permute-done | bytes 49184 | tf_op jit(solution)/shard_map/ppermute | solution.py:434
  31.5 2.8 %collective-permute-done.6 = f32[48,256]{1,0:T(8,128)S(1)} collective-permute-done((f32[48,256]{1,0:T(8,128)S(1)}, f32[48,256]{1,0:T(8,128)S(1)}, u32[]{:S(2)}, u32[]{:S(2)}) %collective-permute-start.6) | collective-permute-done | bytes 49184 | tf_op jit(solution)/shard_map/ppermute | solution.py:434
  34.3 0.0 collective-permute-done.5
  34.4 2.2 %collective-permute-start.10 = (f32[48,256]{1,0:T(8,128)S(1)}, f32[48,256]{1,0:T(8,128)S(1)}, u32[]{:S(2)}, u32[]{:S(2)}) collective-permute-start(f32[48,256]{1,0:T(8,128)S(1)} %fusion.8), channel_id=1, source_target_pairs={{0,24},{1,25},{2,26},{3,27},{4,28},{5,29},{6,30},{7,31},{8,16},{9,... | collective-permute-start | bytes 147464 | tf_op jit(solution)/shard_map/ppermute | solution.py:434
  36.6 0.1 collective-permute-start.9
  36.7 2.1 %collective-permute-start.8 = (f32[48,256]{1,0:T(8,128)S(1)}, f32[48,256]{1,0:T(8,128)S(1)}, u32[]{:S(2)}, u32[]{:S(2)}) collective-permute-start(f32[48,256]{1,0:T(8,128)S(1)} %fusion.8), channel_id=1, source_target_pairs={{0,8},{1,9},{2,10},{3,11},{4,12},{5,13},{6,14},{7,15},{8,0},{9,1},... | collective-permute-start | bytes 147464 | tf_op jit(solution)/shard_map/ppermute | solution.py:434
  38.8 1.9 %collective-permute-done.10 = f32[48,256]{1,0:T(8,128)S(1)} collective-permute-done((f32[48,256]{1,0:T(8,128)S(1)}, f32[48,256]{1,0:T(8,128)S(1)}, u32[]{:S(2)}, u32[]{:S(2)}) %collective-permute-start.10) | collective-permute-done | bytes 49184 | tf_op jit(solution)/shard_map/ppermute | solution.py:434
  40.7 1.3 %collective-permute-done.9 = f32[48,256]{1,0:T(8,128)S(1)} collective-permute-done((f32[48,256]{1,0:T(8,128)S(1)}, f32[48,256]{1,0:T(8,128)S(1)}, u32[]{:S(2)}, u32[]{:S(2)}) %collective-permute-start.9) | collective-permute-done | bytes 49184 | tf_op jit(solution)/shard_map/ppermute | solution.py:434
  42.0 0.0 collective-permute-done.8
  42.0 1.5 %collective-permute-start.13 = (f32[4,48,256]{2,1,0:T(8,128)S(1)}, f32[4,48,256]{2,1,0:T(8,128)S(1)}, u32[]{:S(2)}, u32[]{:S(2)}) collective-permute-start(f32[4,48,256]{2,1,0:T(8,128)S(1)} %pad_maximum_fusion.2.rest_0_.refs_0_), channel_id=1, source_target_pairs={{0,6},{1,7},{2,4},{3,5},{4,2},{5,3},{6,0},{7,1},{8,14},{9,15},{10,... | collective-permute-start | bytes 589832 | tf_op jit(solution)/shard_map/ppermute | solution.py:434
  43.5 1.5 %collective-permute-start.12 = (f32[4,48,256]{2,1,0:T(8,128)S(1)}, f32[4,48,256]{2,1,0:T(8,128)S(1)}, u32[]{:S(2)}, u32[]{:S(2)}) collective-permute-start(f32[4,48,256]{2,1,0:T(8,128)S(1)} %pad_maximum_fusion.2.rest_0_.refs_0_), channel_id=1, source_target_pairs={{0,2},{1,3},{2,0},{3,1},{4,6},{5,7},{6,4},{7,5},{8,10},{9,11},{10,... | collective-permute-start | bytes 589832 | tf_op jit(solution)/shard_map/ppermute | solution.py:434
  45.0 0.5 collective-permute-start.11
  45.6 0.0 collective-permute-start.14
  45.6 4.9 %collective-permute-done.13.rest_3_ = f32[4,48,256]{2,1,0:T(8,128)S(1)} collective-permute-done((f32[4,48,256]{2,1,0:T(8,128)S(1)}, f32[4,48,256]{2,1,0:T(8,128)S(1)}, u32[]{:S(2)}, u32[]{:S(2)}) %collective-permute-start.13) | collective-permute-done | bytes 196640 | tf_op jit(solution)/shard_map/ppermute | solution.py:434
  50.4 0.0 collective-permute-start.17
  50.4 2.0 %collective-permute-done.12.rest_2_.refs_2_ = f32[4,48,256]{2,1,0:T(8,128)S(1)} collective-permute-done((f32[4,48,256]{2,1,0:T(8,128)S(1)}, f32[4,48,256]{2,1,0:T(8,128)S(1)}, u32[]{:S(2)}, u32[]{:S(2)}) %collective-permute-start.12) | collective-permute-done | bytes 196640 | tf_op jit(solution)/shard_map/ppermute | solution.py:434
  52.5 0.0 collective-permute-start.16
  52.5 0.1 collective-permute-done.11.rest_1_
  52.6 0.4 collective-permute-start.15
  53.0 1.1 %shard_map.71.total_ref = f32[288,96]{1,0:T(8,128)S(1)} custom-call(bf16[32,96,256]{2,1,0:T(8,128)(2,1)S(1)} %get-tuple-element.13.xh_ref, bf16[32,96,256]{2,1,0:T(8,128)(2,1)S(1)} %get-tuple-element.14.xl_ref, f32[4,48,256]{2,1,0:T(8,128)S(1)} %pad_maximum_fusion.2.rest_0_.refs_0_, f32[4,48,256]{2,1,0:T(8,128)S(1)} %collective-permute-done.11.rest_1_, ...), custom_call_target="tpu_custom_call" | custom-call | tf_op jit(solution)/shard_map/pallas_call | solution.py:347
  54.0 0.0 collective-permute-done.14.rest_0_.refs_1_
  54.0 0.0 collective-permute-done.17.rest_3_
  54.0 0.0 collective-permute-done.16.rest_2_.refs_3_
  54.1 0.1 collective-permute-done.15.rest_1_
  54.2 1.4 %shard_map.72 = f32[48,96]{1,0:T(8,128)S(1)} custom-call(bf16[32,96,256]{2,1,0:T(8,128)(2,1)S(1)} %get-tuple-element.13.xh_ref, bf16[32,96,256]{2,1,0:T(8,128)(2,1)S(1)} %get-tuple-element.14.xl_ref, f32[48,96]{1,0:T(8,128)S(1)} %get-tuple-element.15.w_ref, f32[288,96]{1,0:T(8,128)S(1)} %shard_map.71.total_ref, ...), custom_call_target="tpu_custom_call" | custom-call | tf_op jit(solution)/shard_map/pallas_call | solution.py:371
  55.6 1.6 %collective-permute-start.18 = (f32[48,96]{1,0:T(8,128)S(1)}, f32[48,96]{1,0:T(8,128)S(1)}, u32[]{:S(2)}, u32[]{:S(2)}) collective-permute-start(f32[48,96]{1,0:T(8,128)S(1)} %shard_map.72), channel_id=1, source_target_pairs={{0,4},{1,5},{2,6},{3,7},{4,0},{5,1},{6,2},{7,3},{8,12},{9,13},{10,... | collective-permute-start | bytes 55304 | tf_op jit(solution)/shard_map/ppermute | solution.py:434
  57.2 2.3 %collective-permute-done.18 = f32[48,96]{1,0:T(8,128)S(1)} collective-permute-done((f32[48,96]{1,0:T(8,128)S(1)}, f32[48,96]{1,0:T(8,128)S(1)}, u32[]{:S(2)}, u32[]{:S(2)}) %collective-permute-start.18) | collective-permute-done | bytes 18464 | tf_op jit(solution)/shard_map/ppermute | solution.py:434
  59.5 0.9 %collective-permute-start.21 = (f32[2,48,96]{2,1,0:T(8,128)S(1)}, f32[2,48,96]{2,1,0:T(8,128)S(1)}, u32[]{:S(2)}, u32[]{:S(2)}) collective-permute-start(f32[2,48,96]{2,1,0:T(8,128)S(1)} %pad_maximum_fusion.4.refs_0_), channel_id=1, source_target_pairs={{0,24},{1,25},{2,26},{3,27},{4,28},{5,29},{6,30},{7,31},{8,16},{9,... | collective-permute-start | bytes 110600 | tf_op jit(solution)/shard_map/ppermute | solution.py:434
  60.4 1.1 %collective-permute-start.20 = (f32[2,48,96]{2,1,0:T(8,128)S(1)}, f32[2,48,96]{2,1,0:T(8,128)S(1)}, u32[]{:S(2)}, u32[]{:S(2)}) collective-permute-start(f32[2,48,96]{2,1,0:T(8,128)S(1)} %pad_maximum_fusion.4.refs_0_), channel_id=1, source_target_pairs={{0,16},{1,17},{2,18},{3,19},{4,20},{5,21},{6,22},{7,23},{8,24},{9,... | collective-permute-start | bytes 110600 | tf_op jit(solution)/shard_map/ppermute | solution.py:434
  61.6 2.4 %collective-permute-start.19 = (f32[2,48,96]{2,1,0:T(8,128)S(1)}, f32[2,48,96]{2,1,0:T(8,128)S(1)}, u32[]{:S(2)}, u32[]{:S(2)}) collective-permute-start(f32[2,48,96]{2,1,0:T(8,128)S(1)} %pad_maximum_fusion.4.refs_0_), channel_id=1, source_target_pairs={{0,8},{1,9},{2,10},{3,11},{4,12},{5,13},{6,14},{7,15},{8,0},{9,1},... | collective-permute-start | bytes 110600 | tf_op jit(solution)/shard_map/ppermute | solution.py:434
  64.0 1.0 %shard_map.74 = f32[32,32,48]{2,1,0:T(8,128)} custom-call(f32[4,48,256]{2,1,0:T(8,128)S(1)} %pad_maximum_fusion.2.rest_0_.refs_0_, f32[4,48,256]{2,1,0:T(8,128)S(1)} %collective-permute-done.14.rest_0_.refs_1_, f32[4,48,256]{2,1,0:T(8,128)S(1)} %collective-permute-done.12.rest_2_.refs_2_, f32[4,48,256]{2,1,0:T(8,128)S(1)} %collective-permute-done.16.rest_2_.refs_3_), custom_call_target="tpu_custom_call" | custom-call | tf_op jit(solution)/shard_map/pallas_call | solution.py:391
  65.0 0.6 collective-permute-done.21.refs_3_
  65.6 0.9 %collective-permute-done.20.refs_2_ = f32[2,48,96]{2,1,0:T(8,128)S(1)} collective-permute-done((f32[2,48,96]{2,1,0:T(8,128)S(1)}, f32[2,48,96]{2,1,0:T(8,128)S(1)}, u32[]{:S(2)}, u32[]{:S(2)}) %collective-permute-start.20) | collective-permute-done | bytes 36896 | tf_op jit(solution)/shard_map/ppermute | solution.py:434
  66.5 0.0 collective-permute-done.19.refs_1_
  66.5 0.8 %shard_map.73 = f32[48,768]{1,0:T(8,128)} custom-call(f32[2,48,96]{2,1,0:T(8,128)S(1)} %pad_maximum_fusion.4.refs_0_, f32[2,48,96]{2,1,0:T(8,128)S(1)} %collective-permute-done.19.refs_1_, f32[2,48,96]{2,1,0:T(8,128)S(1)} %collective-permute-done.20.refs_2_, f32[2,48,96]{2,1,0:T(8,128)S(1)} %collective-permute-done.21.refs_3_), custom_call_target="tpu_custom_call" | custom-call | tf_op jit(solution)/shard_map/pallas_call | solution.py:418
  (9 shorter events, 0.1 us)
Async XLA Ops:
  8.1 1.9 %collective-permute-start = (f32[792,128]{1,0:T(8,128)S(1)}, f32[792,128]{1,0:T(8,128)S(1)}, u32[]{:S(2)}, u32[]{:S(2)}) collective-permute-start(f32[792,128]{1,0:T(8,128)S(1)} %get-tuple-element.17), channel_id=1, source_target_pairs={{0,1},{1,0},{2,3},{3,2},{4,5},{5,4},{6,7},{7,6},{8,9},{9,8},{10,11... | collective-permute-start | bytes 1216520 | tf_op jit(solution)/shard_map/ppermute | solution.py:434
  10.0 1.7 %collective-permute-start.1 = (f32[768,128]{1,0:T(8,128)S(1)}, f32[768,128]{1,0:T(8,128)S(1)}, u32[]{:S(2)}, u32[]{:S(2)}) collective-permute-start(f32[768,128]{1,0:T(8,128)S(1)} %get-tuple-element.23), channel_id=1, source_target_pairs={{0,1},{1,0},{2,3},{3,2},{4,5},{5,4},{6,7},{7,6},{8,9},{9,8},{10,11... | collective-permute-start | bytes 1179656 | tf_op jit(solution)/shard_map/ppermute | solution.py:434
  10.4 19.6 %copy-start = (f32[48,32,32]{0,2,1:T(8,128)S(1)}, f32[48,32,32]{0,2,1:T(8,128)}, u32[]{:S(2)}) copy-start(f32[48,32,32]{0,2,1:T(8,128)} %param.9) | copy-start | bytes 589828
  11.8 9.6 %collective-permute-start.4 = (f32[192,256]{1,0:T(8,128)S(1)}, f32[192,256]{1,0:T(8,128)S(1)}, u32[]{:S(2)}, u32[]{:S(2)}) collective-permute-start(f32[192,256]{1,0:T(8,128)S(1)} %pad_maximum_fusion.1), channel_id=1, source_target_pairs={{0,6},{1,7},{2,4},{3,5},{4,2},{5,3},{6,0},{7,1},{8,14},{9,15},{10,... | collective-permute-start | bytes 589832 | tf_op jit(solution)/shard_map/ppermute | solution.py:434
  15.7 9.7 %collective-permute-start.2 = (f32[208,256]{1,0:T(8,128)S(1)}, f32[208,256]{1,0:T(8,128)S(1)}, u32[]{:S(2)}, u32[]{:S(2)}) collective-permute-start(f32[208,256]{1,0:T(8,128)S(1)} %select_maximum_fusion.mine_ref), channel_id=1, source_target_pairs={{0,2},{1,3},{2,0},{3,1},{4,6},{5,7},{6,4},{7,5},{8,10},{9,11},{10,... | collective-permute-start | bytes 638984 | tf_op jit(solution)/shard_map/ppermute | solution.py:434
  16.3 9.1 %collective-permute-start.3 = (f32[192,256]{1,0:T(8,128)S(1)}, f32[192,256]{1,0:T(8,128)S(1)}, u32[]{:S(2)}, u32[]{:S(2)}) collective-permute-start(f32[192,256]{1,0:T(8,128)S(1)} %pad_maximum_fusion), channel_id=1, source_target_pairs={{0,4},{1,5},{2,6},{3,7},{4,0},{5,1},{6,2},{7,3},{8,12},{9,13},{10,... | collective-permute-start | bytes 589832 | tf_op jit(solution)/shard_map/ppermute | solution.py:434
  25.5 6.0 %collective-permute-start.7 = (f32[48,256]{1,0:T(8,128)S(1)}, f32[48,256]{1,0:T(8,128)S(1)}, u32[]{:S(2)}, u32[]{:S(2)}) collective-permute-start(f32[48,256]{1,0:T(8,128)S(1)} %get-tuple-element.28), channel_id=1, source_target_pairs={{0,24},{1,25},{2,26},{3,27},{4,28},{5,29},{6,30},{7,31},{8,16},{9,... | collective-permute-start | bytes 147464 | tf_op jit(solution)/shard_map/ppermute | solution.py:434
  29.4 5.0 %collective-permute-start.6 = (f32[48,256]{1,0:T(8,128)S(1)}, f32[48,256]{1,0:T(8,128)S(1)}, u32[]{:S(2)}, u32[]{:S(2)}) collective-permute-start(f32[48,256]{1,0:T(8,128)S(1)} %get-tuple-element.29), channel_id=1, source_target_pairs={{0,16},{1,17},{2,18},{3,19},{4,20},{5,21},{6,22},{7,23},{8,24},{9,... | collective-permute-start | bytes 147464 | tf_op jit(solution)/shard_map/ppermute | solution.py:434
  29.4 5.0 %collective-permute-start.5 = (f32[48,256]{1,0:T(8,128)S(1)}, f32[48,256]{1,0:T(8,128)S(1)}, u32[]{:S(2)}, u32[]{:S(2)}) collective-permute-start(f32[48,256]{1,0:T(8,128)S(1)} %get-tuple-element.30), channel_id=1, source_target_pairs={{0,8},{1,9},{2,10},{3,11},{4,12},{5,13},{6,14},{7,15},{8,0},{9,1},... | collective-permute-start | bytes 147464 | tf_op jit(solution)/shard_map/ppermute | solution.py:434
  34.4 6.3 %collective-permute-start.10 = (f32[48,256]{1,0:T(8,128)S(1)}, f32[48,256]{1,0:T(8,128)S(1)}, u32[]{:S(2)}, u32[]{:S(2)}) collective-permute-start(f32[48,256]{1,0:T(8,128)S(1)} %fusion.8), channel_id=1, source_target_pairs={{0,24},{1,25},{2,26},{3,27},{4,28},{5,29},{6,30},{7,31},{8,16},{9,... | collective-permute-start | bytes 147464 | tf_op jit(solution)/shard_map/ppermute | solution.py:434
  36.6 5.4 %collective-permute-start.9 = (f32[48,256]{1,0:T(8,128)S(1)}, f32[48,256]{1,0:T(8,128)S(1)}, u32[]{:S(2)}, u32[]{:S(2)}) collective-permute-start(f32[48,256]{1,0:T(8,128)S(1)} %fusion.8), channel_id=1, source_target_pairs={{0,16},{1,17},{2,18},{3,19},{4,20},{5,21},{6,22},{7,23},{8,24},{9,... | collective-permute-start | bytes 147464 | tf_op jit(solution)/shard_map/ppermute | solution.py:434
  36.7 5.3 %collective-permute-start.8 = (f32[48,256]{1,0:T(8,128)S(1)}, f32[48,256]{1,0:T(8,128)S(1)}, u32[]{:S(2)}, u32[]{:S(2)}) collective-permute-start(f32[48,256]{1,0:T(8,128)S(1)} %fusion.8), channel_id=1, source_target_pairs={{0,8},{1,9},{2,10},{3,11},{4,12},{5,13},{6,14},{7,15},{8,0},{9,1},... | collective-permute-start | bytes 147464 | tf_op jit(solution)/shard_map/ppermute | solution.py:434
  42.0 8.4 %collective-permute-start.13 = (f32[4,48,256]{2,1,0:T(8,128)S(1)}, f32[4,48,256]{2,1,0:T(8,128)S(1)}, u32[]{:S(2)}, u32[]{:S(2)}) collective-permute-start(f32[4,48,256]{2,1,0:T(8,128)S(1)} %pad_maximum_fusion.2.rest_0_.refs_0_), channel_id=1, source_target_pairs={{0,6},{1,7},{2,4},{3,5},{4,2},{5,3},{6,0},{7,1},{8,14},{9,15},{10,... | collective-permute-start | bytes 589832 | tf_op jit(solution)/shard_map/ppermute | solution.py:434
  43.5 8.9 %collective-permute-start.12 = (f32[4,48,256]{2,1,0:T(8,128)S(1)}, f32[4,48,256]{2,1,0:T(8,128)S(1)}, u32[]{:S(2)}, u32[]{:S(2)}) collective-permute-start(f32[4,48,256]{2,1,0:T(8,128)S(1)} %pad_maximum_fusion.2.rest_0_.refs_0_), channel_id=1, source_target_pairs={{0,2},{1,3},{2,0},{3,1},{4,6},{5,7},{6,4},{7,5},{8,10},{9,11},{10,... | collective-permute-start | bytes 589832 | tf_op jit(solution)/shard_map/ppermute | solution.py:434
  45.0 7.5 %collective-permute-start.11 = (f32[4,48,256]{2,1,0:T(8,128)S(1)}, f32[4,48,256]{2,1,0:T(8,128)S(1)}, u32[]{:S(2)}, u32[]{:S(2)}) collective-permute-start(f32[4,48,256]{2,1,0:T(8,128)S(1)} %pad_maximum_fusion.2.rest_0_.refs_0_), channel_id=1, source_target_pairs={{0,4},{1,5},{2,6},{3,7},{4,0},{5,1},{6,2},{7,3},{8,12},{9,13},{10,... | collective-permute-start | bytes 589832 | tf_op jit(solution)/shard_map/ppermute | solution.py:434
  45.6 8.5 %collective-permute-start.14 = (f32[4,48,256]{2,1,0:T(8,128)S(1)}, f32[4,48,256]{2,1,0:T(8,128)S(1)}, u32[]{:S(2)}, u32[]{:S(2)}) collective-permute-start(f32[4,48,256]{2,1,0:T(8,128)S(1)} %pad_maximum_fusion.2.rest_0_.refs_0_), channel_id=1, source_target_pairs={{0,1},{1,0},{2,3},{3,2},{4,5},{5,4},{6,7},{7,6},{8,9},{9,8},{10,11... | collective-permute-start | bytes 589832 | tf_op jit(solution)/shard_map/ppermute | solution.py:434
  50.4 3.6 %collective-permute-start.17 = (f32[4,48,256]{2,1,0:T(8,128)S(1)}, f32[4,48,256]{2,1,0:T(8,128)S(1)}, u32[]{:S(2)}, u32[]{:S(2)}) collective-permute-start(f32[4,48,256]{2,1,0:T(8,128)S(1)} %collective-permute-done.13.rest_3_), channel_id=1, source_target_pairs={{0,1},{1,0},{2,3},{3,2},{4,5},{5,4},{6,7},{7,6},{8,9},{9,8},{10,11... | collective-permute-start | bytes 589832 | tf_op jit(solution)/shard_map/ppermute | solution.py:434
  52.5 1.6 %collective-permute-start.16 = (f32[4,48,256]{2,1,0:T(8,128)S(1)}, f32[4,48,256]{2,1,0:T(8,128)S(1)}, u32[]{:S(2)}, u32[]{:S(2)}) collective-permute-start(f32[4,48,256]{2,1,0:T(8,128)S(1)} %collective-permute-done.12.rest_2_.refs_2_), channel_id=1, source_target_pairs={{0,1},{1,0},{2,3},{3,2},{4,5},{5,4},{6,7},{7,6},{8,9},{9,8},{10,11... | collective-permute-start | bytes 589832 | tf_op jit(solution)/shard_map/ppermute | solution.py:434
  52.6 1.6 %collective-permute-start.15 = (f32[4,48,256]{2,1,0:T(8,128)S(1)}, f32[4,48,256]{2,1,0:T(8,128)S(1)}, u32[]{:S(2)}, u32[]{:S(2)}) collective-permute-start(f32[4,48,256]{2,1,0:T(8,128)S(1)} %collective-permute-done.11.rest_1_), channel_id=1, source_target_pairs={{0,1},{1,0},{2,3},{3,2},{4,5},{5,4},{6,7},{7,6},{8,9},{9,8},{10,11... | collective-permute-start | bytes 589832 | tf_op jit(solution)/shard_map/ppermute | solution.py:434
  55.6 3.9 %collective-permute-start.18 = (f32[48,96]{1,0:T(8,128)S(1)}, f32[48,96]{1,0:T(8,128)S(1)}, u32[]{:S(2)}, u32[]{:S(2)}) collective-permute-start(f32[48,96]{1,0:T(8,128)S(1)} %shard_map.72), channel_id=1, source_target_pairs={{0,4},{1,5},{2,6},{3,7},{4,0},{5,1},{6,2},{7,3},{8,12},{9,13},{10,... | collective-permute-start | bytes 55304 | tf_op jit(solution)/shard_map/ppermute | solution.py:434
  59.5 6.0 %collective-permute-start.21 = (f32[2,48,96]{2,1,0:T(8,128)S(1)}, f32[2,48,96]{2,1,0:T(8,128)S(1)}, u32[]{:S(2)}, u32[]{:S(2)}) collective-permute-start(f32[2,48,96]{2,1,0:T(8,128)S(1)} %pad_maximum_fusion.4.refs_0_), channel_id=1, source_target_pairs={{0,24},{1,25},{2,26},{3,27},{4,28},{5,29},{6,30},{7,31},{8,16},{9,... | collective-permute-start | bytes 110600 | tf_op jit(solution)/shard_map/ppermute | solution.py:434
  60.4 6.0 %collective-permute-start.20 = (f32[2,48,96]{2,1,0:T(8,128)S(1)}, f32[2,48,96]{2,1,0:T(8,128)S(1)}, u32[]{:S(2)}, u32[]{:S(2)}) collective-permute-start(f32[2,48,96]{2,1,0:T(8,128)S(1)} %pad_maximum_fusion.4.refs_0_), channel_id=1, source_target_pairs={{0,16},{1,17},{2,18},{3,19},{4,20},{5,21},{6,22},{7,23},{8,24},{9,... | collective-permute-start | bytes 110600 | tf_op jit(solution)/shard_map/ppermute | solution.py:434
  61.6 4.9 %collective-permute-start.19 = (f32[2,48,96]{2,1,0:T(8,128)S(1)}, f32[2,48,96]{2,1,0:T(8,128)S(1)}, u32[]{:S(2)}, u32[]{:S(2)}) collective-permute-start(f32[2,48,96]{2,1,0:T(8,128)S(1)} %pad_maximum_fusion.4.refs_0_), channel_id=1, source_target_pairs={{0,8},{1,9},{2,10},{3,11},{4,12},{5,13},{6,14},{7,15},{8,0},{9,1},... | collective-permute-start | bytes 110600 | tf_op jit(solution)/shard_map/ppermute | solution.py:434

commit v19 on v17

--- a/solution.py
+++ b/solution.py
@@ -101,23 +101,33 @@
     return jnp.concatenate([blocks[:height], blocks[height:]], axis=1)
 
 
-def row_table(base, margin, height):
-    high = base.astype(BF16).astype(F32)
-    low = base - high
-    plane = lax.broadcasted_iota(jnp.int32, (8, LANES), 0)
+def blur_rows_of(images, rows, margin):
+    height = images[0].shape[0]
+    sub = lax.broadcasted_iota(jnp.int32, (8, LANES), 0)
     lane = lax.broadcasted_iota(jnp.int32, (8, LANES), 1)
-    per_vector = LANES // height
-    own = lane // height == plane % per_vector
-    masks = [own & (plane // per_vector == part) for part in range(8 * height // LANES)]
-
-    def table(part):
-        strips = []
-        for row in range(height):
-            rolled = pltpu.roll(part, (row - margin) % LANES, 1)
-            strips.append(jnp.concatenate([jnp.where(mask, rolled, 0.0) for mask in masks], axis=1))
-        return jnp.concatenate(strips, axis=0).astype(BF16)
-
-    return table(high), table(low)
+    lower = sub < 4
+    own = lane // height == sub % 4
+    moved = pltpu.roll(pltpu.roll(rows, 4, 0), 1, 1)
+    results = []
+    for group, base in ((0, jnp.where(lower, rows, moved)), (1, jnp.where(lower, moved, rows))):
+        high = base.astype(BF16).astype(F32)
+        strips = [
+            jnp.where(own, pltpu.roll(part, (2 * pair - margin) % LANES, 1), 0.0)
+            for part in (high, base - high) for pair in range(height // 2)]
+        table = jnp.concatenate(strips, axis=0).astype(BF16)
+        table = jnp.concatenate([table, table], axis=1)
+        image = jnp.concatenate(split(jnp.concatenate(images[4 * group:4 * group + 4], axis=0)), axis=0)
+        product = dot(table, image)
+        half = product.shape[0] // 2
+        results.append(product[:half] + product[half:])
+    lower = lax.broadcasted_iota(jnp.int32, (8, results[0].shape[1]), 0) < 4
+    out = []
+    for pair in range(height // 2):
+        here = slice(8 * pair, 8 * pair + 8)
+        one, two = results[0][here], results[1][here]
+        out.append(jnp.where(lower, one, two))
+        out.append(pltpu.roll(jnp.where(lower, two, one), 4, 0))
+    return jnp.concatenate(out, axis=0).reshape(height, 8, results[0].shape[1])
 
 
 def fold(square):
@@ -149,18 +159,14 @@
 
 
 def blur_group(step, cube_ref, kx_ref, ky_ref, xh_ref, xl_ref, margin):
-    height = cube_ref.shape[1]
     halves = []
     for half in range(GROUP // 8):
         done = []
         for k in range(8 * half, 8 * half + 8):
             plane = step * GROUP + k
             done.append(blur_plane(cube_ref[plane], kx_ref[pl.ds(plane, 1), :], margin))
-        high, low = split(jnp.concatenate(done, axis=0))
         rows = ky_ref[pl.ds(pl.multiple_of(step * GROUP + 8 * half, 8), 8), :]
-        table_high, table_low = row_table(rows, margin, height)
-        result = dot(table_high, high) + (dot(table_low, high) + dot(table_high, low))
-        halves.append(result.reshape(height, 8, result.shape[1]))
+        halves.append(blur_rows_of(done, rows, margin))
     high, low = split(jnp.concatenate(halves, axis=1))
     planes_here = pl.ds(pl.multiple_of(step * GROUP, GROUP), GROUP)
     xh_ref[:, planes_here, :] = high
@@ -361,7 +367,11 @@
     gram = total[2 * planes:]
     gram = gram[:rank, :rank] + (gram[:rank, rank:] + gram[rank:, :rank])
     w_here = w_ref[...]
-    w_out[...] = w_here * jnp.transpose(numer) / dot_exact(gram, w_here)
+    gram_high, gram_low = split(gram)
+    w_high, w_low = split(w_here)
+    both = dot(jnp.concatenate([gram_high, gram_low], axis=0), w_high)
+    denominator = both[:rank] + (both[rank:] + dot(gram_high, w_low))
+    w_out[...] = w_here * jnp.transpose(numer) / denominator
 
 
 def second_call(x_high, x_low, w_here, total, parts):
@@ -540,7 +550,7 @@
     out_specs = (P("bd", None, None), P(None, None, "sp"))
 
     def body(cube, *rest):
-        suits = lax.axis_size("sp") == 8 and lax.axis_size("bd") == 4 and cube.shape[1] % GROUP == 0
+        suits = lax.axis_size("sp") == 8 and lax.axis_size("bd") == 4 and cube.shape[1:] == (96, 32, 2 * LANES)
         return (local if suits else local_any)(cube, *rest)
 
     return jax.shard_map(body, mesh=mesh, in_specs=in_specs, out_specs=out_specs, check_vma=False)

time: 66 us -> 65.8 us (level)
  no operation moved by 1% of the time
where the time goes in v19:
time: 65.8 us; the launch traced here: 65.6 us
  starting transfers between devices  28.7 us (44%)
  waiting for transfers between devices  23.4 us (36%)
  Pallas kernels  12.5 us (19%)
  between operations  0.75 us (1%)
    ppermute x25, starting transfers between devices, send(): return lax.ppermute(value, ('sp', 'bd'), pairs)  28.7 us
    ppermute x25, waiting for transfers between devices, send(): return lax.ppermute(value, ('sp', 'bd'), pairs)  23.4 us
    pallas_call x1, Pallas kernels, blur_call(): pl.pallas_call(blur_kernel, out_shape=[jax.ShapeDtypeStruct(image, BF16)]...  7.33 us
    pallas_call x1, Pallas kernels, second_call(): pl.pallas_call(second_kernel, out_shape=jax.ShapeDtypeStruct(w_here.shape...  1.39 us
  transfers between devices with their start and end apart: 25, of which 15 were waited for; matrix products, arithmetic and copies ran while one was open for 0% of the time, Pallas kernels for 5%

profile of v19, /device:TPU:0, one launch (start us, length us, event | category | flops | bytes accessed | tf_op | source)
XLA Modules:
  0.0 65.6 jit_solution(1519995436280321879)
XLA Ops:
  0.6 7.3 %shard_map.68 = (bf16[32,96,256]{2,1,0:T(8,128)(2,1)S(1)}, bf16[32,96,256]{2,1,0:T(8,128)(2,1)S(1)}, f32[48,96]{1,0:T(8,128)S(1)}, bf16[96,256]{1,0:T(8,128)(2,1...) custom-call(f32[96,32,256]{2,1,0:T(8,128)} %bitcast.19, f32[25,1,96]{2,1,0:T(1,128)} %bitcast.28, ...), custom_call_target="tpu_custom_call" | custom-call | tf_op jit(solution)/shard_map/pallas_call | solution.py:280
  8.0 0.5 collective-permute-start
  8.5 0.7 %shard_map.69 = (f32[768,128]{1,0:T(8,128)S(1)}, f32[768,128]{1,0:T(8,128)S(1)}) custom-call(bf16[32,96,256]{2,1,0:T(8,128)(2,1)S(1)} %get-tuple-element.13.xh_ref, bf16[32,96,256]{2,1,0:T(8,128)(2,1)S(1)} %get-tuple-element.14.xl_ref, bf16[96,256]{1,0:T(8,128)(2,1)S(1)} %get-tuple-element.18.w_both_ref), custom_call_target="tpu_custom_call" | custom-call | tf_op jit(solution)/shard_map/pallas_call | solution.py:263
  9.2 0.7 %collective-permute-done = f32[792,128]{1,0:T(8,128)S(1)} collective-permute-done((f32[792,128]{1,0:T(8,128)S(1)}, f32[792,128]{1,0:T(8,128)S(1)}, u32[]{:S(2)}, u32[]{:S(2)}) %collective-permute-start) | collective-permute-done | bytes 405536 | tf_op jit(solution)/shard_map/ppermute | solution.py:442
  9.9 0.4 collective-permute-start.4
  10.3 0.0 copy-start
  10.3 3.7 %collective-permute-start.3 = (f32[192,128]{1,0:T(8,128)S(1)}, f32[192,128]{1,0:T(8,128)S(1)}, u32[]{:S(2)}, u32[]{:S(2)}) collective-permute-start(f32[192,128]{1,0:T(8,128)S(1)} %get-tuple-element.25), channel_id=1, source_target_pairs={{0,6},{1,7},{2,4},{3,5},{4,2},{5,3},{6,0},{7,1},{8,14},{9,15},{10,... | collective-permute-start | bytes 294920 | tf_op jit(solution)/shard_map/ppermute | solution.py:442
  13.9 0.5 collective-permute-start.2
  14.5 0.2 collective-permute-start.1
  14.7 0.0 collective-permute-done.4
  14.7 0.1 slice_add_fusion.4
  14.7 2.9 %collective-permute-start.7 = (f32[192,128]{1,0:T(8,128)S(1)}, f32[192,128]{1,0:T(8,128)S(1)}, u32[]{:S(2)}, u32[]{:S(2)}) collective-permute-start(f32[192,128]{1,0:T(8,128)S(1)} %get-tuple-element.28), channel_id=1, source_target_pairs={{0,6},{1,7},{2,4},{3,5},{4,2},{5,3},{6,0},{7,1},{8,14},{9,15},{10,... | collective-permute-start | bytes 294920 | tf_op jit(solution)/shard_map/ppermute | solution.py:442
  17.6 0.5 collective-permute-start.6
  18.1 0.0 collective-permute-done.3
  18.1 1.3 %collective-permute-start.5 = (f32[192,128]{1,0:T(8,128)S(1)}, f32[192,128]{1,0:T(8,128)S(1)}, u32[]{:S(2)}, u32[]{:S(2)}) collective-permute-start(f32[192,128]{1,0:T(8,128)S(1)} %get-tuple-element.30), channel_id=1, source_target_pairs={{0,4},{1,5},{2,6},{3,7},{4,0},{5,1},{6,2},{7,3},{8,12},{9,13},{10,... | collective-permute-start | bytes 294920 | tf_op jit(solution)/shard_map/ppermute | solution.py:442
  19.5 0.7 %collective-permute-done.2 = f32[192,128]{1,0:T(8,128)S(1)} collective-permute-done((f32[192,128]{1,0:T(8,128)S(1)}, f32[192,128]{1,0:T(8,128)S(1)}, u32[]{:S(2)}, u32[]{:S(2)}) %collective-permute-start.2) | collective-permute-done | bytes 98336 | tf_op jit(solution)/shard_map/ppermute | solution.py:442
  20.2 1.9 %collective-permute-done.1.other_ref = f32[216,128]{1,0:T(8,128)S(1)} collective-permute-done((f32[216,128]{1,0:T(8,128)S(1)}, f32[216,128]{1,0:T(8,128)S(1)}, u32[]{:S(2)}, u32[]{:S(2)}) %collective-permute-start.1) | collective-permute-done | bytes 110624 | tf_op jit(solution)/shard_map/ppermute | solution.py:442
  22.1 0.0 collective-permute-done.7
  22.1 1.7 %collective-permute-done.6 = f32[192,128]{1,0:T(8,128)S(1)} collective-permute-done((f32[192,128]{1,0:T(8,128)S(1)}, f32[192,128]{1,0:T(8,128)S(1)}, u32[]{:S(2)}, u32[]{:S(2)}) %collective-permute-start.6) | collective-permute-done | bytes 98336 | tf_op jit(solution)/shard_map/ppermute | solution.py:442
  23.8 0.0 collective-permute-done.5
  23.9 3.9 %collective-permute-start.8 = (f32[48,256]{1,0:T(8,128)S(1)}, f32[48,256]{1,0:T(8,128)S(1)}, u32[]{:S(2)}, u32[]{:S(2)}) collective-permute-start(f32[48,256]{1,0:T(8,128)S(1)} %pad_maximum_fusion.1), channel_id=1, source_target_pairs={{0,24},{1,25},{2,26},{3,27},{4,28},{5,29},{6,30},{7,31},{8,16},{9,... | collective-permute-start | bytes 147464 | tf_op jit(solution)/shard_map/ppermute | solution.py:442
  27.8 0.0 collective-permute-start.9
  27.8 0.6 collective-permute-start.10
  28.4 0.0 copy-done
  28.4 0.3 shard_map.70
  28.7 1.5 %collective-permute-done.8 = f32[48,256]{1,0:T(8,128)S(1)} collective-permute-done((f32[48,256]{1,0:T(8,128)S(1)}, f32[48,256]{1,0:T(8,128)S(1)}, u32[]{:S(2)}, u32[]{:S(2)}) %collective-permute-start.8) | collective-permute-done | bytes 49184 | tf_op jit(solution)/shard_map/ppermute | solution.py:442
  30.2 2.6 %collective-permute-done.9 = f32[48,256]{1,0:T(8,128)S(1)} collective-permute-done((f32[48,256]{1,0:T(8,128)S(1)}, f32[48,256]{1,0:T(8,128)S(1)}, u32[]{:S(2)}, u32[]{:S(2)}) %collective-permute-start.9) | collective-permute-done | bytes 49184 | tf_op jit(solution)/shard_map/ppermute | solution.py:442
  32.8 0.0 collective-permute-done.10
  32.8 1.9 %collective-permute-start.13 = (f32[48,256]{1,0:T(8,128)S(1)}, f32[48,256]{1,0:T(8,128)S(1)}, u32[]{:S(2)}, u32[]{:S(2)}) collective-permute-start(f32[48,256]{1,0:T(8,128)S(1)} %fusion.1), channel_id=1, source_target_pairs={{0,24},{1,25},{2,26},{3,27},{4,28},{5,29},{6,30},{7,31},{8,16},{9,... | collective-permute-start | bytes 147464 | tf_op jit(solution)/shard_map/ppermute | solution.py:442
  34.7 0.3 collective-permute-start.12
  35.0 2.3 %collective-permute-start.11 = (f32[48,256]{1,0:T(8,128)S(1)}, f32[48,256]{1,0:T(8,128)S(1)}, u32[]{:S(2)}, u32[]{:S(2)}) collective-permute-start(f32[48,256]{1,0:T(8,128)S(1)} %fusion.1), channel_id=1, source_target_pairs={{0,8},{1,9},{2,10},{3,11},{4,12},{5,13},{6,14},{7,15},{8,0},{9,1},... | collective-permute-start | bytes 147464 | tf_op jit(solution)/shard_map/ppermute | solution.py:442
  37.2 1.5 %collective-permute-done.13 = f32[48,256]{1,0:T(8,128)S(1)} collective-permute-done((f32[48,256]{1,0:T(8,128)S(1)}, f32[48,256]{1,0:T(8,128)S(1)}, u32[]{:S(2)}, u32[]{:S(2)}) %collective-permute-start.13) | collective-permute-done | bytes 49184 | tf_op jit(solution)/shard_map/ppermute | solution.py:442
  38.7 1.4 %collective-permute-done.12 = f32[48,256]{1,0:T(8,128)S(1)} collective-permute-done((f32[48,256]{1,0:T(8,128)S(1)}, f32[48,256]{1,0:T(8,128)S(1)}, u32[]{:S(2)}, u32[]{:S(2)}) %collective-permute-start.12) | collective-permute-done | bytes 49184 | tf_op jit(solution)/shard_map/ppermute | solution.py:442
  40.2 0.0 collective-permute-done.11
  40.2 2.7 %collective-permute-start.16 = (f32[4,48,256]{2,1,0:T(8,128)S(1)}, f32[4,48,256]{2,1,0:T(8,128)S(1)}, u32[]{:S(2)}, u32[]{:S(2)}) collective-permute-start(f32[4,48,256]{2,1,0:T(8,128)S(1)} %pad_maximum_fusion.rest_0_.refs_0_), channel_id=1, source_target_pairs={{0,6},{1,7},{2,4},{3,5},{4,2},{5,3},{6,0},{7,1},{8,14},{9,15},{10,... | collective-permute-start | bytes 589832 | tf_op jit(solution)/shard_map/ppermute | solution.py:442
  42.9 0.2 collective-permute-start.15
  43.1 0.6 collective-permute-start.14
  43.8 0.0 collective-permute-start.17
  43.8 4.9 %collective-permute-done.16.rest_3_ = f32[4,48,256]{2,1,0:T(8,128)S(1)} collective-permute-done((f32[4,48,256]{2,1,0:T(8,128)S(1)}, f32[4,48,256]{2,1,0:T(8,128)S(1)}, u32[]{:S(2)}, u32[]{:S(2)}) %collective-permute-start.16) | collective-permute-done | bytes 196640 | tf_op jit(solution)/shard_map/ppermute | solution.py:442
  48.7 0.0 collective-permute-start.20
  48.7 2.1 %collective-permute-done.15.rest_2_.refs_2_ = f32[4,48,256]{2,1,0:T(8,128)S(1)} collective-permute-done((f32[4,48,256]{2,1,0:T(8,128)S(1)}, f32[4,48,256]{2,1,0:T(8,128)S(1)}, u32[]{:S(2)}, u32[]{:S(2)}) %collective-permute-start.15) | collective-permute-done | bytes 196640 | tf_op jit(solution)/shard_map/ppermute | solution.py:442
  50.8 0.0 collective-permute-start.19
  50.8 0.3 collective-permute-done.14.rest_1_
  51.1 0.2 collective-permute-start.18
  51.3 1.0 %shard_map.71.total_ref = f32[288,96]{1,0:T(8,128)S(1)} custom-call(bf16[32,96,256]{2,1,0:T(8,128)(2,1)S(1)} %get-tuple-element.13.xh_ref, bf16[32,96,256]{2,1,0:T(8,128)(2,1)S(1)} %get-tuple-element.14.xl_ref, f32[4,48,256]{2,1,0:T(8,128)S(1)} %pad_maximum_fusion.rest_0_.refs_0_, f32[4,48,256]{2,1,0:T(8,128)S(1)} %collective-permute-done.14.rest_1_, ...), custom_call_target="tpu_custom_call" | custom-call | tf_op jit(solution)/shard_map/pallas_call | solution.py:351
  52.3 0.0 collective-permute-done.17.rest_0_.refs_1_
  52.3 0.0 collective-permute-done.20.rest_3_
  52.4 0.0 collective-permute-done.19.rest_2_.refs_3_
  52.4 0.1 collective-permute-done.18.rest_1_
  52.5 1.4 %shard_map.72 = f32[48,96]{1,0:T(8,128)S(1)} custom-call(bf16[32,96,256]{2,1,0:T(8,128)(2,1)S(1)} %get-tuple-element.13.xh_ref, bf16[32,96,256]{2,1,0:T(8,128)(2,1)S(1)} %get-tuple-element.14.xl_ref, f32[48,96]{1,0:T(8,128)S(1)} %get-tuple-element.15.w_ref, f32[288,96]{1,0:T(8,128)S(1)} %shard_map.71.total_ref, ...), custom_call_target="tpu_custom_call" | custom-call | tf_op jit(solution)/shard_map/pallas_call | solution.py:379
  53.9 1.5 %collective-permute-start.21 = (f32[48,96]{1,0:T(8,128)S(1)}, f32[48,96]{1,0:T(8,128)S(1)}, u32[]{:S(2)}, u32[]{:S(2)}) collective-permute-start(f32[48,96]{1,0:T(8,128)S(1)} %shard_map.72), channel_id=1, source_target_pairs={{0,4},{1,5},{2,6},{3,7},{4,0},{5,1},{6,2},{7,3},{8,12},{9,13},{10,... | collective-permute-start | bytes 55304 | tf_op jit(solution)/shard_map/ppermute | solution.py:442
  55.5 2.3 %collective-permute-done.21 = f32[48,96]{1,0:T(8,128)S(1)} collective-permute-done((f32[48,96]{1,0:T(8,128)S(1)}, f32[48,96]{1,0:T(8,128)S(1)}, u32[]{:S(2)}, u32[]{:S(2)}) %collective-permute-start.21) | collective-permute-done | bytes 18464 | tf_op jit(solution)/shard_map/ppermute | solution.py:442
  57.8 1.0 %collective-permute-start.24 = (f32[2,48,96]{2,1,0:T(8,128)S(1)}, f32[2,48,96]{2,1,0:T(8,128)S(1)}, u32[]{:S(2)}, u32[]{:S(2)}) collective-permute-start(f32[2,48,96]{2,1,0:T(8,128)S(1)} %pad_maximum_fusion.4.refs_0_), channel_id=1, source_target_pairs={{0,24},{1,25},{2,26},{3,27},{4,28},{5,29},{6,30},{7,31},{8,16},{9,... | collective-permute-start | bytes 110600 | tf_op jit(solution)/shard_map/ppermute | solution.py:442
  58.9 1.0 %collective-permute-start.23 = (f32[2,48,96]{2,1,0:T(8,128)S(1)}, f32[2,48,96]{2,1,0:T(8,128)S(1)}, u32[]{:S(2)}, u32[]{:S(2)}) collective-permute-start(f32[2,48,96]{2,1,0:T(8,128)S(1)} %pad_maximum_fusion.4.refs_0_), channel_id=1, source_target_pairs={{0,16},{1,17},{2,18},{3,19},{4,20},{5,21},{6,22},{7,23},{8,24},{9,... | collective-permute-start | bytes 110600 | tf_op jit(solution)/shard_map/ppermute | solution.py:442
  59.9 2.4 %collective-permute-start.22 = (f32[2,48,96]{2,1,0:T(8,128)S(1)}, f32[2,48,96]{2,1,0:T(8,128)S(1)}, u32[]{:S(2)}, u32[]{:S(2)}) collective-permute-start(f32[2,48,96]{2,1,0:T(8,128)S(1)} %pad_maximum_fusion.4.refs_0_), channel_id=1, source_target_pairs={{0,8},{1,9},{2,10},{3,11},{4,12},{5,13},{6,14},{7,15},{8,0},{9,1},... | collective-permute-start | bytes 110600 | tf_op jit(solution)/shard_map/ppermute | solution.py:442
  62.3 1.0 %shard_map.74 = f32[32,32,48]{2,1,0:T(8,128)} custom-call(f32[4,48,256]{2,1,0:T(8,128)S(1)} %pad_maximum_fusion.rest_0_.refs_0_, f32[4,48,256]{2,1,0:T(8,128)S(1)} %collective-permute-done.17.rest_0_.refs_1_, f32[4,48,256]{2,1,0:T(8,128)S(1)} %collective-permute-done.15.rest_2_.refs_2_, f32[4,48,256]{2,1,0:T(8,128)S(1)} %collective-permute-done.19.rest_2_.refs_3_), custom_call_target="tpu_custom_call" | custom-call | tf_op jit(solution)/shard_map/pallas_call | solution.py:399
  63.3 0.6 collective-permute-done.24.refs_3_
  63.8 1.0 %collective-permute-done.23.refs_2_ = f32[2,48,96]{2,1,0:T(8,128)S(1)} collective-permute-done((f32[2,48,96]{2,1,0:T(8,128)S(1)}, f32[2,48,96]{2,1,0:T(8,128)S(1)}, u32[]{:S(2)}, u32[]{:S(2)}) %collective-permute-start.23) | collective-permute-done | bytes 36896 | tf_op jit(solution)/shard_map/ppermute | solution.py:442
  64.9 0.0 collective-permute-done.22.refs_1_
  64.9 0.8 %shard_map.73 = f32[48,768]{1,0:T(8,128)} custom-call(f32[2,48,96]{2,1,0:T(8,128)S(1)} %pad_maximum_fusion.4.refs_0_, f32[2,48,96]{2,1,0:T(8,128)S(1)} %collective-permute-done.22.refs_1_, f32[2,48,96]{2,1,0:T(8,128)S(1)} %collective-permute-done.23.refs_2_, f32[2,48,96]{2,1,0:T(8,128)S(1)} %collective-permute-done.24.refs_3_), custom_call_target="tpu_custom_call" | custom-call | tf_op jit(solution)/shard_map/pallas_call | solution.py:426
  (10 shorter events, 0.2 us)
Async XLA Ops:
  8.0 1.9 %collective-permute-start = (f32[792,128]{1,0:T(8,128)S(1)}, f32[792,128]{1,0:T(8,128)S(1)}, u32[]{:S(2)}, u32[]{:S(2)}) collective-permute-start(f32[792,128]{1,0:T(8,128)S(1)} %get-tuple-element.17), channel_id=1, source_target_pairs={{0,1},{1,0},{2,3},{3,2},{4,5},{5,4},{6,7},{7,6},{8,9},{9,8},{10,11... | collective-permute-start | bytes 1216520 | tf_op jit(solution)/shard_map/ppermute | solution.py:442
  9.9 4.8 %collective-permute-start.4 = (f32[768,128]{1,0:T(8,128)S(1)}, f32[768,128]{1,0:T(8,128)S(1)}, u32[]{:S(2)}, u32[]{:S(2)}) collective-permute-start(f32[768,128]{1,0:T(8,128)S(1)} %get-tuple-element.23), channel_id=1, source_target_pairs={{0,1},{1,0},{2,3},{3,2},{4,5},{5,4},{6,7},{7,6},{8,9},{9,8},{10,11... | collective-permute-start | bytes 1179656 | tf_op jit(solution)/shard_map/ppermute | solution.py:442
  10.3 18.2 %copy-start = (f32[48,32,32]{0,2,1:T(8,128)S(1)}, f32[48,32,32]{0,2,1:T(8,128)}, u32[]{:S(2)}) copy-start(f32[48,32,32]{0,2,1:T(8,128)} %param.9) | copy-start | bytes 589828
  10.3 7.9 %collective-permute-start.3 = (f32[192,128]{1,0:T(8,128)S(1)}, f32[192,128]{1,0:T(8,128)S(1)}, u32[]{:S(2)}, u32[]{:S(2)}) collective-permute-start(f32[192,128]{1,0:T(8,128)S(1)} %get-tuple-element.25), channel_id=1, source_target_pairs={{0,6},{1,7},{2,4},{3,5},{4,2},{5,3},{6,0},{7,1},{8,14},{9,15},{10,... | collective-permute-start | bytes 294920 | tf_op jit(solution)/shard_map/ppermute | solution.py:442
  13.9 6.2 %collective-permute-start.2 = (f32[192,128]{1,0:T(8,128)S(1)}, f32[192,128]{1,0:T(8,128)S(1)}, u32[]{:S(2)}, u32[]{:S(2)}) collective-permute-start(f32[192,128]{1,0:T(8,128)S(1)} %get-tuple-element.26), channel_id=1, source_target_pairs={{0,4},{1,5},{2,6},{3,7},{4,0},{5,1},{6,2},{7,3},{8,12},{9,13},{10,... | collective-permute-start | bytes 294920 | tf_op jit(solution)/shard_map/ppermute | solution.py:442
  14.5 7.6 %collective-permute-start.1 = (f32[216,128]{1,0:T(8,128)S(1)}, f32[216,128]{1,0:T(8,128)S(1)}, u32[]{:S(2)}, u32[]{:S(2)}) collective-permute-start(f32[216,128]{1,0:T(8,128)S(1)} %slice_add_fusion.mine_ref), channel_id=1, source_target_pairs={{0,2},{1,3},{2,0},{3,1},{4,6},{5,7},{6,4},{7,5},{8,10},{9,11},{10,... | collective-permute-start | bytes 331784 | tf_op jit(solution)/shard_map/ppermute | solution.py:442
  14.7 7.4 %collective-permute-start.7 = (f32[192,128]{1,0:T(8,128)S(1)}, f32[192,128]{1,0:T(8,128)S(1)}, u32[]{:S(2)}, u32[]{:S(2)}) collective-permute-start(f32[192,128]{1,0:T(8,128)S(1)} %get-tuple-element.28), channel_id=1, source_target_pairs={{0,6},{1,7},{2,4},{3,5},{4,2},{5,3},{6,0},{7,1},{8,14},{9,15},{10,... | collective-permute-start | bytes 294920 | tf_op jit(solution)/shard_map/ppermute | solution.py:442
  17.6 6.2 %collective-permute-start.6 = (f32[192,128]{1,0:T(8,128)S(1)}, f32[192,128]{1,0:T(8,128)S(1)}, u32[]{:S(2)}, u32[]{:S(2)}) collective-permute-start(f32[192,128]{1,0:T(8,128)S(1)} %get-tuple-element.29), channel_id=1, source_target_pairs={{0,2},{1,3},{2,0},{3,1},{4,6},{5,7},{6,4},{7,5},{8,10},{9,11},{10,... | collective-permute-start | bytes 294920 | tf_op jit(solution)/shard_map/ppermute | solution.py:442
  18.1 5.7 %collective-permute-start.5 = (f32[192,128]{1,0:T(8,128)S(1)}, f32[192,128]{1,0:T(8,128)S(1)}, u32[]{:S(2)}, u32[]{:S(2)}) collective-permute-start(f32[192,128]{1,0:T(8,128)S(1)} %get-tuple-element.30), channel_id=1, source_target_pairs={{0,4},{1,5},{2,6},{3,7},{4,0},{5,1},{6,2},{7,3},{8,12},{9,13},{10,... | collective-permute-start | bytes 294920 | tf_op jit(solution)/shard_map/ppermute | solution.py:442
  23.9 6.3 %collective-permute-start.8 = (f32[48,256]{1,0:T(8,128)S(1)}, f32[48,256]{1,0:T(8,128)S(1)}, u32[]{:S(2)}, u32[]{:S(2)}) collective-permute-start(f32[48,256]{1,0:T(8,128)S(1)} %pad_maximum_fusion.1), channel_id=1, source_target_pairs={{0,24},{1,25},{2,26},{3,27},{4,28},{5,29},{6,30},{7,31},{8,16},{9,... | collective-permute-start | bytes 147464 | tf_op jit(solution)/shard_map/ppermute | solution.py:442
  27.8 5.0 %collective-permute-start.9 = (f32[48,256]{1,0:T(8,128)S(1)}, f32[48,256]{1,0:T(8,128)S(1)}, u32[]{:S(2)}, u32[]{:S(2)}) collective-permute-start(f32[48,256]{1,0:T(8,128)S(1)} %pad_maximum_fusion.2), channel_id=1, source_target_pairs={{0,16},{1,17},{2,18},{3,19},{4,20},{5,21},{6,22},{7,23},{8,24},{9,... | collective-permute-start | bytes 147464 | tf_op jit(solution)/shard_map/ppermute | solution.py:442
  27.8 5.0 %collective-permute-start.10 = (f32[48,256]{1,0:T(8,128)S(1)}, f32[48,256]{1,0:T(8,128)S(1)}, u32[]{:S(2)}, u32[]{:S(2)}) collective-permute-start(f32[48,256]{1,0:T(8,128)S(1)} %pad_maximum_fusion.3), channel_id=1, source_target_pairs={{0,8},{1,9},{2,10},{3,11},{4,12},{5,13},{6,14},{7,15},{8,0},{9,1},... | collective-permute-start | bytes 147464 | tf_op jit(solution)/shard_map/ppermute | solution.py:442
  32.8 6.0 %collective-permute-start.13 = (f32[48,256]{1,0:T(8,128)S(1)}, f32[48,256]{1,0:T(8,128)S(1)}, u32[]{:S(2)}, u32[]{:S(2)}) collective-permute-start(f32[48,256]{1,0:T(8,128)S(1)} %fusion.1), channel_id=1, source_target_pairs={{0,24},{1,25},{2,26},{3,27},{4,28},{5,29},{6,30},{7,31},{8,16},{9,... | collective-permute-start | bytes 147464 | tf_op jit(solution)/shard_map/ppermute | solution.py:442
  34.7 5.5 %collective-permute-start.12 = (f32[48,256]{1,0:T(8,128)S(1)}, f32[48,256]{1,0:T(8,128)S(1)}, u32[]{:S(2)}, u32[]{:S(2)}) collective-permute-start(f32[48,256]{1,0:T(8,128)S(1)} %fusion.1), channel_id=1, source_target_pairs={{0,16},{1,17},{2,18},{3,19},{4,20},{5,21},{6,22},{7,23},{8,24},{9,... | collective-permute-start | bytes 147464 | tf_op jit(solution)/shard_map/ppermute | solution.py:442
  35.0 5.2 %collective-permute-start.11 = (f32[48,256]{1,0:T(8,128)S(1)}, f32[48,256]{1,0:T(8,128)S(1)}, u32[]{:S(2)}, u32[]{:S(2)}) collective-permute-start(f32[48,256]{1,0:T(8,128)S(1)} %fusion.1), channel_id=1, source_target_pairs={{0,8},{1,9},{2,10},{3,11},{4,12},{5,13},{6,14},{7,15},{8,0},{9,1},... | collective-permute-start | bytes 147464 | tf_op jit(solution)/shard_map/ppermute | solution.py:442
  40.2 8.5 %collective-permute-start.16 = (f32[4,48,256]{2,1,0:T(8,128)S(1)}, f32[4,48,256]{2,1,0:T(8,128)S(1)}, u32[]{:S(2)}, u32[]{:S(2)}) collective-permute-start(f32[4,48,256]{2,1,0:T(8,128)S(1)} %pad_maximum_fusion.rest_0_.refs_0_), channel_id=1, source_target_pairs={{0,6},{1,7},{2,4},{3,5},{4,2},{5,3},{6,0},{7,1},{8,14},{9,15},{10,... | collective-permute-start | bytes 589832 | tf_op jit(solution)/shard_map/ppermute | solution.py:442
  42.9 7.9 %collective-permute-start.15 = (f32[4,48,256]{2,1,0:T(8,128)S(1)}, f32[4,48,256]{2,1,0:T(8,128)S(1)}, u32[]{:S(2)}, u32[]{:S(2)}) collective-permute-start(f32[4,48,256]{2,1,0:T(8,128)S(1)} %pad_maximum_fusion.rest_0_.refs_0_), channel_id=1, source_target_pairs={{0,2},{1,3},{2,0},{3,1},{4,6},{5,7},{6,4},{7,5},{8,10},{9,11},{10,... | collective-permute-start | bytes 589832 | tf_op jit(solution)/shard_map/ppermute | solution.py:442
  43.1 7.9 %collective-permute-start.14 = (f32[4,48,256]{2,1,0:T(8,128)S(1)}, f32[4,48,256]{2,1,0:T(8,128)S(1)}, u32[]{:S(2)}, u32[]{:S(2)}) collective-permute-start(f32[4,48,256]{2,1,0:T(8,128)S(1)} %pad_maximum_fusion.rest_0_.refs_0_), channel_id=1, source_target_pairs={{0,4},{1,5},{2,6},{3,7},{4,0},{5,1},{6,2},{7,3},{8,12},{9,13},{10,... | collective-permute-start | bytes 589832 | tf_op jit(solution)/shard_map/ppermute | solution.py:442
  43.8 8.6 %collective-permute-start.17 = (f32[4,48,256]{2,1,0:T(8,128)S(1)}, f32[4,48,256]{2,1,0:T(8,128)S(1)}, u32[]{:S(2)}, u32[]{:S(2)}) collective-permute-start(f32[4,48,256]{2,1,0:T(8,128)S(1)} %pad_maximum_fusion.rest_0_.refs_0_), channel_id=1, source_target_pairs={{0,1},{1,0},{2,3},{3,2},{4,5},{5,4},{6,7},{7,6},{8,9},{9,8},{10,11... | collective-permute-start | bytes 589832 | tf_op jit(solution)/shard_map/ppermute | solution.py:442
  48.7 3.6 %collective-permute-start.20 = (f32[4,48,256]{2,1,0:T(8,128)S(1)}, f32[4,48,256]{2,1,0:T(8,128)S(1)}, u32[]{:S(2)}, u32[]{:S(2)}) collective-permute-start(f32[4,48,256]{2,1,0:T(8,128)S(1)} %collective-permute-done.16.rest_3_), channel_id=1, source_target_pairs={{0,1},{1,0},{2,3},{3,2},{4,5},{5,4},{6,7},{7,6},{8,9},{9,8},{10,11... | collective-permute-start | bytes 589832 | tf_op jit(solution)/shard_map/ppermute | solution.py:442
  50.8 1.6 %collective-permute-start.19 = (f32[4,48,256]{2,1,0:T(8,128)S(1)}, f32[4,48,256]{2,1,0:T(8,128)S(1)}, u32[]{:S(2)}, u32[]{:S(2)}) collective-permute-start(f32[4,48,256]{2,1,0:T(8,128)S(1)} %collective-permute-done.15.rest_2_.refs_2_), channel_id=1, source_target_pairs={{0,1},{1,0},{2,3},{3,2},{4,5},{5,4},{6,7},{7,6},{8,9},{9,8},{10,11... | collective-permute-start | bytes 589832 | tf_op jit(solution)/shard_map/ppermute | solution.py:442
  51.1 1.4 %collective-permute-start.18 = (f32[4,48,256]{2,1,0:T(8,128)S(1)}, f32[4,48,256]{2,1,0:T(8,128)S(1)}, u32[]{:S(2)}, u32[]{:S(2)}) collective-permute-start(f32[4,48,256]{2,1,0:T(8,128)S(1)} %collective-permute-done.14.rest_1_), channel_id=1, source_target_pairs={{0,1},{1,0},{2,3},{3,2},{4,5},{5,4},{6,7},{7,6},{8,9},{9,8},{10,11... | collective-permute-start | bytes 589832 | tf_op jit(solution)/shard_map/ppermute | solution.py:442
  53.9 3.9 %collective-permute-start.21 = (f32[48,96]{1,0:T(8,128)S(1)}, f32[48,96]{1,0:T(8,128)S(1)}, u32[]{:S(2)}, u32[]{:S(2)}) collective-permute-start(f32[48,96]{1,0:T(8,128)S(1)} %shard_map.72), channel_id=1, source_target_pairs={{0,4},{1,5},{2,6},{3,7},{4,0},{5,1},{6,2},{7,3},{8,12},{9,13},{10,... | collective-permute-start | bytes 55304 | tf_op jit(solution)/shard_map/ppermute | solution.py:442
  57.8 6.0 %collective-permute-start.24 = (f32[2,48,96]{2,1,0:T(8,128)S(1)}, f32[2,48,96]{2,1,0:T(8,128)S(1)}, u32[]{:S(2)}, u32[]{:S(2)}) collective-permute-start(f32[2,48,96]{2,1,0:T(8,128)S(1)} %pad_maximum_fusion.4.refs_0_), channel_id=1, source_target_pairs={{0,24},{1,25},{2,26},{3,27},{4,28},{5,29},{6,30},{7,31},{8,16},{9,... | collective-permute-start | bytes 110600 | tf_op jit(solution)/shard_map/ppermute | solution.py:442
  58.9 6.0 %collective-permute-start.23 = (f32[2,48,96]{2,1,0:T(8,128)S(1)}, f32[2,48,96]{2,1,0:T(8,128)S(1)}, u32[]{:S(2)}, u32[]{:S(2)}) collective-permute-start(f32[2,48,96]{2,1,0:T(8,128)S(1)} %pad_maximum_fusion.4.refs_0_), channel_id=1, source_target_pairs={{0,16},{1,17},{2,18},{3,19},{4,20},{5,21},{6,22},{7,23},{8,24},{9,... | collective-permute-start | bytes 110600 | tf_op jit(solution)/shard_map/ppermute | solution.py:442
  59.9 5.0 %collective-permute-start.22 = (f32[2,48,96]{2,1,0:T(8,128)S(1)}, f32[2,48,96]{2,1,0:T(8,128)S(1)}, u32[]{:S(2)}, u32[]{:S(2)}) collective-permute-start(f32[2,48,96]{2,1,0:T(8,128)S(1)} %pad_maximum_fusion.4.refs_0_), channel_id=1, source_target_pairs={{0,8},{1,9},{2,10},{3,11},{4,12},{5,13},{6,14},{7,15},{8,0},{9,1},... | collective-permute-start | bytes 110600 | tf_op jit(solution)/shard_map/ppermute | solution.py:442

commit v20 on v19

--- a/solution.py
+++ b/solution.py
@@ -173,7 +173,7 @@
     xl_ref[:, planes_here, :] = low
 
 
-def blur_kernel(cube_hbm, taps_x_hbm, taps_y_hbm, w_hbm, xh_ref, xl_ref, w_here_ref, w_both_ref, keep_ref, give_ref,
+def blur_kernel(cube_hbm, taps_x_hbm, taps_y_hbm, w_hbm, xh_ref, xl_ref, w_here_ref, w_both_ref, give_ref,
                 cube_ref, taps_x_ref, taps_y_ref, w_ref, sems, chunk_sems, work_ref, kx_ref, ky_ref):
     taps = taps_x_ref.shape[0]
     margin = (taps - 1) // 2
@@ -213,7 +213,6 @@
     for step in range(groups):
         blur_group(step, cube_ref, kx_ref, ky_ref, xh_ref, xl_ref, margin)
     gram = fold(band_gram(w_ref[...])[:, :rank])
-    keep_ref[PIECES * rank:] = gram
     give_ref[PIECES * rank:] = gram
     planes = xh_ref.shape[1]
     band = w_ref.shape[1]
@@ -225,24 +224,23 @@
     w_high = w_here.astype(BF16).astype(F32)
     w_both = jnp.concatenate([w_high + pltpu.roll(w_high, planes, 1), w_here - w_high], axis=0).astype(BF16)
     w_both_ref[...] = w_both
-    project(xh_ref, xl_ref, w_both[:, :2 * planes], keep_ref, give_ref, 0)
-
-
-def project(xh_ref, xl_ref, w_both, keep_ref, give_ref, chain):
+    project(xh_ref, xl_ref, w_both[:, :2 * planes], give_ref, 0, 1)
+
+
+def project(xh_ref, xl_ref, w_both, part_ref, chain, rel_core):
     height = xh_ref.shape[0]
     rank = w_both.shape[0] // 2
     me_sp = lax.axis_index("sp")
     me_bd = lax.axis_index("bd")
     tall = height // lax.axis_size("bd")
     wide = 2 * LANES // lax.axis_size("sp")
-    for rel_bd in (1, 3, 0, 2):
+    for rel_bd in (rel_core, rel_core + 2):
         first_row = lax.bitwise_xor(me_bd, rel_bd) * tall + 4 * chain
         sums = []
         for row in range(4):
             image = jnp.concatenate([xh_ref[first_row + row], xl_ref[first_row + row]], axis=0)
             both = dot(w_both, image)
             sums.append(both[:rank] + both[rank:])
-        part_ref = (keep_ref, give_ref)[rel_bd % 2]
         for column in range(2):
             pieces = exchange_blocks(
                 [value[:, column * LANES:(column + 1) * LANES] for value in sums], wide)
@@ -253,20 +251,24 @@
                 part_ref[pl.ds(first, rank)] = pieces[k]
 
 
-def project_kernel(xh_ref, xl_ref, w_both_ref, keep_ref, give_ref):
-    planes = xh_ref.shape[1]
-    project(xh_ref, xl_ref, w_both_ref[:, :2 * planes], keep_ref, give_ref, 1)
-
-
-def project_call(x_high, x_low, w_both):
+def project_kernel(xh_ref, xl_ref, w_both_ref, first_ref, keep_0, keep_1, give_1):
+    w_both = w_both_ref[:, :2 * xh_ref.shape[1]]
+    end = first_ref.shape[0] - FOLDED
+    keep_0[end:] = first_ref[end:]
+    project(xh_ref, xl_ref, w_both, give_1, 1, 1)
+    project(xh_ref, xl_ref, w_both, keep_0, 0, 0)
+    project(xh_ref, xl_ref, w_both, keep_1, 1, 0)
+
+
+def project_call(x_high, x_low, w_both, first):
     part = jax.ShapeDtypeStruct((PIECES * w_both.shape[0] // 2, LANES), F32)
     return pl.pallas_call(
         project_kernel,
-        out_shape=[part, part],
-        in_specs=in_vmem(3),
-        out_specs=in_vmem(2),
-        compiler_params=pltpu.CompilerParams(vmem_limit_bytes=VMEM_LIMIT),
-    )(x_high, x_low, w_both)
+        out_shape=[jax.ShapeDtypeStruct(first.shape, F32), part, part],
+        in_specs=in_vmem(4),
+        out_specs=in_vmem(3),
+        compiler_params=pltpu.CompilerParams(vmem_limit_bytes=VMEM_LIMIT),
+    )(x_high, x_low, w_both, first)
 
 
 def blur_call(cube, taps_x, taps_y, w_rows):
@@ -279,9 +281,9 @@
     in_hbm = [pltpu.with_memory_space_constraint(value, pltpu.HBM) for value in (cube, taps_x, taps_y, w_rows)]
     return pl.pallas_call(
         blur_kernel,
-        out_shape=[jax.ShapeDtypeStruct(image, BF16)] * 2 + [mine, both, first, first],
+        out_shape=[jax.ShapeDtypeStruct(image, BF16)] * 2 + [mine, both, first],
         in_specs=[pl.BlockSpec(memory_space=pltpu.HBM)] * 4,
-        out_specs=in_vmem(6),
+        out_specs=in_vmem(5),
         scratch_shapes=[pltpu.VMEM(value.shape, F32) for value in (cube, taps_x, taps_y, w_rows)]
         + [pltpu.SemaphoreType.DMA((3,)), pltpu.SemaphoreType.DMA((planes // GROUP,))]
         + [pltpu.VMEM((LANES, LANES), F32)] * 3,
@@ -452,11 +454,11 @@
     taps_y = jnp.transpose(taps_y, (2, 0, 1))
     h_columns = jnp.transpose(factor_h, (1, 2, 0))
     rank = w_rows.shape[0]
-    x_high, x_low, w_here, w_both, keep_0, give_0 = blur_call(cube[0], taps_x, taps_y, w_rows)
+    x_high, x_low, w_here, w_both, give_0 = blur_call(cube[0], taps_x, taps_y, w_rows)
     chains = []
     taken_0 = send(give_0, 0, 1)
-    keep_1, give_1 = project_call(x_high, x_low, w_both)
-    taken_0, keep_1, give_1 = lax.optimization_barrier((taken_0, keep_1, give_1))
+    keep_0, keep_1, give_1 = project_call(x_high, x_low, w_both, give_0)
+    taken_0, keep_0, keep_1, give_1 = lax.optimization_barrier((taken_0, keep_0, keep_1, give_1))
     for keep, taken in ((keep_0, taken_0), (keep_1, send(give_1, 0, 1))):
         bounds = [place * 4 * rank for place in (0, 1, 3, 2)]
         sides = []
@@ -469,20 +471,20 @@
     for k in range(4):
         part = slice(k * rank, (k + 1) * rank)
         line.append(jnp.concatenate(
-            [(sides[0][part] + others[0][part]) + (others[1][part] + others[2][part]) for sides, others in chains],
+            [(sides[0][part] + others[2][part]) + (others[1][part] + others[0][part]) for sides, others in chains],
             axis=1))
-    line = [line[0]] + [send(line[k], 2 * k, 0) for k in (3, 2, 1)]
+    line = [line[0]] + [send(line[k], 2 * k, 0) for k in range(1, 4)]
     h_piece = ratio * ((line[0] + line[1]) + (line[2] + line[3]))
-    h_line = [h_piece] + [send(h_piece, 2 * k, 0) for k in range(1, 4)]
+    h_line = [h_piece] + [send(h_piece, 2 * k, 0) for k in (3, 2, 1)][::-1]
     mine = jnp.stack(h_line)
-    first_parts = [mine] + around([mine] * 4)
+    first_parts = [mine] + [send(mine, k % 2, 2 * (k // 2)) for k in (3, 2, 1)][::-1]
     second_parts = [send(value, 0, 1) for value in first_parts]
     total = first_call(x_high, x_low, first_parts)
     w_piece = second_call(x_high, x_low, w_here, total, second_parts)
     own = [parts[k] for k in (0, 2) for parts in (first_parts, second_parts)]
     h_next = place_h_call(own, h_columns.shape)
     w_pair = jnp.stack([w_piece, send(w_piece, 1, 0)])
-    w_next = gather_w_call([w_pair] + [send(w_pair, 2 * k, 0) for k in range(1, 4)])
+    w_next = gather_w_call([w_pair] + [send(w_pair, 2 * k, 0) for k in (3, 2, 1)][::-1])
     return jnp.transpose(w_next)[None], jnp.transpose(h_next, (2, 0, 1))
 
 

time: 65.8 us -> 66.9 us (1.017)
  waiting for transfers between devices: 23.4 us -> 24.4 us
    ppermute x25, waiting for transfers between devices: 23.4 us -> 24.4 us  [send(): return lax.ppermute(value, ('sp', 'bd'), pairs)]
  transfers between devices with their start and end apart: 25 -> 25, of which waited for: 15 -> 14; matrix products, arithmetic and copies ran while one was open for 0% -> 0% of each run, Pallas kernels for 5% -> 5%
where the time goes in v20:
time: 66.9 us; the launch traced here: 66.8 us
  starting transfers between devices  28.6 us (43%)
  waiting for transfers between devices  24.4 us (36%)
  Pallas kernels  12.8 us (19%)
  between operations  0.77 us (1%)
    ppermute x25, starting transfers between devices, send(): return lax.ppermute(value, ('sp', 'bd'), pairs)  28.6 us
    ppermute x25, waiting for transfers between devices, send(): return lax.ppermute(value, ('sp', 'bd'), pairs)  24.4 us
    pallas_call x1, Pallas kernels, blur_call(): pl.pallas_call(blur_kernel, out_shape=[jax.ShapeDtypeStruct(image, BF16)]...  7.15 us
    pallas_call x1, Pallas kernels, second_call(): pl.pallas_call(second_kernel, out_shape=jax.ShapeDtypeStruct(w_here.shape...  1.39 us
  transfers between devices with their start and end apart: 25, of which 14 were waited for; matrix products, arithmetic and copies ran while one was open for 0% of the time, Pallas kernels for 5%

profile of v20, /device:TPU:0, one launch (start us, length us, event | category | flops | bytes accessed | tf_op | source)
XLA Modules:
  0.0 66.8 jit_solution(13391676383987557912)
XLA Ops:
  0.6 7.1 %shard_map.68 = (bf16[32,96,256]{2,1,0:T(8,128)(2,1)S(1)}, bf16[32,96,256]{2,1,0:T(8,128)(2,1)S(1)}, f32[48,96]{1,0:T(8,128)S(1)}, bf16[96,256]{1,0:T(8,128)(2,1)S(1)}, f32[792,128]{1,0:T(8,128)S(1)}) custom-call(f32[96,32,256]{2,1,0:T(8,128)} %bitcast.19, f32[25,1,96]{2,1,0:T(1,128)} %bitcast.28, f32[25,1,96]{2,1,0:T(1,128)} %bitcast.29, f32[48,768]{1,0:T(8,128)} %bitcast.22), custom_call_target="tpu_custom_call" | custom-call | tf_op jit(solution)/shard_map/pallas_call | solution.py:282
  7.8 0.5 collective-permute-start
  8.3 1.1 %shard_map.69 = (f32[792,128]{1,0:T(8,128)S(1)}, f32[768,128]{1,0:T(8,128)S(1)}, f32[768,128]{1,0:T(8,128)S(1)}) custom-call(bf16[32,96,256]{2,1,0:T(8,128)(2,1)S(1)} %get-tuple-element.14.xh_ref, bf16[32,96,256]{2,1,0:T(8,128)(2,1)S(1)} %get-tuple-element.15.xl_ref, bf16[96,256]{1,0:T(8,128)(2,1)S(1)} %get-tuple-element.18.w_both_ref, ...), custom_call_target="tpu_custom_call" | custom-call | tf_op jit(solution)/shard_map/pallas_call | solution.py:265
  9.4 0.2 collective-permute-done
  9.7 0.4 collective-permute-start.4
  10.1 0.0 copy-start
  10.1 3.7 %collective-permute-start.2 = (f32[192,128]{1,0:T(8,128)S(1)}, f32[192,128]{1,0:T(8,128)S(1)}, u32[]{:S(2)}, u32[]{:S(2)}) collective-permute-start(f32[192,128]{1,0:T(8,128)S(1)} %get-tuple-element.28), channel_id=1, source_target_pairs={{0,6},{1,7},{2,4},{3,5},{4,2},{5,3},{6,0},{7,1},{8,14},{9,15},{10,... | collective-permute-start | bytes 294920 | tf_op jit(solution)/shard_map/ppermute | solution.py:444
  13.8 0.5 collective-permute-start.3
  14.3 0.2 collective-permute-start.1
  14.5 0.0 collective-permute-done.4
  14.5 0.1 slice_add_fusion.4
  14.5 2.9 %collective-permute-start.5 = (f32[192,128]{1,0:T(8,128)S(1)}, f32[192,128]{1,0:T(8,128)S(1)}, u32[]{:S(2)}, u32[]{:S(2)}) collective-permute-start(f32[192,128]{1,0:T(8,128)S(1)} %get-tuple-element.32), channel_id=1, source_target_pairs={{0,6},{1,7},{2,4},{3,5},{4,2},{5,3},{6,0},{7,1},{8,14},{9,15},{10,... | collective-permute-start | bytes 294920 | tf_op jit(solution)/shard_map/ppermute | solution.py:444
  17.5 0.5 collective-permute-start.6
  18.0 0.0 collective-permute-done.2
  18.0 1.4 %collective-permute-start.7 = (f32[192,128]{1,0:T(8,128)S(1)}, f32[192,128]{1,0:T(8,128)S(1)}, u32[]{:S(2)}, u32[]{:S(2)}) collective-permute-start(f32[192,128]{1,0:T(8,128)S(1)} %get-tuple-element.30), channel_id=1, source_target_pairs={{0,4},{1,5},{2,6},{3,7},{4,0},{5,1},{6,2},{7,3},{8,12},{9,13},{10,... | collective-permute-start | bytes 294920 | tf_op jit(solution)/shard_map/ppermute | solution.py:444
  19.3 0.7 %collective-permute-done.3 = f32[192,128]{1,0:T(8,128)S(1)} collective-permute-done((f32[192,128]{1,0:T(8,128)S(1)}, f32[192,128]{1,0:T(8,128)S(1)}, u32[]{:S(2)}, u32[]{:S(2)}) %collective-permute-start.3) | collective-permute-done | bytes 98336 | tf_op jit(solution)/shard_map/ppermute | solution.py:444
  20.0 1.9 %collective-permute-done.1.other_ref = f32[216,128]{1,0:T(8,128)S(1)} collective-permute-done((f32[216,128]{1,0:T(8,128)S(1)}, f32[216,128]{1,0:T(8,128)S(1)}, u32[]{:S(2)}, u32[]{:S(2)}) %collective-permute-start.1) | collective-permute-done | bytes 110624 | tf_op jit(solution)/shard_map/ppermute | solution.py:444
  21.9 0.0 collective-permute-done.5
  21.9 1.7 %collective-permute-done.6 = f32[192,128]{1,0:T(8,128)S(1)} collective-permute-done((f32[192,128]{1,0:T(8,128)S(1)}, f32[192,128]{1,0:T(8,128)S(1)}, u32[]{:S(2)}, u32[]{:S(2)}) %collective-permute-start.6) | collective-permute-done | bytes 98336 | tf_op jit(solution)/shard_map/ppermute | solution.py:444
  23.7 0.0 collective-permute-done.7
  23.7 3.9 %collective-permute-start.10 = (f32[48,256]{1,0:T(8,128)S(1)}, f32[48,256]{1,0:T(8,128)S(1)}, u32[]{:S(2)}, u32[]{:S(2)}) collective-permute-start(f32[48,256]{1,0:T(8,128)S(1)} %pad_maximum_fusion.3), channel_id=1, source_target_pairs={{0,24},{1,25},{2,26},{3,27},{4,28},{5,29},{6,30},{7,31},{8,16},{9,... | collective-permute-start | bytes 147464 | tf_op jit(solution)/shard_map/ppermute | solution.py:444
  27.6 0.0 collective-permute-start.9
  27.6 0.6 collective-permute-start.8
  28.3 0.0 copy-done
  28.3 0.3 shard_map.70
  28.5 1.5 %collective-permute-done.10 = f32[48,256]{1,0:T(8,128)S(1)} collective-permute-done((f32[48,256]{1,0:T(8,128)S(1)}, f32[48,256]{1,0:T(8,128)S(1)}, u32[]{:S(2)}, u32[]{:S(2)}) %collective-permute-start.10) | collective-permute-done | bytes 49184 | tf_op jit(solution)/shard_map/ppermute | solution.py:444
  30.0 2.6 %collective-permute-done.9 = f32[48,256]{1,0:T(8,128)S(1)} collective-permute-done((f32[48,256]{1,0:T(8,128)S(1)}, f32[48,256]{1,0:T(8,128)S(1)}, u32[]{:S(2)}, u32[]{:S(2)}) %collective-permute-start.9) | collective-permute-done | bytes 49184 | tf_op jit(solution)/shard_map/ppermute | solution.py:444
  32.6 0.0 collective-permute-done.8
  32.6 0.4 collective-permute-start.11
  33.0 2.0 %collective-permute-start.12 = (f32[48,256]{1,0:T(8,128)S(1)}, f32[48,256]{1,0:T(8,128)S(1)}, u32[]{:S(2)}, u32[]{:S(2)}) collective-permute-start(f32[48,256]{1,0:T(8,128)S(1)} %fusion.1), channel_id=1, source_target_pairs={{0,16},{1,17},{2,18},{3,19},{4,20},{5,21},{6,22},{7,23},{8,24},{9,... | collective-permute-start | bytes 147464 | tf_op jit(solution)/shard_map/ppermute | solution.py:444
  35.1 2.0 %collective-permute-start.13 = (f32[48,256]{1,0:T(8,128)S(1)}, f32[48,256]{1,0:T(8,128)S(1)}, u32[]{:S(2)}, u32[]{:S(2)}) collective-permute-start(f32[48,256]{1,0:T(8,128)S(1)} %fusion.1), channel_id=1, source_target_pairs={{0,24},{1,25},{2,26},{3,27},{4,28},{5,29},{6,30},{7,31},{8,16},{9,... | collective-permute-start | bytes 147464 | tf_op jit(solution)/shard_map/ppermute | solution.py:444
  37.1 0.0 collective-permute-done.11
  37.1 1.0 %collective-permute-done.12 = f32[48,256]{1,0:T(8,128)S(1)} collective-permute-done((f32[48,256]{1,0:T(8,128)S(1)}, f32[48,256]{1,0:T(8,128)S(1)}, u32[]{:S(2)}, u32[]{:S(2)}) %collective-permute-start.12) | collective-permute-done | bytes 49184 | tf_op jit(solution)/shard_map/ppermute | solution.py:444
  38.0 2.9 %collective-permute-done.13 = f32[48,256]{1,0:T(8,128)S(1)} collective-permute-done((f32[48,256]{1,0:T(8,128)S(1)}, f32[48,256]{1,0:T(8,128)S(1)}, u32[]{:S(2)}, u32[]{:S(2)}) %collective-permute-start.13) | collective-permute-done | bytes 49184 | tf_op jit(solution)/shard_map/ppermute | solution.py:444
  41.0 1.9 %collective-permute-start.15 = (f32[4,48,256]{2,1,0:T(8,128)S(1)}, f32[4,48,256]{2,1,0:T(8,128)S(1)}, u32[]{:S(2)}, u32[]{:S(2)}) collective-permute-start(f32[4,48,256]{2,1,0:T(8,128)S(1)} %pad_maximum_fusion.rest_0_.refs_0_), channel_id=1, source_target_pairs={{0,2},{1,3},{2,0},{3,1},{4,6},{5,7},{6,4},{7,5},{8,10},{9,11},{10,... | collective-permute-start | bytes 589832 | tf_op jit(solution)/shard_map/ppermute | solution.py:444
  42.8 1.5 %collective-permute-start.14 = (f32[4,48,256]{2,1,0:T(8,128)S(1)}, f32[4,48,256]{2,1,0:T(8,128)S(1)}, u32[]{:S(2)}, u32[]{:S(2)}) collective-permute-start(f32[4,48,256]{2,1,0:T(8,128)S(1)} %pad_maximum_fusion.rest_0_.refs_0_), channel_id=1, source_target_pairs={{0,4},{1,5},{2,6},{3,7},{4,0},{5,1},{6,2},{7,3},{8,12},{9,13},{10,... | collective-permute-start | bytes 589832 | tf_op jit(solution)/shard_map/ppermute | solution.py:444
  44.3 0.2 collective-permute-start.16
  44.5 0.0 collective-permute-start.17
  44.5 4.3 %collective-permute-done.15.rest_2_.refs_2_ = f32[4,48,256]{2,1,0:T(8,128)S(1)} collective-permute-done((f32[4,48,256]{2,1,0:T(8,128)S(1)}, f32[4,48,256]{2,1,0:T(8,128)S(1)}, u32[]{:S(2)}, u32[]{:S(2)}) %collective-permute-start.15) | collective-permute-done | bytes 196640 | tf_op jit(solution)/shard_map/ppermute | solution.py:444
  48.8 0.0 collective-permute-start.19
  48.8 0.3 collective-permute-done.14.rest_1_
  49.1 0.2 collective-permute-start.18
  49.3 1.9 %collective-permute-done.16.rest_3_ = f32[4,48,256]{2,1,0:T(8,128)S(1)} collective-permute-done((f32[4,48,256]{2,1,0:T(8,128)S(1)}, f32[4,48,256]{2,1,0:T(8,128)S(1)}, u32[]{:S(2)}, u32[]{:S(2)}) %collective-permute-start.16) | collective-permute-done | bytes 196640 | tf_op jit(solution)/shard_map/ppermute | solution.py:444
  51.2 0.0 collective-permute-start.20
  51.2 1.1 %shard_map.71.total_ref = f32[288,96]{1,0:T(8,128)S(1)} custom-call(bf16[32,96,256]{2,1,0:T(8,128)(2,1)S(1)} %get-tuple-element.14.xh_ref, bf16[32,96,256]{2,1,0:T(8,128)(2,1)S(1)} %get-tuple-element.15.xl_ref, f32[4,48,256]{2,1,0:T(8,128)S(1)} %pad_maximum_fusion.rest_0_.refs_0_, f32[4,48,256]{2,1,0:T(8,128)S(1)} %collective-permute-done.14.rest_1_, ...), custom_call_target="tpu_custom_call" | custom-call | tf_op jit(solution)/shard_map/pallas_call | solution.py:353
  52.3 0.0 collective-permute-done.17.rest_0_.refs_1_
  52.3 0.0 collective-permute-done.19.rest_2_.refs_3_
  52.3 0.0 collective-permute-done.18.rest_1_
  52.4 0.3 collective-permute-done.20.rest_3_
  52.7 1.4 %shard_map.72 = f32[48,96]{1,0:T(8,128)S(1)} custom-call(bf16[32,96,256]{2,1,0:T(8,128)(2,1)S(1)} %get-tuple-element.14.xh_ref, bf16[32,96,256]{2,1,0:T(8,128)(2,1)S(1)} %get-tuple-element.15.xl_ref, f32[48,96]{1,0:T(8,128)S(1)} %get-tuple-element.16.w_ref, f32[288,96]{1,0:T(8,128)S(1)} %shard_map.71.total_ref, ...), custom_call_target="tpu_custom_call" | custom-call | tf_op jit(solution)/shard_map/pallas_call | solution.py:381
  54.1 1.4 %collective-permute-start.21 = (f32[48,96]{1,0:T(8,128)S(1)}, f32[48,96]{1,0:T(8,128)S(1)}, u32[]{:S(2)}, u32[]{:S(2)}) collective-permute-start(f32[48,96]{1,0:T(8,128)S(1)} %shard_map.72), channel_id=1, source_target_pairs={{0,4},{1,5},{2,6},{3,7},{4,0},{5,1},{6,2},{7,3},{8,12},{9,13},{10,... | collective-permute-start | bytes 55304 | tf_op jit(solution)/shard_map/ppermute | solution.py:444
  55.4 2.5 %collective-permute-done.21 = f32[48,96]{1,0:T(8,128)S(1)} collective-permute-done((f32[48,96]{1,0:T(8,128)S(1)}, f32[48,96]{1,0:T(8,128)S(1)}, u32[]{:S(2)}, u32[]{:S(2)}) %collective-permute-start.21) | collective-permute-done | bytes 18464 | tf_op jit(solution)/shard_map/ppermute | solution.py:444
  58.0 0.1 collective-permute-start.22
  58.0 2.1 %collective-permute-start.23 = (f32[2,48,96]{2,1,0:T(8,128)S(1)}, f32[2,48,96]{2,1,0:T(8,128)S(1)}, u32[]{:S(2)}, u32[]{:S(2)}) collective-permute-start(f32[2,48,96]{2,1,0:T(8,128)S(1)} %pad_maximum_fusion.4.refs_0_), channel_id=1, source_target_pairs={{0,16},{1,17},{2,18},{3,19},{4,20},{5,21},{6,22},{7,23},{8,24},{9,... | collective-permute-start | bytes 110600 | tf_op jit(solution)/shard_map/ppermute | solution.py:444
  60.1 2.3 %collective-permute-start.24 = (f32[2,48,96]{2,1,0:T(8,128)S(1)}, f32[2,48,96]{2,1,0:T(8,128)S(1)}, u32[]{:S(2)}, u32[]{:S(2)}) collective-permute-start(f32[2,48,96]{2,1,0:T(8,128)S(1)} %pad_maximum_fusion.4.refs_0_), channel_id=1, source_target_pairs={{0,24},{1,25},{2,26},{3,27},{4,28},{5,29},{6,30},{7,31},{8,16},{9,... | collective-permute-start | bytes 110600 | tf_op jit(solution)/shard_map/ppermute | solution.py:444
  62.4 1.0 %shard_map.74 = f32[32,32,48]{2,1,0:T(8,128)} custom-call(f32[4,48,256]{2,1,0:T(8,128)S(1)} %pad_maximum_fusion.rest_0_.refs_0_, f32[4,48,256]{2,1,0:T(8,128)S(1)} %collective-permute-done.17.rest_0_.refs_1_, f32[4,48,256]{2,1,0:T(8,128)S(1)} %collective-permute-done.15.rest_2_.refs_2_, f32[4,48,256]{2,1,0:T(8,128)S(1)} %collective-permute-done.19.rest_2_.refs_3_), custom_call_target="tpu_custom_call" | custom-call | tf_op jit(solution)/shard_map/pallas_call | solution.py:401
  63.4 0.0 collective-permute-done.22.refs_1_
  63.4 0.0 collective-permute-done.23.refs_2_
  63.4 2.6 %collective-permute-done.24.refs_3_ = f32[2,48,96]{2,1,0:T(8,128)S(1)} collective-permute-done((f32[2,48,96]{2,1,0:T(8,128)S(1)}, f32[2,48,96]{2,1,0:T(8,128)S(1)}, u32[]{:S(2)}, u32[]{:S(2)}) %collective-permute-start.24) | collective-permute-done | bytes 36896 | tf_op jit(solution)/shard_map/ppermute | solution.py:444
  66.0 0.8 %shard_map.73 = f32[48,768]{1,0:T(8,128)} custom-call(f32[2,48,96]{2,1,0:T(8,128)S(1)} %pad_maximum_fusion.4.refs_0_, f32[2,48,96]{2,1,0:T(8,128)S(1)} %collective-permute-done.22.refs_1_, f32[2,48,96]{2,1,0:T(8,128)S(1)} %collective-permute-done.23.refs_2_, f32[2,48,96]{2,1,0:T(8,128)S(1)} %collective-permute-done.24.refs_3_), custom_call_target="tpu_custom_call" | custom-call | tf_op jit(solution)/shard_map/pallas_call | solution.py:428
  (10 shorter events, 0.2 us)
Async XLA Ops:
  7.8 1.9 %collective-permute-start = (f32[792,128]{1,0:T(8,128)S(1)}, f32[792,128]{1,0:T(8,128)S(1)}, u32[]{:S(2)}, u32[]{:S(2)}) collective-permute-start(f32[792,128]{1,0:T(8,128)S(1)} %get-tuple-element.17.first_ref), channel_id=1, source_target_pairs={{0,1},{1,0},{2,3},{3,2},{4,5},{5,4},{6,7},{7,6},{8,9},{9,8},{10,11... | collective-permute-start | bytes 1216520 | tf_op jit(solution)/shard_map/ppermute | solution.py:444
  9.7 4.8 %collective-permute-start.4 = (f32[768,128]{1,0:T(8,128)S(1)}, f32[768,128]{1,0:T(8,128)S(1)}, u32[]{:S(2)}, u32[]{:S(2)}) collective-permute-start(f32[768,128]{1,0:T(8,128)S(1)} %get-tuple-element.25), channel_id=1, source_target_pairs={{0,1},{1,0},{2,3},{3,2},{4,5},{5,4},{6,7},{7,6},{8,9},{9,8},{10,11... | collective-permute-start | bytes 1179656 | tf_op jit(solution)/shard_map/ppermute | solution.py:444
  10.1 18.2 %copy-start = (f32[48,32,32]{0,2,1:T(8,128)S(1)}, f32[48,32,32]{0,2,1:T(8,128)}, u32[]{:S(2)}) copy-start(f32[48,32,32]{0,2,1:T(8,128)} %param.9) | copy-start | bytes 589828
  10.1 7.9 %collective-permute-start.2 = (f32[192,128]{1,0:T(8,128)S(1)}, f32[192,128]{1,0:T(8,128)S(1)}, u32[]{:S(2)}, u32[]{:S(2)}) collective-permute-start(f32[192,128]{1,0:T(8,128)S(1)} %get-tuple-element.28), channel_id=1, source_target_pairs={{0,6},{1,7},{2,4},{3,5},{4,2},{5,3},{6,0},{7,1},{8,14},{9,15},{10,... | collective-permute-start | bytes 294920 | tf_op jit(solution)/shard_map/ppermute | solution.py:444
  13.8 6.2 %collective-permute-start.3 = (f32[192,128]{1,0:T(8,128)S(1)}, f32[192,128]{1,0:T(8,128)S(1)}, u32[]{:S(2)}, u32[]{:S(2)}) collective-permute-start(f32[192,128]{1,0:T(8,128)S(1)} %get-tuple-element.27), channel_id=1, source_target_pairs={{0,4},{1,5},{2,6},{3,7},{4,0},{5,1},{6,2},{7,3},{8,12},{9,13},{10,... | collective-permute-start | bytes 294920 | tf_op jit(solution)/shard_map/ppermute | solution.py:444
  14.3 7.6 %collective-permute-start.1 = (f32[216,128]{1,0:T(8,128)S(1)}, f32[216,128]{1,0:T(8,128)S(1)}, u32[]{:S(2)}, u32[]{:S(2)}) collective-permute-start(f32[216,128]{1,0:T(8,128)S(1)} %slice_add_fusion.mine_ref), channel_id=1, source_target_pairs={{0,2},{1,3},{2,0},{3,1},{4,6},{5,7},{6,4},{7,5},{8,10},{9,11},{10,... | collective-permute-start | bytes 331784 | tf_op jit(solution)/shard_map/ppermute | solution.py:444
  14.5 7.4 %collective-permute-start.5 = (f32[192,128]{1,0:T(8,128)S(1)}, f32[192,128]{1,0:T(8,128)S(1)}, u32[]{:S(2)}, u32[]{:S(2)}) collective-permute-start(f32[192,128]{1,0:T(8,128)S(1)} %get-tuple-element.32), channel_id=1, source_target_pairs={{0,6},{1,7},{2,4},{3,5},{4,2},{5,3},{6,0},{7,1},{8,14},{9,15},{10,... | collective-permute-start | bytes 294920 | tf_op jit(solution)/shard_map/ppermute | solution.py:444
  17.5 6.2 %collective-permute-start.6 = (f32[192,128]{1,0:T(8,128)S(1)}, f32[192,128]{1,0:T(8,128)S(1)}, u32[]{:S(2)}, u32[]{:S(2)}) collective-permute-start(f32[192,128]{1,0:T(8,128)S(1)} %get-tuple-element.31), channel_id=1, source_target_pairs={{0,2},{1,3},{2,0},{3,1},{4,6},{5,7},{6,4},{7,5},{8,10},{9,11},{10,... | collective-permute-start | bytes 294920 | tf_op jit(solution)/shard_map/ppermute | solution.py:444
  18.0 5.7 %collective-permute-start.7 = (f32[192,128]{1,0:T(8,128)S(1)}, f32[192,128]{1,0:T(8,128)S(1)}, u32[]{:S(2)}, u32[]{:S(2)}) collective-permute-start(f32[192,128]{1,0:T(8,128)S(1)} %get-tuple-element.30), channel_id=1, source_target_pairs={{0,4},{1,5},{2,6},{3,7},{4,0},{5,1},{6,2},{7,3},{8,12},{9,13},{10,... | collective-permute-start | bytes 294920 | tf_op jit(solution)/shard_map/ppermute | solution.py:444
  23.7 6.3 %collective-permute-start.10 = (f32[48,256]{1,0:T(8,128)S(1)}, f32[48,256]{1,0:T(8,128)S(1)}, u32[]{:S(2)}, u32[]{:S(2)}) collective-permute-start(f32[48,256]{1,0:T(8,128)S(1)} %pad_maximum_fusion.3), channel_id=1, source_target_pairs={{0,24},{1,25},{2,26},{3,27},{4,28},{5,29},{6,30},{7,31},{8,16},{9,... | collective-permute-start | bytes 147464 | tf_op jit(solution)/shard_map/ppermute | solution.py:444
  27.6 5.0 %collective-permute-start.9 = (f32[48,256]{1,0:T(8,128)S(1)}, f32[48,256]{1,0:T(8,128)S(1)}, u32[]{:S(2)}, u32[]{:S(2)}) collective-permute-start(f32[48,256]{1,0:T(8,128)S(1)} %pad_maximum_fusion.2), channel_id=1, source_target_pairs={{0,16},{1,17},{2,18},{3,19},{4,20},{5,21},{6,22},{7,23},{8,24},{9,... | collective-permute-start | bytes 147464 | tf_op jit(solution)/shard_map/ppermute | solution.py:444
  27.6 5.0 %collective-permute-start.8 = (f32[48,256]{1,0:T(8,128)S(1)}, f32[48,256]{1,0:T(8,128)S(1)}, u32[]{:S(2)}, u32[]{:S(2)}) collective-permute-start(f32[48,256]{1,0:T(8,128)S(1)} %pad_maximum_fusion.1), channel_id=1, source_target_pairs={{0,8},{1,9},{2,10},{3,11},{4,12},{5,13},{6,14},{7,15},{8,0},{9,1},... | collective-permute-start | bytes 147464 | tf_op jit(solution)/shard_map/ppermute | solution.py:444
  32.6 4.5 %collective-permute-start.11 = (f32[48,256]{1,0:T(8,128)S(1)}, f32[48,256]{1,0:T(8,128)S(1)}, u32[]{:S(2)}, u32[]{:S(2)}) collective-permute-start(f32[48,256]{1,0:T(8,128)S(1)} %fusion.1), channel_id=1, source_target_pairs={{0,8},{1,9},{2,10},{3,11},{4,12},{5,13},{6,14},{7,15},{8,0},{9,1},... | collective-permute-start | bytes 147464 | tf_op jit(solution)/shard_map/ppermute | solution.py:444
  33.0 5.0 %collective-permute-start.12 = (f32[48,256]{1,0:T(8,128)S(1)}, f32[48,256]{1,0:T(8,128)S(1)}, u32[]{:S(2)}, u32[]{:S(2)}) collective-permute-start(f32[48,256]{1,0:T(8,128)S(1)} %fusion.1), channel_id=1, source_target_pairs={{0,16},{1,17},{2,18},{3,19},{4,20},{5,21},{6,22},{7,23},{8,24},{9,... | collective-permute-start | bytes 147464 | tf_op jit(solution)/shard_map/ppermute | solution.py:444
  35.1 5.9 %collective-permute-start.13 = (f32[48,256]{1,0:T(8,128)S(1)}, f32[48,256]{1,0:T(8,128)S(1)}, u32[]{:S(2)}, u32[]{:S(2)}) collective-permute-start(f32[48,256]{1,0:T(8,128)S(1)} %fusion.1), channel_id=1, source_target_pairs={{0,24},{1,25},{2,26},{3,27},{4,28},{5,29},{6,30},{7,31},{8,16},{9,... | collective-permute-start | bytes 147464 | tf_op jit(solution)/shard_map/ppermute | solution.py:444
  41.0 7.8 %collective-permute-start.15 = (f32[4,48,256]{2,1,0:T(8,128)S(1)}, f32[4,48,256]{2,1,0:T(8,128)S(1)}, u32[]{:S(2)}, u32[]{:S(2)}) collective-permute-start(f32[4,48,256]{2,1,0:T(8,128)S(1)} %pad_maximum_fusion.rest_0_.refs_0_), channel_id=1, source_target_pairs={{0,2},{1,3},{2,0},{3,1},{4,6},{5,7},{6,4},{7,5},{8,10},{9,11},{10,... | collective-permute-start | bytes 589832 | tf_op jit(solution)/shard_map/ppermute | solution.py:444
  42.8 6.2 %collective-permute-start.14 = (f32[4,48,256]{2,1,0:T(8,128)S(1)}, f32[4,48,256]{2,1,0:T(8,128)S(1)}, u32[]{:S(2)}, u32[]{:S(2)}) collective-permute-start(f32[4,48,256]{2,1,0:T(8,128)S(1)} %pad_maximum_fusion.rest_0_.refs_0_), channel_id=1, source_target_pairs={{0,4},{1,5},{2,6},{3,7},{4,0},{5,1},{6,2},{7,3},{8,12},{9,13},{10,... | collective-permute-start | bytes 589832 | tf_op jit(solution)/shard_map/ppermute | solution.py:444
  44.3 6.9 %collective-permute-start.16 = (f32[4,48,256]{2,1,0:T(8,128)S(1)}, f32[4,48,256]{2,1,0:T(8,128)S(1)}, u32[]{:S(2)}, u32[]{:S(2)}) collective-permute-start(f32[4,48,256]{2,1,0:T(8,128)S(1)} %pad_maximum_fusion.rest_0_.refs_0_), channel_id=1, source_target_pairs={{0,6},{1,7},{2,4},{3,5},{4,2},{5,3},{6,0},{7,1},{8,14},{9,15},{10,... | collective-permute-start | bytes 589832 | tf_op jit(solution)/shard_map/ppermute | solution.py:444
  44.5 7.8 %collective-permute-start.17 = (f32[4,48,256]{2,1,0:T(8,128)S(1)}, f32[4,48,256]{2,1,0:T(8,128)S(1)}, u32[]{:S(2)}, u32[]{:S(2)}) collective-permute-start(f32[4,48,256]{2,1,0:T(8,128)S(1)} %pad_maximum_fusion.rest_0_.refs_0_), channel_id=1, source_target_pairs={{0,1},{1,0},{2,3},{3,2},{4,5},{5,4},{6,7},{7,6},{8,9},{9,8},{10,11... | collective-permute-start | bytes 589832 | tf_op jit(solution)/shard_map/ppermute | solution.py:444
  48.8 3.5 %collective-permute-start.19 = (f32[4,48,256]{2,1,0:T(8,128)S(1)}, f32[4,48,256]{2,1,0:T(8,128)S(1)}, u32[]{:S(2)}, u32[]{:S(2)}) collective-permute-start(f32[4,48,256]{2,1,0:T(8,128)S(1)} %collective-permute-done.15.rest_2_.refs_2_), channel_id=1, source_target_pairs={{0,1},{1,0},{2,3},{3,2},{4,5},{5,4},{6,7},{7,6},{8,9},{9,8},{10,11... | collective-permute-start | bytes 589832 | tf_op jit(solution)/shard_map/ppermute | solution.py:444
  49.1 3.3 %collective-permute-start.18 = (f32[4,48,256]{2,1,0:T(8,128)S(1)}, f32[4,48,256]{2,1,0:T(8,128)S(1)}, u32[]{:S(2)}, u32[]{:S(2)}) collective-permute-start(f32[4,48,256]{2,1,0:T(8,128)S(1)} %collective-permute-done.14.rest_1_), channel_id=1, source_target_pairs={{0,1},{1,0},{2,3},{3,2},{4,5},{5,4},{6,7},{7,6},{8,9},{9,8},{10,11... | collective-permute-start | bytes 589832 | tf_op jit(solution)/shard_map/ppermute | solution.py:444
  51.2 1.4 %collective-permute-start.20 = (f32[4,48,256]{2,1,0:T(8,128)S(1)}, f32[4,48,256]{2,1,0:T(8,128)S(1)}, u32[]{:S(2)}, u32[]{:S(2)}) collective-permute-start(f32[4,48,256]{2,1,0:T(8,128)S(1)} %collective-permute-done.16.rest_3_), channel_id=1, source_target_pairs={{0,1},{1,0},{2,3},{3,2},{4,5},{5,4},{6,7},{7,6},{8,9},{9,8},{10,11... | collective-permute-start | bytes 589832 | tf_op jit(solution)/shard_map/ppermute | solution.py:444
  54.1 3.9 %collective-permute-start.21 = (f32[48,96]{1,0:T(8,128)S(1)}, f32[48,96]{1,0:T(8,128)S(1)}, u32[]{:S(2)}, u32[]{:S(2)}) collective-permute-start(f32[48,96]{1,0:T(8,128)S(1)} %shard_map.72), channel_id=1, source_target_pairs={{0,4},{1,5},{2,6},{3,7},{4,0},{5,1},{6,2},{7,3},{8,12},{9,13},{10,... | collective-permute-start | bytes 55304 | tf_op jit(solution)/shard_map/ppermute | solution.py:444
  58.0 5.5 %collective-permute-start.22 = (f32[2,48,96]{2,1,0:T(8,128)S(1)}, f32[2,48,96]{2,1,0:T(8,128)S(1)}, u32[]{:S(2)}, u32[]{:S(2)}) collective-permute-start(f32[2,48,96]{2,1,0:T(8,128)S(1)} %pad_maximum_fusion.4.refs_0_), channel_id=1, source_target_pairs={{0,8},{1,9},{2,10},{3,11},{4,12},{5,13},{6,14},{7,15},{8,0},{9,1},... | collective-permute-start | bytes 110600 | tf_op jit(solution)/shard_map/ppermute | solution.py:444
  58.0 5.4 %collective-permute-start.23 = (f32[2,48,96]{2,1,0:T(8,128)S(1)}, f32[2,48,96]{2,1,0:T(8,128)S(1)}, u32[]{:S(2)}, u32[]{:S(2)}) collective-permute-start(f32[2,48,96]{2,1,0:T(8,128)S(1)} %pad_maximum_fusion.4.refs_0_), channel_id=1, source_target_pairs={{0,16},{1,17},{2,18},{3,19},{4,20},{5,21},{6,22},{7,23},{8,24},{9,... | collective-permute-start | bytes 110600 | tf_op jit(solution)/shard_map/ppermute | solution.py:444
  60.1 5.9 %collective-permute-start.24 = (f32[2,48,96]{2,1,0:T(8,128)S(1)}, f32[2,48,96]{2,1,0:T(8,128)S(1)}, u32[]{:S(2)}, u32[]{:S(2)}) collective-permute-start(f32[2,48,96]{2,1,0:T(8,128)S(1)} %pad_maximum_fusion.4.refs_0_), channel_id=1, source_target_pairs={{0,24},{1,25},{2,26},{3,27},{4,28},{5,29},{6,30},{7,31},{8,16},{9,... | collective-permute-start | bytes 110600 | tf_op jit(solution)/shard_map/ppermute | solution.py:444
